TPU v7x, 128 devices: a whole 4x4x4 slice. The times are simulated.
128 devices in a mesh: dp: 16 (over x, z_hi, core), tensor: 8 (over z_lo, y).
Axes of the slice: x: 4, y: 4, z: 4 (z_hi: 2, z_lo: 2; z = z_hi * 2 + z_lo), core: 2. Of those that a mesh axis runs over, the one named last changes fastest.
Arguments:
- queries: bfloat16 [4096, 8192], P('dp', 'tensor'), may hold values from -5 to 5
- keys: bfloat16 [4096, 1024], P('dp', 'tensor'), may hold values from -5 to 5
- values: bfloat16 [4096, 1024], P('dp', 'tensor'), may hold values from -6 to 6
- grad_out: bfloat16 [4096, 8192], P('dp', 'tensor'), may hold values from -6 to 6
- out_weight: bfloat16 [8192, 8192], P('tensor', 'dp'), may hold values from -0.0625 to 0.0625
- lengths: int32 [8], replicated, may hold values from 1 to 2560, 4096 in all
Outputs:
- grad_queries: bfloat16 [4096, 8192], P('dp', 'tensor')
- key_gradient: bfloat16 [4096, 1024], P('dp', 'tensor')
- value_gradient: bfloat16 [4096, 1024], P('dp', 'tensor')
All inputs are finite; a program needn't handle non-finite values.
Results may differ from a plain program's by a relative error of at most 0.0083.
Values may be sent and summed in bfloat16 or wider, within the bound.
No kernel may reach another device: no remote copies, remote signals or barrier semaphores. Data moves between devices by JAX's collectives and lax.ppermute only.
A program may use at most 128 MiB of HBM per device.

v0:
```python
import math

import jax
import jax.numpy as jnp
from jax import lax
from jax.sharding import PartitionSpec as P

HEAD_WIDTH = 128


floor_score = -1e30


def doc_index(lengths, positions):
    bounds = jnp.cumsum(lengths)[:-1]
    return jnp.sum((bounds[None, :] <= positions[:, None]).astype(jnp.int32), axis=1)


def split_heads(rows, kv_heads):
    return rows.reshape(
        rows.shape[0], kv_heads, rows.shape[1] // (kv_heads * HEAD_WIDTH), HEAD_WIDTH
    )


def head_products(left_heads, right_rows, kv_heads):
    right = right_rows.reshape(right_rows.shape[0], kv_heads, HEAD_WIDTH)
    return jnp.einsum("tgcd,ugd->gctu", left_heads, right, preferred_element_type=jnp.float32)


def pair_mask(query_docs, query_pos, key_docs, key_pos):
    return (query_docs[:, None] == key_docs[None, :]) & (key_pos[None, :] <= query_pos[:, None])


def row_statistics(
    query_heads,
    grad_split,
    keys_all,
    values_all,
    lengths,
    query_pos,
    query_docs,
    block_size,
    kv_heads,
    scale_factor,
):
    rows_here = query_pos.shape[0]
    shape = (kv_heads, query_heads.shape[2], rows_here)
    init = (
        jnp.full(shape, floor_score, jnp.float32),
        jnp.zeros(shape, jnp.float32),
        jnp.zeros(shape, jnp.float32),
    )

    def row_step(index, carry):
        start = index * block_size
        key_pos = start + jnp.arange(block_size, dtype=jnp.int32)
        key_docs = doc_index(lengths, key_pos)
        live = (start <= query_pos[-1]) & (key_docs[-1] >= query_docs[0])

        def row_compute(state):
            top, mass, weighted = state
            key_block = lax.dynamic_slice_in_dim(keys_all, start, block_size, 0)
            value_block = lax.dynamic_slice_in_dim(values_all, start, block_size, 0)
            mask = pair_mask(query_docs, query_pos, key_docs, key_pos)
            score = jnp.where(
                mask, scale_factor * head_products(query_heads, key_block, kv_heads), floor_score
            )
            dprob = head_products(grad_split, value_block, kv_heads)
            new_top = jnp.maximum(top, jnp.max(score, axis=-1))
            fade = jnp.exp(top - new_top)
            weights = jnp.where(mask, jnp.exp(score - new_top[..., None]), 0.0)
            return (
                new_top,
                mass * fade + jnp.sum(weights, axis=-1),
                weighted * fade + jnp.sum(weights * dprob, axis=-1),
            )

        return lax.cond(live, row_compute, lambda state: state, carry)

    top, mass, weighted = lax.fori_loop(0, keys_all.shape[0] // block_size, row_step, init)
    return (top + jnp.log(mass), weighted / mass)


def query_pass(
    query_heads,
    grad_split,
    keys_all,
    values_all,
    lengths,
    query_pos,
    query_docs,
    log_total,
    delta,
    block_size,
    kv_heads,
    scale_factor,
):
    total_rows = keys_all.shape[0]
    grad_q = jnp.zeros(query_heads.shape, jnp.float32)
    init = (grad_q, jnp.zeros(keys_all.shape, jnp.float32), jnp.zeros(keys_all.shape, jnp.float32))

    def query_step(index, carry):
        start = index * block_size
        key_pos = start + jnp.arange(block_size, dtype=jnp.int32)
        key_docs = doc_index(lengths, key_pos)
        live = (start <= query_pos[-1]) & (key_docs[-1] >= query_docs[0])

        def query_compute(state):
            key_block = lax.dynamic_slice_in_dim(keys_all, start, block_size, 0)
            value_block = lax.dynamic_slice_in_dim(values_all, start, block_size, 0)
            mask = pair_mask(query_docs, query_pos, key_docs, key_pos)
            score = scale_factor * head_products(query_heads, key_block, kv_heads)
            probs = jnp.where(mask, jnp.exp(score - log_total[..., None]), 0.0)
            dprob = head_products(grad_split, value_block, kv_heads)
            dscore = (probs * (dprob - delta[..., None])).astype(jnp.bfloat16)
            key_split = key_block.reshape(block_size, kv_heads, HEAD_WIDTH)
            new_q = state[0] + scale_factor * jnp.einsum(
                "gctu,ugd->tgcd", dscore, key_split, preferred_element_type=jnp.float32
            )
            key_term = scale_factor * jnp.einsum(
                "gctu,tgcd->ugd", dscore, query_heads, preferred_element_type=jnp.float32
            )
            value_term = jnp.einsum(
                "gctu,tgcd->ugd",
                probs.astype(jnp.bfloat16),
                grad_split,
                preferred_element_type=jnp.float32,
            )
            key_sums = lax.dynamic_update_slice_in_dim(
                state[1], key_term.reshape(block_size, -1), start, 0
            )
            value_sums = lax.dynamic_update_slice_in_dim(
                state[2], value_term.reshape(block_size, -1), start, 0
            )
            return (new_q, key_sums, value_sums)

        return lax.cond(live, query_compute, lambda state: state, carry)

    return lax.fori_loop(0, total_rows // block_size, query_step, init)


def local(queries, keys, values, grad_out, out_weight, lengths):
    rows_here = queries.shape[0]
    kv_heads = keys.shape[1] // HEAD_WIDTH
    ranks = lax.axis_size("dp")
    start_here = lax.axis_index("dp") * rows_here
    block_size = math.gcd(rows_here * ranks, 512)
    scale_factor = 1.0 / math.sqrt(HEAD_WIDTH)
    full_grad = lax.all_gather(grad_out, "tensor", axis=1, tiled=True)
    gradient_heads = lax.dot_general(
        full_grad,
        lax.all_gather(out_weight, "dp", axis=1, tiled=True),
        (((1,), (1,)), ((), ())),
        preferred_element_type=jnp.float32,
    )
    grad_rows_b = gradient_heads.astype(jnp.bfloat16)
    query_heads = split_heads(queries, kv_heads)
    grad_split = split_heads(grad_rows_b, kv_heads)
    query_pos = start_here + jnp.arange(rows_here, dtype=jnp.int32)
    query_docs = doc_index(lengths, query_pos)
    keys_all, values_all = (
        lax.all_gather(keys, "dp", axis=0, tiled=True),
        lax.all_gather(values, "dp", axis=0, tiled=True),
    )
    log_total, delta = row_statistics(
        query_heads,
        grad_split,
        keys_all,
        values_all,
        lengths,
        query_pos,
        query_docs,
        block_size,
        kv_heads,
        scale_factor,
    )
    grad_q, key_terms, value_terms = query_pass(
        query_heads,
        grad_split,
        keys_all,
        values_all,
        lengths,
        query_pos,
        query_docs,
        log_total,
        delta,
        block_size,
        kv_heads,
        scale_factor,
    )
    key_gradient, value_gradient = (
        lax.psum_scatter(key_terms, "dp", scatter_dimension=0, tiled=True),
        lax.psum_scatter(value_terms, "dp", scatter_dimension=0, tiled=True),
    )
    grad_queries = grad_q.reshape(rows_here, -1).astype(jnp.bfloat16)
    return (grad_queries, key_gradient.astype(jnp.bfloat16), value_gradient.astype(jnp.bfloat16))


def solution(mesh):
    return jax.shard_map(
        local,
        mesh=mesh,
        in_specs=(
            P("dp", "tensor"),
            P("dp", "tensor"),
            P("dp", "tensor"),
            P("dp", "tensor"),
            P("tensor", "dp"),
            P(),
        ),
        out_specs=(P("dp", "tensor"), P("dp", "tensor"), P("dp", "tensor")),
        check_vma=False,
    )
```

profile of v0, /device:TPU:0, one launch (start us, length us, event | category | flops | bytes accessed | tf_op | source)
XLA Modules:
  0.0 577.7 jit_solution(13319978807276102411)
XLA Ops:
  10.8 1.2 copy.24
  12.5 52.3 %all-gather.9.cloned.1.call-done = bf16[256,8192]{1,0:T(8,128)(2,1)} async-done(((bf16[256,1024]{1,0:T(8,128)(2,1)}), bf16[256,8192]{1,0:T(8,128)(2,1)}) %all-gather.9.cloned.1.call-update) | async-done | bytes 4194320 | tf_op jit(solution)/shard_map/all_gather | solution.py:149
  64.8 124.3 %all-gather.11.cloned.1.call-done = bf16[1024,8192]{1,0:T(8,128)(2,1)} async-done(((bf16[1024,512]{1,0:T(8,128)(2,1)}), bf16[1024,8192]{1,0:T(8,128)(2,1)}) %all-gather.11.cloned.1.call-update) | async-done | bytes 16777232 | tf_op jit(solution)/shard_map/all_gather | solution.py:152
  189.2 11.6 %fusion.65 = bf16[32,8,8,128]{3,1,2,0:T(8,128)(2,1)S(1)} fusion(bf16[256,8192]{1,0:T(8,128)(2,1)} %all-gather.9.cloned.1.call-done, bf16[1024,8192]{1,0:T(8,128)(2,1)} %all-gather.11.cloned.1.call-done), kind=kOutput, calls=%fused_computation.68 | convolution fusion | flops 4295229440 | bytes 21495808 | tf_op jit(solution)/shard_map/dot_general | solution.py:150
  200.9 33.7 %all-gather.5.cloned.1.call-done = bf16[4096,128]{1,0:T(8,128)(2,1)} async-done(((bf16[256,128]{1,0:T(8,128)(2,1)}), bf16[4096,128]{1,0:T(8,128)(2,1)}) %all-gather.5.cloned.1.call-update) | async-done | bytes 1048592 | tf_op jit(solution)/shard_map/all_gather | solution.py:162
  234.6 46.0 %all-gather.7.cloned.1.call-done = bf16[4096,128]{1,0:T(8,128)(2,1)} async-done(((bf16[256,128]{1,0:T(8,128)(2,1)}), bf16[4096,128]{1,0:T(8,128)(2,1)}) %all-gather.7.cloned.1.call-update) | async-done | bytes 1048592 | tf_op jit(solution)/shard_map/all_gather | solution.py:163
  280.6 35.4 %while.38 = (s32[]{:T(128)}, f32[1,8,256]{2,1,0:T(8,128)S(1)}, f32[1,8,256]{2,1,0:T(8,128)S(1)}, f32[1,8,256]{2,1,0:T(8,128)S(1)}, s32[256]{0:T(256)S(1)}, /*ind...) while((s32[]{:T(128)}, f32[1,8,256]{2,1,0:T(8,128)S(1)}, ...), condition=%wide.region_9.10_spmd, body=%wide.region_2.9_spmd.sunk | while | flops 551961600 | bytes 14584281 | solution.py:80
  284.3 5.4 conditional.4
  284.5 1.7 fusion.1
  286.2 1.0 fusion.2
  287.2 2.4 fusion
  315.9 1.5 broadcast.67
  317.4 1.4 broadcast.67.clone
  318.9 38.1 %while.39 = (s32[]{:T(128)}, f32[256,1,8,128]{0,3,2,1:T(8,128)S(1)}, f32[4096,128]{1,0:T(8,128)}, f32[4096,128]{1,0:T(8,128)}, s32[256]{0:T(256)S(1)}, /*index=5...) while((s32[]{:T(128)}, ...), condition=%wide.region_14.15_spmd, body=%wide.region_10.14_spmd.sunk | while | flops 1353657344 | bytes 24422916 | solution.py:139
  322.6 8.6 %conditional.5 = ((f32[256,1,8,128]{0,3,2,1:T(8,128)S(1)}, f32[4096,128]{1,0:T(8,128)}, f32[4096,128]{1,0:T(8,128)})) conditional(s32[]{:T(128)} %convert_element_type.88, (f32[256,1,8,128]{0,3,2,1:T(8,128)S(1)}, f32[4096,128]{1,0:T(8,128)}, f32[4096,128]{1,0:T(8,128)}) %tuple.98, (s32[]{:T(128)}, bf16[4096,128]{1,0:T(8,128)(2,1)}, ...), branch_computations={%region_12.12_spmd, %region_13.13_spmd} | conditional | flops 1353646592 | bytes 24414298 | solution.py:137
  322.6 1.6 fusion.52
  324.5 2.3 fusion.13
  326.8 1.4 fusion.46
  328.2 1.4 fusion.31
  329.6 1.6 fusion.37
  358.7 136.8 %reduce-scatter.3.cloned.1.call-done = f32[256,128]{1,0:T(8,128)} async-done(((f32[4096,128]{1,0:T(8,128)}), f32[256,128]{1,0:T(8,128)}) %reduce-scatter.3.cloned.1.call-update) | async-done | bytes 131088 | tf_op jit(solution)/shard_map/reduce_scatter | solution.py:192
  495.6 1.5 convert_element_type.64
  497.1 72.2 %reduce-scatter.5.cloned.1.call-done = f32[256,128]{1,0:T(8,128)} async-done(((f32[4096,128]{1,0:T(8,128)}), f32[256,128]{1,0:T(8,128)}) %reduce-scatter.5.cloned.1.call-update) | async-done | bytes 131088 | tf_op jit(solution)/shard_map/reduce_scatter | solution.py:193
  569.3 1.5 convert_element_type.65
  (159 shorter events, 35.3 us)
Async XLA Ops:
  7.2 57.7 %all-gather.9.cloned.1.call-start = ((), (), s32[]{:S(2)}) async-start(), calls=%async_computation.4 | async-start | bytes 4718592 | tf_op jit(solution)/shard_map/all_gather | solution.py:149
  7.9 181.3 %all-gather.11.cloned.1.call-start = ((), (), s32[]{:S(2)}) async-start(), calls=%async_computation.5 | async-start | bytes 17825792 | tf_op jit(solution)/shard_map/all_gather | solution.py:152
  8.6 225.9 %all-gather.5.cloned.1.call-start = ((), (), s32[]{:S(2)}) async-start(), calls=%async_computation.2 | async-start | bytes 1114112 | tf_op jit(solution)/shard_map/all_gather | solution.py:162
  9.4 271.2 %all-gather.7.cloned.1.call-start = ((), (), s32[]{:S(2)}) async-start(), calls=%async_computation.3 | async-start | bytes 1114112 | tf_op jit(solution)/shard_map/all_gather | solution.py:163
  10.0 485.6 %reduce-scatter.3.cloned.1.call-start = ((), (), s32[]{:S(2)}) async-start(), calls=%async_computation.6 | async-start | bytes 2228224 | tf_op jit(solution)/shard_map/reduce_scatter | solution.py:192
  357.1 212.2 %reduce-scatter.5.cloned.1.call-start = ((), (), s32[]{:S(2)}) async-start(), calls=%async_computation.7 | async-start | bytes 2228224 | tf_op jit(solution)/shard_map/reduce_scatter | solution.py:193
Sparse Core Ops, SparseCore 0:
  9.6 55.1 all-gather.8
  67.1 122.0 all-gather.10
  191.6 42.9 all-gather.4
  236.8 43.6 all-gather.6
  357.2 138.3 reduce-scatter.2
  499.4 69.8 reduce-scatter.4
where the time goes:
time: 579 us; the launch traced here: 578 us
  waiting for transfers between devices  468 us (81%)
  local copies, waits for them, and re-layouts  33.1 us (6%)
  loops' own time  30.8 us (5%)
  matrix products  24 us (4%)
  between operations  14.2 us (2%)
  other arithmetic  6.96 us (1%)
    reduce_scatter x1, waiting for transfers between devices, local(): lax.psum_scatter(key_terms, 'dp', scatter_dimension=0, tiled=True)  137 us
    all_gather x1, waiting for transfers between devices, local(): lax.all_gather(out_weight, 'dp', axis=1, tiled=True)  124 us
    reduce_scatter x1, waiting for transfers between devices, local(): lax.psum_scatter(value_terms, 'dp', scatter_dimension=0, tiled=True)  72.2 us
    all_gather x1, waiting for transfers between devices, local(): full_grad = lax.all_gather(grad_out, 'tensor', axis=1, tiled=True)  52.3 us
    all_gather x1, waiting for transfers between devices, local(): lax.all_gather(values, 'dp', axis=0, tiled=True)  46 us
    all_gather x1, waiting for transfers between devices, local(): lax.all_gather(keys, 'dp', axis=0, tiled=True)  33.7 us
    another operation x1, loops' own time, query_pass(): return lax.fori_loop(0, total_rows // block_size, query_step, init)  15.3 us
    another operation x1, loops' own time, row_statistics(): lax.fori_loop(0, keys_all.shape[0] // block_size, row_step, init)  15.1 us
  transfers between devices with their start and end apart: 6, of which 6 were waited for; matrix products, arithmetic and copies ran while one was open for 3% of the time, Pallas kernels for 0%

commit v1 on v0

v1 whole, which is shorter than its diff:
```python
import functools
import math

import jax
import jax.numpy as jnp
from jax import lax
from jax.experimental import pallas as pl
from jax.experimental.pallas import tpu as pltpu
from jax.sharding import PartitionSpec as P

HEAD_WIDTH = 128
KEY_BLOCK = 256
MOST = 2560
CHUNKS = 2
MASKED = -1e30
SCALE = 1.0 / math.sqrt(HEAD_WIDTH)
BF16 = jnp.bfloat16
F32 = jnp.float32


def dp_move(value, dx, dz, dc):
    pairs = []
    for x in range(4):
        for z in range(2):
            for c in range(2):
                target = ((x + dx) % 4) * 4 + ((z + dz) % 2) * 2 + (c + dc) % 2
                pairs.append((x * 4 + z * 2 + c, target))
    return lax.ppermute(value, "dp", pairs)


def dot(left, right):
    return lax.dot_general(left, right, (((1,), (0,)), ((), ())), preferred_element_type=F32)


def forward_kernel(
    range_ref, pos_ref, start_ref, q_ref, k_ref, v_ref, probs_ref, out_ref, score, vt
):
    head = pl.program_id(0)
    first = range_ref[0]
    count = range_ref[1]
    rows = q_ref.shape[0]
    query_t = q_ref[...].T
    query_pos = pos_ref[...]
    query_start = start_ref[...]

    @pl.when(head == 0)
    def _():
        def turn(index, _):
            at = pl.multiple_of((first + index) * KEY_BLOCK, KEY_BLOCK)
            vt[:, pl.ds(at, KEY_BLOCK)] = v_ref[pl.ds(at, KEY_BLOCK), :].T
            return 0

        lax.fori_loop(0, count, turn, 0)

    def score_step(index, top):
        at = pl.multiple_of((first + index) * KEY_BLOCK, KEY_BLOCK)
        raw = dot(k_ref[pl.ds(at, KEY_BLOCK), :], query_t)
        key_pos = at + lax.broadcasted_iota(jnp.int32, (KEY_BLOCK, rows), 0)
        live = (key_pos >= query_start) & (key_pos <= query_pos)
        raw = jnp.where(live, raw, MASKED)
        score[pl.ds(at, KEY_BLOCK), :] = raw
        return jnp.maximum(top, jnp.max(raw, axis=0, keepdims=True))

    top = lax.fori_loop(0, count, score_step, jnp.full((1, rows), MASKED, F32))

    def mass_step(index, mass):
        at = pl.multiple_of((first + index) * KEY_BLOCK, KEY_BLOCK)
        weights = jnp.exp((score[pl.ds(at, KEY_BLOCK), :] - top) * SCALE)
        score[pl.ds(at, KEY_BLOCK), :] = weights
        return mass + jnp.sum(weights, axis=0, keepdims=True)

    mass = lax.fori_loop(0, count, mass_step, jnp.zeros((1, rows), F32))
    share = 1.0 / mass

    def probs_step(index, total):
        at = pl.multiple_of((first + index) * KEY_BLOCK, KEY_BLOCK)
        probs = (score[pl.ds(at, KEY_BLOCK), :] * share).astype(BF16)
        probs_ref[pl.ds(at, KEY_BLOCK), :] = probs
        return total + dot(vt[:, pl.ds(at, KEY_BLOCK)], probs)

    out_ref[...] = lax.fori_loop(0, count, probs_step, jnp.zeros((HEAD_WIDTH, rows), F32))


def forward(live_range, query_pos, query_start, queries, keys_all, values_all):
    rows, width = queries.shape
    heads = width // HEAD_WIDTH
    total = keys_all.shape[0]
    whole = pl.BlockSpec((total, HEAD_WIDTH), lambda h, r: (0, 0))
    line = pl.BlockSpec((1, rows), lambda h, r: (0, 0))
    return pl.pallas_call(
        forward_kernel,
        grid_spec=pltpu.PrefetchScalarGridSpec(
            num_scalar_prefetch=1,
            grid=(heads,),
            in_specs=[line, line, pl.BlockSpec((rows, HEAD_WIDTH), lambda h, r: (0, h)), whole, whole],
            out_specs=[
                pl.BlockSpec((total, rows), lambda h, r: (0, h)),
                pl.BlockSpec((HEAD_WIDTH, rows), lambda h, r: (0, h)),
            ],
            scratch_shapes=[
                pltpu.VMEM((total, rows), F32),
                pltpu.VMEM((HEAD_WIDTH, total), BF16),
            ],
        ),
        out_shape=[
            jax.ShapeDtypeStruct((total, heads * rows), BF16),
            jax.ShapeDtypeStruct((HEAD_WIDTH, heads * rows), F32),
        ],
        compiler_params=pltpu.CompilerParams(vmem_limit_bytes=40 * 2**20),
        cost_estimate=pl.CostEstimate(
            flops=6 * rows * heads * 1024 * HEAD_WIDTH * 8, bytes_accessed=20 * 2**20, transcendentals=0
        ),
        name="forward",
    )(live_range, query_pos, query_start, queries, keys_all, values_all)


def backward_kernel(
    heads, range_ref, probs_ref, out_ref, grad_ref, q_ref, k_ref, v_ref, *rest
):
    if len(rest) == 8:
        old_k_ref, old_v_ref, gq_ref, gk_ref, gv_ref, grad_t, delta, total_q = rest
    else:
        gq_ref, gk_ref, gv_ref, grad_t, delta, total_q = rest
        old_k_ref = old_v_ref = None
    step = pl.program_id(0)
    rows = q_ref.shape[0]

    @pl.when(step == 0)
    def _():
        if old_k_ref is None:
            gk_ref[...] = jnp.zeros_like(gk_ref)
            gv_ref[...] = jnp.zeros_like(gv_ref)
        else:
            gk_ref[...] = old_k_ref[...]
            gv_ref[...] = old_v_ref[...]
        total_q[...] = jnp.zeros_like(total_q)
        for h in range(heads):
            at = h * rows
            turned = grad_ref[:, h * HEAD_WIDTH : (h + 1) * HEAD_WIDTH].T
            grad_t[:, at : at + rows] = turned
            delta[:, at : at + rows] = jnp.sum(
                turned.astype(F32) * out_ref[:, at : at + rows], axis=0, keepdims=True
            )

    @pl.when(step < range_ref[1])
    def _():
        at = pl.multiple_of((range_ref[0] + step) * KEY_BLOCK, KEY_BLOCK)
        values = v_ref[...]
        keys_t = k_ref[...].T
        key_sum = jnp.zeros((KEY_BLOCK, HEAD_WIDTH), F32)
        value_sum = jnp.zeros((KEY_BLOCK, HEAD_WIDTH), F32)
        for h in range(heads):
            cols = slice(h * rows, (h + 1) * rows)
            wide = slice(h * HEAD_WIDTH, (h + 1) * HEAD_WIDTH)
            probs = probs_ref[:, cols]
            dprob = dot(values, grad_t[:, cols])
            dscore = (probs.astype(F32) * (dprob - delta[:, cols])).astype(BF16)
            value_sum = value_sum + dot(probs, grad_ref[:, wide])
            key_sum = key_sum + dot(dscore, q_ref[:, wide])
            total_q[:, cols] += dot(keys_t, dscore)
        gk_ref[pl.ds(at, KEY_BLOCK), :] += key_sum * SCALE
        gv_ref[pl.ds(at, KEY_BLOCK), :] += value_sum

    @pl.when(step == range_ref[1] - 1)
    def _():
        for h in range(heads):
            cols = slice(h * rows, (h + 1) * rows)
            wide = slice(h * HEAD_WIDTH, (h + 1) * HEAD_WIDTH)
            gq_ref[:, wide] = (total_q[:, cols].T * SCALE).astype(BF16)


def backward(live_range, part, parts, probs, outs, grads, queries, keys_all, values_all, sums):
    rows, width = queries.shape
    heads = width // HEAD_WIDTH // parts
    total = keys_all.shape[0]
    steps = (MOST + rows - 2) // KEY_BLOCK + 1

    def block(i, r):
        return r[0] + jnp.minimum(i, r[1] - 1)

    key_spec = pl.BlockSpec((KEY_BLOCK, HEAD_WIDTH), lambda i, r: (block(i, r), 0))
    sum_spec = pl.BlockSpec((total, HEAD_WIDTH), lambda i, r: (0, 0))
    return pl.pallas_call(
        functools.partial(backward_kernel, heads),
        grid_spec=pltpu.PrefetchScalarGridSpec(
            num_scalar_prefetch=1,
            grid=(steps,),
            in_specs=[
                pl.BlockSpec((KEY_BLOCK, heads * rows), lambda i, r: (block(i, r), part)),
                pl.BlockSpec((HEAD_WIDTH, heads * rows), lambda i, r: (0, part)),
                pl.BlockSpec((rows, heads * HEAD_WIDTH), lambda i, r: (0, 0)),
                pl.BlockSpec((rows, heads * HEAD_WIDTH), lambda i, r: (0, part)),
                key_spec,
                key_spec,
            ]
            + [sum_spec] * len(sums),
            out_specs=[
                pl.BlockSpec((rows, heads * HEAD_WIDTH), lambda i, r: (0, 0)),
                sum_spec,
                sum_spec,
            ],
            scratch_shapes=[
                pltpu.VMEM((HEAD_WIDTH, heads * rows), BF16),
                pltpu.VMEM((1, heads * rows), F32),
                pltpu.VMEM((HEAD_WIDTH, heads * rows), F32),
            ],
        ),
        out_shape=[
            jax.ShapeDtypeStruct((rows, heads * HEAD_WIDTH), BF16),
            jax.ShapeDtypeStruct((total, HEAD_WIDTH), F32),
            jax.ShapeDtypeStruct((total, HEAD_WIDTH), F32),
        ],
        compiler_params=pltpu.CompilerParams(vmem_limit_bytes=40 * 2**20),
        cost_estimate=pl.CostEstimate(
            flops=8 * rows * heads * 1024 * HEAD_WIDTH * 4, bytes_accessed=10 * 2**20, transcendentals=0
        ),
        name="backward%d" % part,
    )(live_range, probs, outs, grads, queries, keys_all, values_all, *sums)


def by_core(core, mine_at_zero, mine_at_one):
    return jnp.where(core == 0, mine_at_zero, mine_at_one)


def gather_keys_values(keys, values, core, rank):
    rows = keys.shape[0]
    kept = by_core(core, keys, values)
    got = dp_move(by_core(core, values, keys), 0, 0, 1)
    chip = jnp.concatenate([by_core(core, kept, got), by_core(core, got, kept)], axis=0)
    pair = dp_move(chip, 0, 1, 0)
    x, z = rank // 4, (rank // 2) % 2
    near = jnp.concatenate([jnp.where(z == 0, chip, pair), jnp.where(z == 0, pair, chip)], axis=0)
    left = dp_move(near, 1, 0, 0)
    right = dp_move(near, -1, 0, 0)
    half = near.shape[0] // 2
    far = jnp.concatenate(
        [dp_move(left[:half], 1, 0, 0), dp_move(right[half:], -1, 0, 0)], axis=0
    )
    ring = jnp.stack([near, right, far, left])
    order = (jnp.arange(4, dtype=jnp.int32) - x) % 4
    mine = jnp.concatenate(
        [lax.dynamic_index_in_dim(ring, order[i], 0, keepdims=False) for i in range(4)], axis=0
    )
    other = dp_move(mine, 0, 0, 1)
    return by_core(core, mine, other), by_core(core, other, mine)


def gather_weight(block):
    found = []
    for start, dz in ((block, 0), (dp_move(block, 0, 1, 0), 1)):
        left = dp_move(start, 1, 0, 0)
        right = dp_move(start, -1, 0, 0)
        half = start.shape[0] // 2
        far = jnp.concatenate(
            [dp_move(left[:half], 1, 0, 0), dp_move(right[half:], -1, 0, 0)], axis=0
        )
        found += [(start, 0, dz), (left, 3, dz), (right, 1, dz), (far, 2, dz)]
    return found


def local(queries, keys, values, grad_out, out_weight, lengths):
    rows = queries.shape[0]
    rank = lax.axis_index("dp")
    core = rank % 2
    x, z = rank // 4, (rank // 2) % 2

    query_pos = rank * rows + jnp.arange(rows, dtype=jnp.int32)
    ends = jnp.cumsum(lengths)[:-1]
    query_start = jnp.max(
        jnp.where(ends[None, :] <= query_pos[:, None], ends[None, :], 0), axis=1
    )
    first = query_start[0] // KEY_BLOCK
    last = query_pos[-1] // KEY_BLOCK
    live_range = jnp.stack([first, last - first + 1]).astype(jnp.int32)

    depth = out_weight.shape[1]
    halves = grad_out.reshape(rows, 2, depth)
    mine = lax.dynamic_index_in_dim(halves, core, 1, keepdims=False)
    other = lax.dynamic_index_in_dim(halves, 1 - core, 1, keepdims=False)
    chip_grad = jnp.concatenate([mine, dp_move(other, 0, 0, 1)], axis=0)
    all_grad = lax.all_gather(chip_grad, "tensor", axis=0, tiled=False)

    keys_all, values_all = gather_keys_values(keys, values, core, rank)
    probs, outs = forward(
        live_range, query_pos[None, :], query_start[None, :], queries, keys_all, values_all
    )

    features = out_weight.shape[0] // CHUNKS
    sums = ()
    grad_queries = []
    for part in range(CHUNKS):
        total = jnp.zeros((2 * rows, features), F32)
        for block, dx, dz in gather_weight(out_weight[part * features : (part + 1) * features]):
            source = 2 * ((x + dx) % 4) + (z + dz) % 2
            piece = lax.dynamic_index_in_dim(all_grad, source, 0, keepdims=False)
            total = total + lax.dot_general(
                piece, block, (((1,), (1,)), ((), ())), preferred_element_type=F32
            )
        grads = (total[:rows] + dp_move(total[rows:], 0, 0, 1)).astype(BF16)
        grad_q, *sums = backward(
            live_range, part, CHUNKS, probs, outs, grads, queries, keys_all, values_all, sums
        )
        grad_queries.append(grad_q)
    grad_queries = jnp.concatenate(grad_queries, axis=1)

    key_terms, value_terms = sums
    kept = by_core(core, key_terms, value_terms)
    got = dp_move(by_core(core, value_terms, key_terms), 0, 0, 1)
    chip_terms = (kept + got).astype(BF16).reshape(8, 2 * rows, HEAD_WIDTH)
    groups = [[2 * i + c for i in range(8)] for c in range(2)]
    terms = lax.all_to_all(
        chip_terms, "dp", 0, 0, axis_index_groups=groups, tiled=True
    )
    done = jnp.sum(terms.astype(F32), axis=0).astype(BF16)
    upper, lower = done[:rows], done[rows:]
    kept = by_core(core, upper, lower)
    got = dp_move(by_core(core, lower, upper), 0, 0, 1)
    return grad_queries, by_core(core, kept, got), by_core(core, got, kept)


def solution(mesh):
    return jax.shard_map(
        local,
        mesh=mesh,
        in_specs=(
            P("dp", "tensor"),
            P("dp", "tensor"),
            P("dp", "tensor"),
            P("dp", "tensor"),
            P("tensor", "dp"),
            P(),
        ),
        out_specs=(P("dp", "tensor"), P("dp", "tensor"), P("dp", "tensor")),
        check_vma=False,
    )
```

time: 579 us -> 247 us (0.43)
  waiting for transfers between devices: 468 us -> 46.7 us
  starting transfers between devices: 0.23 us -> 73.2 us
  blocking collectives: 0 us -> 39.8 us
  loops' own time: 30.8 us -> 0 us
  local copies, waits for them, and re-layouts: 33.1 us -> 14.4 us
  Pallas kernels: 0 us -> 16.7 us
  between operations: 14.2 us -> 27.6 us
    all_gather x4 -> x1, waiting for transfers between devices: 256 us -> 0.01 us  [local(): all_grad = lax.all_gather(chip_grad, 'tensor', axis=0, tiled=False)]
    reduce_scatter x2 -> x0, waiting for transfers between devices: 209 us -> none  [the longest x1 137 us: local(): lax.psum_scatter(key_terms, 'dp', scatter_dimension=0, tiled=True)]
    ppermute x0 -> x30, starting transfers between devices: none -> 73.1 us  [dp_move(): return lax.ppermute(value, 'dp', pairs)]
    ppermute x0 -> x30, waiting for transfers between devices: none -> 46.7 us  [dp_move(): return lax.ppermute(value, 'dp', pairs)]
    all_to_all x0 -> x1, blocking collectives: none -> 39.8 us  [local(): lax.all_to_all(chip_terms, 'dp', 0, 0, axis_index_groups=groups, tiled=True)]
    another operation x18 -> x0, loops' own time: 30.8 us -> none  [the longest x1 15.3 us: query_pass(): return lax.fori_loop(0, total_rows // block_size, query_step, init)]
    pallas_call x0 -> x3, Pallas kernels: none -> 16.7 us  [the longest x1 8.9 us: forward(): pl.pallas_call(forward_kernel, grid_spec=pltpu.PrefetchScalarGridSpec(num...]
    slice x48 -> x16, local copies, waits for them, and re-layouts: 27.3 us -> 12.6 us  [the longest x4 4.86 us: gather_weight(): right[half:]]
  transfers between devices with their start and end apart: 6 -> 31, of which waited for: 6 -> 8; matrix products, arithmetic and copies ran while one was open for 3% -> 15% of each run, Pallas kernels for 0% -> 5%
where the time goes in v1:
time: 247 us; the launch traced here: 245 us
  starting transfers between devices  73.2 us (30%)
  waiting for transfers between devices  46.7 us (19%)
  blocking collectives  39.8 us (16%)
  between operations  27.6 us (11%)
  matrix products  19.5 us (8%)
  Pallas kernels  16.7 us (7%)
  local copies, waits for them, and re-layouts  14.4 us (6%)
  other arithmetic  7.54 us (3%)
    ppermute x30, starting transfers between devices, dp_move(): return lax.ppermute(value, 'dp', pairs)  73.1 us
    ppermute x30, waiting for transfers between devices, dp_move(): return lax.ppermute(value, 'dp', pairs)  46.7 us
    all_to_all x1, blocking collectives, local(): lax.all_to_all(chip_terms, 'dp', 0, 0, axis_index_groups=groups, tiled=True)  39.8 us
    dot_general x16, matrix products, local(): lax.dot_general(piece, block, (((1,), (1,)), ((), ())), preferred_element...  19.5 us
    pallas_call x1, Pallas kernels, forward(): pl.pallas_call(forward_kernel, grid_spec=pltpu.PrefetchScalarGridSpec(num...  8.9 us
    pallas_call x2, Pallas kernels, backward(): pl.pallas_call(functools.partial(backward_kernel, heads), grid_spec=pltpu...  7.75 us
  transfers between devices with their start and end apart: 31, of which 8 were waited for; matrix products, arithmetic and copies ran while one was open for 15% of the time, Pallas kernels for 5%

profile of v1, /device:TPU:0, one launch (start us, length us, event | category | flops | bytes accessed | tf_op | source)
XLA Modules:
  0.0 245.5 jit_solution(3941191707007491516)
XLA Ops:
  12.7 4.0 %collective-permute-start.1 = (bf16[512,128]{1,0:T(8,128)(2,1)S(1)}, bf16[512,128]{1,0:T(8,128)(2,1)S(1)}, u32[]{:S(2)}, u32[]{:S(2)}) collective-permute-start(bf16[512,128]{1,0:T(8,128)(2,1)S(1)} %pad_maximum_fusion.5), channel_id=1, source_target_pairs={{0,16},{8,24},{16,0},{24,8},{32,48},{40,56},{48,32},{56,40},{64,80... | collective-permute-start | bytes 393224 | tf_op jit(solution)/shard_map/ppermute | solution.py:28
  16.8 3.8 %collective-permute-done.1 = bf16[512,128]{1,0:T(8,128)(2,1)S(1)} collective-permute-done((bf16[512,128]{1,0:T(8,128)(2,1)S(1)}, bf16[512,128]{1,0:T(8,128)(2,1)S(1)}, u32[]{:S(2)}, u32[]{:S(2)}) %collective-permute-start.1) | collective-permute-done | bytes 131104 | tf_op jit(solution)/shard_map/ppermute | solution.py:28
  20.7 2.8 %collective-permute-start.2 = (bf16[1024,128]{1,0:T(8,128)(2,1)S(1)}, bf16[1024,128]{1,0:T(8,128)(2,1)S(1)}, u32[]{:S(2)}, u32[]{:S(2)}) collective-permute-start(bf16[1024,128]{1,0:T(8,128)(2,1)S(1)} %get-tuple-element.30), channel_id=1, source_target_pairs={{0,96},{8,104},{16,112},{24,120},{32,0},{40,8},{48,16},{56,24},{64... | collective-permute-start | bytes 786440 | tf_op jit(solution)/shard_map/ppermute | solution.py:28
  24.6 3.2 %collective-permute-start.9 = (bf16[512,512]{1,0:T(8,128)(2,1)}, bf16[512,512]{1,0:T(8,128)(2,1)S(1)}, u32[]{:S(2)}, u32[]{:S(2)}) collective-permute-start(bf16[512,512]{1,0:T(8,128)(2,1)} %get-tuple-element.21), channel_id=1, source_target_pairs={{0,96},{8,104},{16,112},{24,120},{32,0},{40,8},{48,16},{56,24},{64... | collective-permute-start | bytes 1572872 | tf_op jit(solution)/shard_map/ppermute | solution.py:28
  27.8 3.2 %collective-permute-start.12 = (bf16[512,512]{1,0:T(8,128)(2,1)}, bf16[512,512]{1,0:T(8,128)(2,1)}, u32[]{:S(2)}, u32[]{:S(2)}) collective-permute-start(bf16[512,512]{1,0:T(8,128)(2,1)} %get-tuple-element.21), channel_id=1, source_target_pairs={{0,16},{8,24},{16,0},{24,8},{32,48},{40,56},{48,32},{56,40},{64,80... | collective-permute-start | bytes 1572872 | tf_op jit(solution)/shard_map/ppermute | solution.py:28
  31.1 3.3 %collective-permute-start.5 = (bf16[512,128]{1,0:T(8,128)(2,1)S(1)}, bf16[512,128]{1,0:T(8,128)(2,1)S(1)}, u32[]{:S(2)}, u32[]{:S(2)}) collective-permute-start(bf16[512,128]{1,0:T(8,128)(2,1)S(1)} %slice.102), channel_id=1, source_target_pairs={{0,96},{8,104},{16,112},{24,120},{32,0},{40,8},{48,16},{56,24},{64... | collective-permute-start | bytes 393224 | tf_op jit(solution)/shard_map/ppermute | solution.py:28
  42.9 3.7 %collective-permute-start.19 = (bf16[512,512]{1,0:T(8,128)(2,1)}, bf16[512,512]{1,0:T(8,128)(2,1)}, u32[]{:S(2)}, u32[]{:S(2)}) collective-permute-start(bf16[512,512]{1,0:T(8,128)(2,1)} %get-tuple-element.22), channel_id=1, source_target_pairs={{0,96},{8,104},{16,112},{24,120},{32,0},{40,8},{48,16},{56,24},{64... | collective-permute-start | bytes 1572872 | tf_op jit(solution)/shard_map/ppermute | solution.py:28
  46.9 3.0 %collective-permute-start.22 = (bf16[512,512]{1,0:T(8,128)(2,1)}, bf16[512,512]{1,0:T(8,128)(2,1)}, u32[]{:S(2)}, u32[]{:S(2)}) collective-permute-start(bf16[512,512]{1,0:T(8,128)(2,1)} %get-tuple-element.22), channel_id=1, source_target_pairs={{0,16},{8,24},{16,0},{24,8},{32,48},{40,56},{48,32},{56,40},{64,80... | collective-permute-start | bytes 1572872 | tf_op jit(solution)/shard_map/ppermute | solution.py:28
  53.9 25.2 %collective-permute-done.12 = bf16[512,512]{1,0:T(8,128)(2,1)} collective-permute-done((bf16[512,512]{1,0:T(8,128)(2,1)}, bf16[512,512]{1,0:T(8,128)(2,1)}, u32[]{:S(2)}, u32[]{:S(2)}) %collective-permute-start.12) | collective-permute-done | bytes 524320 | tf_op jit(solution)/shard_map/ppermute | solution.py:28
  79.0 2.7 %collective-permute-start.14 = (bf16[512,512]{1,0:T(8,128)(2,1)}, bf16[512,512]{1,0:T(8,128)(2,1)S(1)}, u32[]{:S(2)}, u32[]{:S(2)}) collective-permute-start(bf16[512,512]{1,0:T(8,128)(2,1)} %collective-permute-done.12), channel_id=1, source_target_pairs={{0,96},{8,104},{16,112},{24,120},{32,0},{40,8},{48,16},{56,24},{64... | collective-permute-start | bytes 1572872 | tf_op jit(solution)/shard_map/ppermute | solution.py:28
  81.7 8.4 %collective-permute-done.22 = bf16[512,512]{1,0:T(8,128)(2,1)} collective-permute-done((bf16[512,512]{1,0:T(8,128)(2,1)}, bf16[512,512]{1,0:T(8,128)(2,1)}, u32[]{:S(2)}, u32[]{:S(2)}) %collective-permute-start.22) | collective-permute-done | bytes 524320 | tf_op jit(solution)/shard_map/ppermute | solution.py:28
  90.2 2.7 %collective-permute-start.24 = (bf16[512,512]{1,0:T(8,128)(2,1)}, bf16[512,512]{1,0:T(8,128)(2,1)S(1)}, u32[]{:S(2)}, u32[]{:S(2)}) collective-permute-start(bf16[512,512]{1,0:T(8,128)(2,1)} %collective-permute-done.22), channel_id=1, source_target_pairs={{0,96},{8,104},{16,112},{24,120},{32,0},{40,8},{48,16},{56,24},{64... | collective-permute-start | bytes 1572872 | tf_op jit(solution)/shard_map/ppermute | solution.py:28
  101.8 3.2 %collective-permute-start.11 = (bf16[256,512]{1,0:T(8,128)(2,1)}, bf16[256,512]{1,0:T(8,128)(2,1)}, u32[]{:S(2)}, u32[]{:S(2)}) collective-permute-start(bf16[256,512]{1,0:T(8,128)(2,1)} %slice.104), channel_id=1, source_target_pairs={{0,96},{8,104},{16,112},{24,120},{32,0},{40,8},{48,16},{56,24},{64... | collective-permute-start | bytes 786440 | tf_op jit(solution)/shard_map/ppermute | solution.py:28
  107.4 3.2 %collective-permute-start.21 = (bf16[256,512]{1,0:T(8,128)(2,1)}, bf16[256,512]{1,0:T(8,128)(2,1)S(1)}, u32[]{:S(2)}, u32[]{:S(2)}) collective-permute-start(bf16[256,512]{1,0:T(8,128)(2,1)} %slice.110), channel_id=1, source_target_pairs={{0,96},{8,104},{16,112},{24,120},{32,0},{40,8},{48,16},{56,24},{64... | collective-permute-start | bytes 786440 | tf_op jit(solution)/shard_map/ppermute | solution.py:28
  113.1 3.5 %collective-permute-start.16 = (bf16[256,512]{1,0:T(8,128)(2,1)}, bf16[256,512]{1,0:T(8,128)(2,1)}, u32[]{:S(2)}, u32[]{:S(2)}) collective-permute-start(bf16[256,512]{1,0:T(8,128)(2,1)} %slice.106), channel_id=1, source_target_pairs={{0,96},{8,104},{16,112},{24,120},{32,0},{40,8},{48,16},{56,24},{64... | collective-permute-start | bytes 786440 | tf_op jit(solution)/shard_map/ppermute | solution.py:28
  118.2 8.9 %forward.1 = (bf16[4096,2048]{1,0:T(8,128)(2,1)}, f32[128,2048]{1,0:T(8,128)S(1)}) custom-call(s32[2]{0:T(128)S(1)} %pad_add_fusion.range_ref, s32[1,256]{1,0:T(1,128)S(1)} %iota_add_fusion.pos_ref, s32[1,256]{1,0:T(1,128)S(1)} %bitcast.81, bf16[256,1024]{1,0:T(8,128)(2,1)S(1)} %copy-done, bf16[4096,128]{1,0:T(8,128)(2,1)S(1)} %get-tuple-element.20.k_ref, ...), custom_call_target="tpu_custom_call" | custom-call | flops 12884901888 | bytes 20971520 | tf_op jit(solution)/shard_map/forward/pallas_call | solution.py:90
  127.1 1.8 fusion.44
  133.7 29.1 %collective-permute-start.26 = (bf16[256,512]{1,0:T(8,128)(2,1)S(1)}, bf16[256,512]{1,0:T(8,128)(2,1)S(1)}, u32[]{:S(2)}, u32[]{:S(2)}) collective-permute-start(bf16[256,512]{1,0:T(8,128)(2,1)S(1)} %copy-done.16), channel_id=1, source_target_pairs={{0,96},{8,104},{16,112},{24,120},{32,0},{40,8},{48,16},{56,24},{64... | collective-permute-start | bytes 786440 | tf_op jit(solution)/shard_map/ppermute | solution.py:28
  166.0 2.7 %collective-permute-done.15 = bf16[256,512]{1,0:T(8,128)(2,1)S(1)} collective-permute-done((bf16[256,512]{1,0:T(8,128)(2,1)S(1)}, bf16[256,512]{1,0:T(8,128)(2,1)S(1)}, u32[]{:S(2)}, u32[]{:S(2)}) %collective-permute-start.15) | collective-permute-done | bytes 262176 | tf_op jit(solution)/shard_map/ppermute | solution.py:28
  181.2 3.9 %backward0.1 = (bf16[256,512]{1,0:T(8,128)(2,1)S(1)}, f32[4096,128]{1,0:T(8,128)S(1)}, f32[4096,128]{1,0:T(8,128)S(1)}) custom-call(s32[2]{0:T(128)S(1)} %pad_add_fusion.range_ref, bf16[4096,2048]{1,0:T(8,128)(2,1)} %get-tuple-element.11.probs_ref, f32[128,2048]{1,0:T(8,128)S(1)} %get-tuple-element.12.out_ref, bf16[256,512]{1,0:T(8,128)(2,1)S(1)} %fusion.9.grad_ref, ...), custom_call_target="tpu_custom_call" | custom-call | flops 4294967296 | bytes 10485760 | tf_op jit(solution)/shard_map/backward0/pallas_call | solution.py:183
  185.2 3.9 %backward1.1 = (bf16[256,512]{1,0:T(8,128)(2,1)S(1)}, f32[4096,128]{1,0:T(8,128)S(1)}, f32[4096,128]{1,0:T(8,128)S(1)}) custom-call(s32[2]{0:T(128)S(1)} %pad_add_fusion.range_ref, bf16[4096,2048]{1,0:T(8,128)(2,1)} %get-tuple-element.11.probs_ref, f32[128,2048]{1,0:T(8,128)S(1)} %get-tuple-element.12.out_ref, bf16[256,512]{1,0:T(8,128)(2,1)S(1)} %fusion.8.grad_ref, ...), custom_call_target="tpu_custom_call" | custom-call | flops 4294967296 | bytes 10485760 | tf_op jit(solution)/shard_map/backward1/pallas_call | solution.py:183
  189.4 2.6 %collective-permute-start.28 = (f32[4096,128]{1,0:T(8,128)S(1)}, f32[4096,128]{1,0:T(8,128)S(1)}, u32[]{:S(2)}, u32[]{:S(2)}) collective-permute-start(f32[4096,128]{1,0:T(8,128)S(1)} %broadcast_select_fusion), channel_id=1, source_target_pairs={{0,8},{8,0},{16,24},{24,16},{32,40},{40,32},{48,56},{56,48},{64,72... | collective-permute-start | bytes 6291464 | tf_op jit(solution)/shard_map/ppermute | solution.py:28
  192.0 3.8 %collective-permute-done.28 = f32[4096,128]{1,0:T(8,128)S(1)} collective-permute-done((f32[4096,128]{1,0:T(8,128)S(1)}, f32[4096,128]{1,0:T(8,128)S(1)}, u32[]{:S(2)}, u32[]{:S(2)}) %collective-permute-start.28) | collective-permute-done | bytes 2097184 | tf_op jit(solution)/shard_map/ppermute | solution.py:28
  196.1 39.8 %all_to_all.5 = bf16[8,512,128]{2,1,0:T(8,128)(2,1)S(1)} all-to-all(bf16[8,512,128]{2,1,0:T(8,128)(2,1)S(1)} %bitcast.98), channel_id=1, replica_groups={{0,16,32,48,64,80,96,112},{8,24,40,56,72,88,104,120},{1,17,33,49,65,81,..., dimensions={0} | all-to-all | bytes 2097152 | tf_op jit(solution)/shard_map/all_to_all | solution.py:311
  (145 shorter events, 45.3 us)
Async XLA Ops:
  7.2 119.9 %all-gather.3.cloned.1.call-start = ((), (), s32[]{:S(2)}) async-start(), calls=%async_computation.1 | async-start | bytes 4718592 | tf_op jit(solution)/shard_map/all_gather | solution.py:281
  20.7 10.4 %collective-permute-start.2 = (bf16[1024,128]{1,0:T(8,128)(2,1)S(1)}, bf16[1024,128]{1,0:T(8,128)(2,1)S(1)}, u32[]{:S(2)}, u32[]{:S(2)}) collective-permute-start(bf16[1024,128]{1,0:T(8,128)(2,1)S(1)} %get-tuple-element.30), channel_id=1, source_target_pairs={{0,96},{8,104},{16,112},{24,120},{32,0},{40,8},{48,16},{56,24},{64... | collective-permute-start | bytes 786440 | tf_op jit(solution)/shard_map/ppermute | solution.py:28
  23.5 10.9 %collective-permute-start.3 = (bf16[1024,128]{1,0:T(8,128)(2,1)S(1)}, bf16[1024,128]{1,0:T(8,128)(2,1)S(1)}, u32[]{:S(2)}, u32[]{:S(2)}) collective-permute-start(bf16[1024,128]{1,0:T(8,128)(2,1)S(1)} %get-tuple-element.30), channel_id=1, source_target_pairs={{0,32},{8,40},{16,48},{24,56},{32,64},{40,72},{48,80},{56,88},{64,... | collective-permute-start | bytes 786440 | tf_op jit(solution)/shard_map/ppermute | solution.py:28
  24.6 22.3 %collective-permute-start.9 = (bf16[512,512]{1,0:T(8,128)(2,1)}, bf16[512,512]{1,0:T(8,128)(2,1)S(1)}, u32[]{:S(2)}, u32[]{:S(2)}) collective-permute-start(bf16[512,512]{1,0:T(8,128)(2,1)} %get-tuple-element.21), channel_id=1, source_target_pairs={{0,96},{8,104},{16,112},{24,120},{32,0},{40,8},{48,16},{56,24},{64... | collective-permute-start | bytes 1572872 | tf_op jit(solution)/shard_map/ppermute | solution.py:28
  27.8 23.2 %collective-permute-start.8 = (bf16[512,512]{1,0:T(8,128)(2,1)}, bf16[512,512]{1,0:T(8,128)(2,1)S(1)}, u32[]{:S(2)}, u32[]{:S(2)}) collective-permute-start(bf16[512,512]{1,0:T(8,128)(2,1)} %get-tuple-element.21), channel_id=1, source_target_pairs={{0,32},{8,40},{16,48},{24,56},{32,64},{40,72},{48,80},{56,88},{64,... | collective-permute-start | bytes 1572872 | tf_op jit(solution)/shard_map/ppermute | solution.py:28
  27.8 51.2 %collective-permute-start.12 = (bf16[512,512]{1,0:T(8,128)(2,1)}, bf16[512,512]{1,0:T(8,128)(2,1)}, u32[]{:S(2)}, u32[]{:S(2)}) collective-permute-start(bf16[512,512]{1,0:T(8,128)(2,1)} %get-tuple-element.21), channel_id=1, source_target_pairs={{0,16},{8,24},{16,0},{24,8},{32,48},{40,56},{48,32},{56,40},{64,80... | collective-permute-start | bytes 1572872 | tf_op jit(solution)/shard_map/ppermute | solution.py:28
  31.1 11.9 %collective-permute-start.5 = (bf16[512,128]{1,0:T(8,128)(2,1)S(1)}, bf16[512,128]{1,0:T(8,128)(2,1)S(1)}, u32[]{:S(2)}, u32[]{:S(2)}) collective-permute-start(bf16[512,128]{1,0:T(8,128)(2,1)S(1)} %slice.102), channel_id=1, source_target_pairs={{0,96},{8,104},{16,112},{24,120},{32,0},{40,8},{48,16},{56,24},{64... | collective-permute-start | bytes 393224 | tf_op jit(solution)/shard_map/ppermute | solution.py:28
  34.4 12.2 %collective-permute-start.4 = (bf16[512,128]{1,0:T(8,128)(2,1)S(1)}, bf16[512,128]{1,0:T(8,128)(2,1)S(1)}, u32[]{:S(2)}, u32[]{:S(2)}) collective-permute-start(bf16[512,128]{1,0:T(8,128)(2,1)S(1)} %slice.101), channel_id=1, source_target_pairs={{0,32},{8,40},{16,48},{24,56},{32,64},{40,72},{48,80},{56,88},{64,... | collective-permute-start | bytes 393224 | tf_op jit(solution)/shard_map/ppermute | solution.py:28
  42.9 38.8 %collective-permute-start.19 = (bf16[512,512]{1,0:T(8,128)(2,1)}, bf16[512,512]{1,0:T(8,128)(2,1)}, u32[]{:S(2)}, u32[]{:S(2)}) collective-permute-start(bf16[512,512]{1,0:T(8,128)(2,1)} %get-tuple-element.22), channel_id=1, source_target_pairs={{0,96},{8,104},{16,112},{24,120},{32,0},{40,8},{48,16},{56,24},{64... | collective-permute-start | bytes 1572872 | tf_op jit(solution)/shard_map/ppermute | solution.py:28
  46.6 46.2 %collective-permute-start.18 = (bf16[512,512]{1,0:T(8,128)(2,1)}, bf16[512,512]{1,0:T(8,128)(2,1)S(1)}, u32[]{:S(2)}, u32[]{:S(2)}) collective-permute-start(bf16[512,512]{1,0:T(8,128)(2,1)} %get-tuple-element.22), channel_id=1, source_target_pairs={{0,32},{8,40},{16,48},{24,56},{32,64},{40,72},{48,80},{56,88},{64,... | collective-permute-start | bytes 1572872 | tf_op jit(solution)/shard_map/ppermute | solution.py:28
  46.9 43.2 %collective-permute-start.22 = (bf16[512,512]{1,0:T(8,128)(2,1)}, bf16[512,512]{1,0:T(8,128)(2,1)}, u32[]{:S(2)}, u32[]{:S(2)}) collective-permute-start(bf16[512,512]{1,0:T(8,128)(2,1)} %get-tuple-element.22), channel_id=1, source_target_pairs={{0,16},{8,24},{16,0},{24,8},{32,48},{40,56},{48,32},{56,40},{64,80... | collective-permute-start | bytes 1572872 | tf_op jit(solution)/shard_map/ppermute | solution.py:28
  51.0 62.0 %collective-permute-start.6 = (bf16[4096,128]{1,0:T(8,128)(2,1)}, bf16[4096,128]{1,0:T(8,128)(2,1)}, u32[]{:S(2)}, u32[]{:S(2)}) collective-permute-start(bf16[4096,128]{1,0:T(8,128)(2,1)} %pad_maximum_fusion.1), channel_id=1, source_target_pairs={{0,8},{8,0},{16,24},{24,16},{32,40},{40,32},{48,56},{56,48},{64,72... | collective-permute-start | bytes 3145736 | tf_op jit(solution)/shard_map/ppermute | solution.py:28
  79.0 22.8 %collective-permute-start.14 = (bf16[512,512]{1,0:T(8,128)(2,1)}, bf16[512,512]{1,0:T(8,128)(2,1)S(1)}, u32[]{:S(2)}, u32[]{:S(2)}) collective-permute-start(bf16[512,512]{1,0:T(8,128)(2,1)} %collective-permute-done.12), channel_id=1, source_target_pairs={{0,96},{8,104},{16,112},{24,120},{32,0},{40,8},{48,16},{56,24},{64... | collective-permute-start | bytes 1572872 | tf_op jit(solution)/shard_map/ppermute | solution.py:28
  81.7 24.0 %collective-permute-start.13 = (bf16[512,512]{1,0:T(8,128)(2,1)}, bf16[512,512]{1,0:T(8,128)(2,1)}, u32[]{:S(2)}, u32[]{:S(2)}) collective-permute-start(bf16[512,512]{1,0:T(8,128)(2,1)} %collective-permute-done.12), channel_id=1, source_target_pairs={{0,32},{8,40},{16,48},{24,56},{32,64},{40,72},{48,80},{56,88},{64,... | collective-permute-start | bytes 1572872 | tf_op jit(solution)/shard_map/ppermute | solution.py:28
  90.2 17.2 %collective-permute-start.24 = (bf16[512,512]{1,0:T(8,128)(2,1)}, bf16[512,512]{1,0:T(8,128)(2,1)S(1)}, u32[]{:S(2)}, u32[]{:S(2)}) collective-permute-start(bf16[512,512]{1,0:T(8,128)(2,1)} %collective-permute-done.22), channel_id=1, source_target_pairs={{0,96},{8,104},{16,112},{24,120},{32,0},{40,8},{48,16},{56,24},{64... | collective-permute-start | bytes 1572872 | tf_op jit(solution)/shard_map/ppermute | solution.py:28
  92.8 18.5 %collective-permute-start.23 = (bf16[512,512]{1,0:T(8,128)(2,1)}, bf16[512,512]{1,0:T(8,128)(2,1)}, u32[]{:S(2)}, u32[]{:S(2)}) collective-permute-start(bf16[512,512]{1,0:T(8,128)(2,1)} %collective-permute-done.22), channel_id=1, source_target_pairs={{0,32},{8,40},{16,48},{24,56},{32,64},{40,72},{48,80},{56,88},{64,... | collective-permute-start | bytes 1572872 | tf_op jit(solution)/shard_map/ppermute | solution.py:28
  101.8 30.9 %collective-permute-start.11 = (bf16[256,512]{1,0:T(8,128)(2,1)}, bf16[256,512]{1,0:T(8,128)(2,1)}, u32[]{:S(2)}, u32[]{:S(2)}) collective-permute-start(bf16[256,512]{1,0:T(8,128)(2,1)} %slice.104), channel_id=1, source_target_pairs={{0,96},{8,104},{16,112},{24,120},{32,0},{40,8},{48,16},{56,24},{64... | collective-permute-start | bytes 786440 | tf_op jit(solution)/shard_map/ppermute | solution.py:28
  105.7 28.1 %collective-permute-start.10 = (bf16[256,512]{1,0:T(8,128)(2,1)}, bf16[256,512]{1,0:T(8,128)(2,1)}, u32[]{:S(2)}, u32[]{:S(2)}) collective-permute-start(bf16[256,512]{1,0:T(8,128)(2,1)} %slice.103), channel_id=1, source_target_pairs={{0,32},{8,40},{16,48},{24,56},{32,64},{40,72},{48,80},{56,88},{64,... | collective-permute-start | bytes 786440 | tf_op jit(solution)/shard_map/ppermute | solution.py:28
  107.4 68.0 %collective-permute-start.21 = (bf16[256,512]{1,0:T(8,128)(2,1)}, bf16[256,512]{1,0:T(8,128)(2,1)S(1)}, u32[]{:S(2)}, u32[]{:S(2)}) collective-permute-start(bf16[256,512]{1,0:T(8,128)(2,1)} %slice.110), channel_id=1, source_target_pairs={{0,96},{8,104},{16,112},{24,120},{32,0},{40,8},{48,16},{56,24},{64... | collective-permute-start | bytes 786440 | tf_op jit(solution)/shard_map/ppermute | solution.py:28
  111.3 64.0 %collective-permute-start.20 = (bf16[256,512]{1,0:T(8,128)(2,1)}, bf16[256,512]{1,0:T(8,128)(2,1)}, u32[]{:S(2)}, u32[]{:S(2)}) collective-permute-start(bf16[256,512]{1,0:T(8,128)(2,1)} %slice.109), channel_id=1, source_target_pairs={{0,32},{8,40},{16,48},{24,56},{32,64},{40,72},{48,80},{56,88},{64,... | collective-permute-start | bytes 786440 | tf_op jit(solution)/shard_map/ppermute | solution.py:28
  113.1 52.8 %collective-permute-start.16 = (bf16[256,512]{1,0:T(8,128)(2,1)}, bf16[256,512]{1,0:T(8,128)(2,1)}, u32[]{:S(2)}, u32[]{:S(2)}) collective-permute-start(bf16[256,512]{1,0:T(8,128)(2,1)} %slice.106), channel_id=1, source_target_pairs={{0,96},{8,104},{16,112},{24,120},{32,0},{40,8},{48,16},{56,24},{64... | collective-permute-start | bytes 786440 | tf_op jit(solution)/shard_map/ppermute | solution.py:28
  132.8 35.9 %collective-permute-start.15 = (bf16[256,512]{1,0:T(8,128)(2,1)S(1)}, bf16[256,512]{1,0:T(8,128)(2,1)S(1)}, u32[]{:S(2)}, u32[]{:S(2)}) collective-permute-start(bf16[256,512]{1,0:T(8,128)(2,1)S(1)} %copy-done.18), channel_id=1, source_target_pairs={{0,32},{8,40},{16,48},{24,56},{32,64},{40,72},{48,80},{56,88},{64,... | collective-permute-start | bytes 786440 | tf_op jit(solution)/shard_map/ppermute | solution.py:28
  133.7 45.2 %collective-permute-start.26 = (bf16[256,512]{1,0:T(8,128)(2,1)S(1)}, bf16[256,512]{1,0:T(8,128)(2,1)S(1)}, u32[]{:S(2)}, u32[]{:S(2)}) collective-permute-start(bf16[256,512]{1,0:T(8,128)(2,1)S(1)} %copy-done.16), channel_id=1, source_target_pairs={{0,96},{8,104},{16,112},{24,120},{32,0},{40,8},{48,16},{56,24},{64... | collective-permute-start | bytes 786440 | tf_op jit(solution)/shard_map/ppermute | solution.py:28
  165.9 13.0 %collective-permute-start.25 = (bf16[256,512]{1,0:T(8,128)(2,1)S(1)}, bf16[256,512]{1,0:T(8,128)(2,1)S(1)}, u32[]{:S(2)}, u32[]{:S(2)}) collective-permute-start(bf16[256,512]{1,0:T(8,128)(2,1)S(1)} %copy-done.17), channel_id=1, source_target_pairs={{0,32},{8,40},{16,48},{24,56},{32,64},{40,72},{48,80},{56,88},{64,... | collective-permute-start | bytes 786440 | tf_op jit(solution)/shard_map/ppermute | solution.py:28
  (27 other events, 346.2 us)
Sparse Core Ops, SparseCore 0:
  11.4 55.2 all-gather.2

commit v2 on v1

v2 whole, which is shorter than its diff:
```python
import functools
import math

import jax
import jax.numpy as jnp
from jax import lax
from jax.experimental import pallas as pl
from jax.experimental.pallas import tpu as pltpu
from jax.sharding import PartitionSpec as P

HEAD_WIDTH = 128
KEY_BLOCK = 256
MOST = 2560
CHUNKS = 2
PIECES = 4
MASKED = -1e30
SCALE = 1.0 / math.sqrt(HEAD_WIDTH)
LOG2E = 1.0 / math.log(2.0)
BF16 = jnp.bfloat16
F32 = jnp.float32
VMEM_LIMIT = 48 * 2**20

FIRST, COUNT, CLEAR, CORE, TABLE = 0, 1, 2, 3, 4


def dp_move(value, dx, dz, dc):
    pairs = []
    for x in range(4):
        for z in range(2):
            for c in range(2):
                target = ((x + dx) % 4) * 4 + ((z + dz) % 2) * 2 + (c + dc) % 2
                pairs.append((x * 4 + z * 2 + c, target))
    return lax.ppermute(value, "dp", pairs)


def after(value, *others):
    return lax.optimization_barrier((value, *others))[0]


def dot(left, right):
    return lax.dot_general(left, right, (((1,), (0,)), ((), ())), preferred_element_type=F32)


def dot_t(left, right):
    return lax.dot_general(left, right, (((1,), (1,)), ((), ())), preferred_element_type=F32)


def block_rows(index):
    return pl.ds(pl.multiple_of(index * KEY_BLOCK, KEY_BLOCK), KEY_BLOCK)


def forward_kernel(info, pos_ref, start_ref, q_ref, kv_ref, probs_ref, out_ref, score, vt):
    first, count = info[FIRST], info[COUNT]
    rows = q_ref.shape[0]
    query_t = q_ref[...].T

    @pl.when(pl.program_id(0) == 0)
    def _():
        def turn(index, _):
            source = info[TABLE + 16 + first + index]
            vt[:, block_rows(index)] = kv_ref[block_rows(source), :].T
            return 0

        lax.fori_loop(0, count, turn, 0)

    def product(index):
        return dot(kv_ref[block_rows(info[TABLE + first + index]), :], query_t)

    def masked_step(index, top):
        key_pos = (first + index) * KEY_BLOCK + lax.broadcasted_iota(jnp.int32, (KEY_BLOCK, rows), 0)
        live = (key_pos >= start_ref[...]) & (key_pos <= pos_ref[...])
        raw = jnp.where(live, product(index), MASKED)
        score[block_rows(index), :] = raw
        return jnp.maximum(top, jnp.max(raw, axis=0, keepdims=True))

    def clear_step(index, top):
        raw = product(index)
        score[block_rows(index), :] = raw
        return jnp.maximum(top, jnp.max(raw, axis=0, keepdims=True))

    clear = jnp.minimum(info[CLEAR] - first, count - 1)
    top = jnp.full((1, rows), MASKED, F32)
    top = lax.fori_loop(0, clear, masked_step, top)
    top = lax.fori_loop(clear, count - 1, clear_step, top)
    top = masked_step(count - 1, top)

    def mass_step(index, mass):
        weights = jnp.exp2((score[block_rows(index), :] - top) * (SCALE * LOG2E))
        score[block_rows(index), :] = weights
        return mass + jnp.sum(weights, axis=0, keepdims=True)

    mass = lax.fori_loop(0, count, mass_step, jnp.zeros((1, rows), F32))
    share = 1.0 / mass

    def probs_step(index, total):
        probs = (score[block_rows(index), :] * share).astype(BF16)
        probs_ref[block_rows(index), :] = probs
        return total + dot(vt[:, block_rows(index)], probs)

    out_ref[...] = lax.fori_loop(0, count, probs_step, jnp.zeros((HEAD_WIDTH, rows), F32))


def most_blocks(rows):
    return (MOST + rows - 2) // KEY_BLOCK + 1


def forward(part, info, query_pos, query_start, queries, kv):
    rows, width = queries.shape
    heads = width // HEAD_WIDTH // CHUNKS
    live = most_blocks(rows) * KEY_BLOCK
    line = pl.BlockSpec((1, rows), lambda h, r: (0, 0))
    return pl.pallas_call(
        forward_kernel,
        grid_spec=pltpu.PrefetchScalarGridSpec(
            num_scalar_prefetch=1,
            grid=(heads,),
            in_specs=[
                line,
                line,
                pl.BlockSpec((rows, HEAD_WIDTH), lambda h, r: (0, part * heads + h)),
                pl.BlockSpec(kv.shape, lambda h, r: (0, 0)),
            ],
            out_specs=[
                pl.BlockSpec((live, rows), lambda h, r: (0, h)),
                pl.BlockSpec((HEAD_WIDTH, rows), lambda h, r: (0, h)),
            ],
            scratch_shapes=[
                pltpu.VMEM((live, rows), F32),
                pltpu.VMEM((HEAD_WIDTH, live), BF16),
            ],
        ),
        out_shape=[
            jax.ShapeDtypeStruct((live, heads * rows), BF16),
            jax.ShapeDtypeStruct((HEAD_WIDTH, heads * rows), F32),
        ],
        compiler_params=pltpu.CompilerParams(vmem_limit_bytes=VMEM_LIMIT),
        cost_estimate=pl.CostEstimate(
            flops=16 * 10**9, bytes_accessed=10 * 2**20, transcendentals=0
        ),
        name="forward%d" % part,
    )(info, query_pos, query_start, queries, kv)


def backward_kernel(heads, part, info, probs_ref, out_ref, grad_ref, q_ref, k_ref, v_ref, *rest):
    if part:
        old_own, old_other, _, gq_ref, own_ref, other_ref, grad_t, delta, total_q, other = rest
    else:
        gq_ref, own_ref, other_ref, grad_t, delta, total_q = rest
        other = other_ref
    step = pl.program_id(0)
    count = info[COUNT]
    rows = q_ref.shape[0]

    @pl.when(step == 0)
    def _():
        if part:
            own_ref[...] = old_own[...]
            other[...] = old_other[...]
        else:
            own_ref[...] = jnp.zeros_like(own_ref)
            other[...] = jnp.zeros_like(other)
        total_q[...] = jnp.zeros_like(total_q)
        for h in range(heads):
            cols = slice(h * rows, (h + 1) * rows)
            turned = grad_ref[:, h * HEAD_WIDTH : (h + 1) * HEAD_WIDTH].T
            grad_t[:, cols] = turned
            delta[:, cols] = jnp.sum(turned.astype(F32) * out_ref[:, cols], axis=0, keepdims=True)

    @pl.when(step < count)
    def _():
        block = info[FIRST] + step
        values = v_ref[...]
        keys_t = k_ref[...].T
        key_sum = jnp.zeros((KEY_BLOCK, HEAD_WIDTH), F32)
        value_sum = jnp.zeros((KEY_BLOCK, HEAD_WIDTH), F32)
        for h in range(heads):
            cols = slice(h * rows, (h + 1) * rows)
            wide = slice(h * HEAD_WIDTH, (h + 1) * HEAD_WIDTH)
            probs = probs_ref[:, cols]
            dprob = dot(values, grad_t[:, cols])
            dscore = (probs.astype(F32) * (dprob - delta[:, cols])).astype(BF16)
            value_sum = value_sum + dot(probs, grad_ref[:, wide])
            key_sum = key_sum + dot(dscore, q_ref[:, wide])
            total_q[:, cols] += dot(keys_t, dscore)

        def add(ref):
            ref[block // 2, :, :HEAD_WIDTH] += key_sum * SCALE
            ref[block // 2, :, HEAD_WIDTH:] += value_sum

        pl.when(block % 2 == info[CORE])(lambda: add(own_ref))
        pl.when(block % 2 != info[CORE])(lambda: add(other))

    @pl.when(step == count - 1)
    def _():
        for h in range(heads):
            cols = slice(h * rows, (h + 1) * rows)
            wide = slice(h * HEAD_WIDTH, (h + 1) * HEAD_WIDTH)
            gq_ref[:, wide] = (total_q[:, cols].T * SCALE).astype(BF16)
        if part:
            other_ref[...] = other[...].astype(BF16)


def backward(part, info, probs, outs, grads, queries, kv, carried):
    rows, width = queries.shape
    heads = width // HEAD_WIDTH // CHUNKS
    last = part == CHUNKS - 1
    sums = (8, KEY_BLOCK, 2 * HEAD_WIDTH)

    def near(i, r):
        return jnp.minimum(i, r[COUNT] - 1)

    sum_spec = pl.BlockSpec(sums, lambda i, r: (0, 0, 0))
    gq_spec = pl.BlockSpec((rows, heads * HEAD_WIDTH), lambda i, r: (0, part))
    scratch = [
        pltpu.VMEM((HEAD_WIDTH, heads * rows), BF16),
        pltpu.VMEM((1, heads * rows), F32),
        pltpu.VMEM((HEAD_WIDTH, heads * rows), F32),
    ]
    in_specs = [
        pl.BlockSpec((KEY_BLOCK, heads * rows), lambda i, r: (near(i, r), 0)),
        pl.BlockSpec((HEAD_WIDTH, heads * rows), lambda i, r: (0, 0)),
        pl.BlockSpec((rows, heads * HEAD_WIDTH), lambda i, r: (0, 0)),
        pl.BlockSpec((rows, heads * HEAD_WIDTH), lambda i, r: (0, part)),
        pl.BlockSpec((KEY_BLOCK, HEAD_WIDTH), lambda i, r: (r[TABLE + r[FIRST] + near(i, r)], 0)),
        pl.BlockSpec(
            (KEY_BLOCK, HEAD_WIDTH), lambda i, r: (r[TABLE + 16 + r[FIRST] + near(i, r)], 0)
        ),
    ]
    aliases = {}
    if part:
        in_specs += [sum_spec, sum_spec, pl.BlockSpec(memory_space=pl.ANY)]
        scratch.append(pltpu.VMEM(sums, F32))
        aliases = {9: 0}
    return pl.pallas_call(
        functools.partial(backward_kernel, heads, part),
        grid_spec=pltpu.PrefetchScalarGridSpec(
            num_scalar_prefetch=1,
            grid=(most_blocks(rows),),
            in_specs=in_specs,
            out_specs=[gq_spec, sum_spec, sum_spec],
            scratch_shapes=scratch,
        ),
        out_shape=[
            jax.ShapeDtypeStruct((rows, width), BF16),
            jax.ShapeDtypeStruct(sums, F32),
            jax.ShapeDtypeStruct(sums, BF16 if last else F32),
        ],
        input_output_aliases=aliases,
        compiler_params=pltpu.CompilerParams(vmem_limit_bytes=VMEM_LIMIT),
        cost_estimate=pl.CostEstimate(
            flops=8 * 10**9, bytes_accessed=10 * 2**20, transcendentals=0
        ),
        name="backward%d" % part,
    )(info, probs, outs, grads, queries, kv, kv, *carried)


def project_kernel(pieces, source, grad_ref, *rest):
    weights, (own_ref, other_ref, grad, weight, grad_sem, weight_sem) = rest[:-6], rest[-6:]
    chips = len(weights) // pieces
    part_rows = weights[0].shape[0]
    copies = []
    for i in range(chips):
        one = [pltpu.make_async_copy(grad_ref.at[source[i]], grad.at[i], grad_sem.at[i])]
        for j in range(pieces):
            k = i * pieces + j
            rows = pl.ds(j * part_rows, part_rows)
            one.append(pltpu.make_async_copy(weights[k], weight.at[i, rows], weight_sem.at[k]))
        for copy in one:
            copy.start()
        copies.append(one)
    half = own_ref.shape[0]
    for i in range(chips):
        for copy in copies[i]:
            copy.wait()
        for ref, at in ((own_ref, 0), (other_ref, half)):
            term = dot_t(grad[i, at : at + half, :], weight[i])
            if i == 0:
                ref[...] = term
            else:
                ref[...] += term


def project(part, source, all_grad, weights):
    chips, tokens, depth = all_grad.shape
    pieces = len(weights[0])
    features = pieces * weights[0][0].shape[0]
    flat = [piece for chip in weights for piece in chip]
    half = jax.ShapeDtypeStruct((tokens // 2, features), F32)
    return pl.pallas_call(
        functools.partial(project_kernel, pieces),
        in_specs=[pl.BlockSpec(memory_space=pltpu.SMEM)]
        + [pl.BlockSpec(memory_space=pl.ANY)] * (1 + len(flat)),
        out_specs=[pl.BlockSpec(memory_space=pltpu.VMEM)] * 2,
        out_shape=[half, half],
        scratch_shapes=[
            pltpu.VMEM((chips, tokens, depth), BF16),
            pltpu.VMEM((chips, features, depth), BF16),
            pltpu.SemaphoreType.DMA((chips,)),
            pltpu.SemaphoreType.DMA((chips * pieces,)),
        ],
        compiler_params=pltpu.CompilerParams(vmem_limit_bytes=VMEM_LIMIT),
        cost_estimate=pl.CostEstimate(
            flops=2 * tokens * features * depth * chips,
            bytes_accessed=12 * 2**20,
            transcendentals=0,
        ),
        name="project%d" % part,
    )(source, all_grad, *flat)


def local(queries, keys, values, grad_out, out_weight, lengths):
    rows = queries.shape[0]
    rank = lax.axis_index("dp")
    core = rank % 2
    x, z = rank // 4, (rank // 2) % 2

    query_pos = rank * rows + jnp.arange(rows, dtype=jnp.int32)
    ends = jnp.cumsum(lengths)[:-1]
    query_start = jnp.max(
        jnp.where(ends[None, :] <= query_pos[:, None], ends[None, :], 0), axis=1
    )
    first = query_start[0] // KEY_BLOCK
    last = query_pos[-1] // KEY_BLOCK
    clear = (query_start[-1] + KEY_BLOCK - 1) // KEY_BLOCK
    block = jnp.arange(16, dtype=jnp.int32)
    distance = (block // 4 - x) % 4
    turn = jnp.where(distance == 0, 0, jnp.where(distance == 3, 1, distance + 1))
    place = jnp.where((block // 2) % 2 == z, 0, 8) + turn * 2
    here = place + jnp.where(block % 2 == core, 0, 1)
    there = 16 + place + jnp.where(block % 2 == core, 1, 0)
    table = [jnp.where(core == 0, here, there), jnp.where(core == 0, there, here)]
    scalars = jnp.stack([first, last - first + 1, clear, core])
    info = jnp.concatenate([scalars, *table]).astype(jnp.int32)
    query_pos, query_start = query_pos[None, :], query_start[None, :]

    depth = out_weight.shape[1]
    mine = lax.dynamic_slice_in_dim(grad_out, core * depth, depth, 1)
    other = lax.dynamic_slice_in_dim(grad_out, (1 - core) * depth, depth, 1)
    chip_grad = jnp.concatenate([mine, dp_move(other, 0, 0, 1)], axis=0)
    all_grad = lax.all_gather(chip_grad, "tensor", axis=0, tiled=False)

    kept = jnp.where(core == 0, keys, values)
    got = dp_move(jnp.where(core == 0, values, keys), 0, 0, 1)
    chip = jnp.concatenate([kept, got], axis=0)
    quad = jnp.concatenate(
        [chip, dp_move(chip, 1, 0, 0), dp_move(chip, -1, 0, 0), dp_move(chip, 2, 0, 0)], axis=0
    )
    ring = jnp.concatenate([quad, dp_move(quad, 0, 1, 0)], axis=0)
    kv = jnp.concatenate([ring, dp_move(ring, 0, 0, 1)], axis=0)

    size = out_weight.shape[0] // PIECES
    own = [out_weight[j * size : (j + 1) * size] for j in range(PIECES)]
    pair = [dp_move(piece, 0, 1, 0) for piece in own]
    held = own + pair
    left = [dp_move(piece, 1, 0, 0) for piece in held]
    right = [dp_move(piece, -1, 0, 0) for piece in held]

    kv = after(kv, *pair)
    parts = [forward(0, info, query_pos, query_start, queries, kv)]

    tied = lax.optimization_barrier((parts[0], left, right))
    parts[0], left, right = tied
    far = [
        dp_move(left[j], 1, 0, 0) if j % 2 == 0 else dp_move(right[j], -1, 0, 0)
        for j in range(2 * PIECES)
    ]
    parts.append(forward(1, info, query_pos, query_start, after(queries, parts[0][1]), kv))

    distances = [(0, 0), (3, 0), (1, 0), (2, 0), (0, 1), (3, 1), (1, 1), (2, 1)]
    source = jnp.stack(
        [2 * ((x + dx) % 4) + (z + dz) % 2 for dx, dz in distances]
    ).astype(jnp.int32)
    carried = ()
    share = PIECES // CHUNKS
    for part in range(CHUNKS):
        weights = [
            [group[dz * PIECES + j] for j in range(part * share, (part + 1) * share)]
            for dz in range(2)
            for group in (held, left, right, far)
        ]
        mine, other = project(part, source, all_grad, weights)
        grads = (mine + dp_move(other, 0, 0, 1)).astype(BF16)
        probs, outs = parts[part]
        grad_queries, own_sums, other_sums = backward(
            part, info, probs, outs, grads, queries, kv, carried
        )
        carried = (own_sums, other_sums, grad_queries)

    chip_sums = (own_sums + dp_move(other_sums, 0, 0, 1).astype(F32)).astype(BF16)
    groups = [[2 * i + c for i in range(8)] for c in range(2)]
    terms = lax.all_to_all(chip_sums, "dp", 0, 0, axis_index_groups=groups, tiled=True)
    done = jnp.sum(terms.astype(F32), axis=0).astype(BF16)
    return grad_queries, done[:, :HEAD_WIDTH], done[:, HEAD_WIDTH:]


def solution(mesh):
    return jax.shard_map(
        local,
        mesh=mesh,
        in_specs=(
            P("dp", "tensor"),
            P("dp", "tensor"),
            P("dp", "tensor"),
            P("dp", "tensor"),
            P("tensor", "dp"),
            P(),
        ),
        out_specs=(P("dp", "tensor"), P("dp", "tensor"), P("dp", "tensor")),
        check_vma=False,
    )
```

time: 247 us -> 269 us (1.089)
  waiting for transfers between devices: 46.7 us -> 73.9 us
  matrix products: 19.5 us -> 0 us
  blocking collectives: 39.8 us -> 55.1 us
  Pallas kernels: 16.7 us -> 30.2 us
  starting transfers between devices: 73.2 us -> 65.7 us
  between operations: 27.6 us -> 20.5 us
  local copies, waits for them, and re-layouts: 14.4 us -> 21.3 us
  other arithmetic: 7.54 us -> 2.42 us
    ppermute x30 -> x38, waiting for transfers between devices: 46.7 us -> 73.9 us  [dp_move(): return lax.ppermute(value, 'dp', pairs)]
    dot_general x16 -> x0, matrix products: 19.5 us -> none  [local(): lax.dot_general(piece, block, (((1,), (1,)), ((), ())), preferred_element...]
    all_to_all x1, blocking collectives: 39.8 us -> 55.1 us  [local(): lax.all_to_all(chip_sums, 'dp', 0, 0, axis_index_groups=groups, tiled=True)]
    unnamed x41 -> x63, local copies, waits for them, and re-layouts: 1.41 us -> 14.9 us
    pallas_call x2 -> x4, Pallas kernels: 7.75 us -> 21 us  [the longest x2 11.3 us: backward(): pl.pallas_call(functools.partial(backward_kernel, heads, part), grid_spec...]
    slice x15 -> x3, local copies, waits for them, and re-layouts: 12 us -> 1.31 us  [the longest x1 0.66 us: local(): return (grad_queries, done[:, :HEAD_WIDTH], done[:, HEAD_WIDTH:])]
    ppermute x30 -> x38, starting transfers between devices: 73.1 us -> 65.7 us  [dp_move(): return lax.ppermute(value, 'dp', pairs)]
    concatenate x0 -> x3, local copies, waits for them, and re-layouts: none -> 3.26 us  [the longest x1 2.29 us: local(): kv = jnp.concatenate([ring, dp_move(ring, 0, 0, 1)], axis=0)]
  transfers between devices with their start and end apart: 31 -> 39, of which waited for: 8 -> 15; matrix products, arithmetic and copies ran while one was open for 15% -> 3% of each run, Pallas kernels for 5% -> 9%
where the time goes in v2:
time: 269 us
  waiting for transfers between devices  73.9 us (27%)
  starting transfers between devices  65.7 us (24%)
  blocking collectives  55.1 us (20%)
  Pallas kernels  30.2 us (11%)
  local copies, waits for them, and re-layouts  21.3 us (8%)
  between operations  20.5 us (8%)
    ppermute x38, waiting for transfers between devices, dp_move(): return lax.ppermute(value, 'dp', pairs)  73.9 us
    ppermute x38, starting transfers between devices, dp_move(): return lax.ppermute(value, 'dp', pairs)  65.7 us
    all_to_all x1, blocking collectives, local(): lax.all_to_all(chip_sums, 'dp', 0, 0, axis_index_groups=groups, tiled=True)  55.1 us
    unnamed x63, local copies, waits for them, and re-layouts  14.9 us
    pallas_call x2, Pallas kernels, backward(): pl.pallas_call(functools.partial(backward_kernel, heads, part), grid_spec...  11.3 us
    pallas_call x2, Pallas kernels, project(): pl.pallas_call(functools.partial(project_kernel, pieces), in_specs=[pl.Bl...  9.78 us
    pallas_call x2, Pallas kernels, forward(): pl.pallas_call(forward_kernel, grid_spec=pltpu.PrefetchScalarGridSpec(num...  9.2 us
  transfers between devices with their start and end apart: 39, of which 15 were waited for; matrix products, arithmetic and copies ran while one was open for 3% of the time, Pallas kernels for 9%

profile of v2, /device:TPU:0, one launch (start us, length us, event | category | flops | bytes accessed | tf_op | source)
XLA Modules:
  0.0 269.1 jit_solution(6484699177145997232)
XLA Ops:
  14.4 2.8 %collective-permute-start.3 = (bf16[512,128]{1,0:T(8,128)(2,1)S(1)}, bf16[512,128]{1,0:T(8,128)(2,1)S(1)}, u32[]{:S(2)}, u32[]{:S(2)}) collective-permute-start(bf16[512,128]{1,0:T(8,128)(2,1)S(1)} %pad_maximum_fusion.1), channel_id=1, source_target_pairs={{0,64},{8,72},{16,80},{24,88},{32,96},{40,104},{48,112},{56,120},{... | collective-permute-start | bytes 393224 | tf_op jit(solution)/shard_map/ppermute | solution.py:33
  20.3 2.8 %collective-permute-done.2 = bf16[512,128]{1,0:T(8,128)(2,1)S(1)} collective-permute-done((bf16[512,128]{1,0:T(8,128)(2,1)S(1)}, bf16[512,128]{1,0:T(8,128)(2,1)S(1)}, u32[]{:S(2)}, u32[]{:S(2)}) %collective-permute-start.2) | collective-permute-done | bytes 131104 | tf_op jit(solution)/shard_map/ppermute | solution.py:33
  24.4 4.0 %collective-permute-start.4 = (bf16[2048,128]{1,0:T(8,128)(2,1)S(1)}, bf16[2048,128]{1,0:T(8,128)(2,1)S(1)}, u32[]{:S(2)}, u32[]{:S(2)}) collective-permute-start(bf16[2048,128]{1,0:T(8,128)(2,1)S(1)} %get-tuple-element.85), channel_id=1, source_target_pairs={{0,16},{8,24},{16,0},{24,8},{32,48},{40,56},{48,32},{56,40},{64,80... | collective-permute-start | bytes 1572872 | tf_op jit(solution)/shard_map/ppermute | solution.py:33
  28.5 2.7 %collective-permute-start.21 = (bf16[256,512]{1,0:T(8,128)(2,1)S(1)}, bf16[256,512]{1,0:T(8,128)(2,1)S(1)}, u32[]{:S(2)}, u32[]{:S(2)}) collective-permute-start(bf16[256,512]{1,0:T(8,128)(2,1)S(1)} %get-tuple-element.73.rest_1_), channel_id=1, source_target_pairs={{0,96},{8,104},{16,112},{24,120},{32,0},{40,8},{48,16},{56,24},{64... | collective-permute-start | bytes 786440 | tf_op jit(solution)/shard_map/ppermute | solution.py:33
  31.2 47.1 %collective-permute-done.4 = bf16[2048,128]{1,0:T(8,128)(2,1)S(1)} collective-permute-done((bf16[2048,128]{1,0:T(8,128)(2,1)S(1)}, bf16[2048,128]{1,0:T(8,128)(2,1)S(1)}, u32[]{:S(2)}, u32[]{:S(2)}) %collective-permute-start.4) | collective-permute-done | bytes 524320 | tf_op jit(solution)/shard_map/ppermute | solution.py:33
  80.5 2.7 %collective-permute-start.19 = (bf16[256,512]{1,0:T(8,128)(2,1)S(1)}, bf16[256,512]{1,0:T(8,128)(2,1)S(1)}, u32[]{:S(2)}, u32[]{:S(2)}) collective-permute-start(bf16[256,512]{1,0:T(8,128)(2,1)S(1)} %get-tuple-element.74.rest_1_), channel_id=1, source_target_pairs={{0,96},{8,104},{16,112},{24,120},{32,0},{40,8},{48,16},{56,24},{64... | collective-permute-start | bytes 786440 | tf_op jit(solution)/shard_map/ppermute | solution.py:33
  85.8 4.0 %collective-permute-done.9.rest_9_ = bf16[256,512]{1,0:T(8,128)(2,1)S(1)} collective-permute-done((bf16[256,512]{1,0:T(8,128)(2,1)S(1)}, bf16[256,512]{1,0:T(8,128)(2,1)S(1)}, u32[]{:S(2)}, u32[]{:S(2)}) %collective-permute-start.9) | collective-permute-done | bytes 262176 | tf_op jit(solution)/shard_map/ppermute | solution.py:33
  89.8 2.7 %collective-permute-start.18 = (bf16[256,512]{1,0:T(8,128)(2,1)S(1)}, bf16[256,512]{1,0:T(8,128)(2,1)S(1)}, u32[]{:S(2)}, u32[]{:S(2)}) collective-permute-start(bf16[256,512]{1,0:T(8,128)(2,1)S(1)} %get-tuple-element.75.rest_0_), channel_id=1, source_target_pairs={{0,96},{8,104},{16,112},{24,120},{32,0},{40,8},{48,16},{56,24},{64... | collective-permute-start | bytes 786440 | tf_op jit(solution)/shard_map/ppermute | solution.py:33
  103.6 3.2 %collective-permute-start.20 = (bf16[256,512]{1,0:T(8,128)(2,1)S(1)}, bf16[256,512]{1,0:T(8,128)(2,1)S(1)}, u32[]{:S(2)}, u32[]{:S(2)}) collective-permute-start(bf16[256,512]{1,0:T(8,128)(2,1)S(1)} %get-tuple-element.76.rest_0_), channel_id=1, source_target_pairs={{0,96},{8,104},{16,112},{24,120},{32,0},{40,8},{48,16},{56,24},{64... | collective-permute-start | bytes 786440 | tf_op jit(solution)/shard_map/ppermute | solution.py:33
  106.8 3.2 %collective-permute-start.25 = (bf16[256,512]{1,0:T(8,128)(2,1)S(1)}, bf16[256,512]{1,0:T(8,128)(2,1)S(1)}, u32[]{:S(2)}, u32[]{:S(2)}) collective-permute-start(bf16[256,512]{1,0:T(8,128)(2,1)S(1)} %collective-permute-done.9.rest_9_), channel_id=1, source_target_pairs={{0,96},{8,104},{16,112},{24,120},{32,0},{40,8},{48,16},{56,24},{64... | collective-permute-start | bytes 786440 | tf_op jit(solution)/shard_map/ppermute | solution.py:33
  110.0 3.2 %collective-permute-start.23 = (bf16[256,512]{1,0:T(8,128)(2,1)S(1)}, bf16[256,512]{1,0:T(8,128)(2,1)}, u32[]{:S(2)}, u32[]{:S(2)}) collective-permute-start(bf16[256,512]{1,0:T(8,128)(2,1)S(1)} %collective-permute-done.7.rest_9_), channel_id=1, source_target_pairs={{0,96},{8,104},{16,112},{24,120},{32,0},{40,8},{48,16},{56,24},{64... | collective-permute-start | bytes 786440 | tf_op jit(solution)/shard_map/ppermute | solution.py:33
  116.9 2.6 collective-permute-start.22
  119.5 3.0 %collective-permute-done.17.rest_11_ = bf16[256,512]{1,0:T(8,128)(2,1)S(1)} collective-permute-done((bf16[256,512]{1,0:T(8,128)(2,1)S(1)}, bf16[256,512]{1,0:T(8,128)(2,1)S(1)}, u32[]{:S(2)}, u32[]{:S(2)}) %collective-permute-start.17) | collective-permute-done | bytes 262176 | tf_op jit(solution)/shard_map/ppermute | solution.py:33
  126.9 4.6 %forward0.1 = (bf16[2816,1024]{1,0:T(8,128)(2,1)}, f32[128,1024]{1,0:T(8,128)S(1)}) custom-call(s32[36]{0:T(128)S(1)} %concatenate.21.info, s32[1,256]{1,0:T(1,128)S(1)} %iota_add_fusion.pos_ref, s32[1,256]{1,0:T(1,128)S(1)} %bitcast.20, bf16[256,1024]{1,0:T(8,128)(2,1)S(1)} %copy-done.19, bf16[8192,128]{1,0:T(8,128)(2,1)S(1)} %copy-done.17), custom_call_target="tpu_custom_call" | custom-call | flops 16000000000 | bytes 10485760 | tf_op jit(solution)/shard_map/forward0/pallas_call | solution.py:112
  137.9 16.0 %collective-permute-start.33 = (bf16[256,512]{1,0:T(8,128)(2,1)S(1)}, bf16[256,512]{1,0:T(8,128)(2,1)}, u32[]{:S(2)}, u32[]{:S(2)}) collective-permute-start(bf16[256,512]{1,0:T(8,128)(2,1)S(1)} %collective-permute-done.19.rest_5_), channel_id=1, source_target_pairs={{0,96},{8,104},{16,112},{24,120},{32,0},{40,8},{48,16},{56,24},{64... | collective-permute-start | bytes 786440 | tf_op jit(solution)/shard_map/ppermute | solution.py:33
  154.0 3.2 %collective-permute-start.35 = (bf16[256,512]{1,0:T(8,128)(2,1)}, bf16[256,512]{1,0:T(8,128)(2,1)}, u32[]{:S(2)}, u32[]{:S(2)}) collective-permute-start(bf16[256,512]{1,0:T(8,128)(2,1)} %collective-permute-done.23.rest_13_), channel_id=1, source_target_pairs={{0,96},{8,104},{16,112},{24,120},{32,0},{40,8},{48,16},{56,24},{64... | collective-permute-start | bytes 786440 | tf_op jit(solution)/shard_map/ppermute | solution.py:33
  157.3 4.0 %collective-permute-done.32.rest_6_ = bf16[256,512]{1,0:T(8,128)(2,1)} collective-permute-done((bf16[256,512]{1,0:T(8,128)(2,1)S(1)}, bf16[256,512]{1,0:T(8,128)(2,1)}, u32[]{:S(2)}, u32[]{:S(2)}) %collective-permute-start.32) | collective-permute-done | bytes 262176 | tf_op jit(solution)/shard_map/ppermute | solution.py:33
  163.3 3.6 %collective-permute-done.34.rest_14_ = bf16[256,512]{1,0:T(8,128)(2,1)} collective-permute-done((bf16[256,512]{1,0:T(8,128)(2,1)}, bf16[256,512]{1,0:T(8,128)(2,1)}, u32[]{:S(2)}, u32[]{:S(2)}) %collective-permute-start.34) | collective-permute-done | bytes 262176 | tf_op jit(solution)/shard_map/ppermute | solution.py:33
  170.8 5.0 %project0.1 = (f32[256,512]{1,0:T(8,128)S(1)}, f32[256,512]{1,0:T(8,128)S(1)}) custom-call(s32[8]{0:T(128)S(1)} %stack.51.source, bf16[8,512,512]{2,1,0:T(8,128)(2,1)} %bitcast.22, bf16[256,512]{1,0:T(8,128)(2,1)S(1)} %get-tuple-element.75.rest_0_, bf16[256,512]{1,0:T(8,128)(2,1)S(1)} %get-tuple-element.74.rest_1_, ...), custom_call_target="tpu_custom_call" | custom-call | flops 2147483648 | bytes 12582912 | tf_op jit(solution)/shard_map/project0/pallas_call | solution.py:289
  176.0 4.7 %forward1.1 = (bf16[2816,1024]{1,0:T(8,128)(2,1)}, f32[128,1024]{1,0:T(8,128)S(1)}) custom-call(s32[36]{0:T(128)S(1)} %concatenate.21.info, s32[1,256]{1,0:T(1,128)S(1)} %iota_add_fusion.pos_ref, s32[1,256]{1,0:T(1,128)S(1)} %bitcast.21, bf16[256,1024]{1,0:T(8,128)(2,1)S(1)} %copy-done.20, bf16[8192,128]{1,0:T(8,128)(2,1)S(1)} %copy-done.18), custom_call_target="tpu_custom_call" | custom-call | flops 16000000000 | bytes 10485760 | tf_op jit(solution)/shard_map/forward1/pallas_call | solution.py:112
  180.8 4.8 %project1.1 = (f32[256,512]{1,0:T(8,128)S(1)}, f32[256,512]{1,0:T(8,128)S(1)}) custom-call(s32[8]{0:T(128)S(1)} %stack.51.source, bf16[8,512,512]{2,1,0:T(8,128)(2,1)} %bitcast.23, bf16[256,512]{1,0:T(8,128)(2,1)S(1)} %get-tuple-element.76.rest_0_, bf16[256,512]{1,0:T(8,128)(2,1)S(1)} %get-tuple-element.73.rest_1_, bf16[256,512]{1,0:T(8,128)(2,1)S(1)} %copy-done.3, ...), custom_call_target="tpu_custom_call" | custom-call | flops 2147483648 | bytes 12582912 | tf_op jit(solution)/shard_map/project1/pallas_call | solution.py:289
  187.6 4.9 %backward0.1 = (bf16[256,1024]{1,0:T(8,128)(2,1)}, f32[8,256,256]{2,1,0:T(8,128)S(1)}, f32[8,256,256]{2,1,0:T(8,128)S(1)}) custom-call(s32[36]{0:T(128)S(1)} %concatenate.21.info, bf16[2816,1024]{1,0:T(8,128)(2,1)} %get-tuple-element.54.probs_ref, f32[128,1024]{1,0:T(8,128)S(1)} %copy-done.24, bf16[256,512]{1,0:T(8,128)(2,1)S(1)} %add_convert_fusion.1.grad_ref, ...), custom_call_target="tpu_custom_call" | custom-call | flops 8000000000 | bytes 10485760 | tf_op jit(solution)/shard_map/backward0/pallas_call | solution.py:234
  195.2 6.3 %backward1.1 = (bf16[256,1024]{1,0:T(8,128)(2,1)}, f32[8,256,256]{2,1,0:T(8,128)S(1)}, bf16[8,256,256]{2,1,0:T(8,128)(2,1)S(1)}) custom-call(s32[36]{0:T(128)S(1)} %concatenate.21.info, bf16[2816,1024]{1,0:T(8,128)(2,1)} %get-tuple-element.42.probs_ref, f32[128,1024]{1,0:T(8,128)S(1)} %get-tuple-element.43.out_ref, ...), custom_call_target="tpu_custom_call", output_to_operand_aliasing={{0}: (9, {})} | custom-call | flops 8000000000 | bytes 10485760 | tf_op jit(solution)/shard_map/backward1/pallas_call | solution.py:234
  206.3 55.1 %all_to_all.5 = bf16[8,256,256]{2,1,0:T(8,128)(2,1)S(1)} all-to-all(bf16[8,256,256]{2,1,0:T(8,128)(2,1)S(1)} %add_convert_fusion), channel_id=1, replica_groups={{0,16,32,48,64,80,96,112},{8,24,40,56,72,88,104,120},{1,17,33,49,65,81,..., dimensions={0} | all-to-all | bytes 2097152 | tf_op jit(solution)/shard_map/all_to_all | solution.py:391
  (147 shorter events, 52.4 us)
Async XLA Ops:
  7.2 161.7 %all-gather.3.cloned.1.call-start = ((), (), s32[]{:S(2)}) async-start(), calls=%async_computation.1 | async-start | bytes 4718592 | tf_op jit(solution)/shard_map/all_gather | solution.py:340
  24.4 53.9 %collective-permute-start.4 = (bf16[2048,128]{1,0:T(8,128)(2,1)S(1)}, bf16[2048,128]{1,0:T(8,128)(2,1)S(1)}, u32[]{:S(2)}, u32[]{:S(2)}) collective-permute-start(bf16[2048,128]{1,0:T(8,128)(2,1)S(1)} %get-tuple-element.85), channel_id=1, source_target_pairs={{0,16},{8,24},{16,0},{24,8},{32,48},{40,56},{48,32},{56,40},{64,80... | collective-permute-start | bytes 1572872 | tf_op jit(solution)/shard_map/ppermute | solution.py:33
  28.5 54.9 %collective-permute-start.21 = (bf16[256,512]{1,0:T(8,128)(2,1)S(1)}, bf16[256,512]{1,0:T(8,128)(2,1)S(1)}, u32[]{:S(2)}, u32[]{:S(2)}) collective-permute-start(bf16[256,512]{1,0:T(8,128)(2,1)S(1)} %get-tuple-element.73.rest_1_), channel_id=1, source_target_pairs={{0,96},{8,104},{16,112},{24,120},{32,0},{40,8},{48,16},{56,24},{64... | collective-permute-start | bytes 786440 | tf_op jit(solution)/shard_map/ppermute | solution.py:33
  31.2 52.2 %collective-permute-start.13 = (bf16[256,512]{1,0:T(8,128)(2,1)S(1)}, bf16[256,512]{1,0:T(8,128)(2,1)S(1)}, u32[]{:S(2)}, u32[]{:S(2)}) collective-permute-start(bf16[256,512]{1,0:T(8,128)(2,1)S(1)} %get-tuple-element.73.rest_1_), channel_id=1, source_target_pairs={{0,32},{8,40},{16,48},{24,56},{32,64},{40,72},{48,80},{56,88},{64,... | collective-permute-start | bytes 786440 | tf_op jit(solution)/shard_map/ppermute | solution.py:33
  79.2 30.9 %collective-permute-start.5 = (bf16[4096,128]{1,0:T(8,128)(2,1)}, bf16[4096,128]{1,0:T(8,128)(2,1)}, u32[]{:S(2)}, u32[]{:S(2)}) collective-permute-start(bf16[4096,128]{1,0:T(8,128)(2,1)} %get-tuple-element.79), channel_id=1, source_target_pairs={{0,8},{8,0},{16,24},{24,16},{32,40},{40,32},{48,56},{56,48},{64,72... | collective-permute-start | bytes 3145736 | tf_op jit(solution)/shard_map/ppermute | solution.py:33
  89.8 13.8 %collective-permute-start.18 = (bf16[256,512]{1,0:T(8,128)(2,1)S(1)}, bf16[256,512]{1,0:T(8,128)(2,1)S(1)}, u32[]{:S(2)}, u32[]{:S(2)}) collective-permute-start(bf16[256,512]{1,0:T(8,128)(2,1)S(1)} %get-tuple-element.75.rest_0_), channel_id=1, source_target_pairs={{0,96},{8,104},{16,112},{24,120},{32,0},{40,8},{48,16},{56,24},{64... | collective-permute-start | bytes 786440 | tf_op jit(solution)/shard_map/ppermute | solution.py:33
  92.5 14.3 %collective-permute-start.10 = (bf16[256,512]{1,0:T(8,128)(2,1)S(1)}, bf16[256,512]{1,0:T(8,128)(2,1)S(1)}, u32[]{:S(2)}, u32[]{:S(2)}) collective-permute-start(bf16[256,512]{1,0:T(8,128)(2,1)S(1)} %get-tuple-element.75.rest_0_), channel_id=1, source_target_pairs={{0,32},{8,40},{16,48},{24,56},{32,64},{40,72},{48,80},{56,88},{64,... | collective-permute-start | bytes 786440 | tf_op jit(solution)/shard_map/ppermute | solution.py:33
  92.5 14.2 %collective-permute-start.6 = (bf16[256,512]{1,0:T(8,128)(2,1)S(1)}, bf16[256,512]{1,0:T(8,128)(2,1)}, u32[]{:S(2)}, u32[]{:S(2)}) collective-permute-start(bf16[256,512]{1,0:T(8,128)(2,1)S(1)} %get-tuple-element.75.rest_0_), channel_id=1, source_target_pairs={{0,16},{8,24},{16,0},{24,8},{32,48},{40,56},{48,32},{56,40},{64,80... | collective-permute-start | bytes 786440 | tf_op jit(solution)/shard_map/ppermute | solution.py:33
  95.0 15.0 %collective-permute-start.8 = (bf16[256,512]{1,0:T(8,128)(2,1)S(1)}, bf16[256,512]{1,0:T(8,128)(2,1)S(1)}, u32[]{:S(2)}, u32[]{:S(2)}) collective-permute-start(bf16[256,512]{1,0:T(8,128)(2,1)S(1)} %get-tuple-element.76.rest_0_), channel_id=1, source_target_pairs={{0,16},{8,24},{16,0},{24,8},{32,48},{40,56},{48,32},{56,40},{64,80... | collective-permute-start | bytes 786440 | tf_op jit(solution)/shard_map/ppermute | solution.py:33
  103.6 12.0 %collective-permute-start.20 = (bf16[256,512]{1,0:T(8,128)(2,1)S(1)}, bf16[256,512]{1,0:T(8,128)(2,1)S(1)}, u32[]{:S(2)}, u32[]{:S(2)}) collective-permute-start(bf16[256,512]{1,0:T(8,128)(2,1)S(1)} %get-tuple-element.76.rest_0_), channel_id=1, source_target_pairs={{0,96},{8,104},{16,112},{24,120},{32,0},{40,8},{48,16},{56,24},{64... | collective-permute-start | bytes 786440 | tf_op jit(solution)/shard_map/ppermute | solution.py:33
  106.8 12.7 %collective-permute-start.25 = (bf16[256,512]{1,0:T(8,128)(2,1)S(1)}, bf16[256,512]{1,0:T(8,128)(2,1)S(1)}, u32[]{:S(2)}, u32[]{:S(2)}) collective-permute-start(bf16[256,512]{1,0:T(8,128)(2,1)S(1)} %collective-permute-done.9.rest_9_), channel_id=1, source_target_pairs={{0,96},{8,104},{16,112},{24,120},{32,0},{40,8},{48,16},{56,24},{64... | collective-permute-start | bytes 786440 | tf_op jit(solution)/shard_map/ppermute | solution.py:33
  110.0 12.5 %collective-permute-start.17 = (bf16[256,512]{1,0:T(8,128)(2,1)S(1)}, bf16[256,512]{1,0:T(8,128)(2,1)S(1)}, u32[]{:S(2)}, u32[]{:S(2)}) collective-permute-start(bf16[256,512]{1,0:T(8,128)(2,1)S(1)} %collective-permute-done.9.rest_9_), channel_id=1, source_target_pairs={{0,32},{8,40},{16,48},{24,56},{32,64},{40,72},{48,80},{56,88},{64,... | collective-permute-start | bytes 786440 | tf_op jit(solution)/shard_map/ppermute | solution.py:33
  110.0 14.7 %collective-permute-start.23 = (bf16[256,512]{1,0:T(8,128)(2,1)S(1)}, bf16[256,512]{1,0:T(8,128)(2,1)}, u32[]{:S(2)}, u32[]{:S(2)}) collective-permute-start(bf16[256,512]{1,0:T(8,128)(2,1)S(1)} %collective-permute-done.7.rest_9_), channel_id=1, source_target_pairs={{0,96},{8,104},{16,112},{24,120},{32,0},{40,8},{48,16},{56,24},{64... | collective-permute-start | bytes 786440 | tf_op jit(solution)/shard_map/ppermute | solution.py:33
  116.3 15.9 %collective-permute-start.15 = (bf16[256,512]{1,0:T(8,128)(2,1)S(1)}, bf16[256,512]{1,0:T(8,128)(2,1)S(1)}, u32[]{:S(2)}, u32[]{:S(2)}) collective-permute-start(bf16[256,512]{1,0:T(8,128)(2,1)S(1)} %collective-permute-done.7.rest_9_), channel_id=1, source_target_pairs={{0,32},{8,40},{16,48},{24,56},{32,64},{40,72},{48,80},{56,88},{64,... | collective-permute-start | bytes 786440 | tf_op jit(solution)/shard_map/ppermute | solution.py:33
  116.9 16.0 %collective-permute-start.22 = (bf16[256,512]{1,0:T(8,128)(2,1)}, bf16[256,512]{1,0:T(8,128)(2,1)S(1)}, u32[]{:S(2)}, u32[]{:S(2)}) collective-permute-start(bf16[256,512]{1,0:T(8,128)(2,1)} %collective-permute-done.6.rest_8_), channel_id=1, source_target_pairs={{0,96},{8,104},{16,112},{24,120},{32,0},{40,8},{48,16},{56,24},{64... | collective-permute-start | bytes 786440 | tf_op jit(solution)/shard_map/ppermute | solution.py:33
  119.5 14.3 %collective-permute-start.14 = (bf16[256,512]{1,0:T(8,128)(2,1)}, bf16[256,512]{1,0:T(8,128)(2,1)}, u32[]{:S(2)}, u32[]{:S(2)}) collective-permute-start(bf16[256,512]{1,0:T(8,128)(2,1)} %collective-permute-done.6.rest_8_), channel_id=1, source_target_pairs={{0,32},{8,40},{16,48},{24,56},{32,64},{40,72},{48,80},{56,88},{64,... | collective-permute-start | bytes 786440 | tf_op jit(solution)/shard_map/ppermute | solution.py:33
  137.3 24.0 %collective-permute-start.32 = (bf16[256,512]{1,0:T(8,128)(2,1)S(1)}, bf16[256,512]{1,0:T(8,128)(2,1)}, u32[]{:S(2)}, u32[]{:S(2)}) collective-permute-start(bf16[256,512]{1,0:T(8,128)(2,1)S(1)} %collective-permute-done.10.rest_2_), channel_id=1, source_target_pairs={{0,32},{8,40},{16,48},{24,56},{32,64},{40,72},{48,80},{56,88},{64,... | collective-permute-start | bytes 786440 | tf_op jit(solution)/shard_map/ppermute | solution.py:33
  137.9 25.4 %collective-permute-start.33 = (bf16[256,512]{1,0:T(8,128)(2,1)S(1)}, bf16[256,512]{1,0:T(8,128)(2,1)}, u32[]{:S(2)}, u32[]{:S(2)}) collective-permute-start(bf16[256,512]{1,0:T(8,128)(2,1)S(1)} %collective-permute-done.19.rest_5_), channel_id=1, source_target_pairs={{0,96},{8,104},{16,112},{24,120},{32,0},{40,8},{48,16},{56,24},{64... | collective-permute-start | bytes 786440 | tf_op jit(solution)/shard_map/ppermute | solution.py:33
  154.0 12.9 %collective-permute-start.34 = (bf16[256,512]{1,0:T(8,128)(2,1)}, bf16[256,512]{1,0:T(8,128)(2,1)}, u32[]{:S(2)}, u32[]{:S(2)}) collective-permute-start(bf16[256,512]{1,0:T(8,128)(2,1)} %collective-permute-done.14.rest_10_), channel_id=1, source_target_pairs={{0,32},{8,40},{16,48},{24,56},{32,64},{40,72},{48,80},{56,88},{64,... | collective-permute-start | bytes 786440 | tf_op jit(solution)/shard_map/ppermute | solution.py:33
  154.0 15.0 %collective-permute-start.35 = (bf16[256,512]{1,0:T(8,128)(2,1)}, bf16[256,512]{1,0:T(8,128)(2,1)}, u32[]{:S(2)}, u32[]{:S(2)}) collective-permute-start(bf16[256,512]{1,0:T(8,128)(2,1)} %collective-permute-done.23.rest_13_), channel_id=1, source_target_pairs={{0,96},{8,104},{16,112},{24,120},{32,0},{40,8},{48,16},{56,24},{64... | collective-permute-start | bytes 786440 | tf_op jit(solution)/shard_map/ppermute | solution.py:33
  157.3 23.4 %collective-permute-start.27 = (bf16[256,512]{1,0:T(8,128)(2,1)}, bf16[256,512]{1,0:T(8,128)(2,1)}, u32[]{:S(2)}, u32[]{:S(2)}) collective-permute-start(bf16[256,512]{1,0:T(8,128)(2,1)} %copy-done.2), channel_id=1, source_target_pairs={{0,32},{8,40},{16,48},{24,56},{32,64},{40,72},{48,80},{56,88},{64,... | collective-permute-start | bytes 786440 | tf_op jit(solution)/shard_map/ppermute | solution.py:33
  161.3 19.4 %collective-permute-start.28 = (bf16[256,512]{1,0:T(8,128)(2,1)S(1)}, bf16[256,512]{1,0:T(8,128)(2,1)}, u32[]{:S(2)}, u32[]{:S(2)}) collective-permute-start(bf16[256,512]{1,0:T(8,128)(2,1)S(1)} %collective-permute-done.21.rest_5_), channel_id=1, source_target_pairs={{0,96},{8,104},{16,112},{24,120},{32,0},{40,8},{48,16},{56,24},{64... | collective-permute-start | bytes 786440 | tf_op jit(solution)/shard_map/ppermute | solution.py:33
  163.3 17.4 %collective-permute-start.29 = (bf16[256,512]{1,0:T(8,128)(2,1)}, bf16[256,512]{1,0:T(8,128)(2,1)}, u32[]{:S(2)}, u32[]{:S(2)}) collective-permute-start(bf16[256,512]{1,0:T(8,128)(2,1)} %copy-done.10), channel_id=1, source_target_pairs={{0,32},{8,40},{16,48},{24,56},{32,64},{40,72},{48,80},{56,88},{64,... | collective-permute-start | bytes 786440 | tf_op jit(solution)/shard_map/ppermute | solution.py:33
  166.9 13.8 %collective-permute-start.30 = (bf16[256,512]{1,0:T(8,128)(2,1)}, bf16[256,512]{1,0:T(8,128)(2,1)}, u32[]{:S(2)}, u32[]{:S(2)}) collective-permute-start(bf16[256,512]{1,0:T(8,128)(2,1)} %copy-done.4), channel_id=1, source_target_pairs={{0,96},{8,104},{16,112},{24,120},{32,0},{40,8},{48,16},{56,24},{64... | collective-permute-start | bytes 786440 | tf_op jit(solution)/shard_map/ppermute | solution.py:33
  (44 other events, 305.9 us)
Sparse Core Ops, SparseCore 0:
  10.9 55.2 all-gather.2

commit v3 on v2

--- a/solution.py
+++ b/solution.py
@@ -12,13 +12,12 @@
 KEY_BLOCK = 256
 MOST = 2560
 CHUNKS = 2
-PIECES = 4
 MASKED = -1e30
 SCALE = 1.0 / math.sqrt(HEAD_WIDTH)
 LOG2E = 1.0 / math.log(2.0)
 BF16 = jnp.bfloat16
 F32 = jnp.float32
-VMEM_LIMIT = 48 * 2**20
+VMEM_LIMIT = 32 * 2**20
 
 FIRST, COUNT, CLEAR, CORE, TABLE = 0, 1, 2, 3, 4
 
@@ -31,6 +30,14 @@
                 target = ((x + dx) % 4) * 4 + ((z + dz) % 2) * 2 + (c + dc) % 2
                 pairs.append((x * 4 + z * 2 + c, target))
     return lax.ppermute(value, "dp", pairs)
+
+
+def tensor_move(value, dz, dy):
+    pairs = []
+    for z in range(2):
+        for y in range(4):
+            pairs.append((z * 4 + y, ((z + dz) % 2) * 4 + (y + dy) % 4))
+    return lax.ppermute(value, "tensor", pairs)
 
 
 def after(value, *others):
@@ -133,7 +140,7 @@
             jax.ShapeDtypeStruct((live, heads * rows), BF16),
             jax.ShapeDtypeStruct((HEAD_WIDTH, heads * rows), F32),
         ],
-        compiler_params=pltpu.CompilerParams(vmem_limit_bytes=VMEM_LIMIT),
+        compiler_params=pltpu.CompilerParams(vmem_limit_bytes=VMEM_LIMIT // 2),
         cost_estimate=pl.CostEstimate(
             flops=16 * 10**9, bytes_accessed=10 * 2**20, transcendentals=0
         ),
@@ -254,58 +261,63 @@
     )(info, probs, outs, grads, queries, kv, kv, *carried)
 
 
-def project_kernel(pieces, source, grad_ref, *rest):
-    weights, (own_ref, other_ref, grad, weight, grad_sem, weight_sem) = rest[:-6], rest[-6:]
-    chips = len(weights) // pieces
-    part_rows = weights[0].shape[0]
+def project_kernel(layout, tokens, slots, *rest):
+    count = sum(len(sizes) for both in layout for sizes in both)
+    pieces, (own_ref, other_ref, grad, weight, grad_sem, weight_sem) = rest[:count], rest[count:]
+    pieces = list(pieces)
     copies = []
-    for i in range(chips):
-        one = [pltpu.make_async_copy(grad_ref.at[source[i]], grad.at[i], grad_sem.at[i])]
-        for j in range(pieces):
-            k = i * pieces + j
-            rows = pl.ds(j * part_rows, part_rows)
-            one.append(pltpu.make_async_copy(weights[k], weight.at[i, rows], weight_sem.at[k]))
+    for target, sems, chips in ((grad, grad_sem, layout[0]), (weight, weight_sem, layout[1])):
+        lists, k = [], 0
+        for i, sizes in enumerate(chips):
+            at, one = 0, []
+            for size in sizes:
+                copy = pltpu.make_async_copy(pieces.pop(0), target.at[i, pl.ds(at, size)], sems.at[k])
+                copy.start()
+                one.append(copy)
+                at, k = at + size, k + 1
+            lists.append(one)
+        copies.append(lists)
+    for one in copies[0]:
         for copy in one:
-            copy.start()
-        copies.append(one)
-    half = own_ref.shape[0]
-    for i in range(chips):
-        for copy in copies[i]:
+            copy.wait()
+    half = tokens // 2
+    for i, one in enumerate(copies[1]):
+        for copy in one:
             copy.wait()
         for ref, at in ((own_ref, 0), (other_ref, half)):
-            term = dot_t(grad[i, at : at + half, :], weight[i])
+            term = dot_t(grad[slots[i], at : at + half, :], weight[i])
             if i == 0:
                 ref[...] = term
             else:
                 ref[...] += term
 
 
-def project(part, source, all_grad, weights):
-    chips, tokens, depth = all_grad.shape
-    pieces = len(weights[0])
-    features = pieces * weights[0][0].shape[0]
-    flat = [piece for chip in weights for piece in chip]
+def project(part, slots, grads, weights):
+    layout = [[[piece.shape[0] for piece in chip] for chip in both] for both in (grads, weights)]
+    flat = [piece for both in (grads, weights) for chip in both for piece in chip]
+    tokens, features = sum(layout[0][0]), sum(layout[1][0])
+    depth, chips = flat[0].shape[1], len(weights)
     half = jax.ShapeDtypeStruct((tokens // 2, features), F32)
     return pl.pallas_call(
-        functools.partial(project_kernel, pieces),
+        functools.partial(project_kernel, layout, tokens),
         in_specs=[pl.BlockSpec(memory_space=pltpu.SMEM)]
-        + [pl.BlockSpec(memory_space=pl.ANY)] * (1 + len(flat)),
+        + [pl.BlockSpec(memory_space=pl.ANY)] * len(flat),
         out_specs=[pl.BlockSpec(memory_space=pltpu.VMEM)] * 2,
         out_shape=[half, half],
         scratch_shapes=[
             pltpu.VMEM((chips, tokens, depth), BF16),
             pltpu.VMEM((chips, features, depth), BF16),
-            pltpu.SemaphoreType.DMA((chips,)),
-            pltpu.SemaphoreType.DMA((chips * pieces,)),
+            pltpu.SemaphoreType.DMA((sum(len(sizes) for sizes in layout[0]),)),
+            pltpu.SemaphoreType.DMA((sum(len(sizes) for sizes in layout[1]),)),
         ],
-        compiler_params=pltpu.CompilerParams(vmem_limit_bytes=VMEM_LIMIT),
+        compiler_params=pltpu.CompilerParams(vmem_limit_bytes=16 * 2**20),
         cost_estimate=pl.CostEstimate(
             flops=2 * tokens * features * depth * chips,
-            bytes_accessed=12 * 2**20,
+            bytes_accessed=10 * 2**20,
             transcendentals=0,
         ),
         name="project%d" % part,
-    )(source, all_grad, *flat)
+    )(slots, *flat)
 
 
 def local(queries, keys, values, grad_out, out_weight, lengths):
@@ -325,7 +337,7 @@
     block = jnp.arange(16, dtype=jnp.int32)
     distance = (block // 4 - x) % 4
     turn = jnp.where(distance == 0, 0, jnp.where(distance == 3, 1, distance + 1))
-    place = jnp.where((block // 2) % 2 == z, 0, 8) + turn * 2
+    place = turn * 4 + jnp.where((block // 2) % 2 == z, 0, 2)
     here = place + jnp.where(block % 2 == core, 0, 1)
     there = 16 + place + jnp.where(block % 2 == core, 1, 0)
     table = [jnp.where(core == 0, here, there), jnp.where(core == 0, there, here)]
@@ -337,54 +349,82 @@
     mine = lax.dynamic_slice_in_dim(grad_out, core * depth, depth, 1)
     other = lax.dynamic_slice_in_dim(grad_out, (1 - core) * depth, depth, 1)
     chip_grad = jnp.concatenate([mine, dp_move(other, 0, 0, 1)], axis=0)
-    all_grad = lax.all_gather(chip_grad, "tensor", axis=0, tiled=False)
 
     kept = jnp.where(core == 0, keys, values)
     got = dp_move(jnp.where(core == 0, values, keys), 0, 0, 1)
     chip = jnp.concatenate([kept, got], axis=0)
-    quad = jnp.concatenate(
-        [chip, dp_move(chip, 1, 0, 0), dp_move(chip, -1, 0, 0), dp_move(chip, 2, 0, 0)], axis=0
+    pair = jnp.concatenate([chip, dp_move(chip, 0, 1, 0)], axis=0)
+    ring = jnp.concatenate(
+        [pair, dp_move(pair, 1, 0, 0), dp_move(pair, -1, 0, 0), dp_move(pair, 2, 0, 0)], axis=0
     )
-    ring = jnp.concatenate([quad, dp_move(quad, 0, 1, 0)], axis=0)
     kv = jnp.concatenate([ring, dp_move(ring, 0, 0, 1)], axis=0)
 
-    size = out_weight.shape[0] // PIECES
-    own = [out_weight[j * size : (j + 1) * size] for j in range(PIECES)]
-    pair = [dp_move(piece, 0, 1, 0) for piece in own]
-    held = own + pair
-    left = [dp_move(piece, 1, 0, 0) for piece in held]
-    right = [dp_move(piece, -1, 0, 0) for piece in held]
-
-    kv = after(kv, *pair)
-    parts = [forward(0, info, query_pos, query_start, queries, kv)]
-
-    tied = lax.optimization_barrier((parts[0], left, right))
-    parts[0], left, right = tied
-    far = [
-        dp_move(left[j], 1, 0, 0) if j % 2 == 0 else dp_move(right[j], -1, 0, 0)
-        for j in range(2 * PIECES)
-    ]
-    parts.append(forward(1, info, query_pos, query_start, after(queries, parts[0][1]), kv))
-
-    distances = [(0, 0), (3, 0), (1, 0), (2, 0), (0, 1), (3, 1), (1, 1), (2, 1)]
-    source = jnp.stack(
-        [2 * ((x + dx) % 4) + (z + dz) % 2 for dx, dz in distances]
-    ).astype(jnp.int32)
-    carried = ()
-    share = PIECES // CHUNKS
-    for part in range(CHUNKS):
-        weights = [
-            [group[dz * PIECES + j] for j in range(part * share, (part + 1) * share)]
-            for dz in range(2)
-            for group in (held, left, right, far)
-        ]
-        mine, other = project(part, source, all_grad, weights)
+    size = out_weight.shape[0] // CHUNKS
+    own = [out_weight[j * size : (j + 1) * size] for j in range(CHUNKS)]
+
+    def both(move, block):
+        return block, move(block, 1), move(block, -1)
+
+    def far(move, ring):
+        half = ring[0].shape[0] // 2
+        return move(ring[1][:half], 1), move(ring[2][half:], -1)
+
+    def along_x(block, step):
+        return dp_move(block, step, 0, 0)
+
+    def along_y(block, step):
+        return tensor_move(block, 0, step)
+
+    paired = [dp_move(block, 0, 1, 0) for block in own]
+    ring00 = both(along_x, own[0])
+    grad0 = both(along_y, chip_grad)
+    grad_pair = tensor_move(chip_grad, 1, 0)
+    kv, ring00, paired, grad0, grad_pair = lax.optimization_barrier(
+        (kv, ring00, paired, grad0, grad_pair)
+    )
+
+    ring01 = both(along_x, paired[0])
+    far00 = far(along_x, ring00)
+    ring10 = both(along_x, own[1])
+    grad1 = both(along_y, grad_pair)
+    grad_far0 = far(along_y, grad0)
+    first_part = forward(0, info, query_pos, query_start, queries, kv)
+    second_part = forward(1, info, query_pos, query_start, after(queries, first_part[1]), kv)
+    parts = [first_part, second_part]
+    parts, ring01, far00, ring10, grad1, grad_far0 = lax.optimization_barrier(
+        (parts, ring01, far00, ring10, grad1, grad_far0)
+    )
+
+    far01 = far(along_x, ring01)
+    grad_far1 = far(along_y, grad1)
+    ring11 = both(along_x, paired[1])
+    far10 = far(along_x, ring10)
+
+    t = lax.axis_index("tensor")
+    slots = []
+    for dz in range(2):
+        for dx in (0, -1, 1, 2):
+            source = 2 * ((x + dx) % 4) + (z + dz) % 2
+            y_distance = (source - t) % 4
+            turn = jnp.where(
+                y_distance == 0, 0, jnp.where(y_distance == 3, 1, jnp.where(y_distance == 1, 2, 3))
+            )
+            slots.append(jnp.where(source // 4 == t // 4, 0, 4) + turn)
+    slots = jnp.stack(slots).astype(jnp.int32)
+    all_grad = [[block] for block in grad0] + [grad_far0] + [[block] for block in grad1] + [grad_far1]
+
+    def one_part(part, weights, carried):
+        mine, other = project(part, slots, all_grad, weights)
         grads = (mine + dp_move(other, 0, 0, 1)).astype(BF16)
         probs, outs = parts[part]
-        grad_queries, own_sums, other_sums = backward(
-            part, info, probs, outs, grads, queries, kv, carried
-        )
-        carried = (own_sums, other_sums, grad_queries)
+        return backward(part, info, probs, outs, grads, queries, kv, carried)
+
+    weights = [[block] for block in ring00] + [far00] + [[block] for block in ring01] + [far01]
+    grad_queries, own_sums, other_sums = one_part(0, weights, ())
+    carried = (own_sums, other_sums, grad_queries)
+    far11 = far(along_x, ring11)
+    weights = [[block] for block in ring10] + [far10] + [[block] for block in ring11] + [far11]
+    grad_queries, own_sums, other_sums = one_part(1, weights, carried)
 
     chip_sums = (own_sums + dp_move(other_sums, 0, 0, 1).astype(F32)).astype(BF16)
     groups = [[2 * i + c for i in range(8)] for c in range(2)]

time: 269 us -> 233 us (0.87)
  waiting for transfers between devices: 73.9 us -> 49.8 us
  between operations: 20.5 us -> 6.96 us
  local copies, waits for them, and re-layouts: 21.3 us -> 32.5 us
  blocking collectives: 55.1 us -> 45.8 us
  Pallas kernels: 30.2 us -> 24.2 us
  starting transfers between devices: 65.7 us -> 70 us
    ppermute x38 -> x28, waiting for transfers between devices: 73.9 us -> 30.8 us  [dp_move(): return lax.ppermute(value, 'dp', pairs)]
    ppermute x0 -> x9, waiting for transfers between devices: none -> 18.9 us  [tensor_move(): return lax.ppermute(value, 'tensor', pairs)]
    ppermute x0 -> x9, starting transfers between devices: none -> 12.9 us  [tensor_move(): return lax.ppermute(value, 'tensor', pairs)]
    all_to_all x1, blocking collectives: 55.1 us -> 45.8 us  [local(): lax.all_to_all(chip_sums, 'dp', 0, 0, axis_index_groups=groups, tiled=True)]
    ppermute x38 -> x28, starting transfers between devices: 65.7 us -> 57.1 us  [dp_move(): return lax.ppermute(value, 'dp', pairs)]
    slice x1 -> x13, local copies, waits for them, and re-layouts: 0.07 us -> 6.21 us  [the longest x12 6.14 us: far(): return (move(ring[1][:half], 1), move(ring[2][half:], -1))]
    unnamed x63 -> x83, local copies, waits for them, and re-layouts: 14.9 us -> 19.4 us
    pallas_call x2, Pallas kernels: 11.3 us -> 6.82 us  [backward(): pl.pallas_call(functools.partial(backward_kernel, heads, part), grid_spec...]
  transfers between devices with their start and end apart: 39 -> 37, of which waited for: 15 -> 16; matrix products, arithmetic and copies ran while one was open for 3% -> 7% of each run, Pallas kernels for 9% -> 9%
where the time goes in v3:
time: 233 us
  starting transfers between devices  70 us (30%)
  waiting for transfers between devices  49.8 us (21%)
  blocking collectives  45.8 us (20%)
  local copies, waits for them, and re-layouts  32.5 us (14%)
  Pallas kernels  24.2 us (10%)
  between operations  6.96 us (3%)
  other arithmetic  3.58 us (2%)
    ppermute x28, starting transfers between devices, dp_move(): return lax.ppermute(value, 'dp', pairs)  57.1 us
    all_to_all x1, blocking collectives, local(): lax.all_to_all(chip_sums, 'dp', 0, 0, axis_index_groups=groups, tiled=True)  45.8 us
    ppermute x28, waiting for transfers between devices, dp_move(): return lax.ppermute(value, 'dp', pairs)  30.8 us
    unnamed x83, local copies, waits for them, and re-layouts  19.4 us
    ppermute x9, waiting for transfers between devices, tensor_move(): return lax.ppermute(value, 'tensor', pairs)  18.9 us
    ppermute x9, starting transfers between devices, tensor_move(): return lax.ppermute(value, 'tensor', pairs)  12.9 us
    pallas_call x2, Pallas kernels, project(): pl.pallas_call(functools.partial(project_kernel, layout, tokens), in_spec...  10.2 us
    pallas_call x2, Pallas kernels, forward(): pl.pallas_call(forward_kernel, grid_spec=pltpu.PrefetchScalarGridSpec(num...  7.15 us
  transfers between devices with their start and end apart: 37, of which 16 were waited for; matrix products, arithmetic and copies ran while one was open for 7% of the time, Pallas kernels for 9%

profile of v3, /device:TPU:0, one launch (start us, length us, event | category | flops | bytes accessed | tf_op | source)
XLA Modules:
  0.0 232.9 jit_solution(15699376759144173986)
XLA Ops:
  3.5 4.0 %collective-permute-start.1 = (bf16[512,128]{1,0:T(8,128)(2,1)S(1)}, bf16[512,128]{1,0:T(8,128)(2,1)S(1)}, u32[]{:S(2)}, u32[]{:S(2)}) collective-permute-start(bf16[512,128]{1,0:T(8,128)(2,1)S(1)} %pad_maximum_fusion.2), channel_id=1, source_target_pairs={{0,16},{8,24},{16,0},{24,8},{32,48},{40,56},{48,32},{56,40},{64,80... | collective-permute-start | bytes 393224 | tf_op jit(solution)/shard_map/ppermute | solution.py:32
  7.6 3.8 %collective-permute-done.1 = bf16[512,128]{1,0:T(8,128)(2,1)S(1)} collective-permute-done((bf16[512,128]{1,0:T(8,128)(2,1)S(1)}, bf16[512,128]{1,0:T(8,128)(2,1)S(1)}, u32[]{:S(2)}, u32[]{:S(2)}) %collective-permute-start.1) | collective-permute-done | bytes 131104 | tf_op jit(solution)/shard_map/ppermute | solution.py:32
  17.9 3.1 %collective-permute-done.2 = bf16[1024,128]{1,0:T(8,128)(2,1)S(1)} collective-permute-done((bf16[1024,128]{1,0:T(8,128)(2,1)S(1)}, bf16[1024,128]{1,0:T(8,128)(2,1)S(1)}, u32[]{:S(2)}, u32[]{:S(2)}) %collective-permute-start.2) | collective-permute-done | bytes 262176 | tf_op jit(solution)/shard_map/ppermute | solution.py:32
  21.7 3.8 %collective-permute-done.3 = bf16[1024,128]{1,0:T(8,128)(2,1)S(1)} collective-permute-done((bf16[1024,128]{1,0:T(8,128)(2,1)S(1)}, bf16[1024,128]{1,0:T(8,128)(2,1)S(1)}, u32[]{:S(2)}, u32[]{:S(2)}) %collective-permute-start.3) | collective-permute-done | bytes 262176 | tf_op jit(solution)/shard_map/ppermute | solution.py:32
  31.3 2.9 %collective-permute-start.8 = (bf16[512,512]{1,0:T(8,128)(2,1)S(1)}, bf16[512,512]{1,0:T(8,128)(2,1)}, u32[]{:S(2)}, u32[]{:S(2)}) collective-permute-start(bf16[512,512]{1,0:T(8,128)(2,1)S(1)} %get-tuple-element.73.rest_10_), channel_id=1, source_target_pairs={{0,16},{8,24},{16,0},{24,8},{32,48},{40,56},{48,32},{56,40},{64,80... | collective-permute-start | bytes 1572872 | tf_op jit(solution)/shard_map/ppermute | solution.py:32
  39.5 4.2 %collective-permute-done.6.rest_11_ = bf16[512,512]{1,0:T(8,128)(2,1)} collective-permute-done((bf16[512,512]{1,0:T(8,128)(2,1)S(1)}, bf16[512,512]{1,0:T(8,128)(2,1)}, u32[]{:S(2)}, u32[]{:S(2)}) %collective-permute-start.6) | collective-permute-done | bytes 524320 | tf_op jit(solution)/shard_map/ppermute | solution.py:32
  60.5 9.0 %collective-permute-done.13.rest_5_ = bf16[512,512]{1,0:T(8,128)(2,1)S(1)} collective-permute-done((bf16[512,512]{1,0:T(8,128)(2,1)S(1)}, bf16[512,512]{1,0:T(8,128)(2,1)S(1)}, u32[]{:S(2)}, u32[]{:S(2)}) %collective-permute-start.13) | collective-permute-done | bytes 524320 | tf_op jit(solution)/shard_map/ppermute | solution.py:40
  71.5 3.3 %collective-permute-start.17 = (bf16[256,512]{1,0:T(8,128)(2,1)S(1)}, bf16[256,512]{1,0:T(8,128)(2,1)S(1)}, u32[]{:S(2)}, u32[]{:S(2)}) collective-permute-start(bf16[256,512]{1,0:T(8,128)(2,1)S(1)} %slice.68), channel_id=1, source_target_pairs={{0,96},{8,104},{16,112},{24,120},{32,0},{40,8},{48,16},{56,24},{64... | collective-permute-start | bytes 786440 | tf_op jit(solution)/shard_map/ppermute | solution.py:32
  78.1 3.6 %forward0.1 = (bf16[2816,1024]{1,0:T(8,128)(2,1)S(1)}, f32[128,1024]{1,0:T(8,128)S(1)}) custom-call(s32[36]{0:T(128)S(1)} %concatenate.21.info, s32[1,256]{1,0:T(1,128)S(1)} %iota_add_fusion.pos_ref, s32[1,256]{1,0:T(1,128)S(1)} %bitcast.19, bf16[256,1024]{1,0:T(8,128)(2,1)S(1)} %copy-done.25, bf16[8192,128]{1,0:T(8,128)(2,1)S(1)} %copy-done.23), custom_call_target="tpu_custom_call" | custom-call | flops 16000000000 | bytes 10485760 | tf_op jit(solution)/shard_map/forward0/pallas_call | solution.py:119
  81.7 2.5 %copy-done.28 = bf16[2816,1024]{1,0:T(8,128)(2,1)} copy-done((bf16[2816,1024]{1,0:T(8,128)(2,1)}, bf16[2816,1024]{1,0:T(8,128)(2,1)S(1)}, u32[]{:S(2)}) %copy-start.28) | copy-done | bytes 5767192
  85.6 14.2 %collective-permute-start.15 = (bf16[512,512]{1,0:T(8,128)(2,1)}, bf16[512,512]{1,0:T(8,128)(2,1)S(1)}, u32[]{:S(2)}, u32[]{:S(2)}) collective-permute-start(bf16[512,512]{1,0:T(8,128)(2,1)} %collective-permute-done.8.rest_15_), channel_id=1, source_target_pairs={{0,96},{8,104},{16,112},{24,120},{32,0},{40,8},{48,16},{56,24},{64... | collective-permute-start | bytes 1572872 | tf_op jit(solution)/shard_map/ppermute | solution.py:32
  104.2 3.6 %forward1.1 = (bf16[2816,1024]{1,0:T(8,128)(2,1)S(1)}, f32[128,1024]{1,0:T(8,128)S(1)}) custom-call(s32[36]{0:T(128)S(1)} %concatenate.21.info, s32[1,256]{1,0:T(1,128)S(1)} %iota_add_fusion.pos_ref, s32[1,256]{1,0:T(1,128)S(1)} %bitcast.20, bf16[256,1024]{1,0:T(8,128)(2,1)S(1)} %copy-done.25, bf16[8192,128]{1,0:T(8,128)(2,1)S(1)} %copy-done.23), custom_call_target="tpu_custom_call" | custom-call | flops 16000000000 | bytes 10485760 | tf_op jit(solution)/shard_map/forward1/pallas_call | solution.py:119
  107.9 2.4 %copy-done.27 = bf16[2816,1024]{1,0:T(8,128)(2,1)} copy-done((bf16[2816,1024]{1,0:T(8,128)(2,1)}, bf16[2816,1024]{1,0:T(8,128)(2,1)S(1)}, u32[]{:S(2)}) %copy-start.27) | copy-done | bytes 5767192
  111.1 9.9 %collective-permute-done.23.rest_4_ = bf16[256,512]{1,0:T(8,128)(2,1)S(1)} collective-permute-done((bf16[256,512]{1,0:T(8,128)(2,1)S(1)}, bf16[256,512]{1,0:T(8,128)(2,1)S(1)}, u32[]{:S(2)}, u32[]{:S(2)}) %collective-permute-start.23) | collective-permute-done | bytes 262176 | tf_op jit(solution)/shard_map/ppermute | solution.py:40
  126.6 6.4 %collective-permute-start.34 = (bf16[256,512]{1,0:T(8,128)(2,1)}, bf16[256,512]{1,0:T(8,128)(2,1)}, u32[]{:S(2)}, u32[]{:S(2)}) collective-permute-start(bf16[256,512]{1,0:T(8,128)(2,1)} %slice.78), channel_id=1, source_target_pairs={{0,96},{8,104},{16,112},{24,120},{32,0},{40,8},{48,16},{56,24},{64... | collective-permute-start | bytes 786440 | tf_op jit(solution)/shard_map/ppermute | solution.py:32
  133.7 4.5 %collective-permute-start.29 = (bf16[512,512]{1,0:T(8,128)(2,1)}, bf16[512,512]{1,0:T(8,128)(2,1)}, u32[]{:S(2)}, u32[]{:S(2)}) collective-permute-start(bf16[512,512]{1,0:T(8,128)(2,1)} %collective-permute-done.9.rest_15_), channel_id=1, source_target_pairs={{0,96},{8,104},{16,112},{24,120},{32,0},{40,8},{48,16},{56,24},{64... | collective-permute-start | bytes 1572872 | tf_op jit(solution)/shard_map/ppermute | solution.py:32
  146.7 5.3 %project0.1 = (f32[256,512]{1,0:T(8,128)S(1)}, f32[256,512]{1,0:T(8,128)S(1)}) custom-call(s32[8]{0:T(128)S(1)} %stack.51.slots, bf16[512,512]{1,0:T(8,128)(2,1)S(1)} %pad_maximum_fusion.rest_0_, bf16[512,512]{1,0:T(8,128)(2,1)S(1)} %collective-permute-done.11.rest_1_, bf16[512,512]{1,0:T(8,128)(2,1)S(1)} %collective-permute-done.12.rest_2_, ...), custom_call_target="tpu_custom_call" | custom-call | flops 2147483648 | bytes 10485760 | tf_op jit(solution)/shard_map/project0/pallas_call | solution.py:301
  158.6 2.6 %collective-permute-start.31 = (bf16[256,512]{1,0:T(8,128)(2,1)S(1)}, bf16[256,512]{1,0:T(8,128)(2,1)S(1)}, u32[]{:S(2)}, u32[]{:S(2)}) collective-permute-start(bf16[256,512]{1,0:T(8,128)(2,1)S(1)} %slice.82), channel_id=1, source_target_pairs={{0,96},{8,104},{16,112},{24,120},{32,0},{40,8},{48,16},{56,24},{64... | collective-permute-start | bytes 786440 | tf_op jit(solution)/shard_map/ppermute | solution.py:32
  163.6 4.7 %collective-permute-done.30.rest_18_ = bf16[256,512]{1,0:T(8,128)(2,1)S(1)} collective-permute-done((bf16[256,512]{1,0:T(8,128)(2,1)S(1)}, bf16[256,512]{1,0:T(8,128)(2,1)S(1)}, u32[]{:S(2)}, u32[]{:S(2)}) %collective-permute-start.30) | collective-permute-done | bytes 262176 | tf_op jit(solution)/shard_map/ppermute | solution.py:32
  168.8 4.9 %project1.1 = (f32[256,512]{1,0:T(8,128)S(1)}, f32[256,512]{1,0:T(8,128)S(1)}) custom-call(s32[8]{0:T(128)S(1)} %stack.51.slots, bf16[512,512]{1,0:T(8,128)(2,1)S(1)} %pad_maximum_fusion.rest_0_, bf16[512,512]{1,0:T(8,128)(2,1)S(1)} %collective-permute-done.11.rest_1_, bf16[512,512]{1,0:T(8,128)(2,1)S(1)} %collective-permute-done.12.rest_2_, ...), custom_call_target="tpu_custom_call" | custom-call | flops 2147483648 | bytes 10485760 | tf_op jit(solution)/shard_map/project1/pallas_call | solution.py:301
  174.0 3.4 %backward0.1 = (bf16[256,1024]{1,0:T(8,128)(2,1)}, f32[8,256,256]{2,1,0:T(8,128)S(1)}, f32[8,256,256]{2,1,0:T(8,128)S(1)}) custom-call(s32[36]{0:T(128)S(1)} %concatenate.21.info, bf16[2816,1024]{1,0:T(8,128)(2,1)S(1)} %bitcast.24, f32[128,1024]{1,0:T(8,128)S(1)} %copy-done.32, bf16[256,512]{1,0:T(8,128)(2,1)S(1)} %add_convert_fusion.1.grad_ref, ...), custom_call_target="tpu_custom_call" | custom-call | flops 8000000000 | bytes 10485760 | tf_op jit(solution)/shard_map/backward0/pallas_call | solution.py:241
  177.6 3.4 %backward1.1 = (bf16[256,1024]{1,0:T(8,128)(2,1)}, f32[8,256,256]{2,1,0:T(8,128)S(1)}, bf16[8,256,256]{2,1,0:T(8,128)(2,1)S(1)}) custom-call(s32[36]{0:T(128)S(1)} %concatenate.21.info, bf16[2816,1024]{1,0:T(8,128)(2,1)S(1)} %bitcast.22, f32[128,1024]{1,0:T(8,128)S(1)} %copy-done.30, ...), custom_call_target="tpu_custom_call", output_to_operand_aliasing={{0}: (9, {})} | custom-call | flops 8000000000 | bytes 10485760 | tf_op jit(solution)/shard_map/backward1/pallas_call | solution.py:241
  181.0 2.6 %collective-permute-start.36 = (bf16[8,256,256]{2,1,0:T(8,128)(2,1)S(1)}, bf16[8,256,256]{2,1,0:T(8,128)(2,1)S(1)}, u32[]{:S(2)}, u32[]{:S(2)}) collective-permute-start(bf16[8,256,256]{2,1,0:T(8,128)(2,1)S(1)} %get-tuple-element.86), channel_id=1, source_target_pairs={{0,8},{8,0},{16,24},{24,16},{32,40},{40,32},{48,56},{56,48},{64,72... | collective-permute-start | bytes 3145736 | tf_op jit(solution)/shard_map/ppermute | solution.py:32
  186.3 45.8 %all_to_all.5 = bf16[8,256,256]{2,1,0:T(8,128)(2,1)S(1)} all-to-all(bf16[8,256,256]{2,1,0:T(8,128)(2,1)S(1)} %add_convert_fusion), channel_id=1, replica_groups={{0,16,32,48,64,80,96,112},{8,24,40,56,72,88,104,120},{1,17,33,49,65,81,..., dimensions={0} | all-to-all | bytes 2097152 | tf_op jit(solution)/shard_map/all_to_all | solution.py:431
  (177 shorter events, 71.8 us)
Async XLA Ops:
  27.9 19.1 %collective-permute-start.5 = (bf16[4096,128]{1,0:T(8,128)(2,1)}, bf16[4096,128]{1,0:T(8,128)(2,1)}, u32[]{:S(2)}, u32[]{:S(2)}) collective-permute-start(bf16[4096,128]{1,0:T(8,128)(2,1)} %get-tuple-element.93), channel_id=1, source_target_pairs={{0,8},{8,0},{16,24},{24,16},{32,40},{40,32},{48,56},{56,48},{64,72... | collective-permute-start | bytes 3145736 | tf_op jit(solution)/shard_map/ppermute | solution.py:32
  28.0 15.7 %collective-permute-start.6 = (bf16[512,512]{1,0:T(8,128)(2,1)S(1)}, bf16[512,512]{1,0:T(8,128)(2,1)}, u32[]{:S(2)}, u32[]{:S(2)}) collective-permute-start(bf16[512,512]{1,0:T(8,128)(2,1)S(1)} %get-tuple-element.73.rest_10_), channel_id=1, source_target_pairs={{0,32},{8,40},{16,48},{24,56},{32,64},{40,72},{48,80},{56,88},{64,... | collective-permute-start | bytes 1572872 | tf_op jit(solution)/shard_map/ppermute | solution.py:32
  29.2 16.1 %collective-permute-start.7 = (bf16[512,512]{1,0:T(8,128)(2,1)S(1)}, bf16[512,512]{1,0:T(8,128)(2,1)}, u32[]{:S(2)}, u32[]{:S(2)}) collective-permute-start(bf16[512,512]{1,0:T(8,128)(2,1)S(1)} %get-tuple-element.73.rest_10_), channel_id=1, source_target_pairs={{0,96},{8,104},{16,112},{24,120},{32,0},{40,8},{48,16},{56,24},{64... | collective-permute-start | bytes 1572872 | tf_op jit(solution)/shard_map/ppermute | solution.py:32
  31.3 25.5 %collective-permute-start.8 = (bf16[512,512]{1,0:T(8,128)(2,1)S(1)}, bf16[512,512]{1,0:T(8,128)(2,1)}, u32[]{:S(2)}, u32[]{:S(2)}) collective-permute-start(bf16[512,512]{1,0:T(8,128)(2,1)S(1)} %get-tuple-element.73.rest_10_), channel_id=1, source_target_pairs={{0,16},{8,24},{16,0},{24,8},{32,48},{40,56},{48,32},{56,40},{64,80... | collective-permute-start | bytes 1572872 | tf_op jit(solution)/shard_map/ppermute | solution.py:32
  37.9 21.1 %collective-permute-start.9 = (bf16[512,512]{1,0:T(8,128)(2,1)S(1)}, bf16[512,512]{1,0:T(8,128)(2,1)}, u32[]{:S(2)}, u32[]{:S(2)}) collective-permute-start(bf16[512,512]{1,0:T(8,128)(2,1)S(1)} %get-tuple-element.65.rest_10_), channel_id=1, source_target_pairs={{0,16},{8,24},{16,0},{24,8},{32,48},{40,56},{48,32},{56,40},{64,80... | collective-permute-start | bytes 1572872 | tf_op jit(solution)/shard_map/ppermute | solution.py:32
  43.7 16.8 %collective-permute-start.11 = (bf16[512,512]{1,0:T(8,128)(2,1)S(1)}, bf16[512,512]{1,0:T(8,128)(2,1)S(1)}, u32[]{:S(2)}, u32[]{:S(2)}) collective-permute-start(bf16[512,512]{1,0:T(8,128)(2,1)S(1)} %pad_maximum_fusion.rest_0_), channel_id=1, source_target_pairs={{0,1},{1,2},{2,3},{3,0},{4,5},{5,6},{6,7},{7,4},{8,9},{9,10},{10,1... | collective-permute-start | bytes 1572872 | tf_op jit(solution)/shard_map/ppermute | solution.py:40
  45.3 15.2 %collective-permute-start.12 = (bf16[512,512]{1,0:T(8,128)(2,1)S(1)}, bf16[512,512]{1,0:T(8,128)(2,1)S(1)}, u32[]{:S(2)}, u32[]{:S(2)}) collective-permute-start(bf16[512,512]{1,0:T(8,128)(2,1)S(1)} %pad_maximum_fusion.rest_0_), channel_id=1, source_target_pairs={{0,3},{1,0},{2,1},{3,2},{4,7},{5,4},{6,5},{7,6},{8,11},{9,8},{10,9... | collective-permute-start | bytes 1572872 | tf_op jit(solution)/shard_map/ppermute | solution.py:40
  47.0 22.5 %collective-permute-start.13 = (bf16[512,512]{1,0:T(8,128)(2,1)S(1)}, bf16[512,512]{1,0:T(8,128)(2,1)S(1)}, u32[]{:S(2)}, u32[]{:S(2)}) collective-permute-start(bf16[512,512]{1,0:T(8,128)(2,1)S(1)} %pad_maximum_fusion.rest_0_), channel_id=1, source_target_pairs={{0,4},{1,5},{2,6},{3,7},{4,0},{5,1},{6,2},{7,3},{8,12},{9,13},{10,... | collective-permute-start | bytes 1572872 | tf_op jit(solution)/shard_map/ppermute | solution.py:40
  56.8 28.2 %collective-permute-start.18 = (bf16[512,512]{1,0:T(8,128)(2,1)S(1)}, bf16[512,512]{1,0:T(8,128)(2,1)S(1)}, u32[]{:S(2)}, u32[]{:S(2)}) collective-permute-start(bf16[512,512]{1,0:T(8,128)(2,1)S(1)} %get-tuple-element.65.rest_10_), channel_id=1, source_target_pairs={{0,32},{8,40},{16,48},{24,56},{32,64},{40,72},{48,80},{56,88},{64,... | collective-permute-start | bytes 1572872 | tf_op jit(solution)/shard_map/ppermute | solution.py:32
  59.0 26.6 %collective-permute-start.19 = (bf16[512,512]{1,0:T(8,128)(2,1)S(1)}, bf16[512,512]{1,0:T(8,128)(2,1)S(1)}, u32[]{:S(2)}, u32[]{:S(2)}) collective-permute-start(bf16[512,512]{1,0:T(8,128)(2,1)S(1)} %get-tuple-element.65.rest_10_), channel_id=1, source_target_pairs={{0,96},{8,104},{16,112},{24,120},{32,0},{40,8},{48,16},{56,24},{64... | collective-permute-start | bytes 1572872 | tf_op jit(solution)/shard_map/ppermute | solution.py:32
  70.5 29.3 %collective-permute-start.16 = (bf16[256,512]{1,0:T(8,128)(2,1)S(1)}, bf16[256,512]{1,0:T(8,128)(2,1)S(1)}, u32[]{:S(2)}, u32[]{:S(2)}) collective-permute-start(bf16[256,512]{1,0:T(8,128)(2,1)S(1)} %slice.67), channel_id=1, source_target_pairs={{0,32},{8,40},{16,48},{24,56},{32,64},{40,72},{48,80},{56,88},{64,... | collective-permute-start | bytes 786440 | tf_op jit(solution)/shard_map/ppermute | solution.py:32
  71.5 30.6 %collective-permute-start.17 = (bf16[256,512]{1,0:T(8,128)(2,1)S(1)}, bf16[256,512]{1,0:T(8,128)(2,1)S(1)}, u32[]{:S(2)}, u32[]{:S(2)}) collective-permute-start(bf16[256,512]{1,0:T(8,128)(2,1)S(1)} %slice.68), channel_id=1, source_target_pairs={{0,96},{8,104},{16,112},{24,120},{32,0},{40,8},{48,16},{56,24},{64... | collective-permute-start | bytes 786440 | tf_op jit(solution)/shard_map/ppermute | solution.py:32
  74.8 29.0 %collective-permute-start.22 = (bf16[256,512]{1,0:T(8,128)(2,1)S(1)}, bf16[256,512]{1,0:T(8,128)(2,1)S(1)}, u32[]{:S(2)}, u32[]{:S(2)}) collective-permute-start(bf16[256,512]{1,0:T(8,128)(2,1)S(1)} %slice.69), channel_id=1, source_target_pairs={{0,1},{1,2},{2,3},{3,0},{4,5},{5,6},{6,7},{7,4},{8,9},{9,10},{10,1... | collective-permute-start | bytes 786440 | tf_op jit(solution)/shard_map/ppermute | solution.py:40
  85.0 36.1 %collective-permute-start.14 = (bf16[512,512]{1,0:T(8,128)(2,1)}, bf16[512,512]{1,0:T(8,128)(2,1)S(1)}, u32[]{:S(2)}, u32[]{:S(2)}) collective-permute-start(bf16[512,512]{1,0:T(8,128)(2,1)} %collective-permute-done.8.rest_15_), channel_id=1, source_target_pairs={{0,32},{8,40},{16,48},{24,56},{32,64},{40,72},{48,80},{56,88},{64,... | collective-permute-start | bytes 1572872 | tf_op jit(solution)/shard_map/ppermute | solution.py:32
  85.6 35.5 %collective-permute-start.15 = (bf16[512,512]{1,0:T(8,128)(2,1)}, bf16[512,512]{1,0:T(8,128)(2,1)S(1)}, u32[]{:S(2)}, u32[]{:S(2)}) collective-permute-start(bf16[512,512]{1,0:T(8,128)(2,1)} %collective-permute-done.8.rest_15_), channel_id=1, source_target_pairs={{0,96},{8,104},{16,112},{24,120},{32,0},{40,8},{48,16},{56,24},{64... | collective-permute-start | bytes 1572872 | tf_op jit(solution)/shard_map/ppermute | solution.py:32
  100.5 20.6 %collective-permute-start.20 = (bf16[512,512]{1,0:T(8,128)(2,1)S(1)}, bf16[512,512]{1,0:T(8,128)(2,1)S(1)}, u32[]{:S(2)}, u32[]{:S(2)}) collective-permute-start(bf16[512,512]{1,0:T(8,128)(2,1)S(1)} %collective-permute-done.13.rest_5_), channel_id=1, source_target_pairs={{0,1},{1,2},{2,3},{3,0},{4,5},{5,6},{6,7},{7,4},{8,9},{9,10},{10,1... | collective-permute-start | bytes 1572872 | tf_op jit(solution)/shard_map/ppermute | solution.py:40
  102.1 19.0 %collective-permute-start.21 = (bf16[512,512]{1,0:T(8,128)(2,1)S(1)}, bf16[512,512]{1,0:T(8,128)(2,1)S(1)}, u32[]{:S(2)}, u32[]{:S(2)}) collective-permute-start(bf16[512,512]{1,0:T(8,128)(2,1)S(1)} %collective-permute-done.13.rest_5_), channel_id=1, source_target_pairs={{0,3},{1,0},{2,1},{3,2},{4,7},{5,4},{6,5},{7,6},{8,11},{9,8},{10,9... | collective-permute-start | bytes 1572872 | tf_op jit(solution)/shard_map/ppermute | solution.py:40
  103.8 17.3 %collective-permute-start.23 = (bf16[256,512]{1,0:T(8,128)(2,1)S(1)}, bf16[256,512]{1,0:T(8,128)(2,1)S(1)}, u32[]{:S(2)}, u32[]{:S(2)}) collective-permute-start(bf16[256,512]{1,0:T(8,128)(2,1)S(1)} %slice.70), channel_id=1, source_target_pairs={{0,3},{1,0},{2,1},{3,2},{4,7},{5,4},{6,5},{7,6},{8,11},{9,8},{10,9... | collective-permute-start | bytes 786440 | tf_op jit(solution)/shard_map/ppermute | solution.py:40
  123.2 15.1 %collective-permute-start.25 = (bf16[256,512]{1,0:T(8,128)(2,1)}, bf16[256,512]{1,0:T(8,128)(2,1)}, u32[]{:S(2)}, u32[]{:S(2)}) collective-permute-start(bf16[256,512]{1,0:T(8,128)(2,1)} %slice.72), channel_id=1, source_target_pairs={{0,3},{1,0},{2,1},{3,2},{4,7},{5,4},{6,5},{7,6},{8,11},{9,8},{10,9... | collective-permute-start | bytes 786440 | tf_op jit(solution)/shard_map/ppermute | solution.py:40
  125.9 13.8 %collective-permute-start.33 = (bf16[256,512]{1,0:T(8,128)(2,1)}, bf16[256,512]{1,0:T(8,128)(2,1)}, u32[]{:S(2)}, u32[]{:S(2)}) collective-permute-start(bf16[256,512]{1,0:T(8,128)(2,1)} %slice.77), channel_id=1, source_target_pairs={{0,32},{8,40},{16,48},{24,56},{32,64},{40,72},{48,80},{56,88},{64,... | collective-permute-start | bytes 786440 | tf_op jit(solution)/shard_map/ppermute | solution.py:32
  126.6 13.1 %collective-permute-start.34 = (bf16[256,512]{1,0:T(8,128)(2,1)}, bf16[256,512]{1,0:T(8,128)(2,1)}, u32[]{:S(2)}, u32[]{:S(2)}) collective-permute-start(bf16[256,512]{1,0:T(8,128)(2,1)} %slice.78), channel_id=1, source_target_pairs={{0,96},{8,104},{16,112},{24,120},{32,0},{40,8},{48,16},{56,24},{64... | collective-permute-start | bytes 786440 | tf_op jit(solution)/shard_map/ppermute | solution.py:32
  133.0 22.9 %collective-permute-start.28 = (bf16[512,512]{1,0:T(8,128)(2,1)}, bf16[512,512]{1,0:T(8,128)(2,1)}, u32[]{:S(2)}, u32[]{:S(2)}) collective-permute-start(bf16[512,512]{1,0:T(8,128)(2,1)} %collective-permute-done.9.rest_15_), channel_id=1, source_target_pairs={{0,32},{8,40},{16,48},{24,56},{32,64},{40,72},{48,80},{56,88},{64,... | collective-permute-start | bytes 1572872 | tf_op jit(solution)/shard_map/ppermute | solution.py:32
  133.7 23.9 %collective-permute-start.29 = (bf16[512,512]{1,0:T(8,128)(2,1)}, bf16[512,512]{1,0:T(8,128)(2,1)}, u32[]{:S(2)}, u32[]{:S(2)}) collective-permute-start(bf16[512,512]{1,0:T(8,128)(2,1)} %collective-permute-done.9.rest_15_), channel_id=1, source_target_pairs={{0,96},{8,104},{16,112},{24,120},{32,0},{40,8},{48,16},{56,24},{64... | collective-permute-start | bytes 1572872 | tf_op jit(solution)/shard_map/ppermute | solution.py:32
  152.0 21.8 %collective-permute-start.35 = (f32[256,512]{1,0:T(8,128)S(1)}, f32[256,512]{1,0:T(8,128)S(1)}, u32[]{:S(2)}, u32[]{:S(2)}) collective-permute-start(f32[256,512]{1,0:T(8,128)S(1)} %get-tuple-element.80), channel_id=1, source_target_pairs={{0,8},{8,0},{16,24},{24,16},{32,40},{40,32},{48,56},{56,48},{64,72... | collective-permute-start | bytes 1572872 | tf_op jit(solution)/shard_map/ppermute | solution.py:32
  (52 other events, 477.6 us)

commit v4 on v3

--- a/solution.py
+++ b/solution.py
@@ -261,35 +261,25 @@
     )(info, probs, outs, grads, queries, kv, kv, *carried)
 
 
-def project_kernel(layout, tokens, slots, *rest):
-    count = sum(len(sizes) for both in layout for sizes in both)
-    pieces, (own_ref, other_ref, grad, weight, grad_sem, weight_sem) = rest[:count], rest[count:]
-    pieces = list(pieces)
-    copies = []
-    for target, sems, chips in ((grad, grad_sem, layout[0]), (weight, weight_sem, layout[1])):
-        lists, k = [], 0
-        for i, sizes in enumerate(chips):
-            at, one = 0, []
-            for size in sizes:
-                copy = pltpu.make_async_copy(pieces.pop(0), target.at[i, pl.ds(at, size)], sems.at[k])
-                copy.start()
-                one.append(copy)
-                at, k = at + size, k + 1
-            lists.append(one)
-        copies.append(lists)
-    for one in copies[0]:
-        for copy in one:
-            copy.wait()
-    half = tokens // 2
-    for i, one in enumerate(copies[1]):
-        for copy in one:
-            copy.wait()
-        for ref, at in ((own_ref, 0), (other_ref, half)):
-            term = dot_t(grad[slots[i], at : at + half, :], weight[i])
-            if i == 0:
-                ref[...] = term
-            else:
-                ref[...] += term
+def project_kernel(layout, slots, *rest):
+    *pieces, own_ref, other_ref, grad = rest
+    at_piece = 0
+    half = own_ref.shape[0]
+    for i, sizes in enumerate(layout[0]):
+        at = 0
+        for size in sizes:
+            grad[i, at : at + size, :] = pieces[at_piece][...]
+            at, at_piece = at + size, at_piece + 1
+    for i, sizes in enumerate(layout[1]):
+        at = 0
+        for size in sizes:
+            for ref, row in ((own_ref, 0), (other_ref, half)):
+                term = dot_t(grad[slots[i], row : row + half, :], pieces[at_piece][...])
+                if i == 0:
+                    ref[:, at : at + size] = term
+                else:
+                    ref[:, at : at + size] += term
+            at, at_piece = at + size, at_piece + 1
 
 
 def project(part, slots, grads, weights):
@@ -299,18 +289,13 @@
     depth, chips = flat[0].shape[1], len(weights)
     half = jax.ShapeDtypeStruct((tokens // 2, features), F32)
     return pl.pallas_call(
-        functools.partial(project_kernel, layout, tokens),
+        functools.partial(project_kernel, layout),
         in_specs=[pl.BlockSpec(memory_space=pltpu.SMEM)]
-        + [pl.BlockSpec(memory_space=pl.ANY)] * len(flat),
+        + [pl.BlockSpec(memory_space=pltpu.VMEM)] * len(flat),
         out_specs=[pl.BlockSpec(memory_space=pltpu.VMEM)] * 2,
         out_shape=[half, half],
-        scratch_shapes=[
-            pltpu.VMEM((chips, tokens, depth), BF16),
-            pltpu.VMEM((chips, features, depth), BF16),
-            pltpu.SemaphoreType.DMA((sum(len(sizes) for sizes in layout[0]),)),
-            pltpu.SemaphoreType.DMA((sum(len(sizes) for sizes in layout[1]),)),
-        ],
-        compiler_params=pltpu.CompilerParams(vmem_limit_bytes=16 * 2**20),
+        scratch_shapes=[pltpu.VMEM((chips, tokens, depth), BF16)],
+        compiler_params=pltpu.CompilerParams(vmem_limit_bytes=20 * 2**20),
         cost_estimate=pl.CostEstimate(
             flops=2 * tokens * features * depth * chips,
             bytes_accessed=10 * 2**20,
@@ -350,53 +335,52 @@
     other = lax.dynamic_slice_in_dim(grad_out, (1 - core) * depth, depth, 1)
     chip_grad = jnp.concatenate([mine, dp_move(other, 0, 0, 1)], axis=0)
 
+    size = out_weight.shape[0] // CHUNKS
+    own = [out_weight[j * size : (j + 1) * size] for j in range(CHUNKS)]
+
+    def both(move, block):
+        return block, move(block, 1), move(block, -1)
+
+    def far(move, ring):
+        half = ring[0].shape[0] // 2
+        return move(ring[1][:half], 1), move(ring[2][half:], -1)
+
+    def along_x(block, step):
+        return dp_move(block, step, 0, 0)
+
+    def along_y(block, step):
+        return tensor_move(block, 0, step)
+
     kept = jnp.where(core == 0, keys, values)
     got = dp_move(jnp.where(core == 0, values, keys), 0, 0, 1)
     chip = jnp.concatenate([kept, got], axis=0)
+    ring00 = both(along_x, own[0])
+    grad0 = both(along_y, chip_grad)
+    grad_pair = tensor_move(chip_grad, 1, 0)
     pair = jnp.concatenate([chip, dp_move(chip, 0, 1, 0)], axis=0)
+    pair, ring00, grad0, grad_pair = lax.optimization_barrier((pair, ring00, grad0, grad_pair))
+
     ring = jnp.concatenate(
         [pair, dp_move(pair, 1, 0, 0), dp_move(pair, -1, 0, 0), dp_move(pair, 2, 0, 0)], axis=0
     )
+    paired = [dp_move(block, 0, 1, 0) for block in own]
+    grad1 = both(along_y, grad_pair)
+    grad_far0 = far(along_y, grad0)
+    ring, paired, grad1, grad_far0 = lax.optimization_barrier((ring, paired, grad1, grad_far0))
     kv = jnp.concatenate([ring, dp_move(ring, 0, 0, 1)], axis=0)
-
-    size = out_weight.shape[0] // CHUNKS
-    own = [out_weight[j * size : (j + 1) * size] for j in range(CHUNKS)]
-
-    def both(move, block):
-        return block, move(block, 1), move(block, -1)
-
-    def far(move, ring):
-        half = ring[0].shape[0] // 2
-        return move(ring[1][:half], 1), move(ring[2][half:], -1)
-
-    def along_x(block, step):
-        return dp_move(block, step, 0, 0)
-
-    def along_y(block, step):
-        return tensor_move(block, 0, step)
-
-    paired = [dp_move(block, 0, 1, 0) for block in own]
-    ring00 = both(along_x, own[0])
-    grad0 = both(along_y, chip_grad)
-    grad_pair = tensor_move(chip_grad, 1, 0)
-    kv, ring00, paired, grad0, grad_pair = lax.optimization_barrier(
-        (kv, ring00, paired, grad0, grad_pair)
-    )
 
     ring01 = both(along_x, paired[0])
     far00 = far(along_x, ring00)
     ring10 = both(along_x, own[1])
-    grad1 = both(along_y, grad_pair)
-    grad_far0 = far(along_y, grad0)
+    grad_far1 = far(along_y, grad1)
     first_part = forward(0, info, query_pos, query_start, queries, kv)
     second_part = forward(1, info, query_pos, query_start, after(queries, first_part[1]), kv)
     parts = [first_part, second_part]
-    parts, ring01, far00, ring10, grad1, grad_far0 = lax.optimization_barrier(
-        (parts, ring01, far00, ring10, grad1, grad_far0)
+    parts, ring01, far00, ring10, grad_far1 = lax.optimization_barrier(
+        (parts, ring01, far00, ring10, grad_far1)
     )
 
     far01 = far(along_x, ring01)
-    grad_far1 = far(along_y, grad1)
     ring11 = both(along_x, paired[1])
     far10 = far(along_x, ring10)
 
@@ -423,6 +407,7 @@
     grad_queries, own_sums, other_sums = one_part(0, weights, ())
     carried = (own_sums, other_sums, grad_queries)
     far11 = far(along_x, ring11)
+    far11 = after(far11, grad_queries)
     weights = [[block] for block in ring10] + [far10] + [[block] for block in ring11] + [far11]
     grad_queries, own_sums, other_sums = one_part(1, weights, carried)
 

time: 233 us -> 224 us (0.961)
  waiting for transfers between devices: 49.8 us -> 34.1 us
  starting transfers between devices: 70 us -> 81.3 us
  blocking collectives: 45.8 us -> 38.5 us
  local copies, waits for them, and re-layouts: 32.5 us -> 35.3 us
  Pallas kernels: 24.2 us -> 21.8 us
    ppermute x28, starting transfers between devices: 57.1 us -> 67.1 us  [dp_move(): return lax.ppermute(value, 'dp', pairs)]
    ppermute x28, waiting for transfers between devices: 30.8 us -> 22.5 us  [dp_move(): return lax.ppermute(value, 'dp', pairs)]
    ppermute x9, waiting for transfers between devices: 18.9 us -> 11.6 us  [tensor_move(): return lax.ppermute(value, 'tensor', pairs)]
    all_to_all x1, blocking collectives: 45.8 us -> 38.5 us  [local(): lax.all_to_all(chip_sums, 'dp', 0, 0, axis_index_groups=groups, tiled=True)]
    unnamed x83, local copies, waits for them, and re-layouts: 19.4 us -> 23.3 us
    pallas_call x2, Pallas kernels: 10.2 us -> 7.87 us  [project(): pl.pallas_call(functools.partial(project_kernel, layout), in_specs=[pl.Bl...]
  transfers between devices with their start and end apart: 37 -> 37, of which waited for: 16 -> 11; matrix products, arithmetic and copies ran while one was open for 7% -> 7% of each run, Pallas kernels for 9% -> 6%
where the time goes in v4:
time: 224 us; the launch traced here: 223 us
  starting transfers between devices  81.3 us (36%)
  blocking collectives  38.5 us (17%)
  local copies, waits for them, and re-layouts  35.3 us (16%)
  waiting for transfers between devices  34.1 us (15%)
  Pallas kernels  21.8 us (10%)
  between operations  7.04 us (3%)
  other arithmetic  4.83 us (2%)
    ppermute x28, starting transfers between devices, dp_move(): return lax.ppermute(value, 'dp', pairs)  67.1 us
    all_to_all x1, blocking collectives, local(): lax.all_to_all(chip_sums, 'dp', 0, 0, axis_index_groups=groups, tiled=True)  38.5 us
    unnamed x83, local copies, waits for them, and re-layouts  23.3 us
    ppermute x28, waiting for transfers between devices, dp_move(): return lax.ppermute(value, 'dp', pairs)  22.5 us
    ppermute x9, starting transfers between devices, tensor_move(): return lax.ppermute(value, 'tensor', pairs)  14.2 us
    ppermute x9, waiting for transfers between devices, tensor_move(): return lax.ppermute(value, 'tensor', pairs)  11.6 us
    pallas_call x2, Pallas kernels, project(): pl.pallas_call(functools.partial(project_kernel, layout), in_specs=[pl.Bl...  7.87 us
    pallas_call x2, Pallas kernels, forward(): pl.pallas_call(forward_kernel, grid_spec=pltpu.PrefetchScalarGridSpec(num...  7.16 us
  transfers between devices with their start and end apart: 37, of which 11 were waited for; matrix products, arithmetic and copies ran while one was open for 7% of the time, Pallas kernels for 6%

profile of v4, /device:TPU:0, one launch (start us, length us, event | category | flops | bytes accessed | tf_op | source)
XLA Modules:
  0.0 222.9 jit_solution(3921130471441136390)
XLA Ops:
  7.0 4.0 %collective-permute-start.1 = (bf16[512,128]{1,0:T(8,128)(2,1)S(1)}, bf16[512,128]{1,0:T(8,128)(2,1)S(1)}, u32[]{:S(2)}, u32[]{:S(2)}) collective-permute-start(bf16[512,128]{1,0:T(8,128)(2,1)S(1)} %pad_maximum_fusion.3), channel_id=1, source_target_pairs={{0,16},{8,24},{16,0},{24,8},{32,48},{40,56},{48,32},{56,40},{64,80... | collective-permute-start | bytes 393224 | tf_op jit(solution)/shard_map/ppermute | solution.py:32
  17.0 3.4 %collective-permute-done.2.rest_11_ = bf16[512,512]{1,0:T(8,128)(2,1)S(1)} collective-permute-done((bf16[512,512]{1,0:T(8,128)(2,1)S(1)}, bf16[512,512]{1,0:T(8,128)(2,1)S(1)}, u32[]{:S(2)}, u32[]{:S(2)}) %collective-permute-start.2) | collective-permute-done | bytes 524320 | tf_op jit(solution)/shard_map/ppermute | solution.py:32
  20.4 4.0 %collective-permute-start.11 = (bf16[512,512]{1,0:T(8,128)(2,1)S(1)}, bf16[512,512]{1,0:T(8,128)(2,1)S(1)}, u32[]{:S(2)}, u32[]{:S(2)}) collective-permute-start(bf16[512,512]{1,0:T(8,128)(2,1)S(1)} %get-tuple-element.79.rest_10_), channel_id=1, source_target_pairs={{0,16},{8,24},{16,0},{24,8},{32,48},{40,56},{48,32},{56,40},{64,80... | collective-permute-start | bytes 1572872 | tf_op jit(solution)/shard_map/ppermute | solution.py:32
  27.1 3.8 %collective-permute-done.7.rest_5_ = bf16[512,512]{1,0:T(8,128)(2,1)S(1)} collective-permute-done((bf16[512,512]{1,0:T(8,128)(2,1)S(1)}, bf16[512,512]{1,0:T(8,128)(2,1)S(1)}, u32[]{:S(2)}, u32[]{:S(2)}) %collective-permute-start.7) | collective-permute-done | bytes 524320 | tf_op jit(solution)/shard_map/ppermute | solution.py:40
  38.4 4.9 %collective-permute-done.11.rest_15_ = bf16[512,512]{1,0:T(8,128)(2,1)S(1)} collective-permute-done((bf16[512,512]{1,0:T(8,128)(2,1)S(1)}, bf16[512,512]{1,0:T(8,128)(2,1)S(1)}, u32[]{:S(2)}, u32[]{:S(2)}) %collective-permute-start.11) | collective-permute-done | bytes 524320 | tf_op jit(solution)/shard_map/ppermute | solution.py:32
  47.3 2.9 %collective-permute-start.16 = (bf16[256,512]{1,0:T(8,128)(2,1)S(1)}, bf16[256,512]{1,0:T(8,128)(2,1)S(1)}, u32[]{:S(2)}, u32[]{:S(2)}) collective-permute-start(bf16[256,512]{1,0:T(8,128)(2,1)S(1)} %slice.68), channel_id=1, source_target_pairs={{0,3},{1,0},{2,1},{3,2},{4,7},{5,4},{6,5},{7,6},{8,11},{9,8},{10,9... | collective-permute-start | bytes 786440 | tf_op jit(solution)/shard_map/ppermute | solution.py:40
  53.9 5.8 %collective-permute-done.15.rest_3_ = bf16[256,512]{1,0:T(8,128)(2,1)S(1)} collective-permute-done((bf16[256,512]{1,0:T(8,128)(2,1)S(1)}, bf16[256,512]{1,0:T(8,128)(2,1)S(1)}, u32[]{:S(2)}, u32[]{:S(2)}) %collective-permute-start.15) | collective-permute-done | bytes 262176 | tf_op jit(solution)/shard_map/ppermute | solution.py:40
  71.9 3.0 %collective-permute-start.21 = (bf16[256,512]{1,0:T(8,128)(2,1)S(1)}, bf16[256,512]{1,0:T(8,128)(2,1)S(1)}, u32[]{:S(2)}, u32[]{:S(2)}) collective-permute-start(bf16[256,512]{1,0:T(8,128)(2,1)S(1)} %slice.70), channel_id=1, source_target_pairs={{0,96},{8,104},{16,112},{24,120},{32,0},{40,8},{48,16},{56,24},{64... | collective-permute-start | bytes 786440 | tf_op jit(solution)/shard_map/ppermute | solution.py:32
  77.8 3.6 %forward0.1 = (bf16[2816,1024]{1,0:T(8,128)(2,1)S(1)}, f32[128,1024]{1,0:T(8,128)S(1)}) custom-call(s32[36]{0:T(128)S(1)} %concatenate.19.info, s32[1,256]{1,0:T(1,128)S(1)} %iota_add_fusion.pos_ref, s32[1,256]{1,0:T(1,128)S(1)} %bitcast.19, bf16[256,1024]{1,0:T(8,128)(2,1)S(1)} %copy-done.28, ...), custom_call_target="tpu_custom_call" | custom-call | flops 16000000000 | bytes 10485760 | tf_op jit(solution)/shard_map/forward0/pallas_call | solution.py:119
  84.6 5.0 %collective-permute-start.19 = (bf16[512,512]{1,0:T(8,128)(2,1)S(1)}, bf16[512,512]{1,0:T(8,128)(2,1)S(1)}, u32[]{:S(2)}, u32[]{:S(2)}) collective-permute-start(bf16[512,512]{1,0:T(8,128)(2,1)S(1)} %copy-done.20), channel_id=1, source_target_pairs={{0,96},{8,104},{16,112},{24,120},{32,0},{40,8},{48,16},{56,24},{64... | collective-permute-start | bytes 1572872 | tf_op jit(solution)/shard_map/ppermute | solution.py:32
  90.7 2.9 %collective-permute-start.25 = (bf16[256,512]{1,0:T(8,128)(2,1)S(1)}, bf16[256,512]{1,0:T(8,128)(2,1)S(1)}, u32[]{:S(2)}, u32[]{:S(2)}) collective-permute-start(bf16[256,512]{1,0:T(8,128)(2,1)S(1)} %slice.72), channel_id=1, source_target_pairs={{0,3},{1,0},{2,1},{3,2},{4,7},{5,4},{6,5},{7,6},{8,11},{9,8},{10,9... | collective-permute-start | bytes 786440 | tf_op jit(solution)/shard_map/ppermute | solution.py:40
  93.6 3.6 %forward1.1 = (bf16[2816,1024]{1,0:T(8,128)(2,1)S(1)}, f32[128,1024]{1,0:T(8,128)S(1)}) custom-call(s32[36]{0:T(128)S(1)} %concatenate.19.info, s32[1,256]{1,0:T(1,128)S(1)} %iota_add_fusion.pos_ref, s32[1,256]{1,0:T(1,128)S(1)} %bitcast.20, bf16[256,1024]{1,0:T(8,128)(2,1)S(1)} %copy-done.28, ...), custom_call_target="tpu_custom_call" | custom-call | flops 16000000000 | bytes 10485760 | tf_op jit(solution)/shard_map/forward1/pallas_call | solution.py:119
  106.0 8.4 %collective-permute-start.32 = (bf16[256,512]{1,0:T(8,128)(2,1)}, bf16[256,512]{1,0:T(8,128)(2,1)}, u32[]{:S(2)}, u32[]{:S(2)}) collective-permute-start(bf16[256,512]{1,0:T(8,128)(2,1)} %slice.77), channel_id=1, source_target_pairs={{0,32},{8,40},{16,48},{24,56},{32,64},{40,72},{48,80},{56,88},{64,... | collective-permute-start | bytes 786440 | tf_op jit(solution)/shard_map/ppermute | solution.py:32
  115.2 3.3 %collective-permute-start.33 = (bf16[256,512]{1,0:T(8,128)(2,1)}, bf16[256,512]{1,0:T(8,128)(2,1)}, u32[]{:S(2)}, u32[]{:S(2)}) collective-permute-start(bf16[256,512]{1,0:T(8,128)(2,1)} %slice.78), channel_id=1, source_target_pairs={{0,96},{8,104},{16,112},{24,120},{32,0},{40,8},{48,16},{56,24},{64... | collective-permute-start | bytes 786440 | tf_op jit(solution)/shard_map/ppermute | solution.py:32
  118.5 12.2 %collective-permute-start.28 = (bf16[512,512]{1,0:T(8,128)(2,1)}, bf16[512,512]{1,0:T(8,128)(2,1)S(1)}, u32[]{:S(2)}, u32[]{:S(2)}) collective-permute-start(bf16[512,512]{1,0:T(8,128)(2,1)} %collective-permute-done.12.rest_15_), channel_id=1, source_target_pairs={{0,32},{8,40},{16,48},{24,56},{32,64},{40,72},{48,80},{56,88},{64,... | collective-permute-start | bytes 1572872 | tf_op jit(solution)/shard_map/ppermute | solution.py:32
  131.3 5.0 %collective-permute-done.33.rest_19_ = bf16[256,512]{1,0:T(8,128)(2,1)} collective-permute-done((bf16[256,512]{1,0:T(8,128)(2,1)}, bf16[256,512]{1,0:T(8,128)(2,1)}, u32[]{:S(2)}, u32[]{:S(2)}) %collective-permute-start.33) | collective-permute-done | bytes 262176 | tf_op jit(solution)/shard_map/ppermute | solution.py:32
  147.3 3.8 %project0.1 = (f32[256,512]{1,0:T(8,128)S(1)}, f32[256,512]{1,0:T(8,128)S(1)}) custom-call(s32[8]{0:T(128)S(1)} %stack.51.slots, bf16[512,512]{1,0:T(8,128)(2,1)S(1)} %pad_maximum_fusion.1.rest_0_, bf16[512,512]{1,0:T(8,128)(2,1)S(1)} %collective-permute-done.5.rest_1_, bf16[512,512]{1,0:T(8,128)(2,1)S(1)} %collective-permute-done.6.rest_2_, ...), custom_call_target="tpu_custom_call" | custom-call | flops 2147483648 | bytes 10485760 | tf_op jit(solution)/shard_map/project0/pallas_call | solution.py:291
  151.1 3.5 %collective-permute-start.34 = (f32[256,512]{1,0:T(8,128)S(1)}, f32[256,512]{1,0:T(8,128)S(1)}, u32[]{:S(2)}, u32[]{:S(2)}) collective-permute-start(f32[256,512]{1,0:T(8,128)S(1)} %get-tuple-element.86), channel_id=1, source_target_pairs={{0,8},{8,0},{16,24},{24,16},{32,40},{40,32},{48,56},{56,48},{64,72... | collective-permute-start | bytes 1572872 | tf_op jit(solution)/shard_map/ppermute | solution.py:32
  160.6 2.8 %collective-permute-start.27 = (bf16[256,512]{1,0:T(8,128)(2,1)S(1)}, bf16[256,512]{1,0:T(8,128)(2,1)S(1)}, u32[]{:S(2)}, u32[]{:S(2)}) collective-permute-start(bf16[256,512]{1,0:T(8,128)(2,1)S(1)} %slice.74), channel_id=1, source_target_pairs={{0,96},{8,104},{16,112},{24,120},{32,0},{40,8},{48,16},{56,24},{64... | collective-permute-start | bytes 786440 | tf_op jit(solution)/shard_map/ppermute | solution.py:32
  163.6 3.4 %backward0.1 = (bf16[256,1024]{1,0:T(8,128)(2,1)}, f32[8,256,256]{2,1,0:T(8,128)S(1)}, f32[8,256,256]{2,1,0:T(8,128)S(1)}) custom-call(s32[36]{0:T(128)S(1)} %concatenate.19.info, bf16[2816,1024]{1,0:T(8,128)(2,1)S(1)} %copy-done.32, f32[128,1024]{1,0:T(8,128)S(1)} %copy-done.36, bf16[256,512]{1,0:T(8,128)(2,1)S(1)} %add_convert_fusion.2.grad_ref, ...), custom_call_target="tpu_custom_call" | custom-call | flops 8000000000 | bytes 10485760 | tf_op jit(solution)/shard_map/backward0/pallas_call | solution.py:241
  166.9 2.8 %collective-permute-done.26.rest_13_ = bf16[256,512]{1,0:T(8,128)(2,1)S(1)} collective-permute-done((bf16[256,512]{1,0:T(8,128)(2,1)S(1)}, bf16[256,512]{1,0:T(8,128)(2,1)S(1)}, u32[]{:S(2)}, u32[]{:S(2)}) %collective-permute-start.26) | collective-permute-done | bytes 262176 | tf_op jit(solution)/shard_map/ppermute | solution.py:32
  170.1 4.1 %project1.1 = (f32[256,512]{1,0:T(8,128)S(1)}, f32[256,512]{1,0:T(8,128)S(1)}) custom-call(s32[8]{0:T(128)S(1)} %stack.51.slots, bf16[512,512]{1,0:T(8,128)(2,1)S(1)} %pad_maximum_fusion.1.rest_0_, bf16[512,512]{1,0:T(8,128)(2,1)S(1)} %collective-permute-done.5.rest_1_, bf16[512,512]{1,0:T(8,128)(2,1)S(1)} %collective-permute-done.6.rest_2_, ...), custom_call_target="tpu_custom_call" | custom-call | flops 2147483648 | bytes 10485760 | tf_op jit(solution)/shard_map/project1/pallas_call | solution.py:291
  176.4 3.4 %backward1.1 = (bf16[256,1024]{1,0:T(8,128)(2,1)}, f32[8,256,256]{2,1,0:T(8,128)S(1)}, bf16[8,256,256]{2,1,0:T(8,128)(2,1)S(1)}) custom-call(s32[36]{0:T(128)S(1)} %concatenate.19.info, bf16[2816,1024]{1,0:T(8,128)(2,1)S(1)} %bitcast.22, f32[128,1024]{1,0:T(8,128)S(1)} %copy-done.34, ...), custom_call_target="tpu_custom_call", output_to_operand_aliasing={{0}: (9, {})} | custom-call | flops 8000000000 | bytes 10485760 | tf_op jit(solution)/shard_map/backward1/pallas_call | solution.py:241
  183.6 38.5 %all_to_all.5 = bf16[8,256,256]{2,1,0:T(8,128)(2,1)S(1)} all-to-all(bf16[8,256,256]{2,1,0:T(8,128)(2,1)S(1)} %add_convert_fusion), channel_id=1, replica_groups={{0,16,32,48,64,80,96,112},{8,24,40,56,72,88,104,120},{1,17,33,49,65,81,..., dimensions={0} | all-to-all | bytes 2097152 | tf_op jit(solution)/shard_map/all_to_all | solution.py:416
  (176 shorter events, 77.8 us)
Async XLA Ops:
  5.4 15.1 %collective-permute-start.2 = (bf16[512,512]{1,0:T(8,128)(2,1)S(1)}, bf16[512,512]{1,0:T(8,128)(2,1)S(1)}, u32[]{:S(2)}, u32[]{:S(2)}) collective-permute-start(bf16[512,512]{1,0:T(8,128)(2,1)S(1)} %get-tuple-element.79.rest_10_), channel_id=1, source_target_pairs={{0,32},{8,40},{16,48},{24,56},{32,64},{40,72},{48,80},{56,88},{64,... | collective-permute-start | bytes 1572872 | tf_op jit(solution)/shard_map/ppermute | solution.py:32
  10.9 14.2 %collective-permute-start.3 = (bf16[512,512]{1,0:T(8,128)(2,1)S(1)}, bf16[512,512]{1,0:T(8,128)(2,1)S(1)}, u32[]{:S(2)}, u32[]{:S(2)}) collective-permute-start(bf16[512,512]{1,0:T(8,128)(2,1)S(1)} %get-tuple-element.79.rest_10_), channel_id=1, source_target_pairs={{0,96},{8,104},{16,112},{24,120},{32,0},{40,8},{48,16},{56,24},{64... | collective-permute-start | bytes 1572872 | tf_op jit(solution)/shard_map/ppermute | solution.py:32
  12.7 14.4 %collective-permute-start.5 = (bf16[512,512]{1,0:T(8,128)(2,1)S(1)}, bf16[512,512]{1,0:T(8,128)(2,1)S(1)}, u32[]{:S(2)}, u32[]{:S(2)}) collective-permute-start(bf16[512,512]{1,0:T(8,128)(2,1)S(1)} %pad_maximum_fusion.1.rest_0_), channel_id=1, source_target_pairs={{0,1},{1,2},{2,3},{3,0},{4,5},{5,6},{6,7},{7,4},{8,9},{9,10},{10,1... | collective-permute-start | bytes 1572872 | tf_op jit(solution)/shard_map/ppermute | solution.py:40
  16.0 14.9 %collective-permute-start.7 = (bf16[512,512]{1,0:T(8,128)(2,1)S(1)}, bf16[512,512]{1,0:T(8,128)(2,1)S(1)}, u32[]{:S(2)}, u32[]{:S(2)}) collective-permute-start(bf16[512,512]{1,0:T(8,128)(2,1)S(1)} %pad_maximum_fusion.1.rest_0_), channel_id=1, source_target_pairs={{0,4},{1,5},{2,6},{3,7},{4,0},{5,1},{6,2},{7,3},{8,12},{9,13},{10,... | collective-permute-start | bytes 1572872 | tf_op jit(solution)/shard_map/ppermute | solution.py:40
  20.4 22.8 %collective-permute-start.11 = (bf16[512,512]{1,0:T(8,128)(2,1)S(1)}, bf16[512,512]{1,0:T(8,128)(2,1)S(1)}, u32[]{:S(2)}, u32[]{:S(2)}) collective-permute-start(bf16[512,512]{1,0:T(8,128)(2,1)S(1)} %get-tuple-element.79.rest_10_), channel_id=1, source_target_pairs={{0,16},{8,24},{16,0},{24,8},{32,48},{40,56},{48,32},{56,40},{64,80... | collective-permute-start | bytes 1572872 | tf_op jit(solution)/shard_map/ppermute | solution.py:32
  30.9 14.0 %collective-permute-start.10 = (bf16[1024,128]{1,0:T(8,128)(2,1)}, bf16[1024,128]{1,0:T(8,128)(2,1)S(1)}, u32[]{:S(2)}, u32[]{:S(2)}) collective-permute-start(bf16[1024,128]{1,0:T(8,128)(2,1)} %pad_maximum_fusion.2), channel_id=1, source_target_pairs={{0,64},{8,72},{16,80},{24,88},{32,96},{40,104},{48,112},{56,120},{... | collective-permute-start | bytes 786440 | tf_op jit(solution)/shard_map/ppermute | solution.py:32
  32.7 14.1 %collective-permute-start.8 = (bf16[1024,128]{1,0:T(8,128)(2,1)}, bf16[1024,128]{1,0:T(8,128)(2,1)}, u32[]{:S(2)}, u32[]{:S(2)}) collective-permute-start(bf16[1024,128]{1,0:T(8,128)(2,1)} %pad_maximum_fusion.2), channel_id=1, source_target_pairs={{0,32},{8,40},{16,48},{24,56},{32,64},{40,72},{48,80},{56,88},{64,... | collective-permute-start | bytes 786440 | tf_op jit(solution)/shard_map/ppermute | solution.py:32
  33.3 14.0 %collective-permute-start.9 = (bf16[1024,128]{1,0:T(8,128)(2,1)}, bf16[1024,128]{1,0:T(8,128)(2,1)}, u32[]{:S(2)}, u32[]{:S(2)}) collective-permute-start(bf16[1024,128]{1,0:T(8,128)(2,1)} %pad_maximum_fusion.2), channel_id=1, source_target_pairs={{0,96},{8,104},{16,112},{24,120},{32,0},{40,8},{48,16},{56,24},{64... | collective-permute-start | bytes 786440 | tf_op jit(solution)/shard_map/ppermute | solution.py:32
  35.9 16.5 %collective-permute-start.12 = (bf16[512,512]{1,0:T(8,128)(2,1)}, bf16[512,512]{1,0:T(8,128)(2,1)}, u32[]{:S(2)}, u32[]{:S(2)}) collective-permute-start(bf16[512,512]{1,0:T(8,128)(2,1)} %get-tuple-element.73.rest_10_), channel_id=1, source_target_pairs={{0,16},{8,24},{16,0},{24,8},{32,48},{40,56},{48,32},{56,40},{64,80... | collective-permute-start | bytes 1572872 | tf_op jit(solution)/shard_map/ppermute | solution.py:32
  43.3 18.9 %collective-permute-start.13 = (bf16[512,512]{1,0:T(8,128)(2,1)S(1)}, bf16[512,512]{1,0:T(8,128)(2,1)S(1)}, u32[]{:S(2)}, u32[]{:S(2)}) collective-permute-start(bf16[512,512]{1,0:T(8,128)(2,1)S(1)} %collective-permute-done.7.rest_5_), channel_id=1, source_target_pairs={{0,1},{1,2},{2,3},{3,0},{4,5},{5,6},{6,7},{7,4},{8,9},{9,10},{10,1... | collective-permute-start | bytes 1572872 | tf_op jit(solution)/shard_map/ppermute | solution.py:40
  44.8 17.3 %collective-permute-start.14 = (bf16[512,512]{1,0:T(8,128)(2,1)S(1)}, bf16[512,512]{1,0:T(8,128)(2,1)S(1)}, u32[]{:S(2)}, u32[]{:S(2)}) collective-permute-start(bf16[512,512]{1,0:T(8,128)(2,1)S(1)} %collective-permute-done.7.rest_5_), channel_id=1, source_target_pairs={{0,3},{1,0},{2,1},{3,2},{4,7},{5,4},{6,5},{7,6},{8,11},{9,8},{10,9... | collective-permute-start | bytes 1572872 | tf_op jit(solution)/shard_map/ppermute | solution.py:40
  46.8 12.9 %collective-permute-start.15 = (bf16[256,512]{1,0:T(8,128)(2,1)S(1)}, bf16[256,512]{1,0:T(8,128)(2,1)S(1)}, u32[]{:S(2)}, u32[]{:S(2)}) collective-permute-start(bf16[256,512]{1,0:T(8,128)(2,1)S(1)} %slice.67), channel_id=1, source_target_pairs={{0,1},{1,2},{2,3},{3,0},{4,5},{5,6},{6,7},{7,4},{8,9},{9,10},{10,1... | collective-permute-start | bytes 786440 | tf_op jit(solution)/shard_map/ppermute | solution.py:40
  47.3 14.2 %collective-permute-start.16 = (bf16[256,512]{1,0:T(8,128)(2,1)S(1)}, bf16[256,512]{1,0:T(8,128)(2,1)S(1)}, u32[]{:S(2)}, u32[]{:S(2)}) collective-permute-start(bf16[256,512]{1,0:T(8,128)(2,1)S(1)} %slice.68), channel_id=1, source_target_pairs={{0,3},{1,0},{2,1},{3,2},{4,7},{5,4},{6,5},{7,6},{8,11},{9,8},{10,9... | collective-permute-start | bytes 786440 | tf_op jit(solution)/shard_map/ppermute | solution.py:40
  52.4 32.2 %collective-permute-start.22 = (bf16[512,512]{1,0:T(8,128)(2,1)}, bf16[512,512]{1,0:T(8,128)(2,1)}, u32[]{:S(2)}, u32[]{:S(2)}) collective-permute-start(bf16[512,512]{1,0:T(8,128)(2,1)} %get-tuple-element.73.rest_10_), channel_id=1, source_target_pairs={{0,32},{8,40},{16,48},{24,56},{32,64},{40,72},{48,80},{56,88},{64,... | collective-permute-start | bytes 1572872 | tf_op jit(solution)/shard_map/ppermute | solution.py:32
  59.7 29.9 %collective-permute-start.23 = (bf16[512,512]{1,0:T(8,128)(2,1)}, bf16[512,512]{1,0:T(8,128)(2,1)}, u32[]{:S(2)}, u32[]{:S(2)}) collective-permute-start(bf16[512,512]{1,0:T(8,128)(2,1)} %get-tuple-element.73.rest_10_), channel_id=1, source_target_pairs={{0,96},{8,104},{16,112},{24,120},{32,0},{40,8},{48,16},{56,24},{64... | collective-permute-start | bytes 1572872 | tf_op jit(solution)/shard_map/ppermute | solution.py:32
  62.2 14.1 %collective-permute-start.17 = (bf16[4096,128]{1,0:T(8,128)(2,1)}, bf16[4096,128]{1,0:T(8,128)(2,1)}, u32[]{:S(2)}, u32[]{:S(2)}) collective-permute-start(bf16[4096,128]{1,0:T(8,128)(2,1)} %pad_maximum_fusion), channel_id=1, source_target_pairs={{0,8},{8,0},{16,24},{24,16},{32,40},{40,32},{48,56},{56,48},{64,72... | collective-permute-start | bytes 3145736 | tf_op jit(solution)/shard_map/ppermute | solution.py:32
  70.6 19.4 %collective-permute-start.20 = (bf16[256,512]{1,0:T(8,128)(2,1)S(1)}, bf16[256,512]{1,0:T(8,128)(2,1)S(1)}, u32[]{:S(2)}, u32[]{:S(2)}) collective-permute-start(bf16[256,512]{1,0:T(8,128)(2,1)S(1)} %slice.69), channel_id=1, source_target_pairs={{0,32},{8,40},{16,48},{24,56},{32,64},{40,72},{48,80},{56,88},{64,... | collective-permute-start | bytes 786440 | tf_op jit(solution)/shard_map/ppermute | solution.py:32
  71.9 28.6 %collective-permute-start.21 = (bf16[256,512]{1,0:T(8,128)(2,1)S(1)}, bf16[256,512]{1,0:T(8,128)(2,1)S(1)}, u32[]{:S(2)}, u32[]{:S(2)}) collective-permute-start(bf16[256,512]{1,0:T(8,128)(2,1)S(1)} %slice.70), channel_id=1, source_target_pairs={{0,96},{8,104},{16,112},{24,120},{32,0},{40,8},{48,16},{56,24},{64... | collective-permute-start | bytes 786440 | tf_op jit(solution)/shard_map/ppermute | solution.py:32
  76.3 26.3 %collective-permute-start.18 = (bf16[512,512]{1,0:T(8,128)(2,1)S(1)}, bf16[512,512]{1,0:T(8,128)(2,1)S(1)}, u32[]{:S(2)}, u32[]{:S(2)}) collective-permute-start(bf16[512,512]{1,0:T(8,128)(2,1)S(1)} %copy-done.20), channel_id=1, source_target_pairs={{0,32},{8,40},{16,48},{24,56},{32,64},{40,72},{48,80},{56,88},{64,... | collective-permute-start | bytes 1572872 | tf_op jit(solution)/shard_map/ppermute | solution.py:32
  84.6 19.8 %collective-permute-start.19 = (bf16[512,512]{1,0:T(8,128)(2,1)S(1)}, bf16[512,512]{1,0:T(8,128)(2,1)S(1)}, u32[]{:S(2)}, u32[]{:S(2)}) collective-permute-start(bf16[512,512]{1,0:T(8,128)(2,1)S(1)} %copy-done.20), channel_id=1, source_target_pairs={{0,96},{8,104},{16,112},{24,120},{32,0},{40,8},{48,16},{56,24},{64... | collective-permute-start | bytes 1572872 | tf_op jit(solution)/shard_map/ppermute | solution.py:32
  106.0 25.3 %collective-permute-start.32 = (bf16[256,512]{1,0:T(8,128)(2,1)}, bf16[256,512]{1,0:T(8,128)(2,1)}, u32[]{:S(2)}, u32[]{:S(2)}) collective-permute-start(bf16[256,512]{1,0:T(8,128)(2,1)} %slice.77), channel_id=1, source_target_pairs={{0,32},{8,40},{16,48},{24,56},{32,64},{40,72},{48,80},{56,88},{64,... | collective-permute-start | bytes 786440 | tf_op jit(solution)/shard_map/ppermute | solution.py:32
  115.2 21.1 %collective-permute-start.33 = (bf16[256,512]{1,0:T(8,128)(2,1)}, bf16[256,512]{1,0:T(8,128)(2,1)}, u32[]{:S(2)}, u32[]{:S(2)}) collective-permute-start(bf16[256,512]{1,0:T(8,128)(2,1)} %slice.78), channel_id=1, source_target_pairs={{0,96},{8,104},{16,112},{24,120},{32,0},{40,8},{48,16},{56,24},{64... | collective-permute-start | bytes 786440 | tf_op jit(solution)/shard_map/ppermute | solution.py:32
  118.5 36.1 %collective-permute-start.28 = (bf16[512,512]{1,0:T(8,128)(2,1)}, bf16[512,512]{1,0:T(8,128)(2,1)S(1)}, u32[]{:S(2)}, u32[]{:S(2)}) collective-permute-start(bf16[512,512]{1,0:T(8,128)(2,1)} %collective-permute-done.12.rest_15_), channel_id=1, source_target_pairs={{0,32},{8,40},{16,48},{24,56},{32,64},{40,72},{48,80},{56,88},{64,... | collective-permute-start | bytes 1572872 | tf_op jit(solution)/shard_map/ppermute | solution.py:32
  130.8 25.7 %collective-permute-start.29 = (bf16[512,512]{1,0:T(8,128)(2,1)}, bf16[512,512]{1,0:T(8,128)(2,1)S(1)}, u32[]{:S(2)}, u32[]{:S(2)}) collective-permute-start(bf16[512,512]{1,0:T(8,128)(2,1)} %collective-permute-done.12.rest_15_), channel_id=1, source_target_pairs={{0,96},{8,104},{16,112},{24,120},{32,0},{40,8},{48,16},{56,24},{64... | collective-permute-start | bytes 1572872 | tf_op jit(solution)/shard_map/ppermute | solution.py:32
  (54 other events, 413.6 us)

commit v5 on v2

--- a/solution.py
+++ b/solution.py
@@ -12,13 +12,12 @@
 KEY_BLOCK = 256
 MOST = 2560
 CHUNKS = 2
-PIECES = 4
 MASKED = -1e30
 SCALE = 1.0 / math.sqrt(HEAD_WIDTH)
 LOG2E = 1.0 / math.log(2.0)
 BF16 = jnp.bfloat16
 F32 = jnp.float32
-VMEM_LIMIT = 48 * 2**20
+VMEM_LIMIT = 18 * 2**20
 
 FIRST, COUNT, CLEAR, CORE, TABLE = 0, 1, 2, 3, 4
 
@@ -31,6 +30,14 @@
                 target = ((x + dx) % 4) * 4 + ((z + dz) % 2) * 2 + (c + dc) % 2
                 pairs.append((x * 4 + z * 2 + c, target))
     return lax.ppermute(value, "dp", pairs)
+
+
+def tensor_move(value, dz, dy):
+    pairs = []
+    for z in range(2):
+        for y in range(4):
+            pairs.append((z * 4 + y, ((z + dz) % 2) * 4 + (y + dy) % 4))
+    return lax.ppermute(value, "tensor", pairs)
 
 
 def after(value, *others):
@@ -130,7 +137,7 @@
             ],
         ),
         out_shape=[
-            jax.ShapeDtypeStruct((live, heads * rows), BF16),
+            pltpu.HBM((live, heads * rows), BF16),
             jax.ShapeDtypeStruct((HEAD_WIDTH, heads * rows), F32),
         ],
         compiler_params=pltpu.CompilerParams(vmem_limit_bytes=VMEM_LIMIT),
@@ -209,7 +216,7 @@
     def near(i, r):
         return jnp.minimum(i, r[COUNT] - 1)
 
-    sum_spec = pl.BlockSpec(sums, lambda i, r: (0, 0, 0))
+    sum_spec = pl.BlockSpec(sums, lambda i, r: (0, 0, 0), pipeline_mode=pl.Buffered(1))
     gq_spec = pl.BlockSpec((rows, heads * HEAD_WIDTH), lambda i, r: (0, part))
     scratch = [
         pltpu.VMEM((HEAD_WIDTH, heads * rows), BF16),
@@ -254,58 +261,54 @@
     )(info, probs, outs, grads, queries, kv, kv, *carried)
 
 
-def project_kernel(pieces, source, grad_ref, *rest):
-    weights, (own_ref, other_ref, grad, weight, grad_sem, weight_sem) = rest[:-6], rest[-6:]
-    chips = len(weights) // pieces
-    part_rows = weights[0].shape[0]
-    copies = []
-    for i in range(chips):
-        one = [pltpu.make_async_copy(grad_ref.at[source[i]], grad.at[i], grad_sem.at[i])]
-        for j in range(pieces):
-            k = i * pieces + j
-            rows = pl.ds(j * part_rows, part_rows)
-            one.append(pltpu.make_async_copy(weights[k], weight.at[i, rows], weight_sem.at[k]))
-        for copy in one:
-            copy.start()
-        copies.append(one)
+def project_kernel(grad_count, slots, *rest):
+    grads, (*stacks, own_ref, other_ref, grad) = rest[:grad_count], rest[grad_count:]
     half = own_ref.shape[0]
-    for i in range(chips):
-        for copy in copies[i]:
-            copy.wait()
-        for ref, at in ((own_ref, 0), (other_ref, half)):
-            term = dot_t(grad[i, at : at + half, :], weight[i])
-            if i == 0:
-                ref[...] = term
-            else:
-                ref[...] += term
-
-
-def project(part, source, all_grad, weights):
-    chips, tokens, depth = all_grad.shape
-    pieces = len(weights[0])
-    features = pieces * weights[0][0].shape[0]
-    flat = [piece for chip in weights for piece in chip]
+    at = 0
+    for ref in grads:
+        chip, row, size = at // (2 * half), at % (2 * half), ref.shape[0]
+        grad[chip, row : row + size, :] = ref[...]
+        at += size
+    k = 0
+    for ref in stacks:
+        for j in range(ref.shape[0]):
+            for out, row in ((own_ref, 0), (other_ref, half)):
+                term = dot_t(grad[slots[k], row : row + half, :], ref[j])
+                if k == 0:
+                    out[...] = term
+                else:
+                    out[...] += term
+            k += 1
+
+
+def project(part, slots, grads, stacks):
+    depth = grads[0].shape[1]
+    chips = slots.shape[0]
+    tokens = sum(ref.shape[0] for ref in grads) // chips
+    features = stacks[0][0].shape[1] // CHUNKS
     half = jax.ShapeDtypeStruct((tokens // 2, features), F32)
+    out_spec = pl.BlockSpec((tokens // 2, features), lambda i: (0, 0))
+    stack_specs = [
+        pl.BlockSpec((stack.shape[0], features, depth), lambda i, at=at: (0, at, 0))
+        for stack, at in stacks
+    ]
     return pl.pallas_call(
-        functools.partial(project_kernel, pieces),
+        functools.partial(project_kernel, len(grads)),
+        grid=(1,),
         in_specs=[pl.BlockSpec(memory_space=pltpu.SMEM)]
-        + [pl.BlockSpec(memory_space=pl.ANY)] * (1 + len(flat)),
-        out_specs=[pl.BlockSpec(memory_space=pltpu.VMEM)] * 2,
+        + [pl.BlockSpec(ref.shape, lambda i: (0, 0)) for ref in grads]
+        + stack_specs,
+        out_specs=[out_spec, out_spec],
         out_shape=[half, half],
-        scratch_shapes=[
-            pltpu.VMEM((chips, tokens, depth), BF16),
-            pltpu.VMEM((chips, features, depth), BF16),
-            pltpu.SemaphoreType.DMA((chips,)),
-            pltpu.SemaphoreType.DMA((chips * pieces,)),
-        ],
-        compiler_params=pltpu.CompilerParams(vmem_limit_bytes=VMEM_LIMIT),
+        scratch_shapes=[pltpu.VMEM((chips, tokens, depth), BF16)],
+        compiler_params=pltpu.CompilerParams(vmem_limit_bytes=24 * 2**20),
         cost_estimate=pl.CostEstimate(
             flops=2 * tokens * features * depth * chips,
-            bytes_accessed=12 * 2**20,
+            bytes_accessed=10 * 2**20,
             transcendentals=0,
         ),
         name="project%d" % part,
-    )(source, all_grad, *flat)
+    )(slots, *grads, *[stack for stack, _ in stacks])
 
 
 def local(queries, keys, values, grad_out, out_weight, lengths):
@@ -323,9 +326,7 @@
     last = query_pos[-1] // KEY_BLOCK
     clear = (query_start[-1] + KEY_BLOCK - 1) // KEY_BLOCK
     block = jnp.arange(16, dtype=jnp.int32)
-    distance = (block // 4 - x) % 4
-    turn = jnp.where(distance == 0, 0, jnp.where(distance == 3, 1, distance + 1))
-    place = jnp.where((block // 2) % 2 == z, 0, 8) + turn * 2
+    place = block // 2 * 2
     here = place + jnp.where(block % 2 == core, 0, 1)
     there = 16 + place + jnp.where(block % 2 == core, 1, 0)
     table = [jnp.where(core == 0, here, there), jnp.where(core == 0, there, here)]
@@ -337,57 +338,83 @@
     mine = lax.dynamic_slice_in_dim(grad_out, core * depth, depth, 1)
     other = lax.dynamic_slice_in_dim(grad_out, (1 - core) * depth, depth, 1)
     chip_grad = jnp.concatenate([mine, dp_move(other, 0, 0, 1)], axis=0)
-    all_grad = lax.all_gather(chip_grad, "tensor", axis=0, tiled=False)
-
+
+    groups_x = [[x_ * 4 + zc for x_ in range(4)] for zc in range(4)]
+    plane = lax.all_gather(out_weight, "dp", axis=0, axis_index_groups=groups_x)
+    size = out_weight.shape[0] // CHUNKS
+    paired = [dp_move(out_weight[j * size : (j + 1) * size], 0, 1, 0) for j in range(CHUNKS)]
+    other_plane = lax.all_gather(paired[0], "dp", axis=0, axis_index_groups=groups_x)
+
+    groups = [[2 * i + c for i in range(8)] for c in range(2)]
     kept = jnp.where(core == 0, keys, values)
     got = dp_move(jnp.where(core == 0, values, keys), 0, 0, 1)
     chip = jnp.concatenate([kept, got], axis=0)
-    quad = jnp.concatenate(
-        [chip, dp_move(chip, 1, 0, 0), dp_move(chip, -1, 0, 0), dp_move(chip, 2, 0, 0)], axis=0
+    ring = lax.all_to_all(
+        jnp.broadcast_to(chip, (8, *chip.shape)), "dp", 0, 0, axis_index_groups=groups, tiled=True
+    ).reshape(-1, HEAD_WIDTH)
+    kv = jnp.concatenate([ring, dp_move(ring, 0, 0, 1)], axis=0)
+
+    def far(ring):
+        half = ring[0].shape[0] // 2
+        return [tensor_move(ring[1][:half], 0, 1), tensor_move(ring[2][half:], 0, -1)]
+
+    def both(block):
+        return [block, tensor_move(block, 0, 1), tensor_move(block, 0, -1)]
+
+    grad0 = both(chip_grad)
+    grad_pair = tensor_move(chip_grad, 1, 0)
+    kv, grad0, grad_pair, paired = lax.optimization_barrier((kv, grad0, grad_pair, paired))
+    first_part = forward(0, info, query_pos, query_start, queries, kv)
+    grad_far0 = far(grad0)
+    grad1 = both(grad_pair)
+    first_part, grad_far0, grad1 = lax.optimization_barrier((first_part, grad_far0, grad1))
+    second_part = forward(1, info, query_pos, query_start, after(queries, first_part[1]), kv)
+    grad_far1 = far(grad1)
+    parts = [first_part, second_part]
+    all_grad = grad0 + grad_far0 + grad1 + grad_far1
+
+    rest = jnp.concatenate(
+        [
+            lax.dynamic_slice(plane, ((x + i) % 4, size, 0), (1, size, depth))
+            for i in range(1, 4)
+        ],
+        axis=0,
     )
-    ring = jnp.concatenate([quad, dp_move(quad, 0, 1, 0)], axis=0)
-    kv = jnp.concatenate([ring, dp_move(ring, 0, 0, 1)], axis=0)
-
-    size = out_weight.shape[0] // PIECES
-    own = [out_weight[j * size : (j + 1) * size] for j in range(PIECES)]
-    pair = [dp_move(piece, 0, 1, 0) for piece in own]
-    held = own + pair
-    left = [dp_move(piece, 1, 0, 0) for piece in held]
-    right = [dp_move(piece, -1, 0, 0) for piece in held]
-
-    kv = after(kv, *pair)
-    parts = [forward(0, info, query_pos, query_start, queries, kv)]
-
-    tied = lax.optimization_barrier((parts[0], left, right))
-    parts[0], left, right = tied
-    far = [
-        dp_move(left[j], 1, 0, 0) if j % 2 == 0 else dp_move(right[j], -1, 0, 0)
-        for j in range(2 * PIECES)
+    rest = dp_move(rest, 0, 1, 0)
+
+    t = lax.axis_index("tensor")
+
+    def slot(x_, z_):
+        source = 2 * (x_ % 4) + z_
+        y_distance = (source - t) % 4
+        turn = jnp.where(
+            y_distance == 0, 0, jnp.where(y_distance == 3, 1, jnp.where(y_distance == 1, 2, 3))
+        )
+        return jnp.where(source // 4 == t // 4, 0, 4) + turn
+
+    same = [slot(i, z) for i in range(4)]
+    slots = [
+        jnp.stack(same + [slot(i, 1 - z) for i in range(4)]).astype(jnp.int32),
+        jnp.stack(same + [slot(x + i, 1 - z) for i in range(4)]).astype(jnp.int32),
     ]
-    parts.append(forward(1, info, query_pos, query_start, after(queries, parts[0][1]), kv))
-
-    distances = [(0, 0), (3, 0), (1, 0), (2, 0), (0, 1), (3, 1), (1, 1), (2, 1)]
-    source = jnp.stack(
-        [2 * ((x + dx) % 4) + (z + dz) % 2 for dx, dz in distances]
-    ).astype(jnp.int32)
+    stacks = [
+        [(plane, 0), (other_plane, 0)],
+        [(plane, 1), (paired[1][None], 0), (rest, 0)],
+    ]
+
+    slots[0] = after(slots[0], second_part[1])
     carried = ()
-    share = PIECES // CHUNKS
     for part in range(CHUNKS):
-        weights = [
-            [group[dz * PIECES + j] for j in range(part * share, (part + 1) * share)]
-            for dz in range(2)
-            for group in (held, left, right, far)
-        ]
-        mine, other = project(part, source, all_grad, weights)
+        mine, other = project(part, slots[part], all_grad, stacks[part])
         grads = (mine + dp_move(other, 0, 0, 1)).astype(BF16)
         probs, outs = parts[part]
         grad_queries, own_sums, other_sums = backward(
             part, info, probs, outs, grads, queries, kv, carried
         )
         carried = (own_sums, other_sums, grad_queries)
+        slots[-1] = after(slots[-1], grad_queries)
 
     chip_sums = (own_sums + dp_move(other_sums, 0, 0, 1).astype(F32)).astype(BF16)
-    groups = [[2 * i + c for i in range(8)] for c in range(2)]
     terms = lax.all_to_all(chip_sums, "dp", 0, 0, axis_index_groups=groups, tiled=True)
     done = jnp.sum(terms.astype(F32), axis=0).astype(BF16)
     return grad_queries, done[:, :HEAD_WIDTH], done[:, HEAD_WIDTH:]

time: 269 us -> 232 us (0.86)
  starting transfers between devices: 65.7 us -> 30.4 us
  Pallas kernels: 30.2 us -> 24.6 us
  blocking collectives: 55.1 us -> 51.1 us
  other arithmetic: 2.42 us -> 6.14 us
  local copies, waits for them, and re-layouts: 21.3 us -> 24.8 us
    ppermute x38 -> x9, starting transfers between devices: 65.7 us -> 8.72 us  [dp_move(): return lax.ppermute(value, 'dp', pairs)]
    ppermute x38 -> x9, waiting for transfers between devices: 73.9 us -> 29.6 us  [dp_move(): return lax.ppermute(value, 'dp', pairs)]
    all_to_all x0 -> x1, waiting for transfers between devices: none -> 25.6 us  [local(): lax.all_to_all(jnp.broadcast_to(chip, (8, *chip.shape)), 'dp', 0, 0, axis...]
    ppermute x0 -> x9, waiting for transfers between devices: none -> 17.5 us  [tensor_move(): return lax.ppermute(value, 'tensor', pairs)]
    ppermute x0 -> x9, starting transfers between devices: none -> 13.9 us  [tensor_move(): return lax.ppermute(value, 'tensor', pairs)]
    all_to_all x0 -> x1, starting transfers between devices: none -> 7.7 us  [local(): lax.all_to_all(jnp.broadcast_to(chip, (8, *chip.shape)), 'dp', 0, 0, axis...]
    pallas_call x2, Pallas kernels: 11.3 us -> 6.78 us  [backward(): pl.pallas_call(functools.partial(backward_kernel, heads, part), grid_spec...]
    all_to_all x1, blocking collectives: 55.1 us -> 51.1 us  [local(): lax.all_to_all(chip_sums, 'dp', 0, 0, axis_index_groups=groups, tiled=True)]
  transfers between devices with their start and end apart: 39 -> 21, of which waited for: 15 -> 10; matrix products, arithmetic and copies ran while one was open for 3% -> 6% of each run, Pallas kernels for 9% -> 7%
where the time goes in v5:
time: 232 us; the launch traced here: 231 us
  waiting for transfers between devices  73.3 us (32%)
  blocking collectives  51.1 us (22%)
  starting transfers between devices  30.4 us (13%)
  local copies, waits for them, and re-layouts  24.8 us (11%)
  Pallas kernels  24.6 us (11%)
  between operations  20.6 us (9%)
  other arithmetic  6.14 us (3%)
    all_to_all x1, blocking collectives, local(): lax.all_to_all(chip_sums, 'dp', 0, 0, axis_index_groups=groups, tiled=True)  51.1 us
    ppermute x9, waiting for transfers between devices, dp_move(): return lax.ppermute(value, 'dp', pairs)  29.6 us
    all_to_all x1, waiting for transfers between devices, local(): lax.all_to_all(jnp.broadcast_to(chip, (8, *chip.shape)), 'dp', 0, 0, axis...  25.6 us
    ppermute x9, waiting for transfers between devices, tensor_move(): return lax.ppermute(value, 'tensor', pairs)  17.5 us
    unnamed x50, local copies, waits for them, and re-layouts  17.1 us
    ppermute x9, starting transfers between devices, tensor_move(): return lax.ppermute(value, 'tensor', pairs)  13.9 us
    pallas_call x2, Pallas kernels, forward(): pl.pallas_call(forward_kernel, grid_spec=pltpu.PrefetchScalarGridSpec(num...  9.12 us
    ppermute x9, starting transfers between devices, dp_move(): return lax.ppermute(value, 'dp', pairs)  8.72 us
  transfers between devices with their start and end apart: 21, of which 10 were waited for; matrix products, arithmetic and copies ran while one was open for 6% of the time, Pallas kernels for 7%

profile of v5, /device:TPU:0, one launch (start us, length us, event | category | flops | bytes accessed | tf_op | source)
XLA Modules:
  0.0 231.0 jit_solution(810255149489289932)
XLA Ops:
  11.4 7.7 %all-to-all-start = ((bf16[8,512,128]{2,1,0:T(8,128)(2,1)}), bf16[8,512,128]{2,1,0:T(8,128)(2,1)}, u32[]{:S(2)}, u32[]{:S(2)}) async-start(bf16[8,512,128]{2,1,0:T(8,128)(2,1)} %broadcast_in_dim.31), calls=%async_computation | async-start | bytes 2097152 | tf_op jit(solution)/shard_map/all_to_all | solution.py:352
  19.9 25.6 %all-to-all-done = bf16[8,512,128]{2,1,0:T(8,128)(2,1)} async-done(((bf16[8,512,128]{2,1,0:T(8,128)(2,1)}), bf16[8,512,128]{2,1,0:T(8,128)(2,1)}, u32[]{:S(2)}, u32[]{:S(2)}) %all-to-all-start) | async-done | bytes 1048608 | tf_op jit(solution)/shard_map/all_to_all | solution.py:352
  47.2 2.7 %collective-permute-start.7 = (bf16[512,512]{1,0:T(8,128)(2,1)}, bf16[512,512]{1,0:T(8,128)(2,1)S(1)}, u32[]{:S(2)}, u32[]{:S(2)}) collective-permute-start(bf16[512,512]{1,0:T(8,128)(2,1)} %get-tuple-element.66), channel_id=1, source_target_pairs={{0,16},{8,24},{16,0},{24,8},{32,48},{40,56},{48,32},{56,40},{64,80... | collective-permute-start | bytes 1572872 | tf_op jit(solution)/shard_map/ppermute | solution.py:32
  63.5 1.7 pad_maximum_fusion.kv_ref.k_ref.v_ref
  65.2 8.6 %collective-permute-done.7 = bf16[512,512]{1,0:T(8,128)(2,1)S(1)} collective-permute-done((bf16[512,512]{1,0:T(8,128)(2,1)}, bf16[512,512]{1,0:T(8,128)(2,1)S(1)}, u32[]{:S(2)}, u32[]{:S(2)}) %collective-permute-start.7) | collective-permute-done | bytes 524320 | tf_op jit(solution)/shard_map/ppermute | solution.py:32
  74.6 8.7 %collective-permute-done.5.rest_5_ = bf16[512,512]{1,0:T(8,128)(2,1)S(1)} collective-permute-done((bf16[512,512]{1,0:T(8,128)(2,1)S(1)}, bf16[512,512]{1,0:T(8,128)(2,1)S(1)}, u32[]{:S(2)}, u32[]{:S(2)}) %collective-permute-start.5) | collective-permute-done | bytes 524320 | tf_op jit(solution)/shard_map/ppermute | solution.py:40
  87.1 2.9 %collective-permute-start.9 = (bf16[256,512]{1,0:T(8,128)(2,1)S(1)}, bf16[256,512]{1,0:T(8,128)(2,1)S(1)}, u32[]{:S(2)}, u32[]{:S(2)}) collective-permute-start(bf16[256,512]{1,0:T(8,128)(2,1)S(1)} %slice.44), channel_id=1, source_target_pairs={{0,3},{1,0},{2,1},{3,2},{4,7},{5,4},{6,5},{7,6},{8,11},{9,8},{10,9... | collective-permute-start | bytes 786440 | tf_op jit(solution)/shard_map/ppermute | solution.py:40
  90.0 4.6 %forward0.1 = (bf16[2816,1024]{1,0:T(8,128)(2,1)}, f32[128,1024]{1,0:T(8,128)S(1)}) custom-call(s32[36]{0:T(128)S(1)} %concatenate.15.info, s32[1,256]{1,0:T(1,128)S(1)} %iota_add_fusion.pos_ref, s32[1,256]{1,0:T(1,128)S(1)} %bitcast.32, bf16[256,1024]{1,0:T(8,128)(2,1)S(1)} %copy-done.12, bf16[8192,128]{1,0:T(8,128)(2,1)S(1)} %pad_maximum_fusion.kv_ref.k_ref.v_ref), custom_call_target="tpu_custom_call" | custom-call | flops 16000000000 | bytes 10485760 | tf_op jit(solution)/shard_map/forward0/pallas_call | solution.py:119
  95.4 8.7 %collective-permute-done.8.rest_3_ = bf16[256,512]{1,0:T(8,128)(2,1)S(1)} collective-permute-done((bf16[256,512]{1,0:T(8,128)(2,1)S(1)}, bf16[256,512]{1,0:T(8,128)(2,1)S(1)}, u32[]{:S(2)}, u32[]{:S(2)}) %collective-permute-start.8) | collective-permute-done | bytes 262176 | tf_op jit(solution)/shard_map/ppermute | solution.py:40
  104.2 4.5 %forward1.1 = (bf16[2816,1024]{1,0:T(8,128)(2,1)}, f32[128,1024]{1,0:T(8,128)S(1)}) custom-call(s32[36]{0:T(128)S(1)} %concatenate.15.info, s32[1,256]{1,0:T(1,128)S(1)} %iota_add_fusion.pos_ref, s32[1,256]{1,0:T(1,128)S(1)} %bitcast.33, bf16[256,1024]{1,0:T(8,128)(2,1)S(1)} %copy-done.12, bf16[8192,128]{1,0:T(8,128)(2,1)S(1)} %pad_maximum_fusion.kv_ref.k_ref.v_ref), custom_call_target="tpu_custom_call" | custom-call | flops 16000000000 | bytes 10485760 | tf_op jit(solution)/shard_map/forward1/pallas_call | solution.py:119
  112.4 1.7 collective-permute-start.13
  117.0 3.8 %collective-permute-start.15 = (bf16[3,512,512]{2,1,0:T(8,128)(2,1)}, bf16[3,512,512]{2,1,0:T(8,128)(2,1)}, u32[]{:S(2)}, u32[]{:S(2)}) collective-permute-start(bf16[3,512,512]{2,1,0:T(8,128)(2,1)} %pad_maximum_fusion.1), channel_id=1, source_target_pairs={{0,16},{8,24},{16,0},{24,8},{32,48},{40,56},{48,32},{56,40},{64,80... | collective-permute-start | bytes 4718600 | tf_op jit(solution)/shard_map/ppermute | solution.py:32
  120.8 2.2 copy-done
  125.5 4.4 %project0.1 = (f32[256,512]{1,0:T(8,128)S(1)}, f32[256,512]{1,0:T(8,128)}) custom-call(s32[8]{0:T(128)S(1)} %stack.75.slots, bf16[512,512]{1,0:T(8,128)(2,1)S(1)} %pad_maximum_fusion.2.rest_0_, bf16[512,512]{1,0:T(8,128)(2,1)S(1)} %collective-permute-done.3.rest_1_, bf16[512,512]{1,0:T(8,128)(2,1)S(1)} %collective-permute-done.4.rest_2_, ...), custom_call_target="tpu_custom_call" | custom-call | flops 2147483648 | bytes 10485760 | tf_op jit(solution)/shard_map/project0/pallas_call | solution.py:295
  130.8 2.2 collective-permute-done.14
  136.9 2.6 %copy-done.16 = bf16[2816,1024]{1,0:T(8,128)(2,1)S(1)} copy-done((bf16[2816,1024]{1,0:T(8,128)(2,1)S(1)}, bf16[2816,1024]{1,0:T(8,128)(2,1)}, u32[]{:S(2)}) %copy-start.16) | copy-done | bytes 5767192
  140.6 3.4 %backward0.1 = (bf16[256,1024]{1,0:T(8,128)(2,1)}, f32[8,256,256]{2,1,0:T(8,128)S(1)}, f32[8,256,256]{2,1,0:T(8,128)S(1)}) custom-call(s32[36]{0:T(128)S(1)} %concatenate.15.info, bf16[2816,1024]{1,0:T(8,128)(2,1)S(1)} %copy-done.16, f32[128,1024]{1,0:T(8,128)S(1)} %copy-done.20, bf16[256,512]{1,0:T(8,128)(2,1)S(1)} %add_convert_fusion.2.grad_ref, ...), custom_call_target="tpu_custom_call" | custom-call | flops 8000000000 | bytes 10485760 | tf_op jit(solution)/shard_map/backward0/pallas_call | solution.py:241
  143.9 12.0 %collective-permute-done.15.rest_12_ = bf16[3,512,512]{2,1,0:T(8,128)(2,1)} collective-permute-done((bf16[3,512,512]{2,1,0:T(8,128)(2,1)}, bf16[3,512,512]{2,1,0:T(8,128)(2,1)}, u32[]{:S(2)}, u32[]{:S(2)}) %collective-permute-start.15) | collective-permute-done | bytes 1572896 | tf_op jit(solution)/shard_map/ppermute | solution.py:32
  156.0 4.3 %project1.1 = (f32[256,512]{1,0:T(8,128)S(1)}, f32[256,512]{1,0:T(8,128)S(1)}) custom-call(s32[8]{0:T(128)S(1)} %stack.70.slots, bf16[512,512]{1,0:T(8,128)(2,1)S(1)} %pad_maximum_fusion.2.rest_0_, bf16[512,512]{1,0:T(8,128)(2,1)S(1)} %collective-permute-done.3.rest_1_, bf16[512,512]{1,0:T(8,128)(2,1)S(1)} %collective-permute-done.4.rest_2_, ...), custom_call_target="tpu_custom_call" | custom-call | flops 2147483648 | bytes 10485760 | tf_op jit(solution)/shard_map/project1/pallas_call | solution.py:295
  160.3 1.9 collective-permute-done.16
  162.4 2.6 %copy-done.15 = bf16[2816,1024]{1,0:T(8,128)(2,1)S(1)} copy-done((bf16[2816,1024]{1,0:T(8,128)(2,1)S(1)}, bf16[2816,1024]{1,0:T(8,128)(2,1)}, u32[]{:S(2)}) %copy-start.15) | copy-done | bytes 5767192
  165.0 3.4 %backward1.1 = (bf16[256,1024]{1,0:T(8,128)(2,1)}, f32[8,256,256]{2,1,0:T(8,128)S(1)}, bf16[8,256,256]{2,1,0:T(8,128)(2,1)S(1)}) custom-call(s32[36]{0:T(128)S(1)} %concatenate.15.info, bf16[2816,1024]{1,0:T(8,128)(2,1)S(1)} %copy-done.15, f32[128,1024]{1,0:T(8,128)S(1)} %copy-done.18, ...), custom_call_target="tpu_custom_call", output_to_operand_aliasing={{0}: (9, {})} | custom-call | flops 8000000000 | bytes 10485760 | tf_op jit(solution)/shard_map/backward1/pallas_call | solution.py:241
  169.6 2.3 collective-permute-done.17
  172.2 51.1 %all_to_all.10 = bf16[8,256,256]{2,1,0:T(8,128)(2,1)S(1)} all-to-all(bf16[8,256,256]{2,1,0:T(8,128)(2,1)S(1)} %add_convert_fusion), channel_id=1, replica_groups={{0,16,32,48,64,80,96,112},{8,24,40,56,72,88,104,120},{1,17,33,49,65,81,..., dimensions={0} | all-to-all | bytes 2097152 | tf_op jit(solution)/shard_map/all_to_all | solution.py:418
  (106 shorter events, 36.6 us)
Async XLA Ops:
  7.2 107.0 %all-gather.5.cloned.1.call-start = ((), (), s32[]{:S(2)}) async-start(), calls=%async_computation.2 | async-start | bytes 5242880 | tf_op jit(solution)/shard_map/all_gather | solution.py:343
  8.9 1.3 collective-permute-start
  10.2 35.3 %copy-start.21 = (bf16[1024,512]{1,0:T(8,128)(2,1)S(1)}, bf16[1024,512]{1,0:T(8,128)(2,1)}, u32[]{:S(2)}) copy-start(bf16[1024,512]{1,0:T(8,128)(2,1)} %param.10) | copy-start | bytes 3145732
  11.4 34.1 %all-to-all-start = ((bf16[8,512,128]{2,1,0:T(8,128)(2,1)}), bf16[8,512,128]{2,1,0:T(8,128)(2,1)}, u32[]{:S(2)}, u32[]{:S(2)}) async-start(bf16[8,512,128]{2,1,0:T(8,128)(2,1)} %broadcast_in_dim.31), calls=%async_computation | async-start | bytes 2097152 | tf_op jit(solution)/shard_map/all_to_all | solution.py:352
  19.1 30.8 %copy-start.24 = (s32[8]{0:T(128)S(1)}, s32[8]{0:T(128)}, u32[]{:S(2)}) copy-start(s32[8]{0:T(128)} %param.11) | copy-start | bytes 100
  19.1 101.7 %all-gather.7.cloned.1.call-start = ((), (), s32[]{:S(2)}) async-start(), calls=%async_computation.3 | async-start | bytes 2621440 | tf_op jit(solution)/shard_map/all_gather | solution.py:346
  19.9 37.9 %collective-permute-start.2 = (bf16[256,512]{1,0:T(8,128)(2,1)}, bf16[256,512]{1,0:T(8,128)(2,1)S(1)}, u32[]{:S(2)}, u32[]{:S(2)}) collective-permute-start(bf16[256,512]{1,0:T(8,128)(2,1)} %get-tuple-element.69), channel_id=1, source_target_pairs={{0,8},{8,0},{16,24},{24,16},{32,40},{40,32},{48,56},{56,48},{64,72... | collective-permute-start | bytes 786440 | tf_op jit(solution)/shard_map/ppermute | solution.py:32
  45.5 18.0 %collective-permute-start.1 = (bf16[4096,128]{1,0:T(8,128)(2,1)}, bf16[4096,128]{1,0:T(8,128)(2,1)}, u32[]{:S(2)}, u32[]{:S(2)}) collective-permute-start(bf16[4096,128]{1,0:T(8,128)(2,1)} %bitcast.10), channel_id=1, source_target_pairs={{0,8},{8,0},{16,24},{24,16},{32,40},{40,32},{48,56},{56,48},{64,72... | collective-permute-start | bytes 3145736 | tf_op jit(solution)/shard_map/ppermute | solution.py:32
  46.4 16.2 %collective-permute-start.6 = (bf16[512,512]{1,0:T(8,128)(2,1)S(1)}, bf16[512,512]{1,0:T(8,128)(2,1)S(1)}, u32[]{:S(2)}, u32[]{:S(2)}) collective-permute-start(bf16[512,512]{1,0:T(8,128)(2,1)S(1)} %get-tuple-element.67), channel_id=1, source_target_pairs={{0,16},{8,24},{16,0},{24,8},{32,48},{40,56},{48,32},{56,40},{64,80... | collective-permute-start | bytes 1572872 | tf_op jit(solution)/shard_map/ppermute | solution.py:32
  47.2 26.7 %collective-permute-start.7 = (bf16[512,512]{1,0:T(8,128)(2,1)}, bf16[512,512]{1,0:T(8,128)(2,1)S(1)}, u32[]{:S(2)}, u32[]{:S(2)}) collective-permute-start(bf16[512,512]{1,0:T(8,128)(2,1)} %get-tuple-element.66), channel_id=1, source_target_pairs={{0,16},{8,24},{16,0},{24,8},{32,48},{40,56},{48,32},{56,40},{64,80... | collective-permute-start | bytes 1572872 | tf_op jit(solution)/shard_map/ppermute | solution.py:32
  57.9 16.7 %collective-permute-start.3 = (bf16[512,512]{1,0:T(8,128)(2,1)S(1)}, bf16[512,512]{1,0:T(8,128)(2,1)S(1)}, u32[]{:S(2)}, u32[]{:S(2)}) collective-permute-start(bf16[512,512]{1,0:T(8,128)(2,1)S(1)} %pad_maximum_fusion.2.rest_0_), channel_id=1, source_target_pairs={{0,1},{1,2},{2,3},{3,0},{4,5},{5,6},{6,7},{7,4},{8,9},{9,10},{10,1... | collective-permute-start | bytes 1572872 | tf_op jit(solution)/shard_map/ppermute | solution.py:40
  59.6 15.0 %collective-permute-start.4 = (bf16[512,512]{1,0:T(8,128)(2,1)S(1)}, bf16[512,512]{1,0:T(8,128)(2,1)S(1)}, u32[]{:S(2)}, u32[]{:S(2)}) collective-permute-start(bf16[512,512]{1,0:T(8,128)(2,1)S(1)} %pad_maximum_fusion.2.rest_0_), channel_id=1, source_target_pairs={{0,3},{1,0},{2,1},{3,2},{4,7},{5,4},{6,5},{7,6},{8,11},{9,8},{10,9... | collective-permute-start | bytes 1572872 | tf_op jit(solution)/shard_map/ppermute | solution.py:40
  62.6 20.7 %collective-permute-start.5 = (bf16[512,512]{1,0:T(8,128)(2,1)S(1)}, bf16[512,512]{1,0:T(8,128)(2,1)S(1)}, u32[]{:S(2)}, u32[]{:S(2)}) collective-permute-start(bf16[512,512]{1,0:T(8,128)(2,1)S(1)} %pad_maximum_fusion.2.rest_0_), channel_id=1, source_target_pairs={{0,4},{1,5},{2,6},{3,7},{4,0},{5,1},{6,2},{7,3},{8,12},{9,13},{10,... | collective-permute-start | bytes 1572872 | tf_op jit(solution)/shard_map/ppermute | solution.py:40
  65.2 39.0 %copy-start.2 = (bf16[8192,128]{1,0:T(8,128)(2,1)}, bf16[8192,128]{1,0:T(8,128)(2,1)S(1)}, u32[]{:S(2)}) copy-start(bf16[8192,128]{1,0:T(8,128)(2,1)S(1)} %pad_maximum_fusion.kv_ref.k_ref.v_ref) | copy-start | bytes 6291460
  83.3 20.8 %collective-permute-start.10 = (bf16[512,512]{1,0:T(8,128)(2,1)S(1)}, bf16[512,512]{1,0:T(8,128)(2,1)S(1)}, u32[]{:S(2)}, u32[]{:S(2)}) collective-permute-start(bf16[512,512]{1,0:T(8,128)(2,1)S(1)} %collective-permute-done.5.rest_5_), channel_id=1, source_target_pairs={{0,1},{1,2},{2,3},{3,0},{4,5},{5,6},{6,7},{7,4},{8,9},{9,10},{10,1... | collective-permute-start | bytes 1572872 | tf_op jit(solution)/shard_map/ppermute | solution.py:40
  85.0 19.2 %collective-permute-start.11 = (bf16[512,512]{1,0:T(8,128)(2,1)S(1)}, bf16[512,512]{1,0:T(8,128)(2,1)S(1)}, u32[]{:S(2)}, u32[]{:S(2)}) collective-permute-start(bf16[512,512]{1,0:T(8,128)(2,1)S(1)} %collective-permute-done.5.rest_5_), channel_id=1, source_target_pairs={{0,3},{1,0},{2,1},{3,2},{4,7},{5,4},{6,5},{7,6},{8,11},{9,8},{10,9... | collective-permute-start | bytes 1572872 | tf_op jit(solution)/shard_map/ppermute | solution.py:40
  86.6 17.5 %collective-permute-start.8 = (bf16[256,512]{1,0:T(8,128)(2,1)S(1)}, bf16[256,512]{1,0:T(8,128)(2,1)S(1)}, u32[]{:S(2)}, u32[]{:S(2)}) collective-permute-start(bf16[256,512]{1,0:T(8,128)(2,1)S(1)} %slice.43), channel_id=1, source_target_pairs={{0,1},{1,2},{2,3},{3,0},{4,5},{5,6},{6,7},{7,4},{8,9},{9,10},{10,1... | collective-permute-start | bytes 786440 | tf_op jit(solution)/shard_map/ppermute | solution.py:40
  87.1 17.0 %collective-permute-start.9 = (bf16[256,512]{1,0:T(8,128)(2,1)S(1)}, bf16[256,512]{1,0:T(8,128)(2,1)S(1)}, u32[]{:S(2)}, u32[]{:S(2)}) collective-permute-start(bf16[256,512]{1,0:T(8,128)(2,1)S(1)} %slice.44), channel_id=1, source_target_pairs={{0,3},{1,0},{2,1},{3,2},{4,7},{5,4},{6,5},{7,6},{8,11},{9,8},{10,9... | collective-permute-start | bytes 786440 | tf_op jit(solution)/shard_map/ppermute | solution.py:40
  110.2 10.6 %collective-permute-start.12 = (bf16[256,512]{1,0:T(8,128)(2,1)}, bf16[256,512]{1,0:T(8,128)(2,1)}, u32[]{:S(2)}, u32[]{:S(2)}) collective-permute-start(bf16[256,512]{1,0:T(8,128)(2,1)} %slice.45), channel_id=1, source_target_pairs={{0,1},{1,2},{2,3},{3,0},{4,5},{5,6},{6,7},{7,4},{8,9},{9,10},{10,1... | collective-permute-start | bytes 786440 | tf_op jit(solution)/shard_map/ppermute | solution.py:40
  112.4 8.4 %collective-permute-start.13 = (bf16[256,512]{1,0:T(8,128)(2,1)}, bf16[256,512]{1,0:T(8,128)(2,1)}, u32[]{:S(2)}, u32[]{:S(2)}) collective-permute-start(bf16[256,512]{1,0:T(8,128)(2,1)} %slice.46), channel_id=1, source_target_pairs={{0,3},{1,0},{2,1},{3,2},{4,7},{5,4},{6,5},{7,6},{8,11},{9,8},{10,9... | collective-permute-start | bytes 786440 | tf_op jit(solution)/shard_map/ppermute | solution.py:40
  117.0 38.9 %collective-permute-start.15 = (bf16[3,512,512]{2,1,0:T(8,128)(2,1)}, bf16[3,512,512]{2,1,0:T(8,128)(2,1)}, u32[]{:S(2)}, u32[]{:S(2)}) collective-permute-start(bf16[3,512,512]{2,1,0:T(8,128)(2,1)} %pad_maximum_fusion.1), channel_id=1, source_target_pairs={{0,16},{8,24},{16,0},{24,8},{32,48},{40,56},{48,32},{56,40},{64,80... | collective-permute-start | bytes 4718600 | tf_op jit(solution)/shard_map/ppermute | solution.py:32
  130.7 2.3 collective-permute-start.14
  160.3 2.0 collective-permute-start.16
  168.4 3.5 %collective-permute-start.17 = (bf16[8,256,256]{2,1,0:T(8,128)(2,1)S(1)}, bf16[8,256,256]{2,1,0:T(8,128)(2,1)S(1)}, u32[]{:S(2)}, u32[]{:S(2)}) collective-permute-start(bf16[8,256,256]{2,1,0:T(8,128)(2,1)S(1)} %get-tuple-element.62), channel_id=1, source_target_pairs={{0,8},{8,0},{16,24},{24,16},{32,40},{40,32},{48,56},{56,48},{64,72... | collective-permute-start | bytes 3145736 | tf_op jit(solution)/shard_map/ppermute | solution.py:32
  (22 other events, 125.4 us)
Sparse Core Ops, SparseCore 0:
  9.7 58.5 all-gather.4
  70.0 30.7 all-gather.6

commit v6 on v5

--- a/solution.py
+++ b/solution.py
@@ -12,12 +12,13 @@
 KEY_BLOCK = 256
 MOST = 2560
 CHUNKS = 2
+PAIR = 2
 MASKED = -1e30
 SCALE = 1.0 / math.sqrt(HEAD_WIDTH)
 LOG2E = 1.0 / math.log(2.0)
 BF16 = jnp.bfloat16
 F32 = jnp.float32
-VMEM_LIMIT = 18 * 2**20
+VMEM_LIMIT = 22 * 2**20
 
 FIRST, COUNT, CLEAR, CORE, TABLE = 0, 1, 2, 3, 4
 
@@ -44,6 +45,10 @@
     return lax.optimization_barrier((value, *others))[0]
 
 
+def in_hbm(value):
+    return pltpu.with_memory_space_constraint(value, pltpu.HBM)
+
+
 def dot(left, right):
     return lax.dot_general(left, right, (((1,), (0,)), ((), ())), preferred_element_type=F32)
 
@@ -59,7 +64,14 @@
 def forward_kernel(info, pos_ref, start_ref, q_ref, kv_ref, probs_ref, out_ref, score, vt):
     first, count = info[FIRST], info[COUNT]
     rows = q_ref.shape[0]
-    query_t = q_ref[...].T
+    heads = q_ref.shape[1] // HEAD_WIDTH
+    query_t = jnp.concatenate(
+        [q_ref[:, h * HEAD_WIDTH : (h + 1) * HEAD_WIDTH].T for h in range(heads)], axis=1
+    )
+    wide = heads * rows
+
+    def groups(values):
+        return values.reshape(KEY_BLOCK // 8, 8, wide)
 
     @pl.when(pl.program_id(0) == 0)
     def _():
@@ -67,7 +79,6 @@
             source = info[TABLE + 16 + first + index]
             vt[:, block_rows(index)] = kv_ref[block_rows(source), :].T
             return 0
-
         lax.fori_loop(0, count, turn, 0)
 
     def product(index):
@@ -76,35 +87,41 @@
     def masked_step(index, top):
         key_pos = (first + index) * KEY_BLOCK + lax.broadcasted_iota(jnp.int32, (KEY_BLOCK, rows), 0)
         live = (key_pos >= start_ref[...]) & (key_pos <= pos_ref[...])
-        raw = jnp.where(live, product(index), MASKED)
+        raw = product(index)
+        raw = jnp.concatenate(
+            [jnp.where(live, raw[:, h * rows : (h + 1) * rows], MASKED) for h in range(heads)], axis=1
+        )
         score[block_rows(index), :] = raw
-        return jnp.maximum(top, jnp.max(raw, axis=0, keepdims=True))
+        return jnp.maximum(top, jnp.max(groups(raw), axis=0))
 
     def clear_step(index, top):
         raw = product(index)
         score[block_rows(index), :] = raw
-        return jnp.maximum(top, jnp.max(raw, axis=0, keepdims=True))
+        return jnp.maximum(top, jnp.max(groups(raw), axis=0))
 
     clear = jnp.minimum(info[CLEAR] - first, count - 1)
-    top = jnp.full((1, rows), MASKED, F32)
+    top = jnp.full((8, wide), MASKED, F32)
     top = lax.fori_loop(0, clear, masked_step, top)
     top = lax.fori_loop(clear, count - 1, clear_step, top)
     top = masked_step(count - 1, top)
+    top = jnp.max(top, axis=0, keepdims=True) * (SCALE * LOG2E)
 
     def mass_step(index, mass):
-        weights = jnp.exp2((score[block_rows(index), :] - top) * (SCALE * LOG2E))
+        weights = jnp.exp2(score[block_rows(index), :] * (SCALE * LOG2E) - top)
         score[block_rows(index), :] = weights
-        return mass + jnp.sum(weights, axis=0, keepdims=True)
-
-    mass = lax.fori_loop(0, count, mass_step, jnp.zeros((1, rows), F32))
-    share = 1.0 / mass
-
-    def probs_step(index, total):
+        return mass + jnp.sum(groups(weights), axis=0)
+
+    mass = lax.fori_loop(0, count, mass_step, jnp.zeros((8, wide), F32))
+    share = 1.0 / jnp.sum(mass, axis=0, keepdims=True)
+    out_ref[...] = jnp.zeros_like(out_ref)
+
+    def probs_step(index, _):
         probs = (score[block_rows(index), :] * share).astype(BF16)
         probs_ref[block_rows(index), :] = probs
-        return total + dot(vt[:, block_rows(index)], probs)
-
-    out_ref[...] = lax.fori_loop(0, count, probs_step, jnp.zeros((HEAD_WIDTH, rows), F32))
+        out_ref[...] += dot(vt[:, block_rows(index)], probs)
+        return 0
+
+    lax.fori_loop(0, count, probs_step, 0)
 
 
 def most_blocks(rows):
@@ -116,23 +133,24 @@
     heads = width // HEAD_WIDTH // CHUNKS
     live = most_blocks(rows) * KEY_BLOCK
     line = pl.BlockSpec((1, rows), lambda h, r: (0, 0))
+    steps = heads // PAIR
     return pl.pallas_call(
         forward_kernel,
         grid_spec=pltpu.PrefetchScalarGridSpec(
             num_scalar_prefetch=1,
-            grid=(heads,),
+            grid=(steps,),
             in_specs=[
                 line,
                 line,
-                pl.BlockSpec((rows, HEAD_WIDTH), lambda h, r: (0, part * heads + h)),
+                pl.BlockSpec((rows, PAIR * HEAD_WIDTH), lambda h, r: (0, part * steps + h)),
                 pl.BlockSpec(kv.shape, lambda h, r: (0, 0)),
             ],
             out_specs=[
-                pl.BlockSpec((live, rows), lambda h, r: (0, h)),
-                pl.BlockSpec((HEAD_WIDTH, rows), lambda h, r: (0, h)),
+                pl.BlockSpec((live, PAIR * rows), lambda h, r: (0, h)),
+                pl.BlockSpec((HEAD_WIDTH, PAIR * rows), lambda h, r: (0, h)),
             ],
             scratch_shapes=[
-                pltpu.VMEM((live, rows), F32),
+                pltpu.VMEM((live, PAIR * rows), F32),
                 pltpu.VMEM((HEAD_WIDTH, live), BF16),
             ],
         ),
@@ -141,18 +159,16 @@
             jax.ShapeDtypeStruct((HEAD_WIDTH, heads * rows), F32),
         ],
         compiler_params=pltpu.CompilerParams(vmem_limit_bytes=VMEM_LIMIT),
-        cost_estimate=pl.CostEstimate(
-            flops=16 * 10**9, bytes_accessed=10 * 2**20, transcendentals=0
-        ),
+        cost_estimate=pl.CostEstimate(flops=10**10, bytes_accessed=10 * 2**20, transcendentals=0),
         name="forward%d" % part,
-    )(info, query_pos, query_start, queries, kv)
+    )(info, query_pos, query_start, in_hbm(queries), in_hbm(kv))
 
 
 def backward_kernel(heads, part, info, probs_ref, out_ref, grad_ref, q_ref, k_ref, v_ref, *rest):
     if part:
-        old_own, old_other, _, gq_ref, own_ref, other_ref, grad_t, delta, total_q, other = rest
+        old_own, old_other, _, gq_ref, own_ref, other_ref, grad_t, stack, delta, total_q, dscores, other = rest
     else:
-        gq_ref, own_ref, other_ref, grad_t, delta, total_q = rest
+        gq_ref, own_ref, other_ref, grad_t, stack, delta, total_q, dscores = rest
         other = other_ref
     step = pl.program_id(0)
     count = info[COUNT]
@@ -169,26 +185,24 @@
         total_q[...] = jnp.zeros_like(total_q)
         for h in range(heads):
             cols = slice(h * rows, (h + 1) * rows)
-            turned = grad_ref[:, h * HEAD_WIDTH : (h + 1) * HEAD_WIDTH].T
+            wide = slice(h * HEAD_WIDTH, (h + 1) * HEAD_WIDTH)
+            turned = grad_ref[:, wide].T
             grad_t[:, cols] = turned
+            stack[cols, :HEAD_WIDTH] = q_ref[:, wide]
+            stack[cols, HEAD_WIDTH:] = grad_ref[:, wide]
             delta[:, cols] = jnp.sum(turned.astype(F32) * out_ref[:, cols], axis=0, keepdims=True)
 
     @pl.when(step < count)
     def _():
         block = info[FIRST] + step
-        values = v_ref[...]
         keys_t = k_ref[...].T
-        key_sum = jnp.zeros((KEY_BLOCK, HEAD_WIDTH), F32)
-        value_sum = jnp.zeros((KEY_BLOCK, HEAD_WIDTH), F32)
         for h in range(heads):
             cols = slice(h * rows, (h + 1) * rows)
-            wide = slice(h * HEAD_WIDTH, (h + 1) * HEAD_WIDTH)
-            probs = probs_ref[:, cols]
-            dprob = dot(values, grad_t[:, cols])
-            dscore = (probs.astype(F32) * (dprob - delta[:, cols])).astype(BF16)
-            value_sum = value_sum + dot(probs, grad_ref[:, wide])
-            key_sum = key_sum + dot(dscore, q_ref[:, wide])
-            total_q[:, cols] += dot(keys_t, dscore)
+            dprob = dot(v_ref[...], grad_t[:, cols])
+            dscores[:, cols] = (probs_ref[:, cols].astype(F32) * (dprob - delta[:, cols])).astype(BF16)
+        total_q[...] += dot(keys_t, dscores[...])
+        key_sum = dot(dscores[...], stack[:, :HEAD_WIDTH])
+        value_sum = dot(probs_ref[...], stack[:, HEAD_WIDTH:])
 
         def add(ref):
             ref[block // 2, :, :HEAD_WIDTH] += key_sum * SCALE
@@ -220,8 +234,10 @@
     gq_spec = pl.BlockSpec((rows, heads * HEAD_WIDTH), lambda i, r: (0, part))
     scratch = [
         pltpu.VMEM((HEAD_WIDTH, heads * rows), BF16),
+        pltpu.VMEM((heads * rows, 2 * HEAD_WIDTH), BF16),
         pltpu.VMEM((1, heads * rows), F32),
         pltpu.VMEM((HEAD_WIDTH, heads * rows), F32),
+        pltpu.VMEM((KEY_BLOCK, heads * rows), BF16),
     ]
     in_specs = [
         pl.BlockSpec((KEY_BLOCK, heads * rows), lambda i, r: (near(i, r), 0)),
@@ -254,11 +270,9 @@
         ],
         input_output_aliases=aliases,
         compiler_params=pltpu.CompilerParams(vmem_limit_bytes=VMEM_LIMIT),
-        cost_estimate=pl.CostEstimate(
-            flops=8 * 10**9, bytes_accessed=10 * 2**20, transcendentals=0
-        ),
+        cost_estimate=pl.CostEstimate(flops=8 * 10**9, bytes_accessed=10 * 2**20, transcendentals=0),
         name="backward%d" % part,
-    )(info, probs, outs, grads, queries, kv, kv, *carried)
+    )(info, in_hbm(probs), outs, grads, in_hbm(queries), in_hbm(kv), in_hbm(kv), *carried)
 
 
 def project_kernel(grad_count, slots, *rest):
@@ -308,7 +322,7 @@
             transcendentals=0,
         ),
         name="project%d" % part,
-    )(slots, *grads, *[stack for stack, _ in stacks])
+    )(slots, *grads, *[in_hbm(stack) for stack, _ in stacks])
 
 
 def local(queries, keys, values, grad_out, out_weight, lengths):
@@ -352,7 +366,6 @@
     ring = lax.all_to_all(
         jnp.broadcast_to(chip, (8, *chip.shape)), "dp", 0, 0, axis_index_groups=groups, tiled=True
     ).reshape(-1, HEAD_WIDTH)
-    kv = jnp.concatenate([ring, dp_move(ring, 0, 0, 1)], axis=0)
 
     def far(ring):
         half = ring[0].shape[0] // 2
@@ -363,15 +376,14 @@
 
     grad0 = both(chip_grad)
     grad_pair = tensor_move(chip_grad, 1, 0)
-    kv, grad0, grad_pair, paired = lax.optimization_barrier((kv, grad0, grad_pair, paired))
-    first_part = forward(0, info, query_pos, query_start, queries, kv)
+    ring, grad0, grad_pair = lax.optimization_barrier((ring, grad0, grad_pair))
+    kv = jnp.concatenate([ring, dp_move(ring, 0, 0, 1)], axis=0)
     grad_far0 = far(grad0)
     grad1 = both(grad_pair)
+    kv, paired = lax.optimization_barrier((kv, paired))
+    first_part = forward(0, info, query_pos, query_start, queries, kv)
     first_part, grad_far0, grad1 = lax.optimization_barrier((first_part, grad_far0, grad1))
-    second_part = forward(1, info, query_pos, query_start, after(queries, first_part[1]), kv)
     grad_far1 = far(grad1)
-    parts = [first_part, second_part]
-    all_grad = grad0 + grad_far0 + grad1 + grad_far1
 
     rest = jnp.concatenate(
         [
@@ -380,7 +392,11 @@
         ],
         axis=0,
     )
-    rest = dp_move(rest, 0, 1, 0)
+    later = lax.optimization_barrier((queries, rest, first_part[1]))
+    rest = dp_move(later[1], 0, 1, 0)
+    second_part = forward(1, info, query_pos, query_start, later[0], kv)
+    parts = [first_part, second_part]
+    all_grad = grad0 + grad_far0 + grad1 + grad_far1
 
     t = lax.axis_index("tensor")
 

time: 232 us -> 209 us (0.901); the launches traced: 231 us -> 212 us
  local copies, waits for them, and re-layouts: 24.8 us -> 13.2 us
  blocking collectives: 51.1 us -> 40.7 us
  Pallas kernels: 24.6 us -> 30.9 us
  starting transfers between devices: 30.4 us -> 27 us
    all_to_all x1, waiting for transfers between devices: 25.6 us -> 2.02 us  [local(): lax.all_to_all(jnp.broadcast_to(chip, (8, *chip.shape)), 'dp', 0, 0, axis...]
    ppermute x9, waiting for transfers between devices: 29.6 us -> 43.4 us  [dp_move(): return lax.ppermute(value, 'dp', pairs)]
    unnamed x50 -> x24, local copies, waits for them, and re-layouts: 17.1 us -> 5.97 us
    all_to_all x1, blocking collectives: 51.1 us -> 40.7 us  [local(): lax.all_to_all(chip_sums, 'dp', 0, 0, axis_index_groups=groups, tiled=True)]
    ppermute x9, waiting for transfers between devices: 17.5 us -> 26 us  [tensor_move(): return lax.ppermute(value, 'tensor', pairs)]
    pallas_call x2, Pallas kernels: 6.78 us -> 9.14 us  [backward(): pl.pallas_call(functools.partial(backward_kernel, heads, part), grid_spec...]
  transfers between devices with their start and end apart: 21 -> 21, of which waited for: 10 -> 11; matrix products, arithmetic and copies ran while one was open for 6% -> 6% of each run, Pallas kernels for 7% -> 10%
where the time goes in v6:
time: 209 us; the launch traced here: 212 us
  waiting for transfers between devices  72.1 us (34%)
  blocking collectives  40.7 us (19%)
  Pallas kernels  30.9 us (15%)
  starting transfers between devices  27 us (13%)
  between operations  20.5 us (10%)
  local copies, waits for them, and re-layouts  13.2 us (6%)
  other arithmetic  7.49 us (4%)
    ppermute x9, waiting for transfers between devices, dp_move(): return lax.ppermute(value, 'dp', pairs)  43.4 us
    all_to_all x1, blocking collectives, local(): lax.all_to_all(chip_sums, 'dp', 0, 0, axis_index_groups=groups, tiled=True)  40.7 us
    ppermute x9, waiting for transfers between devices, tensor_move(): return lax.ppermute(value, 'tensor', pairs)  26 us
    ppermute x9, starting transfers between devices, tensor_move(): return lax.ppermute(value, 'tensor', pairs)  12.5 us
    pallas_call x2, Pallas kernels, forward(): pl.pallas_call(forward_kernel, grid_spec=pltpu.PrefetchScalarGridSpec(num...  11 us
    pallas_call x2, Pallas kernels, project(): pl.pallas_call(functools.partial(project_kernel, len(grads)), grid=(1,),...  10.8 us
    pallas_call x2, Pallas kernels, backward(): pl.pallas_call(functools.partial(backward_kernel, heads, part), grid_spec...  9.14 us
    all_to_all x1, starting transfers between devices, local(): lax.all_to_all(jnp.broadcast_to(chip, (8, *chip.shape)), 'dp', 0, 0, axis...  7.83 us
  transfers between devices with their start and end apart: 21, of which 11 were waited for; matrix products, arithmetic and copies ran while one was open for 6% of the time, Pallas kernels for 10%

profile of v6, /device:TPU:0, one launch (start us, length us, event | category | flops | bytes accessed | tf_op | source)
XLA Modules:
  0.0 211.9 jit_solution(5298993230301197510)
XLA Ops:
  11.3 7.8 %all-to-all-start = ((bf16[8,512,128]{2,1,0:T(8,128)(2,1)}), bf16[8,512,128]{2,1,0:T(8,128)(2,1)}, u32[]{:S(2)}, u32[]{:S(2)}) async-start(bf16[8,512,128]{2,1,0:T(8,128)(2,1)} %broadcast_in_dim.31), calls=%async_computation | async-start | bytes 2097152 | tf_op jit(solution)/shard_map/all_to_all | solution.py:366
  22.0 3.0 %collective-permute-start.3 = (bf16[512,512]{1,0:T(8,128)(2,1)S(1)}, bf16[512,512]{1,0:T(8,128)(2,1)S(1)}, u32[]{:S(2)}, u32[]{:S(2)}) collective-permute-start(bf16[512,512]{1,0:T(8,128)(2,1)S(1)} %pad_maximum_fusion.2.rest_0_), channel_id=1, source_target_pairs={{0,3},{1,0},{2,1},{3,2},{4,7},{5,4},{6,5},{7,6},{8,11},{9,8},{10,9... | collective-permute-start | bytes 1572872 | tf_op jit(solution)/shard_map/ppermute | solution.py:41
  25.0 18.5 %collective-permute-done.4.rest_5_ = bf16[512,512]{1,0:T(8,128)(2,1)S(1)} collective-permute-done((bf16[512,512]{1,0:T(8,128)(2,1)S(1)}, bf16[512,512]{1,0:T(8,128)(2,1)S(1)}, u32[]{:S(2)}, u32[]{:S(2)}) %collective-permute-start.4) | collective-permute-done | bytes 524320 | tf_op jit(solution)/shard_map/ppermute | solution.py:41
  43.6 2.0 all-to-all-done
  46.7 1.9 collective-permute-start.7
  51.1 22.9 %collective-permute-done.6 = bf16[512,512]{1,0:T(8,128)(2,1)S(1)} collective-permute-done((bf16[512,512]{1,0:T(8,128)(2,1)}, bf16[512,512]{1,0:T(8,128)(2,1)S(1)}, u32[]{:S(2)}, u32[]{:S(2)}) %collective-permute-start.6) | collective-permute-done | bytes 524320 | tf_op jit(solution)/shard_map/ppermute | solution.py:33
  81.8 3.1 %collective-permute-start.11 = (bf16[512,512]{1,0:T(8,128)(2,1)S(1)}, bf16[512,512]{1,0:T(8,128)(2,1)S(1)}, u32[]{:S(2)}, u32[]{:S(2)}) collective-permute-start(bf16[512,512]{1,0:T(8,128)(2,1)S(1)} %collective-permute-done.4.rest_5_), channel_id=1, source_target_pairs={{0,3},{1,0},{2,1},{3,2},{4,7},{5,4},{6,5},{7,6},{8,11},{9,8},{10,9... | collective-permute-start | bytes 1572872 | tf_op jit(solution)/shard_map/ppermute | solution.py:41
  84.9 3.3 %collective-permute-start.9 = (bf16[256,512]{1,0:T(8,128)(2,1)S(1)}, bf16[256,512]{1,0:T(8,128)(2,1)S(1)}, u32[]{:S(2)}, u32[]{:S(2)}) collective-permute-start(bf16[256,512]{1,0:T(8,128)(2,1)S(1)} %slice.44), channel_id=1, source_target_pairs={{0,3},{1,0},{2,1},{3,2},{4,7},{5,4},{6,5},{7,6},{8,11},{9,8},{10,9... | collective-permute-start | bytes 786440 | tf_op jit(solution)/shard_map/ppermute | solution.py:41
  88.2 3.0 %pad_maximum_fusion.kv_ref.k_ref.v_ref = bf16[8192,128]{1,0:T(8,128)(2,1)} fusion(bf16[4096,128]{1,0:T(8,128)(2,1)} %collective-permute-done.5, bf16[4096,128]{1,0:T(8,128)(2,1)} %bitcast.11), kind=kLoop, calls=%fused_computation | loop fusion | flops 4194304 | bytes 4194304 | tf_op jit(solution)/shard_map/concatenate | solution.py:380
  91.2 5.5 %forward0.1 = (bf16[2816,1024]{1,0:T(8,128)(2,1)}, f32[128,1024]{1,0:T(8,128)S(1)}) custom-call(s32[36]{0:T(128)S(1)} %concatenate.15.info, s32[1,256]{1,0:T(1,128)S(1)} %iota_add_fusion.pos_ref, s32[1,256]{1,0:T(1,128)S(1)} %bitcast.27, bf16[256,1024]{1,0:T(8,128)(2,1)} %q_ref.6, bf16[8192,128]{1,0:T(8,128)(2,1)} %pad_maximum_fusion.kv_ref.k_ref.v_ref), custom_call_target="tpu_custom_call" | custom-call | flops 10000000000 | bytes 10485760 | tf_op jit(solution)/shard_map/forward0/pallas_call | solution.py:137
  97.6 4.0 %collective-permute-done.9.rest_4_ = bf16[256,512]{1,0:T(8,128)(2,1)S(1)} collective-permute-done((bf16[256,512]{1,0:T(8,128)(2,1)S(1)}, bf16[256,512]{1,0:T(8,128)(2,1)S(1)}, u32[]{:S(2)}, u32[]{:S(2)}) %collective-permute-start.9) | collective-permute-done | bytes 262176 | tf_op jit(solution)/shard_map/ppermute | solution.py:41
  101.6 3.4 %collective-permute-done.8.rest_3_ = bf16[256,512]{1,0:T(8,128)(2,1)S(1)} collective-permute-done((bf16[256,512]{1,0:T(8,128)(2,1)S(1)}, bf16[256,512]{1,0:T(8,128)(2,1)S(1)}, u32[]{:S(2)}, u32[]{:S(2)}) %collective-permute-start.8) | collective-permute-done | bytes 262176 | tf_op jit(solution)/shard_map/ppermute | solution.py:41
  107.5 1.7 collective-permute-start.12
  112.0 1.8 collective-permute-start.15
  113.9 5.4 %forward1.1 = (bf16[2816,1024]{1,0:T(8,128)(2,1)}, f32[128,1024]{1,0:T(8,128)S(1)}) custom-call(s32[36]{0:T(128)S(1)} %concatenate.15.info, s32[1,256]{1,0:T(1,128)S(1)} %iota_add_fusion.pos_ref, s32[1,256]{1,0:T(1,128)S(1)} %bitcast.28, bf16[256,1024]{1,0:T(8,128)(2,1)} %q_ref.6, bf16[8192,128]{1,0:T(8,128)(2,1)} %pad_maximum_fusion.kv_ref.k_ref.v_ref), custom_call_target="tpu_custom_call" | custom-call | flops 10000000000 | bytes 10485760 | tf_op jit(solution)/shard_map/forward1/pallas_call | solution.py:137
  121.1 5.8 %project0.1 = (f32[256,512]{1,0:T(8,128)S(1)}, f32[256,512]{1,0:T(8,128)}) custom-call(s32[8]{0:T(128)S(1)} %stack.75.slots, bf16[512,512]{1,0:T(8,128)(2,1)S(1)} %pad_maximum_fusion.2.rest_0_, bf16[512,512]{1,0:T(8,128)(2,1)S(1)} %collective-permute-done.2.rest_1_, bf16[512,512]{1,0:T(8,128)(2,1)S(1)} %collective-permute-done.3.rest_2_, ...), custom_call_target="tpu_custom_call" | custom-call | flops 2147483648 | bytes 10485760 | tf_op jit(solution)/shard_map/project0/pallas_call | solution.py:309
  127.8 2.2 %collective-permute-done.14 = f32[256,512]{1,0:T(8,128)} collective-permute-done((f32[256,512]{1,0:T(8,128)}, f32[256,512]{1,0:T(8,128)}, u32[]{:S(2)}, u32[]{:S(2)}) %collective-permute-start.14) | collective-permute-done | bytes 524320 | tf_op jit(solution)/shard_map/ppermute | solution.py:33
  132.3 4.5 %backward0.1 = (bf16[256,1024]{1,0:T(8,128)(2,1)}, f32[8,256,256]{2,1,0:T(8,128)S(1)}, f32[8,256,256]{2,1,0:T(8,128)S(1)}) custom-call(s32[36]{0:T(128)S(1)} %concatenate.15.info, bf16[2816,1024]{1,0:T(8,128)(2,1)} %get-tuple-element.46.probs_ref, f32[128,1024]{1,0:T(8,128)S(1)} %copy-done.7, bf16[256,512]{1,0:T(8,128)(2,1)S(1)} %add_convert_fusion.2.grad_ref, ...), custom_call_target="tpu_custom_call" | custom-call | flops 8000000000 | bytes 10485760 | tf_op jit(solution)/shard_map/backward0/pallas_call | solution.py:257
  136.8 11.4 %collective-permute-done.15.rest_12_ = bf16[3,512,512]{2,1,0:T(8,128)(2,1)} collective-permute-done((bf16[3,512,512]{2,1,0:T(8,128)(2,1)}, bf16[3,512,512]{2,1,0:T(8,128)(2,1)}, u32[]{:S(2)}, u32[]{:S(2)}) %collective-permute-start.15) | collective-permute-done | bytes 1572896 | tf_op jit(solution)/shard_map/ppermute | solution.py:33
  148.2 5.0 %project1.1 = (f32[256,512]{1,0:T(8,128)S(1)}, f32[256,512]{1,0:T(8,128)S(1)}) custom-call(s32[8]{0:T(128)S(1)} %stack.70.slots, bf16[512,512]{1,0:T(8,128)(2,1)S(1)} %pad_maximum_fusion.2.rest_0_, bf16[512,512]{1,0:T(8,128)(2,1)S(1)} %collective-permute-done.2.rest_1_, bf16[512,512]{1,0:T(8,128)(2,1)S(1)} %collective-permute-done.3.rest_2_, ...), custom_call_target="tpu_custom_call" | custom-call | flops 2147483648 | bytes 10485760 | tf_op jit(solution)/shard_map/project1/pallas_call | solution.py:309
  153.3 1.9 collective-permute-done.16
  155.3 4.6 %backward1.1 = (bf16[256,1024]{1,0:T(8,128)(2,1)}, f32[8,256,256]{2,1,0:T(8,128)S(1)}, bf16[8,256,256]{2,1,0:T(8,128)(2,1)S(1)}) custom-call(s32[36]{0:T(128)S(1)} %concatenate.15.info, bf16[2816,1024]{1,0:T(8,128)(2,1)} %get-tuple-element.44.probs_ref, f32[128,1024]{1,0:T(8,128)S(1)} %copy-done.5, ...), custom_call_target="tpu_custom_call", output_to_operand_aliasing={{0}: (9, {})} | custom-call | flops 8000000000 | bytes 10485760 | tf_op jit(solution)/shard_map/backward1/pallas_call | solution.py:257
  160.9 2.3 %collective-permute-done.17 = bf16[8,256,256]{2,1,0:T(8,128)(2,1)S(1)} collective-permute-done((bf16[8,256,256]{2,1,0:T(8,128)(2,1)S(1)}, bf16[8,256,256]{2,1,0:T(8,128)(2,1)S(1)}, u32[]{:S(2)}, u32[]{:S(2)}) %collective-permute-start.17) | collective-permute-done | bytes 1048608 | tf_op jit(solution)/shard_map/ppermute | solution.py:33
  163.5 40.7 %all_to_all.10 = bf16[8,256,256]{2,1,0:T(8,128)(2,1)S(1)} all-to-all(bf16[8,256,256]{2,1,0:T(8,128)(2,1)S(1)} %add_convert_fusion), channel_id=1, replica_groups={{0,16,32,48,64,80,96,112},{8,24,40,56,72,88,104,120},{1,17,33,49,65,81,..., dimensions={0} | all-to-all | bytes 2097152 | tf_op jit(solution)/shard_map/all_to_all | solution.py:434
  (80 shorter events, 25.4 us)
Async XLA Ops:
  7.2 102.0 %all-gather.5.cloned.1.call-start = ((), (), s32[]{:S(2)}) async-start(), calls=%async_computation.2 | async-start | bytes 5242880 | tf_op jit(solution)/shard_map/all_gather | solution.py:357
  8.9 1.3 collective-permute-start
  11.3 34.3 %copy-start.8 = (bf16[1024,512]{1,0:T(8,128)(2,1)S(1)}, bf16[1024,512]{1,0:T(8,128)(2,1)}, u32[]{:S(2)}) copy-start(bf16[1024,512]{1,0:T(8,128)(2,1)} %param.10) | copy-start | bytes 3145732
  11.3 34.3 %all-to-all-start = ((bf16[8,512,128]{2,1,0:T(8,128)(2,1)}), bf16[8,512,128]{2,1,0:T(8,128)(2,1)}, u32[]{:S(2)}, u32[]{:S(2)}) async-start(bf16[8,512,128]{2,1,0:T(8,128)(2,1)} %broadcast_in_dim.31), calls=%async_computation | async-start | bytes 2097152 | tf_op jit(solution)/shard_map/all_to_all | solution.py:366
  19.2 31.0 %copy-start.11 = (s32[8]{0:T(128)S(1)}, s32[8]{0:T(128)}, u32[]{:S(2)}) copy-start(s32[8]{0:T(128)} %param.11) | copy-start | bytes 100
  19.2 101.0 %all-gather.7.cloned.1.call-start = ((), (), s32[]{:S(2)}) async-start(), calls=%async_computation.3 | async-start | bytes 2621440 | tf_op jit(solution)/shard_map/all_gather | solution.py:360
  19.3 1.6 collective-permute-start.1
  20.9 22.7 %collective-permute-start.4 = (bf16[512,512]{1,0:T(8,128)(2,1)S(1)}, bf16[512,512]{1,0:T(8,128)(2,1)S(1)}, u32[]{:S(2)}, u32[]{:S(2)}) collective-permute-start(bf16[512,512]{1,0:T(8,128)(2,1)S(1)} %pad_maximum_fusion.2.rest_0_), channel_id=1, source_target_pairs={{0,4},{1,5},{2,6},{3,7},{4,0},{5,1},{6,2},{7,3},{8,12},{9,13},{10,... | collective-permute-start | bytes 1572872 | tf_op jit(solution)/shard_map/ppermute | solution.py:41
  22.0 21.6 %collective-permute-start.3 = (bf16[512,512]{1,0:T(8,128)(2,1)S(1)}, bf16[512,512]{1,0:T(8,128)(2,1)S(1)}, u32[]{:S(2)}, u32[]{:S(2)}) collective-permute-start(bf16[512,512]{1,0:T(8,128)(2,1)S(1)} %pad_maximum_fusion.2.rest_0_), channel_id=1, source_target_pairs={{0,3},{1,0},{2,1},{3,2},{4,7},{5,4},{6,5},{7,6},{8,11},{9,8},{10,9... | collective-permute-start | bytes 1572872 | tf_op jit(solution)/shard_map/ppermute | solution.py:41
  25.0 18.5 %collective-permute-start.2 = (bf16[512,512]{1,0:T(8,128)(2,1)S(1)}, bf16[512,512]{1,0:T(8,128)(2,1)S(1)}, u32[]{:S(2)}, u32[]{:S(2)}) collective-permute-start(bf16[512,512]{1,0:T(8,128)(2,1)S(1)} %pad_maximum_fusion.2.rest_0_), channel_id=1, source_target_pairs={{0,1},{1,2},{2,3},{3,0},{4,5},{5,6},{6,7},{7,4},{8,9},{9,10},{10,1... | collective-permute-start | bytes 1572872 | tf_op jit(solution)/shard_map/ppermute | solution.py:41
  45.6 42.6 %collective-permute-start.5 = (bf16[4096,128]{1,0:T(8,128)(2,1)}, bf16[4096,128]{1,0:T(8,128)(2,1)}, u32[]{:S(2)}, u32[]{:S(2)}) collective-permute-start(bf16[4096,128]{1,0:T(8,128)(2,1)} %bitcast.11), channel_id=1, source_target_pairs={{0,8},{8,0},{16,24},{24,16},{32,40},{40,32},{48,56},{56,48},{64,72... | collective-permute-start | bytes 3145736 | tf_op jit(solution)/shard_map/ppermute | solution.py:33
  46.7 44.6 %collective-permute-start.7 = (bf16[512,512]{1,0:T(8,128)(2,1)}, bf16[512,512]{1,0:T(8,128)(2,1)}, u32[]{:S(2)}, u32[]{:S(2)}) collective-permute-start(bf16[512,512]{1,0:T(8,128)(2,1)} %get-tuple-element.70), channel_id=1, source_target_pairs={{0,16},{8,24},{16,0},{24,8},{32,48},{40,56},{48,32},{56,40},{64,80... | collective-permute-start | bytes 1572872 | tf_op jit(solution)/shard_map/ppermute | solution.py:33
  48.6 25.4 %collective-permute-start.6 = (bf16[512,512]{1,0:T(8,128)(2,1)}, bf16[512,512]{1,0:T(8,128)(2,1)S(1)}, u32[]{:S(2)}, u32[]{:S(2)}) collective-permute-start(bf16[512,512]{1,0:T(8,128)(2,1)} %get-tuple-element.71), channel_id=1, source_target_pairs={{0,16},{8,24},{16,0},{24,8},{32,48},{40,56},{48,32},{56,40},{64,80... | collective-permute-start | bytes 1572872 | tf_op jit(solution)/shard_map/ppermute | solution.py:33
  81.8 23.9 %collective-permute-start.11 = (bf16[512,512]{1,0:T(8,128)(2,1)S(1)}, bf16[512,512]{1,0:T(8,128)(2,1)S(1)}, u32[]{:S(2)}, u32[]{:S(2)}) collective-permute-start(bf16[512,512]{1,0:T(8,128)(2,1)S(1)} %collective-permute-done.4.rest_5_), channel_id=1, source_target_pairs={{0,3},{1,0},{2,1},{3,2},{4,7},{5,4},{6,5},{7,6},{8,11},{9,8},{10,9... | collective-permute-start | bytes 1572872 | tf_op jit(solution)/shard_map/ppermute | solution.py:41
  84.9 20.8 %collective-permute-start.10 = (bf16[512,512]{1,0:T(8,128)(2,1)S(1)}, bf16[512,512]{1,0:T(8,128)(2,1)S(1)}, u32[]{:S(2)}, u32[]{:S(2)}) collective-permute-start(bf16[512,512]{1,0:T(8,128)(2,1)S(1)} %collective-permute-done.4.rest_5_), channel_id=1, source_target_pairs={{0,1},{1,2},{2,3},{3,0},{4,5},{5,6},{6,7},{7,4},{8,9},{9,10},{10,1... | collective-permute-start | bytes 1572872 | tf_op jit(solution)/shard_map/ppermute | solution.py:41
  84.9 16.6 %collective-permute-start.9 = (bf16[256,512]{1,0:T(8,128)(2,1)S(1)}, bf16[256,512]{1,0:T(8,128)(2,1)S(1)}, u32[]{:S(2)}, u32[]{:S(2)}) collective-permute-start(bf16[256,512]{1,0:T(8,128)(2,1)S(1)} %slice.44), channel_id=1, source_target_pairs={{0,3},{1,0},{2,1},{3,2},{4,7},{5,4},{6,5},{7,6},{8,11},{9,8},{10,9... | collective-permute-start | bytes 786440 | tf_op jit(solution)/shard_map/ppermute | solution.py:41
  88.2 16.7 %collective-permute-start.8 = (bf16[256,512]{1,0:T(8,128)(2,1)S(1)}, bf16[256,512]{1,0:T(8,128)(2,1)S(1)}, u32[]{:S(2)}, u32[]{:S(2)}) collective-permute-start(bf16[256,512]{1,0:T(8,128)(2,1)S(1)} %slice.43), channel_id=1, source_target_pairs={{0,1},{1,2},{2,3},{3,0},{4,5},{5,6},{6,7},{7,4},{8,9},{9,10},{10,1... | collective-permute-start | bytes 786440 | tf_op jit(solution)/shard_map/ppermute | solution.py:41
  107.2 13.0 %collective-permute-start.13 = (bf16[256,512]{1,0:T(8,128)(2,1)}, bf16[256,512]{1,0:T(8,128)(2,1)}, u32[]{:S(2)}, u32[]{:S(2)}) collective-permute-start(bf16[256,512]{1,0:T(8,128)(2,1)} %slice.46), channel_id=1, source_target_pairs={{0,3},{1,0},{2,1},{3,2},{4,7},{5,4},{6,5},{7,6},{8,11},{9,8},{10,9... | collective-permute-start | bytes 786440 | tf_op jit(solution)/shard_map/ppermute | solution.py:41
  107.5 12.7 %collective-permute-start.12 = (bf16[256,512]{1,0:T(8,128)(2,1)}, bf16[256,512]{1,0:T(8,128)(2,1)}, u32[]{:S(2)}, u32[]{:S(2)}) collective-permute-start(bf16[256,512]{1,0:T(8,128)(2,1)} %slice.45), channel_id=1, source_target_pairs={{0,1},{1,2},{2,3},{3,0},{4,5},{5,6},{6,7},{7,4},{8,9},{9,10},{10,1... | collective-permute-start | bytes 786440 | tf_op jit(solution)/shard_map/ppermute | solution.py:41
  112.0 36.2 %collective-permute-start.15 = (bf16[3,512,512]{2,1,0:T(8,128)(2,1)}, bf16[3,512,512]{2,1,0:T(8,128)(2,1)}, u32[]{:S(2)}, u32[]{:S(2)}) collective-permute-start(bf16[3,512,512]{2,1,0:T(8,128)(2,1)} %pad_maximum_fusion.1), channel_id=1, source_target_pairs={{0,16},{8,24},{16,0},{24,8},{32,48},{40,56},{48,32},{56,40},{64,80... | collective-permute-start | bytes 4718600 | tf_op jit(solution)/shard_map/ppermute | solution.py:33
  127.7 2.3 %collective-permute-start.14 = (f32[256,512]{1,0:T(8,128)}, f32[256,512]{1,0:T(8,128)}, u32[]{:S(2)}, u32[]{:S(2)}) collective-permute-start(f32[256,512]{1,0:T(8,128)} %get-tuple-element.55), channel_id=1, source_target_pairs={{0,8},{8,0},{16,24},{24,16},{32,40},{40,32},{48,56},{56,48},{64,72... | collective-permute-start | bytes 1572872 | tf_op jit(solution)/shard_map/ppermute | solution.py:33
  132.3 16.0 %copy-start.2 = (bf16[256,512]{1,0:T(8,128)(2,1)S(1)}, bf16[256,512]{1,0:T(8,128)(2,1)}, u32[]{:S(2)}) copy-start(bf16[256,512]{1,0:T(8,128)(2,1)} %copy-done) | copy-start | bytes 786436
  153.2 2.0 collective-permute-start.16
  159.9 3.2 %collective-permute-start.17 = (bf16[8,256,256]{2,1,0:T(8,128)(2,1)S(1)}, bf16[8,256,256]{2,1,0:T(8,128)(2,1)S(1)}, u32[]{:S(2)}, u32[]{:S(2)}) collective-permute-start(bf16[8,256,256]{2,1,0:T(8,128)(2,1)S(1)} %get-tuple-element.66), channel_id=1, source_target_pairs={{0,8},{8,0},{16,24},{24,16},{32,40},{40,32},{48,56},{56,48},{64,72... | collective-permute-start | bytes 3145736 | tf_op jit(solution)/shard_map/ppermute | solution.py:33
  (9 other events, 24.4 us)
Sparse Core Ops, SparseCore 0:
  9.7 58.6 all-gather.4
  74.9 30.9 all-gather.6

commit v7 on v6

--- a/solution.py
+++ b/solution.py
@@ -164,7 +164,7 @@
     )(info, query_pos, query_start, in_hbm(queries), in_hbm(kv))
 
 
-def backward_kernel(heads, part, info, probs_ref, out_ref, grad_ref, q_ref, k_ref, v_ref, *rest):
+def backward_kernel(heads, part, info, probs_ref, out_ref, mine_ref, got_ref, q_ref, k_ref, v_ref, *rest):
     if part:
         old_own, old_other, _, gq_ref, own_ref, other_ref, grad_t, stack, delta, total_q, dscores, other = rest
     else:
@@ -186,10 +186,11 @@
         for h in range(heads):
             cols = slice(h * rows, (h + 1) * rows)
             wide = slice(h * HEAD_WIDTH, (h + 1) * HEAD_WIDTH)
-            turned = grad_ref[:, wide].T
+            grad = (mine_ref[:, wide] + got_ref[:, wide]).astype(BF16)
+            turned = grad.T
             grad_t[:, cols] = turned
             stack[cols, :HEAD_WIDTH] = q_ref[:, wide]
-            stack[cols, HEAD_WIDTH:] = grad_ref[:, wide]
+            stack[cols, HEAD_WIDTH:] = grad
             delta[:, cols] = jnp.sum(turned.astype(F32) * out_ref[:, cols], axis=0, keepdims=True)
 
     @pl.when(step < count)
@@ -221,7 +222,7 @@
             other_ref[...] = other[...].astype(BF16)
 
 
-def backward(part, info, probs, outs, grads, queries, kv, carried):
+def backward(part, info, probs, outs, mine, got, queries, kv, carried):
     rows, width = queries.shape
     heads = width // HEAD_WIDTH // CHUNKS
     last = part == CHUNKS - 1
@@ -243,6 +244,7 @@
         pl.BlockSpec((KEY_BLOCK, heads * rows), lambda i, r: (near(i, r), 0)),
         pl.BlockSpec((HEAD_WIDTH, heads * rows), lambda i, r: (0, 0)),
         pl.BlockSpec((rows, heads * HEAD_WIDTH), lambda i, r: (0, 0)),
+        pl.BlockSpec((rows, heads * HEAD_WIDTH), lambda i, r: (0, 0)),
         pl.BlockSpec((rows, heads * HEAD_WIDTH), lambda i, r: (0, part)),
         pl.BlockSpec((KEY_BLOCK, HEAD_WIDTH), lambda i, r: (r[TABLE + r[FIRST] + near(i, r)], 0)),
         pl.BlockSpec(
@@ -253,7 +255,7 @@
     if part:
         in_specs += [sum_spec, sum_spec, pl.BlockSpec(memory_space=pl.ANY)]
         scratch.append(pltpu.VMEM(sums, F32))
-        aliases = {9: 0}
+        aliases = {10: 0}
     return pl.pallas_call(
         functools.partial(backward_kernel, heads, part),
         grid_spec=pltpu.PrefetchScalarGridSpec(
@@ -272,7 +274,7 @@
         compiler_params=pltpu.CompilerParams(vmem_limit_bytes=VMEM_LIMIT),
         cost_estimate=pl.CostEstimate(flops=8 * 10**9, bytes_accessed=10 * 2**20, transcendentals=0),
         name="backward%d" % part,
-    )(info, in_hbm(probs), outs, grads, in_hbm(queries), in_hbm(kv), in_hbm(kv), *carried)
+    )(info, in_hbm(probs), outs, mine, got, in_hbm(queries), in_hbm(kv), in_hbm(kv), *carried)
 
 
 def project_kernel(grad_count, slots, *rest):
@@ -299,13 +301,10 @@
     depth = grads[0].shape[1]
     chips = slots.shape[0]
     tokens = sum(ref.shape[0] for ref in grads) // chips
-    features = stacks[0][0].shape[1] // CHUNKS
+    features = stacks[0].shape[1]
     half = jax.ShapeDtypeStruct((tokens // 2, features), F32)
     out_spec = pl.BlockSpec((tokens // 2, features), lambda i: (0, 0))
-    stack_specs = [
-        pl.BlockSpec((stack.shape[0], features, depth), lambda i, at=at: (0, at, 0))
-        for stack, at in stacks
-    ]
+    stack_specs = [pl.BlockSpec(stack.shape, lambda i: (0, 0, 0)) for stack in stacks]
     return pl.pallas_call(
         functools.partial(project_kernel, len(grads)),
         grid=(1,),
@@ -322,7 +321,7 @@
             transcendentals=0,
         ),
         name="project%d" % part,
-    )(slots, *grads, *[in_hbm(stack) for stack, _ in stacks])
+    )(slots, *grads, *[in_hbm(stack) for stack in stacks])
 
 
 def local(queries, keys, values, grad_out, out_weight, lengths):
@@ -354,10 +353,14 @@
     chip_grad = jnp.concatenate([mine, dp_move(other, 0, 0, 1)], axis=0)
 
     groups_x = [[x_ * 4 + zc for x_ in range(4)] for zc in range(4)]
-    plane = lax.all_gather(out_weight, "dp", axis=0, axis_index_groups=groups_x)
+
+    def gather_x(block):
+        return lax.all_gather(block, "dp", axis=0, axis_index_groups=groups_x)
+
     size = out_weight.shape[0] // CHUNKS
-    paired = [dp_move(out_weight[j * size : (j + 1) * size], 0, 1, 0) for j in range(CHUNKS)]
-    other_plane = lax.all_gather(paired[0], "dp", axis=0, axis_index_groups=groups_x)
+    own = [out_weight[:size], out_weight[size:]]
+    planes = [gather_x(own[0])]
+    planes.append(gather_x(after(own[1], planes[0])))
 
     groups = [[2 * i + c for i in range(8)] for c in range(2)]
     kept = jnp.where(core == 0, keys, values)
@@ -378,19 +381,17 @@
     grad_pair = tensor_move(chip_grad, 1, 0)
     ring, grad0, grad_pair = lax.optimization_barrier((ring, grad0, grad_pair))
     kv = jnp.concatenate([ring, dp_move(ring, 0, 0, 1)], axis=0)
+    own, _ = lax.optimization_barrier((own, ring))
+    paired = [dp_move(block, 0, 1, 0) for block in own]
+    other_plane = gather_x(after(paired[1], planes[1]))
     grad_far0 = far(grad0)
     grad1 = both(grad_pair)
-    kv, paired = lax.optimization_barrier((kv, paired))
     first_part = forward(0, info, query_pos, query_start, queries, kv)
     first_part, grad_far0, grad1 = lax.optimization_barrier((first_part, grad_far0, grad1))
     grad_far1 = far(grad1)
 
     rest = jnp.concatenate(
-        [
-            lax.dynamic_slice(plane, ((x + i) % 4, size, 0), (1, size, depth))
-            for i in range(1, 4)
-        ],
-        axis=0,
+        [lax.dynamic_slice_in_dim(planes[0], (x + i) % 4, 1, 0) for i in range(1, 4)], axis=0
     )
     later = lax.optimization_barrier((queries, rest, first_part[1]))
     rest = dp_move(later[1], 0, 1, 0)
@@ -410,22 +411,19 @@
 
     same = [slot(i, z) for i in range(4)]
     slots = [
+        jnp.stack(same + [slot(x + i, 1 - z) for i in range(4)]).astype(jnp.int32),
         jnp.stack(same + [slot(i, 1 - z) for i in range(4)]).astype(jnp.int32),
-        jnp.stack(same + [slot(x + i, 1 - z) for i in range(4)]).astype(jnp.int32),
     ]
-    stacks = [
-        [(plane, 0), (other_plane, 0)],
-        [(plane, 1), (paired[1][None], 0), (rest, 0)],
-    ]
+    stacks = [[planes[0], paired[0][None], rest], [planes[1], other_plane]]
 
     slots[0] = after(slots[0], second_part[1])
     carried = ()
     for part in range(CHUNKS):
         mine, other = project(part, slots[part], all_grad, stacks[part])
-        grads = (mine + dp_move(other, 0, 0, 1)).astype(BF16)
+        got = dp_move(other, 0, 0, 1)
         probs, outs = parts[part]
         grad_queries, own_sums, other_sums = backward(
-            part, info, probs, outs, grads, queries, kv, carried
+            part, info, probs, outs, mine, got, queries, kv, carried
         )
         carried = (own_sums, other_sums, grad_queries)
         slots[-1] = after(slots[-1], grad_queries)

time: 209 us -> 225 us (1.077); the launches traced: 212 us -> 225 us
  local copies, waits for them, and re-layouts: 13.2 us -> 22.3 us
  starting transfers between devices: 27 us -> 31.4 us
  other arithmetic: 7.49 us -> 3.43 us
    all_gather x2 -> x3, waiting for transfers between devices: 0.01 us -> 28.3 us  [gather_x(): return lax.all_gather(block, 'dp', axis=0, axis_index_groups=groups_x)]
    ppermute x9, waiting for transfers between devices: 26 us -> 1.13 us  [tensor_move(): return lax.ppermute(value, 'tensor', pairs)]
    unnamed x24 -> x49, local copies, waits for them, and re-layouts: 5.97 us -> 14.2 us
    ppermute x9, starting transfers between devices: 6.56 us -> 9.09 us  [dp_move(): return lax.ppermute(value, 'dp', pairs)]
  transfers between devices with their start and end apart: 21 -> 22, of which waited for: 11 -> 10; matrix products, arithmetic and copies ran while one was open for 6% -> 4% of each run, Pallas kernels for 10% -> 10%
where the time goes in v7:
time: 225 us
  waiting for transfers between devices  73.9 us (33%)
  blocking collectives  42.6 us (19%)
  starting transfers between devices  31.4 us (14%)
  Pallas kernels  31.1 us (14%)
  local copies, waits for them, and re-layouts  22.3 us (10%)
  between operations  19.9 us (9%)
  other arithmetic  3.43 us (2%)
    ppermute x9, waiting for transfers between devices, dp_move(): return lax.ppermute(value, 'dp', pairs)  44.4 us
    all_to_all x1, blocking collectives, local(): lax.all_to_all(chip_sums, 'dp', 0, 0, axis_index_groups=groups, tiled=True)  42.6 us
    all_gather x3, waiting for transfers between devices, gather_x(): return lax.all_gather(block, 'dp', axis=0, axis_index_groups=groups_x)  28.3 us
    ppermute x9, starting transfers between devices, tensor_move(): return lax.ppermute(value, 'tensor', pairs)  14.4 us
    unnamed x49, local copies, waits for them, and re-layouts  14.2 us
    pallas_call x2, Pallas kernels, forward(): pl.pallas_call(forward_kernel, grid_spec=pltpu.PrefetchScalarGridSpec(num...  11.1 us
    pallas_call x2, Pallas kernels, project(): pl.pallas_call(functools.partial(project_kernel, len(grads)), grid=(1,),...  10.6 us
    pallas_call x2, Pallas kernels, backward(): pl.pallas_call(functools.partial(backward_kernel, heads, part), grid_spec...  9.32 us
  transfers between devices with their start and end apart: 22, of which 10 were waited for; matrix products, arithmetic and copies ran while one was open for 4% of the time, Pallas kernels for 10%

profile of v7, /device:TPU:0, one launch (start us, length us, event | category | flops | bytes accessed | tf_op | source)
XLA Modules:
  0.0 224.7 jit_solution(9128615824199054741)
XLA Ops:
  7.2 2.3 %fusion.3 = (bf16[512,512]{1,0:T(8,128)(2,1)}, bf16[512,512]{1,0:T(8,128)(2,1)}) fusion(bf16[1024,512]{1,0:T(8,128)(2,1)} %param.10), kind=kLoop, calls=%fused_computation.29 | loop fusion | bytes 2097152 | tf_op jit(solution)/shard_map/slice | solution.py:361
  12.0 7.8 %all-to-all-start = ((bf16[8,512,128]{2,1,0:T(8,128)(2,1)}), bf16[8,512,128]{2,1,0:T(8,128)(2,1)}, u32[]{:S(2)}, u32[]{:S(2)}) async-start(bf16[8,512,128]{2,1,0:T(8,128)(2,1)} %broadcast_in_dim.31), calls=%async_computation | async-start | bytes 2097152 | tf_op jit(solution)/shard_map/all_to_all | solution.py:369
  21.6 1.6 collective-permute-start.2
  23.3 1.7 collective-permute-start.3
  25.9 26.3 %all-gather.7.cloned.1.call-done = bf16[2048,512]{1,0:T(8,128)(2,1)} async-done(((bf16[512,512]{1,0:T(8,128)(2,1)}), bf16[2048,512]{1,0:T(8,128)(2,1)}) %all-gather.7.cloned.1.call-update) | async-done | bytes 2097168 | tf_op jit(solution)/shard_map/all_gather | solution.py:358
  60.0 1.6 collective-permute-start.8
  61.6 1.7 collective-permute-start.9
  63.7 2.9 %collective-permute-start.7 = (bf16[256,512]{1,0:T(8,128)(2,1)S(1)}, bf16[256,512]{1,0:T(8,128)(2,1)S(1)}, u32[]{:S(2)}, u32[]{:S(2)}) collective-permute-start(bf16[256,512]{1,0:T(8,128)(2,1)S(1)} %slice.43), channel_id=1, source_target_pairs={{0,3},{1,0},{2,1},{3,2},{4,7},{5,4},{6,5},{7,6},{8,11},{9,8},{10,9... | collective-permute-start | bytes 786440 | tf_op jit(solution)/shard_map/ppermute | solution.py:41
  68.0 3.0 %collective-permute-start.15 = (bf16[512,512]{1,0:T(8,128)(2,1)}, bf16[512,512]{1,0:T(8,128)(2,1)}, u32[]{:S(2)}, u32[]{:S(2)}) collective-permute-start(bf16[512,512]{1,0:T(8,128)(2,1)} %get-tuple-element.62), channel_id=1, source_target_pairs={{0,16},{8,24},{16,0},{24,8},{32,48},{40,56},{48,32},{56,40},{64,80... | collective-permute-start | bytes 1572872 | tf_op jit(solution)/shard_map/ppermute | solution.py:33
  73.8 5.5 %forward0.1 = (bf16[2816,1024]{1,0:T(8,128)(2,1)}, f32[128,1024]{1,0:T(8,128)S(1)}) custom-call(s32[36]{0:T(128)S(1)} %concatenate.15.info, s32[1,256]{1,0:T(1,128)S(1)} %iota_add_fusion.pos_ref, s32[1,256]{1,0:T(1,128)S(1)} %bitcast.28, bf16[256,1024]{1,0:T(8,128)(2,1)} %q_ref.6, bf16[8192,128]{1,0:T(8,128)(2,1)} %copy-done.20), custom_call_target="tpu_custom_call" | custom-call | flops 10000000000 | bytes 10485760 | tf_op jit(solution)/shard_map/forward0/pallas_call | solution.py:137
  83.2 2.1 all-gather.9.cloned.1.call-done
  85.3 2.7 %pad_maximum_fusion = bf16[3,512,512]{2,1,0:T(8,128)(2,1)} fusion(bf16[1,512,512]{2,1,0:T(8,128)(2,1)} %get-tuple-element.72, bf16[1,512,512]{2,1,0:T(8,128)(2,1)} %get-tuple-element.73, bf16[1,512,512]{2,1,0:T(8,128)(2,1)} %get-tuple-element.71), kind=kLoop, calls=%fused_computation.1 | loop fusion | flops 1572864 | bytes 3145728 | tf_op jit(solution)/shard_map/concatenate | solution.py:393
  88.0 3.1 %collective-permute-start.13 = (bf16[3,512,512]{2,1,0:T(8,128)(2,1)}, bf16[3,512,512]{2,1,0:T(8,128)(2,1)}, u32[]{:S(2)}, u32[]{:S(2)}) collective-permute-start(bf16[3,512,512]{2,1,0:T(8,128)(2,1)} %pad_maximum_fusion), channel_id=1, source_target_pairs={{0,16},{8,24},{16,0},{24,8},{32,48},{40,56},{48,32},{56,40},{64,80... | collective-permute-start | bytes 4718600 | tf_op jit(solution)/shard_map/ppermute | solution.py:33
  91.6 1.6 collective-permute-start.10
  93.2 1.8 collective-permute-start.11
  95.0 5.6 %forward1.1 = (bf16[2816,1024]{1,0:T(8,128)(2,1)}, f32[128,1024]{1,0:T(8,128)S(1)}) custom-call(s32[36]{0:T(128)S(1)} %concatenate.15.info, s32[1,256]{1,0:T(1,128)S(1)} %iota_add_fusion.pos_ref, s32[1,256]{1,0:T(1,128)S(1)} %bitcast.29, bf16[256,1024]{1,0:T(8,128)(2,1)} %q_ref.6, bf16[8192,128]{1,0:T(8,128)(2,1)} %copy-done.20), custom_call_target="tpu_custom_call" | custom-call | flops 10000000000 | bytes 10485760 | tf_op jit(solution)/shard_map/forward1/pallas_call | solution.py:137
  101.4 35.6 %collective-permute-done.12 = bf16[512,512]{1,0:T(8,128)(2,1)S(1)} collective-permute-done((bf16[512,512]{1,0:T(8,128)(2,1)}, bf16[512,512]{1,0:T(8,128)(2,1)S(1)}, u32[]{:S(2)}, u32[]{:S(2)}) %collective-permute-start.12) | collective-permute-done | bytes 524320 | tf_op jit(solution)/shard_map/ppermute | solution.py:33
  137.8 5.7 %project0.1 = (f32[256,512]{1,0:T(8,128)S(1)}, f32[256,512]{1,0:T(8,128)}) custom-call(s32[8]{0:T(128)S(1)} %stack.75.slots, bf16[512,512]{1,0:T(8,128)(2,1)S(1)} %pad_maximum_fusion.1.rest_0_, bf16[512,512]{1,0:T(8,128)(2,1)S(1)} %collective-permute-done.2.rest_1_, bf16[512,512]{1,0:T(8,128)(2,1)S(1)} %collective-permute-done.3.rest_2_, ...), custom_call_target="tpu_custom_call" | custom-call | flops 2147483648 | bytes 10485760 | tf_op jit(solution)/shard_map/project0/pallas_call | solution.py:308
  144.3 2.2 collective-permute-done.14.got_ref
  148.6 4.7 %backward0.1 = (bf16[256,1024]{1,0:T(8,128)(2,1)}, f32[8,256,256]{2,1,0:T(8,128)S(1)}, f32[8,256,256]{2,1,0:T(8,128)S(1)}) custom-call(s32[36]{0:T(128)S(1)} %concatenate.15.info, bf16[2816,1024]{1,0:T(8,128)(2,1)} %get-tuple-element.47.probs_ref, f32[128,1024]{1,0:T(8,128)S(1)} %copy-done.16, f32[256,512]{1,0:T(8,128)S(1)} %copy-done.8, ...), custom_call_target="tpu_custom_call" | custom-call | flops 8000000000 | bytes 10485760 | tf_op jit(solution)/shard_map/backward0/pallas_call | solution.py:259
  158.9 5.0 %project1.1 = (f32[256,512]{1,0:T(8,128)S(1)}, f32[256,512]{1,0:T(8,128)S(1)}) custom-call(s32[8]{0:T(128)S(1)} %stack.70.slots, bf16[512,512]{1,0:T(8,128)(2,1)S(1)} %pad_maximum_fusion.1.rest_0_, bf16[512,512]{1,0:T(8,128)(2,1)S(1)} %collective-permute-done.2.rest_1_, bf16[512,512]{1,0:T(8,128)(2,1)S(1)} %collective-permute-done.3.rest_2_, ...), custom_call_target="tpu_custom_call" | custom-call | flops 2147483648 | bytes 10485760 | tf_op jit(solution)/shard_map/project1/pallas_call | solution.py:308
  166.4 4.6 %backward1.1 = (bf16[256,1024]{1,0:T(8,128)(2,1)}, f32[8,256,256]{2,1,0:T(8,128)S(1)}, bf16[8,256,256]{2,1,0:T(8,128)(2,1)S(1)}) custom-call(s32[36]{0:T(128)S(1)} %concatenate.15.info, bf16[2816,1024]{1,0:T(8,128)(2,1)} %get-tuple-element.45.probs_ref, f32[128,1024]{1,0:T(8,128)S(1)} %copy-done.14, ...), custom_call_target="tpu_custom_call", output_to_operand_aliasing={{0}: (10, {})} | custom-call | flops 8000000000 | bytes 10485760 | tf_op jit(solution)/shard_map/backward1/pallas_call | solution.py:259
  172.2 2.3 %collective-permute-done.17 = bf16[8,256,256]{2,1,0:T(8,128)(2,1)S(1)} collective-permute-done((bf16[8,256,256]{2,1,0:T(8,128)(2,1)S(1)}, bf16[8,256,256]{2,1,0:T(8,128)(2,1)S(1)}, u32[]{:S(2)}, u32[]{:S(2)}) %collective-permute-start.17) | collective-permute-done | bytes 1048608 | tf_op jit(solution)/shard_map/ppermute | solution.py:33
  174.7 42.6 %all_to_all.10 = bf16[8,256,256]{2,1,0:T(8,128)(2,1)S(1)} all-to-all(bf16[8,256,256]{2,1,0:T(8,128)(2,1)S(1)} %add_convert_fusion), channel_id=1, replica_groups={{0,16,32,48,64,80,96,112},{8,24,40,56,72,88,104,120},{1,17,33,49,65,81,..., dimensions={0} | all-to-all | bytes 2097152 | tf_op jit(solution)/shard_map/all_to_all | solution.py:432
  (106 shorter events, 30.8 us)
Async XLA Ops:
  7.2 45.0 %all-gather.7.cloned.1.call-start = ((), (), s32[]{:S(2)}) async-start(), calls=%async_computation.2 | async-start | bytes 2621440 | tf_op jit(solution)/shard_map/all_gather | solution.py:358
  9.6 1.3 collective-permute-start
  12.0 40.3 %copy-start.23 = (s32[8]{0:T(128)S(1)}, s32[8]{0:T(128)}, u32[]{:S(2)}) copy-start(s32[8]{0:T(128)} %param.11) | copy-start | bytes 100
  12.0 40.5 %all-to-all-start = ((bf16[8,512,128]{2,1,0:T(8,128)(2,1)}), bf16[8,512,128]{2,1,0:T(8,128)(2,1)}, u32[]{:S(2)}, u32[]{:S(2)}) async-start(bf16[8,512,128]{2,1,0:T(8,128)(2,1)} %broadcast_in_dim.31), calls=%async_computation | async-start | bytes 2097152 | tf_op jit(solution)/shard_map/all_to_all | solution.py:369
  19.9 65.4 %all-gather.9.cloned.1.call-start = ((), (), s32[]{:S(2)}) async-start(), calls=%async_computation.3 | async-start | bytes 2621440 | tf_op jit(solution)/shard_map/all_gather | solution.py:358
  20.0 1.6 collective-permute-start.1
  21.6 30.9 %collective-permute-start.2 = (bf16[512,512]{1,0:T(8,128)(2,1)S(1)}, bf16[512,512]{1,0:T(8,128)(2,1)S(1)}, u32[]{:S(2)}, u32[]{:S(2)}) collective-permute-start(bf16[512,512]{1,0:T(8,128)(2,1)S(1)} %pad_maximum_fusion.1.rest_0_), channel_id=1, source_target_pairs={{0,1},{1,2},{2,3},{3,0},{4,5},{5,6},{6,7},{7,4},{8,9},{9,10},{10,1... | collective-permute-start | bytes 1572872 | tf_op jit(solution)/shard_map/ppermute | solution.py:41
  23.3 29.2 %collective-permute-start.3 = (bf16[512,512]{1,0:T(8,128)(2,1)S(1)}, bf16[512,512]{1,0:T(8,128)(2,1)S(1)}, u32[]{:S(2)}, u32[]{:S(2)}) collective-permute-start(bf16[512,512]{1,0:T(8,128)(2,1)S(1)} %pad_maximum_fusion.1.rest_0_), channel_id=1, source_target_pairs={{0,3},{1,0},{2,1},{3,2},{4,7},{5,4},{6,5},{7,6},{8,11},{9,8},{10,9... | collective-permute-start | bytes 1572872 | tf_op jit(solution)/shard_map/ppermute | solution.py:41
  24.9 27.6 %collective-permute-start.4 = (bf16[512,512]{1,0:T(8,128)(2,1)S(1)}, bf16[512,512]{1,0:T(8,128)(2,1)S(1)}, u32[]{:S(2)}, u32[]{:S(2)}) collective-permute-start(bf16[512,512]{1,0:T(8,128)(2,1)S(1)} %pad_maximum_fusion.1.rest_0_), channel_id=1, source_target_pairs={{0,4},{1,5},{2,6},{3,7},{4,0},{5,1},{6,2},{7,3},{8,12},{9,13},{10,... | collective-permute-start | bytes 1572872 | tf_op jit(solution)/shard_map/ppermute | solution.py:41
  52.3 103.8 %all-gather.11.cloned.1.call-start = ((), (), s32[]{:S(2)}) async-start(), calls=%async_computation.4 | async-start | bytes 2621440 | tf_op jit(solution)/shard_map/all_gather | solution.py:358
  52.5 15.5 %collective-permute-start.5 = (bf16[4096,128]{1,0:T(8,128)(2,1)}, bf16[4096,128]{1,0:T(8,128)(2,1)}, u32[]{:S(2)}, u32[]{:S(2)}) collective-permute-start(bf16[4096,128]{1,0:T(8,128)(2,1)} %bitcast.11), channel_id=1, source_target_pairs={{0,8},{8,0},{16,24},{24,16},{32,40},{40,32},{48,56},{56,48},{64,72... | collective-permute-start | bytes 3145736 | tf_op jit(solution)/shard_map/ppermute | solution.py:33
  60.0 22.0 %collective-permute-start.8 = (bf16[512,512]{1,0:T(8,128)(2,1)S(1)}, bf16[512,512]{1,0:T(8,128)(2,1)S(1)}, u32[]{:S(2)}, u32[]{:S(2)}) collective-permute-start(bf16[512,512]{1,0:T(8,128)(2,1)S(1)} %collective-permute-done.4.rest_5_), channel_id=1, source_target_pairs={{0,1},{1,2},{2,3},{3,0},{4,5},{5,6},{6,7},{7,4},{8,9},{9,10},{10,1... | collective-permute-start | bytes 1572872 | tf_op jit(solution)/shard_map/ppermute | solution.py:41
  61.6 20.3 %collective-permute-start.9 = (bf16[512,512]{1,0:T(8,128)(2,1)S(1)}, bf16[512,512]{1,0:T(8,128)(2,1)S(1)}, u32[]{:S(2)}, u32[]{:S(2)}) collective-permute-start(bf16[512,512]{1,0:T(8,128)(2,1)S(1)} %collective-permute-done.4.rest_5_), channel_id=1, source_target_pairs={{0,3},{1,0},{2,1},{3,2},{4,7},{5,4},{6,5},{7,6},{8,11},{9,8},{10,9... | collective-permute-start | bytes 1572872 | tf_op jit(solution)/shard_map/ppermute | solution.py:41
  63.3 17.9 %collective-permute-start.6 = (bf16[256,512]{1,0:T(8,128)(2,1)S(1)}, bf16[256,512]{1,0:T(8,128)(2,1)S(1)}, u32[]{:S(2)}, u32[]{:S(2)}) collective-permute-start(bf16[256,512]{1,0:T(8,128)(2,1)S(1)} %slice.42), channel_id=1, source_target_pairs={{0,1},{1,2},{2,3},{3,0},{4,5},{5,6},{6,7},{7,4},{8,9},{9,10},{10,1... | collective-permute-start | bytes 786440 | tf_op jit(solution)/shard_map/ppermute | solution.py:41
  63.7 17.5 %collective-permute-start.7 = (bf16[256,512]{1,0:T(8,128)(2,1)S(1)}, bf16[256,512]{1,0:T(8,128)(2,1)S(1)}, u32[]{:S(2)}, u32[]{:S(2)}) collective-permute-start(bf16[256,512]{1,0:T(8,128)(2,1)S(1)} %slice.43), channel_id=1, source_target_pairs={{0,3},{1,0},{2,1},{3,2},{4,7},{5,4},{6,5},{7,6},{8,11},{9,8},{10,9... | collective-permute-start | bytes 786440 | tf_op jit(solution)/shard_map/ppermute | solution.py:41
  68.0 15.2 %collective-permute-start.15 = (bf16[512,512]{1,0:T(8,128)(2,1)}, bf16[512,512]{1,0:T(8,128)(2,1)}, u32[]{:S(2)}, u32[]{:S(2)}) collective-permute-start(bf16[512,512]{1,0:T(8,128)(2,1)} %get-tuple-element.62), channel_id=1, source_target_pairs={{0,16},{8,24},{16,0},{24,8},{32,48},{40,56},{48,32},{56,40},{64,80... | collective-permute-start | bytes 1572872 | tf_op jit(solution)/shard_map/ppermute | solution.py:33
  88.0 49.1 %collective-permute-start.13 = (bf16[3,512,512]{2,1,0:T(8,128)(2,1)}, bf16[3,512,512]{2,1,0:T(8,128)(2,1)}, u32[]{:S(2)}, u32[]{:S(2)}) collective-permute-start(bf16[3,512,512]{2,1,0:T(8,128)(2,1)} %pad_maximum_fusion), channel_id=1, source_target_pairs={{0,16},{8,24},{16,0},{24,8},{32,48},{40,56},{48,32},{56,40},{64,80... | collective-permute-start | bytes 4718600 | tf_op jit(solution)/shard_map/ppermute | solution.py:33
  91.2 45.8 %collective-permute-start.12 = (bf16[512,512]{1,0:T(8,128)(2,1)}, bf16[512,512]{1,0:T(8,128)(2,1)S(1)}, u32[]{:S(2)}, u32[]{:S(2)}) collective-permute-start(bf16[512,512]{1,0:T(8,128)(2,1)} %get-tuple-element.55), channel_id=1, source_target_pairs={{0,16},{8,24},{16,0},{24,8},{32,48},{40,56},{48,32},{56,40},{64,80... | collective-permute-start | bytes 1572872 | tf_op jit(solution)/shard_map/ppermute | solution.py:33
  91.6 45.4 %collective-permute-start.10 = (bf16[256,512]{1,0:T(8,128)(2,1)S(1)}, bf16[256,512]{1,0:T(8,128)(2,1)S(1)}, u32[]{:S(2)}, u32[]{:S(2)}) collective-permute-start(bf16[256,512]{1,0:T(8,128)(2,1)S(1)} %slice.44), channel_id=1, source_target_pairs={{0,1},{1,2},{2,3},{3,0},{4,5},{5,6},{6,7},{7,4},{8,9},{9,10},{10,1... | collective-permute-start | bytes 786440 | tf_op jit(solution)/shard_map/ppermute | solution.py:41
  93.2 44.6 %copy-start.1 = (bf16[256,512]{1,0:T(8,128)(2,1)S(1)}, bf16[256,512]{1,0:T(8,128)(2,1)}, u32[]{:S(2)}) copy-start(bf16[256,512]{1,0:T(8,128)(2,1)} %copy-done) | copy-start | bytes 786436
  93.2 43.8 %collective-permute-start.11 = (bf16[256,512]{1,0:T(8,128)(2,1)S(1)}, bf16[256,512]{1,0:T(8,128)(2,1)S(1)}, u32[]{:S(2)}, u32[]{:S(2)}) collective-permute-start(bf16[256,512]{1,0:T(8,128)(2,1)S(1)} %slice.45), channel_id=1, source_target_pairs={{0,3},{1,0},{2,1},{3,2},{4,7},{5,4},{6,5},{7,6},{8,11},{9,8},{10,9... | collective-permute-start | bytes 786440 | tf_op jit(solution)/shard_map/ppermute | solution.py:41
  144.3 2.3 %collective-permute-start.14 = (f32[256,512]{1,0:T(8,128)}, f32[256,512]{1,0:T(8,128)}, u32[]{:S(2)}, u32[]{:S(2)}) collective-permute-start(f32[256,512]{1,0:T(8,128)} %get-tuple-element.58), channel_id=1, source_target_pairs={{0,8},{8,0},{16,24},{24,16},{32,40},{40,32},{48,56},{56,48},{64,72... | collective-permute-start | bytes 1572872 | tf_op jit(solution)/shard_map/ppermute | solution.py:33
  163.8 2.5 %collective-permute-start.16 = (f32[256,512]{1,0:T(8,128)S(1)}, f32[256,512]{1,0:T(8,128)S(1)}, u32[]{:S(2)}, u32[]{:S(2)}) collective-permute-start(f32[256,512]{1,0:T(8,128)S(1)} %get-tuple-element.65), channel_id=1, source_target_pairs={{0,8},{8,0},{16,24},{24,16},{32,40},{40,32},{48,56},{56,48},{64,72... | collective-permute-start | bytes 1572872 | tf_op jit(solution)/shard_map/ppermute | solution.py:33
  171.0 3.5 %collective-permute-start.17 = (bf16[8,256,256]{2,1,0:T(8,128)(2,1)S(1)}, bf16[8,256,256]{2,1,0:T(8,128)(2,1)S(1)}, u32[]{:S(2)}, u32[]{:S(2)}) collective-permute-start(bf16[8,256,256]{2,1,0:T(8,128)(2,1)S(1)} %get-tuple-element.70), channel_id=1, source_target_pairs={{0,8},{8,0},{16,24},{24,16},{32,40},{40,32},{48,56},{56,48},{64,72... | collective-permute-start | bytes 3145736 | tf_op jit(solution)/shard_map/ppermute | solution.py:33
  (22 other events, 71.6 us)
Sparse Core Ops, SparseCore 0:
  9.7 42.5 all-gather.6
  54.5 30.7 all-gather.8
  86.9 30.8 all-gather.10

commit v8 on v7

--- a/solution.py
+++ b/solution.py
@@ -277,40 +277,38 @@
     )(info, in_hbm(probs), outs, mine, got, in_hbm(queries), in_hbm(kv), in_hbm(kv), *carried)
 
 
-def project_kernel(grad_count, slots, *rest):
-    grads, (*stacks, own_ref, other_ref, grad) = rest[:grad_count], rest[grad_count:]
+def project_kernel(grad_count, places, slots, *rest):
+    grads, (*blocks, own_ref, other_ref, grad) = rest[:grad_count], rest[grad_count:]
     half = own_ref.shape[0]
     at = 0
     for ref in grads:
         chip, row, size = at // (2 * half), at % (2 * half), ref.shape[0]
         grad[chip, row : row + size, :] = ref[...]
         at += size
-    k = 0
-    for ref in stacks:
+    for i, (ref, (slot, feature)) in enumerate(zip(blocks, places)):
+        cols = slice(feature, feature + ref.shape[1])
         for j in range(ref.shape[0]):
             for out, row in ((own_ref, 0), (other_ref, half)):
-                term = dot_t(grad[slots[k], row : row + half, :], ref[j])
-                if k == 0:
-                    out[...] = term
+                term = dot_t(grad[slots[slot + j], row : row + half, :], ref[j])
+                if i == 0 and j == 0:
+                    out[:, cols] = term
                 else:
-                    out[...] += term
-            k += 1
-
-
-def project(part, slots, grads, stacks):
+                    out[:, cols] += term
+
+
+def project(part, slots, grads, blocks):
     depth = grads[0].shape[1]
     chips = slots.shape[0]
     tokens = sum(ref.shape[0] for ref in grads) // chips
-    features = stacks[0].shape[1]
+    features = blocks[0][0].shape[1]
     half = jax.ShapeDtypeStruct((tokens // 2, features), F32)
     out_spec = pl.BlockSpec((tokens // 2, features), lambda i: (0, 0))
-    stack_specs = [pl.BlockSpec(stack.shape, lambda i: (0, 0, 0)) for stack in stacks]
     return pl.pallas_call(
-        functools.partial(project_kernel, len(grads)),
+        functools.partial(project_kernel, len(grads), [(slot, at) for _, slot, at in blocks]),
         grid=(1,),
         in_specs=[pl.BlockSpec(memory_space=pltpu.SMEM)]
         + [pl.BlockSpec(ref.shape, lambda i: (0, 0)) for ref in grads]
-        + stack_specs,
+        + [pl.BlockSpec(block.shape, lambda i: (0, 0, 0)) for block, _, _ in blocks],
         out_specs=[out_spec, out_spec],
         out_shape=[half, half],
         scratch_shapes=[pltpu.VMEM((chips, tokens, depth), BF16)],
@@ -321,7 +319,7 @@
             transcendentals=0,
         ),
         name="project%d" % part,
-    )(slots, *grads, *[in_hbm(stack) for stack in stacks])
+    )(slots, *grads, *[in_hbm(block) if block.shape[0] > 1 else block for block, _, _ in blocks])
 
 
 def local(queries, keys, values, grad_out, out_weight, lengths):
@@ -352,16 +350,6 @@
     other = lax.dynamic_slice_in_dim(grad_out, (1 - core) * depth, depth, 1)
     chip_grad = jnp.concatenate([mine, dp_move(other, 0, 0, 1)], axis=0)
 
-    groups_x = [[x_ * 4 + zc for x_ in range(4)] for zc in range(4)]
-
-    def gather_x(block):
-        return lax.all_gather(block, "dp", axis=0, axis_index_groups=groups_x)
-
-    size = out_weight.shape[0] // CHUNKS
-    own = [out_weight[:size], out_weight[size:]]
-    planes = [gather_x(own[0])]
-    planes.append(gather_x(after(own[1], planes[0])))
-
     groups = [[2 * i + c for i in range(8)] for c in range(2)]
     kept = jnp.where(core == 0, keys, values)
     got = dp_move(jnp.where(core == 0, values, keys), 0, 0, 1)
@@ -370,33 +358,52 @@
         jnp.broadcast_to(chip, (8, *chip.shape)), "dp", 0, 0, axis_index_groups=groups, tiled=True
     ).reshape(-1, HEAD_WIDTH)
 
-    def far(ring):
+    def far(move, ring):
         half = ring[0].shape[0] // 2
-        return [tensor_move(ring[1][:half], 0, 1), tensor_move(ring[2][half:], 0, -1)]
-
-    def both(block):
-        return [block, tensor_move(block, 0, 1), tensor_move(block, 0, -1)]
-
-    grad0 = both(chip_grad)
+        return [move(ring[1][:half], 1), move(ring[2][half:], -1)]
+
+    def both(move, block):
+        return [block, move(block, 1), move(block, -1)]
+
+    def along_x(block, step):
+        return dp_move(block, step, 0, 0)
+
+    def along_y(block, step):
+        return tensor_move(block, 0, step)
+
+    grad0 = both(along_y, chip_grad)
     grad_pair = tensor_move(chip_grad, 1, 0)
     ring, grad0, grad_pair = lax.optimization_barrier((ring, grad0, grad_pair))
     kv = jnp.concatenate([ring, dp_move(ring, 0, 0, 1)], axis=0)
-    own, _ = lax.optimization_barrier((own, ring))
+
+    groups_x = [[x_ * 4 + zc for x_ in range(4)] for zc in range(4)]
+
+    def gather_x(block):
+        return lax.all_gather(block, "dp", axis=0, axis_index_groups=groups_x)
+
+    size = out_weight.shape[0] // CHUNKS
+    own, _ = lax.optimization_barrier(([out_weight[:size], out_weight[size:]], ring))
+    plane1 = gather_x(own[1])
     paired = [dp_move(block, 0, 1, 0) for block in own]
-    other_plane = gather_x(after(paired[1], planes[1]))
-    grad_far0 = far(grad0)
-    grad1 = both(grad_pair)
-    first_part = forward(0, info, query_pos, query_start, queries, kv)
-    first_part, grad_far0, grad1 = lax.optimization_barrier((first_part, grad_far0, grad1))
-    grad_far1 = far(grad1)
-
+    kv, grad_pair, own0 = lax.optimization_barrier((kv, grad_pair, own[0]))
+    plane0 = gather_x(own0)
+
+    grad_far0 = far(along_y, grad0)
+    grad1 = both(along_y, grad_pair)
+    parts = [forward(0, info, query_pos, query_start, queries, kv)]
+    parts[0], paired, grad_far0, grad1 = lax.optimization_barrier(
+        (parts[0], paired, grad_far0, grad1)
+    )
+    ring0 = both(along_x, paired[0])
+    grad_far1 = far(along_y, grad1)
     rest = jnp.concatenate(
-        [lax.dynamic_slice_in_dim(planes[0], (x + i) % 4, 1, 0) for i in range(1, 4)], axis=0
+        [lax.dynamic_slice_in_dim(plane1, (x + i) % 4, 1, 0) for i in range(1, 4)], axis=0
     )
-    later = lax.optimization_barrier((queries, rest, first_part[1]))
-    rest = dp_move(later[1], 0, 1, 0)
-    second_part = forward(1, info, query_pos, query_start, later[0], kv)
-    parts = [first_part, second_part]
+    rest, later = lax.optimization_barrier((rest, queries))
+    rest = dp_move(rest, 0, 1, 0)
+    parts.append(forward(1, info, query_pos, query_start, later, kv))
+    parts[1], ring0 = lax.optimization_barrier((parts[1], ring0))
+    ring0 += far(along_x, ring0)
     all_grad = grad0 + grad_far0 + grad1 + grad_far1
 
     t = lax.axis_index("tensor")
@@ -411,22 +418,24 @@
 
     same = [slot(i, z) for i in range(4)]
     slots = [
+        jnp.stack(same + [slot(x + i, 1 - z) for i in (0, -1, 1, 2)]).astype(jnp.int32),
         jnp.stack(same + [slot(x + i, 1 - z) for i in range(4)]).astype(jnp.int32),
-        jnp.stack(same + [slot(i, 1 - z) for i in range(4)]).astype(jnp.int32),
     ]
-    stacks = [[planes[0], paired[0][None], rest], [planes[1], other_plane]]
-
-    slots[0] = after(slots[0], second_part[1])
+    blocks = [
+        [(plane0, 0, 0)] + [(ring0[i][None], 4 + i, 0) for i in range(3)],
+        [(plane1, 0, 0), (paired[1][None], 4, 0), (rest, 5, 0)],
+    ]
+    blocks[0] += [(ring0[3][None], 7, 0), (ring0[4][None], 7, size // 2)]
+
     carried = ()
     for part in range(CHUNKS):
-        mine, other = project(part, slots[part], all_grad, stacks[part])
+        mine, other = project(part, slots[part], all_grad, blocks[part])
         got = dp_move(other, 0, 0, 1)
         probs, outs = parts[part]
         grad_queries, own_sums, other_sums = backward(
             part, info, probs, outs, mine, got, queries, kv, carried
         )
         carried = (own_sums, other_sums, grad_queries)
-        slots[-1] = after(slots[-1], grad_queries)
 
     chip_sums = (own_sums + dp_move(other_sums, 0, 0, 1).astype(F32)).astype(BF16)
     terms = lax.all_to_all(chip_sums, "dp", 0, 0, axis_index_groups=groups, tiled=True)

time: 225 us -> 201 us (0.89)
  waiting for transfers between devices: 73.9 us -> 53.9 us
  blocking collectives: 42.6 us -> 36.6 us
  local copies, waits for them, and re-layouts: 22.3 us -> 18.7 us
  starting transfers between devices: 31.4 us -> 34.7 us
  other arithmetic: 3.43 us -> 5.8 us
    all_gather x3 -> x2, waiting for transfers between devices: 28.3 us -> 0.01 us  [gather_x(): return lax.all_gather(block, 'dp', axis=0, axis_index_groups=groups_x)]
    ppermute x9, waiting for transfers between devices: 1.13 us -> 17.2 us  [tensor_move(): return lax.ppermute(value, 'tensor', pairs)]
    ppermute x9 -> x13, waiting for transfers between devices: 44.4 us -> 36.6 us  [dp_move(): return lax.ppermute(value, 'dp', pairs)]
    unnamed x49 -> x26, local copies, waits for them, and re-layouts: 14.2 us -> 6.88 us
    all_to_all x1, blocking collectives: 42.6 us -> 36.6 us  [local(): lax.all_to_all(chip_sums, 'dp', 0, 0, axis_index_groups=groups, tiled=True)]
    ppermute x9 -> x13, starting transfers between devices: 9.09 us -> 14.4 us  [dp_move(): return lax.ppermute(value, 'dp', pairs)]
    slice x5 -> x7, local copies, waits for them, and re-layouts: 2.32 us -> 7.1 us  [the longest x6 4.85 us: far(): return [move(ring[1][:half], 1), move(ring[2][half:], -1)]]
  transfers between devices with their start and end apart: 22 -> 25, of which waited for: 10 -> 12; matrix products, arithmetic and copies ran while one was open for 4% -> 7% of each run, Pallas kernels for 10% -> 13%
where the time goes in v8:
time: 201 us; the launch traced here: 200 us
  waiting for transfers between devices  53.9 us (27%)
  blocking collectives  36.6 us (18%)
  starting transfers between devices  34.7 us (17%)
  Pallas kernels  30.9 us (15%)
  between operations  19.9 us (10%)
  local copies, waits for them, and re-layouts  18.7 us (9%)
  other arithmetic  5.8 us (3%)
    ppermute x13, waiting for transfers between devices, dp_move(): return lax.ppermute(value, 'dp', pairs)  36.6 us
    all_to_all x1, blocking collectives, local(): lax.all_to_all(chip_sums, 'dp', 0, 0, axis_index_groups=groups, tiled=True)  36.6 us
    ppermute x9, waiting for transfers between devices, tensor_move(): return lax.ppermute(value, 'tensor', pairs)  17.2 us
    ppermute x13, starting transfers between devices, dp_move(): return lax.ppermute(value, 'dp', pairs)  14.4 us
    ppermute x9, starting transfers between devices, tensor_move(): return lax.ppermute(value, 'tensor', pairs)  12.5 us
    pallas_call x2, Pallas kernels, forward(): pl.pallas_call(forward_kernel, grid_spec=pltpu.PrefetchScalarGridSpec(num...  11 us
    pallas_call x2, Pallas kernels, project(): pl.pallas_call(functools.partial(project_kernel, len(grads), [(slot, at)...  10.5 us
    pallas_call x2, Pallas kernels, backward(): pl.pallas_call(functools.partial(backward_kernel, heads, part), grid_spec...  9.33 us
  transfers between devices with their start and end apart: 25, of which 12 were waited for; matrix products, arithmetic and copies ran while one was open for 7% of the time, Pallas kernels for 13%

profile of v8, /device:TPU:0, one launch (start us, length us, event | category | flops | bytes accessed | tf_op | source)
XLA Modules:
  0.0 200.5 jit_solution(13999994818249216546)
XLA Ops:
  10.6 7.7 %all-to-all-start = ((bf16[8,512,128]{2,1,0:T(8,128)(2,1)}), bf16[8,512,128]{2,1,0:T(8,128)(2,1)S(1)}, u32[]{:S(2)}, u32[]{:S(2)}) async-start(bf16[8,512,128]{2,1,0:T(8,128)(2,1)} %broadcast_in_dim.46), calls=%async_computation | async-start | bytes 2097152 | tf_op jit(solution)/shard_map/all_to_all | solution.py:357
  21.2 3.0 %collective-permute-start.3 = (bf16[512,512]{1,0:T(8,128)(2,1)S(1)}, bf16[512,512]{1,0:T(8,128)(2,1)S(1)}, u32[]{:S(2)}, u32[]{:S(2)}) collective-permute-start(bf16[512,512]{1,0:T(8,128)(2,1)S(1)} %pad_maximum_fusion.2.rest_0_), channel_id=1, source_target_pairs={{0,3},{1,0},{2,1},{3,2},{4,7},{5,4},{6,5},{7,6},{8,11},{9,8},{10,9... | collective-permute-start | bytes 1572872 | tf_op jit(solution)/shard_map/ppermute | solution.py:41
  24.2 2.2 %fusion.3 = (bf16[512,512]{1,0:T(8,128)(2,1)}, bf16[512,512]{1,0:T(8,128)(2,1)}) fusion(bf16[1024,512]{1,0:T(8,128)(2,1)} %param.10), kind=kLoop, calls=%fused_computation.28 | loop fusion | bytes 2097152 | tf_op jit(solution)/shard_map/slice | solution.py:385
  26.4 16.3 %collective-permute-done.4.rest_5_ = bf16[512,512]{1,0:T(8,128)(2,1)S(1)} collective-permute-done((bf16[512,512]{1,0:T(8,128)(2,1)S(1)}, bf16[512,512]{1,0:T(8,128)(2,1)S(1)}, u32[]{:S(2)}, u32[]{:S(2)}) %collective-permute-start.4) | collective-permute-done | bytes 524320 | tf_op jit(solution)/shard_map/ppermute | solution.py:41
  42.9 2.8 %collective-permute-done.5 = bf16[4096,128]{1,0:T(8,128)(2,1)} collective-permute-done((bf16[4096,128]{1,0:T(8,128)(2,1)S(1)}, bf16[4096,128]{1,0:T(8,128)(2,1)}, u32[]{:S(2)}, u32[]{:S(2)}) %collective-permute-start.5) | collective-permute-done | bytes 1048608 | tf_op jit(solution)/shard_map/ppermute | solution.py:33
  45.7 2.7 %pad_maximum_fusion.kv_ref.k_ref.v_ref = bf16[8192,128]{1,0:T(8,128)(2,1)} fusion(bf16[4096,128]{1,0:T(8,128)(2,1)} %collective-permute-done.5, bf16[4096,128]{1,0:T(8,128)(2,1)S(1)} %bitcast.35), kind=kLoop, calls=%fused_computation | loop fusion | flops 4194304 | bytes 4194304 | tf_op jit(solution)/shard_map/concatenate | solution.py:377
  48.8 3.1 %collective-permute-start.9 = (bf16[256,512]{1,0:T(8,128)(2,1)S(1)}, bf16[256,512]{1,0:T(8,128)(2,1)S(1)}, u32[]{:S(2)}, u32[]{:S(2)}) collective-permute-start(bf16[256,512]{1,0:T(8,128)(2,1)S(1)} %slice.50), channel_id=1, source_target_pairs={{0,3},{1,0},{2,1},{3,2},{4,7},{5,4},{6,5},{7,6},{8,11},{9,8},{10,9... | collective-permute-start | bytes 786440 | tf_op jit(solution)/shard_map/ppermute | solution.py:41
  58.8 3.9 %collective-permute-start.7 = (bf16[512,512]{1,0:T(8,128)(2,1)}, bf16[512,512]{1,0:T(8,128)(2,1)S(1)}, u32[]{:S(2)}, u32[]{:S(2)}) collective-permute-start(bf16[512,512]{1,0:T(8,128)(2,1)} %get-tuple-element.44), channel_id=1, source_target_pairs={{0,16},{8,24},{16,0},{24,8},{32,48},{40,56},{48,32},{56,40},{64,80... | collective-permute-start | bytes 1572872 | tf_op jit(solution)/shard_map/ppermute | solution.py:33
  62.9 3.2 %collective-permute-start.11 = (bf16[512,512]{1,0:T(8,128)(2,1)S(1)}, bf16[512,512]{1,0:T(8,128)(2,1)S(1)}, u32[]{:S(2)}, u32[]{:S(2)}) collective-permute-start(bf16[512,512]{1,0:T(8,128)(2,1)S(1)} %collective-permute-done.4.rest_5_), channel_id=1, source_target_pairs={{0,3},{1,0},{2,1},{3,2},{4,7},{5,4},{6,5},{7,6},{8,11},{9,8},{10,9... | collective-permute-start | bytes 1572872 | tf_op jit(solution)/shard_map/ppermute | solution.py:41
  66.1 5.5 %forward0.1 = (bf16[2816,1024]{1,0:T(8,128)(2,1)}, f32[128,1024]{1,0:T(8,128)S(1)}) custom-call(s32[36]{0:T(128)S(1)} %concatenate.15.info, s32[1,256]{1,0:T(1,128)S(1)} %iota_add_fusion.pos_ref, s32[1,256]{1,0:T(1,128)S(1)} %bitcast.30, bf16[256,1024]{1,0:T(8,128)(2,1)} %q_ref.6, bf16[8192,128]{1,0:T(8,128)(2,1)} %pad_maximum_fusion.kv_ref.k_ref.v_ref), custom_call_target="tpu_custom_call" | custom-call | flops 10000000000 | bytes 10485760 | tf_op jit(solution)/shard_map/forward0/pallas_call | solution.py:137
  76.4 9.7 %collective-permute-done.6 = bf16[512,512]{1,0:T(8,128)(2,1)} collective-permute-done((bf16[512,512]{1,0:T(8,128)(2,1)}, bf16[512,512]{1,0:T(8,128)(2,1)}, u32[]{:S(2)}, u32[]{:S(2)}) %collective-permute-start.6) | collective-permute-done | bytes 524320 | tf_op jit(solution)/shard_map/ppermute | solution.py:33
  86.2 2.7 %collective-permute-start.13 = (bf16[512,512]{1,0:T(8,128)(2,1)}, bf16[512,512]{1,0:T(8,128)(2,1)}, u32[]{:S(2)}, u32[]{:S(2)}) collective-permute-start(bf16[512,512]{1,0:T(8,128)(2,1)} %collective-permute-done.6), channel_id=1, source_target_pairs={{0,96},{8,104},{16,112},{24,120},{32,0},{40,8},{48,16},{56,24},{64... | collective-permute-start | bytes 1572872 | tf_op jit(solution)/shard_map/ppermute | solution.py:33
  95.1 3.2 %collective-permute-start.16 = (bf16[3,512,512]{2,1,0:T(8,128)(2,1)}, bf16[3,512,512]{2,1,0:T(8,128)(2,1)}, u32[]{:S(2)}, u32[]{:S(2)}) collective-permute-start(bf16[3,512,512]{2,1,0:T(8,128)(2,1)} %pad_maximum_fusion.1), channel_id=1, source_target_pairs={{0,16},{8,24},{16,0},{24,8},{32,48},{40,56},{48,32},{56,40},{64,80... | collective-permute-start | bytes 4718600 | tf_op jit(solution)/shard_map/ppermute | solution.py:33
  98.4 5.5 %forward1.1 = (bf16[2816,1024]{1,0:T(8,128)(2,1)}, f32[128,1024]{1,0:T(8,128)S(1)}) custom-call(s32[36]{0:T(128)S(1)} %concatenate.15.info, s32[1,256]{1,0:T(1,128)S(1)} %iota_add_fusion.pos_ref, s32[1,256]{1,0:T(1,128)S(1)} %bitcast.31, bf16[256,1024]{1,0:T(8,128)(2,1)} %q_ref.6, bf16[8192,128]{1,0:T(8,128)(2,1)} %pad_maximum_fusion.kv_ref.k_ref.v_ref), custom_call_target="tpu_custom_call" | custom-call | flops 10000000000 | bytes 10485760 | tf_op jit(solution)/shard_map/forward1/pallas_call | solution.py:137
  104.7 7.4 %collective-permute-done.13 = bf16[512,512]{1,0:T(8,128)(2,1)} collective-permute-done((bf16[512,512]{1,0:T(8,128)(2,1)}, bf16[512,512]{1,0:T(8,128)(2,1)}, u32[]{:S(2)}, u32[]{:S(2)}) %collective-permute-start.13) | collective-permute-done | bytes 524320 | tf_op jit(solution)/shard_map/ppermute | solution.py:33
  112.0 3.6 %collective-permute-done.12 = bf16[512,512]{1,0:T(8,128)(2,1)} collective-permute-done((bf16[512,512]{1,0:T(8,128)(2,1)}, bf16[512,512]{1,0:T(8,128)(2,1)}, u32[]{:S(2)}, u32[]{:S(2)}) %collective-permute-start.12) | collective-permute-done | bytes 524320 | tf_op jit(solution)/shard_map/ppermute | solution.py:33
  121.1 4.6 %collective-permute-done.19 = bf16[256,512]{1,0:T(8,128)(2,1)} collective-permute-done((bf16[256,512]{1,0:T(8,128)(2,1)}, bf16[256,512]{1,0:T(8,128)(2,1)}, u32[]{:S(2)}, u32[]{:S(2)}) %collective-permute-start.19) | collective-permute-done | bytes 262176 | tf_op jit(solution)/shard_map/ppermute | solution.py:33
  125.6 2.0 %collective-permute-done.18 = bf16[256,512]{1,0:T(8,128)(2,1)} collective-permute-done((bf16[256,512]{1,0:T(8,128)(2,1)}, bf16[256,512]{1,0:T(8,128)(2,1)}, u32[]{:S(2)}, u32[]{:S(2)}) %collective-permute-start.18) | collective-permute-done | bytes 262176 | tf_op jit(solution)/shard_map/ppermute | solution.py:33
  128.6 5.7 %project0.1 = (f32[256,512]{1,0:T(8,128)S(1)}, f32[256,512]{1,0:T(8,128)}) custom-call(s32[8]{0:T(128)S(1)} %stack.66.slots, bf16[512,512]{1,0:T(8,128)(2,1)S(1)} %pad_maximum_fusion.2.rest_0_, bf16[512,512]{1,0:T(8,128)(2,1)S(1)} %collective-permute-done.2.rest_1_, bf16[512,512]{1,0:T(8,128)(2,1)S(1)} %collective-permute-done.3.rest_2_, ...), custom_call_target="tpu_custom_call" | custom-call | flops 2147483648 | bytes 10485760 | tf_op jit(solution)/shard_map/project0/pallas_call | solution.py:306
  137.2 4.9 %project1.1 = (f32[256,512]{1,0:T(8,128)S(1)}, f32[256,512]{1,0:T(8,128)S(1)}) custom-call(s32[8]{0:T(128)S(1)} %stack.64.slots, bf16[512,512]{1,0:T(8,128)(2,1)S(1)} %pad_maximum_fusion.2.rest_0_, bf16[512,512]{1,0:T(8,128)(2,1)S(1)} %collective-permute-done.2.rest_1_, bf16[512,512]{1,0:T(8,128)(2,1)S(1)} %collective-permute-done.3.rest_2_, ...), custom_call_target="tpu_custom_call" | custom-call | flops 2147483648 | bytes 10485760 | tf_op jit(solution)/shard_map/project1/pallas_call | solution.py:306
  142.6 4.7 %backward0.1 = (bf16[256,1024]{1,0:T(8,128)(2,1)}, f32[8,256,256]{2,1,0:T(8,128)S(1)}, f32[8,256,256]{2,1,0:T(8,128)S(1)}) custom-call(s32[36]{0:T(128)S(1)} %concatenate.15.info, bf16[2816,1024]{1,0:T(8,128)(2,1)} %get-tuple-element.69.probs_ref, f32[128,1024]{1,0:T(8,128)S(1)} %copy-done.10, f32[256,512]{1,0:T(8,128)S(1)} %copy-done.6, ...), custom_call_target="tpu_custom_call" | custom-call | flops 8000000000 | bytes 10485760 | tf_op jit(solution)/shard_map/backward0/pallas_call | solution.py:259
  147.4 4.6 %backward1.1 = (bf16[256,1024]{1,0:T(8,128)(2,1)}, f32[8,256,256]{2,1,0:T(8,128)S(1)}, bf16[8,256,256]{2,1,0:T(8,128)(2,1)S(1)}) custom-call(s32[36]{0:T(128)S(1)} %concatenate.15.info, bf16[2816,1024]{1,0:T(8,128)(2,1)} %get-tuple-element.57.probs_ref, f32[128,1024]{1,0:T(8,128)S(1)} %copy-done.8, ...), custom_call_target="tpu_custom_call", output_to_operand_aliasing={{0}: (10, {})} | custom-call | flops 8000000000 | bytes 10485760 | tf_op jit(solution)/shard_map/backward1/pallas_call | solution.py:259
  153.6 2.3 %collective-permute-done.21 = bf16[8,256,256]{2,1,0:T(8,128)(2,1)S(1)} collective-permute-done((bf16[8,256,256]{2,1,0:T(8,128)(2,1)S(1)}, bf16[8,256,256]{2,1,0:T(8,128)(2,1)S(1)}, u32[]{:S(2)}, u32[]{:S(2)}) %collective-permute-start.21) | collective-permute-done | bytes 1048608 | tf_op jit(solution)/shard_map/ppermute | solution.py:33
  156.2 36.6 %all_to_all.10 = bf16[8,256,256]{2,1,0:T(8,128)(2,1)S(1)} all-to-all(bf16[8,256,256]{2,1,0:T(8,128)(2,1)S(1)} %add_convert_fusion), channel_id=1, replica_groups={{0,16,32,48,64,80,96,112},{8,24,40,56,72,88,104,120},{1,17,33,49,65,81,..., dimensions={0} | all-to-all | bytes 2097152 | tf_op jit(solution)/shard_map/all_to_all | solution.py:441
  (90 shorter events, 32.8 us)
Async XLA Ops:
  10.6 32.1 %all-to-all-start = ((bf16[8,512,128]{2,1,0:T(8,128)(2,1)}), bf16[8,512,128]{2,1,0:T(8,128)(2,1)S(1)}, u32[]{:S(2)}, u32[]{:S(2)}) async-start(bf16[8,512,128]{2,1,0:T(8,128)(2,1)} %broadcast_in_dim.46), calls=%async_computation | async-start | bytes 2097152 | tf_op jit(solution)/shard_map/all_to_all | solution.py:357
  18.3 74.0 %all-gather.5.cloned.1.call-start = ((), (), s32[]{:S(2)}) async-start(), calls=%async_computation.2 | async-start | bytes 2621440 | tf_op jit(solution)/shard_map/all_gather | solution.py:382
  18.4 1.6 collective-permute-start.1
  20.1 22.7 %collective-permute-start.4 = (bf16[512,512]{1,0:T(8,128)(2,1)S(1)}, bf16[512,512]{1,0:T(8,128)(2,1)S(1)}, u32[]{:S(2)}, u32[]{:S(2)}) collective-permute-start(bf16[512,512]{1,0:T(8,128)(2,1)S(1)} %pad_maximum_fusion.2.rest_0_), channel_id=1, source_target_pairs={{0,4},{1,5},{2,6},{3,7},{4,0},{5,1},{6,2},{7,3},{8,12},{9,13},{10,... | collective-permute-start | bytes 1572872 | tf_op jit(solution)/shard_map/ppermute | solution.py:41
  21.2 21.6 %collective-permute-start.3 = (bf16[512,512]{1,0:T(8,128)(2,1)S(1)}, bf16[512,512]{1,0:T(8,128)(2,1)S(1)}, u32[]{:S(2)}, u32[]{:S(2)}) collective-permute-start(bf16[512,512]{1,0:T(8,128)(2,1)S(1)} %pad_maximum_fusion.2.rest_0_), channel_id=1, source_target_pairs={{0,3},{1,0},{2,1},{3,2},{4,7},{5,4},{6,5},{7,6},{8,11},{9,8},{10,9... | collective-permute-start | bytes 1572872 | tf_op jit(solution)/shard_map/ppermute | solution.py:41
  24.2 18.6 %collective-permute-start.2 = (bf16[512,512]{1,0:T(8,128)(2,1)S(1)}, bf16[512,512]{1,0:T(8,128)(2,1)S(1)}, u32[]{:S(2)}, u32[]{:S(2)}) collective-permute-start(bf16[512,512]{1,0:T(8,128)(2,1)S(1)} %pad_maximum_fusion.2.rest_0_), channel_id=1, source_target_pairs={{0,1},{1,2},{2,3},{3,0},{4,5},{5,6},{6,7},{7,4},{8,9},{9,10},{10,1... | collective-permute-start | bytes 1572872 | tf_op jit(solution)/shard_map/ppermute | solution.py:41
  42.8 84.9 %all-gather.7.cloned.1.call-start = ((), (), s32[]{:S(2)}) async-start(), calls=%async_computation.3 | async-start | bytes 2621440 | tf_op jit(solution)/shard_map/all_gather | solution.py:382
  42.8 2.9 %collective-permute-start.5 = (bf16[4096,128]{1,0:T(8,128)(2,1)S(1)}, bf16[4096,128]{1,0:T(8,128)(2,1)}, u32[]{:S(2)}, u32[]{:S(2)}) collective-permute-start(bf16[4096,128]{1,0:T(8,128)(2,1)S(1)} %bitcast.34), channel_id=1, source_target_pairs={{0,8},{8,0},{16,24},{24,16},{32,40},{40,32},{48,56},{56,48},{64,72... | collective-permute-start | bytes 3145736 | tf_op jit(solution)/shard_map/ppermute | solution.py:33
  48.8 17.3 %collective-permute-start.9 = (bf16[256,512]{1,0:T(8,128)(2,1)S(1)}, bf16[256,512]{1,0:T(8,128)(2,1)S(1)}, u32[]{:S(2)}, u32[]{:S(2)}) collective-permute-start(bf16[256,512]{1,0:T(8,128)(2,1)S(1)} %slice.50), channel_id=1, source_target_pairs={{0,3},{1,0},{2,1},{3,2},{4,7},{5,4},{6,5},{7,6},{8,11},{9,8},{10,9... | collective-permute-start | bytes 786440 | tf_op jit(solution)/shard_map/ppermute | solution.py:41
  58.8 16.9 %collective-permute-start.7 = (bf16[512,512]{1,0:T(8,128)(2,1)}, bf16[512,512]{1,0:T(8,128)(2,1)S(1)}, u32[]{:S(2)}, u32[]{:S(2)}) collective-permute-start(bf16[512,512]{1,0:T(8,128)(2,1)} %get-tuple-element.44), channel_id=1, source_target_pairs={{0,16},{8,24},{16,0},{24,8},{32,48},{40,56},{48,32},{56,40},{64,80... | collective-permute-start | bytes 1572872 | tf_op jit(solution)/shard_map/ppermute | solution.py:33
  62.7 23.5 %collective-permute-start.6 = (bf16[512,512]{1,0:T(8,128)(2,1)}, bf16[512,512]{1,0:T(8,128)(2,1)}, u32[]{:S(2)}, u32[]{:S(2)}) collective-permute-start(bf16[512,512]{1,0:T(8,128)(2,1)} %get-tuple-element.71), channel_id=1, source_target_pairs={{0,16},{8,24},{16,0},{24,8},{32,48},{40,56},{48,32},{56,40},{64,80... | collective-permute-start | bytes 1572872 | tf_op jit(solution)/shard_map/ppermute | solution.py:33
  62.8 10.5 %collective-permute-start.8 = (bf16[256,512]{1,0:T(8,128)(2,1)S(1)}, bf16[256,512]{1,0:T(8,128)(2,1)S(1)}, u32[]{:S(2)}, u32[]{:S(2)}) collective-permute-start(bf16[256,512]{1,0:T(8,128)(2,1)S(1)} %slice.49), channel_id=1, source_target_pairs={{0,1},{1,2},{2,3},{3,0},{4,5},{5,6},{6,7},{7,4},{8,9},{9,10},{10,1... | collective-permute-start | bytes 786440 | tf_op jit(solution)/shard_map/ppermute | solution.py:41
  62.9 23.3 %collective-permute-start.11 = (bf16[512,512]{1,0:T(8,128)(2,1)S(1)}, bf16[512,512]{1,0:T(8,128)(2,1)S(1)}, u32[]{:S(2)}, u32[]{:S(2)}) collective-permute-start(bf16[512,512]{1,0:T(8,128)(2,1)S(1)} %collective-permute-done.4.rest_5_), channel_id=1, source_target_pairs={{0,3},{1,0},{2,1},{3,2},{4,7},{5,4},{6,5},{7,6},{8,11},{9,8},{10,9... | collective-permute-start | bytes 1572872 | tf_op jit(solution)/shard_map/ppermute | solution.py:41
  66.1 20.1 %collective-permute-start.10 = (bf16[512,512]{1,0:T(8,128)(2,1)S(1)}, bf16[512,512]{1,0:T(8,128)(2,1)S(1)}, u32[]{:S(2)}, u32[]{:S(2)}) collective-permute-start(bf16[512,512]{1,0:T(8,128)(2,1)S(1)} %collective-permute-done.4.rest_5_), channel_id=1, source_target_pairs={{0,1},{1,2},{2,3},{3,0},{4,5},{5,6},{6,7},{7,4},{8,9},{9,10},{10,1... | collective-permute-start | bytes 1572872 | tf_op jit(solution)/shard_map/ppermute | solution.py:41
  86.2 25.9 %collective-permute-start.13 = (bf16[512,512]{1,0:T(8,128)(2,1)}, bf16[512,512]{1,0:T(8,128)(2,1)}, u32[]{:S(2)}, u32[]{:S(2)}) collective-permute-start(bf16[512,512]{1,0:T(8,128)(2,1)} %collective-permute-done.6), channel_id=1, source_target_pairs={{0,96},{8,104},{16,112},{24,120},{32,0},{40,8},{48,16},{56,24},{64... | collective-permute-start | bytes 1572872 | tf_op jit(solution)/shard_map/ppermute | solution.py:33
  88.8 26.8 %collective-permute-start.12 = (bf16[512,512]{1,0:T(8,128)(2,1)}, bf16[512,512]{1,0:T(8,128)(2,1)}, u32[]{:S(2)}, u32[]{:S(2)}) collective-permute-start(bf16[512,512]{1,0:T(8,128)(2,1)} %collective-permute-done.6), channel_id=1, source_target_pairs={{0,32},{8,40},{16,48},{24,56},{32,64},{40,72},{48,80},{56,88},{64,... | collective-permute-start | bytes 1572872 | tf_op jit(solution)/shard_map/ppermute | solution.py:33
  90.3 30.8 %collective-permute-start.15 = (bf16[256,512]{1,0:T(8,128)(2,1)}, bf16[256,512]{1,0:T(8,128)(2,1)}, u32[]{:S(2)}, u32[]{:S(2)}) collective-permute-start(bf16[256,512]{1,0:T(8,128)(2,1)} %slice.52), channel_id=1, source_target_pairs={{0,3},{1,0},{2,1},{3,2},{4,7},{5,4},{6,5},{7,6},{8,11},{9,8},{10,9... | collective-permute-start | bytes 786440 | tf_op jit(solution)/shard_map/ppermute | solution.py:41
  91.1 30.0 %collective-permute-start.14 = (bf16[256,512]{1,0:T(8,128)(2,1)}, bf16[256,512]{1,0:T(8,128)(2,1)}, u32[]{:S(2)}, u32[]{:S(2)}) collective-permute-start(bf16[256,512]{1,0:T(8,128)(2,1)} %slice.51), channel_id=1, source_target_pairs={{0,1},{1,2},{2,3},{3,0},{4,5},{5,6},{6,7},{7,4},{8,9},{9,10},{10,1... | collective-permute-start | bytes 786440 | tf_op jit(solution)/shard_map/ppermute | solution.py:41
  95.1 40.0 %collective-permute-start.16 = (bf16[3,512,512]{2,1,0:T(8,128)(2,1)}, bf16[3,512,512]{2,1,0:T(8,128)(2,1)}, u32[]{:S(2)}, u32[]{:S(2)}) collective-permute-start(bf16[3,512,512]{2,1,0:T(8,128)(2,1)} %pad_maximum_fusion.1), channel_id=1, source_target_pairs={{0,16},{8,24},{16,0},{24,8},{32,48},{40,56},{48,32},{56,40},{64,80... | collective-permute-start | bytes 4718600 | tf_op jit(solution)/shard_map/ppermute | solution.py:33
  119.0 6.7 %collective-permute-start.19 = (bf16[256,512]{1,0:T(8,128)(2,1)}, bf16[256,512]{1,0:T(8,128)(2,1)}, u32[]{:S(2)}, u32[]{:S(2)}) collective-permute-start(bf16[256,512]{1,0:T(8,128)(2,1)} %slice.54), channel_id=1, source_target_pairs={{0,96},{8,104},{16,112},{24,120},{32,0},{40,8},{48,16},{56,24},{64... | collective-permute-start | bytes 786440 | tf_op jit(solution)/shard_map/ppermute | solution.py:33
  119.5 8.1 %collective-permute-start.18 = (bf16[256,512]{1,0:T(8,128)(2,1)}, bf16[256,512]{1,0:T(8,128)(2,1)}, u32[]{:S(2)}, u32[]{:S(2)}) collective-permute-start(bf16[256,512]{1,0:T(8,128)(2,1)} %slice.53), channel_id=1, source_target_pairs={{0,32},{8,40},{16,48},{24,56},{32,64},{40,72},{48,80},{56,88},{64,... | collective-permute-start | bytes 786440 | tf_op jit(solution)/shard_map/ppermute | solution.py:33
  135.1 7.5 %collective-permute-start.20 = (f32[256,512]{1,0:T(8,128)}, f32[256,512]{1,0:T(8,128)}, u32[]{:S(2)}, u32[]{:S(2)}) collective-permute-start(f32[256,512]{1,0:T(8,128)} %get-tuple-element.76), channel_id=1, source_target_pairs={{0,8},{8,0},{16,24},{24,16},{32,40},{40,32},{48,56},{56,48},{64,72... | collective-permute-start | bytes 1572872 | tf_op jit(solution)/shard_map/ppermute | solution.py:33
  142.0 5.3 %collective-permute-start.17 = (f32[256,512]{1,0:T(8,128)S(1)}, f32[256,512]{1,0:T(8,128)S(1)}, u32[]{:S(2)}, u32[]{:S(2)}) collective-permute-start(f32[256,512]{1,0:T(8,128)S(1)} %get-tuple-element.68), channel_id=1, source_target_pairs={{0,8},{8,0},{16,24},{24,16},{32,40},{40,32},{48,56},{56,48},{64,72... | collective-permute-start | bytes 1572872 | tf_op jit(solution)/shard_map/ppermute | solution.py:33
  152.0 3.9 %collective-permute-start.21 = (bf16[8,256,256]{2,1,0:T(8,128)(2,1)S(1)}, bf16[8,256,256]{2,1,0:T(8,128)(2,1)S(1)}, u32[]{:S(2)}, u32[]{:S(2)}) collective-permute-start(bf16[8,256,256]{2,1,0:T(8,128)(2,1)S(1)} %get-tuple-element.82), channel_id=1, source_target_pairs={{0,8},{8,0},{16,24},{24,16},{32,40},{40,32},{48,56},{56,48},{64,72... | collective-permute-start | bytes 3145736 | tf_op jit(solution)/shard_map/ppermute | solution.py:33
  (14 other events, 40.6 us)
Sparse Core Ops, SparseCore 0:
  42.9 32.9 all-gather.4
  77.5 42.0 all-gather.6

commit v9 on v7

v9 whole, which is shorter than its diff:
```python
import functools
import math

import jax
import jax.numpy as jnp
from jax import lax
from jax.experimental import pallas as pl
from jax.experimental.pallas import tpu as pltpu
from jax.sharding import PartitionSpec as P

HEAD_WIDTH = 128
KEY_BLOCK = 256
MOST = 2560
CHUNKS = 2
PAIR = 2
MASKED = -1e30
SCALE = 1.0 / math.sqrt(HEAD_WIDTH)
LOG2E = 1.0 / math.log(2.0)
BF16 = jnp.bfloat16
F32 = jnp.float32
VMEM_LIMIT = 24 * 2**20

FIRST, COUNT, CLEAR, CORE, TABLE = 0, 1, 2, 3, 4


def dp_move(value, dx, dz, dc):
    pairs = []
    for x in range(4):
        for z in range(2):
            for c in range(2):
                target = ((x + dx) % 4) * 4 + ((z + dz) % 2) * 2 + (c + dc) % 2
                pairs.append((x * 4 + z * 2 + c, target))
    return lax.ppermute(value, "dp", pairs)


def tensor_move(value, dz, dy):
    pairs = []
    for z in range(2):
        for y in range(4):
            pairs.append((z * 4 + y, ((z + dz) % 2) * 4 + (y + dy) % 4))
    return lax.ppermute(value, "tensor", pairs)


def after(value, *others):
    return lax.optimization_barrier((value, *others))[0]


def in_hbm(value):
    return pltpu.with_memory_space_constraint(value, pltpu.HBM)


def dot(left, right):
    return lax.dot_general(left, right, (((1,), (0,)), ((), ())), preferred_element_type=F32)


def dot_t(left, right):
    return lax.dot_general(left, right, (((1,), (1,)), ((), ())), preferred_element_type=F32)


def block_rows(index):
    return pl.ds(pl.multiple_of(index * KEY_BLOCK, KEY_BLOCK), KEY_BLOCK)


def forward_kernel(info, pos_ref, start_ref, q_ref, kv_ref, probs_ref, out_ref, score, vt):
    first, count = info[FIRST], info[COUNT]
    rows = q_ref.shape[0]
    heads = q_ref.shape[1] // HEAD_WIDTH
    query_t = jnp.concatenate(
        [q_ref[:, h * HEAD_WIDTH : (h + 1) * HEAD_WIDTH].T for h in range(heads)], axis=1
    )
    wide = heads * rows

    def groups(values):
        return values.reshape(KEY_BLOCK // 8, 8, wide)

    @pl.when(pl.program_id(0) == 0)
    def _():
        def turn(index, _):
            source = info[TABLE + 16 + first + index]
            vt[:, block_rows(index)] = kv_ref[block_rows(source), :].T
            return 0
        lax.fori_loop(0, count, turn, 0)

    def product(index):
        return dot(kv_ref[block_rows(info[TABLE + first + index]), :], query_t)

    def masked_step(index, top):
        key_pos = (first + index) * KEY_BLOCK + lax.broadcasted_iota(jnp.int32, (KEY_BLOCK, rows), 0)
        live = (key_pos >= start_ref[...]) & (key_pos <= pos_ref[...])
        raw = product(index)
        raw = jnp.concatenate(
            [jnp.where(live, raw[:, h * rows : (h + 1) * rows], MASKED) for h in range(heads)], axis=1
        )
        score[block_rows(index), :] = raw
        return jnp.maximum(top, jnp.max(groups(raw), axis=0))

    def clear_step(index, top):
        raw = product(index)
        score[block_rows(index), :] = raw
        return jnp.maximum(top, jnp.max(groups(raw), axis=0))

    clear = jnp.minimum(info[CLEAR] - first, count - 1)
    top = jnp.full((8, wide), MASKED, F32)
    top = lax.fori_loop(0, clear, masked_step, top)
    top = lax.fori_loop(clear, count - 1, clear_step, top)
    top = masked_step(count - 1, top)
    top = jnp.max(top, axis=0, keepdims=True) * (SCALE * LOG2E)

    def mass_step(index, mass):
        weights = jnp.exp2(score[block_rows(index), :] * (SCALE * LOG2E) - top)
        score[block_rows(index), :] = weights
        return mass + jnp.sum(groups(weights), axis=0)

    mass = lax.fori_loop(0, count, mass_step, jnp.zeros((8, wide), F32))
    share = 1.0 / jnp.sum(mass, axis=0, keepdims=True)
    out_ref[...] = jnp.zeros_like(out_ref)

    def probs_step(index, _):
        probs = (score[block_rows(index), :] * share).astype(BF16)
        probs_ref[block_rows(index), :] = probs
        out_ref[...] += dot(vt[:, block_rows(index)], probs)
        return 0

    lax.fori_loop(0, count, probs_step, 0)


def most_blocks(rows):
    return (MOST + rows - 2) // KEY_BLOCK + 1


def forward(info, query_pos, query_start, queries, kv):
    rows, width = queries.shape
    heads = width // HEAD_WIDTH
    live = most_blocks(rows) * KEY_BLOCK
    line = pl.BlockSpec((1, rows), lambda h, r: (0, 0))
    return pl.pallas_call(
        forward_kernel,
        grid_spec=pltpu.PrefetchScalarGridSpec(
            num_scalar_prefetch=1,
            grid=(heads // PAIR,),
            in_specs=[
                line,
                line,
                pl.BlockSpec((rows, PAIR * HEAD_WIDTH), lambda h, r: (0, h)),
                pl.BlockSpec(kv.shape, lambda h, r: (0, 0), pipeline_mode=pl.Buffered(1)),
            ],
            out_specs=[
                pl.BlockSpec((live, PAIR * rows), lambda h, r: (0, h)),
                pl.BlockSpec((HEAD_WIDTH, PAIR * rows), lambda h, r: (0, h)),
            ],
            scratch_shapes=[
                pltpu.VMEM((live, PAIR * rows), F32),
                pltpu.VMEM((HEAD_WIDTH, live), BF16),
            ],
        ),
        out_shape=[
            pltpu.HBM((live, heads * rows), BF16),
            jax.ShapeDtypeStruct((HEAD_WIDTH, heads * rows), F32),
        ],
        compiler_params=pltpu.CompilerParams(vmem_limit_bytes=VMEM_LIMIT),
        cost_estimate=pl.CostEstimate(flops=10**10, bytes_accessed=10 * 2**20, transcendentals=0),
        name="forward",
    )(info, query_pos, query_start, in_hbm(queries), in_hbm(kv))


def backward_kernel(heads, info, *rest):
    terms, rest = rest[: 2 * CHUNKS], rest[2 * CHUNKS :]
    probs_ref, out_ref, q_ref, k_ref, v_ref, gq_ref, own_ref, other_ref, *scratch = rest
    grad_t, stack, delta, total_q, dscores, other = scratch
    step = pl.program_id(0)
    count = info[COUNT]
    rows = q_ref.shape[0]

    @pl.when(step == 0)
    def _():
        own_ref[...] = jnp.zeros_like(own_ref)
        other[...] = jnp.zeros_like(other)
        total_q[...] = jnp.zeros_like(total_q)
        for h in range(heads):
            cols = slice(h * rows, (h + 1) * rows)
            wide = slice(h * HEAD_WIDTH, (h + 1) * HEAD_WIDTH)
            part, at = divmod(h * CHUNKS, heads)
            here = slice(at // CHUNKS * HEAD_WIDTH, (at // CHUNKS + 1) * HEAD_WIDTH)
            mine, got = terms[2 * part], terms[2 * part + 1]
            grad = (mine[:, here] + got[:, here]).astype(BF16)
            turned = grad.T
            grad_t[:, cols] = turned
            stack[cols, :HEAD_WIDTH] = q_ref[:, wide]
            stack[cols, HEAD_WIDTH:] = grad
            delta[:, cols] = jnp.sum(turned.astype(F32) * out_ref[:, cols], axis=0, keepdims=True)

    @pl.when(step < count)
    def _():
        block = info[FIRST] + step
        keys_t = k_ref[...].T
        for h in range(heads):
            cols = slice(h * rows, (h + 1) * rows)
            dprob = dot(v_ref[...], grad_t[:, cols])
            dscores[:, cols] = (probs_ref[:, cols].astype(F32) * (dprob - delta[:, cols])).astype(BF16)
        total_q[...] += dot(keys_t, dscores[...])
        key_sum = dot(dscores[...], stack[:, :HEAD_WIDTH])
        value_sum = dot(probs_ref[...], stack[:, HEAD_WIDTH:])

        def add(ref):
            ref[block // 2, :, :HEAD_WIDTH] += key_sum * SCALE
            ref[block // 2, :, HEAD_WIDTH:] += value_sum

        pl.when(block % 2 == info[CORE])(lambda: add(own_ref))
        pl.when(block % 2 != info[CORE])(lambda: add(other))

    @pl.when(step == count - 1)
    def _():
        for h in range(heads):
            cols = slice(h * rows, (h + 1) * rows)
            wide = slice(h * HEAD_WIDTH, (h + 1) * HEAD_WIDTH)
            gq_ref[:, wide] = (total_q[:, cols].T * SCALE).astype(BF16)
        other_ref[...] = other[...].astype(BF16)


def backward(info, terms, probs, outs, queries, kv):
    rows, width = queries.shape
    heads = width // HEAD_WIDTH
    sums = (8, KEY_BLOCK, 2 * HEAD_WIDTH)

    def near(i, r):
        return jnp.minimum(i, r[COUNT] - 1)

    def once(shape):
        return pl.BlockSpec(shape, lambda i, r: (0,) * len(shape), pipeline_mode=pl.Buffered(1))

    return pl.pallas_call(
        functools.partial(backward_kernel, heads),
        grid_spec=pltpu.PrefetchScalarGridSpec(
            num_scalar_prefetch=1,
            grid=(most_blocks(rows),),
            in_specs=[once(term.shape) for term in terms]
            + [
                pl.BlockSpec((KEY_BLOCK, heads * rows), lambda i, r: (near(i, r), 0)),
                once(outs.shape),
                once(queries.shape),
                pl.BlockSpec(
                    (KEY_BLOCK, HEAD_WIDTH), lambda i, r: (r[TABLE + r[FIRST] + near(i, r)], 0)
                ),
                pl.BlockSpec(
                    (KEY_BLOCK, HEAD_WIDTH), lambda i, r: (r[TABLE + 16 + r[FIRST] + near(i, r)], 0)
                ),
            ],
            out_specs=[once((rows, width)), once(sums), once(sums)],
            scratch_shapes=[
                pltpu.VMEM((HEAD_WIDTH, heads * rows), BF16),
                pltpu.VMEM((heads * rows, 2 * HEAD_WIDTH), BF16),
                pltpu.VMEM((1, heads * rows), F32),
                pltpu.VMEM((HEAD_WIDTH, heads * rows), F32),
                pltpu.VMEM((KEY_BLOCK, heads * rows), BF16),
                pltpu.VMEM(sums, F32),
            ],
        ),
        out_shape=[
            jax.ShapeDtypeStruct((rows, width), BF16),
            jax.ShapeDtypeStruct(sums, F32),
            jax.ShapeDtypeStruct(sums, BF16),
        ],
        compiler_params=pltpu.CompilerParams(vmem_limit_bytes=VMEM_LIMIT),
        cost_estimate=pl.CostEstimate(
            flops=8 * 10**9, bytes_accessed=10 * 2**20, transcendentals=0
        ),
        name="backward",
    )(info, *terms, in_hbm(probs), outs, in_hbm(queries), in_hbm(kv), in_hbm(kv))


def project_kernel(slots, grad_ref, *rest):
    *stacks, own_ref, other_ref = rest
    half = own_ref.shape[0]
    k = 0
    for ref in stacks:
        for j in range(ref.shape[0]):
            for out, row in ((own_ref, 0), (other_ref, half)):
                term = dot_t(grad_ref[slots[k], row : row + half, :], ref[j])
                if k == 0:
                    out[...] = term
                else:
                    out[...] += term
            k += 1


def project(part, slots, grads, stacks):
    chips, tokens, depth = grads.shape
    features = stacks[0].shape[1]
    half = jax.ShapeDtypeStruct((tokens // 2, features), F32)
    out_spec = pl.BlockSpec((tokens // 2, features), lambda i: (0, 0))
    return pl.pallas_call(
        project_kernel,
        grid=(1,),
        in_specs=[pl.BlockSpec(memory_space=pltpu.SMEM)]
        + [pl.BlockSpec(ref.shape, lambda i: (0, 0, 0)) for ref in (grads, *stacks)],
        out_specs=[out_spec, out_spec],
        out_shape=[half, half],
        compiler_params=pltpu.CompilerParams(vmem_limit_bytes=VMEM_LIMIT),
        cost_estimate=pl.CostEstimate(
            flops=2 * tokens * features * depth * chips,
            bytes_accessed=10 * 2**20,
            transcendentals=0,
        ),
        name="project%d" % part,
    )(slots, in_hbm(grads), *[in_hbm(stack) if stack.shape[0] > 1 else stack for stack in stacks])


def local(queries, keys, values, grad_out, out_weight, lengths):
    rows = queries.shape[0]
    rank = lax.axis_index("dp")
    core = rank % 2
    x, z = rank // 4, (rank // 2) % 2

    query_pos = rank * rows + jnp.arange(rows, dtype=jnp.int32)
    ends = jnp.cumsum(lengths)[:-1]
    query_start = jnp.max(
        jnp.where(ends[None, :] <= query_pos[:, None], ends[None, :], 0), axis=1
    )
    first = query_start[0] // KEY_BLOCK
    last = query_pos[-1] // KEY_BLOCK
    clear = (query_start[-1] + KEY_BLOCK - 1) // KEY_BLOCK
    block = jnp.arange(16, dtype=jnp.int32)
    place = block // 2 * 2
    here = place + jnp.where(block % 2 == core, 0, 1)
    there = 16 + place + jnp.where(block % 2 == core, 1, 0)
    table = [jnp.where(core == 0, here, there), jnp.where(core == 0, there, here)]
    scalars = jnp.stack([first, last - first + 1, clear, core])
    info = jnp.concatenate([scalars, *table]).astype(jnp.int32)
    query_pos, query_start = query_pos[None, :], query_start[None, :]

    groups_x = [[x_ * 4 + zc for x_ in range(4)] for zc in range(4)]

    def gather_x(block):
        return lax.all_gather(block, "dp", axis=0, axis_index_groups=groups_x)

    def spread(block, axis, groups):
        copies = jnp.broadcast_to(block, (len(groups[0]), *block.shape))
        return lax.all_to_all(copies, axis, 0, 0, axis_index_groups=groups, tiled=True)

    size = out_weight.shape[0] // CHUNKS
    own = [out_weight[:size], out_weight[size:]]
    plane1 = gather_x(own[1])

    groups = [[2 * i + c for i in range(8)] for c in range(2)]
    kept = jnp.where(core == 0, keys, values)
    got = dp_move(jnp.where(core == 0, values, keys), 0, 0, 1)
    plane0 = gather_x(after(own[0], got))
    ring = spread(jnp.concatenate([kept, got], axis=0), "dp", groups).reshape(-1, HEAD_WIDTH)

    depth = out_weight.shape[1]
    mine = lax.dynamic_slice_in_dim(grad_out, core * depth, depth, 1)
    other = lax.dynamic_slice_in_dim(grad_out, (1 - core) * depth, depth, 1)
    chip_grad = jnp.concatenate([mine, dp_move(other, 0, 0, 1)], axis=0)
    grad_pair = jnp.stack([chip_grad, tensor_move(chip_grad, 1, 0)])
    groups_y = [[z_ * 4 + y_ for y_ in range(4)] for z_ in range(2)]
    all_grad = spread(grad_pair, "tensor", groups_y).reshape(8, 2 * rows, depth)

    paired = [dp_move(block, 0, 1, 0) for block in own]
    ring, paired, grad_pair = lax.optimization_barrier((ring, paired, grad_pair))
    kv = jnp.concatenate([ring, dp_move(ring, 0, 0, 1)], axis=0)
    other_plane = spread(paired[0], "dp", groups_x).reshape(4, size, depth)
    rest = jnp.concatenate(
        [lax.dynamic_slice_in_dim(plane1, (x + i) % 4, 1, 0) for i in range(1, 4)], axis=0
    )
    rest, kv = lax.optimization_barrier((rest, kv))
    rest = dp_move(rest, 0, 1, 0)
    probs, outs = forward(info, query_pos, query_start, queries, kv)

    t = lax.axis_index("tensor")

    def slot(x_, z_):
        source = 2 * (x_ % 4) + z_
        return source % 4 * 2 + jnp.where(source // 4 == t // 4, 0, 1)

    same = [slot(i, z) for i in range(4)]
    slots = [
        jnp.stack(same + [slot(i, 1 - z) for i in range(4)]).astype(jnp.int32),
        jnp.stack(same + [slot(x + i, 1 - z) for i in range(4)]).astype(jnp.int32),
    ]
    slots[0] = after(slots[0], outs)
    stacks = [[plane0, other_plane], [plane1, paired[1][None], rest]]
    terms = []
    for part in range(CHUNKS):
        mine, other = project(part, slots[part], all_grad, stacks[part])
        terms += [mine, dp_move(other, 0, 0, 1)]
    grad_queries, own_sums, other_sums = backward(info, terms, probs, outs, queries, kv)

    chip_sums = (own_sums + dp_move(other_sums, 0, 0, 1).astype(F32)).astype(BF16)
    terms = lax.all_to_all(chip_sums, "dp", 0, 0, axis_index_groups=groups, tiled=True)
    done = jnp.sum(terms.astype(F32), axis=0).astype(BF16)
    return grad_queries, done[:, :HEAD_WIDTH], done[:, HEAD_WIDTH:]


def solution(mesh):
    return jax.shard_map(
        local,
        mesh=mesh,
        in_specs=(
            P("dp", "tensor"),
            P("dp", "tensor"),
            P("dp", "tensor"),
            P("dp", "tensor"),
            P("tensor", "dp"),
            P(),
        ),
        out_specs=(P("dp", "tensor"), P("dp", "tensor"), P("dp", "tensor")),
        check_vma=False,
    )
```

time: 225 us -> 231 us (1.027)
  waiting for transfers between devices: 73.9 us -> 106 us
  blocking collectives: 42.6 us -> 29.8 us
  local copies, waits for them, and re-layouts: 22.3 us -> 15.9 us
  Pallas kernels: 31.1 us -> 24.9 us
  starting transfers between devices: 31.4 us -> 25.2 us
  other arithmetic: 3.43 us -> 8.18 us
    all_to_all x1 -> x3, waiting for transfers between devices: 0.01 us -> 61 us  [spread(): lax.all_to_all(copies, axis, 0, 0, axis_index_groups=groups, tiled=True)]
    all_gather x3 -> x2, waiting for transfers between devices: 28.3 us -> 0.01 us  [gather_x(): return lax.all_gather(block, 'dp', axis=0, axis_index_groups=groups_x)]
    ppermute x9, waiting for transfers between devices: 44.4 us -> 25.3 us  [dp_move(): return lax.ppermute(value, 'dp', pairs)]
    ppermute x9 -> x1, waiting for transfers between devices: 1.13 us -> 19.2 us  [tensor_move(): return lax.ppermute(value, 'tensor', pairs)]
    ppermute x9 -> x1, starting transfers between devices: 14.4 us -> 1.02 us  [tensor_move(): return lax.ppermute(value, 'tensor', pairs)]
    all_to_all x1, blocking collectives: 42.6 us -> 29.8 us  [local(): lax.all_to_all(chip_sums, 'dp', 0, 0, axis_index_groups=groups, tiled=True)]
    unnamed x49 -> x20, local copies, waits for them, and re-layouts: 14.2 us -> 1.95 us
    all_to_all x1 -> x3, starting transfers between devices: 7.83 us -> 17.1 us  [spread(): lax.all_to_all(copies, axis, 0, 0, axis_index_groups=groups, tiled=True)]
  transfers between devices with their start and end apart: 22 -> 15, of which waited for: 10 -> 8; matrix products, arithmetic and copies ran while one was open for 4% -> 8% of each run, Pallas kernels for 10% -> 8%
where the time goes in v9:
time: 231 us
  waiting for transfers between devices  106 us (46%)
  blocking collectives  29.8 us (13%)
  starting transfers between devices  25.2 us (11%)
  Pallas kernels  24.9 us (11%)
  between operations  20.8 us (9%)
  local copies, waits for them, and re-layouts  15.9 us (7%)
  other arithmetic  8.18 us (4%)
    all_to_all x3, waiting for transfers between devices, spread(): lax.all_to_all(copies, axis, 0, 0, axis_index_groups=groups, tiled=True)  61 us
    all_to_all x1, blocking collectives, local(): lax.all_to_all(chip_sums, 'dp', 0, 0, axis_index_groups=groups, tiled=True)  29.8 us
    ppermute x9, waiting for transfers between devices, dp_move(): return lax.ppermute(value, 'dp', pairs)  25.3 us
    ppermute x1, waiting for transfers between devices, tensor_move(): return lax.ppermute(value, 'tensor', pairs)  19.2 us
    all_to_all x3, starting transfers between devices, spread(): lax.all_to_all(copies, axis, 0, 0, axis_index_groups=groups, tiled=True)  17.1 us
    pallas_call x2, Pallas kernels, project(): pl.pallas_call(project_kernel, grid=(1,), in_specs=[pl.BlockSpec(memory_s...  11.4 us
    broadcast_in_dim x3, local copies, waits for them, and re-layouts, spread(): copies = jnp.broadcast_to(block, (len(groups[0]), *block.shape))  8.27 us
    pallas_call x1, Pallas kernels, forward(): pl.pallas_call(forward_kernel, grid_spec=pltpu.PrefetchScalarGridSpec(num...  7.83 us
  transfers between devices with their start and end apart: 15, of which 8 were waited for; matrix products, arithmetic and copies ran while one was open for 8% of the time, Pallas kernels for 8%

profile of v9, /device:TPU:0, one launch (start us, length us, event | category | flops | bytes accessed | tf_op | source)
XLA Modules:
  0.0 231.1 jit_solution(7167875465913304073)
XLA Ops:
  7.2 2.1 fusion.4
  11.9 7.8 %all-to-all-start = ((bf16[8,512,128]{2,1,0:T(8,128)(2,1)}), bf16[8,512,128]{2,1,0:T(8,128)(2,1)S(1)}, u32[]{:S(2)}, u32[]{:S(2)}) async-start(bf16[8,512,128]{2,1,0:T(8,128)(2,1)} %broadcast_in_dim.37), calls=%async_computation | async-start | bytes 2097152 | tf_op jit(solution)/shard_map/all_to_all | solution.py:338
  21.6 4.1 %collective-permute-start.1 = (bf16[512,512]{1,0:T(8,128)(2,1)S(1)}, bf16[512,512]{1,0:T(8,128)(2,1)S(1)}, u32[]{:S(2)}, u32[]{:S(2)}) collective-permute-start(bf16[512,512]{1,0:T(8,128)(2,1)S(1)} %get-tuple-element.23), channel_id=1, source_target_pairs={{0,16},{8,24},{16,0},{24,8},{32,48},{40,56},{48,32},{56,40},{64,80... | collective-permute-start | bytes 1572872 | tf_op jit(solution)/shard_map/ppermute | solution.py:33
  25.8 19.2 %collective-permute-done.4 = bf16[512,512]{1,0:T(8,128)(2,1)} collective-permute-done((bf16[512,512]{1,0:T(8,128)(2,1)}, bf16[512,512]{1,0:T(8,128)(2,1)}, u32[]{:S(2)}, u32[]{:S(2)}) %collective-permute-start.4) | collective-permute-done | bytes 524320 | tf_op jit(solution)/shard_map/ppermute | solution.py:41
  45.0 2.1 pad_maximum_fusion.2
  47.2 11.0 %collective-permute-done.1 = bf16[512,512]{1,0:T(8,128)(2,1)S(1)} collective-permute-done((bf16[512,512]{1,0:T(8,128)(2,1)S(1)}, bf16[512,512]{1,0:T(8,128)(2,1)S(1)}, u32[]{:S(2)}, u32[]{:S(2)}) %collective-permute-start.1) | collective-permute-done | bytes 524320 | tf_op jit(solution)/shard_map/ppermute | solution.py:33
  59.0 9.9 %collective-permute-done.2 = bf16[512,512]{1,0:T(8,128)(2,1)S(1)} collective-permute-done((bf16[512,512]{1,0:T(8,128)(2,1)S(1)}, bf16[512,512]{1,0:T(8,128)(2,1)S(1)}, u32[]{:S(2)}, u32[]{:S(2)}) %collective-permute-start.2) | collective-permute-done | bytes 524320 | tf_op jit(solution)/shard_map/ppermute | solution.py:33
  68.9 2.9 %broadcast_in_dim.39 = bf16[4,512,512]{2,1,0:T(8,128)(2,1)} broadcast(bf16[512,512]{1,0:T(8,128)(2,1)} %copy-done.5), dimensions={1,2} | broadcast | bytes 2621440 | tf_op jit(solution)/shard_map/broadcast_in_dim | solution.py:337
  71.7 4.2 %all-to-all-start.2 = ((bf16[4,512,512]{2,1,0:T(8,128)(2,1)}), bf16[4,512,512]{2,1,0:T(8,128)(2,1)S(1)}, u32[]{:S(2)}, u32[]{:S(2)}) async-start(bf16[4,512,512]{2,1,0:T(8,128)(2,1)} %broadcast_in_dim.39), calls=%async_computation.2 | async-start | bytes 4194304 | tf_op jit(solution)/shard_map/all_to_all | solution.py:338
  76.7 37.2 %all-to-all-done.2.rest_1_ = bf16[4,512,512]{2,1,0:T(8,128)(2,1)S(1)} async-done(((bf16[4,512,512]{2,1,0:T(8,128)(2,1)}), bf16[4,512,512]{2,1,0:T(8,128)(2,1)S(1)}, u32[]{:S(2)}, u32[]{:S(2)}) %all-to-all-start.2) | async-done | bytes 2097184 | tf_op jit(solution)/shard_map/all_to_all | solution.py:338
  113.9 4.3 %broadcast_in_dim.38 = bf16[4,2,512,512]{3,2,1,0:T(8,128)(2,1)} broadcast(bf16[2,512,512]{2,1,0:T(8,128)(2,1)} %pad_maximum_fusion.2), dimensions={1,2,3} | broadcast | bytes 5242880 | tf_op jit(solution)/shard_map/broadcast_in_dim | solution.py:337
  118.2 5.0 %all-to-all-start.1 = ((bf16[4,2,512,512]{3,2,1,0:T(8,128)(2,1)}), bf16[4,2,512,512]{3,2,1,0:T(8,128)(2,1)}, u32[]{:S(2)}, u32[]{:S(2)}) async-start(bf16[4,2,512,512]{3,2,1,0:T(8,128)(2,1)} %broadcast_in_dim.38), calls=%async_computation.1 | async-start | bytes 8388608 | tf_op jit(solution)/shard_map/all_to_all | solution.py:338
  126.2 3.0 %pad_maximum_fusion.kv_ref.rest_7_.rest_8_ = bf16[8192,128]{1,0:T(8,128)(2,1)} fusion(bf16[4096,128]{1,0:T(8,128)(2,1)} %collective-permute-done.5, bf16[4096,128]{1,0:T(8,128)(2,1)} %bitcast.36), kind=kLoop, calls=%fused_computation | loop fusion | flops 4194304 | bytes 4194304 | tf_op jit(solution)/shard_map/concatenate | solution.py:360
  129.2 1.5 constant_dynamic-slice_fusion.4
  130.7 1.4 pad_maximum_fusion.1
  137.3 7.8 %forward.1 = (bf16[2816,2048]{1,0:T(8,128)(2,1)}, f32[128,2048]{1,0:T(8,128)S(1)}) custom-call(s32[36]{0:T(128)S(1)} %concatenate.15.info, s32[1,256]{1,0:T(1,128)S(1)} %iota_add_fusion.pos_ref, s32[1,256]{1,0:T(1,128)S(1)} %bitcast.32, bf16[256,1024]{1,0:T(8,128)(2,1)} %rest_6_.1, bf16[8192,128]{1,0:T(8,128)(2,1)} %pad_maximum_fusion.kv_ref.rest_7_.rest_8_), custom_call_target="tpu_custom_call" | custom-call | flops 10000000000 | bytes 10485760 | tf_op jit(solution)/shard_map/forward/pallas_call | solution.py:136
  145.2 23.8 %all-to-all-done.1 = bf16[4,2,512,512]{3,2,1,0:T(8,128)(2,1)} async-done(((bf16[4,2,512,512]{3,2,1,0:T(8,128)(2,1)}), bf16[4,2,512,512]{3,2,1,0:T(8,128)(2,1)}, u32[]{:S(2)}, u32[]{:S(2)}) %all-to-all-start.1) | async-done | bytes 4194336 | tf_op jit(solution)/shard_map/all_to_all | solution.py:338
  168.9 5.8 %project0.1 = (f32[256,512]{1,0:T(8,128)S(1)}, f32[256,512]{1,0:T(8,128)S(1)}) custom-call(s32[8]{0:T(128)S(1)} %stack.79.slots, bf16[8,512,512]{2,1,0:T(8,128)(2,1)} %bitcast.22.grad_ref, bf16[4,512,512]{2,1,0:T(8,128)(2,1)} %bitcast.37, bf16[4,512,512]{2,1,0:T(8,128)(2,1)} %copy-done), custom_call_target="tpu_custom_call" | custom-call | flops 2147483648 | bytes 10485760 | tf_op jit(solution)/shard_map/project0/pallas_call | solution.py:291
  176.0 5.6 %project1.1 = (f32[256,512]{1,0:T(8,128)S(1)}, f32[256,512]{1,0:T(8,128)S(1)}) custom-call(s32[8]{0:T(128)S(1)} %stack.87.slots, bf16[8,512,512]{2,1,0:T(8,128)(2,1)} %bitcast.22.grad_ref, bf16[4,512,512]{2,1,0:T(8,128)(2,1)} %bitcast.34, bf16[1,512,512]{2,1,0:T(8,128)(2,1)S(1)} %bitcast.31, bf16[3,512,512]{2,1,0:T(8,128)(2,1)} %copy-done.4), custom_call_target="tpu_custom_call" | custom-call | flops 2147483648 | bytes 10485760 | tf_op jit(solution)/shard_map/project1/pallas_call | solution.py:291
  182.2 1.5 collective-permute-done.8.rest_3_
  183.7 5.7 %backward.1 = (bf16[256,1024]{1,0:T(8,128)(2,1)}, f32[8,256,256]{2,1,0:T(8,128)S(1)}, bf16[8,256,256]{2,1,0:T(8,128)(2,1)S(1)}) custom-call(s32[36]{0:T(128)S(1)} %concatenate.15.info, f32[256,512]{1,0:T(8,128)S(1)} %get-tuple-element.25.rest_0_, f32[256,512]{1,0:T(8,128)S(1)} %collective-permute-done.6.rest_1_, f32[256,512]{1,0:T(8,128)S(1)} %get-tuple-element.29.rest_2_, ...), custom_call_target="tpu_custom_call" | custom-call | flops 8000000000 | bytes 10485760 | tf_op jit(solution)/shard_map/backward/pallas_call | solution.py:231
  189.4 1.6 collective-permute-start.9
  191.0 2.3 collective-permute-done.9
  193.6 29.8 %all_to_all.20 = bf16[8,256,256]{2,1,0:T(8,128)(2,1)S(1)} all-to-all(bf16[8,256,256]{2,1,0:T(8,128)(2,1)S(1)} %add_convert_fusion), channel_id=1, replica_groups={{0,16,32,48,64,80,96,112},{8,24,40,56,72,88,104,120},{1,17,33,49,65,81,..., dimensions={0} | all-to-all | bytes 2097152 | tf_op jit(solution)/shard_map/all_to_all | solution.py:389
  (59 shorter events, 10.7 us)
Async XLA Ops:
  7.2 2.2 copy-start.8
  7.2 2.2 copy-start.7
  7.2 2.4 %copy-start.6 = (bf16[256,1024]{1,0:T(8,128)(2,1)S(1)}, bf16[256,1024]{1,0:T(8,128)(2,1)}, u32[]{:S(2)}) copy-start(bf16[256,1024]{1,0:T(8,128)(2,1)} %param.9) | copy-start | bytes 1572868
  7.2 122.0 %all-gather.5.cloned.1.call-start = ((), (), s32[]{:S(2)}) async-start(), calls=%async_computation.4 | async-start | bytes 2621440 | tf_op jit(solution)/shard_map/all_gather | solution.py:334
  9.4 12.3 %copy-start.2 = (bf16[512,512]{1,0:T(8,128)(2,1)}, bf16[512,512]{1,0:T(8,128)(2,1)S(1)}, u32[]{:S(2)}) copy-start(bf16[512,512]{1,0:T(8,128)(2,1)S(1)} %get-tuple-element.23) | copy-start | bytes 1572868
  9.5 1.3 collective-permute-start
  9.6 10.1 %collective-permute-start.3 = (bf16[256,512]{1,0:T(8,128)(2,1)S(1)}, bf16[256,512]{1,0:T(8,128)(2,1)S(1)}, u32[]{:S(2)}, u32[]{:S(2)}) collective-permute-start(bf16[256,512]{1,0:T(8,128)(2,1)S(1)} %get-tuple-element.43), channel_id=1, source_target_pairs={{0,8},{8,0},{16,24},{24,16},{32,40},{40,32},{48,56},{56,48},{64,72... | collective-permute-start | bytes 786440 | tf_op jit(solution)/shard_map/ppermute | solution.py:33
  11.9 13.9 %copy-start.3 = (bf16[512,512]{1,0:T(8,128)(2,1)S(1)}, bf16[512,512]{1,0:T(8,128)(2,1)}, u32[]{:S(2)}) copy-start(bf16[512,512]{1,0:T(8,128)(2,1)} %get-tuple-element.39) | copy-start | bytes 1572868
  11.9 57.0 %all-to-all-start = ((bf16[8,512,128]{2,1,0:T(8,128)(2,1)}), bf16[8,512,128]{2,1,0:T(8,128)(2,1)S(1)}, u32[]{:S(2)}, u32[]{:S(2)}) async-start(bf16[8,512,128]{2,1,0:T(8,128)(2,1)} %broadcast_in_dim.37), calls=%async_computation | async-start | bytes 2097152 | tf_op jit(solution)/shard_map/all_to_all | solution.py:338
  20.6 24.4 %collective-permute-start.4 = (bf16[512,512]{1,0:T(8,128)(2,1)}, bf16[512,512]{1,0:T(8,128)(2,1)}, u32[]{:S(2)}, u32[]{:S(2)}) collective-permute-start(bf16[512,512]{1,0:T(8,128)(2,1)} %get-tuple-element.41), channel_id=1, source_target_pairs={{0,4},{1,5},{2,6},{3,7},{4,0},{5,1},{6,2},{7,3},{8,12},{9,13},{10,... | collective-permute-start | bytes 1572872 | tf_op jit(solution)/shard_map/ppermute | solution.py:41
  21.6 36.6 %collective-permute-start.1 = (bf16[512,512]{1,0:T(8,128)(2,1)S(1)}, bf16[512,512]{1,0:T(8,128)(2,1)S(1)}, u32[]{:S(2)}, u32[]{:S(2)}) collective-permute-start(bf16[512,512]{1,0:T(8,128)(2,1)S(1)} %get-tuple-element.23), channel_id=1, source_target_pairs={{0,16},{8,24},{16,0},{24,8},{32,48},{40,56},{48,32},{56,40},{64,80... | collective-permute-start | bytes 1572872 | tf_op jit(solution)/shard_map/ppermute | solution.py:33
  25.8 43.1 %collective-permute-start.2 = (bf16[512,512]{1,0:T(8,128)(2,1)S(1)}, bf16[512,512]{1,0:T(8,128)(2,1)S(1)}, u32[]{:S(2)}, u32[]{:S(2)}) collective-permute-start(bf16[512,512]{1,0:T(8,128)(2,1)S(1)} %copy-done.3), channel_id=1, source_target_pairs={{0,16},{8,24},{16,0},{24,8},{32,48},{40,56},{48,32},{56,40},{64,80... | collective-permute-start | bytes 1572872 | tf_op jit(solution)/shard_map/ppermute | solution.py:33
  68.9 2.9 %copy-start.1 = (bf16[8,512,128]{2,1,0:T(8,128)(2,1)}, bf16[8,512,128]{2,1,0:T(8,128)(2,1)S(1)}, u32[]{:S(2)}) copy-start(bf16[8,512,128]{2,1,0:T(8,128)(2,1)S(1)} %all-to-all-done) | copy-start | bytes 3145732
  71.7 42.2 %all-to-all-start.2 = ((bf16[4,512,512]{2,1,0:T(8,128)(2,1)}), bf16[4,512,512]{2,1,0:T(8,128)(2,1)S(1)}, u32[]{:S(2)}, u32[]{:S(2)}) async-start(bf16[4,512,512]{2,1,0:T(8,128)(2,1)} %broadcast_in_dim.39), calls=%async_computation.2 | async-start | bytes 4194304 | tf_op jit(solution)/shard_map/all_to_all | solution.py:338
  76.0 69.2 %all-gather.7.cloned.1.call-start = ((), (), s32[]{:S(2)}) async-start(), calls=%async_computation.5 | async-start | bytes 2621440 | tf_op jit(solution)/shard_map/all_gather | solution.py:334
  76.0 50.3 %collective-permute-start.5 = (bf16[4096,128]{1,0:T(8,128)(2,1)}, bf16[4096,128]{1,0:T(8,128)(2,1)}, u32[]{:S(2)}, u32[]{:S(2)}) collective-permute-start(bf16[4096,128]{1,0:T(8,128)(2,1)} %bitcast.35), channel_id=1, source_target_pairs={{0,8},{8,0},{16,24},{24,16},{32,40},{40,32},{48,56},{56,48},{64,72... | collective-permute-start | bytes 3145736 | tf_op jit(solution)/shard_map/ppermute | solution.py:33
  113.9 4.3 %copy-start = (bf16[4,512,512]{2,1,0:T(8,128)(2,1)}, bf16[4,512,512]{2,1,0:T(8,128)(2,1)S(1)}, u32[]{:S(2)}) copy-start(bf16[4,512,512]{2,1,0:T(8,128)(2,1)S(1)} %all-to-all-done.2.rest_1_) | copy-start | bytes 6291460
  118.2 7.8 %copy-start.9 = (s32[8]{0:T(128)S(1)}, s32[8]{0:T(128)}, u32[]{:S(2)}) copy-start(s32[8]{0:T(128)} %param.11) | copy-start | bytes 100
  118.2 50.7 %all-to-all-start.1 = ((bf16[4,2,512,512]{3,2,1,0:T(8,128)(2,1)}), bf16[4,2,512,512]{3,2,1,0:T(8,128)(2,1)}, u32[]{:S(2)}, u32[]{:S(2)}) async-start(bf16[4,2,512,512]{3,2,1,0:T(8,128)(2,1)} %broadcast_in_dim.38), calls=%async_computation.1 | async-start | bytes 8388608 | tf_op jit(solution)/shard_map/all_to_all | solution.py:338
  132.1 42.8 %collective-permute-start.7 = (bf16[3,512,512]{2,1,0:T(8,128)(2,1)}, bf16[3,512,512]{2,1,0:T(8,128)(2,1)S(1)}, u32[]{:S(2)}, u32[]{:S(2)}) collective-permute-start(bf16[3,512,512]{2,1,0:T(8,128)(2,1)} %pad_maximum_fusion.1), channel_id=1, source_target_pairs={{0,16},{8,24},{16,0},{24,8},{32,48},{40,56},{48,32},{56,40},{64,80... | collective-permute-start | bytes 4718600 | tf_op jit(solution)/shard_map/ppermute | solution.py:33
  174.7 7.4 %collective-permute-start.6 = (f32[256,512]{1,0:T(8,128)S(1)}, f32[256,512]{1,0:T(8,128)S(1)}, u32[]{:S(2)}, u32[]{:S(2)}) collective-permute-start(f32[256,512]{1,0:T(8,128)S(1)} %get-tuple-element.26), channel_id=1, source_target_pairs={{0,8},{8,0},{16,24},{24,16},{32,40},{40,32},{48,56},{56,48},{64,72... | collective-permute-start | bytes 1572872 | tf_op jit(solution)/shard_map/ppermute | solution.py:33
  174.8 1.1 copy-start.4
  181.6 2.1 collective-permute-start.8
  189.4 3.8 %collective-permute-start.9 = (bf16[8,256,256]{2,1,0:T(8,128)(2,1)S(1)}, bf16[8,256,256]{2,1,0:T(8,128)(2,1)S(1)}, u32[]{:S(2)}, u32[]{:S(2)}) collective-permute-start(bf16[8,256,256]{2,1,0:T(8,128)(2,1)S(1)} %get-tuple-element.34), channel_id=1, source_target_pairs={{0,8},{8,0},{16,24},{24,16},{32,40},{40,32},{48,56},{56,48},{64,72... | collective-permute-start | bytes 3145736 | tf_op jit(solution)/shard_map/ppermute | solution.py:33
  (1 other events, 0.8 us)
Sparse Core Ops, SparseCore 0:
  9.7 42.3 all-gather.4
  78.5 40.9 all-gather.6

commit v10 on v9

--- a/solution.py
+++ b/solution.py
@@ -12,13 +12,14 @@
 KEY_BLOCK = 256
 MOST = 2560
 CHUNKS = 2
+SPLIT = 5 * HEAD_WIDTH
 PAIR = 2
 MASKED = -1e30
 SCALE = 1.0 / math.sqrt(HEAD_WIDTH)
 LOG2E = 1.0 / math.log(2.0)
 BF16 = jnp.bfloat16
 F32 = jnp.float32
-VMEM_LIMIT = 24 * 2**20
+VMEM_LIMIT = 26 * 2**20
 
 FIRST, COUNT, CLEAR, CORE, TABLE = 0, 1, 2, 3, 4
 
@@ -128,20 +129,21 @@
     return (MOST + rows - 2) // KEY_BLOCK + 1
 
 
-def forward(info, query_pos, query_start, queries, kv):
+def forward(part, info, query_pos, query_start, queries, kv):
     rows, width = queries.shape
-    heads = width // HEAD_WIDTH
+    heads = width // HEAD_WIDTH // CHUNKS
+    steps = heads // PAIR
     live = most_blocks(rows) * KEY_BLOCK
     line = pl.BlockSpec((1, rows), lambda h, r: (0, 0))
     return pl.pallas_call(
         forward_kernel,
         grid_spec=pltpu.PrefetchScalarGridSpec(
             num_scalar_prefetch=1,
-            grid=(heads // PAIR,),
+            grid=(steps,),
             in_specs=[
                 line,
                 line,
-                pl.BlockSpec((rows, PAIR * HEAD_WIDTH), lambda h, r: (0, h)),
+                pl.BlockSpec((rows, PAIR * HEAD_WIDTH), lambda h, r: (0, part * steps + h)),
                 pl.BlockSpec(kv.shape, lambda h, r: (0, 0), pipeline_mode=pl.Buffered(1)),
             ],
             out_specs=[
@@ -159,17 +161,22 @@
         ],
         compiler_params=pltpu.CompilerParams(vmem_limit_bytes=VMEM_LIMIT),
         cost_estimate=pl.CostEstimate(flops=10**10, bytes_accessed=10 * 2**20, transcendentals=0),
-        name="forward",
+        name="forward%d" % part,
     )(info, query_pos, query_start, in_hbm(queries), in_hbm(kv))
 
 
 def backward_kernel(heads, info, *rest):
-    terms, rest = rest[: 2 * CHUNKS], rest[2 * CHUNKS :]
-    probs_ref, out_ref, q_ref, k_ref, v_ref, gq_ref, own_ref, other_ref, *scratch = rest
+    terms, all_probs, all_outs = rest[:4], rest[4:6], rest[6:8]
+    q_ref, k_ref, v_ref, gq_ref, own_ref, other_ref, *scratch = rest[8:]
     grad_t, stack, delta, total_q, dscores, other = scratch
     step = pl.program_id(0)
     count = info[COUNT]
     rows = q_ref.shape[0]
+    width = heads // 2 * rows
+
+    def columns(refs, h):
+        at = h * rows % width
+        return refs[h * rows // width][:, at : at + rows]
 
     @pl.when(step == 0)
     def _():
@@ -179,15 +186,18 @@
         for h in range(heads):
             cols = slice(h * rows, (h + 1) * rows)
             wide = slice(h * HEAD_WIDTH, (h + 1) * HEAD_WIDTH)
-            part, at = divmod(h * CHUNKS, heads)
-            here = slice(at // CHUNKS * HEAD_WIDTH, (at // CHUNKS + 1) * HEAD_WIDTH)
-            mine, got = terms[2 * part], terms[2 * part + 1]
+            at = h * HEAD_WIDTH
+            mine, got = terms[:2]
+            if at >= mine.shape[1]:
+                at -= mine.shape[1]
+                mine, got = terms[2:]
+            here = slice(at, at + HEAD_WIDTH)
             grad = (mine[:, here] + got[:, here]).astype(BF16)
             turned = grad.T
             grad_t[:, cols] = turned
             stack[cols, :HEAD_WIDTH] = q_ref[:, wide]
             stack[cols, HEAD_WIDTH:] = grad
-            delta[:, cols] = jnp.sum(turned.astype(F32) * out_ref[:, cols], axis=0, keepdims=True)
+            delta[:, cols] = jnp.sum(turned.astype(F32) * columns(all_outs, h), axis=0, keepdims=True)
 
     @pl.when(step < count)
     def _():
@@ -196,10 +206,11 @@
         for h in range(heads):
             cols = slice(h * rows, (h + 1) * rows)
             dprob = dot(v_ref[...], grad_t[:, cols])
-            dscores[:, cols] = (probs_ref[:, cols].astype(F32) * (dprob - delta[:, cols])).astype(BF16)
+            dscores[:, cols] = (columns(all_probs, h).astype(F32) * (dprob - delta[:, cols])).astype(BF16)
         total_q[...] += dot(keys_t, dscores[...])
         key_sum = dot(dscores[...], stack[:, :HEAD_WIDTH])
-        value_sum = dot(probs_ref[...], stack[:, HEAD_WIDTH:])
+        value_sum = dot(all_probs[0][...], stack[:width, HEAD_WIDTH:])
+        value_sum = value_sum + dot(all_probs[1][...], stack[width:, HEAD_WIDTH:])
 
         def add(ref):
             ref[block // 2, :, :HEAD_WIDTH] += key_sum * SCALE
@@ -234,9 +245,9 @@
             num_scalar_prefetch=1,
             grid=(most_blocks(rows),),
             in_specs=[once(term.shape) for term in terms]
+            + [pl.BlockSpec((KEY_BLOCK, p.shape[1]), lambda i, r: (near(i, r), 0)) for p in probs]
+            + [once(out.shape) for out in outs]
             + [
-                pl.BlockSpec((KEY_BLOCK, heads * rows), lambda i, r: (near(i, r), 0)),
-                once(outs.shape),
                 once(queries.shape),
                 pl.BlockSpec(
                     (KEY_BLOCK, HEAD_WIDTH), lambda i, r: (r[TABLE + r[FIRST] + near(i, r)], 0)
@@ -265,17 +276,19 @@
             flops=8 * 10**9, bytes_accessed=10 * 2**20, transcendentals=0
         ),
         name="backward",
-    )(info, *terms, in_hbm(probs), outs, in_hbm(queries), in_hbm(kv), in_hbm(kv))
-
-
-def project_kernel(slots, grad_ref, *rest):
-    *stacks, own_ref, other_ref = rest
+    )(info, *terms, *[in_hbm(p) for p in probs], *outs, in_hbm(queries), in_hbm(kv), in_hbm(kv))
+
+
+def project_kernel(chips, slots, *rest):
+    grads, (*stacks, own_ref, other_ref, grad) = rest[:chips], rest[chips:]
+    for i, ref in enumerate(grads):
+        grad[i] = ref[...]
     half = own_ref.shape[0]
     k = 0
     for ref in stacks:
         for j in range(ref.shape[0]):
             for out, row in ((own_ref, 0), (other_ref, half)):
-                term = dot_t(grad_ref[slots[k], row : row + half, :], ref[j])
+                term = dot_t(grad[slots[k], row : row + half, :], ref[j])
                 if k == 0:
                     out[...] = term
                 else:
@@ -284,17 +297,20 @@
 
 
 def project(part, slots, grads, stacks):
-    chips, tokens, depth = grads.shape
+    chips = len(grads)
+    tokens, depth = grads[0].shape
     features = stacks[0].shape[1]
     half = jax.ShapeDtypeStruct((tokens // 2, features), F32)
     out_spec = pl.BlockSpec((tokens // 2, features), lambda i: (0, 0))
     return pl.pallas_call(
-        project_kernel,
+        functools.partial(project_kernel, chips),
         grid=(1,),
         in_specs=[pl.BlockSpec(memory_space=pltpu.SMEM)]
-        + [pl.BlockSpec(ref.shape, lambda i: (0, 0, 0)) for ref in (grads, *stacks)],
+        + [pl.BlockSpec(ref.shape, lambda i: (0, 0)) for ref in grads]
+        + [pl.BlockSpec(ref.shape, lambda i: (0, 0, 0)) for ref in stacks],
         out_specs=[out_spec, out_spec],
         out_shape=[half, half],
+        scratch_shapes=[pltpu.VMEM((chips, tokens, depth), BF16)],
         compiler_params=pltpu.CompilerParams(vmem_limit_bytes=VMEM_LIMIT),
         cost_estimate=pl.CostEstimate(
             flops=2 * tokens * features * depth * chips,
@@ -302,7 +318,7 @@
             transcendentals=0,
         ),
         name="project%d" % part,
-    )(slots, in_hbm(grads), *[in_hbm(stack) if stack.shape[0] > 1 else stack for stack in stacks])
+    )(slots, *grads, *[in_hbm(stack) if stack.shape[0] > 1 else stack for stack in stacks])
 
 
 def local(queries, keys, values, grad_out, out_weight, lengths):
@@ -328,61 +344,65 @@
     info = jnp.concatenate([scalars, *table]).astype(jnp.int32)
     query_pos, query_start = query_pos[None, :], query_start[None, :]
 
-    groups_x = [[x_ * 4 + zc for x_ in range(4)] for zc in range(4)]
-
-    def gather_x(block):
-        return lax.all_gather(block, "dp", axis=0, axis_index_groups=groups_x)
-
     def spread(block, axis, groups):
         copies = jnp.broadcast_to(block, (len(groups[0]), *block.shape))
         return lax.all_to_all(copies, axis, 0, 0, axis_index_groups=groups, tiled=True)
 
-    size = out_weight.shape[0] // CHUNKS
-    own = [out_weight[:size], out_weight[size:]]
-    plane1 = gather_x(own[1])
-
     groups = [[2 * i + c for i in range(8)] for c in range(2)]
     kept = jnp.where(core == 0, keys, values)
     got = dp_move(jnp.where(core == 0, values, keys), 0, 0, 1)
-    plane0 = gather_x(after(own[0], got))
     ring = spread(jnp.concatenate([kept, got], axis=0), "dp", groups).reshape(-1, HEAD_WIDTH)
 
     depth = out_weight.shape[1]
     mine = lax.dynamic_slice_in_dim(grad_out, core * depth, depth, 1)
     other = lax.dynamic_slice_in_dim(grad_out, (1 - core) * depth, depth, 1)
     chip_grad = jnp.concatenate([mine, dp_move(other, 0, 0, 1)], axis=0)
-    grad_pair = jnp.stack([chip_grad, tensor_move(chip_grad, 1, 0)])
-    groups_y = [[z_ * 4 + y_ for y_ in range(4)] for z_ in range(2)]
-    all_grad = spread(grad_pair, "tensor", groups_y).reshape(8, 2 * rows, depth)
-
+    all_grad = [chip_grad] + [tensor_move(chip_grad, 0, step) for step in (-1, -2, 1)]
+
+    groups_x = [[x_ * 4 + zc for x_ in range(4)] for zc in range(4)]
+
+    def gather_x(block):
+        return lax.all_gather(block, "dp", axis=0, axis_index_groups=groups_x)
+
+    own = [out_weight[:SPLIT], out_weight[SPLIT:]]
+    ring, own, chip_grad = lax.optimization_barrier((ring, own, chip_grad))
+    plane1 = gather_x(own[1])
+    swapped = dp_move(ring, 0, 0, 1)
+    grad_pair = tensor_move(chip_grad, 1, 0)
     paired = [dp_move(block, 0, 1, 0) for block in own]
-    ring, paired, grad_pair = lax.optimization_barrier((ring, paired, grad_pair))
-    kv = jnp.concatenate([ring, dp_move(ring, 0, 0, 1)], axis=0)
-    other_plane = spread(paired[0], "dp", groups_x).reshape(4, size, depth)
+    swapped, own0 = lax.optimization_barrier((swapped, own[0]))
+    plane0 = gather_x(own0)
+    kv = jnp.concatenate([ring, swapped], axis=0)
+
+    first = forward(0, info, query_pos, query_start, queries, kv)
+    first, grad_pair, pair0 = lax.optimization_barrier((first, grad_pair, paired[0]))
+    all_grad += [grad_pair] + [tensor_move(grad_pair, 0, step) for step in (-1, -2, 1)]
+    other_plane = spread(pair0, "dp", groups_x).reshape(4, SPLIT, depth)
     rest = jnp.concatenate(
         [lax.dynamic_slice_in_dim(plane1, (x + i) % 4, 1, 0) for i in range(1, 4)], axis=0
     )
-    rest, kv = lax.optimization_barrier((rest, kv))
+    rest, later, _ = lax.optimization_barrier((rest, queries, first[1]))
     rest = dp_move(rest, 0, 1, 0)
-    probs, outs = forward(info, query_pos, query_start, queries, kv)
+    second = forward(1, info, query_pos, query_start, later, kv)
 
     t = lax.axis_index("tensor")
 
     def slot(x_, z_):
         source = 2 * (x_ % 4) + z_
-        return source % 4 * 2 + jnp.where(source // 4 == t // 4, 0, 1)
+        return (source - t) % 4 + jnp.where(source // 4 == t // 4, 0, 4)
 
     same = [slot(i, z) for i in range(4)]
     slots = [
         jnp.stack(same + [slot(i, 1 - z) for i in range(4)]).astype(jnp.int32),
         jnp.stack(same + [slot(x + i, 1 - z) for i in range(4)]).astype(jnp.int32),
     ]
-    slots[0] = after(slots[0], outs)
+    slots[0] = after(slots[0], second[1])
     stacks = [[plane0, other_plane], [plane1, paired[1][None], rest]]
     terms = []
     for part in range(CHUNKS):
         mine, other = project(part, slots[part], all_grad, stacks[part])
         terms += [mine, dp_move(other, 0, 0, 1)]
+    probs, outs = zip(first, second)
     grad_queries, own_sums, other_sums = backward(info, terms, probs, outs, queries, kv)
 
     chip_sums = (own_sums + dp_move(other_sums, 0, 0, 1).astype(F32)).astype(BF16)

time: 231 us -> 201 us (0.87); the launches traced: 231 us -> 198 us
  waiting for transfers between devices: 106 us -> 55.4 us
  starting transfers between devices: 25.2 us -> 41 us
  other arithmetic: 8.18 us -> 2.95 us
  Pallas kernels: 24.9 us -> 28.4 us
  blocking collectives: 29.8 us -> 32.3 us
    all_to_all x3 -> x2, waiting for transfers between devices: 61 us -> 14.6 us  [spread(): lax.all_to_all(copies, axis, 0, 0, axis_index_groups=groups, tiled=True)]
    ppermute x9, waiting for transfers between devices: 25.3 us -> 4.89 us  [dp_move(): return lax.ppermute(value, 'dp', pairs)]
    ppermute x1 -> x7, starting transfers between devices: 1.02 us -> 19.5 us  [tensor_move(): return lax.ppermute(value, 'tensor', pairs)]
    ppermute x1 -> x7, waiting for transfers between devices: 19.2 us -> 35.9 us  [tensor_move(): return lax.ppermute(value, 'tensor', pairs)]
    unnamed x20 -> x35, local copies, waits for them, and re-layouts: 1.95 us -> 8.89 us
    broadcast_in_dim x3 -> x2, local copies, waits for them, and re-layouts: 8.27 us -> 2.82 us  [spread(): copies = jnp.broadcast_to(block, (len(groups[0]), *block.shape))]
    all_to_all x3 -> x2, starting transfers between devices: 17.1 us -> 12.2 us  [spread(): lax.all_to_all(copies, axis, 0, 0, axis_index_groups=groups, tiled=True)]
    pallas_call x1 -> x2, Pallas kernels: 7.83 us -> 10.9 us  [forward(): pl.pallas_call(forward_kernel, grid_spec=pltpu.PrefetchScalarGridSpec(num...]
  transfers between devices with their start and end apart: 15 -> 20, of which waited for: 8 -> 7; matrix products, arithmetic and copies ran while one was open for 8% -> 5% of each run, Pallas kernels for 8% -> 11%
where the time goes in v10:
time: 201 us; the launch traced here: 198 us
  waiting for transfers between devices  55.4 us (28%)
  starting transfers between devices  41 us (20%)
  blocking collectives  32.3 us (16%)
  Pallas kernels  28.4 us (14%)
  between operations  20.2 us (10%)
  local copies, waits for them, and re-layouts  18.1 us (9%)
  other arithmetic  2.95 us (1%)
    ppermute x7, waiting for transfers between devices, tensor_move(): return lax.ppermute(value, 'tensor', pairs)  35.9 us
    all_to_all x1, blocking collectives, local(): lax.all_to_all(chip_sums, 'dp', 0, 0, axis_index_groups=groups, tiled=True)  32.3 us
    ppermute x7, starting transfers between devices, tensor_move(): return lax.ppermute(value, 'tensor', pairs)  19.5 us
    all_to_all x2, waiting for transfers between devices, spread(): lax.all_to_all(copies, axis, 0, 0, axis_index_groups=groups, tiled=True)  14.6 us
    all_to_all x2, starting transfers between devices, spread(): lax.all_to_all(copies, axis, 0, 0, axis_index_groups=groups, tiled=True)  12.2 us
    pallas_call x2, Pallas kernels, project(): pl.pallas_call(functools.partial(project_kernel, chips), grid=(1,), in_sp...  11.5 us
    pallas_call x2, Pallas kernels, forward(): pl.pallas_call(forward_kernel, grid_spec=pltpu.PrefetchScalarGridSpec(num...  10.9 us
    ppermute x9, starting transfers between devices, dp_move(): return lax.ppermute(value, 'dp', pairs)  9.11 us
  transfers between devices with their start and end apart: 20, of which 7 were waited for; matrix products, arithmetic and copies ran while one was open for 5% of the time, Pallas kernels for 11%

profile of v10, /device:TPU:0, one launch (start us, length us, event | category | flops | bytes accessed | tf_op | source)
XLA Modules:
  0.0 198.4 jit_solution(8364348980725341811)
XLA Ops:
  10.6 7.7 %all-to-all-start = ((bf16[8,512,128]{2,1,0:T(8,128)(2,1)}), bf16[8,512,128]{2,1,0:T(8,128)(2,1)S(1)}, u32[]{:S(2)}, u32[]{:S(2)}) async-start(bf16[8,512,128]{2,1,0:T(8,128)(2,1)} %broadcast_in_dim.34), calls=%async_computation | async-start | bytes 2097152 | tf_op jit(solution)/shard_map/all_to_all | solution.py:349
  20.2 14.6 %all-to-all-done = bf16[8,512,128]{2,1,0:T(8,128)(2,1)S(1)} async-done(((bf16[8,512,128]{2,1,0:T(8,128)(2,1)}), bf16[8,512,128]{2,1,0:T(8,128)(2,1)S(1)}, u32[]{:S(2)}, u32[]{:S(2)}) %all-to-all-start) | async-done | bytes 1048608 | tf_op jit(solution)/shard_map/all_to_all | solution.py:349
  42.5 2.0 collective-permute-start.4
  45.6 1.4 constant_dynamic-update-slice_fusion.kv_ref.rest_9_.rest_10_
  47.0 1.3 copy-done.15
  48.3 5.5 %forward0.1 = (bf16[2816,1024]{1,0:T(8,128)(2,1)}, f32[128,1024]{1,0:T(8,128)S(1)}) custom-call(s32[36]{0:T(128)S(1)} %concatenate.15.info, s32[1,256]{1,0:T(1,128)S(1)} %iota_add_fusion.pos_ref, s32[1,256]{1,0:T(1,128)S(1)} %bitcast.28, bf16[256,1024]{1,0:T(8,128)(2,1)} %rest_8_.1, bf16[8192,128]{1,0:T(8,128)(2,1)} %copy-done.15), custom_call_target="tpu_custom_call" | custom-call | flops 10000000000 | bytes 10485760 | tf_op jit(solution)/shard_map/forward0/pallas_call | solution.py:138
  53.8 18.0 %collective-permute-done.3.rest_4_ = bf16[512,512]{1,0:T(8,128)(2,1)S(1)} collective-permute-done((bf16[512,512]{1,0:T(8,128)(2,1)S(1)}, bf16[512,512]{1,0:T(8,128)(2,1)S(1)}, u32[]{:S(2)}, u32[]{:S(2)}) %collective-permute-start.3) | collective-permute-done | bytes 524320 | tf_op jit(solution)/shard_map/ppermute | solution.py:42
  71.9 1.7 broadcast_in_dim.35
  73.6 4.5 %all-to-all-start.1 = ((bf16[4,640,512]{2,1,0:T(8,128)(2,1)}), bf16[4,640,512]{2,1,0:T(8,128)(2,1)}, u32[]{:S(2)}, u32[]{:S(2)}) async-start(bf16[4,640,512]{2,1,0:T(8,128)(2,1)} %broadcast_in_dim.35), calls=%async_computation.1 | async-start | bytes 5242880 | tf_op jit(solution)/shard_map/all_to_all | solution.py:349
  78.1 1.6 collective-permute-start.7
  79.8 2.9 %collective-permute-start.6 = (bf16[512,512]{1,0:T(8,128)(2,1)S(1)}, bf16[512,512]{1,0:T(8,128)(2,1)S(1)}, u32[]{:S(2)}, u32[]{:S(2)}) collective-permute-start(bf16[512,512]{1,0:T(8,128)(2,1)S(1)} %pad_maximum_fusion.1.rest_0_), channel_id=1, source_target_pairs={{0,2},{1,3},{2,0},{3,1},{4,6},{5,7},{6,4},{7,5},{8,10},{9,11},{10,... | collective-permute-start | bytes 1572872 | tf_op jit(solution)/shard_map/ppermute | solution.py:42
  84.1 2.3 %collective-permute-start.12 = (bf16[384,512]{1,0:T(8,128)(2,1)}, bf16[384,512]{1,0:T(8,128)(2,1)S(1)}, u32[]{:S(2)}, u32[]{:S(2)}) collective-permute-start(bf16[384,512]{1,0:T(8,128)(2,1)} %slice.30), channel_id=1, source_target_pairs={{0,16},{8,24},{16,0},{24,8},{32,48},{40,56},{48,32},{56,40},{64,80... | collective-permute-start | bytes 1179656 | tf_op jit(solution)/shard_map/ppermute | solution.py:34
  89.6 5.9 %collective-permute-done.7.rest_3_ = bf16[512,512]{1,0:T(8,128)(2,1)S(1)} collective-permute-done((bf16[512,512]{1,0:T(8,128)(2,1)S(1)}, bf16[512,512]{1,0:T(8,128)(2,1)S(1)}, u32[]{:S(2)}, u32[]{:S(2)}) %collective-permute-start.7) | collective-permute-done | bytes 524320 | tf_op jit(solution)/shard_map/ppermute | solution.py:42
  95.5 11.9 %collective-permute-start.9 = (bf16[512,512]{1,0:T(8,128)(2,1)S(1)}, bf16[512,512]{1,0:T(8,128)(2,1)S(1)}, u32[]{:S(2)}, u32[]{:S(2)}) collective-permute-start(bf16[512,512]{1,0:T(8,128)(2,1)S(1)} %collective-permute-done.3.rest_4_), channel_id=1, source_target_pairs={{0,2},{1,3},{2,0},{3,1},{4,6},{5,7},{6,4},{7,5},{8,10},{9,11},{10,... | collective-permute-start | bytes 1572872 | tf_op jit(solution)/shard_map/ppermute | solution.py:42
  107.5 2.3 %collective-permute-start.13 = (bf16[3,384,512]{2,1,0:T(8,128)(2,1)}, bf16[3,384,512]{2,1,0:T(8,128)(2,1)}, u32[]{:S(2)}, u32[]{:S(2)}) collective-permute-start(bf16[3,384,512]{2,1,0:T(8,128)(2,1)} %pad_maximum_fusion), channel_id=1, source_target_pairs={{0,16},{8,24},{16,0},{24,8},{32,48},{40,56},{48,32},{56,40},{64,80... | collective-permute-start | bytes 3538952 | tf_op jit(solution)/shard_map/ppermute | solution.py:34
  109.8 5.4 %forward1.1 = (bf16[2816,1024]{1,0:T(8,128)(2,1)}, f32[128,1024]{1,0:T(8,128)S(1)}) custom-call(s32[36]{0:T(128)S(1)} %concatenate.15.info, s32[1,256]{1,0:T(1,128)S(1)} %iota_add_fusion.pos_ref, s32[1,256]{1,0:T(1,128)S(1)} %bitcast.29, bf16[256,1024]{1,0:T(8,128)(2,1)} %rest_8_.1, bf16[8192,128]{1,0:T(8,128)(2,1)} %copy-done.15), custom_call_target="tpu_custom_call" | custom-call | flops 10000000000 | bytes 10485760 | tf_op jit(solution)/shard_map/forward1/pallas_call | solution.py:138
  116.0 11.9 %collective-permute-done.9.rest_6_ = bf16[512,512]{1,0:T(8,128)(2,1)S(1)} collective-permute-done((bf16[512,512]{1,0:T(8,128)(2,1)S(1)}, bf16[512,512]{1,0:T(8,128)(2,1)S(1)}, u32[]{:S(2)}, u32[]{:S(2)}) %collective-permute-start.9) | collective-permute-done | bytes 524320 | tf_op jit(solution)/shard_map/ppermute | solution.py:42
  131.6 7.1 %project0.1 = (f32[256,640]{1,0:T(8,128)S(1)}, f32[256,640]{1,0:T(8,128)}) custom-call(s32[8]{0:T(128)S(1)} %stack.70.slots, bf16[512,512]{1,0:T(8,128)(2,1)S(1)} %pad_maximum_fusion.1.rest_0_, bf16[512,512]{1,0:T(8,128)(2,1)S(1)} %collective-permute-done.5.rest_1_, bf16[512,512]{1,0:T(8,128)(2,1)S(1)} %collective-permute-done.6.rest_2_, ...), custom_call_target="tpu_custom_call" | custom-call | flops 2684354560 | bytes 10485760 | tf_op jit(solution)/shard_map/project0/pallas_call | solution.py:305
  141.7 4.4 %project1.1 = (f32[256,384]{1,0:T(8,128)S(1)}, f32[256,384]{1,0:T(8,128)S(1)}) custom-call(s32[8]{0:T(128)S(1)} %stack.75.slots, bf16[512,512]{1,0:T(8,128)(2,1)S(1)} %pad_maximum_fusion.1.rest_0_, bf16[512,512]{1,0:T(8,128)(2,1)S(1)} %collective-permute-done.5.rest_1_, bf16[512,512]{1,0:T(8,128)(2,1)S(1)} %collective-permute-done.6.rest_2_, ...), custom_call_target="tpu_custom_call" | custom-call | flops 1610612736 | bytes 10485760 | tf_op jit(solution)/shard_map/project1/pallas_call | solution.py:305
  146.8 1.3 collective-permute-done.14.rest_3_
  148.1 6.0 %backward.1 = (bf16[256,1024]{1,0:T(8,128)(2,1)}, f32[8,256,256]{2,1,0:T(8,128)S(1)}, bf16[8,256,256]{2,1,0:T(8,128)(2,1)S(1)}) custom-call(s32[36]{0:T(128)S(1)} %concatenate.15.info, f32[256,640]{1,0:T(8,128)S(1)} %copy-done.7, f32[256,640]{1,0:T(8,128)} %collective-permute-done.11.rest_1_, f32[256,384]{1,0:T(8,128)S(1)} %get-tuple-element.44.rest_2_, ...), custom_call_target="tpu_custom_call" | custom-call | flops 8000000000 | bytes 10485760 | tf_op jit(solution)/shard_map/backward/pallas_call | solution.py:242
  154.1 1.7 collective-permute-start.15
  155.8 2.3 %collective-permute-done.15 = bf16[8,256,256]{2,1,0:T(8,128)(2,1)S(1)} collective-permute-done((bf16[8,256,256]{2,1,0:T(8,128)(2,1)S(1)}, bf16[8,256,256]{2,1,0:T(8,128)(2,1)S(1)}, u32[]{:S(2)}, u32[]{:S(2)}) %collective-permute-start.15) | collective-permute-done | bytes 1048608 | tf_op jit(solution)/shard_map/ppermute | solution.py:34
  158.4 32.3 %all_to_all.15 = bf16[8,256,256]{2,1,0:T(8,128)(2,1)S(1)} all-to-all(bf16[8,256,256]{2,1,0:T(8,128)(2,1)S(1)} %add_convert_fusion), channel_id=1, replica_groups={{0,16,32,48,64,80,96,112},{8,24,40,56,72,88,104,120},{1,17,33,49,65,81,..., dimensions={0} | all-to-all | bytes 2097152 | tf_op jit(solution)/shard_map/all_to_all | solution.py:409
  (84 shorter events, 22.0 us)
Async XLA Ops:
  7.2 11.2 %copy-start.14 = (bf16[256,1024]{1,0:T(8,128)(2,1)S(1)}, bf16[256,1024]{1,0:T(8,128)(2,1)}, u32[]{:S(2)}) copy-start(bf16[256,1024]{1,0:T(8,128)(2,1)} %param.9) | copy-start | bytes 1572868
  8.1 1.3 collective-permute-start
  10.6 24.2 %all-to-all-start = ((bf16[8,512,128]{2,1,0:T(8,128)(2,1)}), bf16[8,512,128]{2,1,0:T(8,128)(2,1)S(1)}, u32[]{:S(2)}, u32[]{:S(2)}) async-start(bf16[8,512,128]{2,1,0:T(8,128)(2,1)} %broadcast_in_dim.34), calls=%async_computation | async-start | bytes 2097152 | tf_op jit(solution)/shard_map/all_to_all | solution.py:349
  18.3 68.7 %all-gather.5.cloned.1.call-start = ((), (), s32[]{:S(2)}) async-start(), calls=%async_computation.3 | async-start | bytes 1966080 | tf_op jit(solution)/shard_map/all_gather | solution.py:365
  18.4 19.2 %copy-start.16 = (s32[8]{0:T(128)S(1)}, s32[8]{0:T(128)}, u32[]{:S(2)}) copy-start(s32[8]{0:T(128)} %param.11) | copy-start | bytes 100
  18.5 1.7 collective-permute-start.1
  20.2 22.4 %copy-start.12 = (bf16[640,512]{1,0:T(8,128)(2,1)S(1)}, bf16[640,512]{1,0:T(8,128)(2,1)}, u32[]{:S(2)}) copy-start(bf16[640,512]{1,0:T(8,128)(2,1)} %slice.29) | copy-start | bytes 1966084
  34.9 94.6 %all-gather.7.cloned.1.call-start = ((), (), s32[]{:S(2)}) async-start(), calls=%async_computation.4 | async-start | bytes 3276800 | tf_op jit(solution)/shard_map/all_gather | solution.py:365
  34.9 7.6 %collective-permute-start.2 = (bf16[4096,128]{1,0:T(8,128)(2,1)S(1)}, bf16[4096,128]{1,0:T(8,128)(2,1)}, u32[]{:S(2)}, u32[]{:S(2)}) collective-permute-start(bf16[4096,128]{1,0:T(8,128)(2,1)S(1)} %bitcast.32), channel_id=1, source_target_pairs={{0,8},{8,0},{16,24},{24,16},{32,40},{40,32},{48,56},{56,48},{64,72... | collective-permute-start | bytes 3145736 | tf_op jit(solution)/shard_map/ppermute | solution.py:34
  42.5 29.3 %collective-permute-start.4 = (bf16[640,512]{1,0:T(8,128)(2,1)S(1)}, bf16[640,512]{1,0:T(8,128)(2,1)S(1)}, u32[]{:S(2)}, u32[]{:S(2)}) collective-permute-start(bf16[640,512]{1,0:T(8,128)(2,1)S(1)} %copy-done.12), channel_id=1, source_target_pairs={{0,16},{8,24},{16,0},{24,8},{32,48},{40,56},{48,32},{56,40},{64,80... | collective-permute-start | bytes 1966088 | tf_op jit(solution)/shard_map/ppermute | solution.py:34
  44.5 27.4 %collective-permute-start.3 = (bf16[512,512]{1,0:T(8,128)(2,1)S(1)}, bf16[512,512]{1,0:T(8,128)(2,1)S(1)}, u32[]{:S(2)}, u32[]{:S(2)}) collective-permute-start(bf16[512,512]{1,0:T(8,128)(2,1)S(1)} %pad_maximum_fusion.1.rest_0_), channel_id=1, source_target_pairs={{0,4},{1,5},{2,6},{3,7},{4,0},{5,1},{6,2},{7,3},{8,12},{9,13},{10,... | collective-permute-start | bytes 1572872 | tf_op jit(solution)/shard_map/ppermute | solution.py:42
  53.8 19.7 %copy-start.8 = (f32[128,1024]{1,0:T(8,128)}, f32[128,1024]{1,0:T(8,128)S(1)}, u32[]{:S(2)}) copy-start(f32[128,1024]{1,0:T(8,128)S(1)} %get-tuple-element.34.rest_6_) | copy-start | bytes 1572868
  73.6 56.0 %all-to-all-start.1 = ((bf16[4,640,512]{2,1,0:T(8,128)(2,1)}), bf16[4,640,512]{2,1,0:T(8,128)(2,1)}, u32[]{:S(2)}, u32[]{:S(2)}) async-start(bf16[4,640,512]{2,1,0:T(8,128)(2,1)} %broadcast_in_dim.35), calls=%async_computation.1 | async-start | bytes 5242880 | tf_op jit(solution)/shard_map/all_to_all | solution.py:349
  78.1 17.4 %collective-permute-start.7 = (bf16[512,512]{1,0:T(8,128)(2,1)S(1)}, bf16[512,512]{1,0:T(8,128)(2,1)S(1)}, u32[]{:S(2)}, u32[]{:S(2)}) collective-permute-start(bf16[512,512]{1,0:T(8,128)(2,1)S(1)} %pad_maximum_fusion.1.rest_0_), channel_id=1, source_target_pairs={{0,1},{1,2},{2,3},{3,0},{4,5},{5,6},{6,7},{7,4},{8,9},{9,10},{10,1... | collective-permute-start | bytes 1572872 | tf_op jit(solution)/shard_map/ppermute | solution.py:42
  79.8 27.7 %collective-permute-start.6 = (bf16[512,512]{1,0:T(8,128)(2,1)S(1)}, bf16[512,512]{1,0:T(8,128)(2,1)S(1)}, u32[]{:S(2)}, u32[]{:S(2)}) collective-permute-start(bf16[512,512]{1,0:T(8,128)(2,1)S(1)} %pad_maximum_fusion.1.rest_0_), channel_id=1, source_target_pairs={{0,2},{1,3},{2,0},{3,1},{4,6},{5,7},{6,4},{7,5},{8,10},{9,11},{10,... | collective-permute-start | bytes 1572872 | tf_op jit(solution)/shard_map/ppermute | solution.py:42
  82.7 24.8 %collective-permute-start.5 = (bf16[512,512]{1,0:T(8,128)(2,1)S(1)}, bf16[512,512]{1,0:T(8,128)(2,1)S(1)}, u32[]{:S(2)}, u32[]{:S(2)}) collective-permute-start(bf16[512,512]{1,0:T(8,128)(2,1)S(1)} %pad_maximum_fusion.1.rest_0_), channel_id=1, source_target_pairs={{0,3},{1,0},{2,1},{3,2},{4,7},{5,4},{6,5},{7,6},{8,11},{9,8},{10,9... | collective-permute-start | bytes 1572872 | tf_op jit(solution)/shard_map/ppermute | solution.py:42
  84.1 55.5 %collective-permute-start.12 = (bf16[384,512]{1,0:T(8,128)(2,1)}, bf16[384,512]{1,0:T(8,128)(2,1)S(1)}, u32[]{:S(2)}, u32[]{:S(2)}) collective-permute-start(bf16[384,512]{1,0:T(8,128)(2,1)} %slice.30), channel_id=1, source_target_pairs={{0,16},{8,24},{16,0},{24,8},{32,48},{40,56},{48,32},{56,40},{64,80... | collective-permute-start | bytes 1179656 | tf_op jit(solution)/shard_map/ppermute | solution.py:34
  86.4 29.7 %collective-permute-start.10 = (bf16[512,512]{1,0:T(8,128)(2,1)S(1)}, bf16[512,512]{1,0:T(8,128)(2,1)S(1)}, u32[]{:S(2)}, u32[]{:S(2)}) collective-permute-start(bf16[512,512]{1,0:T(8,128)(2,1)S(1)} %collective-permute-done.3.rest_4_), channel_id=1, source_target_pairs={{0,1},{1,2},{2,3},{3,0},{4,5},{5,6},{6,7},{7,4},{8,9},{9,10},{10,1... | collective-permute-start | bytes 1572872 | tf_op jit(solution)/shard_map/ppermute | solution.py:42
  95.5 32.4 %collective-permute-start.9 = (bf16[512,512]{1,0:T(8,128)(2,1)S(1)}, bf16[512,512]{1,0:T(8,128)(2,1)S(1)}, u32[]{:S(2)}, u32[]{:S(2)}) collective-permute-start(bf16[512,512]{1,0:T(8,128)(2,1)S(1)} %collective-permute-done.3.rest_4_), channel_id=1, source_target_pairs={{0,2},{1,3},{2,0},{3,1},{4,6},{5,7},{6,4},{7,5},{8,10},{9,11},{10,... | collective-permute-start | bytes 1572872 | tf_op jit(solution)/shard_map/ppermute | solution.py:42
  107.4 21.3 %collective-permute-start.8 = (bf16[512,512]{1,0:T(8,128)(2,1)S(1)}, bf16[512,512]{1,0:T(8,128)(2,1)S(1)}, u32[]{:S(2)}, u32[]{:S(2)}) collective-permute-start(bf16[512,512]{1,0:T(8,128)(2,1)S(1)} %collective-permute-done.3.rest_4_), channel_id=1, source_target_pairs={{0,3},{1,0},{2,1},{3,2},{4,7},{5,4},{6,5},{7,6},{8,11},{9,8},{10,9... | collective-permute-start | bytes 1572872 | tf_op jit(solution)/shard_map/ppermute | solution.py:42
  107.5 32.2 %collective-permute-start.13 = (bf16[3,384,512]{2,1,0:T(8,128)(2,1)}, bf16[3,384,512]{2,1,0:T(8,128)(2,1)}, u32[]{:S(2)}, u32[]{:S(2)}) collective-permute-start(bf16[3,384,512]{2,1,0:T(8,128)(2,1)} %pad_maximum_fusion), channel_id=1, source_target_pairs={{0,16},{8,24},{16,0},{24,8},{32,48},{40,56},{48,32},{56,40},{64,80... | collective-permute-start | bytes 3538952 | tf_op jit(solution)/shard_map/ppermute | solution.py:34
  139.5 8.6 %collective-permute-start.11 = (f32[256,640]{1,0:T(8,128)}, f32[256,640]{1,0:T(8,128)}, u32[]{:S(2)}, u32[]{:S(2)}) collective-permute-start(f32[256,640]{1,0:T(8,128)} %get-tuple-element.42), channel_id=1, source_target_pairs={{0,8},{8,0},{16,24},{24,16},{32,40},{40,32},{48,56},{56,48},{64,72... | collective-permute-start | bytes 1966088 | tf_op jit(solution)/shard_map/ppermute | solution.py:34
  146.2 1.9 collective-permute-start.14
  154.1 4.0 %collective-permute-start.15 = (bf16[8,256,256]{2,1,0:T(8,128)(2,1)S(1)}, bf16[8,256,256]{2,1,0:T(8,128)(2,1)S(1)}, u32[]{:S(2)}, u32[]{:S(2)}) collective-permute-start(bf16[8,256,256]{2,1,0:T(8,128)(2,1)S(1)} %get-tuple-element.50), channel_id=1, source_target_pairs={{0,8},{8,0},{16,24},{24,16},{32,40},{40,32},{48,56},{56,48},{64,72... | collective-permute-start | bytes 3145736 | tf_op jit(solution)/shard_map/ppermute | solution.py:34
  (13 other events, 37.1 us)
Sparse Core Ops, SparseCore 0:
  35.0 25.0 all-gather.4
  61.7 49.6 all-gather.6

commit v11 on v10

--- a/solution.py
+++ b/solution.py
@@ -365,19 +365,18 @@
         return lax.all_gather(block, "dp", axis=0, axis_index_groups=groups_x)
 
     own = [out_weight[:SPLIT], out_weight[SPLIT:]]
-    ring, own, chip_grad = lax.optimization_barrier((ring, own, chip_grad))
     plane1 = gather_x(own[1])
+    grad_pair = tensor_move(chip_grad, 1, 0)
+    ring, own, all_grad, grad_pair = lax.optimization_barrier((ring, own, all_grad, grad_pair))
     swapped = dp_move(ring, 0, 0, 1)
-    grad_pair = tensor_move(chip_grad, 1, 0)
+    all_grad += [grad_pair] + [tensor_move(grad_pair, 0, step) for step in (-1, -2, 1)]
     paired = [dp_move(block, 0, 1, 0) for block in own]
-    swapped, own0 = lax.optimization_barrier((swapped, own[0]))
-    plane0 = gather_x(own0)
+    plane0 = gather_x(own[0])
     kv = jnp.concatenate([ring, swapped], axis=0)
 
     first = forward(0, info, query_pos, query_start, queries, kv)
-    first, grad_pair, pair0 = lax.optimization_barrier((first, grad_pair, paired[0]))
-    all_grad += [grad_pair] + [tensor_move(grad_pair, 0, step) for step in (-1, -2, 1)]
-    other_plane = spread(pair0, "dp", groups_x).reshape(4, SPLIT, depth)
+    first, all_grad, paired = lax.optimization_barrier((first, all_grad, paired))
+    other_plane = spread(paired[0], "dp", groups_x).reshape(4, SPLIT, depth)
     rest = jnp.concatenate(
         [lax.dynamic_slice_in_dim(plane1, (x + i) % 4, 1, 0) for i in range(1, 4)], axis=0
     )

time: 201 us -> 196 us (0.975)
  starting transfers between devices: 41 us -> 34.4 us
  local copies, waits for them, and re-layouts: 18.1 us -> 22.3 us
    ppermute x7, waiting for transfers between devices: 35.9 us -> 16.9 us  [tensor_move(): return lax.ppermute(value, 'tensor', pairs)]
    ppermute x9, waiting for transfers between devices: 4.89 us -> 19.2 us  [dp_move(): return lax.ppermute(value, 'dp', pairs)]
    ppermute x7, starting transfers between devices: 19.5 us -> 12.2 us  [tensor_move(): return lax.ppermute(value, 'tensor', pairs)]
    all_to_all x2, waiting for transfers between devices: 14.6 us -> 19 us  [spread(): lax.all_to_all(copies, axis, 0, 0, axis_index_groups=groups, tiled=True)]
    slice x2, local copies, waits for them, and re-layouts: 1.63 us -> 3.75 us  [local(): own = [out_weight[:SPLIT], out_weight[SPLIT:]]]
    unnamed x35 -> x31, local copies, waits for them, and re-layouts: 8.89 us -> 10.9 us
  transfers between devices with their start and end apart: 20 -> 20, of which waited for: 7 -> 8; matrix products, arithmetic and copies ran while one was open for 5% -> 7% of each run, Pallas kernels for 11% -> 12%
where the time goes in v11:
time: 196 us; the launch traced here: 194 us
  waiting for transfers between devices  55.1 us (28%)
  starting transfers between devices  34.4 us (18%)
  blocking collectives  30.8 us (16%)
  Pallas kernels  28.4 us (14%)
  local copies, waits for them, and re-layouts  22.3 us (11%)
  between operations  20.5 us (10%)
  other arithmetic  2.95 us (2%)
    all_to_all x1, blocking collectives, local(): lax.all_to_all(chip_sums, 'dp', 0, 0, axis_index_groups=groups, tiled=True)  30.8 us
    ppermute x9, waiting for transfers between devices, dp_move(): return lax.ppermute(value, 'dp', pairs)  19.2 us
    all_to_all x2, waiting for transfers between devices, spread(): lax.all_to_all(copies, axis, 0, 0, axis_index_groups=groups, tiled=True)  19 us
    ppermute x7, waiting for transfers between devices, tensor_move(): return lax.ppermute(value, 'tensor', pairs)  16.9 us
    all_to_all x2, starting transfers between devices, spread(): lax.all_to_all(copies, axis, 0, 0, axis_index_groups=groups, tiled=True)  12.2 us
    ppermute x7, starting transfers between devices, tensor_move(): return lax.ppermute(value, 'tensor', pairs)  12.2 us
    pallas_call x2, Pallas kernels, project(): pl.pallas_call(functools.partial(project_kernel, chips), grid=(1,), in_sp...  11.5 us
    pallas_call x2, Pallas kernels, forward(): pl.pallas_call(forward_kernel, grid_spec=pltpu.PrefetchScalarGridSpec(num...  10.9 us
  transfers between devices with their start and end apart: 20, of which 8 were waited for; matrix products, arithmetic and copies ran while one was open for 7% of the time, Pallas kernels for 12%

profile of v11, /device:TPU:0, one launch (start us, length us, event | category | flops | bytes accessed | tf_op | source)
XLA Modules:
  0.0 194.5 jit_solution(5396624055715814774)
XLA Ops:
  7.2 1.8 slice.29
  12.4 7.7 %all-to-all-start = ((bf16[8,512,128]{2,1,0:T(8,128)(2,1)}), bf16[8,512,128]{2,1,0:T(8,128)(2,1)}, u32[]{:S(2)}, u32[]{:S(2)}) async-start(bf16[8,512,128]{2,1,0:T(8,128)(2,1)} %broadcast_in_dim.34), calls=%async_computation | async-start | bytes 2097152 | tf_op jit(solution)/shard_map/all_to_all | solution.py:349
  20.4 1.5 collective-permute-done.1
  23.0 1.6 collective-permute-start.4
  24.6 2.9 %collective-permute-start.3 = (bf16[512,512]{1,0:T(8,128)(2,1)S(1)}, bf16[512,512]{1,0:T(8,128)(2,1)S(1)}, u32[]{:S(2)}, u32[]{:S(2)}) collective-permute-start(bf16[512,512]{1,0:T(8,128)(2,1)S(1)} %pad_maximum_fusion.1.rest_0_), channel_id=1, source_target_pairs={{0,2},{1,3},{2,0},{3,1},{4,6},{5,7},{6,4},{7,5},{8,10},{9,11},{10,... | collective-permute-start | bytes 1572872 | tf_op jit(solution)/shard_map/ppermute | solution.py:42
  31.4 2.0 %slice.30 = bf16[640,512]{1,0:T(8,128)(2,1)} slice(bf16[1024,512]{1,0:T(8,128)(2,1)} %param.10), slice={[0:640], [0:512]} | slice | bytes 1310720 | tf_op jit(solution)/shard_map/slice | solution.py:367
  33.5 11.1 %collective-permute-done.5.rest_4_ = bf16[512,512]{1,0:T(8,128)(2,1)S(1)} collective-permute-done((bf16[512,512]{1,0:T(8,128)(2,1)S(1)}, bf16[512,512]{1,0:T(8,128)(2,1)S(1)}, u32[]{:S(2)}, u32[]{:S(2)}) %collective-permute-start.5) | collective-permute-done | bytes 524320 | tf_op jit(solution)/shard_map/ppermute | solution.py:42
  44.6 5.8 %collective-permute-done.3.rest_2_ = bf16[512,512]{1,0:T(8,128)(2,1)S(1)} collective-permute-done((bf16[512,512]{1,0:T(8,128)(2,1)S(1)}, bf16[512,512]{1,0:T(8,128)(2,1)S(1)}, u32[]{:S(2)}, u32[]{:S(2)}) %collective-permute-start.3) | collective-permute-done | bytes 524320 | tf_op jit(solution)/shard_map/ppermute | solution.py:42
  56.4 2.4 %collective-permute-start.8 = (bf16[512,512]{1,0:T(8,128)(2,1)S(1)}, bf16[512,512]{1,0:T(8,128)(2,1)S(1)}, u32[]{:S(2)}, u32[]{:S(2)}) collective-permute-start(bf16[512,512]{1,0:T(8,128)(2,1)S(1)} %collective-permute-done.5.rest_4_), channel_id=1, source_target_pairs={{0,2},{1,3},{2,0},{3,1},{4,6},{5,7},{6,4},{7,5},{8,10},{9,11},{10,... | collective-permute-start | bytes 1572872 | tf_op jit(solution)/shard_map/ppermute | solution.py:42
  58.8 1.7 collective-permute-start.7
  60.4 4.1 %collective-permute-start.10 = (bf16[640,512]{1,0:T(8,128)(2,1)}, bf16[640,512]{1,0:T(8,128)(2,1)S(1)}, u32[]{:S(2)}, u32[]{:S(2)}) collective-permute-start(bf16[640,512]{1,0:T(8,128)(2,1)} %slice.30), channel_id=1, source_target_pairs={{0,16},{8,24},{16,0},{24,8},{32,48},{40,56},{48,32},{56,40},{64,80... | collective-permute-start | bytes 1966088 | tf_op jit(solution)/shard_map/ppermute | solution.py:34
  68.7 5.5 %forward0.1 = (bf16[2816,1024]{1,0:T(8,128)(2,1)}, f32[128,1024]{1,0:T(8,128)S(1)}) custom-call(s32[36]{0:T(128)S(1)} %concatenate.15.info, s32[1,256]{1,0:T(1,128)S(1)} %iota_add_fusion.pos_ref, s32[1,256]{1,0:T(1,128)S(1)} %bitcast.28, bf16[256,1024]{1,0:T(8,128)(2,1)} %rest_8_.1, bf16[8192,128]{1,0:T(8,128)(2,1)} %copy-done.13), custom_call_target="tpu_custom_call" | custom-call | flops 10000000000 | bytes 10485760 | tf_op jit(solution)/shard_map/forward0/pallas_call | solution.py:138
  74.9 12.8 %collective-permute-done.11 = bf16[384,512]{1,0:T(8,128)(2,1)S(1)} collective-permute-done((bf16[384,512]{1,0:T(8,128)(2,1)}, bf16[384,512]{1,0:T(8,128)(2,1)S(1)}, u32[]{:S(2)}, u32[]{:S(2)}) %collective-permute-start.11) | collective-permute-done | bytes 393248 | tf_op jit(solution)/shard_map/ppermute | solution.py:34
  89.3 1.7 broadcast_in_dim.35
  91.0 4.5 %all-to-all-start.1 = ((bf16[4,640,512]{2,1,0:T(8,128)(2,1)}), bf16[4,640,512]{2,1,0:T(8,128)(2,1)}, u32[]{:S(2)}, u32[]{:S(2)}) async-start(bf16[4,640,512]{2,1,0:T(8,128)(2,1)} %broadcast_in_dim.35), calls=%async_computation.1 | async-start | bytes 5242880 | tf_op jit(solution)/shard_map/all_to_all | solution.py:349
  98.6 3.2 %collective-permute-start.13 = (bf16[3,384,512]{2,1,0:T(8,128)(2,1)}, bf16[3,384,512]{2,1,0:T(8,128)(2,1)}, u32[]{:S(2)}, u32[]{:S(2)}) collective-permute-start(bf16[3,384,512]{2,1,0:T(8,128)(2,1)} %pad_maximum_fusion), channel_id=1, source_target_pairs={{0,16},{8,24},{16,0},{24,8},{32,48},{40,56},{48,32},{56,40},{64,80... | collective-permute-start | bytes 3538952 | tf_op jit(solution)/shard_map/ppermute | solution.py:34
  101.8 5.5 %forward1.1 = (bf16[2816,1024]{1,0:T(8,128)(2,1)}, f32[128,1024]{1,0:T(8,128)S(1)}) custom-call(s32[36]{0:T(128)S(1)} %concatenate.15.info, s32[1,256]{1,0:T(1,128)S(1)} %iota_add_fusion.pos_ref, s32[1,256]{1,0:T(1,128)S(1)} %bitcast.29, bf16[256,1024]{1,0:T(8,128)(2,1)} %rest_8_.1, bf16[8192,128]{1,0:T(8,128)(2,1)} %copy-done.13), custom_call_target="tpu_custom_call" | custom-call | flops 10000000000 | bytes 10485760 | tf_op jit(solution)/shard_map/forward1/pallas_call | solution.py:138
  108.0 19.0 %all-to-all-done.1.rest_9_ = bf16[4,640,512]{2,1,0:T(8,128)(2,1)} async-done(((bf16[4,640,512]{2,1,0:T(8,128)(2,1)}), bf16[4,640,512]{2,1,0:T(8,128)(2,1)}, u32[]{:S(2)}, u32[]{:S(2)}) %all-to-all-start.1) | async-done | bytes 2621472 | tf_op jit(solution)/shard_map/all_to_all | solution.py:349
  129.2 7.0 %project0.1 = (f32[256,640]{1,0:T(8,128)S(1)}, f32[256,640]{1,0:T(8,128)}) custom-call(s32[8]{0:T(128)S(1)} %stack.70.slots, bf16[512,512]{1,0:T(8,128)(2,1)S(1)} %pad_maximum_fusion.1.rest_0_, bf16[512,512]{1,0:T(8,128)(2,1)S(1)} %collective-permute-done.2.rest_1_, bf16[512,512]{1,0:T(8,128)(2,1)S(1)} %collective-permute-done.3.rest_2_, ...), custom_call_target="tpu_custom_call" | custom-call | flops 2684354560 | bytes 10485760 | tf_op jit(solution)/shard_map/project0/pallas_call | solution.py:305
  139.3 4.4 %project1.1 = (f32[256,384]{1,0:T(8,128)S(1)}, f32[256,384]{1,0:T(8,128)S(1)}) custom-call(s32[8]{0:T(128)S(1)} %stack.75.slots, bf16[512,512]{1,0:T(8,128)(2,1)S(1)} %pad_maximum_fusion.1.rest_0_, bf16[512,512]{1,0:T(8,128)(2,1)S(1)} %collective-permute-done.2.rest_1_, bf16[512,512]{1,0:T(8,128)(2,1)S(1)} %collective-permute-done.3.rest_2_, ...), custom_call_target="tpu_custom_call" | custom-call | flops 1610612736 | bytes 10485760 | tf_op jit(solution)/shard_map/project1/pallas_call | solution.py:305
  145.7 6.0 %backward.1 = (bf16[256,1024]{1,0:T(8,128)(2,1)}, f32[8,256,256]{2,1,0:T(8,128)S(1)}, bf16[8,256,256]{2,1,0:T(8,128)(2,1)S(1)}) custom-call(s32[36]{0:T(128)S(1)} %concatenate.15.info, f32[256,640]{1,0:T(8,128)S(1)} %copy-done.7, f32[256,640]{1,0:T(8,128)} %collective-permute-done.12.rest_1_, f32[256,384]{1,0:T(8,128)S(1)} %get-tuple-element.64.rest_2_, ...), custom_call_target="tpu_custom_call" | custom-call | flops 8000000000 | bytes 10485760 | tf_op jit(solution)/shard_map/backward/pallas_call | solution.py:242
  151.7 1.7 collective-permute-start.15
  153.4 2.3 %collective-permute-done.15 = bf16[8,256,256]{2,1,0:T(8,128)(2,1)S(1)} collective-permute-done((bf16[8,256,256]{2,1,0:T(8,128)(2,1)S(1)}, bf16[8,256,256]{2,1,0:T(8,128)(2,1)S(1)}, u32[]{:S(2)}, u32[]{:S(2)}) %collective-permute-start.15) | collective-permute-done | bytes 1048608 | tf_op jit(solution)/shard_map/ppermute | solution.py:34
  156.0 30.8 %all_to_all.15 = bf16[8,256,256]{2,1,0:T(8,128)(2,1)S(1)} all-to-all(bf16[8,256,256]{2,1,0:T(8,128)(2,1)S(1)} %add_convert_fusion), channel_id=1, replica_groups={{0,16,32,48,64,80,96,112},{8,24,40,56,72,88,104,120},{1,17,33,49,65,81,..., dimensions={0} | all-to-all | bytes 2097152 | tf_op jit(solution)/shard_map/all_to_all | solution.py:408
  (80 shorter events, 27.0 us)
Async XLA Ops:
  7.2 88.8 %all-gather.5.cloned.1.call-start = ((), (), s32[]{:S(2)}) async-start(), calls=%async_computation.3 | async-start | bytes 1966080 | tf_op jit(solution)/shard_map/all_gather | solution.py:365
  9.0 11.2 %copy-start.12 = (bf16[256,1024]{1,0:T(8,128)(2,1)S(1)}, bf16[256,1024]{1,0:T(8,128)(2,1)}, u32[]{:S(2)}) copy-start(bf16[256,1024]{1,0:T(8,128)(2,1)} %param.9) | copy-start | bytes 1572868
  10.0 1.3 collective-permute-start
  12.4 37.9 %all-to-all-start = ((bf16[8,512,128]{2,1,0:T(8,128)(2,1)}), bf16[8,512,128]{2,1,0:T(8,128)(2,1)}, u32[]{:S(2)}, u32[]{:S(2)}) async-start(bf16[8,512,128]{2,1,0:T(8,128)(2,1)} %broadcast_in_dim.34), calls=%async_computation | async-start | bytes 2097152 | tf_op jit(solution)/shard_map/all_to_all | solution.py:349
  20.1 13.2 %copy-start.14 = (s32[8]{0:T(128)S(1)}, s32[8]{0:T(128)}, u32[]{:S(2)}) copy-start(s32[8]{0:T(128)} %param.11) | copy-start | bytes 100
  20.1 106.9 %all-gather.7.cloned.1.call-start = ((), (), s32[]{:S(2)}) async-start(), calls=%async_computation.4 | async-start | bytes 3276800 | tf_op jit(solution)/shard_map/all_gather | solution.py:365
  20.3 1.6 collective-permute-start.1
  21.9 22.7 %collective-permute-start.5 = (bf16[512,512]{1,0:T(8,128)(2,1)S(1)}, bf16[512,512]{1,0:T(8,128)(2,1)S(1)}, u32[]{:S(2)}, u32[]{:S(2)}) collective-permute-start(bf16[512,512]{1,0:T(8,128)(2,1)S(1)} %pad_maximum_fusion.1.rest_0_), channel_id=1, source_target_pairs={{0,4},{1,5},{2,6},{3,7},{4,0},{5,1},{6,2},{7,3},{8,12},{9,13},{10,... | collective-permute-start | bytes 1572872 | tf_op jit(solution)/shard_map/ppermute | solution.py:42
  23.0 21.6 %collective-permute-start.4 = (bf16[512,512]{1,0:T(8,128)(2,1)S(1)}, bf16[512,512]{1,0:T(8,128)(2,1)S(1)}, u32[]{:S(2)}, u32[]{:S(2)}) collective-permute-start(bf16[512,512]{1,0:T(8,128)(2,1)S(1)} %pad_maximum_fusion.1.rest_0_), channel_id=1, source_target_pairs={{0,1},{1,2},{2,3},{3,0},{4,5},{5,6},{6,7},{7,4},{8,9},{9,10},{10,1... | collective-permute-start | bytes 1572872 | tf_op jit(solution)/shard_map/ppermute | solution.py:42
  24.6 25.8 %collective-permute-start.3 = (bf16[512,512]{1,0:T(8,128)(2,1)S(1)}, bf16[512,512]{1,0:T(8,128)(2,1)S(1)}, u32[]{:S(2)}, u32[]{:S(2)}) collective-permute-start(bf16[512,512]{1,0:T(8,128)(2,1)S(1)} %pad_maximum_fusion.1.rest_0_), channel_id=1, source_target_pairs={{0,2},{1,3},{2,0},{3,1},{4,6},{5,7},{6,4},{7,5},{8,10},{9,11},{10,... | collective-permute-start | bytes 1572872 | tf_op jit(solution)/shard_map/ppermute | solution.py:42
  27.5 22.9 %collective-permute-start.2 = (bf16[512,512]{1,0:T(8,128)(2,1)S(1)}, bf16[512,512]{1,0:T(8,128)(2,1)S(1)}, u32[]{:S(2)}, u32[]{:S(2)}) collective-permute-start(bf16[512,512]{1,0:T(8,128)(2,1)S(1)} %pad_maximum_fusion.1.rest_0_), channel_id=1, source_target_pairs={{0,3},{1,0},{2,1},{3,2},{4,7},{5,4},{6,5},{7,6},{8,11},{9,8},{10,9... | collective-permute-start | bytes 1572872 | tf_op jit(solution)/shard_map/ppermute | solution.py:42
  50.4 15.4 %collective-permute-start.6 = (bf16[4096,128]{1,0:T(8,128)(2,1)}, bf16[4096,128]{1,0:T(8,128)(2,1)}, u32[]{:S(2)}, u32[]{:S(2)}) collective-permute-start(bf16[4096,128]{1,0:T(8,128)(2,1)} %bitcast.19), channel_id=1, source_target_pairs={{0,8},{8,0},{16,24},{24,16},{32,40},{40,32},{48,56},{56,48},{64,72... | collective-permute-start | bytes 3145736 | tf_op jit(solution)/shard_map/ppermute | solution.py:34
  55.2 32.5 %collective-permute-start.9 = (bf16[512,512]{1,0:T(8,128)(2,1)S(1)}, bf16[512,512]{1,0:T(8,128)(2,1)S(1)}, u32[]{:S(2)}, u32[]{:S(2)}) collective-permute-start(bf16[512,512]{1,0:T(8,128)(2,1)S(1)} %collective-permute-done.5.rest_4_), channel_id=1, source_target_pairs={{0,1},{1,2},{2,3},{3,0},{4,5},{5,6},{6,7},{7,4},{8,9},{9,10},{10,1... | collective-permute-start | bytes 1572872 | tf_op jit(solution)/shard_map/ppermute | solution.py:42
  56.4 31.3 %collective-permute-start.8 = (bf16[512,512]{1,0:T(8,128)(2,1)S(1)}, bf16[512,512]{1,0:T(8,128)(2,1)S(1)}, u32[]{:S(2)}, u32[]{:S(2)}) collective-permute-start(bf16[512,512]{1,0:T(8,128)(2,1)S(1)} %collective-permute-done.5.rest_4_), channel_id=1, source_target_pairs={{0,2},{1,3},{2,0},{3,1},{4,6},{5,7},{6,4},{7,5},{8,10},{9,11},{10,... | collective-permute-start | bytes 1572872 | tf_op jit(solution)/shard_map/ppermute | solution.py:42
  58.8 29.8 %collective-permute-start.7 = (bf16[512,512]{1,0:T(8,128)(2,1)S(1)}, bf16[512,512]{1,0:T(8,128)(2,1)S(1)}, u32[]{:S(2)}, u32[]{:S(2)}) collective-permute-start(bf16[512,512]{1,0:T(8,128)(2,1)S(1)} %collective-permute-done.5.rest_4_), channel_id=1, source_target_pairs={{0,3},{1,0},{2,1},{3,2},{4,7},{5,4},{6,5},{7,6},{8,11},{9,8},{10,9... | collective-permute-start | bytes 1572872 | tf_op jit(solution)/shard_map/ppermute | solution.py:42
  60.4 28.9 %collective-permute-start.10 = (bf16[640,512]{1,0:T(8,128)(2,1)}, bf16[640,512]{1,0:T(8,128)(2,1)S(1)}, u32[]{:S(2)}, u32[]{:S(2)}) collective-permute-start(bf16[640,512]{1,0:T(8,128)(2,1)} %slice.30), channel_id=1, source_target_pairs={{0,16},{8,24},{16,0},{24,8},{32,48},{40,56},{48,32},{56,40},{64,80... | collective-permute-start | bytes 1966088 | tf_op jit(solution)/shard_map/ppermute | solution.py:34
  65.8 21.9 %collective-permute-start.11 = (bf16[384,512]{1,0:T(8,128)(2,1)}, bf16[384,512]{1,0:T(8,128)(2,1)S(1)}, u32[]{:S(2)}, u32[]{:S(2)}) collective-permute-start(bf16[384,512]{1,0:T(8,128)(2,1)} %slice.29), channel_id=1, source_target_pairs={{0,16},{8,24},{16,0},{24,8},{32,48},{40,56},{48,32},{56,40},{64,80... | collective-permute-start | bytes 1179656 | tf_op jit(solution)/shard_map/ppermute | solution.py:34
  91.0 36.1 %all-to-all-start.1 = ((bf16[4,640,512]{2,1,0:T(8,128)(2,1)}), bf16[4,640,512]{2,1,0:T(8,128)(2,1)}, u32[]{:S(2)}, u32[]{:S(2)}) async-start(bf16[4,640,512]{2,1,0:T(8,128)(2,1)} %broadcast_in_dim.35), calls=%async_computation.1 | async-start | bytes 5242880 | tf_op jit(solution)/shard_map/all_to_all | solution.py:349
  98.6 38.6 %collective-permute-start.13 = (bf16[3,384,512]{2,1,0:T(8,128)(2,1)}, bf16[3,384,512]{2,1,0:T(8,128)(2,1)}, u32[]{:S(2)}, u32[]{:S(2)}) collective-permute-start(bf16[3,384,512]{2,1,0:T(8,128)(2,1)} %pad_maximum_fusion), channel_id=1, source_target_pairs={{0,16},{8,24},{16,0},{24,8},{32,48},{40,56},{48,32},{56,40},{64,80... | collective-permute-start | bytes 3538952 | tf_op jit(solution)/shard_map/ppermute | solution.py:34
  137.1 8.6 %collective-permute-start.12 = (f32[256,640]{1,0:T(8,128)}, f32[256,640]{1,0:T(8,128)}, u32[]{:S(2)}, u32[]{:S(2)}) collective-permute-start(f32[256,640]{1,0:T(8,128)} %get-tuple-element.61), channel_id=1, source_target_pairs={{0,8},{8,0},{16,24},{24,16},{32,40},{40,32},{48,56},{56,48},{64,72... | collective-permute-start | bytes 1966088 | tf_op jit(solution)/shard_map/ppermute | solution.py:34
  139.3 6.4 %copy-start.9 = (f32[128,1024]{1,0:T(8,128)S(1)}, f32[128,1024]{1,0:T(8,128)}, u32[]{:S(2)}) copy-start(f32[128,1024]{1,0:T(8,128)} %copy-done.8) | copy-start | bytes 1572868
  139.3 6.4 %copy-start.11 = (f32[128,1024]{1,0:T(8,128)S(1)}, f32[128,1024]{1,0:T(8,128)}, u32[]{:S(2)}) copy-start(f32[128,1024]{1,0:T(8,128)} %copy-done.10) | copy-start | bytes 1572868
  143.7 1.9 collective-permute-start.14
  151.7 4.0 %collective-permute-start.15 = (bf16[8,256,256]{2,1,0:T(8,128)(2,1)S(1)}, bf16[8,256,256]{2,1,0:T(8,128)(2,1)S(1)}, u32[]{:S(2)}, u32[]{:S(2)}) collective-permute-start(bf16[8,256,256]{2,1,0:T(8,128)(2,1)S(1)} %get-tuple-element.70), channel_id=1, source_target_pairs={{0,8},{8,0},{16,24},{24,16},{32,40},{40,32},{48,56},{56,48},{64,72... | collective-permute-start | bytes 3145736 | tf_op jit(solution)/shard_map/ppermute | solution.py:34
  (11 other events, 16.0 us)
Sparse Core Ops, SparseCore 0:
  9.7 38.5 all-gather.4
  55.3 37.0 all-gather.6

commit v12 on v10

--- a/solution.py
+++ b/solution.py
@@ -19,7 +19,7 @@
 LOG2E = 1.0 / math.log(2.0)
 BF16 = jnp.bfloat16
 F32 = jnp.float32
-VMEM_LIMIT = 26 * 2**20
+VMEM_LIMIT = 20 * 2**20
 
 FIRST, COUNT, CLEAR, CORE, TABLE = 0, 1, 2, 3, 4
 
@@ -157,10 +157,10 @@
         ),
         out_shape=[
             pltpu.HBM((live, heads * rows), BF16),
-            jax.ShapeDtypeStruct((HEAD_WIDTH, heads * rows), F32),
+            pltpu.HBM((HEAD_WIDTH, heads * rows), F32),
         ],
         compiler_params=pltpu.CompilerParams(vmem_limit_bytes=VMEM_LIMIT),
-        cost_estimate=pl.CostEstimate(flops=10**10, bytes_accessed=10 * 2**20, transcendentals=0),
+        cost_estimate=pl.CostEstimate(flops=10**8, bytes_accessed=2**20, transcendentals=0),
         name="forward%d" % part,
     )(info, query_pos, query_start, in_hbm(queries), in_hbm(kv))
 
@@ -301,14 +301,16 @@
     tokens, depth = grads[0].shape
     features = stacks[0].shape[1]
     half = jax.ShapeDtypeStruct((tokens // 2, features), F32)
-    out_spec = pl.BlockSpec((tokens // 2, features), lambda i: (0, 0))
+
+    def once(shape):
+        return pl.BlockSpec(shape, lambda i: (0,) * len(shape), pipeline_mode=pl.Buffered(1))
+
     return pl.pallas_call(
         functools.partial(project_kernel, chips),
         grid=(1,),
         in_specs=[pl.BlockSpec(memory_space=pltpu.SMEM)]
-        + [pl.BlockSpec(ref.shape, lambda i: (0, 0)) for ref in grads]
-        + [pl.BlockSpec(ref.shape, lambda i: (0, 0, 0)) for ref in stacks],
-        out_specs=[out_spec, out_spec],
+        + [once(ref.shape) for ref in (*grads, *stacks)],
+        out_specs=[once(half.shape)] * 2,
         out_shape=[half, half],
         scratch_shapes=[pltpu.VMEM((chips, tokens, depth), BF16)],
         compiler_params=pltpu.CompilerParams(vmem_limit_bytes=VMEM_LIMIT),
@@ -344,9 +346,14 @@
     info = jnp.concatenate([scalars, *table]).astype(jnp.int32)
     query_pos, query_start = query_pos[None, :], query_start[None, :]
 
+    def copy(block, groups):
+        return jnp.broadcast_to(block, (len(groups[0]), *block.shape))
+
+    def exchange(copies, axis, groups):
+        return lax.all_to_all(copies, axis, 0, 0, axis_index_groups=groups, tiled=True)
+
     def spread(block, axis, groups):
-        copies = jnp.broadcast_to(block, (len(groups[0]), *block.shape))
-        return lax.all_to_all(copies, axis, 0, 0, axis_index_groups=groups, tiled=True)
+        return exchange(copy(block, groups), axis, groups)
 
     groups = [[2 * i + c for i in range(8)] for c in range(2)]
     kept = jnp.where(core == 0, keys, values)
@@ -365,19 +372,22 @@
         return lax.all_gather(block, "dp", axis=0, axis_index_groups=groups_x)
 
     own = [out_weight[:SPLIT], out_weight[SPLIT:]]
-    ring, own, chip_grad = lax.optimization_barrier((ring, own, chip_grad))
     plane1 = gather_x(own[1])
+    pair0 = dp_move(own[0], 0, 1, 0)
+    ring, own, all_grad, pair0, chip_grad = lax.optimization_barrier(
+        (ring, own, all_grad, pair0, chip_grad)
+    )
+    plane0 = gather_x(own[0])
     swapped = dp_move(ring, 0, 0, 1)
+    swapped, copies = lax.optimization_barrier((swapped, copy(pair0, groups_x)))
+    other_plane = exchange(copies, "dp", groups_x).reshape(4, SPLIT, depth)
     grad_pair = tensor_move(chip_grad, 1, 0)
-    paired = [dp_move(block, 0, 1, 0) for block in own]
-    swapped, own0 = lax.optimization_barrier((swapped, own[0]))
-    plane0 = gather_x(own0)
+    pair1 = dp_move(own[1], 0, 1, 0)
     kv = jnp.concatenate([ring, swapped], axis=0)
 
     first = forward(0, info, query_pos, query_start, queries, kv)
-    first, grad_pair, pair0 = lax.optimization_barrier((first, grad_pair, paired[0]))
+    first, grad_pair, pair1 = lax.optimization_barrier((first, grad_pair, pair1))
     all_grad += [grad_pair] + [tensor_move(grad_pair, 0, step) for step in (-1, -2, 1)]
-    other_plane = spread(pair0, "dp", groups_x).reshape(4, SPLIT, depth)
     rest = jnp.concatenate(
         [lax.dynamic_slice_in_dim(plane1, (x + i) % 4, 1, 0) for i in range(1, 4)], axis=0
     )
@@ -397,7 +407,7 @@
         jnp.stack(same + [slot(x + i, 1 - z) for i in range(4)]).astype(jnp.int32),
     ]
     slots[0] = after(slots[0], second[1])
-    stacks = [[plane0, other_plane], [plane1, paired[1][None], rest]]
+    stacks = [[plane0, other_plane], [plane1, pair1[None], rest]]
     terms = []
     for part in range(CHUNKS):
         mine, other = project(part, slots[part], all_grad, stacks[part])

time: 201 us -> 184 us (0.915)
  waiting for transfers between devices: 55.4 us -> 46.4 us
  starting transfers between devices: 41 us -> 34.2 us
  local copies, waits for them, and re-layouts: 18.1 us -> 14.2 us
  blocking collectives: 32.3 us -> 35.7 us
    ppermute x9, waiting for transfers between devices: 4.89 us -> 28.1 us  [dp_move(): return lax.ppermute(value, 'dp', pairs)]
    ppermute x7, waiting for transfers between devices: 35.9 us -> 17.7 us  [tensor_move(): return lax.ppermute(value, 'tensor', pairs)]
    all_to_all x2, waiting for transfers between devices: 14.6 us -> 0.6 us  [exchange(): lax.all_to_all(copies, axis, 0, 0, axis_index_groups=groups, tiled=True)]
    ppermute x7, starting transfers between devices: 19.5 us -> 12.2 us  [tensor_move(): return lax.ppermute(value, 'tensor', pairs)]
    unnamed x35 -> x23, local copies, waits for them, and re-layouts: 8.89 us -> 3.6 us
    all_to_all x1, blocking collectives: 32.3 us -> 35.7 us  [local(): lax.all_to_all(chip_sums, 'dp', 0, 0, axis_index_groups=groups, tiled=True)]
  transfers between devices with their start and end apart: 20 -> 20, of which waited for: 7 -> 10; matrix products, arithmetic and copies ran while one was open for 5% -> 7% of each run, Pallas kernels for 11% -> 13%
where the time goes in v12:
time: 184 us; the launch traced here: 183 us
  waiting for transfers between devices  46.4 us (25%)
  blocking collectives  35.7 us (19%)
  starting transfers between devices  34.2 us (19%)
  Pallas kernels  29.4 us (16%)
  between operations  20.3 us (11%)
  local copies, waits for them, and re-layouts  14.2 us (8%)
  other arithmetic  2.87 us (2%)
    all_to_all x1, blocking collectives, local(): lax.all_to_all(chip_sums, 'dp', 0, 0, axis_index_groups=groups, tiled=True)  35.7 us
    ppermute x9, waiting for transfers between devices, dp_move(): return lax.ppermute(value, 'dp', pairs)  28.1 us
    ppermute x7, waiting for transfers between devices, tensor_move(): return lax.ppermute(value, 'tensor', pairs)  17.7 us
    all_to_all x2, starting transfers between devices, exchange(): lax.all_to_all(copies, axis, 0, 0, axis_index_groups=groups, tiled=True)  12.2 us
    ppermute x7, starting transfers between devices, tensor_move(): return lax.ppermute(value, 'tensor', pairs)  12.2 us
    pallas_call x2, Pallas kernels, project(): pl.pallas_call(functools.partial(project_kernel, chips), grid=(1,), in_sp...  12.2 us
    pallas_call x2, Pallas kernels, forward(): pl.pallas_call(forward_kernel, grid_spec=pltpu.PrefetchScalarGridSpec(num...  11.2 us
    ppermute x9, starting transfers between devices, dp_move(): return lax.ppermute(value, 'dp', pairs)  9.68 us
  transfers between devices with their start and end apart: 20, of which 10 were waited for; matrix products, arithmetic and copies ran while one was open for 7% of the time, Pallas kernels for 13%

profile of v12, /device:TPU:0, one launch (start us, length us, event | category | flops | bytes accessed | tf_op | source)
XLA Modules:
  0.0 183.0 jit_solution(1358029243416583352)
XLA Ops:
  7.2 1.8 slice.29
  12.4 7.7 %all-to-all-start = ((bf16[8,512,128]{2,1,0:T(8,128)(2,1)}), bf16[8,512,128]{2,1,0:T(8,128)(2,1)}, u32[]{:S(2)}, u32[]{:S(2)}) async-start(bf16[8,512,128]{2,1,0:T(8,128)(2,1)} %broadcast_in_dim.34), calls=%async_computation | async-start | bytes 2097152 | tf_op jit(solution)/shard_map/all_to_all | solution.py:353
  20.4 3.6 %collective-permute-start.5 = (bf16[640,512]{1,0:T(8,128)(2,1)S(1)}, bf16[640,512]{1,0:T(8,128)(2,1)S(1)}, u32[]{:S(2)}, u32[]{:S(2)}) collective-permute-start(bf16[640,512]{1,0:T(8,128)(2,1)S(1)} %slice.30), channel_id=1, source_target_pairs={{0,16},{8,24},{16,0},{24,8},{32,48},{40,56},{48,32},{56,40},{64,80... | collective-permute-start | bytes 1966088 | tf_op jit(solution)/shard_map/ppermute | solution.py:34
  24.0 1.6 collective-permute-start.4
  25.6 2.9 %collective-permute-start.3 = (bf16[512,512]{1,0:T(8,128)(2,1)S(1)}, bf16[512,512]{1,0:T(8,128)(2,1)S(1)}, u32[]{:S(2)}, u32[]{:S(2)}) collective-permute-start(bf16[512,512]{1,0:T(8,128)(2,1)S(1)} %pad_maximum_fusion.1.rest_0_), channel_id=1, source_target_pairs={{0,2},{1,3},{2,0},{3,1},{4,6},{5,7},{6,4},{7,5},{8,10},{9,11},{10,... | collective-permute-start | bytes 1572872 | tf_op jit(solution)/shard_map/ppermute | solution.py:42
  29.9 19.7 %collective-permute-done.5 = bf16[640,512]{1,0:T(8,128)(2,1)S(1)} collective-permute-done((bf16[640,512]{1,0:T(8,128)(2,1)S(1)}, bf16[640,512]{1,0:T(8,128)(2,1)S(1)}, u32[]{:S(2)}, u32[]{:S(2)}) %collective-permute-start.5) | collective-permute-done | bytes 655392 | tf_op jit(solution)/shard_map/ppermute | solution.py:34
  49.6 2.2 %collective-permute-done.3.rest_2_ = bf16[512,512]{1,0:T(8,128)(2,1)S(1)} collective-permute-done((bf16[512,512]{1,0:T(8,128)(2,1)S(1)}, bf16[512,512]{1,0:T(8,128)(2,1)S(1)}, u32[]{:S(2)}, u32[]{:S(2)}) %collective-permute-start.3) | collective-permute-done | bytes 524320 | tf_op jit(solution)/shard_map/ppermute | solution.py:42
  60.6 2.8 %broadcast_in_dim.35 = bf16[4,640,512]{2,1,0:T(8,128)(2,1)} broadcast(bf16[640,512]{1,0:T(8,128)(2,1)} %copy-done.8), dimensions={1,2} | broadcast | bytes 3276800 | tf_op jit(solution)/shard_map/broadcast_in_dim | solution.py:350
  63.4 4.5 %all-to-all-start.1 = ((bf16[4,640,512]{2,1,0:T(8,128)(2,1)}), bf16[4,640,512]{2,1,0:T(8,128)(2,1)}, u32[]{:S(2)}, u32[]{:S(2)}) async-start(bf16[4,640,512]{2,1,0:T(8,128)(2,1)} %broadcast_in_dim.35), calls=%async_computation.1 | async-start | bytes 5242880 | tf_op jit(solution)/shard_map/all_to_all | solution.py:353
  69.3 2.0 %collective-permute-start.8 = (bf16[384,512]{1,0:T(8,128)(2,1)S(1)}, bf16[384,512]{1,0:T(8,128)(2,1)S(1)}, u32[]{:S(2)}, u32[]{:S(2)}) collective-permute-start(bf16[384,512]{1,0:T(8,128)(2,1)S(1)} %copy-done.6), channel_id=1, source_target_pairs={{0,16},{8,24},{16,0},{24,8},{32,48},{40,56},{48,32},{56,40},{64,80... | collective-permute-start | bytes 1179656 | tf_op jit(solution)/shard_map/ppermute | solution.py:34
  74.0 5.6 %forward0.1 = (bf16[2816,1024]{1,0:T(8,128)(2,1)}, f32[128,1024]{1,0:T(8,128)}) custom-call(s32[36]{0:T(128)S(1)} %concatenate.15.info, s32[1,256]{1,0:T(1,128)S(1)} %iota_add_fusion.pos_ref, s32[1,256]{1,0:T(1,128)S(1)} %bitcast.28, bf16[256,1024]{1,0:T(8,128)(2,1)} %rest_8_.1, bf16[8192,128]{1,0:T(8,128)(2,1)} %copy-done.4), custom_call_target="tpu_custom_call" | custom-call | flops 100000000 | bytes 1048576 | tf_op jit(solution)/shard_map/forward0/pallas_call | solution.py:138
  79.6 3.5 %collective-permute-done.8 = bf16[384,512]{1,0:T(8,128)(2,1)S(1)} collective-permute-done((bf16[384,512]{1,0:T(8,128)(2,1)S(1)}, bf16[384,512]{1,0:T(8,128)(2,1)S(1)}, u32[]{:S(2)}, u32[]{:S(2)}) %collective-permute-start.8) | collective-permute-done | bytes 393248 | tf_op jit(solution)/shard_map/ppermute | solution.py:34
  85.7 1.6 collective-permute-start.13
  88.5 2.4 %collective-permute-start.10 = (bf16[512,512]{1,0:T(8,128)(2,1)S(1)}, bf16[512,512]{1,0:T(8,128)(2,1)}, u32[]{:S(2)}, u32[]{:S(2)}) collective-permute-start(bf16[512,512]{1,0:T(8,128)(2,1)S(1)} %collective-permute-done.7.rest_4_), channel_id=1, source_target_pairs={{0,2},{1,3},{2,0},{3,1},{4,6},{5,7},{6,4},{7,5},{8,10},{9,11},{10,... | collective-permute-start | bytes 1572872 | tf_op jit(solution)/shard_map/ppermute | solution.py:42
  90.9 1.6 collective-permute-start.9
  92.6 5.6 %forward1.1 = (bf16[2816,1024]{1,0:T(8,128)(2,1)}, f32[128,1024]{1,0:T(8,128)}) custom-call(s32[36]{0:T(128)S(1)} %concatenate.15.info, s32[1,256]{1,0:T(1,128)S(1)} %iota_add_fusion.pos_ref, s32[1,256]{1,0:T(1,128)S(1)} %bitcast.29, bf16[256,1024]{1,0:T(8,128)(2,1)} %rest_8_.1, bf16[8192,128]{1,0:T(8,128)(2,1)} %copy-done.4), custom_call_target="tpu_custom_call" | custom-call | flops 100000000 | bytes 1048576 | tf_op jit(solution)/shard_map/forward1/pallas_call | solution.py:138
  98.2 4.7 %collective-permute-done.11.rest_7_ = bf16[512,512]{1,0:T(8,128)(2,1)S(1)} collective-permute-done((bf16[512,512]{1,0:T(8,128)(2,1)S(1)}, bf16[512,512]{1,0:T(8,128)(2,1)S(1)}, u32[]{:S(2)}, u32[]{:S(2)}) %collective-permute-start.11) | collective-permute-done | bytes 524320 | tf_op jit(solution)/shard_map/ppermute | solution.py:42
  102.9 10.6 %collective-permute-done.10.rest_6_ = bf16[512,512]{1,0:T(8,128)(2,1)} collective-permute-done((bf16[512,512]{1,0:T(8,128)(2,1)S(1)}, bf16[512,512]{1,0:T(8,128)(2,1)}, u32[]{:S(2)}, u32[]{:S(2)}) %collective-permute-start.10) | collective-permute-done | bytes 524320 | tf_op jit(solution)/shard_map/ppermute | solution.py:42
  114.3 7.4 %project0.1 = (f32[256,640]{1,0:T(8,128)S(1)}, f32[256,640]{1,0:T(8,128)}) custom-call(s32[8]{0:T(128)S(1)} %stack.70.slots, bf16[512,512]{1,0:T(8,128)(2,1)S(1)} %pad_maximum_fusion.1.rest_0_, bf16[512,512]{1,0:T(8,128)(2,1)S(1)} %collective-permute-done.2.rest_1_, bf16[512,512]{1,0:T(8,128)(2,1)S(1)} %collective-permute-done.3.rest_2_, ...), custom_call_target="tpu_custom_call" | custom-call | flops 2684354560 | bytes 10485760 | tf_op jit(solution)/shard_map/project0/pallas_call | solution.py:308
  122.7 4.8 %project1.1 = (f32[256,384]{1,0:T(8,128)S(1)}, f32[256,384]{1,0:T(8,128)S(1)}) custom-call(s32[8]{0:T(128)S(1)} %stack.75.slots, bf16[512,512]{1,0:T(8,128)(2,1)S(1)} %pad_maximum_fusion.1.rest_0_, bf16[512,512]{1,0:T(8,128)(2,1)S(1)} %collective-permute-done.2.rest_1_, bf16[512,512]{1,0:T(8,128)(2,1)S(1)} %collective-permute-done.3.rest_2_, ...), custom_call_target="tpu_custom_call" | custom-call | flops 1610612736 | bytes 10485760 | tf_op jit(solution)/shard_map/project1/pallas_call | solution.py:308
  129.4 6.0 %backward.1 = (bf16[256,1024]{1,0:T(8,128)(2,1)}, f32[8,256,256]{2,1,0:T(8,128)S(1)}, bf16[8,256,256]{2,1,0:T(8,128)(2,1)S(1)}) custom-call(s32[36]{0:T(128)S(1)} %concatenate.15.info, f32[256,640]{1,0:T(8,128)S(1)} %copy-done.3, f32[256,640]{1,0:T(8,128)} %collective-permute-done.12.rest_1_, f32[256,384]{1,0:T(8,128)S(1)} %get-tuple-element.54.rest_2_, ...), custom_call_target="tpu_custom_call" | custom-call | flops 8000000000 | bytes 10485760 | tf_op jit(solution)/shard_map/backward/pallas_call | solution.py:242
  135.4 1.7 collective-permute-start.15
  137.2 2.3 %collective-permute-done.15 = bf16[8,256,256]{2,1,0:T(8,128)(2,1)S(1)} collective-permute-done((bf16[8,256,256]{2,1,0:T(8,128)(2,1)S(1)}, bf16[8,256,256]{2,1,0:T(8,128)(2,1)S(1)}, u32[]{:S(2)}, u32[]{:S(2)}) %collective-permute-start.15) | collective-permute-done | bytes 1048608 | tf_op jit(solution)/shard_map/ppermute | solution.py:34
  139.7 35.7 %all_to_all.15 = bf16[8,256,256]{2,1,0:T(8,128)(2,1)S(1)} all-to-all(bf16[8,256,256]{2,1,0:T(8,128)(2,1)S(1)} %add_convert_fusion), channel_id=1, replica_groups={{0,16,32,48,64,80,96,112},{8,24,40,56,72,88,104,120},{1,17,33,49,65,81,..., dimensions={0} | all-to-all | bytes 2097152 | tf_op jit(solution)/shard_map/all_to_all | solution.py:419
  (72 shorter events, 20.5 us)
Async XLA Ops:
  7.2 76.0 %all-gather.5.cloned.1.call-start = ((), (), s32[]{:S(2)}) async-start(), calls=%async_computation.3 | async-start | bytes 1966080 | tf_op jit(solution)/shard_map/all_gather | solution.py:372
  9.0 11.2 %copy-start.9 = (bf16[256,1024]{1,0:T(8,128)(2,1)S(1)}, bf16[256,1024]{1,0:T(8,128)(2,1)}, u32[]{:S(2)}) copy-start(bf16[256,1024]{1,0:T(8,128)(2,1)} %param.9) | copy-start | bytes 1572868
  9.9 1.3 collective-permute-start
  11.3 9.0 %copy-start.7 = (bf16[1024,512]{1,0:T(8,128)(2,1)S(1)}, bf16[1024,512]{1,0:T(8,128)(2,1)}, u32[]{:S(2)}) copy-start(bf16[1024,512]{1,0:T(8,128)(2,1)} %param.10) | copy-start | bytes 3145732
  12.4 39.4 %all-to-all-start = ((bf16[8,512,128]{2,1,0:T(8,128)(2,1)}), bf16[8,512,128]{2,1,0:T(8,128)(2,1)}, u32[]{:S(2)}, u32[]{:S(2)}) async-start(bf16[8,512,128]{2,1,0:T(8,128)(2,1)} %broadcast_in_dim.34), calls=%async_computation | async-start | bytes 2097152 | tf_op jit(solution)/shard_map/all_to_all | solution.py:353
  20.1 34.4 %copy-start.10 = (s32[8]{0:T(128)S(1)}, s32[8]{0:T(128)}, u32[]{:S(2)}) copy-start(s32[8]{0:T(128)} %param.11) | copy-start | bytes 100
  20.1 94.2 %all-gather.7.cloned.1.call-start = ((), (), s32[]{:S(2)}) async-start(), calls=%async_computation.4 | async-start | bytes 3276800 | tf_op jit(solution)/shard_map/all_gather | solution.py:372
  20.2 3.7 %collective-permute-start.1 = (bf16[256,512]{1,0:T(8,128)(2,1)S(1)}, bf16[256,512]{1,0:T(8,128)(2,1)S(1)}, u32[]{:S(2)}, u32[]{:S(2)}) collective-permute-start(bf16[256,512]{1,0:T(8,128)(2,1)S(1)} %get-tuple-element.65), channel_id=1, source_target_pairs={{0,8},{8,0},{16,24},{24,16},{32,40},{40,32},{48,56},{56,48},{64,72... | collective-permute-start | bytes 786440 | tf_op jit(solution)/shard_map/ppermute | solution.py:34
  20.4 31.4 %copy-start.5 = (bf16[640,512]{1,0:T(8,128)(2,1)}, bf16[640,512]{1,0:T(8,128)(2,1)S(1)}, u32[]{:S(2)}) copy-start(bf16[640,512]{1,0:T(8,128)(2,1)S(1)} %slice.30) | copy-start | bytes 1966084
  20.4 29.2 %collective-permute-start.5 = (bf16[640,512]{1,0:T(8,128)(2,1)S(1)}, bf16[640,512]{1,0:T(8,128)(2,1)S(1)}, u32[]{:S(2)}, u32[]{:S(2)}) collective-permute-start(bf16[640,512]{1,0:T(8,128)(2,1)S(1)} %slice.30), channel_id=1, source_target_pairs={{0,16},{8,24},{16,0},{24,8},{32,48},{40,56},{48,32},{56,40},{64,80... | collective-permute-start | bytes 1966088 | tf_op jit(solution)/shard_map/ppermute | solution.py:34
  24.0 25.6 %collective-permute-start.4 = (bf16[512,512]{1,0:T(8,128)(2,1)S(1)}, bf16[512,512]{1,0:T(8,128)(2,1)S(1)}, u32[]{:S(2)}, u32[]{:S(2)}) collective-permute-start(bf16[512,512]{1,0:T(8,128)(2,1)S(1)} %pad_maximum_fusion.1.rest_0_), channel_id=1, source_target_pairs={{0,1},{1,2},{2,3},{3,0},{4,5},{5,6},{6,7},{7,4},{8,9},{9,10},{10,1... | collective-permute-start | bytes 1572872 | tf_op jit(solution)/shard_map/ppermute | solution.py:42
  25.6 26.1 %collective-permute-start.3 = (bf16[512,512]{1,0:T(8,128)(2,1)S(1)}, bf16[512,512]{1,0:T(8,128)(2,1)S(1)}, u32[]{:S(2)}, u32[]{:S(2)}) collective-permute-start(bf16[512,512]{1,0:T(8,128)(2,1)S(1)} %pad_maximum_fusion.1.rest_0_), channel_id=1, source_target_pairs={{0,2},{1,3},{2,0},{3,1},{4,6},{5,7},{6,4},{7,5},{8,10},{9,11},{10,... | collective-permute-start | bytes 1572872 | tf_op jit(solution)/shard_map/ppermute | solution.py:42
  28.5 23.2 %collective-permute-start.2 = (bf16[512,512]{1,0:T(8,128)(2,1)S(1)}, bf16[512,512]{1,0:T(8,128)(2,1)S(1)}, u32[]{:S(2)}, u32[]{:S(2)}) collective-permute-start(bf16[512,512]{1,0:T(8,128)(2,1)S(1)} %pad_maximum_fusion.1.rest_0_), channel_id=1, source_target_pairs={{0,3},{1,0},{2,1},{3,2},{4,7},{5,4},{6,5},{7,6},{8,11},{9,8},{10,9... | collective-permute-start | bytes 1572872 | tf_op jit(solution)/shard_map/ppermute | solution.py:42
  51.8 8.7 %collective-permute-start.6 = (bf16[4096,128]{1,0:T(8,128)(2,1)}, bf16[4096,128]{1,0:T(8,128)(2,1)}, u32[]{:S(2)}, u32[]{:S(2)}) collective-permute-start(bf16[4096,128]{1,0:T(8,128)(2,1)} %bitcast.19), channel_id=1, source_target_pairs={{0,8},{8,0},{16,24},{24,16},{32,40},{40,32},{48,56},{56,48},{64,72... | collective-permute-start | bytes 3145736 | tf_op jit(solution)/shard_map/ppermute | solution.py:34
  59.5 23.7 %collective-permute-start.7 = (bf16[512,512]{1,0:T(8,128)(2,1)S(1)}, bf16[512,512]{1,0:T(8,128)(2,1)S(1)}, u32[]{:S(2)}, u32[]{:S(2)}) collective-permute-start(bf16[512,512]{1,0:T(8,128)(2,1)S(1)} %pad_maximum_fusion.1.rest_0_), channel_id=1, source_target_pairs={{0,4},{1,5},{2,6},{3,7},{4,0},{5,1},{6,2},{7,3},{8,12},{9,13},{10,... | collective-permute-start | bytes 1572872 | tf_op jit(solution)/shard_map/ppermute | solution.py:42
  63.4 51.0 %all-to-all-start.1 = ((bf16[4,640,512]{2,1,0:T(8,128)(2,1)}), bf16[4,640,512]{2,1,0:T(8,128)(2,1)}, u32[]{:S(2)}, u32[]{:S(2)}) async-start(bf16[4,640,512]{2,1,0:T(8,128)(2,1)} %broadcast_in_dim.35), calls=%async_computation.1 | async-start | bytes 5242880 | tf_op jit(solution)/shard_map/all_to_all | solution.py:353
  69.3 13.8 %collective-permute-start.8 = (bf16[384,512]{1,0:T(8,128)(2,1)S(1)}, bf16[384,512]{1,0:T(8,128)(2,1)S(1)}, u32[]{:S(2)}, u32[]{:S(2)}) collective-permute-start(bf16[384,512]{1,0:T(8,128)(2,1)S(1)} %copy-done.6), channel_id=1, source_target_pairs={{0,16},{8,24},{16,0},{24,8},{32,48},{40,56},{48,32},{56,40},{64,80... | collective-permute-start | bytes 1179656 | tf_op jit(solution)/shard_map/ppermute | solution.py:34
  85.7 37.0 %collective-permute-start.13 = (bf16[3,384,512]{2,1,0:T(8,128)(2,1)}, bf16[3,384,512]{2,1,0:T(8,128)(2,1)}, u32[]{:S(2)}, u32[]{:S(2)}) collective-permute-start(bf16[3,384,512]{2,1,0:T(8,128)(2,1)} %pad_maximum_fusion), channel_id=1, source_target_pairs={{0,16},{8,24},{16,0},{24,8},{32,48},{40,56},{48,32},{56,40},{64,80... | collective-permute-start | bytes 3538952 | tf_op jit(solution)/shard_map/ppermute | solution.py:34
  87.3 15.7 %collective-permute-start.11 = (bf16[512,512]{1,0:T(8,128)(2,1)S(1)}, bf16[512,512]{1,0:T(8,128)(2,1)S(1)}, u32[]{:S(2)}, u32[]{:S(2)}) collective-permute-start(bf16[512,512]{1,0:T(8,128)(2,1)S(1)} %collective-permute-done.7.rest_4_), channel_id=1, source_target_pairs={{0,1},{1,2},{2,3},{3,0},{4,5},{5,6},{6,7},{7,4},{8,9},{9,10},{10,1... | collective-permute-start | bytes 1572872 | tf_op jit(solution)/shard_map/ppermute | solution.py:42
  88.5 25.0 %collective-permute-start.10 = (bf16[512,512]{1,0:T(8,128)(2,1)S(1)}, bf16[512,512]{1,0:T(8,128)(2,1)}, u32[]{:S(2)}, u32[]{:S(2)}) collective-permute-start(bf16[512,512]{1,0:T(8,128)(2,1)S(1)} %collective-permute-done.7.rest_4_), channel_id=1, source_target_pairs={{0,2},{1,3},{2,0},{3,1},{4,6},{5,7},{6,4},{7,5},{8,10},{9,11},{10,... | collective-permute-start | bytes 1572872 | tf_op jit(solution)/shard_map/ppermute | solution.py:42
  90.9 22.8 %collective-permute-start.9 = (bf16[512,512]{1,0:T(8,128)(2,1)S(1)}, bf16[512,512]{1,0:T(8,128)(2,1)}, u32[]{:S(2)}, u32[]{:S(2)}) collective-permute-start(bf16[512,512]{1,0:T(8,128)(2,1)S(1)} %collective-permute-done.7.rest_4_), channel_id=1, source_target_pairs={{0,3},{1,0},{2,1},{3,2},{4,7},{5,4},{6,5},{7,6},{8,11},{9,8},{10,9... | collective-permute-start | bytes 1572872 | tf_op jit(solution)/shard_map/ppermute | solution.py:42
  122.6 6.8 %collective-permute-start.12 = (f32[256,640]{1,0:T(8,128)}, f32[256,640]{1,0:T(8,128)}, u32[]{:S(2)}, u32[]{:S(2)}) collective-permute-start(f32[256,640]{1,0:T(8,128)} %get-tuple-element.51), channel_id=1, source_target_pairs={{0,8},{8,0},{16,24},{24,16},{32,40},{40,32},{48,56},{56,48},{64,72... | collective-permute-start | bytes 1966088 | tf_op jit(solution)/shard_map/ppermute | solution.py:34
  127.5 1.9 %collective-permute-start.14 = (f32[256,384]{1,0:T(8,128)S(1)}, f32[256,384]{1,0:T(8,128)S(1)}, u32[]{:S(2)}, u32[]{:S(2)}) collective-permute-start(f32[256,384]{1,0:T(8,128)S(1)} %get-tuple-element.55), channel_id=1, source_target_pairs={{0,8},{8,0},{16,24},{24,16},{32,40},{40,32},{48,56},{56,48},{64,72... | collective-permute-start | bytes 1179656 | tf_op jit(solution)/shard_map/ppermute | solution.py:34
  135.4 4.0 %collective-permute-start.15 = (bf16[8,256,256]{2,1,0:T(8,128)(2,1)S(1)}, bf16[8,256,256]{2,1,0:T(8,128)(2,1)S(1)}, u32[]{:S(2)}, u32[]{:S(2)}) collective-permute-start(bf16[8,256,256]{2,1,0:T(8,128)(2,1)S(1)} %get-tuple-element.60), channel_id=1, source_target_pairs={{0,8},{8,0},{16,24},{24,16},{32,40},{40,32},{48,56},{56,48},{64,72... | collective-permute-start | bytes 3145736 | tf_op jit(solution)/shard_map/ppermute | solution.py:34
  (7 other events, 26.0 us)
Sparse Core Ops, SparseCore 0:
  9.7 38.5 all-gather.4
  51.9 48.0 all-gather.6

commit v13 on v12

--- a/solution.py
+++ b/solution.py
@@ -19,7 +19,7 @@
 LOG2E = 1.0 / math.log(2.0)
 BF16 = jnp.bfloat16
 F32 = jnp.float32
-VMEM_LIMIT = 20 * 2**20
+VMEM_LIMIT = 22 * 2**20
 
 FIRST, COUNT, CLEAR, CORE, TABLE = 0, 1, 2, 3, 4
 
@@ -62,7 +62,9 @@
     return pl.ds(pl.multiple_of(index * KEY_BLOCK, KEY_BLOCK), KEY_BLOCK)
 
 
-def forward_kernel(info, pos_ref, start_ref, q_ref, kv_ref, probs_ref, out_ref, score, vt):
+def forward_kernel(
+    info, pos_ref, start_ref, q_ref, here_ref, there_ref, probs_ref, out_ref, score, keys, vt
+):
     first, count = info[FIRST], info[COUNT]
     rows = q_ref.shape[0]
     heads = q_ref.shape[1] // HEAD_WIDTH
@@ -77,13 +79,15 @@
     @pl.when(pl.program_id(0) == 0)
     def _():
         def turn(index, _):
-            source = info[TABLE + 16 + first + index]
-            vt[:, block_rows(index)] = kv_ref[block_rows(source), :].T
+            here = here_ref[block_rows(info[TABLE + first + index]), :]
+            there = there_ref[block_rows(info[TABLE + 16 + first + index]), :]
+            keys[block_rows(index), :] = jnp.where(info[CORE] == 0, here, there)
+            vt[:, block_rows(index)] = jnp.where(info[CORE] == 0, there, here).T
             return 0
         lax.fori_loop(0, count, turn, 0)
 
     def product(index):
-        return dot(kv_ref[block_rows(info[TABLE + first + index]), :], query_t)
+        return dot(keys[block_rows(index), :], query_t)
 
     def masked_step(index, top):
         key_pos = (first + index) * KEY_BLOCK + lax.broadcasted_iota(jnp.int32, (KEY_BLOCK, rows), 0)
@@ -129,29 +133,29 @@
     return (MOST + rows - 2) // KEY_BLOCK + 1
 
 
-def forward(part, info, query_pos, query_start, queries, kv):
+def forward(info, query_pos, query_start, queries, here, there):
     rows, width = queries.shape
-    heads = width // HEAD_WIDTH // CHUNKS
-    steps = heads // PAIR
+    heads = width // HEAD_WIDTH
     live = most_blocks(rows) * KEY_BLOCK
     line = pl.BlockSpec((1, rows), lambda h, r: (0, 0))
     return pl.pallas_call(
         forward_kernel,
         grid_spec=pltpu.PrefetchScalarGridSpec(
             num_scalar_prefetch=1,
-            grid=(steps,),
+            grid=(heads // PAIR,),
             in_specs=[
                 line,
                 line,
-                pl.BlockSpec((rows, PAIR * HEAD_WIDTH), lambda h, r: (0, part * steps + h)),
-                pl.BlockSpec(kv.shape, lambda h, r: (0, 0), pipeline_mode=pl.Buffered(1)),
-            ],
+                pl.BlockSpec((rows, PAIR * HEAD_WIDTH), lambda h, r: (0, h)),
+            ]
+            + [pl.BlockSpec(here.shape, lambda h, r: (0, 0), pipeline_mode=pl.Buffered(1))] * 2,
             out_specs=[
                 pl.BlockSpec((live, PAIR * rows), lambda h, r: (0, h)),
                 pl.BlockSpec((HEAD_WIDTH, PAIR * rows), lambda h, r: (0, h)),
             ],
             scratch_shapes=[
                 pltpu.VMEM((live, PAIR * rows), F32),
+                pltpu.VMEM((live, HEAD_WIDTH), BF16),
                 pltpu.VMEM((HEAD_WIDTH, live), BF16),
             ],
         ),
@@ -161,22 +165,17 @@
         ],
         compiler_params=pltpu.CompilerParams(vmem_limit_bytes=VMEM_LIMIT),
         cost_estimate=pl.CostEstimate(flops=10**8, bytes_accessed=2**20, transcendentals=0),
-        name="forward%d" % part,
-    )(info, query_pos, query_start, in_hbm(queries), in_hbm(kv))
+        name="forward",
+    )(info, query_pos, query_start, in_hbm(queries), here, there)
 
 
 def backward_kernel(heads, info, *rest):
-    terms, all_probs, all_outs = rest[:4], rest[4:6], rest[6:8]
-    q_ref, k_ref, v_ref, gq_ref, own_ref, other_ref, *scratch = rest[8:]
+    terms, rest = rest[:4], rest[4:]
+    probs_ref, out_ref, q_ref, here_ref, there_ref, gq_ref, own_ref, other_ref, *scratch = rest
     grad_t, stack, delta, total_q, dscores, other = scratch
     step = pl.program_id(0)
     count = info[COUNT]
     rows = q_ref.shape[0]
-    width = heads // 2 * rows
-
-    def columns(refs, h):
-        at = h * rows % width
-        return refs[h * rows // width][:, at : at + rows]
 
     @pl.when(step == 0)
     def _():
@@ -197,20 +196,20 @@
             grad_t[:, cols] = turned
             stack[cols, :HEAD_WIDTH] = q_ref[:, wide]
             stack[cols, HEAD_WIDTH:] = grad
-            delta[:, cols] = jnp.sum(turned.astype(F32) * columns(all_outs, h), axis=0, keepdims=True)
+            delta[:, cols] = jnp.sum(turned.astype(F32) * out_ref[:, cols], axis=0, keepdims=True)
 
     @pl.when(step < count)
     def _():
         block = info[FIRST] + step
-        keys_t = k_ref[...].T
+        keys_t = jnp.where(info[CORE] == 0, here_ref[...], there_ref[...]).T
+        values = jnp.where(info[CORE] == 0, there_ref[...], here_ref[...])
         for h in range(heads):
             cols = slice(h * rows, (h + 1) * rows)
-            dprob = dot(v_ref[...], grad_t[:, cols])
-            dscores[:, cols] = (columns(all_probs, h).astype(F32) * (dprob - delta[:, cols])).astype(BF16)
+            dprob = dot(values, grad_t[:, cols])
+            dscores[:, cols] = (probs_ref[:, cols].astype(F32) * (dprob - delta[:, cols])).astype(BF16)
         total_q[...] += dot(keys_t, dscores[...])
         key_sum = dot(dscores[...], stack[:, :HEAD_WIDTH])
-        value_sum = dot(all_probs[0][...], stack[:width, HEAD_WIDTH:])
-        value_sum = value_sum + dot(all_probs[1][...], stack[width:, HEAD_WIDTH:])
+        value_sum = dot(probs_ref[...], stack[:, HEAD_WIDTH:])
 
         def add(ref):
             ref[block // 2, :, :HEAD_WIDTH] += key_sum * SCALE
@@ -228,7 +227,7 @@
         other_ref[...] = other[...].astype(BF16)
 
 
-def backward(info, terms, probs, outs, queries, kv):
+def backward(info, terms, probs, outs, queries, here, there):
     rows, width = queries.shape
     heads = width // HEAD_WIDTH
     sums = (8, KEY_BLOCK, 2 * HEAD_WIDTH)
@@ -245,9 +244,9 @@
             num_scalar_prefetch=1,
             grid=(most_blocks(rows),),
             in_specs=[once(term.shape) for term in terms]
-            + [pl.BlockSpec((KEY_BLOCK, p.shape[1]), lambda i, r: (near(i, r), 0)) for p in probs]
-            + [once(out.shape) for out in outs]
             + [
+                pl.BlockSpec((KEY_BLOCK, heads * rows), lambda i, r: (near(i, r), 0)),
+                once(outs.shape),
                 once(queries.shape),
                 pl.BlockSpec(
                     (KEY_BLOCK, HEAD_WIDTH), lambda i, r: (r[TABLE + r[FIRST] + near(i, r)], 0)
@@ -276,7 +275,7 @@
             flops=8 * 10**9, bytes_accessed=10 * 2**20, transcendentals=0
         ),
         name="backward",
-    )(info, *terms, *[in_hbm(p) for p in probs], *outs, in_hbm(queries), in_hbm(kv), in_hbm(kv))
+    )(info, *terms, in_hbm(probs), outs, in_hbm(queries), here, there)
 
 
 def project_kernel(chips, slots, *rest):
@@ -340,10 +339,9 @@
     block = jnp.arange(16, dtype=jnp.int32)
     place = block // 2 * 2
     here = place + jnp.where(block % 2 == core, 0, 1)
-    there = 16 + place + jnp.where(block % 2 == core, 1, 0)
-    table = [jnp.where(core == 0, here, there), jnp.where(core == 0, there, here)]
+    there = place + jnp.where(block % 2 == core, 1, 0)
     scalars = jnp.stack([first, last - first + 1, clear, core])
-    info = jnp.concatenate([scalars, *table]).astype(jnp.int32)
+    info = jnp.concatenate([scalars, here, there]).astype(jnp.int32)
     query_pos, query_start = query_pos[None, :], query_start[None, :]
 
     def copy(block, groups):
@@ -374,26 +372,22 @@
     own = [out_weight[:SPLIT], out_weight[SPLIT:]]
     plane1 = gather_x(own[1])
     pair0 = dp_move(own[0], 0, 1, 0)
-    ring, own, all_grad, pair0, chip_grad = lax.optimization_barrier(
-        (ring, own, all_grad, pair0, chip_grad)
+    ring, own, all_grad, pair0, chip_grad, info, query_pos, query_start = lax.optimization_barrier(
+        (ring, own, all_grad, pair0, chip_grad, info, query_pos, query_start)
     )
     plane0 = gather_x(own[0])
+    grad_pair = tensor_move(chip_grad, 1, 0)
+    pair1 = dp_move(own[1], 0, 1, 0)
     swapped = dp_move(ring, 0, 0, 1)
     swapped, copies = lax.optimization_barrier((swapped, copy(pair0, groups_x)))
     other_plane = exchange(copies, "dp", groups_x).reshape(4, SPLIT, depth)
-    grad_pair = tensor_move(chip_grad, 1, 0)
-    pair1 = dp_move(own[1], 0, 1, 0)
-    kv = jnp.concatenate([ring, swapped], axis=0)
-
-    first = forward(0, info, query_pos, query_start, queries, kv)
-    first, grad_pair, pair1 = lax.optimization_barrier((first, grad_pair, pair1))
-    all_grad += [grad_pair] + [tensor_move(grad_pair, 0, step) for step in (-1, -2, 1)]
     rest = jnp.concatenate(
         [lax.dynamic_slice_in_dim(plane1, (x + i) % 4, 1, 0) for i in range(1, 4)], axis=0
     )
-    rest, later, _ = lax.optimization_barrier((rest, queries, first[1]))
+    rest, grad_pair, later = lax.optimization_barrier((rest, grad_pair, queries))
     rest = dp_move(rest, 0, 1, 0)
-    second = forward(1, info, query_pos, query_start, later, kv)
+    all_grad += [grad_pair] + [tensor_move(grad_pair, 0, step) for step in (-1, -2, 1)]
+    probs, outs = forward(info, query_pos, query_start, later, ring, swapped)
 
     t = lax.axis_index("tensor")
 
@@ -406,14 +400,13 @@
         jnp.stack(same + [slot(i, 1 - z) for i in range(4)]).astype(jnp.int32),
         jnp.stack(same + [slot(x + i, 1 - z) for i in range(4)]).astype(jnp.int32),
     ]
-    slots[0] = after(slots[0], second[1])
+    slots[0] = after(slots[0], outs)
     stacks = [[plane0, other_plane], [plane1, pair1[None], rest]]
     terms = []
     for part in range(CHUNKS):
         mine, other = project(part, slots[part], all_grad, stacks[part])
         terms += [mine, dp_move(other, 0, 0, 1)]
-    probs, outs = zip(first, second)
-    grad_queries, own_sums, other_sums = backward(info, terms, probs, outs, queries, kv)
+    grad_queries, own_sums, other_sums = backward(info, terms, probs, outs, queries, ring, swapped)
 
     chip_sums = (own_sums + dp_move(other_sums, 0, 0, 1).astype(F32)).astype(BF16)
     terms = lax.all_to_all(chip_sums, "dp", 0, 0, axis_index_groups=groups, tiled=True)

time: 184 us -> 185 us (level)
  waiting for transfers between devices: 46.4 us -> 52.9 us
  blocking collectives: 35.7 us -> 31 us
  Pallas kernels: 29.4 us -> 25.8 us
  local copies, waits for them, and re-layouts: 14.2 us -> 16.8 us
    all_to_all x2, waiting for transfers between devices: 0.6 us -> 10.4 us  [exchange(): lax.all_to_all(copies, axis, 0, 0, axis_index_groups=groups, tiled=True)]
    ppermute x9, waiting for transfers between devices: 28.1 us -> 18.6 us  [dp_move(): return lax.ppermute(value, 'dp', pairs)]
    ppermute x7, waiting for transfers between devices: 17.7 us -> 23.8 us  [tensor_move(): return lax.ppermute(value, 'tensor', pairs)]
    all_to_all x1, blocking collectives: 35.7 us -> 31 us  [local(): lax.all_to_all(chip_sums, 'dp', 0, 0, axis_index_groups=groups, tiled=True)]
    pallas_call x2 -> x1, Pallas kernels: 11.2 us -> 7.34 us  [forward(): pl.pallas_call(forward_kernel, grid_spec=pltpu.PrefetchScalarGridSpec(num...]
    unnamed x23 -> x24, local copies, waits for them, and re-layouts: 3.6 us -> 6.67 us
  transfers between devices with their start and end apart: 20 -> 20, of which waited for: 10 -> 10; matrix products, arithmetic and copies ran while one was open for 7% -> 5% of each run, Pallas kernels for 13% -> 11%
where the time goes in v13:
time: 185 us; the launch traced here: 183 us
  waiting for transfers between devices  52.9 us (29%)
  starting transfers between devices  33.9 us (18%)
  blocking collectives  31 us (17%)
  Pallas kernels  25.8 us (14%)
  between operations  20.1 us (11%)
  local copies, waits for them, and re-layouts  16.8 us (9%)
  other arithmetic  2.85 us (2%)
    all_to_all x1, blocking collectives, local(): lax.all_to_all(chip_sums, 'dp', 0, 0, axis_index_groups=groups, tiled=True)  31 us
    ppermute x7, waiting for transfers between devices, tensor_move(): return lax.ppermute(value, 'tensor', pairs)  23.8 us
    ppermute x9, waiting for transfers between devices, dp_move(): return lax.ppermute(value, 'dp', pairs)  18.6 us
    pallas_call x2, Pallas kernels, project(): pl.pallas_call(functools.partial(project_kernel, chips), grid=(1,), in_sp...  12.8 us
    all_to_all x2, starting transfers between devices, exchange(): lax.all_to_all(copies, axis, 0, 0, axis_index_groups=groups, tiled=True)  12.4 us
    ppermute x7, starting transfers between devices, tensor_move(): return lax.ppermute(value, 'tensor', pairs)  11.3 us
    all_to_all x2, waiting for transfers between devices, exchange(): lax.all_to_all(copies, axis, 0, 0, axis_index_groups=groups, tiled=True)  10.4 us
    ppermute x9, starting transfers between devices, dp_move(): return lax.ppermute(value, 'dp', pairs)  10.1 us
  transfers between devices with their start and end apart: 20, of which 10 were waited for; matrix products, arithmetic and copies ran while one was open for 5% of the time, Pallas kernels for 11%

profile of v13, /device:TPU:0, one launch (start us, length us, event | category | flops | bytes accessed | tf_op | source)
XLA Modules:
  0.0 183.3 jit_solution(9388828928687018745)
XLA Ops:
  7.2 1.8 slice.26
  12.5 7.8 %all-to-all-start = ((bf16[8,512,128]{2,1,0:T(8,128)(2,1)}), bf16[8,512,128]{2,1,0:T(8,128)(2,1)S(1)}, u32[]{:S(2)}, u32[]{:S(2)}) async-start(bf16[8,512,128]{2,1,0:T(8,128)(2,1)} %broadcast_in_dim.32), calls=%async_computation | async-start | bytes 2097152 | tf_op jit(solution)/shard_map/all_to_all | solution.py:351
  21.3 3.5 %collective-permute-start.5 = (bf16[640,512]{1,0:T(8,128)(2,1)}, bf16[640,512]{1,0:T(8,128)(2,1)}, u32[]{:S(2)}, u32[]{:S(2)}) collective-permute-start(bf16[640,512]{1,0:T(8,128)(2,1)} %slice.25), channel_id=1, source_target_pairs={{0,16},{8,24},{16,0},{24,8},{32,48},{40,56},{48,32},{56,40},{64,80... | collective-permute-start | bytes 1966088 | tf_op jit(solution)/shard_map/ppermute | solution.py:34
  25.0 1.6 collective-permute-start.4
  26.6 2.9 %collective-permute-start.3 = (bf16[512,512]{1,0:T(8,128)(2,1)S(1)}, bf16[512,512]{1,0:T(8,128)(2,1)S(1)}, u32[]{:S(2)}, u32[]{:S(2)}) collective-permute-start(bf16[512,512]{1,0:T(8,128)(2,1)S(1)} %pad_maximum_fusion.1.rest_0_), channel_id=1, source_target_pairs={{0,2},{1,3},{2,0},{3,1},{4,6},{5,7},{6,4},{7,5},{8,10},{9,11},{10,... | collective-permute-start | bytes 1572872 | tf_op jit(solution)/shard_map/ppermute | solution.py:42
  38.1 11.7 %collective-permute-done.5 = bf16[640,512]{1,0:T(8,128)(2,1)} collective-permute-done((bf16[640,512]{1,0:T(8,128)(2,1)}, bf16[640,512]{1,0:T(8,128)(2,1)}, u32[]{:S(2)}, u32[]{:S(2)}) %collective-permute-start.5) | collective-permute-done | bytes 655392 | tf_op jit(solution)/shard_map/ppermute | solution.py:34
  49.8 2.0 %collective-permute-done.3.rest_2_ = bf16[512,512]{1,0:T(8,128)(2,1)S(1)} collective-permute-done((bf16[512,512]{1,0:T(8,128)(2,1)S(1)}, bf16[512,512]{1,0:T(8,128)(2,1)S(1)}, u32[]{:S(2)}, u32[]{:S(2)}) %collective-permute-start.3) | collective-permute-done | bytes 524320 | tf_op jit(solution)/shard_map/ppermute | solution.py:42
  53.7 2.6 %collective-permute-done.7.there_ref.rest_8_ = bf16[4096,128]{1,0:T(8,128)(2,1)S(1)} collective-permute-done((bf16[4096,128]{1,0:T(8,128)(2,1)S(1)}, bf16[4096,128]{1,0:T(8,128)(2,1)S(1)}, u32[]{:S(2)}, u32[]{:S(2)}) %collective-permute-start.7) | collective-permute-done | bytes 1048608 | tf_op jit(solution)/shard_map/ppermute | solution.py:34
  56.3 2.8 %broadcast_in_dim.35 = bf16[4,640,512]{2,1,0:T(8,128)(2,1)} broadcast(bf16[640,512]{1,0:T(8,128)(2,1)} %collective-permute-done.5), dimensions={1,2} | broadcast | bytes 3276800 | tf_op jit(solution)/shard_map/broadcast_in_dim | solution.py:348
  59.1 4.6 %all-to-all-start.1 = ((bf16[4,640,512]{2,1,0:T(8,128)(2,1)}), bf16[4,640,512]{2,1,0:T(8,128)(2,1)}, u32[]{:S(2)}, u32[]{:S(2)}) async-start(bf16[4,640,512]{2,1,0:T(8,128)(2,1)} %broadcast_in_dim.35), calls=%async_computation.1 | async-start | bytes 5242880 | tf_op jit(solution)/shard_map/all_to_all | solution.py:351
  67.3 10.6 %collective-permute-done.6.rest_4_ = bf16[512,512]{1,0:T(8,128)(2,1)} collective-permute-done((bf16[512,512]{1,0:T(8,128)(2,1)S(1)}, bf16[512,512]{1,0:T(8,128)(2,1)}, u32[]{:S(2)}, u32[]{:S(2)}) %collective-permute-start.6) | collective-permute-done | bytes 524320 | tf_op jit(solution)/shard_map/ppermute | solution.py:42
  78.5 2.4 %collective-permute-start.9 = (bf16[512,512]{1,0:T(8,128)(2,1)}, bf16[512,512]{1,0:T(8,128)(2,1)}, u32[]{:S(2)}, u32[]{:S(2)}) collective-permute-start(bf16[512,512]{1,0:T(8,128)(2,1)} %collective-permute-done.6.rest_4_), channel_id=1, source_target_pairs={{0,2},{1,3},{2,0},{3,1},{4,6},{5,7},{6,4},{7,5},{8,10},{9,11},{10,... | collective-permute-start | bytes 1572872 | tf_op jit(solution)/shard_map/ppermute | solution.py:42
  80.9 1.6 collective-permute-start.8
  82.5 3.2 %collective-permute-start.12 = (bf16[384,512]{1,0:T(8,128)(2,1)}, bf16[384,512]{1,0:T(8,128)(2,1)S(1)}, u32[]{:S(2)}, u32[]{:S(2)}) collective-permute-start(bf16[384,512]{1,0:T(8,128)(2,1)} %slice.26), channel_id=1, source_target_pairs={{0,16},{8,24},{16,0},{24,8},{32,48},{40,56},{48,32},{56,40},{64,80... | collective-permute-start | bytes 1179656 | tf_op jit(solution)/shard_map/ppermute | solution.py:34
  85.8 7.3 %forward.1 = (bf16[2816,2048]{1,0:T(8,128)(2,1)}, f32[128,2048]{1,0:T(8,128)}) custom-call(s32[36]{0:T(128)S(1)} %concatenate.14.info, s32[1,256]{1,0:T(1,128)S(1)} %iota_add_fusion.pos_ref, s32[1,256]{1,0:T(1,128)S(1)} %bitcast.31, bf16[256,1024]{1,0:T(8,128)(2,1)} %rest_6_.1, bf16[4096,128]{1,0:T(8,128)(2,1)S(1)} %bitcast.28, ...), custom_call_target="tpu_custom_call" | custom-call | flops 100000000 | bytes 1048576 | tf_op jit(solution)/shard_map/forward/pallas_call | solution.py:141
  93.1 10.6 %collective-permute-done.10.rest_7_ = bf16[512,512]{1,0:T(8,128)(2,1)} collective-permute-done((bf16[512,512]{1,0:T(8,128)(2,1)}, bf16[512,512]{1,0:T(8,128)(2,1)}, u32[]{:S(2)}, u32[]{:S(2)}) %collective-permute-start.10) | collective-permute-done | bytes 524320 | tf_op jit(solution)/shard_map/ppermute | solution.py:42
  104.4 10.4 %all-to-all-done.1.rest_9_ = bf16[4,640,512]{2,1,0:T(8,128)(2,1)} async-done(((bf16[4,640,512]{2,1,0:T(8,128)(2,1)}), bf16[4,640,512]{2,1,0:T(8,128)(2,1)}, u32[]{:S(2)}, u32[]{:S(2)}) %all-to-all-start.1) | async-done | bytes 2621472 | tf_op jit(solution)/shard_map/all_to_all | solution.py:351
  116.9 7.7 %project0.1 = (f32[256,640]{1,0:T(8,128)S(1)}, f32[256,640]{1,0:T(8,128)}) custom-call(s32[8]{0:T(128)S(1)} %stack.70.slots, bf16[512,512]{1,0:T(8,128)(2,1)S(1)} %pad_maximum_fusion.1.rest_0_, bf16[512,512]{1,0:T(8,128)(2,1)S(1)} %copy-done.4, bf16[512,512]{1,0:T(8,128)(2,1)S(1)} %copy-done.1, bf16[512,512]{1,0:T(8,128)(2,1)S(1)} %collective-permute-done.4.rest_3_, ...), custom_call_target="tpu_custom_call" | custom-call | flops 2684354560 | bytes 10485760 | tf_op jit(solution)/shard_map/project0/pallas_call | solution.py:307
  127.6 5.1 %project1.1 = (f32[256,384]{1,0:T(8,128)S(1)}, f32[256,384]{1,0:T(8,128)S(1)}) custom-call(s32[8]{0:T(128)S(1)} %stack.75.slots, bf16[512,512]{1,0:T(8,128)(2,1)S(1)} %pad_maximum_fusion.1.rest_0_, bf16[512,512]{1,0:T(8,128)(2,1)S(1)} %copy-done.5, bf16[512,512]{1,0:T(8,128)(2,1)S(1)} %copy-done.2, bf16[512,512]{1,0:T(8,128)(2,1)S(1)} %collective-permute-done.4.rest_3_, ...), custom_call_target="tpu_custom_call" | custom-call | flops 1610612736 | bytes 10485760 | tf_op jit(solution)/shard_map/project1/pallas_call | solution.py:307
  133.5 1.3 collective-permute-done.14.rest_3_
  134.8 5.7 %backward.1 = (bf16[256,1024]{1,0:T(8,128)(2,1)}, f32[8,256,256]{2,1,0:T(8,128)S(1)}, bf16[8,256,256]{2,1,0:T(8,128)(2,1)S(1)}) custom-call(s32[36]{0:T(128)S(1)} %concatenate.14.info, f32[256,640]{1,0:T(8,128)S(1)} %copy-done.8, f32[256,640]{1,0:T(8,128)} %collective-permute-done.11.rest_1_, f32[256,384]{1,0:T(8,128)S(1)} %get-tuple-element.51.rest_2_, ...), custom_call_target="tpu_custom_call" | custom-call | flops 8000000000 | bytes 10485760 | tf_op jit(solution)/shard_map/backward/pallas_call | solution.py:241
  140.5 1.6 collective-permute-start.15
  142.1 2.3 %collective-permute-done.15 = bf16[8,256,256]{2,1,0:T(8,128)(2,1)S(1)} collective-permute-done((bf16[8,256,256]{2,1,0:T(8,128)(2,1)S(1)}, bf16[8,256,256]{2,1,0:T(8,128)(2,1)S(1)}, u32[]{:S(2)}, u32[]{:S(2)}) %collective-permute-start.15) | collective-permute-done | bytes 1048608 | tf_op jit(solution)/shard_map/ppermute | solution.py:34
  144.7 31.0 %all_to_all.15 = bf16[8,256,256]{2,1,0:T(8,128)(2,1)S(1)} all-to-all(bf16[8,256,256]{2,1,0:T(8,128)(2,1)S(1)} %add_convert_fusion), channel_id=1, replica_groups={{0,16,32,48,64,80,96,112},{8,24,40,56,72,88,104,120},{1,17,33,49,65,81,..., dimensions={0} | all-to-all | bytes 2097152 | tf_op jit(solution)/shard_map/all_to_all | solution.py:412
  (71 shorter events, 21.0 us)
Async XLA Ops:
  7.2 57.6 %all-gather.5.cloned.1.call-start = ((), (), s32[]{:S(2)}) async-start(), calls=%async_computation.3 | async-start | bytes 1966080 | tf_op jit(solution)/shard_map/all_gather | solution.py:370
  10.0 1.3 collective-permute-start
  10.1 14.8 %collective-permute-start.1 = (bf16[256,512]{1,0:T(8,128)(2,1)S(1)}, bf16[256,512]{1,0:T(8,128)(2,1)S(1)}, u32[]{:S(2)}, u32[]{:S(2)}) collective-permute-start(bf16[256,512]{1,0:T(8,128)(2,1)S(1)} %get-tuple-element.61), channel_id=1, source_target_pairs={{0,8},{8,0},{16,24},{24,16},{32,40},{40,32},{48,56},{56,48},{64,72... | collective-permute-start | bytes 786440 | tf_op jit(solution)/shard_map/ppermute | solution.py:34
  11.3 9.0 %copy-start.9 = (bf16[1024,512]{1,0:T(8,128)(2,1)S(1)}, bf16[1024,512]{1,0:T(8,128)(2,1)}, u32[]{:S(2)}) copy-start(bf16[1024,512]{1,0:T(8,128)(2,1)} %param.10) | copy-start | bytes 3145732
  12.4 12.3 %copy-start.11 = (s32[8]{0:T(128)S(1)}, s32[8]{0:T(128)}, u32[]{:S(2)}) copy-start(s32[8]{0:T(128)} %param.11) | copy-start | bytes 100
  12.5 41.1 %all-to-all-start = ((bf16[8,512,128]{2,1,0:T(8,128)(2,1)}), bf16[8,512,128]{2,1,0:T(8,128)(2,1)S(1)}, u32[]{:S(2)}, u32[]{:S(2)}) async-start(bf16[8,512,128]{2,1,0:T(8,128)(2,1)} %broadcast_in_dim.32), calls=%async_computation | async-start | bytes 2097152 | tf_op jit(solution)/shard_map/all_to_all | solution.py:351
  20.3 94.5 %all-gather.7.cloned.1.call-start = ((), (), s32[]{:S(2)}) async-start(), calls=%async_computation.4 | async-start | bytes 3276800 | tf_op jit(solution)/shard_map/all_gather | solution.py:370
  21.3 28.6 %collective-permute-start.5 = (bf16[640,512]{1,0:T(8,128)(2,1)}, bf16[640,512]{1,0:T(8,128)(2,1)}, u32[]{:S(2)}, u32[]{:S(2)}) collective-permute-start(bf16[640,512]{1,0:T(8,128)(2,1)} %slice.25), channel_id=1, source_target_pairs={{0,16},{8,24},{16,0},{24,8},{32,48},{40,56},{48,32},{56,40},{64,80... | collective-permute-start | bytes 1966088 | tf_op jit(solution)/shard_map/ppermute | solution.py:34
  25.0 24.9 %collective-permute-start.4 = (bf16[512,512]{1,0:T(8,128)(2,1)S(1)}, bf16[512,512]{1,0:T(8,128)(2,1)S(1)}, u32[]{:S(2)}, u32[]{:S(2)}) collective-permute-start(bf16[512,512]{1,0:T(8,128)(2,1)S(1)} %pad_maximum_fusion.1.rest_0_), channel_id=1, source_target_pairs={{0,1},{1,2},{2,3},{3,0},{4,5},{5,6},{6,7},{7,4},{8,9},{9,10},{10,1... | collective-permute-start | bytes 1572872 | tf_op jit(solution)/shard_map/ppermute | solution.py:42
  26.6 25.3 %collective-permute-start.3 = (bf16[512,512]{1,0:T(8,128)(2,1)S(1)}, bf16[512,512]{1,0:T(8,128)(2,1)S(1)}, u32[]{:S(2)}, u32[]{:S(2)}) collective-permute-start(bf16[512,512]{1,0:T(8,128)(2,1)S(1)} %pad_maximum_fusion.1.rest_0_), channel_id=1, source_target_pairs={{0,2},{1,3},{2,0},{3,1},{4,6},{5,7},{6,4},{7,5},{8,10},{9,11},{10,... | collective-permute-start | bytes 1572872 | tf_op jit(solution)/shard_map/ppermute | solution.py:42
  29.5 23.2 %collective-permute-start.2 = (bf16[512,512]{1,0:T(8,128)(2,1)S(1)}, bf16[512,512]{1,0:T(8,128)(2,1)S(1)}, u32[]{:S(2)}, u32[]{:S(2)}) collective-permute-start(bf16[512,512]{1,0:T(8,128)(2,1)S(1)} %pad_maximum_fusion.1.rest_0_), channel_id=1, source_target_pairs={{0,3},{1,0},{2,1},{3,2},{4,7},{5,4},{6,5},{7,6},{8,11},{9,8},{10,9... | collective-permute-start | bytes 1572872 | tf_op jit(solution)/shard_map/ppermute | solution.py:42
  53.6 2.7 %collective-permute-start.7 = (bf16[4096,128]{1,0:T(8,128)(2,1)S(1)}, bf16[4096,128]{1,0:T(8,128)(2,1)S(1)}, u32[]{:S(2)}, u32[]{:S(2)}) collective-permute-start(bf16[4096,128]{1,0:T(8,128)(2,1)S(1)} %bitcast.27), channel_id=1, source_target_pairs={{0,8},{8,0},{16,24},{24,16},{32,40},{40,32},{48,56},{56,48},{64,72... | collective-permute-start | bytes 3145736 | tf_op jit(solution)/shard_map/ppermute | solution.py:34
  59.1 55.7 %all-to-all-start.1 = ((bf16[4,640,512]{2,1,0:T(8,128)(2,1)}), bf16[4,640,512]{2,1,0:T(8,128)(2,1)}, u32[]{:S(2)}, u32[]{:S(2)}) async-start(bf16[4,640,512]{2,1,0:T(8,128)(2,1)} %broadcast_in_dim.35), calls=%async_computation.1 | async-start | bytes 5242880 | tf_op jit(solution)/shard_map/all_to_all | solution.py:351
  63.7 14.1 %collective-permute-start.6 = (bf16[512,512]{1,0:T(8,128)(2,1)S(1)}, bf16[512,512]{1,0:T(8,128)(2,1)}, u32[]{:S(2)}, u32[]{:S(2)}) collective-permute-start(bf16[512,512]{1,0:T(8,128)(2,1)S(1)} %pad_maximum_fusion.1.rest_0_), channel_id=1, source_target_pairs={{0,4},{1,5},{2,6},{3,7},{4,0},{5,1},{6,2},{7,3},{8,12},{9,13},{10,... | collective-permute-start | bytes 1572872 | tf_op jit(solution)/shard_map/ppermute | solution.py:42
  77.8 47.7 %collective-permute-start.13 = (bf16[3,384,512]{2,1,0:T(8,128)(2,1)}, bf16[3,384,512]{2,1,0:T(8,128)(2,1)}, u32[]{:S(2)}, u32[]{:S(2)}) collective-permute-start(bf16[3,384,512]{2,1,0:T(8,128)(2,1)} %pad_maximum_fusion), channel_id=1, source_target_pairs={{0,16},{8,24},{16,0},{24,8},{32,48},{40,56},{48,32},{56,40},{64,80... | collective-permute-start | bytes 3538952 | tf_op jit(solution)/shard_map/ppermute | solution.py:34
  78.1 25.6 %collective-permute-start.10 = (bf16[512,512]{1,0:T(8,128)(2,1)}, bf16[512,512]{1,0:T(8,128)(2,1)}, u32[]{:S(2)}, u32[]{:S(2)}) collective-permute-start(bf16[512,512]{1,0:T(8,128)(2,1)} %collective-permute-done.6.rest_4_), channel_id=1, source_target_pairs={{0,1},{1,2},{2,3},{3,0},{4,5},{5,6},{6,7},{7,4},{8,9},{9,10},{10,1... | collective-permute-start | bytes 1572872 | tf_op jit(solution)/shard_map/ppermute | solution.py:42
  78.5 25.3 %collective-permute-start.9 = (bf16[512,512]{1,0:T(8,128)(2,1)}, bf16[512,512]{1,0:T(8,128)(2,1)}, u32[]{:S(2)}, u32[]{:S(2)}) collective-permute-start(bf16[512,512]{1,0:T(8,128)(2,1)} %collective-permute-done.6.rest_4_), channel_id=1, source_target_pairs={{0,2},{1,3},{2,0},{3,1},{4,6},{5,7},{6,4},{7,5},{8,10},{9,11},{10,... | collective-permute-start | bytes 1572872 | tf_op jit(solution)/shard_map/ppermute | solution.py:42
  80.9 23.5 %collective-permute-start.8 = (bf16[512,512]{1,0:T(8,128)(2,1)}, bf16[512,512]{1,0:T(8,128)(2,1)}, u32[]{:S(2)}, u32[]{:S(2)}) collective-permute-start(bf16[512,512]{1,0:T(8,128)(2,1)} %collective-permute-done.6.rest_4_), channel_id=1, source_target_pairs={{0,3},{1,0},{2,1},{3,2},{4,7},{5,4},{6,5},{7,6},{8,11},{9,8},{10,9... | collective-permute-start | bytes 1572872 | tf_op jit(solution)/shard_map/ppermute | solution.py:42
  82.5 43.0 %collective-permute-start.12 = (bf16[384,512]{1,0:T(8,128)(2,1)}, bf16[384,512]{1,0:T(8,128)(2,1)S(1)}, u32[]{:S(2)}, u32[]{:S(2)}) collective-permute-start(bf16[384,512]{1,0:T(8,128)(2,1)} %slice.26), channel_id=1, source_target_pairs={{0,16},{8,24},{16,0},{24,8},{32,48},{40,56},{48,32},{56,40},{64,80... | collective-permute-start | bytes 1179656 | tf_op jit(solution)/shard_map/ppermute | solution.py:34
  125.4 9.4 %collective-permute-start.11 = (f32[256,640]{1,0:T(8,128)}, f32[256,640]{1,0:T(8,128)}, u32[]{:S(2)}, u32[]{:S(2)}) collective-permute-start(f32[256,640]{1,0:T(8,128)} %get-tuple-element.48), channel_id=1, source_target_pairs={{0,8},{8,0},{16,24},{24,16},{32,40},{40,32},{48,56},{56,48},{64,72... | collective-permute-start | bytes 1966088 | tf_op jit(solution)/shard_map/ppermute | solution.py:34
  127.6 7.2 %copy-start.6 = (f32[128,2048]{1,0:T(8,128)S(1)}, f32[128,2048]{1,0:T(8,128)}, u32[]{:S(2)}) copy-start(f32[128,2048]{1,0:T(8,128)} %get-tuple-element.38.rest_5_) | copy-start | bytes 3145732
  127.6 7.2 %copy-start.8 = (f32[256,640]{1,0:T(8,128)S(1)}, f32[256,640]{1,0:T(8,128)}, u32[]{:S(2)}) copy-start(f32[256,640]{1,0:T(8,128)} %copy-done.7) | copy-start | bytes 1966084
  132.7 2.1 %collective-permute-start.14 = (f32[256,384]{1,0:T(8,128)S(1)}, f32[256,384]{1,0:T(8,128)S(1)}, u32[]{:S(2)}, u32[]{:S(2)}) collective-permute-start(f32[256,384]{1,0:T(8,128)S(1)} %get-tuple-element.52), channel_id=1, source_target_pairs={{0,8},{8,0},{16,24},{24,16},{32,40},{40,32},{48,56},{56,48},{64,72... | collective-permute-start | bytes 1179656 | tf_op jit(solution)/shard_map/ppermute | solution.py:34
  140.5 3.9 %collective-permute-start.15 = (bf16[8,256,256]{2,1,0:T(8,128)(2,1)S(1)}, bf16[8,256,256]{2,1,0:T(8,128)(2,1)S(1)}, u32[]{:S(2)}, u32[]{:S(2)}) collective-permute-start(bf16[8,256,256]{2,1,0:T(8,128)(2,1)S(1)} %get-tuple-element.56), channel_id=1, source_target_pairs={{0,8},{8,0},{16,24},{24,16},{32,40},{40,32},{48,56},{56,48},{64,72... | collective-permute-start | bytes 3145736 | tf_op jit(solution)/shard_map/ppermute | solution.py:34
  (8 other events, 9.6 us)
Sparse Core Ops, SparseCore 0:
  9.7 38.7 all-gather.4
  53.7 50.9 all-gather.6

commit v14 on v13

--- a/solution.py
+++ b/solution.py
@@ -12,7 +12,7 @@
 KEY_BLOCK = 256
 MOST = 2560
 CHUNKS = 2
-SPLIT = 5 * HEAD_WIDTH
+SPLIT = 4 * HEAD_WIDTH
 PAIR = 2
 MASKED = -1e30
 SCALE = 1.0 / math.sqrt(HEAD_WIDTH)
@@ -337,7 +337,7 @@
     last = query_pos[-1] // KEY_BLOCK
     clear = (query_start[-1] + KEY_BLOCK - 1) // KEY_BLOCK
     block = jnp.arange(16, dtype=jnp.int32)
-    place = block // 2 * 2
+    place = block // 4 * 4 + jnp.where(block // 2 % 2 == z, 0, 2)
     here = place + jnp.where(block % 2 == core, 0, 1)
     there = place + jnp.where(block % 2 == core, 1, 0)
     scalars = jnp.stack([first, last - first + 1, clear, core])
@@ -353,10 +353,12 @@
     def spread(block, axis, groups):
         return exchange(copy(block, groups), axis, groups)
 
-    groups = [[2 * i + c for i in range(8)] for c in range(2)]
+    groups_x = [[x_ * 4 + zc for x_ in range(4)] for zc in range(4)]
     kept = jnp.where(core == 0, keys, values)
     got = dp_move(jnp.where(core == 0, values, keys), 0, 0, 1)
-    ring = spread(jnp.concatenate([kept, got], axis=0), "dp", groups).reshape(-1, HEAD_WIDTH)
+    chip = jnp.concatenate([kept, got], axis=0)
+    chip_pair = jnp.concatenate([chip, dp_move(chip, 0, 1, 0)], axis=0)
+    ring = spread(chip_pair, "dp", groups_x).reshape(-1, HEAD_WIDTH)
 
     depth = out_weight.shape[1]
     mine = lax.dynamic_slice_in_dim(grad_out, core * depth, depth, 1)
@@ -364,19 +366,18 @@
     chip_grad = jnp.concatenate([mine, dp_move(other, 0, 0, 1)], axis=0)
     all_grad = [chip_grad] + [tensor_move(chip_grad, 0, step) for step in (-1, -2, 1)]
 
-    groups_x = [[x_ * 4 + zc for x_ in range(4)] for zc in range(4)]
-
     def gather_x(block):
         return lax.all_gather(block, "dp", axis=0, axis_index_groups=groups_x)
 
     own = [out_weight[:SPLIT], out_weight[SPLIT:]]
     plane1 = gather_x(own[1])
-    pair0 = dp_move(own[0], 0, 1, 0)
-    ring, own, all_grad, pair0, chip_grad, info, query_pos, query_start = lax.optimization_barrier(
-        (ring, own, all_grad, pair0, chip_grad, info, query_pos, query_start)
+    pair0 = dp_move(after(own[0], chip_pair), 0, 1, 0)
+    grad_pair = tensor_move(chip_grad, 1, 0)
+    ring, own, all_grad, pair0, grad_pair, info, query_pos, query_start = lax.optimization_barrier(
+        (ring, own, all_grad, pair0, grad_pair, info, query_pos, query_start)
     )
     plane0 = gather_x(own[0])
-    grad_pair = tensor_move(chip_grad, 1, 0)
+    all_grad += [grad_pair] + [tensor_move(grad_pair, 0, step) for step in (-1, -2, 1)]
     pair1 = dp_move(own[1], 0, 1, 0)
     swapped = dp_move(ring, 0, 0, 1)
     swapped, copies = lax.optimization_barrier((swapped, copy(pair0, groups_x)))
@@ -384,9 +385,8 @@
     rest = jnp.concatenate(
         [lax.dynamic_slice_in_dim(plane1, (x + i) % 4, 1, 0) for i in range(1, 4)], axis=0
     )
-    rest, grad_pair, later = lax.optimization_barrier((rest, grad_pair, queries))
+    rest, later = lax.optimization_barrier((rest, queries))
     rest = dp_move(rest, 0, 1, 0)
-    all_grad += [grad_pair] + [tensor_move(grad_pair, 0, step) for step in (-1, -2, 1)]
     probs, outs = forward(info, query_pos, query_start, later, ring, swapped)
 
     t = lax.axis_index("tensor")
@@ -408,6 +408,7 @@
         terms += [mine, dp_move(other, 0, 0, 1)]
     grad_queries, own_sums, other_sums = backward(info, terms, probs, outs, queries, ring, swapped)
 
+    groups = [[2 * i + c for i in range(8)] for c in range(2)]
     chip_sums = (own_sums + dp_move(other_sums, 0, 0, 1).astype(F32)).astype(BF16)
     terms = lax.all_to_all(chip_sums, "dp", 0, 0, axis_index_groups=groups, tiled=True)
     done = jnp.sum(terms.astype(F32), axis=0).astype(BF16)

time: 185 us -> 175 us (0.946)
  local copies, waits for them, and re-layouts: 16.8 us -> 9.7 us
    unnamed x24 -> x10, local copies, waits for them, and re-layouts: 6.67 us -> 0.02 us
    ppermute x9 -> x10, waiting for transfers between devices: 18.6 us -> 14.7 us  [dp_move(): return lax.ppermute(value, 'dp', pairs)]
    all_to_all x2, starting transfers between devices: 12.4 us -> 8.81 us  [exchange(): lax.all_to_all(copies, axis, 0, 0, axis_index_groups=groups, tiled=True)]
    ppermute x9 -> x10, starting transfers between devices: 10.1 us -> 12.7 us  [dp_move(): return lax.ppermute(value, 'dp', pairs)]
    all_to_all x2, waiting for transfers between devices: 10.4 us -> 12.9 us  [exchange(): lax.all_to_all(copies, axis, 0, 0, axis_index_groups=groups, tiled=True)]
  transfers between devices with their start and end apart: 20 -> 21, of which waited for: 10 -> 11; matrix products, arithmetic and copies ran while one was open for 5% -> 5% of each run, Pallas kernels for 11% -> 11%
where the time goes in v14:
time: 175 us
  waiting for transfers between devices  51.5 us (29%)
  starting transfers between devices  33.8 us (19%)
  blocking collectives  32.8 us (19%)
  Pallas kernels  24.4 us (14%)
  between operations  20.3 us (12%)
  local copies, waits for them, and re-layouts  9.7 us (6%)
  other arithmetic  2.21 us (1%)
    all_to_all x1, blocking collectives, local(): lax.all_to_all(chip_sums, 'dp', 0, 0, axis_index_groups=groups, tiled=True)  32.8 us
    ppermute x7, waiting for transfers between devices, tensor_move(): return lax.ppermute(value, 'tensor', pairs)  23.8 us
    ppermute x10, waiting for transfers between devices, dp_move(): return lax.ppermute(value, 'dp', pairs)  14.7 us
    all_to_all x2, waiting for transfers between devices, exchange(): lax.all_to_all(copies, axis, 0, 0, axis_index_groups=groups, tiled=True)  12.9 us
    ppermute x10, starting transfers between devices, dp_move(): return lax.ppermute(value, 'dp', pairs)  12.7 us
    ppermute x7, starting transfers between devices, tensor_move(): return lax.ppermute(value, 'tensor', pairs)  12.2 us
    pallas_call x2, Pallas kernels, project(): pl.pallas_call(functools.partial(project_kernel, chips), grid=(1,), in_sp...  10.9 us
    all_to_all x2, starting transfers between devices, exchange(): lax.all_to_all(copies, axis, 0, 0, axis_index_groups=groups, tiled=True)  8.81 us
  transfers between devices with their start and end apart: 21, of which 11 were waited for; matrix products, arithmetic and copies ran while one was open for 5% of the time, Pallas kernels for 11%

profile of v14, /device:TPU:0, one launch (start us, length us, event | category | flops | bytes accessed | tf_op | source)
XLA Modules:
  0.0 174.7 jit_solution(7499420137477428841)
XLA Ops:
  7.3 2.3 %fusion.5 = (bf16[512,512]{1,0:T(8,128)(2,1)}, bf16[512,512]{1,0:T(8,128)(2,1)}) fusion(bf16[1024,512]{1,0:T(8,128)(2,1)} %param.10), kind=kLoop, calls=%fused_computation.35 | loop fusion | bytes 2097152 | tf_op jit(solution)/shard_map/slice | solution.py:372
  11.0 4.0 %collective-permute-start.1 = (bf16[512,128]{1,0:T(8,128)(2,1)S(1)}, bf16[512,128]{1,0:T(8,128)(2,1)S(1)}, u32[]{:S(2)}, u32[]{:S(2)}) collective-permute-start(bf16[512,128]{1,0:T(8,128)(2,1)S(1)} %pad_maximum_fusion.3), channel_id=1, source_target_pairs={{0,16},{8,24},{16,0},{24,8},{32,48},{40,56},{48,32},{56,40},{64,80... | collective-permute-start | bytes 393224 | tf_op jit(solution)/shard_map/ppermute | solution.py:34
  15.3 3.5 %collective-permute-done.1 = bf16[512,128]{1,0:T(8,128)(2,1)S(1)} collective-permute-done((bf16[512,128]{1,0:T(8,128)(2,1)S(1)}, bf16[512,128]{1,0:T(8,128)(2,1)S(1)}, u32[]{:S(2)}, u32[]{:S(2)}) %collective-permute-start.1) | collective-permute-done | bytes 131104 | tf_op jit(solution)/shard_map/ppermute | solution.py:34
  20.0 4.3 %all-to-all-start = ((bf16[4,1024,128]{2,1,0:T(8,128)(2,1)}), bf16[4,1024,128]{2,1,0:T(8,128)(2,1)S(1)}, u32[]{:S(2)}, u32[]{:S(2)}) async-start(bf16[4,1024,128]{2,1,0:T(8,128)(2,1)} %broadcast_in_dim.34), calls=%async_computation | async-start | bytes 2097152 | tf_op jit(solution)/shard_map/all_to_all | solution.py:351
  24.3 3.2 %collective-permute-start.6 = (bf16[512,512]{1,0:T(8,128)(2,1)}, bf16[512,512]{1,0:T(8,128)(2,1)}, u32[]{:S(2)}, u32[]{:S(2)}) collective-permute-start(bf16[512,512]{1,0:T(8,128)(2,1)} %get-tuple-element.45), channel_id=1, source_target_pairs={{0,16},{8,24},{16,0},{24,8},{32,48},{40,56},{48,32},{56,40},{64,80... | collective-permute-start | bytes 1572872 | tf_op jit(solution)/shard_map/ppermute | solution.py:34
  30.2 2.9 %collective-permute-start.4 = (bf16[512,512]{1,0:T(8,128)(2,1)S(1)}, bf16[512,512]{1,0:T(8,128)(2,1)S(1)}, u32[]{:S(2)}, u32[]{:S(2)}) collective-permute-start(bf16[512,512]{1,0:T(8,128)(2,1)S(1)} %pad_maximum_fusion.1.rest_0_), channel_id=1, source_target_pairs={{0,2},{1,3},{2,0},{3,1},{4,6},{5,7},{6,4},{7,5},{8,10},{9,11},{10,... | collective-permute-start | bytes 1572872 | tf_op jit(solution)/shard_map/ppermute | solution.py:42
  41.9 8.9 %collective-permute-done.7.rest_4_ = bf16[512,512]{1,0:T(8,128)(2,1)S(1)} collective-permute-done((bf16[512,512]{1,0:T(8,128)(2,1)S(1)}, bf16[512,512]{1,0:T(8,128)(2,1)S(1)}, u32[]{:S(2)}, u32[]{:S(2)}) %collective-permute-start.7) | collective-permute-done | bytes 524320 | tf_op jit(solution)/shard_map/ppermute | solution.py:42
  50.8 3.8 %collective-permute-done.4.rest_2_ = bf16[512,512]{1,0:T(8,128)(2,1)S(1)} collective-permute-done((bf16[512,512]{1,0:T(8,128)(2,1)S(1)}, bf16[512,512]{1,0:T(8,128)(2,1)S(1)}, u32[]{:S(2)}, u32[]{:S(2)}) %collective-permute-start.4) | collective-permute-done | bytes 524320 | tf_op jit(solution)/shard_map/ppermute | solution.py:42
  54.9 2.7 %collective-permute-done.8.there_ref.rest_8_ = bf16[4096,128]{1,0:T(8,128)(2,1)} collective-permute-done((bf16[4096,128]{1,0:T(8,128)(2,1)S(1)}, bf16[4096,128]{1,0:T(8,128)(2,1)}, u32[]{:S(2)}, u32[]{:S(2)}) %collective-permute-start.8) | collective-permute-done | bytes 1048608 | tf_op jit(solution)/shard_map/ppermute | solution.py:34
  57.6 2.5 %broadcast_in_dim.37 = bf16[4,512,512]{2,1,0:T(8,128)(2,1)} broadcast(bf16[512,512]{1,0:T(8,128)(2,1)} %collective-permute-done.6), dimensions={1,2} | broadcast | bytes 2621440 | tf_op jit(solution)/shard_map/broadcast_in_dim | solution.py:348
  60.1 4.5 %all-to-all-start.1 = ((bf16[4,512,512]{2,1,0:T(8,128)(2,1)}), bf16[4,512,512]{2,1,0:T(8,128)(2,1)}, u32[]{:S(2)}, u32[]{:S(2)}) async-start(bf16[4,512,512]{2,1,0:T(8,128)(2,1)} %broadcast_in_dim.37), calls=%async_computation.1 | async-start | bytes 4194304 | tf_op jit(solution)/shard_map/all_to_all | solution.py:351
  69.9 2.4 %collective-permute-start.10 = (bf16[512,512]{1,0:T(8,128)(2,1)S(1)}, bf16[512,512]{1,0:T(8,128)(2,1)}, u32[]{:S(2)}, u32[]{:S(2)}) collective-permute-start(bf16[512,512]{1,0:T(8,128)(2,1)S(1)} %collective-permute-done.7.rest_4_), channel_id=1, source_target_pairs={{0,2},{1,3},{2,0},{3,1},{4,6},{5,7},{6,4},{7,5},{8,10},{9,11},{10,... | collective-permute-start | bytes 1572872 | tf_op jit(solution)/shard_map/ppermute | solution.py:42
  72.3 1.7 collective-permute-start.9
  73.9 2.5 %collective-permute-start.13 = (bf16[512,512]{1,0:T(8,128)(2,1)}, bf16[512,512]{1,0:T(8,128)(2,1)}, u32[]{:S(2)}, u32[]{:S(2)}) collective-permute-start(bf16[512,512]{1,0:T(8,128)(2,1)} %get-tuple-element.49), channel_id=1, source_target_pairs={{0,16},{8,24},{16,0},{24,8},{32,48},{40,56},{48,32},{56,40},{64,80... | collective-permute-start | bytes 1572872 | tf_op jit(solution)/shard_map/ppermute | solution.py:34
  76.6 7.8 %forward.1 = (bf16[2816,2048]{1,0:T(8,128)(2,1)}, f32[128,2048]{1,0:T(8,128)}) custom-call(s32[36]{0:T(128)S(1)} %concatenate.19.info, s32[1,256]{1,0:T(1,128)S(1)} %iota_add_fusion.pos_ref, s32[1,256]{1,0:T(1,128)S(1)} %bitcast.30, bf16[256,1024]{1,0:T(8,128)(2,1)} %rest_6_.1, bf16[4096,128]{1,0:T(8,128)(2,1)S(1)} %bitcast.28, ...), custom_call_target="tpu_custom_call" | custom-call | flops 100000000 | bytes 1048576 | tf_op jit(solution)/shard_map/forward/pallas_call | solution.py:141
  84.4 10.9 %collective-permute-done.10.rest_6_ = bf16[512,512]{1,0:T(8,128)(2,1)} collective-permute-done((bf16[512,512]{1,0:T(8,128)(2,1)S(1)}, bf16[512,512]{1,0:T(8,128)(2,1)}, u32[]{:S(2)}, u32[]{:S(2)}) %collective-permute-start.10) | collective-permute-done | bytes 524320 | tf_op jit(solution)/shard_map/ppermute | solution.py:42
  95.5 12.9 %all-to-all-done.1.rest_9_ = bf16[4,512,512]{2,1,0:T(8,128)(2,1)} async-done(((bf16[4,512,512]{2,1,0:T(8,128)(2,1)}), bf16[4,512,512]{2,1,0:T(8,128)(2,1)}, u32[]{:S(2)}, u32[]{:S(2)}) %all-to-all-start.1) | async-done | bytes 2097184 | tf_op jit(solution)/shard_map/all_to_all | solution.py:351
  108.4 5.5 %project0.1 = (f32[256,512]{1,0:T(8,128)S(1)}, f32[256,512]{1,0:T(8,128)S(1)}) custom-call(s32[8]{0:T(128)S(1)} %stack.70.slots, bf16[512,512]{1,0:T(8,128)(2,1)S(1)} %pad_maximum_fusion.1.rest_0_, bf16[512,512]{1,0:T(8,128)(2,1)} %collective-permute-done.3.rest_1_, bf16[512,512]{1,0:T(8,128)(2,1)S(1)} %collective-permute-done.4.rest_2_, ...), custom_call_target="tpu_custom_call" | custom-call | flops 2147483648 | bytes 10485760 | tf_op jit(solution)/shard_map/project0/pallas_call | solution.py:307
  114.0 3.1 %collective-permute-done.13 = bf16[512,512]{1,0:T(8,128)(2,1)} collective-permute-done((bf16[512,512]{1,0:T(8,128)(2,1)}, bf16[512,512]{1,0:T(8,128)(2,1)}, u32[]{:S(2)}, u32[]{:S(2)}) %collective-permute-start.13) | collective-permute-done | bytes 524320 | tf_op jit(solution)/shard_map/ppermute | solution.py:34
  117.0 5.5 %project1.1 = (f32[256,512]{1,0:T(8,128)S(1)}, f32[256,512]{1,0:T(8,128)S(1)}) custom-call(s32[8]{0:T(128)S(1)} %stack.75.slots, bf16[512,512]{1,0:T(8,128)(2,1)S(1)} %pad_maximum_fusion.1.rest_0_, bf16[512,512]{1,0:T(8,128)(2,1)} %collective-permute-done.3.rest_1_, bf16[512,512]{1,0:T(8,128)(2,1)S(1)} %collective-permute-done.4.rest_2_, ...), custom_call_target="tpu_custom_call" | custom-call | flops 2147483648 | bytes 10485760 | tf_op jit(solution)/shard_map/project1/pallas_call | solution.py:307
  122.8 1.9 %collective-permute-done.15.rest_3_ = f32[256,512]{1,0:T(8,128)S(1)} collective-permute-done((f32[256,512]{1,0:T(8,128)S(1)}, f32[256,512]{1,0:T(8,128)S(1)}, u32[]{:S(2)}, u32[]{:S(2)}) %collective-permute-start.15) | collective-permute-done | bytes 524320 | tf_op jit(solution)/shard_map/ppermute | solution.py:34
  124.7 5.6 %backward.1 = (bf16[256,1024]{1,0:T(8,128)(2,1)}, f32[8,256,256]{2,1,0:T(8,128)S(1)}, bf16[8,256,256]{2,1,0:T(8,128)(2,1)S(1)}) custom-call(s32[36]{0:T(128)S(1)} %concatenate.19.info, f32[256,512]{1,0:T(8,128)S(1)} %get-tuple-element.47.rest_0_, f32[256,512]{1,0:T(8,128)S(1)} %collective-permute-done.12.rest_1_, f32[256,512]{1,0:T(8,128)S(1)} %get-tuple-element.51.rest_2_, ...), custom_call_target="tpu_custom_call" | custom-call | flops 8000000000 | bytes 10485760 | tf_op jit(solution)/shard_map/backward/pallas_call | solution.py:241
  131.7 2.3 %collective-permute-done.16 = bf16[8,256,256]{2,1,0:T(8,128)(2,1)S(1)} collective-permute-done((bf16[8,256,256]{2,1,0:T(8,128)(2,1)S(1)}, bf16[8,256,256]{2,1,0:T(8,128)(2,1)S(1)}, u32[]{:S(2)}, u32[]{:S(2)}) %collective-permute-start.16) | collective-permute-done | bytes 1048608 | tf_op jit(solution)/shard_map/ppermute | solution.py:34
  134.3 32.8 %all_to_all.15 = bf16[8,256,256]{2,1,0:T(8,128)(2,1)S(1)} all-to-all(bf16[8,256,256]{2,1,0:T(8,128)(2,1)S(1)} %add_convert_fusion), channel_id=1, replica_groups={{0,16,32,48,64,80,96,112},{8,24,40,56,72,88,104,120},{1,17,33,49,65,81,..., dimensions={0} | all-to-all | bytes 2097152 | tf_op jit(solution)/shard_map/all_to_all | solution.py:413
  (59 shorter events, 16.9 us)
Async XLA Ops:
  7.2 7.8 %copy-start.1 = (bf16[256,1024]{1,0:T(8,128)(2,1)S(1)}, bf16[256,1024]{1,0:T(8,128)(2,1)}, u32[]{:S(2)}) copy-start(bf16[256,1024]{1,0:T(8,128)(2,1)} %param.9) | copy-start | bytes 1572868
  7.2 8.0 %copy-start.4 = (s32[8]{0:T(128)S(1)}, s32[8]{0:T(128)}, u32[]{:S(2)}) copy-start(s32[8]{0:T(128)} %param.11) | copy-start | bytes 100
  7.2 57.4 %all-gather.5.cloned.1.call-start = ((), (), s32[]{:S(2)}) async-start(), calls=%async_computation.3 | async-start | bytes 2621440 | tf_op jit(solution)/shard_map/all_gather | solution.py:370
  9.6 1.3 collective-permute-start
  11.0 7.9 %collective-permute-start.1 = (bf16[512,128]{1,0:T(8,128)(2,1)S(1)}, bf16[512,128]{1,0:T(8,128)(2,1)S(1)}, u32[]{:S(2)}, u32[]{:S(2)}) collective-permute-start(bf16[512,128]{1,0:T(8,128)(2,1)S(1)} %pad_maximum_fusion.3), channel_id=1, source_target_pairs={{0,16},{8,24},{16,0},{24,8},{32,48},{40,56},{48,32},{56,40},{64,80... | collective-permute-start | bytes 393224 | tf_op jit(solution)/shard_map/ppermute | solution.py:34
  15.1 12.5 %collective-permute-start.2 = (bf16[256,512]{1,0:T(8,128)(2,1)S(1)}, bf16[256,512]{1,0:T(8,128)(2,1)S(1)}, u32[]{:S(2)}, u32[]{:S(2)}) collective-permute-start(bf16[256,512]{1,0:T(8,128)(2,1)S(1)} %get-tuple-element.63), channel_id=1, source_target_pairs={{0,8},{8,0},{16,24},{24,16},{32,40},{40,32},{48,56},{56,48},{64,72... | collective-permute-start | bytes 786440 | tf_op jit(solution)/shard_map/ppermute | solution.py:34
  20.0 34.7 %all-to-all-start = ((bf16[4,1024,128]{2,1,0:T(8,128)(2,1)}), bf16[4,1024,128]{2,1,0:T(8,128)(2,1)S(1)}, u32[]{:S(2)}, u32[]{:S(2)}) async-start(bf16[4,1024,128]{2,1,0:T(8,128)(2,1)} %broadcast_in_dim.34), calls=%async_computation | async-start | bytes 2097152 | tf_op jit(solution)/shard_map/all_to_all | solution.py:351
  24.3 84.1 %all-gather.7.cloned.1.call-start = ((), (), s32[]{:S(2)}) async-start(), calls=%async_computation.4 | async-start | bytes 2621440 | tf_op jit(solution)/shard_map/all_gather | solution.py:370
  24.3 17.6 %collective-permute-start.6 = (bf16[512,512]{1,0:T(8,128)(2,1)}, bf16[512,512]{1,0:T(8,128)(2,1)}, u32[]{:S(2)}, u32[]{:S(2)}) collective-permute-start(bf16[512,512]{1,0:T(8,128)(2,1)} %get-tuple-element.45), channel_id=1, source_target_pairs={{0,16},{8,24},{16,0},{24,8},{32,48},{40,56},{48,32},{56,40},{64,80... | collective-permute-start | bytes 1572872 | tf_op jit(solution)/shard_map/ppermute | solution.py:34
  27.6 23.3 %collective-permute-start.7 = (bf16[512,512]{1,0:T(8,128)(2,1)S(1)}, bf16[512,512]{1,0:T(8,128)(2,1)S(1)}, u32[]{:S(2)}, u32[]{:S(2)}) collective-permute-start(bf16[512,512]{1,0:T(8,128)(2,1)S(1)} %pad_maximum_fusion.1.rest_0_), channel_id=1, source_target_pairs={{0,4},{1,5},{2,6},{3,7},{4,0},{5,1},{6,2},{7,3},{8,12},{9,13},{10,... | collective-permute-start | bytes 1572872 | tf_op jit(solution)/shard_map/ppermute | solution.py:42
  28.7 22.2 %collective-permute-start.5 = (bf16[512,512]{1,0:T(8,128)(2,1)S(1)}, bf16[512,512]{1,0:T(8,128)(2,1)S(1)}, u32[]{:S(2)}, u32[]{:S(2)}) collective-permute-start(bf16[512,512]{1,0:T(8,128)(2,1)S(1)} %pad_maximum_fusion.1.rest_0_), channel_id=1, source_target_pairs={{0,1},{1,2},{2,3},{3,0},{4,5},{5,6},{6,7},{7,4},{8,9},{9,10},{10,1... | collective-permute-start | bytes 1572872 | tf_op jit(solution)/shard_map/ppermute | solution.py:42
  30.2 24.4 %collective-permute-start.4 = (bf16[512,512]{1,0:T(8,128)(2,1)S(1)}, bf16[512,512]{1,0:T(8,128)(2,1)S(1)}, u32[]{:S(2)}, u32[]{:S(2)}) collective-permute-start(bf16[512,512]{1,0:T(8,128)(2,1)S(1)} %pad_maximum_fusion.1.rest_0_), channel_id=1, source_target_pairs={{0,2},{1,3},{2,0},{3,1},{4,6},{5,7},{6,4},{7,5},{8,10},{9,11},{10,... | collective-permute-start | bytes 1572872 | tf_op jit(solution)/shard_map/ppermute | solution.py:42
  33.1 21.5 %collective-permute-start.3 = (bf16[512,512]{1,0:T(8,128)(2,1)S(1)}, bf16[512,512]{1,0:T(8,128)(2,1)}, u32[]{:S(2)}, u32[]{:S(2)}) collective-permute-start(bf16[512,512]{1,0:T(8,128)(2,1)S(1)} %pad_maximum_fusion.1.rest_0_), channel_id=1, source_target_pairs={{0,3},{1,0},{2,1},{3,2},{4,7},{5,4},{6,5},{7,6},{8,11},{9,8},{10,9... | collective-permute-start | bytes 1572872 | tf_op jit(solution)/shard_map/ppermute | solution.py:42
  54.7 2.9 %collective-permute-start.8 = (bf16[4096,128]{1,0:T(8,128)(2,1)S(1)}, bf16[4096,128]{1,0:T(8,128)(2,1)}, u32[]{:S(2)}, u32[]{:S(2)}) collective-permute-start(bf16[4096,128]{1,0:T(8,128)(2,1)S(1)} %bitcast.27), channel_id=1, source_target_pairs={{0,8},{8,0},{16,24},{24,16},{32,40},{40,32},{48,56},{56,48},{64,72... | collective-permute-start | bytes 3145736 | tf_op jit(solution)/shard_map/ppermute | solution.py:34
  60.1 48.3 %all-to-all-start.1 = ((bf16[4,512,512]{2,1,0:T(8,128)(2,1)}), bf16[4,512,512]{2,1,0:T(8,128)(2,1)}, u32[]{:S(2)}, u32[]{:S(2)}) async-start(bf16[4,512,512]{2,1,0:T(8,128)(2,1)} %broadcast_in_dim.37), calls=%async_computation.1 | async-start | bytes 4194304 | tf_op jit(solution)/shard_map/all_to_all | solution.py:351
  67.6 49.5 %collective-permute-start.14 = (bf16[3,512,512]{2,1,0:T(8,128)(2,1)}, bf16[3,512,512]{2,1,0:T(8,128)(2,1)}, u32[]{:S(2)}, u32[]{:S(2)}) collective-permute-start(bf16[3,512,512]{2,1,0:T(8,128)(2,1)} %pad_maximum_fusion), channel_id=1, source_target_pairs={{0,16},{8,24},{16,0},{24,8},{32,48},{40,56},{48,32},{56,40},{64,80... | collective-permute-start | bytes 4718600 | tf_op jit(solution)/shard_map/ppermute | solution.py:34
  68.6 15.8 %collective-permute-start.11 = (bf16[512,512]{1,0:T(8,128)(2,1)S(1)}, bf16[512,512]{1,0:T(8,128)(2,1)}, u32[]{:S(2)}, u32[]{:S(2)}) collective-permute-start(bf16[512,512]{1,0:T(8,128)(2,1)S(1)} %collective-permute-done.7.rest_4_), channel_id=1, source_target_pairs={{0,1},{1,2},{2,3},{3,0},{4,5},{5,6},{6,7},{7,4},{8,9},{9,10},{10,1... | collective-permute-start | bytes 1572872 | tf_op jit(solution)/shard_map/ppermute | solution.py:42
  69.9 25.4 %collective-permute-start.10 = (bf16[512,512]{1,0:T(8,128)(2,1)S(1)}, bf16[512,512]{1,0:T(8,128)(2,1)}, u32[]{:S(2)}, u32[]{:S(2)}) collective-permute-start(bf16[512,512]{1,0:T(8,128)(2,1)S(1)} %collective-permute-done.7.rest_4_), channel_id=1, source_target_pairs={{0,2},{1,3},{2,0},{3,1},{4,6},{5,7},{6,4},{7,5},{8,10},{9,11},{10,... | collective-permute-start | bytes 1572872 | tf_op jit(solution)/shard_map/ppermute | solution.py:42
  72.3 23.2 %collective-permute-start.9 = (bf16[512,512]{1,0:T(8,128)(2,1)S(1)}, bf16[512,512]{1,0:T(8,128)(2,1)}, u32[]{:S(2)}, u32[]{:S(2)}) collective-permute-start(bf16[512,512]{1,0:T(8,128)(2,1)S(1)} %collective-permute-done.7.rest_4_), channel_id=1, source_target_pairs={{0,3},{1,0},{2,1},{3,2},{4,7},{5,4},{6,5},{7,6},{8,11},{9,8},{10,9... | collective-permute-start | bytes 1572872 | tf_op jit(solution)/shard_map/ppermute | solution.py:42
  73.9 43.1 %collective-permute-start.13 = (bf16[512,512]{1,0:T(8,128)(2,1)}, bf16[512,512]{1,0:T(8,128)(2,1)}, u32[]{:S(2)}, u32[]{:S(2)}) collective-permute-start(bf16[512,512]{1,0:T(8,128)(2,1)} %get-tuple-element.49), channel_id=1, source_target_pairs={{0,16},{8,24},{16,0},{24,8},{32,48},{40,56},{48,32},{56,40},{64,80... | collective-permute-start | bytes 1572872 | tf_op jit(solution)/shard_map/ppermute | solution.py:34
  113.9 9.0 %collective-permute-start.12 = (f32[256,512]{1,0:T(8,128)S(1)}, f32[256,512]{1,0:T(8,128)S(1)}, u32[]{:S(2)}, u32[]{:S(2)}) collective-permute-start(f32[256,512]{1,0:T(8,128)S(1)} %get-tuple-element.48), channel_id=1, source_target_pairs={{0,8},{8,0},{16,24},{24,16},{32,40},{40,32},{48,56},{56,48},{64,72... | collective-permute-start | bytes 1572872 | tf_op jit(solution)/shard_map/ppermute | solution.py:34
  117.0 7.7 %copy-start = (f32[128,2048]{1,0:T(8,128)S(1)}, f32[128,2048]{1,0:T(8,128)}, u32[]{:S(2)}) copy-start(f32[128,2048]{1,0:T(8,128)} %get-tuple-element.38.rest_5_) | copy-start | bytes 3145732
  122.5 2.2 %collective-permute-start.15 = (f32[256,512]{1,0:T(8,128)S(1)}, f32[256,512]{1,0:T(8,128)S(1)}, u32[]{:S(2)}, u32[]{:S(2)}) collective-permute-start(f32[256,512]{1,0:T(8,128)S(1)} %get-tuple-element.52), channel_id=1, source_target_pairs={{0,8},{8,0},{16,24},{24,16},{32,40},{40,32},{48,56},{56,48},{64,72... | collective-permute-start | bytes 1572872 | tf_op jit(solution)/shard_map/ppermute | solution.py:34
  130.4 3.6 %collective-permute-start.16 = (bf16[8,256,256]{2,1,0:T(8,128)(2,1)S(1)}, bf16[8,256,256]{2,1,0:T(8,128)(2,1)S(1)}, u32[]{:S(2)}, u32[]{:S(2)}) collective-permute-start(bf16[8,256,256]{2,1,0:T(8,128)(2,1)S(1)} %get-tuple-element.56), channel_id=1, source_target_pairs={{0,8},{8,0},{16,24},{24,16},{32,40},{40,32},{48,56},{56,48},{64,72... | collective-permute-start | bytes 3145736 | tf_op jit(solution)/shard_map/ppermute | solution.py:34
  (2 other events, 4.9 us)
Sparse Core Ops, SparseCore 0:
  10.3 44.4 all-gather.4
  56.5 47.3 all-gather.6

commit v15 on v14

--- a/solution.py
+++ b/solution.py
@@ -285,9 +285,10 @@
     half = own_ref.shape[0]
     k = 0
     for ref in stacks:
-        for j in range(ref.shape[0]):
+        blocks = [ref] if len(ref.shape) == 2 else [ref.at[j] for j in range(ref.shape[0])]
+        for block in blocks:
             for out, row in ((own_ref, 0), (other_ref, half)):
-                term = dot_t(grad[slots[k], row : row + half, :], ref[j])
+                term = dot_t(grad[slots[k], row : row + half, :], block[...])
                 if k == 0:
                     out[...] = term
                 else:
@@ -298,7 +299,7 @@
 def project(part, slots, grads, stacks):
     chips = len(grads)
     tokens, depth = grads[0].shape
-    features = stacks[0].shape[1]
+    features = stacks[0].shape[-2]
     half = jax.ShapeDtypeStruct((tokens // 2, features), F32)
 
     def once(shape):
@@ -319,7 +320,7 @@
             transcendentals=0,
         ),
         name="project%d" % part,
-    )(slots, *grads, *[in_hbm(stack) if stack.shape[0] > 1 else stack for stack in stacks])
+    )(slots, *grads, *[in_hbm(stack) if len(stack.shape) == 3 else stack for stack in stacks])
 
 
 def local(queries, keys, values, grad_out, out_weight, lengths):
@@ -366,28 +367,26 @@
     chip_grad = jnp.concatenate([mine, dp_move(other, 0, 0, 1)], axis=0)
     all_grad = [chip_grad] + [tensor_move(chip_grad, 0, step) for step in (-1, -2, 1)]
 
-    def gather_x(block):
-        return lax.all_gather(block, "dp", axis=0, axis_index_groups=groups_x)
+    def around_x(block):
+        return [dp_move(block, step, 0, 0) for step in (1, -1, 2)]
 
     own = [out_weight[:SPLIT], out_weight[SPLIT:]]
-    plane1 = gather_x(own[1])
-    pair0 = dp_move(after(own[0], chip_pair), 0, 1, 0)
+    plane1 = around_x(own[1])
+    own0 = after(own[0], chip_pair)
+    pair0 = dp_move(own0, 0, 1, 0)
     grad_pair = tensor_move(chip_grad, 1, 0)
-    ring, own, all_grad, pair0, grad_pair, info, query_pos, query_start = lax.optimization_barrier(
-        (ring, own, all_grad, pair0, grad_pair, info, query_pos, query_start)
+    ring, plane1, all_grad, pair0, grad_pair, info, query_pos, query_start = lax.optimization_barrier(
+        (ring, plane1, all_grad, pair0, grad_pair, info, query_pos, query_start)
     )
-    plane0 = gather_x(own[0])
+    plane0 = around_x(own0)
     all_grad += [grad_pair] + [tensor_move(grad_pair, 0, step) for step in (-1, -2, 1)]
-    pair1 = dp_move(own[1], 0, 1, 0)
+    rest = jnp.stack(plane1)
     swapped = dp_move(ring, 0, 0, 1)
-    swapped, copies = lax.optimization_barrier((swapped, copy(pair0, groups_x)))
+    swapped, copies, rest = lax.optimization_barrier((swapped, copy(pair0, groups_x), rest))
     other_plane = exchange(copies, "dp", groups_x).reshape(4, SPLIT, depth)
-    rest = jnp.concatenate(
-        [lax.dynamic_slice_in_dim(plane1, (x + i) % 4, 1, 0) for i in range(1, 4)], axis=0
-    )
-    rest, later = lax.optimization_barrier((rest, queries))
+    pair1 = dp_move(after(own[1], ring), 0, 1, 0)
     rest = dp_move(rest, 0, 1, 0)
-    probs, outs = forward(info, query_pos, query_start, later, ring, swapped)
+    probs, outs = forward(info, query_pos, query_start, queries, ring, swapped)
 
     t = lax.axis_index("tensor")
 
@@ -395,13 +394,13 @@
         source = 2 * (x_ % 4) + z_
         return (source - t) % 4 + jnp.where(source // 4 == t // 4, 0, 4)
 
-    same = [slot(i, z) for i in range(4)]
+    near = [slot(x + i, z) for i in (0, -1, 1, 2)]
     slots = [
-        jnp.stack(same + [slot(i, 1 - z) for i in range(4)]).astype(jnp.int32),
-        jnp.stack(same + [slot(x + i, 1 - z) for i in range(4)]).astype(jnp.int32),
+        jnp.stack(near + [slot(i, 1 - z) for i in range(4)]).astype(jnp.int32),
+        jnp.stack(near + [slot(x + i, 1 - z) for i in (0, -1, 1, 2)]).astype(jnp.int32),
     ]
     slots[0] = after(slots[0], outs)
-    stacks = [[plane0, other_plane], [plane1, pair1[None], rest]]
+    stacks = [[own0, *plane0, other_plane], [own[1], *plane1, pair1, rest]]
     terms = []
     for part in range(CHUNKS):
         mine, other = project(part, slots[part], all_grad, stacks[part])

time: 175 us -> 210 us (1.20); the launches traced: 175 us -> 207 us
  waiting for transfers between devices: 51.5 us -> 75.5 us
  between operations: 20.3 us -> 6.73 us
  blocking collectives: 32.8 us -> 40.1 us
  starting transfers between devices: 33.8 us -> 40 us
  local copies, waits for them, and re-layouts: 9.7 us -> 15.6 us
  other arithmetic: 2.21 us -> 4.46 us
    ppermute x10 -> x16, waiting for transfers between devices: 14.7 us -> 62.1 us  [dp_move(): return lax.ppermute(value, 'dp', pairs)]
    all_to_all x2, waiting for transfers between devices: 12.9 us -> 0.01 us  [exchange(): lax.all_to_all(copies, axis, 0, 0, axis_index_groups=groups, tiled=True)]
    ppermute x7, waiting for transfers between devices: 23.8 us -> 13.4 us  [tensor_move(): return lax.ppermute(value, 'tensor', pairs)]
    unnamed x10 -> x32, local copies, waits for them, and re-layouts: 0.02 us -> 7.54 us
    all_to_all x1, blocking collectives: 32.8 us -> 40.1 us  [local(): lax.all_to_all(chip_sums, 'dp', 0, 0, axis_index_groups=groups, tiled=True)]
    ppermute x10 -> x16, starting transfers between devices: 12.7 us -> 20 us  [dp_move(): return lax.ppermute(value, 'dp', pairs)]
    another operation x1 -> x2, other arithmetic: 0.18 us -> 2.88 us  [the longest x1 2.7 us: local(): rest = jnp.stack(plane1)]
  transfers between devices with their start and end apart: 21 -> 25, of which waited for: 11 -> 9; matrix products, arithmetic and copies ran while one was open for 5% -> 4% of each run, Pallas kernels for 11% -> 9%
where the time goes in v15:
time: 210 us; the launch traced here: 207 us
  waiting for transfers between devices  75.5 us (36%)
  blocking collectives  40.1 us (19%)
  starting transfers between devices  40 us (19%)
  Pallas kernels  24 us (11%)
  local copies, waits for them, and re-layouts  15.6 us (7%)
  between operations  6.73 us (3%)
  other arithmetic  4.46 us (2%)
    ppermute x16, waiting for transfers between devices, dp_move(): return lax.ppermute(value, 'dp', pairs)  62.1 us
    all_to_all x1, blocking collectives, local(): lax.all_to_all(chip_sums, 'dp', 0, 0, axis_index_groups=groups, tiled=True)  40.1 us
    ppermute x16, starting transfers between devices, dp_move(): return lax.ppermute(value, 'dp', pairs)  20 us
    ppermute x7, waiting for transfers between devices, tensor_move(): return lax.ppermute(value, 'tensor', pairs)  13.4 us
    ppermute x7, starting transfers between devices, tensor_move(): return lax.ppermute(value, 'tensor', pairs)  11.8 us
    pallas_call x2, Pallas kernels, project(): pl.pallas_call(functools.partial(project_kernel, chips), grid=(1,), in_sp...  11 us
    all_to_all x2, starting transfers between devices, exchange(): lax.all_to_all(copies, axis, 0, 0, axis_index_groups=groups, tiled=True)  8.21 us
    unnamed x32, local copies, waits for them, and re-layouts  7.54 us
  transfers between devices with their start and end apart: 25, of which 9 were waited for; matrix products, arithmetic and copies ran while one was open for 4% of the time, Pallas kernels for 9%

profile of v15, /device:TPU:0, one launch (start us, length us, event | category | flops | bytes accessed | tf_op | source)
XLA Modules:
  0.0 206.5 jit_solution(8915875907235429725)
XLA Ops:
  3.0 4.0 %collective-permute-start.1 = (bf16[512,128]{1,0:T(8,128)(2,1)S(1)}, bf16[512,128]{1,0:T(8,128)(2,1)S(1)}, u32[]{:S(2)}, u32[]{:S(2)}) collective-permute-start(bf16[512,128]{1,0:T(8,128)(2,1)S(1)} %pad_maximum_fusion.3), channel_id=1, source_target_pairs={{0,16},{8,24},{16,0},{24,8},{32,48},{40,56},{48,32},{56,40},{64,80... | collective-permute-start | bytes 393224 | tf_op jit(solution)/shard_map/ppermute | solution.py:34
  7.0 2.2 %fusion.5 = (bf16[512,512]{1,0:T(8,128)(2,1)}, bf16[512,512]{1,0:T(8,128)(2,1)}) fusion(bf16[1024,512]{1,0:T(8,128)(2,1)} %param.10), kind=kLoop, calls=%fused_computation.32 | loop fusion | bytes 2097152 | tf_op jit(solution)/shard_map/slice | solution.py:373
  9.2 3.0 %collective-permute-start.4 = (bf16[512,512]{1,0:T(8,128)(2,1)}, bf16[512,512]{1,0:T(8,128)(2,1)}, u32[]{:S(2)}, u32[]{:S(2)}) collective-permute-start(bf16[512,512]{1,0:T(8,128)(2,1)} %get-tuple-element.51.rest_8_), channel_id=1, source_target_pairs={{0,64},{8,72},{16,80},{24,88},{32,96},{40,104},{48,112},{56,120},{... | collective-permute-start | bytes 1572872 | tf_op jit(solution)/shard_map/ppermute | solution.py:34
  15.8 3.6 %all-to-all-start = ((bf16[4,1024,128]{2,1,0:T(8,128)(2,1)}), bf16[4,1024,128]{2,1,0:T(8,128)(2,1)S(1)}, u32[]{:S(2)}, u32[]{:S(2)}) async-start(bf16[4,1024,128]{2,1,0:T(8,128)(2,1)} %broadcast_in_dim.31), calls=%async_computation | async-start | bytes 2097152 | tf_op jit(solution)/shard_map/all_to_all | solution.py:352
  21.1 4.8 %collective-permute-done.4.rest_11_ = bf16[512,512]{1,0:T(8,128)(2,1)} collective-permute-done((bf16[512,512]{1,0:T(8,128)(2,1)}, bf16[512,512]{1,0:T(8,128)(2,1)}, u32[]{:S(2)}, u32[]{:S(2)}) %collective-permute-start.4) | collective-permute-done | bytes 524320 | tf_op jit(solution)/shard_map/ppermute | solution.py:34
  27.5 9.7 %collective-permute-done.3.rest_10_ = bf16[512,512]{1,0:T(8,128)(2,1)} collective-permute-done((bf16[512,512]{1,0:T(8,128)(2,1)}, bf16[512,512]{1,0:T(8,128)(2,1)}, u32[]{:S(2)}, u32[]{:S(2)}) %collective-permute-start.3) | collective-permute-done | bytes 524320 | tf_op jit(solution)/shard_map/ppermute | solution.py:34
  37.2 3.2 %collective-permute-start.7 = (bf16[512,512]{1,0:T(8,128)(2,1)S(1)}, bf16[512,512]{1,0:T(8,128)(2,1)S(1)}, u32[]{:S(2)}, u32[]{:S(2)}) collective-permute-start(bf16[512,512]{1,0:T(8,128)(2,1)S(1)} %pad_maximum_fusion.1.rest_0_), channel_id=1, source_target_pairs={{0,2},{1,3},{2,0},{3,1},{4,6},{5,7},{6,4},{7,5},{8,10},{9,11},{10,... | collective-permute-start | bytes 1572872 | tf_op jit(solution)/shard_map/ppermute | solution.py:42
  48.8 2.6 %collective-permute-done.7.rest_2_ = bf16[512,512]{1,0:T(8,128)(2,1)S(1)} collective-permute-done((bf16[512,512]{1,0:T(8,128)(2,1)S(1)}, bf16[512,512]{1,0:T(8,128)(2,1)S(1)}, u32[]{:S(2)}, u32[]{:S(2)}) %collective-permute-start.7) | collective-permute-done | bytes 524320 | tf_op jit(solution)/shard_map/ppermute | solution.py:42
  51.3 10.9 %collective-permute-done.6.rest_1_ = bf16[512,512]{1,0:T(8,128)(2,1)} collective-permute-done((bf16[512,512]{1,0:T(8,128)(2,1)S(1)}, bf16[512,512]{1,0:T(8,128)(2,1)}, u32[]{:S(2)}, u32[]{:S(2)}) %collective-permute-start.6) | collective-permute-done | bytes 524320 | tf_op jit(solution)/shard_map/ppermute | solution.py:42
  62.2 2.7 %pad_maximum_fusion = bf16[3,512,512]{2,1,0:T(8,128)(2,1)} fusion(bf16[1,512,512]{2,1,0:T(8,128)(2,1)} %bitcast.21, bf16[1,512,512]{2,1,0:T(8,128)(2,1)} %bitcast.20, bf16[1,512,512]{2,1,0:T(8,128)(2,1)} %bitcast.19), kind=kLoop, calls=%fused_computation.1 | loop fusion | flops 1572864 | bytes 3145728 | tf_op jit(solution)/shard_map/stack | solution.py:383
  65.9 2.5 %broadcast_in_dim.34 = bf16[4,512,512]{2,1,0:T(8,128)(2,1)} broadcast(bf16[512,512]{1,0:T(8,128)(2,1)} %collective-permute-done.9), dimensions={1,2} | broadcast | bytes 2621440 | tf_op jit(solution)/shard_map/broadcast_in_dim | solution.py:349
  69.0 4.6 %all-to-all-start.1 = ((bf16[4,512,512]{2,1,0:T(8,128)(2,1)}), bf16[4,512,512]{2,1,0:T(8,128)(2,1)}, u32[]{:S(2)}, u32[]{:S(2)}) async-start(bf16[4,512,512]{2,1,0:T(8,128)(2,1)} %broadcast_in_dim.34), calls=%async_computation.1 | async-start | bytes 4194304 | tf_op jit(solution)/shard_map/all_to_all | solution.py:352
  73.6 3.2 %collective-permute-start.19 = (bf16[512,512]{1,0:T(8,128)(2,1)}, bf16[512,512]{1,0:T(8,128)(2,1)S(1)}, u32[]{:S(2)}, u32[]{:S(2)}) collective-permute-start(bf16[512,512]{1,0:T(8,128)(2,1)} %get-tuple-element.51.rest_8_), channel_id=1, source_target_pairs={{0,16},{8,24},{16,0},{24,8},{32,48},{40,56},{48,32},{56,40},{64,80... | collective-permute-start | bytes 1572872 | tf_op jit(solution)/shard_map/ppermute | solution.py:34
  78.1 2.9 %collective-permute-start.13 = (bf16[512,512]{1,0:T(8,128)(2,1)S(1)}, bf16[512,512]{1,0:T(8,128)(2,1)S(1)}, u32[]{:S(2)}, u32[]{:S(2)}) collective-permute-start(bf16[512,512]{1,0:T(8,128)(2,1)S(1)} %collective-permute-done.10.rest_4_), channel_id=1, source_target_pairs={{0,2},{1,3},{2,0},{3,1},{4,6},{5,7},{6,4},{7,5},{8,10},{9,11},{10,... | collective-permute-start | bytes 1572872 | tf_op jit(solution)/shard_map/ppermute | solution.py:42
  81.3 36.8 %collective-permute-done.19.rest_12_ = bf16[512,512]{1,0:T(8,128)(2,1)S(1)} collective-permute-done((bf16[512,512]{1,0:T(8,128)(2,1)}, bf16[512,512]{1,0:T(8,128)(2,1)S(1)}, u32[]{:S(2)}, u32[]{:S(2)}) %collective-permute-start.19) | collective-permute-done | bytes 524320 | tf_op jit(solution)/shard_map/ppermute | solution.py:34
  119.0 2.0 collective-permute-start.17
  121.8 3.0 %collective-permute-start.16 = (bf16[512,512]{1,0:T(8,128)(2,1)}, bf16[512,512]{1,0:T(8,128)(2,1)}, u32[]{:S(2)}, u32[]{:S(2)}) collective-permute-start(bf16[512,512]{1,0:T(8,128)(2,1)} %get-tuple-element.31.rest_8_), channel_id=1, source_target_pairs={{0,96},{8,104},{16,112},{24,120},{32,0},{40,8},{48,16},{56,24},{64... | collective-permute-start | bytes 1572872 | tf_op jit(solution)/shard_map/ppermute | solution.py:34
  127.0 7.4 %forward.1 = (bf16[2816,2048]{1,0:T(8,128)(2,1)}, f32[128,2048]{1,0:T(8,128)}) custom-call(s32[36]{0:T(128)S(1)} %concatenate.16.info, s32[1,256]{1,0:T(1,128)S(1)} %iota_add_fusion.pos_ref, s32[1,256]{1,0:T(1,128)S(1)} %bitcast.30, bf16[256,1024]{1,0:T(8,128)(2,1)} %rest_6_.1, bf16[4096,128]{1,0:T(8,128)(2,1)S(1)} %bitcast.28, bf16[4096,128]{1,0:T(8,128)(2,1)S(1)} %copy-done.7), custom_call_target="tpu_custom_call" | custom-call | flops 100000000 | bytes 1048576 | tf_op jit(solution)/shard_map/forward/pallas_call | solution.py:141
  134.5 5.8 %project1.1 = (f32[256,512]{1,0:T(8,128)S(1)}, f32[256,512]{1,0:T(8,128)}) custom-call(s32[8]{0:T(128)S(1)} %stack.91.slots, bf16[512,512]{1,0:T(8,128)(2,1)S(1)} %pad_maximum_fusion.1.rest_0_, bf16[512,512]{1,0:T(8,128)(2,1)} %collective-permute-done.6.rest_1_, bf16[512,512]{1,0:T(8,128)(2,1)S(1)} %collective-permute-done.7.rest_2_, ...), custom_call_target="tpu_custom_call" | custom-call | flops 2147483648 | bytes 10485760 | tf_op jit(solution)/shard_map/project1/pallas_call | solution.py:308
  141.4 5.3 %collective-permute-done.16.rest_10_ = bf16[512,512]{1,0:T(8,128)(2,1)} collective-permute-done((bf16[512,512]{1,0:T(8,128)(2,1)}, bf16[512,512]{1,0:T(8,128)(2,1)}, u32[]{:S(2)}, u32[]{:S(2)}) %collective-permute-start.16) | collective-permute-done | bytes 524320 | tf_op jit(solution)/shard_map/ppermute | solution.py:34
  148.7 5.3 %project0.1 = (f32[256,512]{1,0:T(8,128)S(1)}, f32[256,512]{1,0:T(8,128)S(1)}) custom-call(s32[8]{0:T(128)S(1)} %stack.82.slots, bf16[512,512]{1,0:T(8,128)(2,1)S(1)} %pad_maximum_fusion.1.rest_0_, bf16[512,512]{1,0:T(8,128)(2,1)} %collective-permute-done.6.rest_1_, bf16[512,512]{1,0:T(8,128)(2,1)S(1)} %collective-permute-done.7.rest_2_, ...), custom_call_target="tpu_custom_call" | custom-call | flops 2147483648 | bytes 10485760 | tf_op jit(solution)/shard_map/project0/pallas_call | solution.py:308
  156.0 5.6 %backward.1 = (bf16[256,1024]{1,0:T(8,128)(2,1)}, f32[8,256,256]{2,1,0:T(8,128)S(1)}, bf16[8,256,256]{2,1,0:T(8,128)(2,1)S(1)}) custom-call(s32[36]{0:T(128)S(1)} %concatenate.16.info, f32[256,512]{1,0:T(8,128)S(1)} %get-tuple-element.49.rest_0_, f32[256,512]{1,0:T(8,128)S(1)} %collective-permute-done.18.rest_1_, f32[256,512]{1,0:T(8,128)S(1)} %copy-done.13, ...), custom_call_target="tpu_custom_call" | custom-call | flops 8000000000 | bytes 10485760 | tf_op jit(solution)/shard_map/backward/pallas_call | solution.py:241
  162.9 2.3 %collective-permute-done.22 = bf16[8,256,256]{2,1,0:T(8,128)(2,1)S(1)} collective-permute-done((bf16[8,256,256]{2,1,0:T(8,128)(2,1)S(1)}, bf16[8,256,256]{2,1,0:T(8,128)(2,1)S(1)}, u32[]{:S(2)}, u32[]{:S(2)}) %collective-permute-start.22) | collective-permute-done | bytes 1048608 | tf_op jit(solution)/shard_map/ppermute | solution.py:34
  165.5 40.1 %all_to_all.15 = bf16[8,256,256]{2,1,0:T(8,128)(2,1)S(1)} all-to-all(bf16[8,256,256]{2,1,0:T(8,128)(2,1)S(1)} %add_convert_fusion), channel_id=1, replica_groups={{0,16,32,48,64,80,96,112},{8,24,40,56,72,88,104,120},{1,17,33,49,65,81,..., dimensions={0} | all-to-all | bytes 2097152 | tf_op jit(solution)/shard_map/all_to_all | solution.py:412
  (86 shorter events, 26.1 us)
Async XLA Ops:
  3.0 11.7 %collective-permute-start.1 = (bf16[512,128]{1,0:T(8,128)(2,1)S(1)}, bf16[512,128]{1,0:T(8,128)(2,1)S(1)}, u32[]{:S(2)}, u32[]{:S(2)}) collective-permute-start(bf16[512,128]{1,0:T(8,128)(2,1)S(1)} %pad_maximum_fusion.3), channel_id=1, source_target_pairs={{0,16},{8,24},{16,0},{24,8},{32,48},{40,56},{48,32},{56,40},{64,80... | collective-permute-start | bytes 393224 | tf_op jit(solution)/shard_map/ppermute | solution.py:34
  9.2 16.7 %collective-permute-start.4 = (bf16[512,512]{1,0:T(8,128)(2,1)}, bf16[512,512]{1,0:T(8,128)(2,1)}, u32[]{:S(2)}, u32[]{:S(2)}) collective-permute-start(bf16[512,512]{1,0:T(8,128)(2,1)} %get-tuple-element.51.rest_8_), channel_id=1, source_target_pairs={{0,64},{8,72},{16,80},{24,88},{32,96},{40,104},{48,112},{56,120},{... | collective-permute-start | bytes 1572872 | tf_op jit(solution)/shard_map/ppermute | solution.py:34
  12.3 25.0 %collective-permute-start.3 = (bf16[512,512]{1,0:T(8,128)(2,1)}, bf16[512,512]{1,0:T(8,128)(2,1)}, u32[]{:S(2)}, u32[]{:S(2)}) collective-permute-start(bf16[512,512]{1,0:T(8,128)(2,1)} %get-tuple-element.51.rest_8_), channel_id=1, source_target_pairs={{0,96},{8,104},{16,112},{24,120},{32,0},{40,8},{48,16},{56,24},{64... | collective-permute-start | bytes 1572872 | tf_op jit(solution)/shard_map/ppermute | solution.py:34
  13.4 27.0 %collective-permute-start.2 = (bf16[512,512]{1,0:T(8,128)(2,1)}, bf16[512,512]{1,0:T(8,128)(2,1)}, u32[]{:S(2)}, u32[]{:S(2)}) collective-permute-start(bf16[512,512]{1,0:T(8,128)(2,1)} %get-tuple-element.51.rest_8_), channel_id=1, source_target_pairs={{0,32},{8,40},{16,48},{24,56},{32,64},{40,72},{48,80},{56,88},{64,... | collective-permute-start | bytes 1572872 | tf_op jit(solution)/shard_map/ppermute | solution.py:34
  14.3 5.2 %collective-permute-start.5 = (bf16[256,512]{1,0:T(8,128)(2,1)S(1)}, bf16[256,512]{1,0:T(8,128)(2,1)S(1)}, u32[]{:S(2)}, u32[]{:S(2)}) collective-permute-start(bf16[256,512]{1,0:T(8,128)(2,1)S(1)} %get-tuple-element.62), channel_id=1, source_target_pairs={{0,8},{8,0},{16,24},{24,16},{32,40},{40,32},{48,56},{56,48},{64,72... | collective-permute-start | bytes 786440 | tf_op jit(solution)/shard_map/ppermute | solution.py:34
  15.8 46.4 %all-to-all-start = ((bf16[4,1024,128]{2,1,0:T(8,128)(2,1)}), bf16[4,1024,128]{2,1,0:T(8,128)(2,1)S(1)}, u32[]{:S(2)}, u32[]{:S(2)}) async-start(bf16[4,1024,128]{2,1,0:T(8,128)(2,1)} %broadcast_in_dim.31), calls=%async_computation | async-start | bytes 2097152 | tf_op jit(solution)/shard_map/all_to_all | solution.py:352
  19.4 29.4 %collective-permute-start.9 = (bf16[512,512]{1,0:T(8,128)(2,1)}, bf16[512,512]{1,0:T(8,128)(2,1)}, u32[]{:S(2)}, u32[]{:S(2)}) collective-permute-start(bf16[512,512]{1,0:T(8,128)(2,1)} %get-tuple-element.31.rest_8_), channel_id=1, source_target_pairs={{0,16},{8,24},{16,0},{24,8},{32,48},{40,56},{48,32},{56,40},{64,80... | collective-permute-start | bytes 1572872 | tf_op jit(solution)/shard_map/ppermute | solution.py:34
  19.5 29.2 %collective-permute-start.10 = (bf16[512,512]{1,0:T(8,128)(2,1)S(1)}, bf16[512,512]{1,0:T(8,128)(2,1)S(1)}, u32[]{:S(2)}, u32[]{:S(2)}) collective-permute-start(bf16[512,512]{1,0:T(8,128)(2,1)S(1)} %pad_maximum_fusion.1.rest_0_), channel_id=1, source_target_pairs={{0,4},{1,5},{2,6},{3,7},{4,0},{5,1},{6,2},{7,3},{8,12},{9,13},{10,... | collective-permute-start | bytes 1572872 | tf_op jit(solution)/shard_map/ppermute | solution.py:42
  25.9 22.9 %collective-permute-start.8 = (bf16[512,512]{1,0:T(8,128)(2,1)S(1)}, bf16[512,512]{1,0:T(8,128)(2,1)S(1)}, u32[]{:S(2)}, u32[]{:S(2)}) collective-permute-start(bf16[512,512]{1,0:T(8,128)(2,1)S(1)} %pad_maximum_fusion.1.rest_0_), channel_id=1, source_target_pairs={{0,1},{1,2},{2,3},{3,0},{4,5},{5,6},{6,7},{7,4},{8,9},{9,10},{10,1... | collective-permute-start | bytes 1572872 | tf_op jit(solution)/shard_map/ppermute | solution.py:42
  37.2 14.1 %collective-permute-start.7 = (bf16[512,512]{1,0:T(8,128)(2,1)S(1)}, bf16[512,512]{1,0:T(8,128)(2,1)S(1)}, u32[]{:S(2)}, u32[]{:S(2)}) collective-permute-start(bf16[512,512]{1,0:T(8,128)(2,1)S(1)} %pad_maximum_fusion.1.rest_0_), channel_id=1, source_target_pairs={{0,2},{1,3},{2,0},{3,1},{4,6},{5,7},{6,4},{7,5},{8,10},{9,11},{10,... | collective-permute-start | bytes 1572872 | tf_op jit(solution)/shard_map/ppermute | solution.py:42
  40.4 21.8 %collective-permute-start.6 = (bf16[512,512]{1,0:T(8,128)(2,1)S(1)}, bf16[512,512]{1,0:T(8,128)(2,1)}, u32[]{:S(2)}, u32[]{:S(2)}) collective-permute-start(bf16[512,512]{1,0:T(8,128)(2,1)S(1)} %pad_maximum_fusion.1.rest_0_), channel_id=1, source_target_pairs={{0,3},{1,0},{2,1},{3,2},{4,7},{5,4},{6,5},{7,6},{8,11},{9,8},{10,9... | collective-permute-start | bytes 1572872 | tf_op jit(solution)/shard_map/ppermute | solution.py:42
  62.2 2.7 %collective-permute-start.11 = (bf16[4096,128]{1,0:T(8,128)(2,1)S(1)}, bf16[4096,128]{1,0:T(8,128)(2,1)S(1)}, u32[]{:S(2)}, u32[]{:S(2)}) collective-permute-start(bf16[4096,128]{1,0:T(8,128)(2,1)S(1)} %bitcast.27), channel_id=1, source_target_pairs={{0,8},{8,0},{16,24},{24,16},{32,40},{40,32},{48,56},{56,48},{64,72... | collective-permute-start | bytes 3145736 | tf_op jit(solution)/shard_map/ppermute | solution.py:34
  68.4 66.0 %collective-permute-start.20 = (bf16[3,512,512]{2,1,0:T(8,128)(2,1)}, bf16[3,512,512]{2,1,0:T(8,128)(2,1)}, u32[]{:S(2)}, u32[]{:S(2)}) collective-permute-start(bf16[3,512,512]{2,1,0:T(8,128)(2,1)} %pad_maximum_fusion), channel_id=1, source_target_pairs={{0,16},{8,24},{16,0},{24,8},{32,48},{40,56},{48,32},{56,40},{64,80... | collective-permute-start | bytes 4718600 | tf_op jit(solution)/shard_map/ppermute | solution.py:34
  69.0 77.6 %all-to-all-start.1 = ((bf16[4,512,512]{2,1,0:T(8,128)(2,1)}), bf16[4,512,512]{2,1,0:T(8,128)(2,1)}, u32[]{:S(2)}, u32[]{:S(2)}) async-start(bf16[4,512,512]{2,1,0:T(8,128)(2,1)} %broadcast_in_dim.34), calls=%async_computation.1 | async-start | bytes 4194304 | tf_op jit(solution)/shard_map/all_to_all | solution.py:352
  73.6 44.6 %collective-permute-start.19 = (bf16[512,512]{1,0:T(8,128)(2,1)}, bf16[512,512]{1,0:T(8,128)(2,1)S(1)}, u32[]{:S(2)}, u32[]{:S(2)}) collective-permute-start(bf16[512,512]{1,0:T(8,128)(2,1)} %get-tuple-element.51.rest_8_), channel_id=1, source_target_pairs={{0,16},{8,24},{16,0},{24,8},{32,48},{40,56},{48,32},{56,40},{64,80... | collective-permute-start | bytes 1572872 | tf_op jit(solution)/shard_map/ppermute | solution.py:34
  76.9 44.1 %collective-permute-start.14 = (bf16[512,512]{1,0:T(8,128)(2,1)S(1)}, bf16[512,512]{1,0:T(8,128)(2,1)S(1)}, u32[]{:S(2)}, u32[]{:S(2)}) collective-permute-start(bf16[512,512]{1,0:T(8,128)(2,1)S(1)} %collective-permute-done.10.rest_4_), channel_id=1, source_target_pairs={{0,1},{1,2},{2,3},{3,0},{4,5},{5,6},{6,7},{7,4},{8,9},{9,10},{10,1... | collective-permute-start | bytes 1572872 | tf_op jit(solution)/shard_map/ppermute | solution.py:42
  78.1 46.8 %collective-permute-start.13 = (bf16[512,512]{1,0:T(8,128)(2,1)S(1)}, bf16[512,512]{1,0:T(8,128)(2,1)S(1)}, u32[]{:S(2)}, u32[]{:S(2)}) collective-permute-start(bf16[512,512]{1,0:T(8,128)(2,1)S(1)} %collective-permute-done.10.rest_4_), channel_id=1, source_target_pairs={{0,2},{1,3},{2,0},{3,1},{4,6},{5,7},{6,4},{7,5},{8,10},{9,11},{10,... | collective-permute-start | bytes 1572872 | tf_op jit(solution)/shard_map/ppermute | solution.py:42
  81.0 53.5 %collective-permute-start.12 = (bf16[512,512]{1,0:T(8,128)(2,1)S(1)}, bf16[512,512]{1,0:T(8,128)(2,1)}, u32[]{:S(2)}, u32[]{:S(2)}) collective-permute-start(bf16[512,512]{1,0:T(8,128)(2,1)S(1)} %collective-permute-done.10.rest_4_), channel_id=1, source_target_pairs={{0,3},{1,0},{2,1},{3,2},{4,7},{5,4},{6,5},{7,6},{8,11},{9,8},{10,9... | collective-permute-start | bytes 1572872 | tf_op jit(solution)/shard_map/ppermute | solution.py:42
  119.0 22.4 %collective-permute-start.17 = (bf16[512,512]{1,0:T(8,128)(2,1)}, bf16[512,512]{1,0:T(8,128)(2,1)}, u32[]{:S(2)}, u32[]{:S(2)}) collective-permute-start(bf16[512,512]{1,0:T(8,128)(2,1)} %get-tuple-element.31.rest_8_), channel_id=1, source_target_pairs={{0,64},{8,72},{16,80},{24,88},{32,96},{40,104},{48,112},{56,120},{... | collective-permute-start | bytes 1572872 | tf_op jit(solution)/shard_map/ppermute | solution.py:34
  121.8 24.8 %collective-permute-start.16 = (bf16[512,512]{1,0:T(8,128)(2,1)}, bf16[512,512]{1,0:T(8,128)(2,1)}, u32[]{:S(2)}, u32[]{:S(2)}) collective-permute-start(bf16[512,512]{1,0:T(8,128)(2,1)} %get-tuple-element.31.rest_8_), channel_id=1, source_target_pairs={{0,96},{8,104},{16,112},{24,120},{32,0},{40,8},{48,16},{56,24},{64... | collective-permute-start | bytes 1572872 | tf_op jit(solution)/shard_map/ppermute | solution.py:34
  125.6 21.0 %collective-permute-start.15 = (bf16[512,512]{1,0:T(8,128)(2,1)}, bf16[512,512]{1,0:T(8,128)(2,1)}, u32[]{:S(2)}, u32[]{:S(2)}) collective-permute-start(bf16[512,512]{1,0:T(8,128)(2,1)} %get-tuple-element.31.rest_8_), channel_id=1, source_target_pairs={{0,32},{8,40},{16,48},{24,56},{32,64},{40,72},{48,80},{56,88},{64,... | collective-permute-start | bytes 1572872 | tf_op jit(solution)/shard_map/ppermute | solution.py:34
  141.0 13.0 %collective-permute-start.21 = (f32[256,512]{1,0:T(8,128)}, f32[256,512]{1,0:T(8,128)}, u32[]{:S(2)}, u32[]{:S(2)}) collective-permute-start(f32[256,512]{1,0:T(8,128)} %get-tuple-element.54), channel_id=1, source_target_pairs={{0,8},{8,0},{16,24},{24,16},{32,40},{40,32},{48,56},{56,48},{64,72... | collective-permute-start | bytes 1572872 | tf_op jit(solution)/shard_map/ppermute | solution.py:34
  154.0 2.0 collective-permute-start.18
  161.6 3.6 %collective-permute-start.22 = (bf16[8,256,256]{2,1,0:T(8,128)(2,1)S(1)}, bf16[8,256,256]{2,1,0:T(8,128)(2,1)S(1)}, u32[]{:S(2)}, u32[]{:S(2)}) collective-permute-start(bf16[8,256,256]{2,1,0:T(8,128)(2,1)S(1)} %get-tuple-element.58), channel_id=1, source_target_pairs={{0,8},{8,0},{16,24},{24,16},{32,40},{40,32},{48,56},{56,48},{64,72... | collective-permute-start | bytes 3145736 | tf_op jit(solution)/shard_map/ppermute | solution.py:34
  (17 other events, 80.2 us)

commit v16 on v15

--- a/solution.py
+++ b/solution.py
@@ -279,9 +279,9 @@
 
 
 def project_kernel(chips, slots, *rest):
-    grads, (*stacks, own_ref, other_ref, grad) = rest[:chips], rest[chips:]
+    grads, (*stacks, own_ref, other_ref, grad) = rest[: chips // 2], rest[chips // 2 :]
     for i, ref in enumerate(grads):
-        grad[i] = ref[...]
+        grad[2 * i : 2 * i + 2] = ref[...]
     half = own_ref.shape[0]
     k = 0
     for ref in stacks:
@@ -297,8 +297,8 @@
 
 
 def project(part, slots, grads, stacks):
-    chips = len(grads)
-    tokens, depth = grads[0].shape
+    chips = 2 * len(grads)
+    _, tokens, depth = grads[0].shape
     features = stacks[0].shape[-2]
     half = jax.ShapeDtypeStruct((tokens // 2, features), F32)
 
@@ -365,7 +365,6 @@
     mine = lax.dynamic_slice_in_dim(grad_out, core * depth, depth, 1)
     other = lax.dynamic_slice_in_dim(grad_out, (1 - core) * depth, depth, 1)
     chip_grad = jnp.concatenate([mine, dp_move(other, 0, 0, 1)], axis=0)
-    all_grad = [chip_grad] + [tensor_move(chip_grad, 0, step) for step in (-1, -2, 1)]
 
     def around_x(block):
         return [dp_move(block, step, 0, 0) for step in (1, -1, 2)]
@@ -375,32 +374,31 @@
     own0 = after(own[0], chip_pair)
     pair0 = dp_move(own0, 0, 1, 0)
     grad_pair = tensor_move(chip_grad, 1, 0)
-    ring, plane1, all_grad, pair0, grad_pair, info, query_pos, query_start = lax.optimization_barrier(
-        (ring, plane1, all_grad, pair0, grad_pair, info, query_pos, query_start)
+    ring, plane1, pair0, grad_pair, info, query_pos, query_start = lax.optimization_barrier(
+        (ring, plane1, pair0, grad_pair, info, query_pos, query_start)
     )
-    plane0 = around_x(own0)
-    all_grad += [grad_pair] + [tensor_move(grad_pair, 0, step) for step in (-1, -2, 1)]
-    rest = jnp.stack(plane1)
     swapped = dp_move(ring, 0, 0, 1)
-    swapped, copies, rest = lax.optimization_barrier((swapped, copy(pair0, groups_x), rest))
-    other_plane = exchange(copies, "dp", groups_x).reshape(4, SPLIT, depth)
+    all_grad = [jnp.stack([chip_grad, grad_pair])]
+    all_grad += [tensor_move(all_grad[0], 0, step) for step in (-1, -2, 1)]
+    copies = copy(jnp.stack([own0, pair0]), groups_x)
+    plane0 = exchange(copies, "dp", groups_x).reshape(8, SPLIT, depth)
     pair1 = dp_move(after(own[1], ring), 0, 1, 0)
-    rest = dp_move(rest, 0, 1, 0)
+    rest = dp_move(jnp.stack(plane1), 0, 1, 0)
     probs, outs = forward(info, query_pos, query_start, queries, ring, swapped)
 
     t = lax.axis_index("tensor")
 
     def slot(x_, z_):
         source = 2 * (x_ % 4) + z_
-        return (source - t) % 4 + jnp.where(source // 4 == t // 4, 0, 4)
+        return (source - t) % 4 * 2 + jnp.where(source // 4 == t // 4, 0, 1)
 
     near = [slot(x + i, z) for i in (0, -1, 1, 2)]
     slots = [
-        jnp.stack(near + [slot(i, 1 - z) for i in range(4)]).astype(jnp.int32),
+        jnp.stack([slot(i, z_) for i in range(4) for z_ in (z, 1 - z)]).astype(jnp.int32),
         jnp.stack(near + [slot(x + i, 1 - z) for i in (0, -1, 1, 2)]).astype(jnp.int32),
     ]
     slots[0] = after(slots[0], outs)
-    stacks = [[own0, *plane0, other_plane], [own[1], *plane1, pair1, rest]]
+    stacks = [[plane0], [own[1], *plane1, pair1, rest]]
     terms = []
     for part in range(CHUNKS):
         mine, other = project(part, slots[part], all_grad, stacks[part])

time: 210 us -> 168 us (0.80); the launches traced: 207 us -> 168 us
  waiting for transfers between devices: 75.5 us -> 55 us
  starting transfers between devices: 40 us -> 31.8 us
  blocking collectives: 40.1 us -> 32.8 us
  local copies, waits for them, and re-layouts: 15.6 us -> 10.7 us
  other arithmetic: 4.46 us -> 6.92 us
    ppermute x16 -> x13, waiting for transfers between devices: 62.1 us -> 42.2 us  [dp_move(): return lax.ppermute(value, 'dp', pairs)]
    all_to_all x1, blocking collectives: 40.1 us -> 32.8 us  [local(): lax.all_to_all(chip_sums, 'dp', 0, 0, axis_index_groups=groups, tiled=True)]
    ppermute x16 -> x13, starting transfers between devices: 20 us -> 15.2 us  [dp_move(): return lax.ppermute(value, 'dp', pairs)]
    unnamed x32 -> x30, local copies, waits for them, and re-layouts: 7.54 us -> 3.08 us
    ppermute x7 -> x4, starting transfers between devices: 11.8 us -> 7.44 us  [tensor_move(): return lax.ppermute(value, 'tensor', pairs)]
    ppermute x7 -> x4, waiting for transfers between devices: 13.4 us -> 11.7 us  [tensor_move(): return lax.ppermute(value, 'tensor', pairs)]
  transfers between devices with their start and end apart: 25 -> 19, of which waited for: 9 -> 9; matrix products, arithmetic and copies ran while one was open for 4% -> 5% of each run, Pallas kernels for 9% -> 11%
where the time goes in v16:
time: 168 us
  waiting for transfers between devices  55 us (33%)
  blocking collectives  32.8 us (20%)
  starting transfers between devices  31.8 us (19%)
  Pallas kernels  24.2 us (14%)
  local copies, waits for them, and re-layouts  10.7 us (6%)
  other arithmetic  6.92 us (4%)
  between operations  6.45 us (4%)
    ppermute x13, waiting for transfers between devices, dp_move(): return lax.ppermute(value, 'dp', pairs)  42.2 us
    all_to_all x1, blocking collectives, local(): lax.all_to_all(chip_sums, 'dp', 0, 0, axis_index_groups=groups, tiled=True)  32.8 us
    ppermute x13, starting transfers between devices, dp_move(): return lax.ppermute(value, 'dp', pairs)  15.2 us
    ppermute x4, waiting for transfers between devices, tensor_move(): return lax.ppermute(value, 'tensor', pairs)  11.7 us
    pallas_call x2, Pallas kernels, project(): pl.pallas_call(functools.partial(project_kernel, chips), grid=(1,), in_sp...  10.7 us
    all_to_all x2, starting transfers between devices, exchange(): lax.all_to_all(copies, axis, 0, 0, axis_index_groups=groups, tiled=True)  9.12 us
    pallas_call x1, Pallas kernels, forward(): pl.pallas_call(forward_kernel, grid_spec=pltpu.PrefetchScalarGridSpec(num...  7.76 us
    ppermute x4, starting transfers between devices, tensor_move(): return lax.ppermute(value, 'tensor', pairs)  7.44 us
  transfers between devices with their start and end apart: 19, of which 9 were waited for; matrix products, arithmetic and copies ran while one was open for 5% of the time, Pallas kernels for 11%

profile of v16, /device:TPU:0, one launch (start us, length us, event | category | flops | bytes accessed | tf_op | source)
XLA Modules:
  0.0 167.9 jit_solution(3387658597860057763)
XLA Ops:
  3.6 4.0 %collective-permute-start.1 = (bf16[512,128]{1,0:T(8,128)(2,1)}, bf16[512,128]{1,0:T(8,128)(2,1)}, u32[]{:S(2)}, u32[]{:S(2)}) collective-permute-start(bf16[512,128]{1,0:T(8,128)(2,1)} %pad_maximum_fusion.5), channel_id=1, source_target_pairs={{0,16},{8,24},{16,0},{24,8},{32,48},{40,56},{48,32},{56,40},{64,80... | collective-permute-start | bytes 393224 | tf_op jit(solution)/shard_map/ppermute | solution.py:34
  7.6 2.1 %fusion.6 = (bf16[512,512]{1,0:T(8,128)(2,1)S(1)}, bf16[512,512]{1,0:T(8,128)(2,1)}) fusion(bf16[1024,512]{1,0:T(8,128)(2,1)} %param.10), kind=kLoop, calls=%fused_computation.35 | loop fusion | bytes 2097152 | tf_op jit(solution)/shard_map/slice | solution.py:372
  9.6 3.0 %collective-permute-start.4 = (bf16[512,512]{1,0:T(8,128)(2,1)}, bf16[512,512]{1,0:T(8,128)(2,1)S(1)}, u32[]{:S(2)}, u32[]{:S(2)}) collective-permute-start(bf16[512,512]{1,0:T(8,128)(2,1)} %get-tuple-element.38.rest_4_), channel_id=1, source_target_pairs={{0,64},{8,72},{16,80},{24,88},{32,96},{40,104},{48,112},{56,120},{... | collective-permute-start | bytes 1572872 | tf_op jit(solution)/shard_map/ppermute | solution.py:34
  17.0 4.2 %all-to-all-start = ((bf16[4,1024,128]{2,1,0:T(8,128)(2,1)}), bf16[4,1024,128]{2,1,0:T(8,128)(2,1)}, u32[]{:S(2)}, u32[]{:S(2)}) async-start(bf16[4,1024,128]{2,1,0:T(8,128)(2,1)} %broadcast_in_dim.31), calls=%async_computation | async-start | bytes 2097152 | tf_op jit(solution)/shard_map/all_to_all | solution.py:352
  22.3 1.5 collective-permute-start.7
  30.8 6.7 %collective-permute-done.3.rest_6_ = bf16[512,512]{1,0:T(8,128)(2,1)S(1)} collective-permute-done((bf16[512,512]{1,0:T(8,128)(2,1)}, bf16[512,512]{1,0:T(8,128)(2,1)S(1)}, u32[]{:S(2)}, u32[]{:S(2)}) %collective-permute-start.3) | collective-permute-done | bytes 524320 | tf_op jit(solution)/shard_map/ppermute | solution.py:34
  37.7 8.8 %collective-permute-done.7 = bf16[512,512]{1,0:T(8,128)(2,1)S(1)} collective-permute-done((bf16[512,512]{1,0:T(8,128)(2,1)}, bf16[512,512]{1,0:T(8,128)(2,1)S(1)}, u32[]{:S(2)}, u32[]{:S(2)}) %collective-permute-start.7) | collective-permute-done | bytes 524320 | tf_op jit(solution)/shard_map/ppermute | solution.py:42
  49.0 2.3 %broadcast_in_dim.34 = bf16[4,2,512,512]{3,2,1,0:T(8,128)(2,1)} broadcast(bf16[2,512,512]{2,1,0:T(8,128)(2,1)S(1)} %pad_maximum_fusion.2), dimensions={1,2,3} | broadcast | bytes 5242880 | tf_op jit(solution)/shard_map/broadcast_in_dim | solution.py:349
  51.3 4.9 %all-to-all-start.1 = ((bf16[4,2,512,512]{3,2,1,0:T(8,128)(2,1)}), bf16[4,2,512,512]{3,2,1,0:T(8,128)(2,1)}, u32[]{:S(2)}, u32[]{:S(2)}) async-start(bf16[4,2,512,512]{3,2,1,0:T(8,128)(2,1)} %broadcast_in_dim.34), calls=%async_computation.1 | async-start | bytes 8388608 | tf_op jit(solution)/shard_map/all_to_all | solution.py:352
  56.3 1.4 pad_maximum_fusion
  57.7 2.4 %collective-permute-start.14 = (bf16[3,512,512]{2,1,0:T(8,128)(2,1)}, bf16[3,512,512]{2,1,0:T(8,128)(2,1)}, u32[]{:S(2)}, u32[]{:S(2)}) collective-permute-start(bf16[3,512,512]{2,1,0:T(8,128)(2,1)} %pad_maximum_fusion), channel_id=1, source_target_pairs={{0,16},{8,24},{16,0},{24,8},{32,48},{40,56},{48,32},{56,40},{64,80... | collective-permute-start | bytes 4718600 | tf_op jit(solution)/shard_map/ppermute | solution.py:34
  60.2 1.6 collective-permute-start.11
  61.8 2.9 %collective-permute-start.10 = (bf16[2,512,512]{2,1,0:T(8,128)(2,1)S(1)}, bf16[2,512,512]{2,1,0:T(8,128)(2,1)S(1)}, u32[]{:S(2)}, u32[]{:S(2)}) collective-permute-start(bf16[2,512,512]{2,1,0:T(8,128)(2,1)S(1)} %pad_maximum_fusion.1.rest_0_), channel_id=1, source_target_pairs={{0,2},{1,3},{2,0},{3,1},{4,6},{5,7},{6,4},{7,5},{8,10},{9,11},{10,... | collective-permute-start | bytes 3145736 | tf_op jit(solution)/shard_map/ppermute | solution.py:42
  64.7 1.3 collective-permute-start.9
  69.6 7.8 %forward.1 = (bf16[2816,2048]{1,0:T(8,128)(2,1)}, f32[128,2048]{1,0:T(8,128)}) custom-call(s32[36]{0:T(128)S(1)} %concatenate.16.info, s32[1,256]{1,0:T(1,128)S(1)} %iota_add_fusion.pos_ref, s32[1,256]{1,0:T(1,128)S(1)} %bitcast.40, bf16[256,1024]{1,0:T(8,128)(2,1)} %rest_6_.1, bf16[4096,128]{1,0:T(8,128)(2,1)} %bitcast.here_ref.rest_7_, ...), custom_call_target="tpu_custom_call" | custom-call | flops 100000000 | bytes 1048576 | tf_op jit(solution)/shard_map/forward/pallas_call | solution.py:141
  77.4 30.1 %collective-permute-done.13.rest_8_ = bf16[512,512]{1,0:T(8,128)(2,1)} collective-permute-done((bf16[512,512]{1,0:T(8,128)(2,1)}, bf16[512,512]{1,0:T(8,128)(2,1)}, u32[]{:S(2)}, u32[]{:S(2)}) %collective-permute-start.13) | collective-permute-done | bytes 524320 | tf_op jit(solution)/shard_map/ppermute | solution.py:34
  107.5 2.9 %collective-permute-done.10.rest_2_ = bf16[2,512,512]{2,1,0:T(8,128)(2,1)S(1)} collective-permute-done((bf16[2,512,512]{2,1,0:T(8,128)(2,1)S(1)}, bf16[2,512,512]{2,1,0:T(8,128)(2,1)S(1)}, u32[]{:S(2)}, u32[]{:S(2)}) %collective-permute-start.10) | collective-permute-done | bytes 1048608 | tf_op jit(solution)/shard_map/ppermute | solution.py:42
  110.5 5.4 %project1.1 = (f32[256,512]{1,0:T(8,128)S(1)}, f32[256,512]{1,0:T(8,128)}) custom-call(s32[8]{0:T(128)S(1)} %stack.123.slots, bf16[2,512,512]{2,1,0:T(8,128)(2,1)S(1)} %pad_maximum_fusion.1.rest_0_, bf16[2,512,512]{2,1,0:T(8,128)(2,1)} %collective-permute-done.9.rest_1_, bf16[2,512,512]{2,1,0:T(8,128)(2,1)S(1)} %collective-permute-done.10.rest_2_, ...), custom_call_target="tpu_custom_call" | custom-call | flops 2147483648 | bytes 10485760 | tf_op jit(solution)/shard_map/project1/pallas_call | solution.py:308
  116.7 5.2 %project0.1 = (f32[256,512]{1,0:T(8,128)S(1)}, f32[256,512]{1,0:T(8,128)S(1)}) custom-call(s32[8]{0:T(128)S(1)} %stack.108.slots, bf16[2,512,512]{2,1,0:T(8,128)(2,1)S(1)} %pad_maximum_fusion.1.rest_0_, bf16[2,512,512]{2,1,0:T(8,128)(2,1)} %collective-permute-done.9.rest_1_, bf16[2,512,512]{2,1,0:T(8,128)(2,1)S(1)} %collective-permute-done.10.rest_2_, ...), custom_call_target="tpu_custom_call" | custom-call | flops 2147483648 | bytes 10485760 | tf_op jit(solution)/shard_map/project0/pallas_call | solution.py:308
  122.8 1.5 collective-permute-done.12.rest_1_
  124.3 5.8 %backward.1 = (bf16[256,1024]{1,0:T(8,128)(2,1)}, f32[8,256,256]{2,1,0:T(8,128)S(1)}, bf16[8,256,256]{2,1,0:T(8,128)(2,1)S(1)}) custom-call(s32[36]{0:T(128)S(1)} %concatenate.16.info, f32[256,512]{1,0:T(8,128)S(1)} %get-tuple-element.33.rest_0_, f32[256,512]{1,0:T(8,128)S(1)} %collective-permute-done.12.rest_1_, f32[256,512]{1,0:T(8,128)S(1)} %copy-done.11, ...), custom_call_target="tpu_custom_call" | custom-call | flops 8000000000 | bytes 10485760 | tf_op jit(solution)/shard_map/backward/pallas_call | solution.py:241
  130.1 1.6 collective-permute-start.16
  131.7 2.3 %collective-permute-done.16 = bf16[8,256,256]{2,1,0:T(8,128)(2,1)S(1)} collective-permute-done((bf16[8,256,256]{2,1,0:T(8,128)(2,1)S(1)}, bf16[8,256,256]{2,1,0:T(8,128)(2,1)S(1)}, u32[]{:S(2)}, u32[]{:S(2)}) %collective-permute-start.16) | collective-permute-done | bytes 1048608 | tf_op jit(solution)/shard_map/ppermute | solution.py:34
  134.3 32.8 %all_to_all.15 = bf16[8,256,256]{2,1,0:T(8,128)(2,1)S(1)} all-to-all(bf16[8,256,256]{2,1,0:T(8,128)(2,1)S(1)} %add_convert_fusion), channel_id=1, replica_groups={{0,16,32,48,64,80,96,112},{8,24,40,56,72,88,104,120},{1,17,33,49,65,81,..., dimensions={0} | all-to-all | bytes 2097152 | tf_op jit(solution)/shard_map/all_to_all | solution.py:410
  (74 shorter events, 18.7 us)
Async XLA Ops:
  1.6 1.3 collective-permute-start
  3.6 11.4 %collective-permute-start.1 = (bf16[512,128]{1,0:T(8,128)(2,1)}, bf16[512,128]{1,0:T(8,128)(2,1)}, u32[]{:S(2)}, u32[]{:S(2)}) collective-permute-start(bf16[512,128]{1,0:T(8,128)(2,1)} %pad_maximum_fusion.5), channel_id=1, source_target_pairs={{0,16},{8,24},{16,0},{24,8},{32,48},{40,56},{48,32},{56,40},{64,80... | collective-permute-start | bytes 393224 | tf_op jit(solution)/shard_map/ppermute | solution.py:34
  9.6 21.1 %collective-permute-start.4 = (bf16[512,512]{1,0:T(8,128)(2,1)}, bf16[512,512]{1,0:T(8,128)(2,1)S(1)}, u32[]{:S(2)}, u32[]{:S(2)}) collective-permute-start(bf16[512,512]{1,0:T(8,128)(2,1)} %get-tuple-element.38.rest_4_), channel_id=1, source_target_pairs={{0,64},{8,72},{16,80},{24,88},{32,96},{40,104},{48,112},{56,120},{... | collective-permute-start | bytes 1572872 | tf_op jit(solution)/shard_map/ppermute | solution.py:34
  12.6 24.9 %collective-permute-start.3 = (bf16[512,512]{1,0:T(8,128)(2,1)}, bf16[512,512]{1,0:T(8,128)(2,1)S(1)}, u32[]{:S(2)}, u32[]{:S(2)}) collective-permute-start(bf16[512,512]{1,0:T(8,128)(2,1)} %get-tuple-element.38.rest_4_), channel_id=1, source_target_pairs={{0,96},{8,104},{16,112},{24,120},{32,0},{40,8},{48,16},{56,24},{64... | collective-permute-start | bytes 1572872 | tf_op jit(solution)/shard_map/ppermute | solution.py:34
  13.8 23.7 %collective-permute-start.2 = (bf16[512,512]{1,0:T(8,128)(2,1)}, bf16[512,512]{1,0:T(8,128)(2,1)S(1)}, u32[]{:S(2)}, u32[]{:S(2)}) collective-permute-start(bf16[512,512]{1,0:T(8,128)(2,1)} %get-tuple-element.38.rest_4_), channel_id=1, source_target_pairs={{0,32},{8,40},{16,48},{24,56},{32,64},{40,72},{48,80},{56,88},{64,... | collective-permute-start | bytes 1572872 | tf_op jit(solution)/shard_map/ppermute | solution.py:34
  14.7 6.7 %collective-permute-start.6 = (bf16[256,512]{1,0:T(8,128)(2,1)S(1)}, bf16[256,512]{1,0:T(8,128)(2,1)S(1)}, u32[]{:S(2)}, u32[]{:S(2)}) collective-permute-start(bf16[256,512]{1,0:T(8,128)(2,1)S(1)} %get-tuple-element.50), channel_id=1, source_target_pairs={{0,8},{8,0},{16,24},{24,16},{32,40},{40,32},{48,56},{56,48},{64,72... | collective-permute-start | bytes 786440 | tf_op jit(solution)/shard_map/ppermute | solution.py:34
  17.0 30.6 %all-to-all-start = ((bf16[4,1024,128]{2,1,0:T(8,128)(2,1)}), bf16[4,1024,128]{2,1,0:T(8,128)(2,1)}, u32[]{:S(2)}, u32[]{:S(2)}) async-start(bf16[4,1024,128]{2,1,0:T(8,128)(2,1)} %broadcast_in_dim.31), calls=%async_computation | async-start | bytes 2097152 | tf_op jit(solution)/shard_map/all_to_all | solution.py:352
  21.3 16.4 %collective-permute-start.5 = (bf16[512,512]{1,0:T(8,128)(2,1)S(1)}, bf16[512,512]{1,0:T(8,128)(2,1)}, u32[]{:S(2)}, u32[]{:S(2)}) collective-permute-start(bf16[512,512]{1,0:T(8,128)(2,1)S(1)} %get-tuple-element.24), channel_id=1, source_target_pairs={{0,16},{8,24},{16,0},{24,8},{32,48},{40,56},{48,32},{56,40},{64,80... | collective-permute-start | bytes 1572872 | tf_op jit(solution)/shard_map/ppermute | solution.py:34
  22.3 24.2 %collective-permute-start.7 = (bf16[512,512]{1,0:T(8,128)(2,1)}, bf16[512,512]{1,0:T(8,128)(2,1)S(1)}, u32[]{:S(2)}, u32[]{:S(2)}) collective-permute-start(bf16[512,512]{1,0:T(8,128)(2,1)} %get-tuple-element.48), channel_id=1, source_target_pairs={{0,4},{1,5},{2,6},{3,7},{4,0},{5,1},{6,2},{7,3},{8,12},{9,13},{10,... | collective-permute-start | bytes 1572872 | tf_op jit(solution)/shard_map/ppermute | solution.py:42
  30.8 25.5 %copy-start = (bf16[512,512]{1,0:T(8,128)(2,1)}, bf16[512,512]{1,0:T(8,128)(2,1)S(1)}, u32[]{:S(2)}) copy-start(bf16[512,512]{1,0:T(8,128)(2,1)S(1)} %collective-permute-done.4.rest_7_) | copy-start | bytes 1572868
  37.5 18.8 %copy-start.4 = (bf16[512,512]{1,0:T(8,128)(2,1)}, bf16[512,512]{1,0:T(8,128)(2,1)S(1)}, u32[]{:S(2)}) copy-start(bf16[512,512]{1,0:T(8,128)(2,1)S(1)} %collective-permute-done.2.rest_5_) | copy-start | bytes 1572868
  51.3 65.4 %all-to-all-start.1 = ((bf16[4,2,512,512]{3,2,1,0:T(8,128)(2,1)}), bf16[4,2,512,512]{3,2,1,0:T(8,128)(2,1)}, u32[]{:S(2)}, u32[]{:S(2)}) async-start(bf16[4,2,512,512]{3,2,1,0:T(8,128)(2,1)} %broadcast_in_dim.34), calls=%async_computation.1 | async-start | bytes 8388608 | tf_op jit(solution)/shard_map/all_to_all | solution.py:352
  56.2 9.9 %collective-permute-start.8 = (bf16[4096,128]{1,0:T(8,128)(2,1)}, bf16[4096,128]{1,0:T(8,128)(2,1)S(1)}, u32[]{:S(2)}, u32[]{:S(2)}) collective-permute-start(bf16[4096,128]{1,0:T(8,128)(2,1)} %bitcast.here_ref.rest_7_), channel_id=1, source_target_pairs={{0,8},{8,0},{16,24},{24,16},{32,40},{40,32},{48,56},{56,48},{64,72... | collective-permute-start | bytes 3145736 | tf_op jit(solution)/shard_map/ppermute | solution.py:34
  57.7 52.8 %collective-permute-start.14 = (bf16[3,512,512]{2,1,0:T(8,128)(2,1)}, bf16[3,512,512]{2,1,0:T(8,128)(2,1)}, u32[]{:S(2)}, u32[]{:S(2)}) collective-permute-start(bf16[3,512,512]{2,1,0:T(8,128)(2,1)} %pad_maximum_fusion), channel_id=1, source_target_pairs={{0,16},{8,24},{16,0},{24,8},{32,48},{40,56},{48,32},{56,40},{64,80... | collective-permute-start | bytes 4718600 | tf_op jit(solution)/shard_map/ppermute | solution.py:34
  60.2 47.3 %collective-permute-start.11 = (bf16[2,512,512]{2,1,0:T(8,128)(2,1)S(1)}, bf16[2,512,512]{2,1,0:T(8,128)(2,1)S(1)}, u32[]{:S(2)}, u32[]{:S(2)}) collective-permute-start(bf16[2,512,512]{2,1,0:T(8,128)(2,1)S(1)} %pad_maximum_fusion.1.rest_0_), channel_id=1, source_target_pairs={{0,1},{1,2},{2,3},{3,0},{4,5},{5,6},{6,7},{7,4},{8,9},{9,10},{10,1... | collective-permute-start | bytes 3145736 | tf_op jit(solution)/shard_map/ppermute | solution.py:42
  61.8 48.6 %collective-permute-start.10 = (bf16[2,512,512]{2,1,0:T(8,128)(2,1)S(1)}, bf16[2,512,512]{2,1,0:T(8,128)(2,1)S(1)}, u32[]{:S(2)}, u32[]{:S(2)}) collective-permute-start(bf16[2,512,512]{2,1,0:T(8,128)(2,1)S(1)} %pad_maximum_fusion.1.rest_0_), channel_id=1, source_target_pairs={{0,2},{1,3},{2,0},{3,1},{4,6},{5,7},{6,4},{7,5},{8,10},{9,11},{10,... | collective-permute-start | bytes 3145736 | tf_op jit(solution)/shard_map/ppermute | solution.py:42
  64.7 45.7 %collective-permute-start.9 = (bf16[2,512,512]{2,1,0:T(8,128)(2,1)S(1)}, bf16[2,512,512]{2,1,0:T(8,128)(2,1)}, u32[]{:S(2)}, u32[]{:S(2)}) collective-permute-start(bf16[2,512,512]{2,1,0:T(8,128)(2,1)S(1)} %pad_maximum_fusion.1.rest_0_), channel_id=1, source_target_pairs={{0,3},{1,0},{2,1},{3,2},{4,7},{5,4},{6,5},{7,6},{8,11},{9,8},{10,9... | collective-permute-start | bytes 3145736 | tf_op jit(solution)/shard_map/ppermute | solution.py:42
  67.1 40.4 %collective-permute-start.13 = (bf16[512,512]{1,0:T(8,128)(2,1)}, bf16[512,512]{1,0:T(8,128)(2,1)}, u32[]{:S(2)}, u32[]{:S(2)}) collective-permute-start(bf16[512,512]{1,0:T(8,128)(2,1)} %get-tuple-element.38.rest_4_), channel_id=1, source_target_pairs={{0,16},{8,24},{16,0},{24,8},{32,48},{40,56},{48,32},{56,40},{64,80... | collective-permute-start | bytes 1572872 | tf_op jit(solution)/shard_map/ppermute | solution.py:34
  69.6 40.8 %copy-start.1 = (bf16[512,512]{1,0:T(8,128)(2,1)S(1)}, bf16[512,512]{1,0:T(8,128)(2,1)}, u32[]{:S(2)}) copy-start(bf16[512,512]{1,0:T(8,128)(2,1)} %copy-done) | copy-start | bytes 1572868
  69.6 40.9 %copy-start.3 = (bf16[512,512]{1,0:T(8,128)(2,1)S(1)}, bf16[512,512]{1,0:T(8,128)(2,1)}, u32[]{:S(2)}) copy-start(bf16[512,512]{1,0:T(8,128)(2,1)} %copy-done.2) | copy-start | bytes 1572868
  69.6 40.9 %copy-start.5 = (bf16[512,512]{1,0:T(8,128)(2,1)S(1)}, bf16[512,512]{1,0:T(8,128)(2,1)}, u32[]{:S(2)}) copy-start(bf16[512,512]{1,0:T(8,128)(2,1)} %copy-done.4) | copy-start | bytes 1572868
  116.7 6.0 %collective-permute-start.15 = (f32[256,512]{1,0:T(8,128)}, f32[256,512]{1,0:T(8,128)}, u32[]{:S(2)}, u32[]{:S(2)}) collective-permute-start(f32[256,512]{1,0:T(8,128)} %get-tuple-element.40), channel_id=1, source_target_pairs={{0,8},{8,0},{16,24},{24,16},{32,40},{40,32},{48,56},{56,48},{64,72... | collective-permute-start | bytes 1572872 | tf_op jit(solution)/shard_map/ppermute | solution.py:34
  122.0 2.3 %collective-permute-start.12 = (f32[256,512]{1,0:T(8,128)S(1)}, f32[256,512]{1,0:T(8,128)S(1)}, u32[]{:S(2)}, u32[]{:S(2)}) collective-permute-start(f32[256,512]{1,0:T(8,128)S(1)} %get-tuple-element.34), channel_id=1, source_target_pairs={{0,8},{8,0},{16,24},{24,16},{32,40},{40,32},{48,56},{56,48},{64,72... | collective-permute-start | bytes 1572872 | tf_op jit(solution)/shard_map/ppermute | solution.py:34
  130.1 3.9 %collective-permute-start.16 = (bf16[8,256,256]{2,1,0:T(8,128)(2,1)S(1)}, bf16[8,256,256]{2,1,0:T(8,128)(2,1)S(1)}, u32[]{:S(2)}, u32[]{:S(2)}) collective-permute-start(bf16[8,256,256]{2,1,0:T(8,128)(2,1)S(1)} %get-tuple-element.44), channel_id=1, source_target_pairs={{0,8},{8,0},{16,24},{24,16},{32,40},{40,32},{48,56},{56,48},{64,72... | collective-permute-start | bytes 3145736 | tf_op jit(solution)/shard_map/ppermute | solution.py:34
  (10 other events, 84.4 us)

commit v17 on v15

--- a/solution.py
+++ b/solution.py
@@ -365,28 +365,30 @@
     mine = lax.dynamic_slice_in_dim(grad_out, core * depth, depth, 1)
     other = lax.dynamic_slice_in_dim(grad_out, (1 - core) * depth, depth, 1)
     chip_grad = jnp.concatenate([mine, dp_move(other, 0, 0, 1)], axis=0)
-    all_grad = [chip_grad] + [tensor_move(chip_grad, 0, step) for step in (-1, -2, 1)]
 
     def around_x(block):
         return [dp_move(block, step, 0, 0) for step in (1, -1, 2)]
+
+    def around_y(block):
+        return [tensor_move(block, 0, step) for step in (-1, -2, 1)]
 
     own = [out_weight[:SPLIT], out_weight[SPLIT:]]
     plane1 = around_x(own[1])
     own0 = after(own[0], chip_pair)
     pair0 = dp_move(own0, 0, 1, 0)
     grad_pair = tensor_move(chip_grad, 1, 0)
-    ring, plane1, all_grad, pair0, grad_pair, info, query_pos, query_start = lax.optimization_barrier(
-        (ring, plane1, all_grad, pair0, grad_pair, info, query_pos, query_start)
+    plane1, chip_grad = lax.optimization_barrier((plane1, chip_grad))
+    rest = dp_move(jnp.stack([own[1], *plane1]), 0, 1, 0)
+    grads_own = around_y(chip_grad)
+    copies = copy(jnp.stack([own0, pair0]), groups_x)
+    ring, copies, grad_pair, info, query_pos, query_start = lax.optimization_barrier(
+        (ring, copies, grad_pair, info, query_pos, query_start)
     )
-    plane0 = around_x(own0)
-    all_grad += [grad_pair] + [tensor_move(grad_pair, 0, step) for step in (-1, -2, 1)]
-    rest = jnp.stack(plane1)
+    plane0 = exchange(copies, "dp", groups_x).reshape(8, SPLIT, depth)
     swapped = dp_move(ring, 0, 0, 1)
-    swapped, copies, rest = lax.optimization_barrier((swapped, copy(pair0, groups_x), rest))
-    other_plane = exchange(copies, "dp", groups_x).reshape(4, SPLIT, depth)
-    pair1 = dp_move(after(own[1], ring), 0, 1, 0)
-    rest = dp_move(rest, 0, 1, 0)
-    probs, outs = forward(info, query_pos, query_start, queries, ring, swapped)
+    grads_own, grad_pair, later = lax.optimization_barrier((grads_own, grad_pair, queries))
+    all_grad = [chip_grad, *grads_own, grad_pair, *around_y(grad_pair)]
+    probs, outs = forward(info, query_pos, query_start, later, ring, swapped)
 
     t = lax.axis_index("tensor")
 
@@ -396,15 +398,14 @@
 
     near = [slot(x + i, z) for i in (0, -1, 1, 2)]
     slots = [
-        jnp.stack(near + [slot(i, 1 - z) for i in range(4)]).astype(jnp.int32),
+        jnp.stack([slot(i, z_) for i in range(4) for z_ in (z, 1 - z)]).astype(jnp.int32),
         jnp.stack(near + [slot(x + i, 1 - z) for i in (0, -1, 1, 2)]).astype(jnp.int32),
     ]
-    slots[0] = after(slots[0], outs)
-    stacks = [[own0, *plane0, other_plane], [own[1], *plane1, pair1, rest]]
-    terms = []
-    for part in range(CHUNKS):
-        mine, other = project(part, slots[part], all_grad, stacks[part])
-        terms += [mine, dp_move(other, 0, 0, 1)]
+    slots = list(lax.optimization_barrier((*slots, outs))[:2])
+    stacks = [[plane0], [own[1], *plane1, rest]]
+    mine1, other1 = project(1, slots[1], all_grad, stacks[1])
+    mine0, other0 = project(0, slots[0], all_grad, stacks[0])
+    terms = [mine0, dp_move(other0, 0, 0, 1), mine1, dp_move(other1, 0, 0, 1)]
     grad_queries, own_sums, other_sums = backward(info, terms, probs, outs, queries, ring, swapped)
 
     groups = [[2 * i + c for i in range(8)] for c in range(2)]

time: 210 us -> 243 us (1.16)
  waiting for transfers between devices: 75.5 us -> 120 us
  blocking collectives: 40.1 us -> 31.8 us
  starting transfers between devices: 40 us -> 37.5 us
    ppermute x7, waiting for transfers between devices: 13.4 us -> 44.1 us  [tensor_move(): return lax.ppermute(value, 'tensor', pairs)]
    ppermute x16 -> x12, waiting for transfers between devices: 62.1 us -> 76 us  [dp_move(): return lax.ppermute(value, 'dp', pairs)]
    all_to_all x1, blocking collectives: 40.1 us -> 31.8 us  [local(): lax.all_to_all(chip_sums, 'dp', 0, 0, axis_index_groups=groups, tiled=True)]
    unnamed x32, local copies, waits for them, and re-layouts: 7.54 us -> 4.53 us
    ppermute x16 -> x12, starting transfers between devices: 20 us -> 17 us  [dp_move(): return lax.ppermute(value, 'dp', pairs)]
    another operation x2 -> x3, other arithmetic: 2.88 us -> 5.08 us  [the longest x1 2.79 us: local(): rest = dp_move(jnp.stack([own[1], *plane1]), 0, 1, 0)]
  transfers between devices with their start and end apart: 25 -> 21, of which waited for: 9 -> 12; matrix products, arithmetic and copies ran while one was open for 4% -> 5% of each run, Pallas kernels for 9% -> 8%
where the time goes in v17:
time: 243 us; the launch traced here: 242 us
  waiting for transfers between devices  120 us (49%)
  starting transfers between devices  37.5 us (15%)
  blocking collectives  31.8 us (13%)
  Pallas kernels  24.5 us (10%)
  local copies, waits for them, and re-layouts  14.5 us (6%)
  between operations  6.84 us (3%)
  other arithmetic  6.6 us (3%)
    ppermute x12, waiting for transfers between devices, dp_move(): return lax.ppermute(value, 'dp', pairs)  76 us
    ppermute x7, waiting for transfers between devices, tensor_move(): return lax.ppermute(value, 'tensor', pairs)  44.1 us
    all_to_all x1, blocking collectives, local(): lax.all_to_all(chip_sums, 'dp', 0, 0, axis_index_groups=groups, tiled=True)  31.8 us
    ppermute x12, starting transfers between devices, dp_move(): return lax.ppermute(value, 'dp', pairs)  17 us
    ppermute x7, starting transfers between devices, tensor_move(): return lax.ppermute(value, 'tensor', pairs)  11.3 us
    pallas_call x2, Pallas kernels, project(): pl.pallas_call(functools.partial(project_kernel, chips), grid=(1,), in_sp...  10.8 us
    all_to_all x2, starting transfers between devices, exchange(): lax.all_to_all(copies, axis, 0, 0, axis_index_groups=groups, tiled=True)  9.18 us
    pallas_call x1, Pallas kernels, forward(): pl.pallas_call(forward_kernel, grid_spec=pltpu.PrefetchScalarGridSpec(num...  7.93 us
  transfers between devices with their start and end apart: 21, of which 12 were waited for; matrix products, arithmetic and copies ran while one was open for 5% of the time, Pallas kernels for 8%

profile of v17, /device:TPU:0, one launch (start us, length us, event | category | flops | bytes accessed | tf_op | source)
XLA Modules:
  0.0 241.9 jit_solution(2210252090194115052)
XLA Ops:
  5.6 4.0 %collective-permute-start.1 = (bf16[512,128]{1,0:T(8,128)(2,1)S(1)}, bf16[512,128]{1,0:T(8,128)(2,1)S(1)}, u32[]{:S(2)}, u32[]{:S(2)}) collective-permute-start(bf16[512,128]{1,0:T(8,128)(2,1)S(1)} %pad_maximum_fusion.4), channel_id=1, source_target_pairs={{0,16},{8,24},{16,0},{24,8},{32,48},{40,56},{48,32},{56,40},{64,80... | collective-permute-start | bytes 393224 | tf_op jit(solution)/shard_map/ppermute | solution.py:34
  9.6 3.7 %collective-permute-done.1 = bf16[512,128]{1,0:T(8,128)(2,1)S(1)} collective-permute-done((bf16[512,128]{1,0:T(8,128)(2,1)S(1)}, bf16[512,128]{1,0:T(8,128)(2,1)S(1)}, u32[]{:S(2)}, u32[]{:S(2)}) %collective-permute-start.1) | collective-permute-done | bytes 131104 | tf_op jit(solution)/shard_map/ppermute | solution.py:34
  14.4 4.3 %all-to-all-start = ((bf16[4,1024,128]{2,1,0:T(8,128)(2,1)}), bf16[4,1024,128]{2,1,0:T(8,128)(2,1)S(1)}, u32[]{:S(2)}, u32[]{:S(2)}) async-start(bf16[4,1024,128]{2,1,0:T(8,128)(2,1)} %broadcast_in_dim.31), calls=%async_computation | async-start | bytes 2097152 | tf_op jit(solution)/shard_map/all_to_all | solution.py:352
  18.7 3.2 %collective-permute-start.2 = (bf16[512,512]{1,0:T(8,128)(2,1)S(1)}, bf16[512,512]{1,0:T(8,128)(2,1)}, u32[]{:S(2)}, u32[]{:S(2)}) collective-permute-start(bf16[512,512]{1,0:T(8,128)(2,1)S(1)} %get-tuple-element.30), channel_id=1, source_target_pairs={{0,16},{8,24},{16,0},{24,8},{32,48},{40,56},{48,32},{56,40},{64,80... | collective-permute-start | bytes 1572872 | tf_op jit(solution)/shard_map/ppermute | solution.py:34
  30.6 4.7 %collective-permute-done.2 = bf16[512,512]{1,0:T(8,128)(2,1)} collective-permute-done((bf16[512,512]{1,0:T(8,128)(2,1)S(1)}, bf16[512,512]{1,0:T(8,128)(2,1)}, u32[]{:S(2)}, u32[]{:S(2)}) %collective-permute-start.2) | collective-permute-done | bytes 524320 | tf_op jit(solution)/shard_map/ppermute | solution.py:34
  35.2 2.1 pad_maximum_fusion.1
  37.3 7.6 %collective-permute-done.4.rest_4_ = bf16[512,512]{1,0:T(8,128)(2,1)S(1)} collective-permute-done((bf16[512,512]{1,0:T(8,128)(2,1)S(1)}, bf16[512,512]{1,0:T(8,128)(2,1)S(1)}, u32[]{:S(2)}, u32[]{:S(2)}) %collective-permute-start.4) | collective-permute-done | bytes 524320 | tf_op jit(solution)/shard_map/ppermute | solution.py:42
  45.0 3.5 %broadcast_in_dim.32 = bf16[4,2,512,512]{3,2,1,0:T(8,128)(2,1)} broadcast(bf16[2,512,512]{2,1,0:T(8,128)(2,1)} %pad_maximum_fusion.1), dimensions={1,2,3} | broadcast | bytes 5242880 | tf_op jit(solution)/shard_map/broadcast_in_dim | solution.py:349
  48.5 4.9 %all-to-all-start.1 = ((bf16[4,2,512,512]{3,2,1,0:T(8,128)(2,1)}), bf16[4,2,512,512]{3,2,1,0:T(8,128)(2,1)}, u32[]{:S(2)}, u32[]{:S(2)}) async-start(bf16[4,2,512,512]{3,2,1,0:T(8,128)(2,1)} %broadcast_in_dim.32), calls=%async_computation.1 | async-start | bytes 8388608 | tf_op jit(solution)/shard_map/all_to_all | solution.py:352
  53.4 3.5 %collective-permute-start.7 = (bf16[512,512]{1,0:T(8,128)(2,1)S(1)}, bf16[512,512]{1,0:T(8,128)(2,1)S(1)}, u32[]{:S(2)}, u32[]{:S(2)}) collective-permute-start(bf16[512,512]{1,0:T(8,128)(2,1)S(1)} %get-tuple-element.58.rest_8_), channel_id=1, source_target_pairs={{0,64},{8,72},{16,80},{24,88},{32,96},{40,104},{48,112},{56,120},{... | collective-permute-start | bytes 1572872 | tf_op jit(solution)/shard_map/ppermute | solution.py:34
  58.9 56.0 %collective-permute-done.7.rest_11_ = bf16[512,512]{1,0:T(8,128)(2,1)S(1)} collective-permute-done((bf16[512,512]{1,0:T(8,128)(2,1)S(1)}, bf16[512,512]{1,0:T(8,128)(2,1)S(1)}, u32[]{:S(2)}, u32[]{:S(2)}) %collective-permute-start.7) | collective-permute-done | bytes 524320 | tf_op jit(solution)/shard_map/ppermute | solution.py:34
  114.9 6.7 %collective-permute-done.6.rest_10_ = bf16[512,512]{1,0:T(8,128)(2,1)S(1)} collective-permute-done((bf16[512,512]{1,0:T(8,128)(2,1)S(1)}, bf16[512,512]{1,0:T(8,128)(2,1)S(1)}, u32[]{:S(2)}, u32[]{:S(2)}) %collective-permute-start.6) | collective-permute-done | bytes 524320 | tf_op jit(solution)/shard_map/ppermute | solution.py:34
  122.7 2.8 %pad_maximum_fusion = bf16[4,512,512]{2,1,0:T(8,128)(2,1)} fusion(bf16[1,512,512]{2,1,0:T(8,128)(2,1)S(1)} %bitcast.39, bf16[1,512,512]{2,1,0:T(8,128)(2,1)S(1)} %bitcast.40, bf16[1,512,512]{2,1,0:T(8,128)(2,1)S(1)} %bitcast.41, bf16[1,512,512]{2,1,0:T(8,128)(2,1)} %get-tuple-element.57), kind=kLoop, calls=%fused_computation | loop fusion | flops 3145728 | bytes 4194304 | tf_op jit(solution)/shard_map/stack | solution.py:381
  128.4 2.9 %collective-permute-start.9 = (bf16[512,512]{1,0:T(8,128)(2,1)S(1)}, bf16[512,512]{1,0:T(8,128)(2,1)S(1)}, u32[]{:S(2)}, u32[]{:S(2)}) collective-permute-start(bf16[512,512]{1,0:T(8,128)(2,1)S(1)} %pad_maximum_fusion.2.rest_0_), channel_id=1, source_target_pairs={{0,2},{1,3},{2,0},{3,1},{4,6},{5,7},{6,4},{7,5},{8,10},{9,11},{10,... | collective-permute-start | bytes 1572872 | tf_op jit(solution)/shard_map/ppermute | solution.py:42
  132.6 9.8 %collective-permute-done.10.rest_3_ = bf16[512,512]{1,0:T(8,128)(2,1)S(1)} collective-permute-done((bf16[512,512]{1,0:T(8,128)(2,1)S(1)}, bf16[512,512]{1,0:T(8,128)(2,1)S(1)}, u32[]{:S(2)}, u32[]{:S(2)}) %collective-permute-start.10) | collective-permute-done | bytes 524320 | tf_op jit(solution)/shard_map/ppermute | solution.py:42
  142.4 12.4 %collective-permute-done.9.rest_2_ = bf16[512,512]{1,0:T(8,128)(2,1)S(1)} collective-permute-done((bf16[512,512]{1,0:T(8,128)(2,1)S(1)}, bf16[512,512]{1,0:T(8,128)(2,1)S(1)}, u32[]{:S(2)}, u32[]{:S(2)}) %collective-permute-start.9) | collective-permute-done | bytes 524320 | tf_op jit(solution)/shard_map/ppermute | solution.py:42
  156.7 2.4 collective-permute-start.13
  161.0 7.9 %forward.1 = (bf16[2816,2048]{1,0:T(8,128)(2,1)}, f32[128,2048]{1,0:T(8,128)}) custom-call(s32[36]{0:T(128)S(1)} %concatenate.16.info, s32[1,256]{1,0:T(1,128)S(1)} %iota_add_fusion.pos_ref, s32[1,256]{1,0:T(1,128)S(1)} %bitcast.42, bf16[256,1024]{1,0:T(8,128)(2,1)} %rest_6_.1, bf16[4096,128]{1,0:T(8,128)(2,1)S(1)} %bitcast.37, ...), custom_call_target="tpu_custom_call" | custom-call | flops 100000000 | bytes 1048576 | tf_op jit(solution)/shard_map/forward/pallas_call | solution.py:141
  169.0 13.7 %collective-permute-done.14.rest_7_ = bf16[512,512]{1,0:T(8,128)(2,1)} collective-permute-done((bf16[512,512]{1,0:T(8,128)(2,1)S(1)}, bf16[512,512]{1,0:T(8,128)(2,1)}, u32[]{:S(2)}, u32[]{:S(2)}) %collective-permute-start.14) | collective-permute-done | bytes 524320 | tf_op jit(solution)/shard_map/ppermute | solution.py:42
  183.3 5.5 %project1.1 = (f32[256,512]{1,0:T(8,128)S(1)}, f32[256,512]{1,0:T(8,128)}) custom-call(s32[8]{0:T(128)S(1)} %stack.114.slots, bf16[512,512]{1,0:T(8,128)(2,1)S(1)} %pad_maximum_fusion.2.rest_0_, bf16[512,512]{1,0:T(8,128)(2,1)S(1)} %copy-done.4, bf16[512,512]{1,0:T(8,128)(2,1)S(1)} %copy-done.1, bf16[512,512]{1,0:T(8,128)(2,1)S(1)} %collective-permute-done.10.rest_3_, ...), custom_call_target="tpu_custom_call" | custom-call | flops 2147483648 | bytes 10485760 | tf_op jit(solution)/shard_map/project1/pallas_call | solution.py:308
  191.7 5.4 %project0.1 = (f32[256,512]{1,0:T(8,128)S(1)}, f32[256,512]{1,0:T(8,128)S(1)}) custom-call(s32[8]{0:T(128)S(1)} %stack.105.slots, bf16[512,512]{1,0:T(8,128)(2,1)S(1)} %pad_maximum_fusion.2.rest_0_, bf16[512,512]{1,0:T(8,128)(2,1)S(1)} %copy-done.5, bf16[512,512]{1,0:T(8,128)(2,1)S(1)} %copy-done.2, bf16[512,512]{1,0:T(8,128)(2,1)S(1)} %collective-permute-done.10.rest_3_, ...), custom_call_target="tpu_custom_call" | custom-call | flops 2147483648 | bytes 10485760 | tf_op jit(solution)/shard_map/project0/pallas_call | solution.py:308
  199.3 5.8 %backward.1 = (bf16[256,1024]{1,0:T(8,128)(2,1)}, f32[8,256,256]{2,1,0:T(8,128)S(1)}, bf16[8,256,256]{2,1,0:T(8,128)(2,1)S(1)}) custom-call(s32[36]{0:T(128)S(1)} %concatenate.16.info, f32[256,512]{1,0:T(8,128)S(1)} %get-tuple-element.45.rest_0_, f32[256,512]{1,0:T(8,128)S(1)} %collective-permute-done.15.rest_1_, f32[256,512]{1,0:T(8,128)S(1)} %copy-done.14, ...), custom_call_target="tpu_custom_call" | custom-call | flops 8000000000 | bytes 10485760 | tf_op jit(solution)/shard_map/backward/pallas_call | solution.py:241
  206.7 2.3 collective-permute-done.18
  209.3 31.8 %all_to_all.15 = bf16[8,256,256]{2,1,0:T(8,128)(2,1)S(1)} all-to-all(bf16[8,256,256]{2,1,0:T(8,128)(2,1)S(1)} %add_convert_fusion), channel_id=1, replica_groups={{0,16,32,48,64,80,96,112},{8,24,40,56,72,88,104,120},{1,17,33,49,65,81,..., dimensions={0} | all-to-all | bytes 2097152 | tf_op jit(solution)/shard_map/all_to_all | solution.py:413
  (79 shorter events, 28.3 us)
Async XLA Ops:
  1.5 4.0 %collective-permute-start = (bf16[256,128]{1,0:T(8,128)(2,1)S(1)}, bf16[256,128]{1,0:T(8,128)(2,1)S(1)}, u32[]{:S(2)}, u32[]{:S(2)}) collective-permute-start(bf16[256,128]{1,0:T(8,128)(2,1)S(1)} %get-tuple-element.65), channel_id=1, source_target_pairs={{0,8},{8,0},{16,24},{24,16},{32,40},{40,32},{48,56},{56,48},{64,72... | collective-permute-start | bytes 196616 | tf_op jit(solution)/shard_map/ppermute | solution.py:34
  2.7 19.3 %collective-permute-start.3 = (bf16[256,512]{1,0:T(8,128)(2,1)S(1)}, bf16[256,512]{1,0:T(8,128)(2,1)S(1)}, u32[]{:S(2)}, u32[]{:S(2)}) collective-permute-start(bf16[256,512]{1,0:T(8,128)(2,1)S(1)} %get-tuple-element.61), channel_id=1, source_target_pairs={{0,8},{8,0},{16,24},{24,16},{32,40},{40,32},{48,56},{56,48},{64,72... | collective-permute-start | bytes 786440 | tf_op jit(solution)/shard_map/ppermute | solution.py:34
  5.6 7.7 %collective-permute-start.1 = (bf16[512,128]{1,0:T(8,128)(2,1)S(1)}, bf16[512,128]{1,0:T(8,128)(2,1)S(1)}, u32[]{:S(2)}, u32[]{:S(2)}) collective-permute-start(bf16[512,128]{1,0:T(8,128)(2,1)S(1)} %pad_maximum_fusion.4), channel_id=1, source_target_pairs={{0,16},{8,24},{16,0},{24,8},{32,48},{40,56},{48,32},{56,40},{64,80... | collective-permute-start | bytes 393224 | tf_op jit(solution)/shard_map/ppermute | solution.py:34
  14.4 30.5 %all-to-all-start = ((bf16[4,1024,128]{2,1,0:T(8,128)(2,1)}), bf16[4,1024,128]{2,1,0:T(8,128)(2,1)S(1)}, u32[]{:S(2)}, u32[]{:S(2)}) async-start(bf16[4,1024,128]{2,1,0:T(8,128)(2,1)} %broadcast_in_dim.31), calls=%async_computation | async-start | bytes 2097152 | tf_op jit(solution)/shard_map/all_to_all | solution.py:352
  18.7 16.5 %collective-permute-start.2 = (bf16[512,512]{1,0:T(8,128)(2,1)S(1)}, bf16[512,512]{1,0:T(8,128)(2,1)}, u32[]{:S(2)}, u32[]{:S(2)}) collective-permute-start(bf16[512,512]{1,0:T(8,128)(2,1)S(1)} %get-tuple-element.30), channel_id=1, source_target_pairs={{0,16},{8,24},{16,0},{24,8},{32,48},{40,56},{48,32},{56,40},{64,80... | collective-permute-start | bytes 1572872 | tf_op jit(solution)/shard_map/ppermute | solution.py:34
  22.0 22.9 %collective-permute-start.4 = (bf16[512,512]{1,0:T(8,128)(2,1)S(1)}, bf16[512,512]{1,0:T(8,128)(2,1)S(1)}, u32[]{:S(2)}, u32[]{:S(2)}) collective-permute-start(bf16[512,512]{1,0:T(8,128)(2,1)S(1)} %pad_maximum_fusion.2.rest_0_), channel_id=1, source_target_pairs={{0,4},{1,5},{2,6},{3,7},{4,0},{5,1},{6,2},{7,3},{8,12},{9,13},{10,... | collective-permute-start | bytes 1572872 | tf_op jit(solution)/shard_map/ppermute | solution.py:42
  48.5 141.1 %all-to-all-start.1 = ((bf16[4,2,512,512]{3,2,1,0:T(8,128)(2,1)}), bf16[4,2,512,512]{3,2,1,0:T(8,128)(2,1)}, u32[]{:S(2)}, u32[]{:S(2)}) async-start(bf16[4,2,512,512]{3,2,1,0:T(8,128)(2,1)} %broadcast_in_dim.32), calls=%async_computation.1 | async-start | bytes 8388608 | tf_op jit(solution)/shard_map/all_to_all | solution.py:352
  53.4 61.5 %collective-permute-start.7 = (bf16[512,512]{1,0:T(8,128)(2,1)S(1)}, bf16[512,512]{1,0:T(8,128)(2,1)S(1)}, u32[]{:S(2)}, u32[]{:S(2)}) collective-permute-start(bf16[512,512]{1,0:T(8,128)(2,1)S(1)} %get-tuple-element.58.rest_8_), channel_id=1, source_target_pairs={{0,64},{8,72},{16,80},{24,88},{32,96},{40,104},{48,112},{56,120},{... | collective-permute-start | bytes 1572872 | tf_op jit(solution)/shard_map/ppermute | solution.py:34
  56.9 64.7 %collective-permute-start.6 = (bf16[512,512]{1,0:T(8,128)(2,1)S(1)}, bf16[512,512]{1,0:T(8,128)(2,1)S(1)}, u32[]{:S(2)}, u32[]{:S(2)}) collective-permute-start(bf16[512,512]{1,0:T(8,128)(2,1)S(1)} %get-tuple-element.58.rest_8_), channel_id=1, source_target_pairs={{0,96},{8,104},{16,112},{24,120},{32,0},{40,8},{48,16},{56,24},{64... | collective-permute-start | bytes 1572872 | tf_op jit(solution)/shard_map/ppermute | solution.py:34
  58.0 64.7 %collective-permute-start.5 = (bf16[512,512]{1,0:T(8,128)(2,1)S(1)}, bf16[512,512]{1,0:T(8,128)(2,1)S(1)}, u32[]{:S(2)}, u32[]{:S(2)}) collective-permute-start(bf16[512,512]{1,0:T(8,128)(2,1)S(1)} %get-tuple-element.58.rest_8_), channel_id=1, source_target_pairs={{0,32},{8,40},{16,48},{24,56},{32,64},{40,72},{48,80},{56,88},{64,... | collective-permute-start | bytes 1572872 | tf_op jit(solution)/shard_map/ppermute | solution.py:34
  125.5 57.7 %collective-permute-start.16 = (bf16[4,512,512]{2,1,0:T(8,128)(2,1)}, bf16[4,512,512]{2,1,0:T(8,128)(2,1)}, u32[]{:S(2)}, u32[]{:S(2)}) collective-permute-start(bf16[4,512,512]{2,1,0:T(8,128)(2,1)} %pad_maximum_fusion), channel_id=1, source_target_pairs={{0,16},{8,24},{16,0},{24,8},{32,48},{40,56},{48,32},{56,40},{64,80... | collective-permute-start | bytes 6291464 | tf_op jit(solution)/shard_map/ppermute | solution.py:34
  126.8 34.2 %collective-permute-start.11 = (bf16[4096,128]{1,0:T(8,128)(2,1)S(1)}, bf16[4096,128]{1,0:T(8,128)(2,1)}, u32[]{:S(2)}, u32[]{:S(2)}) collective-permute-start(bf16[4096,128]{1,0:T(8,128)(2,1)S(1)} %bitcast.36), channel_id=1, source_target_pairs={{0,8},{8,0},{16,24},{24,16},{32,40},{40,32},{48,56},{56,48},{64,72... | collective-permute-start | bytes 3145736 | tf_op jit(solution)/shard_map/ppermute | solution.py:34
  126.8 15.6 %collective-permute-start.10 = (bf16[512,512]{1,0:T(8,128)(2,1)S(1)}, bf16[512,512]{1,0:T(8,128)(2,1)S(1)}, u32[]{:S(2)}, u32[]{:S(2)}) collective-permute-start(bf16[512,512]{1,0:T(8,128)(2,1)S(1)} %pad_maximum_fusion.2.rest_0_), channel_id=1, source_target_pairs={{0,1},{1,2},{2,3},{3,0},{4,5},{5,6},{6,7},{7,4},{8,9},{9,10},{10,1... | collective-permute-start | bytes 1572872 | tf_op jit(solution)/shard_map/ppermute | solution.py:42
  128.4 26.4 %collective-permute-start.9 = (bf16[512,512]{1,0:T(8,128)(2,1)S(1)}, bf16[512,512]{1,0:T(8,128)(2,1)S(1)}, u32[]{:S(2)}, u32[]{:S(2)}) collective-permute-start(bf16[512,512]{1,0:T(8,128)(2,1)S(1)} %pad_maximum_fusion.2.rest_0_), channel_id=1, source_target_pairs={{0,2},{1,3},{2,0},{3,1},{4,6},{5,7},{6,4},{7,5},{8,10},{9,11},{10,... | collective-permute-start | bytes 1572872 | tf_op jit(solution)/shard_map/ppermute | solution.py:42
  131.3 24.3 %collective-permute-start.8 = (bf16[512,512]{1,0:T(8,128)(2,1)S(1)}, bf16[512,512]{1,0:T(8,128)(2,1)S(1)}, u32[]{:S(2)}, u32[]{:S(2)}) collective-permute-start(bf16[512,512]{1,0:T(8,128)(2,1)S(1)} %pad_maximum_fusion.2.rest_0_), channel_id=1, source_target_pairs={{0,3},{1,0},{2,1},{3,2},{4,7},{5,4},{6,5},{7,6},{8,11},{9,8},{10,9... | collective-permute-start | bytes 1572872 | tf_op jit(solution)/shard_map/ppermute | solution.py:42
  156.4 26.2 %collective-permute-start.14 = (bf16[512,512]{1,0:T(8,128)(2,1)S(1)}, bf16[512,512]{1,0:T(8,128)(2,1)}, u32[]{:S(2)}, u32[]{:S(2)}) collective-permute-start(bf16[512,512]{1,0:T(8,128)(2,1)S(1)} %collective-permute-done.4.rest_4_), channel_id=1, source_target_pairs={{0,1},{1,2},{2,3},{3,0},{4,5},{5,6},{6,7},{7,4},{8,9},{9,10},{10,1... | collective-permute-start | bytes 1572872 | tf_op jit(solution)/shard_map/ppermute | solution.py:42
  156.7 25.9 %collective-permute-start.13 = (bf16[512,512]{1,0:T(8,128)(2,1)S(1)}, bf16[512,512]{1,0:T(8,128)(2,1)}, u32[]{:S(2)}, u32[]{:S(2)}) collective-permute-start(bf16[512,512]{1,0:T(8,128)(2,1)S(1)} %collective-permute-done.4.rest_4_), channel_id=1, source_target_pairs={{0,2},{1,3},{2,0},{3,1},{4,6},{5,7},{6,4},{7,5},{8,10},{9,11},{10,... | collective-permute-start | bytes 1572872 | tf_op jit(solution)/shard_map/ppermute | solution.py:42
  159.1 24.1 %collective-permute-start.12 = (bf16[512,512]{1,0:T(8,128)(2,1)S(1)}, bf16[512,512]{1,0:T(8,128)(2,1)}, u32[]{:S(2)}, u32[]{:S(2)}) collective-permute-start(bf16[512,512]{1,0:T(8,128)(2,1)S(1)} %collective-permute-done.4.rest_4_), channel_id=1, source_target_pairs={{0,3},{1,0},{2,1},{3,2},{4,7},{5,4},{6,5},{7,6},{8,11},{9,8},{10,9... | collective-permute-start | bytes 1572872 | tf_op jit(solution)/shard_map/ppermute | solution.py:42
  161.0 22.3 %copy-start.1 = (bf16[512,512]{1,0:T(8,128)(2,1)S(1)}, bf16[512,512]{1,0:T(8,128)(2,1)}, u32[]{:S(2)}) copy-start(bf16[512,512]{1,0:T(8,128)(2,1)} %copy-done) | copy-start | bytes 1572868
  161.0 22.3 %copy-start.4 = (bf16[512,512]{1,0:T(8,128)(2,1)S(1)}, bf16[512,512]{1,0:T(8,128)(2,1)}, u32[]{:S(2)}) copy-start(bf16[512,512]{1,0:T(8,128)(2,1)} %copy-done.3) | copy-start | bytes 1572868
  161.0 22.3 %copy-start.7 = (bf16[512,512]{1,0:T(8,128)(2,1)S(1)}, bf16[512,512]{1,0:T(8,128)(2,1)}, u32[]{:S(2)}) copy-start(bf16[512,512]{1,0:T(8,128)(2,1)} %copy-done.6) | copy-start | bytes 1572868
  189.6 8.2 %collective-permute-start.17 = (f32[256,512]{1,0:T(8,128)}, f32[256,512]{1,0:T(8,128)}, u32[]{:S(2)}, u32[]{:S(2)}) collective-permute-start(f32[256,512]{1,0:T(8,128)} %get-tuple-element.52), channel_id=1, source_target_pairs={{0,8},{8,0},{16,24},{24,16},{32,40},{40,32},{48,56},{56,48},{64,72... | collective-permute-start | bytes 1572872 | tf_op jit(solution)/shard_map/ppermute | solution.py:34
  197.0 2.3 collective-permute-start.15
  205.1 3.8 %collective-permute-start.18 = (bf16[8,256,256]{2,1,0:T(8,128)(2,1)S(1)}, bf16[8,256,256]{2,1,0:T(8,128)(2,1)S(1)}, u32[]{:S(2)}, u32[]{:S(2)}) collective-permute-start(bf16[8,256,256]{2,1,0:T(8,128)(2,1)S(1)} %get-tuple-element.56), channel_id=1, source_target_pairs={{0,8},{8,0},{16,24},{24,16},{32,40},{40,32},{48,56},{56,48},{64,72... | collective-permute-start | bytes 3145736 | tf_op jit(solution)/shard_map/ppermute | solution.py:34
  (13 other events, 86.5 us)

commit v18 on v16

--- a/solution.py
+++ b/solution.py
@@ -374,16 +374,16 @@
     own0 = after(own[0], chip_pair)
     pair0 = dp_move(own0, 0, 1, 0)
     grad_pair = tensor_move(chip_grad, 1, 0)
-    ring, plane1, pair0, grad_pair, info, query_pos, query_start = lax.optimization_barrier(
-        (ring, plane1, pair0, grad_pair, info, query_pos, query_start)
+    copies = copy(jnp.stack([own0, pair0]), groups_x)
+    both_grads = jnp.stack([chip_grad, grad_pair])
+    sent = jnp.stack([own[1], *plane1])
+    ring, copies, both_grads, sent, info, query_pos, query_start = lax.optimization_barrier(
+        (ring, copies, both_grads, sent, info, query_pos, query_start)
     )
+    plane0 = exchange(copies, "dp", groups_x).reshape(8, SPLIT, depth)
+    rest = dp_move(sent, 0, 1, 0)
     swapped = dp_move(ring, 0, 0, 1)
-    all_grad = [jnp.stack([chip_grad, grad_pair])]
-    all_grad += [tensor_move(all_grad[0], 0, step) for step in (-1, -2, 1)]
-    copies = copy(jnp.stack([own0, pair0]), groups_x)
-    plane0 = exchange(copies, "dp", groups_x).reshape(8, SPLIT, depth)
-    pair1 = dp_move(after(own[1], ring), 0, 1, 0)
-    rest = dp_move(jnp.stack(plane1), 0, 1, 0)
+    all_grad = [both_grads] + [tensor_move(both_grads, 0, step) for step in (-1, -2, 1)]
     probs, outs = forward(info, query_pos, query_start, queries, ring, swapped)
 
     t = lax.axis_index("tensor")
@@ -398,7 +398,7 @@
         jnp.stack(near + [slot(x + i, 1 - z) for i in (0, -1, 1, 2)]).astype(jnp.int32),
     ]
     slots[0] = after(slots[0], outs)
-    stacks = [[plane0], [own[1], *plane1, pair1, rest]]
+    stacks = [[plane0], [sent, rest]]
     terms = []
     for part in range(CHUNKS):
         mine, other = project(part, slots[part], all_grad, stacks[part])

time: 168 us -> 170 us (1.012)
  waiting for transfers between devices: 55 us -> 58.7 us
  local copies, waits for them, and re-layouts: 10.7 us -> 7.76 us
    ppermute x4, waiting for transfers between devices: 11.7 us -> 43.5 us  [tensor_move(): return lax.ppermute(value, 'tensor', pairs)]
    ppermute x13 -> x12, waiting for transfers between devices: 42.2 us -> 15.2 us  [dp_move(): return lax.ppermute(value, 'dp', pairs)]
    another operation x4, other arithmetic: 2.52 us -> 5.17 us  [the longest x1 2.99 us: local(): sent = jnp.stack([own[1], *plane1])]
    unnamed x30 -> x14, local copies, waits for them, and re-layouts: 3.08 us -> 0.81 us
    slice x1 -> x0, local copies, waits for them, and re-layouts: 2.05 us -> none  [local(): own = [out_weight[:SPLIT], out_weight[SPLIT:]]]
    ppermute x13 -> x12, starting transfers between devices: 15.2 us -> 15.9 us  [dp_move(): return lax.ppermute(value, 'dp', pairs)]
  transfers between devices with their start and end apart: 19 -> 18, of which waited for: 9 -> 9; matrix products, arithmetic and copies ran while one was open for 5% -> 5% of each run, Pallas kernels for 11% -> 11%
where the time goes in v18:
time: 170 us; the launch traced here: 169 us
  waiting for transfers between devices  58.7 us (35%)
  starting transfers between devices  32.4 us (19%)
  blocking collectives  31.3 us (18%)
  Pallas kernels  25 us (15%)
  local copies, waits for them, and re-layouts  7.76 us (5%)
  other arithmetic  6.93 us (4%)
  between operations  6.71 us (4%)
    ppermute x4, waiting for transfers between devices, tensor_move(): return lax.ppermute(value, 'tensor', pairs)  43.5 us
    all_to_all x1, blocking collectives, local(): lax.all_to_all(chip_sums, 'dp', 0, 0, axis_index_groups=groups, tiled=True)  31.3 us
    ppermute x12, starting transfers between devices, dp_move(): return lax.ppermute(value, 'dp', pairs)  15.9 us
    ppermute x12, waiting for transfers between devices, dp_move(): return lax.ppermute(value, 'dp', pairs)  15.2 us
    pallas_call x2, Pallas kernels, project(): pl.pallas_call(functools.partial(project_kernel, chips), grid=(1,), in_sp...  11.1 us
    all_to_all x2, starting transfers between devices, exchange(): lax.all_to_all(copies, axis, 0, 0, axis_index_groups=groups, tiled=True)  9.11 us
    pallas_call x1, Pallas kernels, forward(): pl.pallas_call(forward_kernel, grid_spec=pltpu.PrefetchScalarGridSpec(num...  8.02 us
    ppermute x4, starting transfers between devices, tensor_move(): return lax.ppermute(value, 'tensor', pairs)  7.37 us
  transfers between devices with their start and end apart: 18, of which 9 were waited for; matrix products, arithmetic and copies ran while one was open for 5% of the time, Pallas kernels for 11%

profile of v18, /device:TPU:0, one launch (start us, length us, event | category | flops | bytes accessed | tf_op | source)
XLA Modules:
  0.0 168.7 jit_solution(4347838724698761799)
XLA Ops:
  2.1 2.9 %collective-permute-start.6 = (bf16[512,512]{1,0:T(8,128)(2,1)S(1)}, bf16[512,512]{1,0:T(8,128)(2,1)}, u32[]{:S(2)}, u32[]{:S(2)}) collective-permute-start(bf16[512,512]{1,0:T(8,128)(2,1)S(1)} %get-tuple-element.40), channel_id=1, source_target_pairs={{0,96},{8,104},{16,112},{24,120},{32,0},{40,8},{48,16},{56,24},{64... | collective-permute-start | bytes 1572872 | tf_op jit(solution)/shard_map/ppermute | solution.py:34
  5.0 2.3 %collective-permute-start.7 = (bf16[512,512]{1,0:T(8,128)(2,1)S(1)}, bf16[512,512]{1,0:T(8,128)(2,1)}, u32[]{:S(2)}, u32[]{:S(2)}) collective-permute-start(bf16[512,512]{1,0:T(8,128)(2,1)S(1)} %get-tuple-element.40), channel_id=1, source_target_pairs={{0,64},{8,72},{16,80},{24,88},{32,96},{40,104},{48,112},{56,120},{... | collective-permute-start | bytes 1572872 | tf_op jit(solution)/shard_map/ppermute | solution.py:34
  8.6 4.0 %collective-permute-start.1 = (bf16[512,128]{1,0:T(8,128)(2,1)S(1)}, bf16[512,128]{1,0:T(8,128)(2,1)S(1)}, u32[]{:S(2)}, u32[]{:S(2)}) collective-permute-start(bf16[512,128]{1,0:T(8,128)(2,1)S(1)} %pad_maximum_fusion.5), channel_id=1, source_target_pairs={{0,16},{8,24},{16,0},{24,8},{32,48},{40,56},{48,32},{56,40},{64,80... | collective-permute-start | bytes 393224 | tf_op jit(solution)/shard_map/ppermute | solution.py:34
  20.9 4.2 %all-to-all-start = ((bf16[4,1024,128]{2,1,0:T(8,128)(2,1)}), bf16[4,1024,128]{2,1,0:T(8,128)(2,1)}, u32[]{:S(2)}, u32[]{:S(2)}) async-start(bf16[4,1024,128]{2,1,0:T(8,128)(2,1)} %broadcast_in_dim.31), calls=%async_computation | async-start | bytes 2097152 | tf_op jit(solution)/shard_map/all_to_all | solution.py:352
  26.1 1.5 collective-permute-start.4
  28.6 3.1 %collective-permute-done.5 = bf16[512,512]{1,0:T(8,128)(2,1)} collective-permute-done((bf16[512,512]{1,0:T(8,128)(2,1)S(1)}, bf16[512,512]{1,0:T(8,128)(2,1)}, u32[]{:S(2)}, u32[]{:S(2)}) %collective-permute-start.5) | collective-permute-done | bytes 524320 | tf_op jit(solution)/shard_map/ppermute | solution.py:34
  31.7 3.0 %pad_maximum_fusion.rest_4_ = bf16[4,512,512]{2,1,0:T(8,128)(2,1)} fusion(bf16[1,512,512]{2,1,0:T(8,128)(2,1)} %bitcast.8, bf16[1,512,512]{2,1,0:T(8,128)(2,1)} %bitcast.7, bf16[1,512,512]{2,1,0:T(8,128)(2,1)} %bitcast.6, bf16[1,512,512]{2,1,0:T(8,128)(2,1)S(1)} %get-tuple-element.39), kind=kLoop, calls=%fused_computation | loop fusion | flops 3145728 | bytes 4194304 | tf_op jit(solution)/shard_map/stack | solution.py:379
  34.7 7.0 %collective-permute-done.2 = bf16[512,512]{1,0:T(8,128)(2,1)} collective-permute-done((bf16[512,512]{1,0:T(8,128)(2,1)S(1)}, bf16[512,512]{1,0:T(8,128)(2,1)}, u32[]{:S(2)}, u32[]{:S(2)}) %collective-permute-start.2) | collective-permute-done | bytes 524320 | tf_op jit(solution)/shard_map/ppermute | solution.py:34
  42.8 7.0 %collective-permute-done.4 = bf16[512,512]{1,0:T(8,128)(2,1)} collective-permute-done((bf16[512,512]{1,0:T(8,128)(2,1)}, bf16[512,512]{1,0:T(8,128)(2,1)}, u32[]{:S(2)}, u32[]{:S(2)}) %collective-permute-start.4) | collective-permute-done | bytes 524320 | tf_op jit(solution)/shard_map/ppermute | solution.py:42
  51.0 2.3 %broadcast_in_dim.32 = bf16[4,2,512,512]{3,2,1,0:T(8,128)(2,1)} broadcast(bf16[2,512,512]{2,1,0:T(8,128)(2,1)S(1)} %pad_maximum_fusion.1), dimensions={1,2,3} | broadcast | bytes 5242880 | tf_op jit(solution)/shard_map/broadcast_in_dim | solution.py:349
  53.3 4.9 %all-to-all-start.1 = ((bf16[4,2,512,512]{3,2,1,0:T(8,128)(2,1)}), bf16[4,2,512,512]{3,2,1,0:T(8,128)(2,1)}, u32[]{:S(2)}, u32[]{:S(2)}) async-start(bf16[4,2,512,512]{3,2,1,0:T(8,128)(2,1)} %broadcast_in_dim.32), calls=%async_computation.1 | async-start | bytes 8388608 | tf_op jit(solution)/shard_map/all_to_all | solution.py:352
  58.2 3.7 %collective-permute-start.13 = (bf16[4,512,512]{2,1,0:T(8,128)(2,1)}, bf16[4,512,512]{2,1,0:T(8,128)(2,1)}, u32[]{:S(2)}, u32[]{:S(2)}) collective-permute-start(bf16[4,512,512]{2,1,0:T(8,128)(2,1)} %pad_maximum_fusion.rest_4_), channel_id=1, source_target_pairs={{0,16},{8,24},{16,0},{24,8},{32,48},{40,56},{48,32},{56,40},{64,80... | collective-permute-start | bytes 6291464 | tf_op jit(solution)/shard_map/ppermute | solution.py:34
  61.8 1.6 collective-permute-start.11
  63.4 2.9 %collective-permute-start.10 = (bf16[2,512,512]{2,1,0:T(8,128)(2,1)S(1)}, bf16[2,512,512]{2,1,0:T(8,128)(2,1)S(1)}, u32[]{:S(2)}, u32[]{:S(2)}) collective-permute-start(bf16[2,512,512]{2,1,0:T(8,128)(2,1)S(1)} %pad_maximum_fusion.2.rest_0_), channel_id=1, source_target_pairs={{0,2},{1,3},{2,0},{3,1},{4,6},{5,7},{6,4},{7,5},{8,10},{9,11},{10,... | collective-permute-start | bytes 3145736 | tf_op jit(solution)/shard_map/ppermute | solution.py:42
  67.8 8.0 %forward.1 = (bf16[2816,2048]{1,0:T(8,128)(2,1)}, f32[128,2048]{1,0:T(8,128)}) custom-call(s32[36]{0:T(128)S(1)} %concatenate.16.info, s32[1,256]{1,0:T(1,128)S(1)} %iota_add_fusion.pos_ref, s32[1,256]{1,0:T(1,128)S(1)} %bitcast.39, bf16[256,1024]{1,0:T(8,128)(2,1)} %rest_6_.1, bf16[4096,128]{1,0:T(8,128)(2,1)} %bitcast.here_ref.rest_7_, ...), custom_call_target="tpu_custom_call" | custom-call | flops 100000000 | bytes 1048576 | tf_op jit(solution)/shard_map/forward/pallas_call | solution.py:141
  75.8 12.8 %collective-permute-done.11.rest_3_ = bf16[2,512,512]{2,1,0:T(8,128)(2,1)S(1)} collective-permute-done((bf16[2,512,512]{2,1,0:T(8,128)(2,1)S(1)}, bf16[2,512,512]{2,1,0:T(8,128)(2,1)S(1)}, u32[]{:S(2)}, u32[]{:S(2)}) %collective-permute-start.11) | collective-permute-done | bytes 1048608 | tf_op jit(solution)/shard_map/ppermute | solution.py:42
  88.7 23.6 %collective-permute-done.10.rest_2_ = bf16[2,512,512]{2,1,0:T(8,128)(2,1)S(1)} collective-permute-done((bf16[2,512,512]{2,1,0:T(8,128)(2,1)S(1)}, bf16[2,512,512]{2,1,0:T(8,128)(2,1)S(1)}, u32[]{:S(2)}, u32[]{:S(2)}) %collective-permute-start.10) | collective-permute-done | bytes 1048608 | tf_op jit(solution)/shard_map/ppermute | solution.py:42
  112.3 5.9 %project1.1 = (f32[256,512]{1,0:T(8,128)S(1)}, f32[256,512]{1,0:T(8,128)}) custom-call(s32[8]{0:T(128)S(1)} %stack.131.slots, bf16[2,512,512]{2,1,0:T(8,128)(2,1)S(1)} %pad_maximum_fusion.2.rest_0_, bf16[2,512,512]{2,1,0:T(8,128)(2,1)} %collective-permute-done.9.rest_1_, bf16[2,512,512]{2,1,0:T(8,128)(2,1)S(1)} %collective-permute-done.10.rest_2_, ...), custom_call_target="tpu_custom_call" | custom-call | flops 2147483648 | bytes 10485760 | tf_op jit(solution)/shard_map/project1/pallas_call | solution.py:308
  119.1 5.2 %project0.1 = (f32[256,512]{1,0:T(8,128)S(1)}, f32[256,512]{1,0:T(8,128)S(1)}) custom-call(s32[8]{0:T(128)S(1)} %stack.122.slots, bf16[2,512,512]{2,1,0:T(8,128)(2,1)S(1)} %pad_maximum_fusion.2.rest_0_, bf16[2,512,512]{2,1,0:T(8,128)(2,1)} %collective-permute-done.9.rest_1_, bf16[2,512,512]{2,1,0:T(8,128)(2,1)S(1)} %collective-permute-done.10.rest_2_, ...), custom_call_target="tpu_custom_call" | custom-call | flops 2147483648 | bytes 10485760 | tf_op jit(solution)/shard_map/project0/pallas_call | solution.py:308
  125.0 1.5 collective-permute-done.12.rest_1_
  126.6 5.9 %backward.1 = (bf16[256,1024]{1,0:T(8,128)(2,1)}, f32[8,256,256]{2,1,0:T(8,128)S(1)}, bf16[8,256,256]{2,1,0:T(8,128)(2,1)S(1)}) custom-call(s32[36]{0:T(128)S(1)} %concatenate.16.info, f32[256,512]{1,0:T(8,128)S(1)} %get-tuple-element.30.rest_0_, f32[256,512]{1,0:T(8,128)S(1)} %collective-permute-done.12.rest_1_, f32[256,512]{1,0:T(8,128)S(1)} %copy-done.2, ...), custom_call_target="tpu_custom_call" | custom-call | flops 8000000000 | bytes 10485760 | tf_op jit(solution)/shard_map/backward/pallas_call | solution.py:241
  132.5 1.6 collective-permute-start.15
  134.0 2.3 %collective-permute-done.15 = bf16[8,256,256]{2,1,0:T(8,128)(2,1)S(1)} collective-permute-done((bf16[8,256,256]{2,1,0:T(8,128)(2,1)S(1)}, bf16[8,256,256]{2,1,0:T(8,128)(2,1)S(1)}, u32[]{:S(2)}, u32[]{:S(2)}) %collective-permute-start.15) | collective-permute-done | bytes 1048608 | tf_op jit(solution)/shard_map/ppermute | solution.py:34
  136.6 31.3 %all_to_all.15 = bf16[8,256,256]{2,1,0:T(8,128)(2,1)S(1)} all-to-all(bf16[8,256,256]{2,1,0:T(8,128)(2,1)S(1)} %add_convert_fusion), channel_id=1, replica_groups={{0,16,32,48,64,80,96,112},{8,24,40,56,72,88,104,120},{1,17,33,49,65,81,..., dimensions={0} | all-to-all | bytes 2097152 | tf_op jit(solution)/shard_map/all_to_all | solution.py:410
  (56 shorter events, 13.5 us)
Async XLA Ops:
  0.6 6.6 %copy-start.5 = (bf16[256,128]{1,0:T(8,128)(2,1)S(1)}, bf16[256,128]{1,0:T(8,128)(2,1)}, u32[]{:S(2)}) copy-start(bf16[256,128]{1,0:T(8,128)(2,1)} %param.8) | copy-start | bytes 196612
  0.6 6.6 %copy-start.4 = (bf16[256,128]{1,0:T(8,128)(2,1)S(1)}, bf16[256,128]{1,0:T(8,128)(2,1)}, u32[]{:S(2)}) copy-start(bf16[256,128]{1,0:T(8,128)(2,1)} %param.7) | copy-start | bytes 196612
  0.7 6.8 %copy-start.3 = (bf16[256,1024]{1,0:T(8,128)(2,1)S(1)}, bf16[256,1024]{1,0:T(8,128)(2,1)}, u32[]{:S(2)}) copy-start(bf16[256,1024]{1,0:T(8,128)(2,1)} %param.9) | copy-start | bytes 1572868
  0.7 7.4 %copy-start.6 = (s32[8]{0:T(128)S(1)}, s32[8]{0:T(128)}, u32[]{:S(2)}) copy-start(s32[8]{0:T(128)} %param.11) | copy-start | bytes 100
  2.1 26.5 %collective-permute-start.6 = (bf16[512,512]{1,0:T(8,128)(2,1)S(1)}, bf16[512,512]{1,0:T(8,128)(2,1)}, u32[]{:S(2)}, u32[]{:S(2)}) collective-permute-start(bf16[512,512]{1,0:T(8,128)(2,1)S(1)} %get-tuple-element.40), channel_id=1, source_target_pairs={{0,96},{8,104},{16,112},{24,120},{32,0},{40,8},{48,16},{56,24},{64... | collective-permute-start | bytes 1572872 | tf_op jit(solution)/shard_map/ppermute | solution.py:34
  5.0 26.7 %collective-permute-start.5 = (bf16[512,512]{1,0:T(8,128)(2,1)S(1)}, bf16[512,512]{1,0:T(8,128)(2,1)}, u32[]{:S(2)}, u32[]{:S(2)}) collective-permute-start(bf16[512,512]{1,0:T(8,128)(2,1)S(1)} %get-tuple-element.40), channel_id=1, source_target_pairs={{0,32},{8,40},{16,48},{24,56},{32,64},{40,72},{48,80},{56,88},{64,... | collective-permute-start | bytes 1572872 | tf_op jit(solution)/shard_map/ppermute | solution.py:34
  5.0 26.7 %collective-permute-start.7 = (bf16[512,512]{1,0:T(8,128)(2,1)S(1)}, bf16[512,512]{1,0:T(8,128)(2,1)}, u32[]{:S(2)}, u32[]{:S(2)}) collective-permute-start(bf16[512,512]{1,0:T(8,128)(2,1)S(1)} %get-tuple-element.40), channel_id=1, source_target_pairs={{0,64},{8,72},{16,80},{24,88},{32,96},{40,104},{48,112},{56,120},{... | collective-permute-start | bytes 1572872 | tf_op jit(solution)/shard_map/ppermute | solution.py:34
  7.3 1.3 collective-permute-start
  7.5 17.8 %collective-permute-start.3 = (bf16[256,512]{1,0:T(8,128)(2,1)S(1)}, bf16[256,512]{1,0:T(8,128)(2,1)S(1)}, u32[]{:S(2)}, u32[]{:S(2)}) collective-permute-start(bf16[256,512]{1,0:T(8,128)(2,1)S(1)} %get-tuple-element.45), channel_id=1, source_target_pairs={{0,8},{8,0},{16,24},{24,16},{32,40},{40,32},{48,56},{56,48},{64,72... | collective-permute-start | bytes 786440 | tf_op jit(solution)/shard_map/ppermute | solution.py:34
  8.6 11.1 %collective-permute-start.1 = (bf16[512,128]{1,0:T(8,128)(2,1)S(1)}, bf16[512,128]{1,0:T(8,128)(2,1)S(1)}, u32[]{:S(2)}, u32[]{:S(2)}) collective-permute-start(bf16[512,128]{1,0:T(8,128)(2,1)S(1)} %pad_maximum_fusion.5), channel_id=1, source_target_pairs={{0,16},{8,24},{16,0},{24,8},{32,48},{40,56},{48,32},{56,40},{64,80... | collective-permute-start | bytes 393224 | tf_op jit(solution)/shard_map/ppermute | solution.py:34
  20.9 30.1 %all-to-all-start = ((bf16[4,1024,128]{2,1,0:T(8,128)(2,1)}), bf16[4,1024,128]{2,1,0:T(8,128)(2,1)}, u32[]{:S(2)}, u32[]{:S(2)}) async-start(bf16[4,1024,128]{2,1,0:T(8,128)(2,1)} %broadcast_in_dim.31), calls=%async_computation | async-start | bytes 2097152 | tf_op jit(solution)/shard_map/all_to_all | solution.py:352
  25.2 16.5 %collective-permute-start.2 = (bf16[512,512]{1,0:T(8,128)(2,1)S(1)}, bf16[512,512]{1,0:T(8,128)(2,1)}, u32[]{:S(2)}, u32[]{:S(2)}) collective-permute-start(bf16[512,512]{1,0:T(8,128)(2,1)S(1)} %get-tuple-element.21), channel_id=1, source_target_pairs={{0,16},{8,24},{16,0},{24,8},{32,48},{40,56},{48,32},{56,40},{64,80... | collective-permute-start | bytes 1572872 | tf_op jit(solution)/shard_map/ppermute | solution.py:34
  26.1 23.7 %collective-permute-start.4 = (bf16[512,512]{1,0:T(8,128)(2,1)}, bf16[512,512]{1,0:T(8,128)(2,1)}, u32[]{:S(2)}, u32[]{:S(2)}) collective-permute-start(bf16[512,512]{1,0:T(8,128)(2,1)} %get-tuple-element.43), channel_id=1, source_target_pairs={{0,4},{1,5},{2,6},{3,7},{4,0},{5,1},{6,2},{7,3},{8,12},{9,13},{10,... | collective-permute-start | bytes 1572872 | tf_op jit(solution)/shard_map/ppermute | solution.py:42
  53.3 65.8 %all-to-all-start.1 = ((bf16[4,2,512,512]{3,2,1,0:T(8,128)(2,1)}), bf16[4,2,512,512]{3,2,1,0:T(8,128)(2,1)}, u32[]{:S(2)}, u32[]{:S(2)}) async-start(bf16[4,2,512,512]{3,2,1,0:T(8,128)(2,1)} %broadcast_in_dim.32), calls=%async_computation.1 | async-start | bytes 8388608 | tf_op jit(solution)/shard_map/all_to_all | solution.py:352
  58.2 54.2 %collective-permute-start.13 = (bf16[4,512,512]{2,1,0:T(8,128)(2,1)}, bf16[4,512,512]{2,1,0:T(8,128)(2,1)}, u32[]{:S(2)}, u32[]{:S(2)}) collective-permute-start(bf16[4,512,512]{2,1,0:T(8,128)(2,1)} %pad_maximum_fusion.rest_4_), channel_id=1, source_target_pairs={{0,16},{8,24},{16,0},{24,8},{32,48},{40,56},{48,32},{56,40},{64,80... | collective-permute-start | bytes 6291464 | tf_op jit(solution)/shard_map/ppermute | solution.py:34
  61.8 6.0 %collective-permute-start.8 = (bf16[4096,128]{1,0:T(8,128)(2,1)}, bf16[4096,128]{1,0:T(8,128)(2,1)}, u32[]{:S(2)}, u32[]{:S(2)}) collective-permute-start(bf16[4096,128]{1,0:T(8,128)(2,1)} %bitcast.here_ref.rest_7_), channel_id=1, source_target_pairs={{0,8},{8,0},{16,24},{24,16},{32,40},{40,32},{48,56},{56,48},{64,72... | collective-permute-start | bytes 3145736 | tf_op jit(solution)/shard_map/ppermute | solution.py:34
  61.8 26.8 %collective-permute-start.11 = (bf16[2,512,512]{2,1,0:T(8,128)(2,1)S(1)}, bf16[2,512,512]{2,1,0:T(8,128)(2,1)S(1)}, u32[]{:S(2)}, u32[]{:S(2)}) collective-permute-start(bf16[2,512,512]{2,1,0:T(8,128)(2,1)S(1)} %pad_maximum_fusion.2.rest_0_), channel_id=1, source_target_pairs={{0,1},{1,2},{2,3},{3,0},{4,5},{5,6},{6,7},{7,4},{8,9},{9,10},{10,1... | collective-permute-start | bytes 3145736 | tf_op jit(solution)/shard_map/ppermute | solution.py:42
  63.4 48.9 %collective-permute-start.10 = (bf16[2,512,512]{2,1,0:T(8,128)(2,1)S(1)}, bf16[2,512,512]{2,1,0:T(8,128)(2,1)S(1)}, u32[]{:S(2)}, u32[]{:S(2)}) collective-permute-start(bf16[2,512,512]{2,1,0:T(8,128)(2,1)S(1)} %pad_maximum_fusion.2.rest_0_), channel_id=1, source_target_pairs={{0,2},{1,3},{2,0},{3,1},{4,6},{5,7},{6,4},{7,5},{8,10},{9,11},{10,... | collective-permute-start | bytes 3145736 | tf_op jit(solution)/shard_map/ppermute | solution.py:42
  66.3 46.0 %collective-permute-start.9 = (bf16[2,512,512]{2,1,0:T(8,128)(2,1)S(1)}, bf16[2,512,512]{2,1,0:T(8,128)(2,1)}, u32[]{:S(2)}, u32[]{:S(2)}) collective-permute-start(bf16[2,512,512]{2,1,0:T(8,128)(2,1)S(1)} %pad_maximum_fusion.2.rest_0_), channel_id=1, source_target_pairs={{0,3},{1,0},{2,1},{3,2},{4,7},{5,4},{6,5},{7,6},{8,11},{9,8},{10,9... | collective-permute-start | bytes 3145736 | tf_op jit(solution)/shard_map/ppermute | solution.py:42
  119.0 6.0 %collective-permute-start.14 = (f32[256,512]{1,0:T(8,128)}, f32[256,512]{1,0:T(8,128)}, u32[]{:S(2)}, u32[]{:S(2)}) collective-permute-start(f32[256,512]{1,0:T(8,128)} %get-tuple-element.34), channel_id=1, source_target_pairs={{0,8},{8,0},{16,24},{24,16},{32,40},{40,32},{48,56},{56,48},{64,72... | collective-permute-start | bytes 1572872 | tf_op jit(solution)/shard_map/ppermute | solution.py:34
  119.0 7.5 %copy-start = (f32[128,2048]{1,0:T(8,128)S(1)}, f32[128,2048]{1,0:T(8,128)}, u32[]{:S(2)}) copy-start(f32[128,2048]{1,0:T(8,128)} %get-tuple-element.26.rest_5_) | copy-start | bytes 3145732
  119.1 7.5 %copy-start.2 = (f32[256,512]{1,0:T(8,128)S(1)}, f32[256,512]{1,0:T(8,128)}, u32[]{:S(2)}) copy-start(f32[256,512]{1,0:T(8,128)} %copy-done.1) | copy-start | bytes 1572868
  124.3 2.3 %collective-permute-start.12 = (f32[256,512]{1,0:T(8,128)S(1)}, f32[256,512]{1,0:T(8,128)S(1)}, u32[]{:S(2)}, u32[]{:S(2)}) collective-permute-start(f32[256,512]{1,0:T(8,128)S(1)} %get-tuple-element.31), channel_id=1, source_target_pairs={{0,8},{8,0},{16,24},{24,16},{32,40},{40,32},{48,56},{56,48},{64,72... | collective-permute-start | bytes 1572872 | tf_op jit(solution)/shard_map/ppermute | solution.py:34
  132.5 3.9 %collective-permute-start.15 = (bf16[8,256,256]{2,1,0:T(8,128)(2,1)S(1)}, bf16[8,256,256]{2,1,0:T(8,128)(2,1)S(1)}, u32[]{:S(2)}, u32[]{:S(2)}) collective-permute-start(bf16[8,256,256]{2,1,0:T(8,128)(2,1)S(1)} %get-tuple-element.38), channel_id=1, source_target_pairs={{0,8},{8,0},{16,24},{24,16},{32,40},{40,32},{48,56},{56,48},{64,72... | collective-permute-start | bytes 3145736 | tf_op jit(solution)/shard_map/ppermute | solution.py:34
  (1 other events, 0.8 us)

commit v19 on v18

--- a/solution.py
+++ b/solution.py
@@ -329,6 +329,26 @@
     core = rank % 2
     x, z = rank // 4, (rank // 2) % 2
 
+    def copy(block, groups):
+        return jnp.broadcast_to(block, (len(groups[0]), *block.shape))
+
+    def exchange(copies, axis, groups):
+        return lax.all_to_all(copies, axis, 0, 0, axis_index_groups=groups, tiled=True)
+
+    groups_x = [[x_ * 4 + zc for x_ in range(4)] for zc in range(4)]
+    kept = jnp.where(core == 0, keys, values)
+    got = dp_move(jnp.where(core == 0, values, keys), 0, 0, 1)
+    chip = jnp.concatenate([kept, got], axis=0)
+    chip_pair = jnp.concatenate([chip, dp_move(chip, 0, 1, 0)], axis=0)
+
+    depth = out_weight.shape[1]
+    mine = lax.dynamic_slice_in_dim(grad_out, core * depth, depth, 1)
+    other = lax.dynamic_slice_in_dim(grad_out, (1 - core) * depth, depth, 1)
+    chip_grad = jnp.concatenate([mine, dp_move(other, 0, 0, 1)], axis=0)
+    copies, chip_grad = lax.optimization_barrier((copy(chip_pair, groups_x), chip_grad))
+    ring = exchange(copies, "dp", groups_x).reshape(-1, HEAD_WIDTH)
+    lengths = after(lengths, copies)
+
     query_pos = rank * rows + jnp.arange(rows, dtype=jnp.int32)
     ends = jnp.cumsum(lengths)[:-1]
     query_start = jnp.max(
@@ -345,26 +365,6 @@
     info = jnp.concatenate([scalars, here, there]).astype(jnp.int32)
     query_pos, query_start = query_pos[None, :], query_start[None, :]
 
-    def copy(block, groups):
-        return jnp.broadcast_to(block, (len(groups[0]), *block.shape))
-
-    def exchange(copies, axis, groups):
-        return lax.all_to_all(copies, axis, 0, 0, axis_index_groups=groups, tiled=True)
-
-    def spread(block, axis, groups):
-        return exchange(copy(block, groups), axis, groups)
-
-    groups_x = [[x_ * 4 + zc for x_ in range(4)] for zc in range(4)]
-    kept = jnp.where(core == 0, keys, values)
-    got = dp_move(jnp.where(core == 0, values, keys), 0, 0, 1)
-    chip = jnp.concatenate([kept, got], axis=0)
-    chip_pair = jnp.concatenate([chip, dp_move(chip, 0, 1, 0)], axis=0)
-    ring = spread(chip_pair, "dp", groups_x).reshape(-1, HEAD_WIDTH)
-
-    depth = out_weight.shape[1]
-    mine = lax.dynamic_slice_in_dim(grad_out, core * depth, depth, 1)
-    other = lax.dynamic_slice_in_dim(grad_out, (1 - core) * depth, depth, 1)
-    chip_grad = jnp.concatenate([mine, dp_move(other, 0, 0, 1)], axis=0)
 
     def around_x(block):
         return [dp_move(block, step, 0, 0) for step in (1, -1, 2)]
@@ -381,8 +381,9 @@
         (ring, copies, both_grads, sent, info, query_pos, query_start)
     )
     plane0 = exchange(copies, "dp", groups_x).reshape(8, SPLIT, depth)
-    rest = dp_move(sent, 0, 1, 0)
     swapped = dp_move(ring, 0, 0, 1)
+    swapped, held = lax.optimization_barrier((swapped, sent))
+    rest = dp_move(held, 0, 1, 0)
     all_grad = [both_grads] + [tensor_move(both_grads, 0, step) for step in (-1, -2, 1)]
     probs, outs = forward(info, query_pos, query_start, queries, ring, swapped)
 

time: 170 us -> 164 us (0.965)
  waiting for transfers between devices: 58.7 us -> 48.9 us
  local copies, waits for them, and re-layouts: 7.76 us -> 12.1 us
    ppermute x12, waiting for transfers between devices: 15.2 us -> 7.22 us  [dp_move(): return lax.ppermute(value, 'dp', pairs)]
    unnamed x14 -> x30, local copies, waits for them, and re-layouts: 0.81 us -> 4.32 us
    ppermute x4, waiting for transfers between devices: 43.5 us -> 41.7 us  [tensor_move(): return lax.ppermute(value, 'tensor', pairs)]
  transfers between devices with their start and end apart: 18 -> 18, of which waited for: 9 -> 8; matrix products, arithmetic and copies ran while one was open for 5% -> 5% of each run, Pallas kernels for 11% -> 11%
where the time goes in v19:
time: 164 us; the launch traced here: 162 us
  waiting for transfers between devices  48.9 us (30%)
  starting transfers between devices  32.3 us (20%)
  blocking collectives  32 us (20%)
  Pallas kernels  24 us (15%)
  local copies, waits for them, and re-layouts  12.1 us (7%)
  between operations  6.75 us (4%)
  other arithmetic  6.19 us (4%)
    ppermute x4, waiting for transfers between devices, tensor_move(): return lax.ppermute(value, 'tensor', pairs)  41.7 us
    all_to_all x1, blocking collectives, local(): lax.all_to_all(chip_sums, 'dp', 0, 0, axis_index_groups=groups, tiled=True)  32 us
    ppermute x12, starting transfers between devices, dp_move(): return lax.ppermute(value, 'dp', pairs)  17.1 us
    pallas_call x2, Pallas kernels, project(): pl.pallas_call(functools.partial(project_kernel, chips), grid=(1,), in_sp...  11.2 us
    all_to_all x2, starting transfers between devices, exchange(): lax.all_to_all(copies, axis, 0, 0, axis_index_groups=groups, tiled=True)  8.39 us
    pallas_call x1, Pallas kernels, forward(): pl.pallas_call(forward_kernel, grid_spec=pltpu.PrefetchScalarGridSpec(num...  7.23 us
    ppermute x12, waiting for transfers between devices, dp_move(): return lax.ppermute(value, 'dp', pairs)  7.22 us
    ppermute x4, starting transfers between devices, tensor_move(): return lax.ppermute(value, 'tensor', pairs)  6.85 us
  transfers between devices with their start and end apart: 18, of which 8 were waited for; matrix products, arithmetic and copies ran while one was open for 5% of the time, Pallas kernels for 11%

profile of v19, /device:TPU:0, one launch (start us, length us, event | category | flops | bytes accessed | tf_op | source)
XLA Modules:
  0.0 162.3 jit_solution(17909854950833472362)
XLA Ops:
  0.7 2.2 %slice_bitcast_fusion.1 = (bf16[1,512,512]{2,1,0:T(8,128)(2,1)S(1)}, bf16[512,512]{1,0:T(8,128)(2,1)}, bf16[512,512]{1,0:T(8,128)(2,1)S(1)}) fusion(bf16[1024,512]{1,0:T(8,128)(2,1)} %param.10), kind=kLoop, calls=%fused_computation.34 | loop fusion | bytes 2621440 | tf_op jit(solution)/shard_map/stack | solution.py:379
  2.8 2.8 %collective-permute-start.6 = (bf16[512,512]{1,0:T(8,128)(2,1)}, bf16[512,512]{1,0:T(8,128)(2,1)}, u32[]{:S(2)}, u32[]{:S(2)}) collective-permute-start(bf16[512,512]{1,0:T(8,128)(2,1)} %get-tuple-element.50), channel_id=1, source_target_pairs={{0,96},{8,104},{16,112},{24,120},{32,0},{40,8},{48,16},{56,24},{64... | collective-permute-start | bytes 1572872 | tf_op jit(solution)/shard_map/ppermute | solution.py:34
  5.7 2.3 %collective-permute-start.7 = (bf16[512,512]{1,0:T(8,128)(2,1)}, bf16[512,512]{1,0:T(8,128)(2,1)}, u32[]{:S(2)}, u32[]{:S(2)}) collective-permute-start(bf16[512,512]{1,0:T(8,128)(2,1)} %get-tuple-element.50), channel_id=1, source_target_pairs={{0,64},{8,72},{16,80},{24,88},{32,96},{40,104},{48,112},{56,120},{... | collective-permute-start | bytes 1572872 | tf_op jit(solution)/shard_map/ppermute | solution.py:34
  9.4 4.0 %collective-permute-start.1 = (bf16[512,128]{1,0:T(8,128)(2,1)S(1)}, bf16[512,128]{1,0:T(8,128)(2,1)S(1)}, u32[]{:S(2)}, u32[]{:S(2)}) collective-permute-start(bf16[512,128]{1,0:T(8,128)(2,1)S(1)} %pad_maximum_fusion.5), channel_id=1, source_target_pairs={{0,16},{8,24},{16,0},{24,8},{32,48},{40,56},{48,32},{56,40},{64,80... | collective-permute-start | bytes 393224 | tf_op jit(solution)/shard_map/ppermute | solution.py:34
  17.2 3.3 %collective-permute-start.3 = (bf16[512,512]{1,0:T(8,128)(2,1)S(1)}, bf16[512,512]{1,0:T(8,128)(2,1)}, u32[]{:S(2)}, u32[]{:S(2)}) collective-permute-start(bf16[512,512]{1,0:T(8,128)(2,1)S(1)} %get-tuple-element.27), channel_id=1, source_target_pairs={{0,16},{8,24},{16,0},{24,8},{32,48},{40,56},{48,32},{56,40},{64,80... | collective-permute-start | bytes 1572872 | tf_op jit(solution)/shard_map/ppermute | solution.py:34
  21.7 3.5 %all-to-all-start = ((bf16[4,1024,128]{2,1,0:T(8,128)(2,1)}), bf16[4,1024,128]{2,1,0:T(8,128)(2,1)S(1)}, u32[]{:S(2)}, u32[]{:S(2)}) async-start(bf16[4,1024,128]{2,1,0:T(8,128)(2,1)} %broadcast_in_dim.31), calls=%async_computation | async-start | bytes 2097152 | tf_op jit(solution)/shard_map/all_to_all | solution.py:336
  30.5 2.2 %collective-permute-done.5 = bf16[512,512]{1,0:T(8,128)(2,1)} collective-permute-done((bf16[512,512]{1,0:T(8,128)(2,1)}, bf16[512,512]{1,0:T(8,128)(2,1)}, u32[]{:S(2)}, u32[]{:S(2)}) %collective-permute-start.5) | collective-permute-done | bytes 524320 | tf_op jit(solution)/shard_map/ppermute | solution.py:34
  32.6 3.0 %pad_maximum_fusion.rest_4_ = bf16[4,512,512]{2,1,0:T(8,128)(2,1)} fusion(bf16[1,512,512]{2,1,0:T(8,128)(2,1)} %bitcast.8, bf16[1,512,512]{2,1,0:T(8,128)(2,1)} %bitcast.7, bf16[1,512,512]{2,1,0:T(8,128)(2,1)} %bitcast.6, bf16[1,512,512]{2,1,0:T(8,128)(2,1)S(1)} %get-tuple-element.49), kind=kLoop, calls=%fused_computation | loop fusion | flops 3145728 | bytes 4194304 | tf_op jit(solution)/shard_map/stack | solution.py:379
  36.8 7.2 %collective-permute-done.4 = bf16[512,512]{1,0:T(8,128)(2,1)} collective-permute-done((bf16[512,512]{1,0:T(8,128)(2,1)S(1)}, bf16[512,512]{1,0:T(8,128)(2,1)}, u32[]{:S(2)}, u32[]{:S(2)}) %collective-permute-start.4) | collective-permute-done | bytes 524320 | tf_op jit(solution)/shard_map/ppermute | solution.py:42
  45.1 2.3 %broadcast_in_dim.32 = bf16[4,2,512,512]{3,2,1,0:T(8,128)(2,1)} broadcast(bf16[2,512,512]{2,1,0:T(8,128)(2,1)S(1)} %pad_maximum_fusion.1), dimensions={1,2,3} | broadcast | bytes 5242880 | tf_op jit(solution)/shard_map/broadcast_in_dim | solution.py:333
  47.4 4.9 %all-to-all-start.1 = ((bf16[4,2,512,512]{3,2,1,0:T(8,128)(2,1)}), bf16[4,2,512,512]{3,2,1,0:T(8,128)(2,1)}, u32[]{:S(2)}, u32[]{:S(2)}) async-start(bf16[4,2,512,512]{3,2,1,0:T(8,128)(2,1)} %broadcast_in_dim.32), calls=%async_computation.1 | async-start | bytes 8388608 | tf_op jit(solution)/shard_map/all_to_all | solution.py:336
  53.3 1.7 %collective-permute-start.13 = (bf16[4,512,512]{2,1,0:T(8,128)(2,1)}, bf16[4,512,512]{2,1,0:T(8,128)(2,1)}, u32[]{:S(2)}, u32[]{:S(2)}) collective-permute-start(bf16[4,512,512]{2,1,0:T(8,128)(2,1)} %pad_maximum_fusion.rest_4_), channel_id=1, source_target_pairs={{0,16},{8,24},{16,0},{24,8},{32,48},{40,56},{48,32},{56,40},{64,80... | collective-permute-start | bytes 6291464 | tf_op jit(solution)/shard_map/ppermute | solution.py:34
  55.1 1.6 collective-permute-start.11
  56.6 2.9 %collective-permute-start.10 = (bf16[2,512,512]{2,1,0:T(8,128)(2,1)S(1)}, bf16[2,512,512]{2,1,0:T(8,128)(2,1)S(1)}, u32[]{:S(2)}, u32[]{:S(2)}) collective-permute-start(bf16[2,512,512]{2,1,0:T(8,128)(2,1)S(1)} %pad_maximum_fusion.2.rest_0_), channel_id=1, source_target_pairs={{0,2},{1,3},{2,0},{3,1},{4,6},{5,7},{6,4},{7,5},{8,10},{9,11},{10,... | collective-permute-start | bytes 3145736 | tf_op jit(solution)/shard_map/ppermute | solution.py:42
  63.5 7.2 %forward.1 = (bf16[2816,2048]{1,0:T(8,128)(2,1)}, f32[128,2048]{1,0:T(8,128)}) custom-call(s32[36]{0:T(128)S(1)} %concatenate.16.info, s32[1,256]{1,0:T(1,128)S(1)} %iota_add_fusion.pos_ref, s32[1,256]{1,0:T(1,128)S(1)} %bitcast.41, bf16[256,1024]{1,0:T(8,128)(2,1)} %rest_6_.1, bf16[4096,128]{1,0:T(8,128)(2,1)S(1)} %bitcast.39, bf16[4096,128]{1,0:T(8,128)(2,1)S(1)} %copy-done.4), custom_call_target="tpu_custom_call" | custom-call | flops 100000000 | bytes 1048576 | tf_op jit(solution)/shard_map/forward/pallas_call | solution.py:141
  70.7 10.9 %collective-permute-done.11.rest_3_ = bf16[2,512,512]{2,1,0:T(8,128)(2,1)S(1)} collective-permute-done((bf16[2,512,512]{2,1,0:T(8,128)(2,1)S(1)}, bf16[2,512,512]{2,1,0:T(8,128)(2,1)S(1)}, u32[]{:S(2)}, u32[]{:S(2)}) %collective-permute-start.11) | collective-permute-done | bytes 1048608 | tf_op jit(solution)/shard_map/ppermute | solution.py:42
  81.6 23.6 %collective-permute-done.10.rest_2_ = bf16[2,512,512]{2,1,0:T(8,128)(2,1)S(1)} collective-permute-done((bf16[2,512,512]{2,1,0:T(8,128)(2,1)S(1)}, bf16[2,512,512]{2,1,0:T(8,128)(2,1)S(1)}, u32[]{:S(2)}, u32[]{:S(2)}) %collective-permute-start.10) | collective-permute-done | bytes 1048608 | tf_op jit(solution)/shard_map/ppermute | solution.py:42
  105.3 5.9 %project1.1 = (f32[256,512]{1,0:T(8,128)S(1)}, f32[256,512]{1,0:T(8,128)}) custom-call(s32[8]{0:T(128)S(1)} %stack.131.slots, bf16[2,512,512]{2,1,0:T(8,128)(2,1)S(1)} %pad_maximum_fusion.2.rest_0_, bf16[2,512,512]{2,1,0:T(8,128)(2,1)} %collective-permute-done.9.rest_1_, bf16[2,512,512]{2,1,0:T(8,128)(2,1)S(1)} %collective-permute-done.10.rest_2_, ...), custom_call_target="tpu_custom_call" | custom-call | flops 2147483648 | bytes 10485760 | tf_op jit(solution)/shard_map/project1/pallas_call | solution.py:308
  112.1 5.2 %project0.1 = (f32[256,512]{1,0:T(8,128)S(1)}, f32[256,512]{1,0:T(8,128)S(1)}) custom-call(s32[8]{0:T(128)S(1)} %stack.122.slots, bf16[2,512,512]{2,1,0:T(8,128)(2,1)S(1)} %pad_maximum_fusion.2.rest_0_, bf16[2,512,512]{2,1,0:T(8,128)(2,1)} %collective-permute-done.9.rest_1_, bf16[2,512,512]{2,1,0:T(8,128)(2,1)S(1)} %collective-permute-done.10.rest_2_, ...), custom_call_target="tpu_custom_call" | custom-call | flops 2147483648 | bytes 10485760 | tf_op jit(solution)/shard_map/project0/pallas_call | solution.py:308
  118.1 1.5 collective-permute-done.12.rest_1_
  119.6 5.6 %backward.1 = (bf16[256,1024]{1,0:T(8,128)(2,1)}, f32[8,256,256]{2,1,0:T(8,128)S(1)}, bf16[8,256,256]{2,1,0:T(8,128)(2,1)S(1)}) custom-call(s32[36]{0:T(128)S(1)} %concatenate.16.info, f32[256,512]{1,0:T(8,128)S(1)} %get-tuple-element.40.rest_0_, f32[256,512]{1,0:T(8,128)S(1)} %collective-permute-done.12.rest_1_, f32[256,512]{1,0:T(8,128)S(1)} %copy-done.8, ...), custom_call_target="tpu_custom_call" | custom-call | flops 8000000000 | bytes 10485760 | tf_op jit(solution)/shard_map/backward/pallas_call | solution.py:241
  125.3 1.6 collective-permute-start.15
  126.8 2.3 %collective-permute-done.15 = bf16[8,256,256]{2,1,0:T(8,128)(2,1)S(1)} collective-permute-done((bf16[8,256,256]{2,1,0:T(8,128)(2,1)S(1)}, bf16[8,256,256]{2,1,0:T(8,128)(2,1)S(1)}, u32[]{:S(2)}, u32[]{:S(2)}) %collective-permute-start.15) | collective-permute-done | bytes 1048608 | tf_op jit(solution)/shard_map/ppermute | solution.py:34
  129.5 32.0 %all_to_all.15 = bf16[8,256,256]{2,1,0:T(8,128)(2,1)S(1)} all-to-all(bf16[8,256,256]{2,1,0:T(8,128)(2,1)S(1)} %add_convert_fusion), channel_id=1, replica_groups={{0,16,32,48,64,80,96,112},{8,24,40,56,72,88,104,120},{1,17,33,49,65,81,..., dimensions={0} | all-to-all | bytes 2097152 | tf_op jit(solution)/shard_map/all_to_all | solution.py:411
  (72 shorter events, 15.8 us)
Async XLA Ops:
  2.8 27.6 %collective-permute-start.6 = (bf16[512,512]{1,0:T(8,128)(2,1)}, bf16[512,512]{1,0:T(8,128)(2,1)}, u32[]{:S(2)}, u32[]{:S(2)}) collective-permute-start(bf16[512,512]{1,0:T(8,128)(2,1)} %get-tuple-element.50), channel_id=1, source_target_pairs={{0,96},{8,104},{16,112},{24,120},{32,0},{40,8},{48,16},{56,24},{64... | collective-permute-start | bytes 1572872 | tf_op jit(solution)/shard_map/ppermute | solution.py:34
  5.7 26.9 %collective-permute-start.5 = (bf16[512,512]{1,0:T(8,128)(2,1)}, bf16[512,512]{1,0:T(8,128)(2,1)}, u32[]{:S(2)}, u32[]{:S(2)}) collective-permute-start(bf16[512,512]{1,0:T(8,128)(2,1)} %get-tuple-element.50), channel_id=1, source_target_pairs={{0,32},{8,40},{16,48},{24,56},{32,64},{40,72},{48,80},{56,88},{64,... | collective-permute-start | bytes 1572872 | tf_op jit(solution)/shard_map/ppermute | solution.py:34
  5.7 26.9 %collective-permute-start.7 = (bf16[512,512]{1,0:T(8,128)(2,1)}, bf16[512,512]{1,0:T(8,128)(2,1)}, u32[]{:S(2)}, u32[]{:S(2)}) collective-permute-start(bf16[512,512]{1,0:T(8,128)(2,1)} %get-tuple-element.50), channel_id=1, source_target_pairs={{0,64},{8,72},{16,80},{24,88},{32,96},{40,104},{48,112},{56,120},{... | collective-permute-start | bytes 1572872 | tf_op jit(solution)/shard_map/ppermute | solution.py:34
  8.0 1.3 collective-permute-start
  8.2 12.3 %collective-permute-start.2 = (bf16[256,512]{1,0:T(8,128)(2,1)S(1)}, bf16[256,512]{1,0:T(8,128)(2,1)S(1)}, u32[]{:S(2)}, u32[]{:S(2)}) collective-permute-start(bf16[256,512]{1,0:T(8,128)(2,1)S(1)} %get-tuple-element.53), channel_id=1, source_target_pairs={{0,8},{8,0},{16,24},{24,16},{32,40},{40,32},{48,56},{56,48},{64,72... | collective-permute-start | bytes 786440 | tf_op jit(solution)/shard_map/ppermute | solution.py:34
  9.4 7.8 %collective-permute-start.1 = (bf16[512,128]{1,0:T(8,128)(2,1)S(1)}, bf16[512,128]{1,0:T(8,128)(2,1)S(1)}, u32[]{:S(2)}, u32[]{:S(2)}) collective-permute-start(bf16[512,128]{1,0:T(8,128)(2,1)S(1)} %pad_maximum_fusion.5), channel_id=1, source_target_pairs={{0,16},{8,24},{16,0},{24,8},{32,48},{40,56},{48,32},{56,40},{64,80... | collective-permute-start | bytes 393224 | tf_op jit(solution)/shard_map/ppermute | solution.py:34
  17.2 18.4 %collective-permute-start.3 = (bf16[512,512]{1,0:T(8,128)(2,1)S(1)}, bf16[512,512]{1,0:T(8,128)(2,1)}, u32[]{:S(2)}, u32[]{:S(2)}) collective-permute-start(bf16[512,512]{1,0:T(8,128)(2,1)S(1)} %get-tuple-element.27), channel_id=1, source_target_pairs={{0,16},{8,24},{16,0},{24,8},{32,48},{40,56},{48,32},{56,40},{64,80... | collective-permute-start | bytes 1572872 | tf_op jit(solution)/shard_map/ppermute | solution.py:34
  20.5 15.1 %copy-start.9 = (bf16[512,512]{1,0:T(8,128)(2,1)}, bf16[512,512]{1,0:T(8,128)(2,1)S(1)}, u32[]{:S(2)}) copy-start(bf16[512,512]{1,0:T(8,128)(2,1)S(1)} %pad_maximum_fusion.3) | copy-start | bytes 1572868
  21.7 23.4 %all-to-all-start = ((bf16[4,1024,128]{2,1,0:T(8,128)(2,1)}), bf16[4,1024,128]{2,1,0:T(8,128)(2,1)S(1)}, u32[]{:S(2)}, u32[]{:S(2)}) async-start(bf16[4,1024,128]{2,1,0:T(8,128)(2,1)} %broadcast_in_dim.31), calls=%async_computation | async-start | bytes 2097152 | tf_op jit(solution)/shard_map/all_to_all | solution.py:336
  25.4 18.6 %collective-permute-start.4 = (bf16[512,512]{1,0:T(8,128)(2,1)S(1)}, bf16[512,512]{1,0:T(8,128)(2,1)}, u32[]{:S(2)}, u32[]{:S(2)}) collective-permute-start(bf16[512,512]{1,0:T(8,128)(2,1)S(1)} %pad_maximum_fusion.3), channel_id=1, source_target_pairs={{0,4},{1,5},{2,6},{3,7},{4,0},{5,1},{6,2},{7,3},{8,12},{9,13},{10,... | collective-permute-start | bytes 1572872 | tf_op jit(solution)/shard_map/ppermute | solution.py:42
  35.6 8.4 %copy-start.10 = (bf16[512,512]{1,0:T(8,128)(2,1)S(1)}, bf16[512,512]{1,0:T(8,128)(2,1)}, u32[]{:S(2)}) copy-start(bf16[512,512]{1,0:T(8,128)(2,1)} %copy-done.9) | copy-start | bytes 1572868
  47.4 4.9 %collective-permute-start.8 = (bf16[4096,128]{1,0:T(8,128)(2,1)S(1)}, bf16[4096,128]{1,0:T(8,128)(2,1)S(1)}, u32[]{:S(2)}, u32[]{:S(2)}) collective-permute-start(bf16[4096,128]{1,0:T(8,128)(2,1)S(1)} %bitcast.38), channel_id=1, source_target_pairs={{0,8},{8,0},{16,24},{24,16},{32,40},{40,32},{48,56},{56,48},{64,72... | collective-permute-start | bytes 3145736 | tf_op jit(solution)/shard_map/ppermute | solution.py:34
  47.4 64.6 %all-to-all-start.1 = ((bf16[4,2,512,512]{3,2,1,0:T(8,128)(2,1)}), bf16[4,2,512,512]{3,2,1,0:T(8,128)(2,1)}, u32[]{:S(2)}, u32[]{:S(2)}) async-start(bf16[4,2,512,512]{3,2,1,0:T(8,128)(2,1)} %broadcast_in_dim.32), calls=%async_computation.1 | async-start | bytes 8388608 | tf_op jit(solution)/shard_map/all_to_all | solution.py:336
  53.3 51.9 %collective-permute-start.13 = (bf16[4,512,512]{2,1,0:T(8,128)(2,1)}, bf16[4,512,512]{2,1,0:T(8,128)(2,1)}, u32[]{:S(2)}, u32[]{:S(2)}) collective-permute-start(bf16[4,512,512]{2,1,0:T(8,128)(2,1)} %pad_maximum_fusion.rest_4_), channel_id=1, source_target_pairs={{0,16},{8,24},{16,0},{24,8},{32,48},{40,56},{48,32},{56,40},{64,80... | collective-permute-start | bytes 6291464 | tf_op jit(solution)/shard_map/ppermute | solution.py:34
  55.1 26.6 %collective-permute-start.11 = (bf16[2,512,512]{2,1,0:T(8,128)(2,1)S(1)}, bf16[2,512,512]{2,1,0:T(8,128)(2,1)S(1)}, u32[]{:S(2)}, u32[]{:S(2)}) collective-permute-start(bf16[2,512,512]{2,1,0:T(8,128)(2,1)S(1)} %pad_maximum_fusion.2.rest_0_), channel_id=1, source_target_pairs={{0,1},{1,2},{2,3},{3,0},{4,5},{5,6},{6,7},{7,4},{8,9},{9,10},{10,1... | collective-permute-start | bytes 3145736 | tf_op jit(solution)/shard_map/ppermute | solution.py:42
  56.6 48.6 %collective-permute-start.10 = (bf16[2,512,512]{2,1,0:T(8,128)(2,1)S(1)}, bf16[2,512,512]{2,1,0:T(8,128)(2,1)S(1)}, u32[]{:S(2)}, u32[]{:S(2)}) collective-permute-start(bf16[2,512,512]{2,1,0:T(8,128)(2,1)S(1)} %pad_maximum_fusion.2.rest_0_), channel_id=1, source_target_pairs={{0,2},{1,3},{2,0},{3,1},{4,6},{5,7},{6,4},{7,5},{8,10},{9,11},{10,... | collective-permute-start | bytes 3145736 | tf_op jit(solution)/shard_map/ppermute | solution.py:42
  59.5 45.7 %collective-permute-start.9 = (bf16[2,512,512]{2,1,0:T(8,128)(2,1)S(1)}, bf16[2,512,512]{2,1,0:T(8,128)(2,1)}, u32[]{:S(2)}, u32[]{:S(2)}) collective-permute-start(bf16[2,512,512]{2,1,0:T(8,128)(2,1)S(1)} %pad_maximum_fusion.2.rest_0_), channel_id=1, source_target_pairs={{0,3},{1,0},{2,1},{3,2},{4,7},{5,4},{6,5},{7,6},{8,11},{9,8},{10,9... | collective-permute-start | bytes 3145736 | tf_op jit(solution)/shard_map/ppermute | solution.py:42
  112.0 6.0 %collective-permute-start.14 = (f32[256,512]{1,0:T(8,128)}, f32[256,512]{1,0:T(8,128)}, u32[]{:S(2)}, u32[]{:S(2)}) collective-permute-start(f32[256,512]{1,0:T(8,128)} %get-tuple-element.44), channel_id=1, source_target_pairs={{0,8},{8,0},{16,24},{24,16},{32,40},{40,32},{48,56},{56,48},{64,72... | collective-permute-start | bytes 1572872 | tf_op jit(solution)/shard_map/ppermute | solution.py:34
  112.0 7.6 %copy-start.2 = (bf16[4,1024,128]{2,1,0:T(8,128)(2,1)S(1)}, bf16[4,1024,128]{2,1,0:T(8,128)(2,1)}, u32[]{:S(2)}) copy-start(bf16[4,1024,128]{2,1,0:T(8,128)(2,1)} %copy-done) | copy-start | bytes 3145732
  112.0 7.6 %copy-start.5 = (bf16[4096,128]{1,0:T(8,128)(2,1)S(1)}, bf16[4096,128]{1,0:T(8,128)(2,1)}, u32[]{:S(2)}) copy-start(bf16[4096,128]{1,0:T(8,128)(2,1)} %copy-done.3) | copy-start | bytes 3145732
  112.0 7.6 %copy-start.6 = (f32[128,2048]{1,0:T(8,128)S(1)}, f32[128,2048]{1,0:T(8,128)}, u32[]{:S(2)}) copy-start(f32[128,2048]{1,0:T(8,128)} %get-tuple-element.36.rest_5_) | copy-start | bytes 3145732
  112.1 7.6 %copy-start.8 = (f32[256,512]{1,0:T(8,128)S(1)}, f32[256,512]{1,0:T(8,128)}, u32[]{:S(2)}) copy-start(f32[256,512]{1,0:T(8,128)} %copy-done.7) | copy-start | bytes 1572868
  117.3 2.3 %collective-permute-start.12 = (f32[256,512]{1,0:T(8,128)S(1)}, f32[256,512]{1,0:T(8,128)S(1)}, u32[]{:S(2)}, u32[]{:S(2)}) collective-permute-start(f32[256,512]{1,0:T(8,128)S(1)} %get-tuple-element.41), channel_id=1, source_target_pairs={{0,8},{8,0},{16,24},{24,16},{32,40},{40,32},{48,56},{56,48},{64,72... | collective-permute-start | bytes 1572872 | tf_op jit(solution)/shard_map/ppermute | solution.py:34
  125.3 3.8 %collective-permute-start.15 = (bf16[8,256,256]{2,1,0:T(8,128)(2,1)S(1)}, bf16[8,256,256]{2,1,0:T(8,128)(2,1)S(1)}, u32[]{:S(2)}, u32[]{:S(2)}) collective-permute-start(bf16[8,256,256]{2,1,0:T(8,128)(2,1)S(1)} %get-tuple-element.48), channel_id=1, source_target_pairs={{0,8},{8,0},{16,24},{24,16},{32,40},{40,32},{48,56},{56,48},{64,72... | collective-permute-start | bytes 3145736 | tf_op jit(solution)/shard_map/ppermute | solution.py:34
  (9 other events, 33.5 us)

commit v20 on v19

--- a/solution.py
+++ b/solution.py
@@ -11,7 +11,6 @@
 HEAD_WIDTH = 128
 KEY_BLOCK = 256
 MOST = 2560
-CHUNKS = 2
 SPLIT = 4 * HEAD_WIDTH
 PAIR = 2
 MASKED = -1e30
@@ -170,7 +169,7 @@
 
 
 def backward_kernel(heads, info, *rest):
-    terms, rest = rest[:4], rest[4:]
+    (mine, got), rest = rest[:2], rest[2:]
     probs_ref, out_ref, q_ref, here_ref, there_ref, gq_ref, own_ref, other_ref, *scratch = rest
     grad_t, stack, delta, total_q, dscores, other = scratch
     step = pl.program_id(0)
@@ -185,13 +184,7 @@
         for h in range(heads):
             cols = slice(h * rows, (h + 1) * rows)
             wide = slice(h * HEAD_WIDTH, (h + 1) * HEAD_WIDTH)
-            at = h * HEAD_WIDTH
-            mine, got = terms[:2]
-            if at >= mine.shape[1]:
-                at -= mine.shape[1]
-                mine, got = terms[2:]
-            here = slice(at, at + HEAD_WIDTH)
-            grad = (mine[:, here] + got[:, here]).astype(BF16)
+            grad = (mine[:, wide] + got[:, wide].astype(F32)).astype(BF16)
             turned = grad.T
             grad_t[:, cols] = turned
             stack[cols, :HEAD_WIDTH] = q_ref[:, wide]
@@ -278,49 +271,64 @@
     )(info, *terms, in_hbm(probs), outs, in_hbm(queries), here, there)
 
 
-def project_kernel(chips, slots, *rest):
-    grads, (*stacks, own_ref, other_ref, grad) = rest[: chips // 2], rest[chips // 2 :]
+def project_kernel(slots, *rest):
+    *operands, own_ref, other_ref, grad, weight, total, sems = rest
+    chips = grad.shape[0]
+    grads, stacks = operands[: chips // 2], operands[chips // 2 :]
+    sources = [ref.at[j] for ref in stacks for j in range(ref.shape[0])]
+    copies = [
+        pltpu.make_async_copy(source, weight.at[k], sems.at[k]) for k, source in enumerate(sources)
+    ]
+    for copy in copies:
+        copy.start()
     for i, ref in enumerate(grads):
         grad[2 * i : 2 * i + 2] = ref[...]
     half = own_ref.shape[0]
-    k = 0
-    for ref in stacks:
-        blocks = [ref] if len(ref.shape) == 2 else [ref.at[j] for j in range(ref.shape[0])]
-        for block in blocks:
-            for out, row in ((own_ref, 0), (other_ref, half)):
-                term = dot_t(grad[slots[k], row : row + half, :], block[...])
-                if k == 0:
-                    out[...] = term
-                else:
-                    out[...] += term
-            k += 1
-
-
-def project(part, slots, grads, stacks):
+    features = weight.shape[1]
+    for k, copy in enumerate(copies):
+        copy.wait()
+        cols = slice(k // chips * features, (k // chips + 1) * features)
+        for out, row in ((own_ref, 0), (total, half)):
+            term = dot_t(grad[slots[k], row : row + half, :], weight[k])
+            if k % chips == 0:
+                out[:, cols] = term
+            else:
+                out[:, cols] += term
+    other_ref[...] = total[...].astype(BF16)
+
+
+def project(slots, grads, stacks):
     chips = 2 * len(grads)
     _, tokens, depth = grads[0].shape
-    features = stacks[0].shape[-2]
-    half = jax.ShapeDtypeStruct((tokens // 2, features), F32)
+    blocks = sum(stack.shape[0] for stack in stacks)
+    features = stacks[0].shape[1]
+    shape = (tokens // 2, blocks // chips * features)
 
     def once(shape):
         return pl.BlockSpec(shape, lambda i: (0,) * len(shape), pipeline_mode=pl.Buffered(1))
 
     return pl.pallas_call(
-        functools.partial(project_kernel, chips),
+        project_kernel,
         grid=(1,),
         in_specs=[pl.BlockSpec(memory_space=pltpu.SMEM)]
-        + [once(ref.shape) for ref in (*grads, *stacks)],
-        out_specs=[once(half.shape)] * 2,
-        out_shape=[half, half],
-        scratch_shapes=[pltpu.VMEM((chips, tokens, depth), BF16)],
+        + [once(ref.shape) for ref in grads]
+        + [pl.BlockSpec(memory_space=pl.ANY)] * len(stacks),
+        out_specs=[once(shape)] * 2,
+        out_shape=[jax.ShapeDtypeStruct(shape, F32), jax.ShapeDtypeStruct(shape, BF16)],
+        scratch_shapes=[
+            pltpu.VMEM((chips, tokens, depth), BF16),
+            pltpu.VMEM((blocks, features, depth), BF16),
+            pltpu.VMEM(shape, F32),
+            pltpu.SemaphoreType.DMA((blocks,)),
+        ],
         compiler_params=pltpu.CompilerParams(vmem_limit_bytes=VMEM_LIMIT),
         cost_estimate=pl.CostEstimate(
-            flops=2 * tokens * features * depth * chips,
-            bytes_accessed=10 * 2**20,
+            flops=2 * tokens * features * depth * blocks,
+            bytes_accessed=12 * 2**20,
             transcendentals=0,
         ),
-        name="project%d" % part,
-    )(slots, *grads, *[in_hbm(stack) if len(stack.shape) == 3 else stack for stack in stacks])
+        name="project",
+    )(slots, *grads, *[in_hbm(stack) for stack in stacks])
 
 
 def local(queries, keys, values, grad_out, out_weight, lengths):
@@ -394,16 +402,11 @@
         return (source - t) % 4 * 2 + jnp.where(source // 4 == t // 4, 0, 1)
 
     near = [slot(x + i, z) for i in (0, -1, 1, 2)]
-    slots = [
-        jnp.stack([slot(i, z_) for i in range(4) for z_ in (z, 1 - z)]).astype(jnp.int32),
-        jnp.stack(near + [slot(x + i, 1 - z) for i in (0, -1, 1, 2)]).astype(jnp.int32),
-    ]
-    slots[0] = after(slots[0], outs)
-    stacks = [[plane0], [sent, rest]]
-    terms = []
-    for part in range(CHUNKS):
-        mine, other = project(part, slots[part], all_grad, stacks[part])
-        terms += [mine, dp_move(other, 0, 0, 1)]
+    slots = [slot(i, z_) for i in range(4) for z_ in (z, 1 - z)]
+    slots += near + [slot(x + i, 1 - z) for i in (0, -1, 1, 2)]
+    slots = after(jnp.stack(slots).astype(jnp.int32), outs)
+    mine, other = project(slots, all_grad, [plane0, sent, rest])
+    terms = [mine, dp_move(other, 0, 0, 1)]
     grad_queries, own_sums, other_sums = backward(info, terms, probs, outs, queries, ring, swapped)
 
     groups = [[2 * i + c for i in range(8)] for c in range(2)]

time: 164 us -> 159 us (0.970)
  local copies, waits for them, and re-layouts: 12.1 us -> 7.76 us
  waiting for transfers between devices: 48.9 us -> 51.8 us
  Pallas kernels: 24 us -> 21.8 us
    unnamed x30 -> x14, local copies, waits for them, and re-layouts: 4.32 us -> 0.03 us
    ppermute x4, waiting for transfers between devices: 41.7 us -> 44.2 us  [tensor_move(): return lax.ppermute(value, 'tensor', pairs)]
    pallas_call x2 -> x1, Pallas kernels: 11.2 us -> 9.07 us  [project(): pl.pallas_call(project_kernel, grid=(1,), in_specs=[pl.BlockSpec(memory_s...]
    ppermute x12 -> x11, starting transfers between devices: 17.1 us -> 16.4 us  [dp_move(): return lax.ppermute(value, 'dp', pairs)]
    ppermute x12 -> x11, waiting for transfers between devices: 7.22 us -> 7.54 us  [dp_move(): return lax.ppermute(value, 'dp', pairs)]
  transfers between devices with their start and end apart: 18 -> 17, of which waited for: 8 -> 8; matrix products, arithmetic and copies ran while one was open for 5% -> 5% of each run, Pallas kernels for 11% -> 5%
where the time goes in v20:
time: 159 us; the launch traced here: 158 us
  waiting for transfers between devices  51.8 us (33%)
  blocking collectives  32 us (20%)
  starting transfers between devices  31.7 us (20%)
  Pallas kernels  21.8 us (14%)
  local copies, waits for them, and re-layouts  7.76 us (5%)
  between operations  6.72 us (4%)
  other arithmetic  6.17 us (4%)
    ppermute x4, waiting for transfers between devices, tensor_move(): return lax.ppermute(value, 'tensor', pairs)  44.2 us
    all_to_all x1, blocking collectives, local(): lax.all_to_all(chip_sums, 'dp', 0, 0, axis_index_groups=groups, tiled=True)  32 us
    ppermute x11, starting transfers between devices, dp_move(): return lax.ppermute(value, 'dp', pairs)  16.4 us
    pallas_call x1, Pallas kernels, project(): pl.pallas_call(project_kernel, grid=(1,), in_specs=[pl.BlockSpec(memory_s...  9.07 us
    all_to_all x2, starting transfers between devices, exchange(): lax.all_to_all(copies, axis, 0, 0, axis_index_groups=groups, tiled=True)  8.38 us
    ppermute x11, waiting for transfers between devices, dp_move(): return lax.ppermute(value, 'dp', pairs)  7.54 us
    pallas_call x1, Pallas kernels, forward(): pl.pallas_call(forward_kernel, grid_spec=pltpu.PrefetchScalarGridSpec(num...  7.29 us
    ppermute x4, starting transfers between devices, tensor_move(): return lax.ppermute(value, 'tensor', pairs)  6.85 us
  transfers between devices with their start and end apart: 17, of which 8 were waited for; matrix products, arithmetic and copies ran while one was open for 5% of the time, Pallas kernels for 5%

profile of v20, /device:TPU:0, one launch (start us, length us, event | category | flops | bytes accessed | tf_op | source)
XLA Modules:
  0.0 157.9 jit_solution(2782516737353372203)
XLA Ops:
  0.7 2.2 %slice_bitcast_fusion.1 = (bf16[1,512,512]{2,1,0:T(8,128)(2,1)S(1)}, bf16[512,512]{1,0:T(8,128)(2,1)}, bf16[512,512]{1,0:T(8,128)(2,1)S(1)}) fusion(bf16[1024,512]{1,0:T(8,128)(2,1)} %param.10), kind=kLoop, calls=%fused_computation.34 | loop fusion | bytes 2621440 | tf_op jit(solution)/shard_map/stack | solution.py:387
  2.9 2.8 %collective-permute-start.6 = (bf16[512,512]{1,0:T(8,128)(2,1)}, bf16[512,512]{1,0:T(8,128)(2,1)}, u32[]{:S(2)}, u32[]{:S(2)}) collective-permute-start(bf16[512,512]{1,0:T(8,128)(2,1)} %get-tuple-element.46), channel_id=1, source_target_pairs={{0,96},{8,104},{16,112},{24,120},{32,0},{40,8},{48,16},{56,24},{64... | collective-permute-start | bytes 1572872 | tf_op jit(solution)/shard_map/ppermute | solution.py:33
  5.7 2.3 %collective-permute-start.7 = (bf16[512,512]{1,0:T(8,128)(2,1)}, bf16[512,512]{1,0:T(8,128)(2,1)}, u32[]{:S(2)}, u32[]{:S(2)}) collective-permute-start(bf16[512,512]{1,0:T(8,128)(2,1)} %get-tuple-element.46), channel_id=1, source_target_pairs={{0,64},{8,72},{16,80},{24,88},{32,96},{40,104},{48,112},{56,120},{... | collective-permute-start | bytes 1572872 | tf_op jit(solution)/shard_map/ppermute | solution.py:33
  9.4 4.0 %collective-permute-start.1 = (bf16[512,128]{1,0:T(8,128)(2,1)S(1)}, bf16[512,128]{1,0:T(8,128)(2,1)S(1)}, u32[]{:S(2)}, u32[]{:S(2)}) collective-permute-start(bf16[512,128]{1,0:T(8,128)(2,1)S(1)} %pad_maximum_fusion.5), channel_id=1, source_target_pairs={{0,16},{8,24},{16,0},{24,8},{32,48},{40,56},{48,32},{56,40},{64,80... | collective-permute-start | bytes 393224 | tf_op jit(solution)/shard_map/ppermute | solution.py:33
  17.2 3.3 %collective-permute-start.3 = (bf16[512,512]{1,0:T(8,128)(2,1)S(1)}, bf16[512,512]{1,0:T(8,128)(2,1)}, u32[]{:S(2)}, u32[]{:S(2)}) collective-permute-start(bf16[512,512]{1,0:T(8,128)(2,1)S(1)} %get-tuple-element.25), channel_id=1, source_target_pairs={{0,16},{8,24},{16,0},{24,8},{32,48},{40,56},{48,32},{56,40},{64,80... | collective-permute-start | bytes 1572872 | tf_op jit(solution)/shard_map/ppermute | solution.py:33
  21.7 3.5 %all-to-all-start = ((bf16[4,1024,128]{2,1,0:T(8,128)(2,1)}), bf16[4,1024,128]{2,1,0:T(8,128)(2,1)S(1)}, u32[]{:S(2)}, u32[]{:S(2)}) async-start(bf16[4,1024,128]{2,1,0:T(8,128)(2,1)} %broadcast_in_dim.31), calls=%async_computation | async-start | bytes 2097152 | tf_op jit(solution)/shard_map/all_to_all | solution.py:344
  30.5 2.1 %collective-permute-done.5 = bf16[512,512]{1,0:T(8,128)(2,1)} collective-permute-done((bf16[512,512]{1,0:T(8,128)(2,1)}, bf16[512,512]{1,0:T(8,128)(2,1)}, u32[]{:S(2)}, u32[]{:S(2)}) %collective-permute-start.5) | collective-permute-done | bytes 524320 | tf_op jit(solution)/shard_map/ppermute | solution.py:33
  32.6 3.0 %pad_maximum_fusion.rest_5_ = bf16[4,512,512]{2,1,0:T(8,128)(2,1)} fusion(bf16[1,512,512]{2,1,0:T(8,128)(2,1)} %bitcast.8, bf16[1,512,512]{2,1,0:T(8,128)(2,1)} %bitcast.7, bf16[1,512,512]{2,1,0:T(8,128)(2,1)} %bitcast.6, bf16[1,512,512]{2,1,0:T(8,128)(2,1)S(1)} %get-tuple-element.45), kind=kLoop, calls=%fused_computation | loop fusion | flops 3145728 | bytes 4194304 | tf_op jit(solution)/shard_map/stack | solution.py:387
  36.8 7.1 %collective-permute-done.4 = bf16[512,512]{1,0:T(8,128)(2,1)} collective-permute-done((bf16[512,512]{1,0:T(8,128)(2,1)S(1)}, bf16[512,512]{1,0:T(8,128)(2,1)}, u32[]{:S(2)}, u32[]{:S(2)}) %collective-permute-start.4) | collective-permute-done | bytes 524320 | tf_op jit(solution)/shard_map/ppermute | solution.py:41
  45.1 2.3 %broadcast_in_dim.32 = bf16[4,2,512,512]{3,2,1,0:T(8,128)(2,1)} broadcast(bf16[2,512,512]{2,1,0:T(8,128)(2,1)S(1)} %pad_maximum_fusion.1), dimensions={1,2,3} | broadcast | bytes 5242880 | tf_op jit(solution)/shard_map/broadcast_in_dim | solution.py:341
  47.4 4.9 %all-to-all-start.1 = ((bf16[4,2,512,512]{3,2,1,0:T(8,128)(2,1)}), bf16[4,2,512,512]{3,2,1,0:T(8,128)(2,1)}, u32[]{:S(2)}, u32[]{:S(2)}) async-start(bf16[4,2,512,512]{3,2,1,0:T(8,128)(2,1)} %broadcast_in_dim.32), calls=%async_computation.1 | async-start | bytes 8388608 | tf_op jit(solution)/shard_map/all_to_all | solution.py:344
  52.3 1.8 %collective-permute-start.12 = (bf16[4,512,512]{2,1,0:T(8,128)(2,1)}, bf16[4,512,512]{2,1,0:T(8,128)(2,1)}, u32[]{:S(2)}, u32[]{:S(2)}) collective-permute-start(bf16[4,512,512]{2,1,0:T(8,128)(2,1)} %pad_maximum_fusion.rest_5_), channel_id=1, source_target_pairs={{0,16},{8,24},{16,0},{24,8},{32,48},{40,56},{48,32},{56,40},{64,80... | collective-permute-start | bytes 6291464 | tf_op jit(solution)/shard_map/ppermute | solution.py:33
  54.1 1.6 collective-permute-start.11
  55.7 2.9 %collective-permute-start.10 = (bf16[2,512,512]{2,1,0:T(8,128)(2,1)S(1)}, bf16[2,512,512]{2,1,0:T(8,128)(2,1)}, u32[]{:S(2)}, u32[]{:S(2)}) collective-permute-start(bf16[2,512,512]{2,1,0:T(8,128)(2,1)S(1)} %pad_maximum_fusion.2.rest_0_), channel_id=1, source_target_pairs={{0,2},{1,3},{2,0},{3,1},{4,6},{5,7},{6,4},{7,5},{8,10},{9,11},{10,... | collective-permute-start | bytes 3145736 | tf_op jit(solution)/shard_map/ppermute | solution.py:41
  58.6 1.3 collective-permute-start.9
  60.0 7.3 %forward.1 = (bf16[2816,2048]{1,0:T(8,128)(2,1)}, f32[128,2048]{1,0:T(8,128)}) custom-call(s32[36]{0:T(128)S(1)} %concatenate.16.info, s32[1,256]{1,0:T(1,128)S(1)} %iota_add_fusion.pos_ref, s32[1,256]{1,0:T(1,128)S(1)} %bitcast.41, bf16[256,1024]{1,0:T(8,128)(2,1)} %rest_4_.1, bf16[4096,128]{1,0:T(8,128)(2,1)S(1)} %bitcast.39, ...), custom_call_target="tpu_custom_call" | custom-call | flops 100000000 | bytes 1048576 | tf_op jit(solution)/shard_map/forward/pallas_call | solution.py:140
  67.3 13.5 %collective-permute-done.11.rest_3_ = bf16[2,512,512]{2,1,0:T(8,128)(2,1)} collective-permute-done((bf16[2,512,512]{2,1,0:T(8,128)(2,1)S(1)}, bf16[2,512,512]{2,1,0:T(8,128)(2,1)}, u32[]{:S(2)}, u32[]{:S(2)}) %collective-permute-start.11) | collective-permute-done | bytes 1048608 | tf_op jit(solution)/shard_map/ppermute | solution.py:41
  80.8 23.6 %collective-permute-done.10.rest_2_ = bf16[2,512,512]{2,1,0:T(8,128)(2,1)} collective-permute-done((bf16[2,512,512]{2,1,0:T(8,128)(2,1)S(1)}, bf16[2,512,512]{2,1,0:T(8,128)(2,1)}, u32[]{:S(2)}, u32[]{:S(2)}) %collective-permute-start.10) | collective-permute-done | bytes 1048608 | tf_op jit(solution)/shard_map/ppermute | solution.py:41
  104.5 9.1 %project.1 = (f32[256,1024]{1,0:T(8,128)S(1)}, bf16[256,1024]{1,0:T(8,128)(2,1)S(1)}) custom-call(s32[16]{0:T(128)S(1)} %stack.127.slots, bf16[2,512,512]{2,1,0:T(8,128)(2,1)S(1)} %pad_maximum_fusion.2.rest_0_, bf16[2,512,512]{2,1,0:T(8,128)(2,1)} %collective-permute-done.9.rest_1_, bf16[2,512,512]{2,1,0:T(8,128)(2,1)} %collective-permute-done.10.rest_2_, ...), custom_call_target="tpu_custom_call" | custom-call | flops 4294967296 | bytes 12582912 | tf_op jit(solution)/shard_map/project/pallas_call | solution.py:310
  113.8 1.9 %collective-permute-done.13.rest_1_ = bf16[256,1024]{1,0:T(8,128)(2,1)S(1)} collective-permute-done((bf16[256,1024]{1,0:T(8,128)(2,1)S(1)}, bf16[256,1024]{1,0:T(8,128)(2,1)S(1)}, u32[]{:S(2)}, u32[]{:S(2)}) %collective-permute-start.13) | collective-permute-done | bytes 524320 | tf_op jit(solution)/shard_map/ppermute | solution.py:33
  115.7 5.4 %backward.1 = (bf16[256,1024]{1,0:T(8,128)(2,1)}, f32[8,256,256]{2,1,0:T(8,128)S(1)}, bf16[8,256,256]{2,1,0:T(8,128)(2,1)S(1)}) custom-call(s32[36]{0:T(128)S(1)} %concatenate.16.info, f32[256,1024]{1,0:T(8,128)S(1)} %get-tuple-element.39.rest_0_, bf16[256,1024]{1,0:T(8,128)(2,1)S(1)} %collective-permute-done.13.rest_1_, ...), custom_call_target="tpu_custom_call" | custom-call | flops 8000000000 | bytes 10485760 | tf_op jit(solution)/shard_map/backward/pallas_call | solution.py:234
  121.1 1.3 collective-permute-start.14
  122.5 2.3 %collective-permute-done.14 = bf16[8,256,256]{2,1,0:T(8,128)(2,1)S(1)} collective-permute-done((bf16[8,256,256]{2,1,0:T(8,128)(2,1)S(1)}, bf16[8,256,256]{2,1,0:T(8,128)(2,1)S(1)}, u32[]{:S(2)}, u32[]{:S(2)}) %collective-permute-start.14) | collective-permute-done | bytes 1048608 | tf_op jit(solution)/shard_map/ppermute | solution.py:33
  125.1 32.0 %all_to_all.15 = bf16[8,256,256]{2,1,0:T(8,128)(2,1)S(1)} all-to-all(bf16[8,256,256]{2,1,0:T(8,128)(2,1)S(1)} %add_convert_fusion), channel_id=1, replica_groups={{0,16,32,48,64,80,96,112},{8,24,40,56,72,88,104,120},{1,17,33,49,65,81,..., dimensions={0} | all-to-all | bytes 2097152 | tf_op jit(solution)/shard_map/all_to_all | solution.py:414
  (52 shorter events, 9.6 us)
Async XLA Ops:
  0.6 7.4 %copy-start.5 = (bf16[256,128]{1,0:T(8,128)(2,1)S(1)}, bf16[256,128]{1,0:T(8,128)(2,1)}, u32[]{:S(2)}) copy-start(bf16[256,128]{1,0:T(8,128)(2,1)} %param.8) | copy-start | bytes 196612
  0.6 7.4 %copy-start.4 = (bf16[256,128]{1,0:T(8,128)(2,1)S(1)}, bf16[256,128]{1,0:T(8,128)(2,1)}, u32[]{:S(2)}) copy-start(bf16[256,128]{1,0:T(8,128)(2,1)} %param.7) | copy-start | bytes 196612
  0.7 7.5 %copy-start.3 = (bf16[256,1024]{1,0:T(8,128)(2,1)S(1)}, bf16[256,1024]{1,0:T(8,128)(2,1)}, u32[]{:S(2)}) copy-start(bf16[256,1024]{1,0:T(8,128)(2,1)} %param.9) | copy-start | bytes 1572868
  2.9 27.6 %collective-permute-start.6 = (bf16[512,512]{1,0:T(8,128)(2,1)}, bf16[512,512]{1,0:T(8,128)(2,1)}, u32[]{:S(2)}, u32[]{:S(2)}) collective-permute-start(bf16[512,512]{1,0:T(8,128)(2,1)} %get-tuple-element.46), channel_id=1, source_target_pairs={{0,96},{8,104},{16,112},{24,120},{32,0},{40,8},{48,16},{56,24},{64... | collective-permute-start | bytes 1572872 | tf_op jit(solution)/shard_map/ppermute | solution.py:33
  5.7 26.9 %collective-permute-start.5 = (bf16[512,512]{1,0:T(8,128)(2,1)}, bf16[512,512]{1,0:T(8,128)(2,1)}, u32[]{:S(2)}, u32[]{:S(2)}) collective-permute-start(bf16[512,512]{1,0:T(8,128)(2,1)} %get-tuple-element.46), channel_id=1, source_target_pairs={{0,32},{8,40},{16,48},{24,56},{32,64},{40,72},{48,80},{56,88},{64,... | collective-permute-start | bytes 1572872 | tf_op jit(solution)/shard_map/ppermute | solution.py:33
  5.7 26.9 %collective-permute-start.7 = (bf16[512,512]{1,0:T(8,128)(2,1)}, bf16[512,512]{1,0:T(8,128)(2,1)}, u32[]{:S(2)}, u32[]{:S(2)}) collective-permute-start(bf16[512,512]{1,0:T(8,128)(2,1)} %get-tuple-element.46), channel_id=1, source_target_pairs={{0,64},{8,72},{16,80},{24,88},{32,96},{40,104},{48,112},{56,120},{... | collective-permute-start | bytes 1572872 | tf_op jit(solution)/shard_map/ppermute | solution.py:33
  8.0 1.3 collective-permute-start
  8.2 12.3 %collective-permute-start.2 = (bf16[256,512]{1,0:T(8,128)(2,1)S(1)}, bf16[256,512]{1,0:T(8,128)(2,1)S(1)}, u32[]{:S(2)}, u32[]{:S(2)}) collective-permute-start(bf16[256,512]{1,0:T(8,128)(2,1)S(1)} %get-tuple-element.49), channel_id=1, source_target_pairs={{0,8},{8,0},{16,24},{24,16},{32,40},{40,32},{48,56},{56,48},{64,72... | collective-permute-start | bytes 786440 | tf_op jit(solution)/shard_map/ppermute | solution.py:33
  9.4 7.8 %collective-permute-start.1 = (bf16[512,128]{1,0:T(8,128)(2,1)S(1)}, bf16[512,128]{1,0:T(8,128)(2,1)S(1)}, u32[]{:S(2)}, u32[]{:S(2)}) collective-permute-start(bf16[512,128]{1,0:T(8,128)(2,1)S(1)} %pad_maximum_fusion.5), channel_id=1, source_target_pairs={{0,16},{8,24},{16,0},{24,8},{32,48},{40,56},{48,32},{56,40},{64,80... | collective-permute-start | bytes 393224 | tf_op jit(solution)/shard_map/ppermute | solution.py:33
  17.2 18.5 %collective-permute-start.3 = (bf16[512,512]{1,0:T(8,128)(2,1)S(1)}, bf16[512,512]{1,0:T(8,128)(2,1)}, u32[]{:S(2)}, u32[]{:S(2)}) collective-permute-start(bf16[512,512]{1,0:T(8,128)(2,1)S(1)} %get-tuple-element.25), channel_id=1, source_target_pairs={{0,16},{8,24},{16,0},{24,8},{32,48},{40,56},{48,32},{56,40},{64,80... | collective-permute-start | bytes 1572872 | tf_op jit(solution)/shard_map/ppermute | solution.py:33
  20.5 4.8 %copy-start.6 = (s32[8]{0:T(128)S(1)}, s32[8]{0:T(128)}, u32[]{:S(2)}) copy-start(s32[8]{0:T(128)} %param.11) | copy-start | bytes 100
  20.5 15.1 %copy-start.1 = (bf16[512,512]{1,0:T(8,128)(2,1)}, bf16[512,512]{1,0:T(8,128)(2,1)S(1)}, u32[]{:S(2)}) copy-start(bf16[512,512]{1,0:T(8,128)(2,1)S(1)} %pad_maximum_fusion.3) | copy-start | bytes 1572868
  21.7 23.4 %all-to-all-start = ((bf16[4,1024,128]{2,1,0:T(8,128)(2,1)}), bf16[4,1024,128]{2,1,0:T(8,128)(2,1)S(1)}, u32[]{:S(2)}, u32[]{:S(2)}) async-start(bf16[4,1024,128]{2,1,0:T(8,128)(2,1)} %broadcast_in_dim.31), calls=%async_computation | async-start | bytes 2097152 | tf_op jit(solution)/shard_map/all_to_all | solution.py:344
  25.4 18.5 %collective-permute-start.4 = (bf16[512,512]{1,0:T(8,128)(2,1)S(1)}, bf16[512,512]{1,0:T(8,128)(2,1)}, u32[]{:S(2)}, u32[]{:S(2)}) collective-permute-start(bf16[512,512]{1,0:T(8,128)(2,1)S(1)} %pad_maximum_fusion.3), channel_id=1, source_target_pairs={{0,4},{1,5},{2,6},{3,7},{4,0},{5,1},{6,2},{7,3},{8,12},{9,13},{10,... | collective-permute-start | bytes 1572872 | tf_op jit(solution)/shard_map/ppermute | solution.py:41
  35.6 8.3 %copy-start.2 = (bf16[512,512]{1,0:T(8,128)(2,1)S(1)}, bf16[512,512]{1,0:T(8,128)(2,1)}, u32[]{:S(2)}) copy-start(bf16[512,512]{1,0:T(8,128)(2,1)} %copy-done.1) | copy-start | bytes 1572868
  47.4 4.9 %collective-permute-start.8 = (bf16[4096,128]{1,0:T(8,128)(2,1)S(1)}, bf16[4096,128]{1,0:T(8,128)(2,1)S(1)}, u32[]{:S(2)}, u32[]{:S(2)}) collective-permute-start(bf16[4096,128]{1,0:T(8,128)(2,1)S(1)} %bitcast.38), channel_id=1, source_target_pairs={{0,8},{8,0},{16,24},{24,16},{32,40},{40,32},{48,56},{56,48},{64,72... | collective-permute-start | bytes 3145736 | tf_op jit(solution)/shard_map/ppermute | solution.py:33
  47.4 57.0 %all-to-all-start.1 = ((bf16[4,2,512,512]{3,2,1,0:T(8,128)(2,1)}), bf16[4,2,512,512]{3,2,1,0:T(8,128)(2,1)}, u32[]{:S(2)}, u32[]{:S(2)}) async-start(bf16[4,2,512,512]{3,2,1,0:T(8,128)(2,1)} %broadcast_in_dim.32), calls=%async_computation.1 | async-start | bytes 8388608 | tf_op jit(solution)/shard_map/all_to_all | solution.py:344
  52.3 52.1 %collective-permute-start.12 = (bf16[4,512,512]{2,1,0:T(8,128)(2,1)}, bf16[4,512,512]{2,1,0:T(8,128)(2,1)}, u32[]{:S(2)}, u32[]{:S(2)}) collective-permute-start(bf16[4,512,512]{2,1,0:T(8,128)(2,1)} %pad_maximum_fusion.rest_5_), channel_id=1, source_target_pairs={{0,16},{8,24},{16,0},{24,8},{32,48},{40,56},{48,32},{56,40},{64,80... | collective-permute-start | bytes 6291464 | tf_op jit(solution)/shard_map/ppermute | solution.py:33
  54.1 26.7 %collective-permute-start.11 = (bf16[2,512,512]{2,1,0:T(8,128)(2,1)S(1)}, bf16[2,512,512]{2,1,0:T(8,128)(2,1)}, u32[]{:S(2)}, u32[]{:S(2)}) collective-permute-start(bf16[2,512,512]{2,1,0:T(8,128)(2,1)S(1)} %pad_maximum_fusion.2.rest_0_), channel_id=1, source_target_pairs={{0,1},{1,2},{2,3},{3,0},{4,5},{5,6},{6,7},{7,4},{8,9},{9,10},{10,1... | collective-permute-start | bytes 3145736 | tf_op jit(solution)/shard_map/ppermute | solution.py:41
  55.7 48.7 %collective-permute-start.10 = (bf16[2,512,512]{2,1,0:T(8,128)(2,1)S(1)}, bf16[2,512,512]{2,1,0:T(8,128)(2,1)}, u32[]{:S(2)}, u32[]{:S(2)}) collective-permute-start(bf16[2,512,512]{2,1,0:T(8,128)(2,1)S(1)} %pad_maximum_fusion.2.rest_0_), channel_id=1, source_target_pairs={{0,2},{1,3},{2,0},{3,1},{4,6},{5,7},{6,4},{7,5},{8,10},{9,11},{10,... | collective-permute-start | bytes 3145736 | tf_op jit(solution)/shard_map/ppermute | solution.py:41
  58.6 45.8 %collective-permute-start.9 = (bf16[2,512,512]{2,1,0:T(8,128)(2,1)S(1)}, bf16[2,512,512]{2,1,0:T(8,128)(2,1)}, u32[]{:S(2)}, u32[]{:S(2)}) collective-permute-start(bf16[2,512,512]{2,1,0:T(8,128)(2,1)S(1)} %pad_maximum_fusion.2.rest_0_), channel_id=1, source_target_pairs={{0,3},{1,0},{2,1},{3,2},{4,7},{5,4},{6,5},{7,6},{8,11},{9,8},{10,9... | collective-permute-start | bytes 3145736 | tf_op jit(solution)/shard_map/ppermute | solution.py:41
  104.5 11.3 %copy-start = (f32[128,2048]{1,0:T(8,128)S(1)}, f32[128,2048]{1,0:T(8,128)}, u32[]{:S(2)}) copy-start(f32[128,2048]{1,0:T(8,128)} %get-tuple-element.34.rest_3_) | copy-start | bytes 3145732
  113.5 2.2 %collective-permute-start.13 = (bf16[256,1024]{1,0:T(8,128)(2,1)S(1)}, bf16[256,1024]{1,0:T(8,128)(2,1)S(1)}, u32[]{:S(2)}, u32[]{:S(2)}) collective-permute-start(bf16[256,1024]{1,0:T(8,128)(2,1)S(1)} %get-tuple-element.40), channel_id=1, source_target_pairs={{0,8},{8,0},{16,24},{24,16},{32,40},{40,32},{48,56},{56,48},{64,72... | collective-permute-start | bytes 1572872 | tf_op jit(solution)/shard_map/ppermute | solution.py:33
  121.1 3.6 %collective-permute-start.14 = (bf16[8,256,256]{2,1,0:T(8,128)(2,1)S(1)}, bf16[8,256,256]{2,1,0:T(8,128)(2,1)S(1)}, u32[]{:S(2)}, u32[]{:S(2)}) collective-permute-start(bf16[8,256,256]{2,1,0:T(8,128)(2,1)S(1)} %get-tuple-element.44), channel_id=1, source_target_pairs={{0,8},{8,0},{16,24},{24,16},{32,40},{40,32},{48,56},{56,48},{64,72... | collective-permute-start | bytes 3145736 | tf_op jit(solution)/shard_map/ppermute | solution.py:33

commit v21 on v20

--- a/solution.py
+++ b/solution.py
@@ -272,29 +272,33 @@
 
 
 def project_kernel(slots, *rest):
-    *operands, own_ref, other_ref, grad, weight, total, sems = rest
-    chips = grad.shape[0]
-    grads, stacks = operands[: chips // 2], operands[chips // 2 :]
+    *operands, own_ref, other_ref, grad, weight, sems = rest
+    parts, features, width = weight.shape
+    count = sems.shape[0]
+    pairs = [ref for ref in operands if ref.shape[0] == 2]
+    stacks = [ref for ref in operands if ref.shape[0] > 2]
+    depth = pairs[0].shape[2]
+    chips = width // depth
     sources = [ref.at[j] for ref in stacks for j in range(ref.shape[0])]
-    copies = [
-        pltpu.make_async_copy(source, weight.at[k], sems.at[k]) for k, source in enumerate(sources)
-    ]
+    copies = []
+    for k in range(count):
+        place = pl.ds(pl.multiple_of(slots[k] * depth, depth), depth)
+        copies.append(
+            pltpu.make_async_copy(sources[k], weight.at[k // chips, :, place], sems.at[k])
+        )
     for copy in copies:
         copy.start()
-    for i, ref in enumerate(grads):
-        grad[2 * i : 2 * i + 2] = ref[...]
+    for i, ref in enumerate(pairs):
+        for j in range(2):
+            at = (2 * i + j) * depth
+            grad[:, at : at + depth] = ref[j]
     half = own_ref.shape[0]
-    features = weight.shape[1]
-    for k, copy in enumerate(copies):
-        copy.wait()
-        cols = slice(k // chips * features, (k // chips + 1) * features)
-        for out, row in ((own_ref, 0), (total, half)):
-            term = dot_t(grad[slots[k], row : row + half, :], weight[k])
-            if k % chips == 0:
-                out[:, cols] = term
-            else:
-                out[:, cols] += term
-    other_ref[...] = total[...].astype(BF16)
+    for part in range(parts):
+        for copy in copies[part * chips : (part + 1) * chips]:
+            copy.wait()
+        cols = slice(part * features, (part + 1) * features)
+        own_ref[:, cols] = dot_t(grad[:half, :], weight[part])
+        other_ref[:, cols] = dot_t(grad[half:, :], weight[part]).astype(BF16)
 
 
 def project(slots, grads, stacks):
@@ -316,9 +320,8 @@
         out_specs=[once(shape)] * 2,
         out_shape=[jax.ShapeDtypeStruct(shape, F32), jax.ShapeDtypeStruct(shape, BF16)],
         scratch_shapes=[
-            pltpu.VMEM((chips, tokens, depth), BF16),
-            pltpu.VMEM((blocks, features, depth), BF16),
-            pltpu.VMEM(shape, F32),
+            pltpu.VMEM((tokens, chips * depth), BF16),
+            pltpu.VMEM((blocks // chips, features, chips * depth), BF16),
             pltpu.SemaphoreType.DMA((blocks,)),
         ],
         compiler_params=pltpu.CompilerParams(vmem_limit_bytes=VMEM_LIMIT),

time: 159 us -> 159 us (level)
  no operation moved by 1% of the time
where the time goes in v21:
time: 159 us; the launch traced here: 158 us
  waiting for transfers between devices  51.8 us (33%)
  blocking collectives  31.9 us (20%)
  starting transfers between devices  31.7 us (20%)
  Pallas kernels  21.7 us (14%)
  local copies, waits for them, and re-layouts  7.76 us (5%)
  between operations  6.72 us (4%)
  other arithmetic  6.17 us (4%)
    ppermute x4, waiting for transfers between devices, tensor_move(): return lax.ppermute(value, 'tensor', pairs)  44.2 us
    all_to_all x1, blocking collectives, local(): lax.all_to_all(chip_sums, 'dp', 0, 0, axis_index_groups=groups, tiled=True)  31.9 us
    ppermute x11, starting transfers between devices, dp_move(): return lax.ppermute(value, 'dp', pairs)  16.4 us
    pallas_call x1, Pallas kernels, project(): pl.pallas_call(project_kernel, grid=(1,), in_specs=[pl.BlockSpec(memory_s...  8.99 us
    all_to_all x2, starting transfers between devices, exchange(): lax.all_to_all(copies, axis, 0, 0, axis_index_groups=groups, tiled=True)  8.38 us
    ppermute x11, waiting for transfers between devices, dp_move(): return lax.ppermute(value, 'dp', pairs)  7.54 us
    pallas_call x1, Pallas kernels, forward(): pl.pallas_call(forward_kernel, grid_spec=pltpu.PrefetchScalarGridSpec(num...  7.29 us
    ppermute x4, starting transfers between devices, tensor_move(): return lax.ppermute(value, 'tensor', pairs)  6.85 us
  transfers between devices with their start and end apart: 17, of which 8 were waited for; matrix products, arithmetic and copies ran while one was open for 5% of the time, Pallas kernels for 5%

profile of v21, /device:TPU:0, one launch (start us, length us, event | category | flops | bytes accessed | tf_op | source)
XLA Modules:
  0.0 157.7 jit_solution(2829021634150479075)
XLA Ops:
  0.7 2.2 %slice_bitcast_fusion.1 = (bf16[1,512,512]{2,1,0:T(8,128)(2,1)S(1)}, bf16[512,512]{1,0:T(8,128)(2,1)}, bf16[512,512]{1,0:T(8,128)(2,1)S(1)}) fusion(bf16[1024,512]{1,0:T(8,128)(2,1)} %param.10), kind=kLoop, calls=%fused_computation.34 | loop fusion | bytes 2621440 | tf_op jit(solution)/shard_map/stack | solution.py:390
  2.9 2.8 %collective-permute-start.6 = (bf16[512,512]{1,0:T(8,128)(2,1)}, bf16[512,512]{1,0:T(8,128)(2,1)}, u32[]{:S(2)}, u32[]{:S(2)}) collective-permute-start(bf16[512,512]{1,0:T(8,128)(2,1)} %get-tuple-element.46), channel_id=1, source_target_pairs={{0,96},{8,104},{16,112},{24,120},{32,0},{40,8},{48,16},{56,24},{64... | collective-permute-start | bytes 1572872 | tf_op jit(solution)/shard_map/ppermute | solution.py:33
  5.7 2.3 %collective-permute-start.7 = (bf16[512,512]{1,0:T(8,128)(2,1)}, bf16[512,512]{1,0:T(8,128)(2,1)}, u32[]{:S(2)}, u32[]{:S(2)}) collective-permute-start(bf16[512,512]{1,0:T(8,128)(2,1)} %get-tuple-element.46), channel_id=1, source_target_pairs={{0,64},{8,72},{16,80},{24,88},{32,96},{40,104},{48,112},{56,120},{... | collective-permute-start | bytes 1572872 | tf_op jit(solution)/shard_map/ppermute | solution.py:33
  9.4 4.0 %collective-permute-start.1 = (bf16[512,128]{1,0:T(8,128)(2,1)S(1)}, bf16[512,128]{1,0:T(8,128)(2,1)S(1)}, u32[]{:S(2)}, u32[]{:S(2)}) collective-permute-start(bf16[512,128]{1,0:T(8,128)(2,1)S(1)} %pad_maximum_fusion.5), channel_id=1, source_target_pairs={{0,16},{8,24},{16,0},{24,8},{32,48},{40,56},{48,32},{56,40},{64,80... | collective-permute-start | bytes 393224 | tf_op jit(solution)/shard_map/ppermute | solution.py:33
  17.2 3.3 %collective-permute-start.3 = (bf16[512,512]{1,0:T(8,128)(2,1)S(1)}, bf16[512,512]{1,0:T(8,128)(2,1)}, u32[]{:S(2)}, u32[]{:S(2)}) collective-permute-start(bf16[512,512]{1,0:T(8,128)(2,1)S(1)} %get-tuple-element.25), channel_id=1, source_target_pairs={{0,16},{8,24},{16,0},{24,8},{32,48},{40,56},{48,32},{56,40},{64,80... | collective-permute-start | bytes 1572872 | tf_op jit(solution)/shard_map/ppermute | solution.py:33
  21.7 3.5 %all-to-all-start = ((bf16[4,1024,128]{2,1,0:T(8,128)(2,1)}), bf16[4,1024,128]{2,1,0:T(8,128)(2,1)S(1)}, u32[]{:S(2)}, u32[]{:S(2)}) async-start(bf16[4,1024,128]{2,1,0:T(8,128)(2,1)} %broadcast_in_dim.31), calls=%async_computation | async-start | bytes 2097152 | tf_op jit(solution)/shard_map/all_to_all | solution.py:347
  30.5 2.1 %collective-permute-done.5 = bf16[512,512]{1,0:T(8,128)(2,1)} collective-permute-done((bf16[512,512]{1,0:T(8,128)(2,1)}, bf16[512,512]{1,0:T(8,128)(2,1)}, u32[]{:S(2)}, u32[]{:S(2)}) %collective-permute-start.5) | collective-permute-done | bytes 524320 | tf_op jit(solution)/shard_map/ppermute | solution.py:33
  32.6 3.0 %pad_maximum_fusion.rest_5_ = bf16[4,512,512]{2,1,0:T(8,128)(2,1)} fusion(bf16[1,512,512]{2,1,0:T(8,128)(2,1)} %bitcast.8, bf16[1,512,512]{2,1,0:T(8,128)(2,1)} %bitcast.7, bf16[1,512,512]{2,1,0:T(8,128)(2,1)} %bitcast.6, bf16[1,512,512]{2,1,0:T(8,128)(2,1)S(1)} %get-tuple-element.45), kind=kLoop, calls=%fused_computation | loop fusion | flops 3145728 | bytes 4194304 | tf_op jit(solution)/shard_map/stack | solution.py:390
  36.8 7.1 %collective-permute-done.4 = bf16[512,512]{1,0:T(8,128)(2,1)} collective-permute-done((bf16[512,512]{1,0:T(8,128)(2,1)S(1)}, bf16[512,512]{1,0:T(8,128)(2,1)}, u32[]{:S(2)}, u32[]{:S(2)}) %collective-permute-start.4) | collective-permute-done | bytes 524320 | tf_op jit(solution)/shard_map/ppermute | solution.py:41
  45.1 2.3 %broadcast_in_dim.32 = bf16[4,2,512,512]{3,2,1,0:T(8,128)(2,1)} broadcast(bf16[2,512,512]{2,1,0:T(8,128)(2,1)S(1)} %pad_maximum_fusion.1), dimensions={1,2,3} | broadcast | bytes 5242880 | tf_op jit(solution)/shard_map/broadcast_in_dim | solution.py:344
  47.4 4.9 %all-to-all-start.1 = ((bf16[4,2,512,512]{3,2,1,0:T(8,128)(2,1)}), bf16[4,2,512,512]{3,2,1,0:T(8,128)(2,1)}, u32[]{:S(2)}, u32[]{:S(2)}) async-start(bf16[4,2,512,512]{3,2,1,0:T(8,128)(2,1)} %broadcast_in_dim.32), calls=%async_computation.1 | async-start | bytes 8388608 | tf_op jit(solution)/shard_map/all_to_all | solution.py:347
  52.3 1.8 %collective-permute-start.12 = (bf16[4,512,512]{2,1,0:T(8,128)(2,1)}, bf16[4,512,512]{2,1,0:T(8,128)(2,1)}, u32[]{:S(2)}, u32[]{:S(2)}) collective-permute-start(bf16[4,512,512]{2,1,0:T(8,128)(2,1)} %pad_maximum_fusion.rest_5_), channel_id=1, source_target_pairs={{0,16},{8,24},{16,0},{24,8},{32,48},{40,56},{48,32},{56,40},{64,80... | collective-permute-start | bytes 6291464 | tf_op jit(solution)/shard_map/ppermute | solution.py:33
  54.1 1.6 collective-permute-start.11
  55.7 2.9 %collective-permute-start.10 = (bf16[2,512,512]{2,1,0:T(8,128)(2,1)S(1)}, bf16[2,512,512]{2,1,0:T(8,128)(2,1)}, u32[]{:S(2)}, u32[]{:S(2)}) collective-permute-start(bf16[2,512,512]{2,1,0:T(8,128)(2,1)S(1)} %pad_maximum_fusion.2.rest_0_), channel_id=1, source_target_pairs={{0,2},{1,3},{2,0},{3,1},{4,6},{5,7},{6,4},{7,5},{8,10},{9,11},{10,... | collective-permute-start | bytes 3145736 | tf_op jit(solution)/shard_map/ppermute | solution.py:41
  58.6 1.3 collective-permute-start.9
  60.0 7.3 %forward.1 = (bf16[2816,2048]{1,0:T(8,128)(2,1)}, f32[128,2048]{1,0:T(8,128)}) custom-call(s32[36]{0:T(128)S(1)} %concatenate.16.info, s32[1,256]{1,0:T(1,128)S(1)} %iota_add_fusion.pos_ref, s32[1,256]{1,0:T(1,128)S(1)} %bitcast.41, bf16[256,1024]{1,0:T(8,128)(2,1)} %rest_4_.1, bf16[4096,128]{1,0:T(8,128)(2,1)S(1)} %bitcast.39, ...), custom_call_target="tpu_custom_call" | custom-call | flops 100000000 | bytes 1048576 | tf_op jit(solution)/shard_map/forward/pallas_call | solution.py:140
  67.3 13.5 %collective-permute-done.11.rest_3_ = bf16[2,512,512]{2,1,0:T(8,128)(2,1)} collective-permute-done((bf16[2,512,512]{2,1,0:T(8,128)(2,1)S(1)}, bf16[2,512,512]{2,1,0:T(8,128)(2,1)}, u32[]{:S(2)}, u32[]{:S(2)}) %collective-permute-start.11) | collective-permute-done | bytes 1048608 | tf_op jit(solution)/shard_map/ppermute | solution.py:41
  80.8 23.6 %collective-permute-done.10.rest_2_ = bf16[2,512,512]{2,1,0:T(8,128)(2,1)} collective-permute-done((bf16[2,512,512]{2,1,0:T(8,128)(2,1)S(1)}, bf16[2,512,512]{2,1,0:T(8,128)(2,1)}, u32[]{:S(2)}, u32[]{:S(2)}) %collective-permute-start.10) | collective-permute-done | bytes 1048608 | tf_op jit(solution)/shard_map/ppermute | solution.py:41
  104.5 9.0 %project.1 = (f32[256,1024]{1,0:T(8,128)S(1)}, bf16[256,1024]{1,0:T(8,128)(2,1)S(1)}) custom-call(s32[16]{0:T(128)S(1)} %stack.127.slots, bf16[2,512,512]{2,1,0:T(8,128)(2,1)S(1)} %pad_maximum_fusion.2.rest_0_, bf16[2,512,512]{2,1,0:T(8,128)(2,1)} %collective-permute-done.9.rest_1_, bf16[2,512,512]{2,1,0:T(8,128)(2,1)} %collective-permute-done.10.rest_2_, ...), custom_call_target="tpu_custom_call" | custom-call | flops 4294967296 | bytes 12582912 | tf_op jit(solution)/shard_map/project/pallas_call | solution.py:314
  113.7 1.9 %collective-permute-done.13.rest_1_ = bf16[256,1024]{1,0:T(8,128)(2,1)S(1)} collective-permute-done((bf16[256,1024]{1,0:T(8,128)(2,1)S(1)}, bf16[256,1024]{1,0:T(8,128)(2,1)S(1)}, u32[]{:S(2)}, u32[]{:S(2)}) %collective-permute-start.13) | collective-permute-done | bytes 524320 | tf_op jit(solution)/shard_map/ppermute | solution.py:33
  115.6 5.4 %backward.1 = (bf16[256,1024]{1,0:T(8,128)(2,1)}, f32[8,256,256]{2,1,0:T(8,128)S(1)}, bf16[8,256,256]{2,1,0:T(8,128)(2,1)S(1)}) custom-call(s32[36]{0:T(128)S(1)} %concatenate.16.info, f32[256,1024]{1,0:T(8,128)S(1)} %get-tuple-element.39.rest_0_, bf16[256,1024]{1,0:T(8,128)(2,1)S(1)} %collective-permute-done.13.rest_1_, ...), custom_call_target="tpu_custom_call" | custom-call | flops 8000000000 | bytes 10485760 | tf_op jit(solution)/shard_map/backward/pallas_call | solution.py:234
  121.1 1.3 collective-permute-start.14
  122.4 2.3 %collective-permute-done.14 = bf16[8,256,256]{2,1,0:T(8,128)(2,1)S(1)} collective-permute-done((bf16[8,256,256]{2,1,0:T(8,128)(2,1)S(1)}, bf16[8,256,256]{2,1,0:T(8,128)(2,1)S(1)}, u32[]{:S(2)}, u32[]{:S(2)}) %collective-permute-start.14) | collective-permute-done | bytes 1048608 | tf_op jit(solution)/shard_map/ppermute | solution.py:33
  125.0 31.9 %all_to_all.15 = bf16[8,256,256]{2,1,0:T(8,128)(2,1)S(1)} all-to-all(bf16[8,256,256]{2,1,0:T(8,128)(2,1)S(1)} %add_convert_fusion), channel_id=1, replica_groups={{0,16,32,48,64,80,96,112},{8,24,40,56,72,88,104,120},{1,17,33,49,65,81,..., dimensions={0} | all-to-all | bytes 2097152 | tf_op jit(solution)/shard_map/all_to_all | solution.py:417
  (52 shorter events, 9.6 us)
Async XLA Ops:
  0.6 7.4 %copy-start.5 = (bf16[256,128]{1,0:T(8,128)(2,1)S(1)}, bf16[256,128]{1,0:T(8,128)(2,1)}, u32[]{:S(2)}) copy-start(bf16[256,128]{1,0:T(8,128)(2,1)} %param.8) | copy-start | bytes 196612
  0.6 7.4 %copy-start.4 = (bf16[256,128]{1,0:T(8,128)(2,1)S(1)}, bf16[256,128]{1,0:T(8,128)(2,1)}, u32[]{:S(2)}) copy-start(bf16[256,128]{1,0:T(8,128)(2,1)} %param.7) | copy-start | bytes 196612
  0.7 7.5 %copy-start.3 = (bf16[256,1024]{1,0:T(8,128)(2,1)S(1)}, bf16[256,1024]{1,0:T(8,128)(2,1)}, u32[]{:S(2)}) copy-start(bf16[256,1024]{1,0:T(8,128)(2,1)} %param.9) | copy-start | bytes 1572868
  2.9 27.6 %collective-permute-start.6 = (bf16[512,512]{1,0:T(8,128)(2,1)}, bf16[512,512]{1,0:T(8,128)(2,1)}, u32[]{:S(2)}, u32[]{:S(2)}) collective-permute-start(bf16[512,512]{1,0:T(8,128)(2,1)} %get-tuple-element.46), channel_id=1, source_target_pairs={{0,96},{8,104},{16,112},{24,120},{32,0},{40,8},{48,16},{56,24},{64... | collective-permute-start | bytes 1572872 | tf_op jit(solution)/shard_map/ppermute | solution.py:33
  5.7 26.9 %collective-permute-start.5 = (bf16[512,512]{1,0:T(8,128)(2,1)}, bf16[512,512]{1,0:T(8,128)(2,1)}, u32[]{:S(2)}, u32[]{:S(2)}) collective-permute-start(bf16[512,512]{1,0:T(8,128)(2,1)} %get-tuple-element.46), channel_id=1, source_target_pairs={{0,32},{8,40},{16,48},{24,56},{32,64},{40,72},{48,80},{56,88},{64,... | collective-permute-start | bytes 1572872 | tf_op jit(solution)/shard_map/ppermute | solution.py:33
  5.7 26.9 %collective-permute-start.7 = (bf16[512,512]{1,0:T(8,128)(2,1)}, bf16[512,512]{1,0:T(8,128)(2,1)}, u32[]{:S(2)}, u32[]{:S(2)}) collective-permute-start(bf16[512,512]{1,0:T(8,128)(2,1)} %get-tuple-element.46), channel_id=1, source_target_pairs={{0,64},{8,72},{16,80},{24,88},{32,96},{40,104},{48,112},{56,120},{... | collective-permute-start | bytes 1572872 | tf_op jit(solution)/shard_map/ppermute | solution.py:33
  8.0 1.3 collective-permute-start
  8.2 12.3 %collective-permute-start.2 = (bf16[256,512]{1,0:T(8,128)(2,1)S(1)}, bf16[256,512]{1,0:T(8,128)(2,1)S(1)}, u32[]{:S(2)}, u32[]{:S(2)}) collective-permute-start(bf16[256,512]{1,0:T(8,128)(2,1)S(1)} %get-tuple-element.49), channel_id=1, source_target_pairs={{0,8},{8,0},{16,24},{24,16},{32,40},{40,32},{48,56},{56,48},{64,72... | collective-permute-start | bytes 786440 | tf_op jit(solution)/shard_map/ppermute | solution.py:33
  9.4 7.8 %collective-permute-start.1 = (bf16[512,128]{1,0:T(8,128)(2,1)S(1)}, bf16[512,128]{1,0:T(8,128)(2,1)S(1)}, u32[]{:S(2)}, u32[]{:S(2)}) collective-permute-start(bf16[512,128]{1,0:T(8,128)(2,1)S(1)} %pad_maximum_fusion.5), channel_id=1, source_target_pairs={{0,16},{8,24},{16,0},{24,8},{32,48},{40,56},{48,32},{56,40},{64,80... | collective-permute-start | bytes 393224 | tf_op jit(solution)/shard_map/ppermute | solution.py:33
  17.2 18.5 %collective-permute-start.3 = (bf16[512,512]{1,0:T(8,128)(2,1)S(1)}, bf16[512,512]{1,0:T(8,128)(2,1)}, u32[]{:S(2)}, u32[]{:S(2)}) collective-permute-start(bf16[512,512]{1,0:T(8,128)(2,1)S(1)} %get-tuple-element.25), channel_id=1, source_target_pairs={{0,16},{8,24},{16,0},{24,8},{32,48},{40,56},{48,32},{56,40},{64,80... | collective-permute-start | bytes 1572872 | tf_op jit(solution)/shard_map/ppermute | solution.py:33
  20.5 4.8 %copy-start.6 = (s32[8]{0:T(128)S(1)}, s32[8]{0:T(128)}, u32[]{:S(2)}) copy-start(s32[8]{0:T(128)} %param.11) | copy-start | bytes 100
  20.5 15.1 %copy-start.1 = (bf16[512,512]{1,0:T(8,128)(2,1)}, bf16[512,512]{1,0:T(8,128)(2,1)S(1)}, u32[]{:S(2)}) copy-start(bf16[512,512]{1,0:T(8,128)(2,1)S(1)} %pad_maximum_fusion.3) | copy-start | bytes 1572868
  21.7 23.4 %all-to-all-start = ((bf16[4,1024,128]{2,1,0:T(8,128)(2,1)}), bf16[4,1024,128]{2,1,0:T(8,128)(2,1)S(1)}, u32[]{:S(2)}, u32[]{:S(2)}) async-start(bf16[4,1024,128]{2,1,0:T(8,128)(2,1)} %broadcast_in_dim.31), calls=%async_computation | async-start | bytes 2097152 | tf_op jit(solution)/shard_map/all_to_all | solution.py:347
  25.4 18.5 %collective-permute-start.4 = (bf16[512,512]{1,0:T(8,128)(2,1)S(1)}, bf16[512,512]{1,0:T(8,128)(2,1)}, u32[]{:S(2)}, u32[]{:S(2)}) collective-permute-start(bf16[512,512]{1,0:T(8,128)(2,1)S(1)} %pad_maximum_fusion.3), channel_id=1, source_target_pairs={{0,4},{1,5},{2,6},{3,7},{4,0},{5,1},{6,2},{7,3},{8,12},{9,13},{10,... | collective-permute-start | bytes 1572872 | tf_op jit(solution)/shard_map/ppermute | solution.py:41
  35.6 8.3 %copy-start.2 = (bf16[512,512]{1,0:T(8,128)(2,1)S(1)}, bf16[512,512]{1,0:T(8,128)(2,1)}, u32[]{:S(2)}) copy-start(bf16[512,512]{1,0:T(8,128)(2,1)} %copy-done.1) | copy-start | bytes 1572868
  47.4 4.9 %collective-permute-start.8 = (bf16[4096,128]{1,0:T(8,128)(2,1)S(1)}, bf16[4096,128]{1,0:T(8,128)(2,1)S(1)}, u32[]{:S(2)}, u32[]{:S(2)}) collective-permute-start(bf16[4096,128]{1,0:T(8,128)(2,1)S(1)} %bitcast.38), channel_id=1, source_target_pairs={{0,8},{8,0},{16,24},{24,16},{32,40},{40,32},{48,56},{56,48},{64,72... | collective-permute-start | bytes 3145736 | tf_op jit(solution)/shard_map/ppermute | solution.py:33
  47.4 57.0 %all-to-all-start.1 = ((bf16[4,2,512,512]{3,2,1,0:T(8,128)(2,1)}), bf16[4,2,512,512]{3,2,1,0:T(8,128)(2,1)}, u32[]{:S(2)}, u32[]{:S(2)}) async-start(bf16[4,2,512,512]{3,2,1,0:T(8,128)(2,1)} %broadcast_in_dim.32), calls=%async_computation.1 | async-start | bytes 8388608 | tf_op jit(solution)/shard_map/all_to_all | solution.py:347
  52.3 52.1 %collective-permute-start.12 = (bf16[4,512,512]{2,1,0:T(8,128)(2,1)}, bf16[4,512,512]{2,1,0:T(8,128)(2,1)}, u32[]{:S(2)}, u32[]{:S(2)}) collective-permute-start(bf16[4,512,512]{2,1,0:T(8,128)(2,1)} %pad_maximum_fusion.rest_5_), channel_id=1, source_target_pairs={{0,16},{8,24},{16,0},{24,8},{32,48},{40,56},{48,32},{56,40},{64,80... | collective-permute-start | bytes 6291464 | tf_op jit(solution)/shard_map/ppermute | solution.py:33
  54.1 26.7 %collective-permute-start.11 = (bf16[2,512,512]{2,1,0:T(8,128)(2,1)S(1)}, bf16[2,512,512]{2,1,0:T(8,128)(2,1)}, u32[]{:S(2)}, u32[]{:S(2)}) collective-permute-start(bf16[2,512,512]{2,1,0:T(8,128)(2,1)S(1)} %pad_maximum_fusion.2.rest_0_), channel_id=1, source_target_pairs={{0,1},{1,2},{2,3},{3,0},{4,5},{5,6},{6,7},{7,4},{8,9},{9,10},{10,1... | collective-permute-start | bytes 3145736 | tf_op jit(solution)/shard_map/ppermute | solution.py:41
  55.7 48.7 %collective-permute-start.10 = (bf16[2,512,512]{2,1,0:T(8,128)(2,1)S(1)}, bf16[2,512,512]{2,1,0:T(8,128)(2,1)}, u32[]{:S(2)}, u32[]{:S(2)}) collective-permute-start(bf16[2,512,512]{2,1,0:T(8,128)(2,1)S(1)} %pad_maximum_fusion.2.rest_0_), channel_id=1, source_target_pairs={{0,2},{1,3},{2,0},{3,1},{4,6},{5,7},{6,4},{7,5},{8,10},{9,11},{10,... | collective-permute-start | bytes 3145736 | tf_op jit(solution)/shard_map/ppermute | solution.py:41
  58.6 45.8 %collective-permute-start.9 = (bf16[2,512,512]{2,1,0:T(8,128)(2,1)S(1)}, bf16[2,512,512]{2,1,0:T(8,128)(2,1)}, u32[]{:S(2)}, u32[]{:S(2)}) collective-permute-start(bf16[2,512,512]{2,1,0:T(8,128)(2,1)S(1)} %pad_maximum_fusion.2.rest_0_), channel_id=1, source_target_pairs={{0,3},{1,0},{2,1},{3,2},{4,7},{5,4},{6,5},{7,6},{8,11},{9,8},{10,9... | collective-permute-start | bytes 3145736 | tf_op jit(solution)/shard_map/ppermute | solution.py:41
  104.5 11.2 %copy-start = (f32[128,2048]{1,0:T(8,128)S(1)}, f32[128,2048]{1,0:T(8,128)}, u32[]{:S(2)}) copy-start(f32[128,2048]{1,0:T(8,128)} %get-tuple-element.34.rest_3_) | copy-start | bytes 3145732
  113.5 2.2 %collective-permute-start.13 = (bf16[256,1024]{1,0:T(8,128)(2,1)S(1)}, bf16[256,1024]{1,0:T(8,128)(2,1)S(1)}, u32[]{:S(2)}, u32[]{:S(2)}) collective-permute-start(bf16[256,1024]{1,0:T(8,128)(2,1)S(1)} %get-tuple-element.40), channel_id=1, source_target_pairs={{0,8},{8,0},{16,24},{24,16},{32,40},{40,32},{48,56},{56,48},{64,72... | collective-permute-start | bytes 1572872 | tf_op jit(solution)/shard_map/ppermute | solution.py:33
  121.1 3.6 %collective-permute-start.14 = (bf16[8,256,256]{2,1,0:T(8,128)(2,1)S(1)}, bf16[8,256,256]{2,1,0:T(8,128)(2,1)S(1)}, u32[]{:S(2)}, u32[]{:S(2)}) collective-permute-start(bf16[8,256,256]{2,1,0:T(8,128)(2,1)S(1)} %get-tuple-element.44), channel_id=1, source_target_pairs={{0,8},{8,0},{16,24},{24,16},{32,40},{40,32},{48,56},{56,48},{64,72... | collective-permute-start | bytes 3145736 | tf_op jit(solution)/shard_map/ppermute | solution.py:33

commit v22 on v21

--- a/solution.py
+++ b/solution.py
@@ -272,7 +272,7 @@
 
 
 def project_kernel(slots, *rest):
-    *operands, own_ref, other_ref, grad, weight, sems = rest
+    *operands, own_ref, other_ref, grad, weight, row_sems, sems = rest
     parts, features, width = weight.shape
     count = sems.shape[0]
     pairs = [ref for ref in operands if ref.shape[0] == 2]
@@ -280,18 +280,22 @@
     depth = pairs[0].shape[2]
     chips = width // depth
     sources = [ref.at[j] for ref in stacks for j in range(ref.shape[0])]
+    rows = []
+    for i in range(chips):
+        place = pl.ds(i * depth, depth)
+        rows.append(
+            pltpu.make_async_copy(pairs[i // 2].at[i % 2], grad.at[:, place], row_sems.at[i])
+        )
     copies = []
     for k in range(count):
         place = pl.ds(pl.multiple_of(slots[k] * depth, depth), depth)
         copies.append(
             pltpu.make_async_copy(sources[k], weight.at[k // chips, :, place], sems.at[k])
         )
-    for copy in copies:
+    for copy in rows + copies:
         copy.start()
-    for i, ref in enumerate(pairs):
-        for j in range(2):
-            at = (2 * i + j) * depth
-            grad[:, at : at + depth] = ref[j]
+    for copy in rows:
+        copy.wait()
     half = own_ref.shape[0]
     for part in range(parts):
         for copy in copies[part * chips : (part + 1) * chips]:
@@ -315,13 +319,13 @@
         project_kernel,
         grid=(1,),
         in_specs=[pl.BlockSpec(memory_space=pltpu.SMEM)]
-        + [once(ref.shape) for ref in grads]
-        + [pl.BlockSpec(memory_space=pl.ANY)] * len(stacks),
+        + [pl.BlockSpec(memory_space=pl.ANY)] * (len(grads) + len(stacks)),
         out_specs=[once(shape)] * 2,
         out_shape=[jax.ShapeDtypeStruct(shape, F32), jax.ShapeDtypeStruct(shape, BF16)],
         scratch_shapes=[
             pltpu.VMEM((tokens, chips * depth), BF16),
             pltpu.VMEM((blocks // chips, features, chips * depth), BF16),
+            pltpu.SemaphoreType.DMA((chips,)),
             pltpu.SemaphoreType.DMA((blocks,)),
         ],
         compiler_params=pltpu.CompilerParams(vmem_limit_bytes=VMEM_LIMIT),
@@ -331,7 +335,7 @@
             transcendentals=0,
         ),
         name="project",
-    )(slots, *grads, *[in_hbm(stack) for stack in stacks])
+    )(slots, *[in_hbm(array) for array in (*grads, *stacks)])
 
 
 def local(queries, keys, values, grad_out, out_weight, lengths):

time: 159 us -> 161 us (1.013)
  transfers between devices with their start and end apart: 17 -> 17, of which waited for: 8 -> 8; matrix products, arithmetic and copies ran while one was open for 5% -> 6% of each run, Pallas kernels for 5% -> 5%
where the time goes in v22:
time: 161 us; the launch traced here: 160 us
  waiting for transfers between devices  51.8 us (32%)
  blocking collectives  32.5 us (20%)
  starting transfers between devices  31.3 us (19%)
  Pallas kernels  22.7 us (14%)
  local copies, waits for them, and re-layouts  7.69 us (5%)
  other arithmetic  7.18 us (4%)
  between operations  6.7 us (4%)
    ppermute x4, waiting for transfers between devices, tensor_move(): return lax.ppermute(value, 'tensor', pairs)  44.1 us
    all_to_all x1, blocking collectives, local(): lax.all_to_all(chip_sums, 'dp', 0, 0, axis_index_groups=groups, tiled=True)  32.5 us
    ppermute x11, starting transfers between devices, dp_move(): return lax.ppermute(value, 'dp', pairs)  16 us
    pallas_call x1, Pallas kernels, project(): pl.pallas_call(project_kernel, grid=(1,), in_specs=[pl.BlockSpec(memory_s...  9.93 us
    all_to_all x2, starting transfers between devices, exchange(): lax.all_to_all(copies, axis, 0, 0, axis_index_groups=groups, tiled=True)  8.51 us
    ppermute x11, waiting for transfers between devices, dp_move(): return lax.ppermute(value, 'dp', pairs)  7.62 us
    pallas_call x1, Pallas kernels, forward(): pl.pallas_call(forward_kernel, grid_spec=pltpu.PrefetchScalarGridSpec(num...  7.3 us
    ppermute x4, starting transfers between devices, tensor_move(): return lax.ppermute(value, 'tensor', pairs)  6.85 us
  transfers between devices with their start and end apart: 17, of which 8 were waited for; matrix products, arithmetic and copies ran while one was open for 6% of the time, Pallas kernels for 5%

profile of v22, /device:TPU:0, one launch (start us, length us, event | category | flops | bytes accessed | tf_op | source)
XLA Modules:
  0.0 159.8 jit_solution(1251206226263280116)
XLA Ops:
  0.7 2.2 %slice_bitcast_fusion.1 = (bf16[1,512,512]{2,1,0:T(8,128)(2,1)S(1)}, bf16[512,512]{1,0:T(8,128)(2,1)}, bf16[512,512]{1,0:T(8,128)(2,1)S(1)}) fusion(bf16[1024,512]{1,0:T(8,128)(2,1)} %param.10), kind=kLoop, calls=%fused_computation.34 | loop fusion | bytes 2621440 | tf_op jit(solution)/shard_map/stack | solution.py:394
  2.9 2.8 %collective-permute-start.6 = (bf16[512,512]{1,0:T(8,128)(2,1)}, bf16[512,512]{1,0:T(8,128)(2,1)}, u32[]{:S(2)}, u32[]{:S(2)}) collective-permute-start(bf16[512,512]{1,0:T(8,128)(2,1)} %get-tuple-element.46), channel_id=1, source_target_pairs={{0,96},{8,104},{16,112},{24,120},{32,0},{40,8},{48,16},{56,24},{64... | collective-permute-start | bytes 1572872 | tf_op jit(solution)/shard_map/ppermute | solution.py:33
  5.7 2.3 %collective-permute-start.7 = (bf16[512,512]{1,0:T(8,128)(2,1)}, bf16[512,512]{1,0:T(8,128)(2,1)}, u32[]{:S(2)}, u32[]{:S(2)}) collective-permute-start(bf16[512,512]{1,0:T(8,128)(2,1)} %get-tuple-element.46), channel_id=1, source_target_pairs={{0,64},{8,72},{16,80},{24,88},{32,96},{40,104},{48,112},{56,120},{... | collective-permute-start | bytes 1572872 | tf_op jit(solution)/shard_map/ppermute | solution.py:33
  9.4 4.0 %collective-permute-start.1 = (bf16[512,128]{1,0:T(8,128)(2,1)S(1)}, bf16[512,128]{1,0:T(8,128)(2,1)S(1)}, u32[]{:S(2)}, u32[]{:S(2)}) collective-permute-start(bf16[512,128]{1,0:T(8,128)(2,1)S(1)} %pad_maximum_fusion.5), channel_id=1, source_target_pairs={{0,16},{8,24},{16,0},{24,8},{32,48},{40,56},{48,32},{56,40},{64,80... | collective-permute-start | bytes 393224 | tf_op jit(solution)/shard_map/ppermute | solution.py:33
  17.2 3.3 %collective-permute-start.3 = (bf16[512,512]{1,0:T(8,128)(2,1)S(1)}, bf16[512,512]{1,0:T(8,128)(2,1)}, u32[]{:S(2)}, u32[]{:S(2)}) collective-permute-start(bf16[512,512]{1,0:T(8,128)(2,1)S(1)} %get-tuple-element.25), channel_id=1, source_target_pairs={{0,16},{8,24},{16,0},{24,8},{32,48},{40,56},{48,32},{56,40},{64,80... | collective-permute-start | bytes 1572872 | tf_op jit(solution)/shard_map/ppermute | solution.py:33
  21.6 3.5 %all-to-all-start = ((bf16[4,1024,128]{2,1,0:T(8,128)(2,1)}), bf16[4,1024,128]{2,1,0:T(8,128)(2,1)S(1)}, u32[]{:S(2)}, u32[]{:S(2)}) async-start(bf16[4,1024,128]{2,1,0:T(8,128)(2,1)} %broadcast_in_dim.31), calls=%async_computation | async-start | bytes 2097152 | tf_op jit(solution)/shard_map/all_to_all | solution.py:351
  30.4 2.2 %collective-permute-done.5 = bf16[512,512]{1,0:T(8,128)(2,1)} collective-permute-done((bf16[512,512]{1,0:T(8,128)(2,1)}, bf16[512,512]{1,0:T(8,128)(2,1)}, u32[]{:S(2)}, u32[]{:S(2)}) %collective-permute-start.5) | collective-permute-done | bytes 524320 | tf_op jit(solution)/shard_map/ppermute | solution.py:33
  32.6 3.0 %pad_maximum_fusion.rest_5_ = bf16[4,512,512]{2,1,0:T(8,128)(2,1)} fusion(bf16[1,512,512]{2,1,0:T(8,128)(2,1)} %bitcast.8, bf16[1,512,512]{2,1,0:T(8,128)(2,1)} %bitcast.7, bf16[1,512,512]{2,1,0:T(8,128)(2,1)} %bitcast.6, bf16[1,512,512]{2,1,0:T(8,128)(2,1)S(1)} %get-tuple-element.45), kind=kLoop, calls=%fused_computation | loop fusion | flops 3145728 | bytes 4194304 | tf_op jit(solution)/shard_map/stack | solution.py:394
  36.8 7.2 %collective-permute-done.4 = bf16[512,512]{1,0:T(8,128)(2,1)} collective-permute-done((bf16[512,512]{1,0:T(8,128)(2,1)S(1)}, bf16[512,512]{1,0:T(8,128)(2,1)}, u32[]{:S(2)}, u32[]{:S(2)}) %collective-permute-start.4) | collective-permute-done | bytes 524320 | tf_op jit(solution)/shard_map/ppermute | solution.py:41
  44.0 2.2 %pad_maximum_fusion.2.rest_0_ = bf16[2,512,512]{2,1,0:T(8,128)(2,1)} fusion(bf16[1,512,512]{2,1,0:T(8,128)(2,1)} %bitcast.4, bf16[1,512,512]{2,1,0:T(8,128)(2,1)S(1)} %bitcast.43), kind=kLoop, calls=%fused_computation.3 | loop fusion | flops 524288 | bytes 2097152 | tf_op jit(solution)/shard_map/stack | solution.py:393
  46.2 2.3 %broadcast_in_dim.32 = bf16[4,2,512,512]{3,2,1,0:T(8,128)(2,1)} broadcast(bf16[2,512,512]{2,1,0:T(8,128)(2,1)S(1)} %pad_maximum_fusion.1), dimensions={1,2,3} | broadcast | bytes 5242880 | tf_op jit(solution)/shard_map/broadcast_in_dim | solution.py:348
  48.5 5.0 %all-to-all-start.1 = ((bf16[4,2,512,512]{3,2,1,0:T(8,128)(2,1)}), bf16[4,2,512,512]{3,2,1,0:T(8,128)(2,1)}, u32[]{:S(2)}, u32[]{:S(2)}) async-start(bf16[4,2,512,512]{3,2,1,0:T(8,128)(2,1)} %broadcast_in_dim.32), calls=%async_computation.1 | async-start | bytes 8388608 | tf_op jit(solution)/shard_map/all_to_all | solution.py:351
  53.5 1.4 collective-permute-start.12
  54.9 1.6 collective-permute-start.11
  56.4 2.9 %collective-permute-start.10 = (bf16[2,512,512]{2,1,0:T(8,128)(2,1)S(1)}, bf16[2,512,512]{2,1,0:T(8,128)(2,1)}, u32[]{:S(2)}, u32[]{:S(2)}) collective-permute-start(bf16[2,512,512]{2,1,0:T(8,128)(2,1)S(1)} %copy-done.1), channel_id=1, source_target_pairs={{0,2},{1,3},{2,0},{3,1},{4,6},{5,7},{6,4},{7,5},{8,10},{9,11},{10,... | collective-permute-start | bytes 3145736 | tf_op jit(solution)/shard_map/ppermute | solution.py:41
  59.3 1.3 collective-permute-start.9
  60.8 7.3 %forward.1 = (bf16[2816,2048]{1,0:T(8,128)(2,1)}, f32[128,2048]{1,0:T(8,128)}) custom-call(s32[36]{0:T(128)S(1)} %concatenate.16.info, s32[1,256]{1,0:T(1,128)S(1)} %iota_add_fusion.pos_ref, s32[1,256]{1,0:T(1,128)S(1)} %bitcast.41, bf16[256,1024]{1,0:T(8,128)(2,1)} %rest_4_.1, bf16[4096,128]{1,0:T(8,128)(2,1)S(1)} %bitcast.39, ...), custom_call_target="tpu_custom_call" | custom-call | flops 100000000 | bytes 1048576 | tf_op jit(solution)/shard_map/forward/pallas_call | solution.py:140
  68.1 13.3 %collective-permute-done.11.rest_3_ = bf16[2,512,512]{2,1,0:T(8,128)(2,1)} collective-permute-done((bf16[2,512,512]{2,1,0:T(8,128)(2,1)S(1)}, bf16[2,512,512]{2,1,0:T(8,128)(2,1)}, u32[]{:S(2)}, u32[]{:S(2)}) %collective-permute-start.11) | collective-permute-done | bytes 1048608 | tf_op jit(solution)/shard_map/ppermute | solution.py:41
  81.4 23.6 %collective-permute-done.10.rest_2_ = bf16[2,512,512]{2,1,0:T(8,128)(2,1)} collective-permute-done((bf16[2,512,512]{2,1,0:T(8,128)(2,1)S(1)}, bf16[2,512,512]{2,1,0:T(8,128)(2,1)}, u32[]{:S(2)}, u32[]{:S(2)}) %collective-permute-start.10) | collective-permute-done | bytes 1048608 | tf_op jit(solution)/shard_map/ppermute | solution.py:41
  105.1 9.9 %project.1 = (f32[256,1024]{1,0:T(8,128)S(1)}, bf16[256,1024]{1,0:T(8,128)(2,1)S(1)}) custom-call(s32[16]{0:T(128)S(1)} %stack.127.slots, bf16[2,512,512]{2,1,0:T(8,128)(2,1)} %pad_maximum_fusion.2.rest_0_, bf16[2,512,512]{2,1,0:T(8,128)(2,1)} %collective-permute-done.9.rest_1_, bf16[2,512,512]{2,1,0:T(8,128)(2,1)} %collective-permute-done.10.rest_2_, ...), custom_call_target="tpu_custom_call" | custom-call | flops 4294967296 | bytes 12582912 | tf_op jit(solution)/shard_map/project/pallas_call | solution.py:318
  115.3 1.9 %collective-permute-done.13.rest_1_ = bf16[256,1024]{1,0:T(8,128)(2,1)S(1)} collective-permute-done((bf16[256,1024]{1,0:T(8,128)(2,1)S(1)}, bf16[256,1024]{1,0:T(8,128)(2,1)S(1)}, u32[]{:S(2)}, u32[]{:S(2)}) %collective-permute-start.13) | collective-permute-done | bytes 524320 | tf_op jit(solution)/shard_map/ppermute | solution.py:33
  117.2 5.4 %backward.1 = (bf16[256,1024]{1,0:T(8,128)(2,1)}, f32[8,256,256]{2,1,0:T(8,128)S(1)}, bf16[8,256,256]{2,1,0:T(8,128)(2,1)S(1)}) custom-call(s32[36]{0:T(128)S(1)} %concatenate.16.info, f32[256,1024]{1,0:T(8,128)S(1)} %get-tuple-element.39.rest_0_, bf16[256,1024]{1,0:T(8,128)(2,1)S(1)} %collective-permute-done.13.rest_1_, ...), custom_call_target="tpu_custom_call" | custom-call | flops 8000000000 | bytes 10485760 | tf_op jit(solution)/shard_map/backward/pallas_call | solution.py:234
  123.9 2.3 %collective-permute-done.14 = bf16[8,256,256]{2,1,0:T(8,128)(2,1)S(1)} collective-permute-done((bf16[8,256,256]{2,1,0:T(8,128)(2,1)S(1)}, bf16[8,256,256]{2,1,0:T(8,128)(2,1)S(1)}, u32[]{:S(2)}, u32[]{:S(2)}) %collective-permute-start.14) | collective-permute-done | bytes 1048608 | tf_op jit(solution)/shard_map/ppermute | solution.py:33
  126.5 32.5 %all_to_all.15 = bf16[8,256,256]{2,1,0:T(8,128)(2,1)S(1)} all-to-all(bf16[8,256,256]{2,1,0:T(8,128)(2,1)S(1)} %add_convert_fusion), channel_id=1, replica_groups={{0,16,32,48,64,80,96,112},{8,24,40,56,72,88,104,120},{1,17,33,49,65,81,..., dimensions={0} | all-to-all | bytes 2097152 | tf_op jit(solution)/shard_map/all_to_all | solution.py:421
  (50 shorter events, 9.6 us)
Async XLA Ops:
  0.6 7.4 %copy-start.4 = (bf16[256,128]{1,0:T(8,128)(2,1)S(1)}, bf16[256,128]{1,0:T(8,128)(2,1)}, u32[]{:S(2)}) copy-start(bf16[256,128]{1,0:T(8,128)(2,1)} %param.8) | copy-start | bytes 196612
  0.6 7.4 %copy-start.3 = (bf16[256,128]{1,0:T(8,128)(2,1)S(1)}, bf16[256,128]{1,0:T(8,128)(2,1)}, u32[]{:S(2)}) copy-start(bf16[256,128]{1,0:T(8,128)(2,1)} %param.7) | copy-start | bytes 196612
  0.7 7.5 %copy-start.2 = (bf16[256,1024]{1,0:T(8,128)(2,1)S(1)}, bf16[256,1024]{1,0:T(8,128)(2,1)}, u32[]{:S(2)}) copy-start(bf16[256,1024]{1,0:T(8,128)(2,1)} %param.9) | copy-start | bytes 1572868
  2.9 27.6 %collective-permute-start.6 = (bf16[512,512]{1,0:T(8,128)(2,1)}, bf16[512,512]{1,0:T(8,128)(2,1)}, u32[]{:S(2)}, u32[]{:S(2)}) collective-permute-start(bf16[512,512]{1,0:T(8,128)(2,1)} %get-tuple-element.46), channel_id=1, source_target_pairs={{0,96},{8,104},{16,112},{24,120},{32,0},{40,8},{48,16},{56,24},{64... | collective-permute-start | bytes 1572872 | tf_op jit(solution)/shard_map/ppermute | solution.py:33
  5.7 26.9 %collective-permute-start.5 = (bf16[512,512]{1,0:T(8,128)(2,1)}, bf16[512,512]{1,0:T(8,128)(2,1)}, u32[]{:S(2)}, u32[]{:S(2)}) collective-permute-start(bf16[512,512]{1,0:T(8,128)(2,1)} %get-tuple-element.46), channel_id=1, source_target_pairs={{0,32},{8,40},{16,48},{24,56},{32,64},{40,72},{48,80},{56,88},{64,... | collective-permute-start | bytes 1572872 | tf_op jit(solution)/shard_map/ppermute | solution.py:33
  5.7 26.9 %collective-permute-start.7 = (bf16[512,512]{1,0:T(8,128)(2,1)}, bf16[512,512]{1,0:T(8,128)(2,1)}, u32[]{:S(2)}, u32[]{:S(2)}) collective-permute-start(bf16[512,512]{1,0:T(8,128)(2,1)} %get-tuple-element.46), channel_id=1, source_target_pairs={{0,64},{8,72},{16,80},{24,88},{32,96},{40,104},{48,112},{56,120},{... | collective-permute-start | bytes 1572872 | tf_op jit(solution)/shard_map/ppermute | solution.py:33
  8.0 1.3 collective-permute-start
  8.2 12.3 %collective-permute-start.2 = (bf16[256,512]{1,0:T(8,128)(2,1)S(1)}, bf16[256,512]{1,0:T(8,128)(2,1)S(1)}, u32[]{:S(2)}, u32[]{:S(2)}) collective-permute-start(bf16[256,512]{1,0:T(8,128)(2,1)S(1)} %get-tuple-element.49), channel_id=1, source_target_pairs={{0,8},{8,0},{16,24},{24,16},{32,40},{40,32},{48,56},{56,48},{64,72... | collective-permute-start | bytes 786440 | tf_op jit(solution)/shard_map/ppermute | solution.py:33
  9.4 7.8 %collective-permute-start.1 = (bf16[512,128]{1,0:T(8,128)(2,1)S(1)}, bf16[512,128]{1,0:T(8,128)(2,1)S(1)}, u32[]{:S(2)}, u32[]{:S(2)}) collective-permute-start(bf16[512,128]{1,0:T(8,128)(2,1)S(1)} %pad_maximum_fusion.5), channel_id=1, source_target_pairs={{0,16},{8,24},{16,0},{24,8},{32,48},{40,56},{48,32},{56,40},{64,80... | collective-permute-start | bytes 393224 | tf_op jit(solution)/shard_map/ppermute | solution.py:33
  17.2 18.5 %collective-permute-start.3 = (bf16[512,512]{1,0:T(8,128)(2,1)S(1)}, bf16[512,512]{1,0:T(8,128)(2,1)}, u32[]{:S(2)}, u32[]{:S(2)}) collective-permute-start(bf16[512,512]{1,0:T(8,128)(2,1)S(1)} %get-tuple-element.25), channel_id=1, source_target_pairs={{0,16},{8,24},{16,0},{24,8},{32,48},{40,56},{48,32},{56,40},{64,80... | collective-permute-start | bytes 1572872 | tf_op jit(solution)/shard_map/ppermute | solution.py:33
  20.5 4.7 %copy-start.5 = (s32[8]{0:T(128)S(1)}, s32[8]{0:T(128)}, u32[]{:S(2)}) copy-start(s32[8]{0:T(128)} %param.11) | copy-start | bytes 100
  21.6 24.5 %all-to-all-start = ((bf16[4,1024,128]{2,1,0:T(8,128)(2,1)}), bf16[4,1024,128]{2,1,0:T(8,128)(2,1)S(1)}, u32[]{:S(2)}, u32[]{:S(2)}) async-start(bf16[4,1024,128]{2,1,0:T(8,128)(2,1)} %broadcast_in_dim.31), calls=%async_computation | async-start | bytes 2097152 | tf_op jit(solution)/shard_map/all_to_all | solution.py:351
  25.4 18.6 %collective-permute-start.4 = (bf16[512,512]{1,0:T(8,128)(2,1)S(1)}, bf16[512,512]{1,0:T(8,128)(2,1)}, u32[]{:S(2)}, u32[]{:S(2)}) collective-permute-start(bf16[512,512]{1,0:T(8,128)(2,1)S(1)} %pad_maximum_fusion.3), channel_id=1, source_target_pairs={{0,4},{1,5},{2,6},{3,7},{4,0},{5,1},{6,2},{7,3},{8,12},{9,13},{10,... | collective-permute-start | bytes 1572872 | tf_op jit(solution)/shard_map/ppermute | solution.py:41
  48.5 6.4 %copy-start.1 = (bf16[2,512,512]{2,1,0:T(8,128)(2,1)S(1)}, bf16[2,512,512]{2,1,0:T(8,128)(2,1)}, u32[]{:S(2)}) copy-start(bf16[2,512,512]{2,1,0:T(8,128)(2,1)} %pad_maximum_fusion.2.rest_0_) | copy-start | bytes 3145732
  48.5 5.0 %collective-permute-start.8 = (bf16[4096,128]{1,0:T(8,128)(2,1)S(1)}, bf16[4096,128]{1,0:T(8,128)(2,1)S(1)}, u32[]{:S(2)}, u32[]{:S(2)}) collective-permute-start(bf16[4096,128]{1,0:T(8,128)(2,1)S(1)} %bitcast.38), channel_id=1, source_target_pairs={{0,8},{8,0},{16,24},{24,16},{32,40},{40,32},{48,56},{56,48},{64,72... | collective-permute-start | bytes 3145736 | tf_op jit(solution)/shard_map/ppermute | solution.py:33
  48.5 56.6 %all-to-all-start.1 = ((bf16[4,2,512,512]{3,2,1,0:T(8,128)(2,1)}), bf16[4,2,512,512]{3,2,1,0:T(8,128)(2,1)}, u32[]{:S(2)}, u32[]{:S(2)}) async-start(bf16[4,2,512,512]{3,2,1,0:T(8,128)(2,1)} %broadcast_in_dim.32), calls=%async_computation.1 | async-start | bytes 8388608 | tf_op jit(solution)/shard_map/all_to_all | solution.py:351
  53.5 51.5 %collective-permute-start.12 = (bf16[4,512,512]{2,1,0:T(8,128)(2,1)}, bf16[4,512,512]{2,1,0:T(8,128)(2,1)}, u32[]{:S(2)}, u32[]{:S(2)}) collective-permute-start(bf16[4,512,512]{2,1,0:T(8,128)(2,1)} %pad_maximum_fusion.rest_5_), channel_id=1, source_target_pairs={{0,16},{8,24},{16,0},{24,8},{32,48},{40,56},{48,32},{56,40},{64,80... | collective-permute-start | bytes 6291464 | tf_op jit(solution)/shard_map/ppermute | solution.py:33
  54.9 26.5 %collective-permute-start.11 = (bf16[2,512,512]{2,1,0:T(8,128)(2,1)S(1)}, bf16[2,512,512]{2,1,0:T(8,128)(2,1)}, u32[]{:S(2)}, u32[]{:S(2)}) collective-permute-start(bf16[2,512,512]{2,1,0:T(8,128)(2,1)S(1)} %copy-done.1), channel_id=1, source_target_pairs={{0,1},{1,2},{2,3},{3,0},{4,5},{5,6},{6,7},{7,4},{8,9},{9,10},{10,1... | collective-permute-start | bytes 3145736 | tf_op jit(solution)/shard_map/ppermute | solution.py:41
  56.4 48.6 %collective-permute-start.10 = (bf16[2,512,512]{2,1,0:T(8,128)(2,1)S(1)}, bf16[2,512,512]{2,1,0:T(8,128)(2,1)}, u32[]{:S(2)}, u32[]{:S(2)}) collective-permute-start(bf16[2,512,512]{2,1,0:T(8,128)(2,1)S(1)} %copy-done.1), channel_id=1, source_target_pairs={{0,2},{1,3},{2,0},{3,1},{4,6},{5,7},{6,4},{7,5},{8,10},{9,11},{10,... | collective-permute-start | bytes 3145736 | tf_op jit(solution)/shard_map/ppermute | solution.py:41
  59.3 45.7 %collective-permute-start.9 = (bf16[2,512,512]{2,1,0:T(8,128)(2,1)S(1)}, bf16[2,512,512]{2,1,0:T(8,128)(2,1)}, u32[]{:S(2)}, u32[]{:S(2)}) collective-permute-start(bf16[2,512,512]{2,1,0:T(8,128)(2,1)S(1)} %copy-done.1), channel_id=1, source_target_pairs={{0,3},{1,0},{2,1},{3,2},{4,7},{5,4},{6,5},{7,6},{8,11},{9,8},{10,9... | collective-permute-start | bytes 3145736 | tf_op jit(solution)/shard_map/ppermute | solution.py:41
  105.1 12.1 %copy-start = (f32[128,2048]{1,0:T(8,128)S(1)}, f32[128,2048]{1,0:T(8,128)}, u32[]{:S(2)}) copy-start(f32[128,2048]{1,0:T(8,128)} %get-tuple-element.34.rest_3_) | copy-start | bytes 3145732
  115.0 2.2 %collective-permute-start.13 = (bf16[256,1024]{1,0:T(8,128)(2,1)S(1)}, bf16[256,1024]{1,0:T(8,128)(2,1)S(1)}, u32[]{:S(2)}, u32[]{:S(2)}) collective-permute-start(bf16[256,1024]{1,0:T(8,128)(2,1)S(1)} %get-tuple-element.40), channel_id=1, source_target_pairs={{0,8},{8,0},{16,24},{24,16},{32,40},{40,32},{48,56},{56,48},{64,72... | collective-permute-start | bytes 1572872 | tf_op jit(solution)/shard_map/ppermute | solution.py:33
  122.6 3.6 %collective-permute-start.14 = (bf16[8,256,256]{2,1,0:T(8,128)(2,1)S(1)}, bf16[8,256,256]{2,1,0:T(8,128)(2,1)S(1)}, u32[]{:S(2)}, u32[]{:S(2)}) collective-permute-start(bf16[8,256,256]{2,1,0:T(8,128)(2,1)S(1)} %get-tuple-element.44), channel_id=1, source_target_pairs={{0,8},{8,0},{16,24},{24,16},{32,40},{40,32},{48,56},{56,48},{64,72... | collective-permute-start | bytes 3145736 | tf_op jit(solution)/shard_map/ppermute | solution.py:33

commit v23 on v21

--- a/solution.py
+++ b/solution.py
@@ -388,15 +388,16 @@
     copies = copy(jnp.stack([own0, pair0]), groups_x)
     both_grads = jnp.stack([chip_grad, grad_pair])
     sent = jnp.stack([own[1], *plane1])
-    ring, copies, both_grads, sent, info, query_pos, query_start = lax.optimization_barrier(
-        (ring, copies, both_grads, sent, info, query_pos, query_start)
+    ring, copies, sent, info, query_pos, query_start = lax.optimization_barrier(
+        (ring, copies, sent, info, query_pos, query_start)
     )
     plane0 = exchange(copies, "dp", groups_x).reshape(8, SPLIT, depth)
     swapped = dp_move(ring, 0, 0, 1)
     swapped, held = lax.optimization_barrier((swapped, sent))
     rest = dp_move(held, 0, 1, 0)
+    both_grads, later = lax.optimization_barrier((both_grads, queries))
     all_grad = [both_grads] + [tensor_move(both_grads, 0, step) for step in (-1, -2, 1)]
-    probs, outs = forward(info, query_pos, query_start, queries, ring, swapped)
+    probs, outs = forward(info, query_pos, query_start, later, ring, swapped)
 
     t = lax.axis_index("tensor")
 

time: 159 us -> 218 us (1.37)
  waiting for transfers between devices: 51.8 us -> 109 us
  starting transfers between devices: 31.7 us -> 33.9 us
    ppermute x4, waiting for transfers between devices: 44.2 us -> 94 us  [tensor_move(): return lax.ppermute(value, 'tensor', pairs)]
    ppermute x11, waiting for transfers between devices: 7.54 us -> 13.2 us  [dp_move(): return lax.ppermute(value, 'dp', pairs)]
  transfers between devices with their start and end apart: 17 -> 17, of which waited for: 8 -> 9; matrix products, arithmetic and copies ran while one was open for 5% -> 4% of each run, Pallas kernels for 5% -> 3%
where the time goes in v23:
time: 218 us; the launch traced here: 216 us
  waiting for transfers between devices  109 us (50%)
  starting transfers between devices  33.9 us (16%)
  blocking collectives  31 us (14%)
  Pallas kernels  21.7 us (10%)
  local copies, waits for them, and re-layouts  7.75 us (4%)
  between operations  6.72 us (3%)
  other arithmetic  6.12 us (3%)
    ppermute x4, waiting for transfers between devices, tensor_move(): return lax.ppermute(value, 'tensor', pairs)  94 us
    all_to_all x1, blocking collectives, local(): lax.all_to_all(chip_sums, 'dp', 0, 0, axis_index_groups=groups, tiled=True)  31 us
    ppermute x11, starting transfers between devices, dp_move(): return lax.ppermute(value, 'dp', pairs)  18.6 us
    ppermute x11, waiting for transfers between devices, dp_move(): return lax.ppermute(value, 'dp', pairs)  13.2 us
    pallas_call x1, Pallas kernels, project(): pl.pallas_call(project_kernel, grid=(1,), in_specs=[pl.BlockSpec(memory_s...  8.98 us
    all_to_all x2, starting transfers between devices, exchange(): lax.all_to_all(copies, axis, 0, 0, axis_index_groups=groups, tiled=True)  8.38 us
    pallas_call x1, Pallas kernels, forward(): pl.pallas_call(forward_kernel, grid_spec=pltpu.PrefetchScalarGridSpec(num...  7.33 us
    ppermute x4, starting transfers between devices, tensor_move(): return lax.ppermute(value, 'tensor', pairs)  6.91 us
  transfers between devices with their start and end apart: 17, of which 9 were waited for; matrix products, arithmetic and copies ran while one was open for 4% of the time, Pallas kernels for 3%

profile of v23, /device:TPU:0, one launch (start us, length us, event | category | flops | bytes accessed | tf_op | source)
XLA Modules:
  0.0 216.0 jit_solution(17114591853805009235)
XLA Ops:
  0.7 2.2 %slice_bitcast_fusion.1 = (bf16[1,512,512]{2,1,0:T(8,128)(2,1)S(1)}, bf16[512,512]{1,0:T(8,128)(2,1)}, bf16[512,512]{1,0:T(8,128)(2,1)S(1)}) fusion(bf16[1024,512]{1,0:T(8,128)(2,1)} %param.10), kind=kLoop, calls=%fused_computation.34 | loop fusion | bytes 2621440 | tf_op jit(solution)/shard_map/stack | solution.py:390
  2.9 2.8 %collective-permute-start.5 = (bf16[512,512]{1,0:T(8,128)(2,1)}, bf16[512,512]{1,0:T(8,128)(2,1)}, u32[]{:S(2)}, u32[]{:S(2)}) collective-permute-start(bf16[512,512]{1,0:T(8,128)(2,1)} %get-tuple-element.48), channel_id=1, source_target_pairs={{0,96},{8,104},{16,112},{24,120},{32,0},{40,8},{48,16},{56,24},{64... | collective-permute-start | bytes 1572872 | tf_op jit(solution)/shard_map/ppermute | solution.py:33
  5.7 2.3 %collective-permute-start.6 = (bf16[512,512]{1,0:T(8,128)(2,1)}, bf16[512,512]{1,0:T(8,128)(2,1)}, u32[]{:S(2)}, u32[]{:S(2)}) collective-permute-start(bf16[512,512]{1,0:T(8,128)(2,1)} %get-tuple-element.48), channel_id=1, source_target_pairs={{0,64},{8,72},{16,80},{24,88},{32,96},{40,104},{48,112},{56,120},{... | collective-permute-start | bytes 1572872 | tf_op jit(solution)/shard_map/ppermute | solution.py:33
  9.4 4.0 %collective-permute-start.1 = (bf16[512,128]{1,0:T(8,128)(2,1)S(1)}, bf16[512,128]{1,0:T(8,128)(2,1)S(1)}, u32[]{:S(2)}, u32[]{:S(2)}) collective-permute-start(bf16[512,128]{1,0:T(8,128)(2,1)S(1)} %pad_maximum_fusion.5), channel_id=1, source_target_pairs={{0,16},{8,24},{16,0},{24,8},{32,48},{40,56},{48,32},{56,40},{64,80... | collective-permute-start | bytes 393224 | tf_op jit(solution)/shard_map/ppermute | solution.py:33
  13.3 3.8 %collective-permute-done.1 = bf16[512,128]{1,0:T(8,128)(2,1)S(1)} collective-permute-done((bf16[512,128]{1,0:T(8,128)(2,1)S(1)}, bf16[512,128]{1,0:T(8,128)(2,1)S(1)}, u32[]{:S(2)}, u32[]{:S(2)}) %collective-permute-start.1) | collective-permute-done | bytes 131104 | tf_op jit(solution)/shard_map/ppermute | solution.py:33
  18.4 3.5 %all-to-all-start = ((bf16[4,1024,128]{2,1,0:T(8,128)(2,1)}), bf16[4,1024,128]{2,1,0:T(8,128)(2,1)S(1)}, u32[]{:S(2)}, u32[]{:S(2)}) async-start(bf16[4,1024,128]{2,1,0:T(8,128)(2,1)} %broadcast_in_dim.31), calls=%async_computation | async-start | bytes 2097152 | tf_op jit(solution)/shard_map/all_to_all | solution.py:347
  25.1 3.3 %collective-permute-start.3 = (bf16[512,512]{1,0:T(8,128)(2,1)S(1)}, bf16[512,512]{1,0:T(8,128)(2,1)}, u32[]{:S(2)}, u32[]{:S(2)}) collective-permute-start(bf16[512,512]{1,0:T(8,128)(2,1)S(1)} %get-tuple-element.26), channel_id=1, source_target_pairs={{0,16},{8,24},{16,0},{24,8},{32,48},{40,56},{48,32},{56,40},{64,80... | collective-permute-start | bytes 1572872 | tf_op jit(solution)/shard_map/ppermute | solution.py:33
  32.7 3.0 %pad_maximum_fusion.rest_5_ = bf16[4,512,512]{2,1,0:T(8,128)(2,1)} fusion(bf16[1,512,512]{2,1,0:T(8,128)(2,1)} %bitcast.6, bf16[1,512,512]{2,1,0:T(8,128)(2,1)} %bitcast.5, bf16[1,512,512]{2,1,0:T(8,128)(2,1)} %bitcast.4, bf16[1,512,512]{2,1,0:T(8,128)(2,1)S(1)} %get-tuple-element.47), kind=kLoop, calls=%fused_computation | loop fusion | flops 3145728 | bytes 4194304 | tf_op jit(solution)/shard_map/stack | solution.py:390
  35.7 4.6 %collective-permute-done.3 = bf16[512,512]{1,0:T(8,128)(2,1)} collective-permute-done((bf16[512,512]{1,0:T(8,128)(2,1)S(1)}, bf16[512,512]{1,0:T(8,128)(2,1)}, u32[]{:S(2)}, u32[]{:S(2)}) %collective-permute-start.3) | collective-permute-done | bytes 524320 | tf_op jit(solution)/shard_map/ppermute | solution.py:33
  41.4 1.5 all-to-all-done
  43.0 2.3 %broadcast_in_dim.32 = bf16[4,2,512,512]{3,2,1,0:T(8,128)(2,1)} broadcast(bf16[2,512,512]{2,1,0:T(8,128)(2,1)S(1)} %pad_maximum_fusion.1), dimensions={1,2,3} | broadcast | bytes 5242880 | tf_op jit(solution)/shard_map/broadcast_in_dim | solution.py:344
  45.3 4.9 %all-to-all-start.1 = ((bf16[4,2,512,512]{3,2,1,0:T(8,128)(2,1)}), bf16[4,2,512,512]{3,2,1,0:T(8,128)(2,1)}, u32[]{:S(2)}, u32[]{:S(2)}) async-start(bf16[4,2,512,512]{3,2,1,0:T(8,128)(2,1)} %broadcast_in_dim.32), calls=%async_computation.1 | async-start | bytes 8388608 | tf_op jit(solution)/shard_map/all_to_all | solution.py:347
  50.2 4.0 %collective-permute-start.12 = (bf16[4,512,512]{2,1,0:T(8,128)(2,1)}, bf16[4,512,512]{2,1,0:T(8,128)(2,1)}, u32[]{:S(2)}, u32[]{:S(2)}) collective-permute-start(bf16[4,512,512]{2,1,0:T(8,128)(2,1)} %pad_maximum_fusion.rest_5_), channel_id=1, source_target_pairs={{0,16},{8,24},{16,0},{24,8},{32,48},{40,56},{48,32},{56,40},{64,80... | collective-permute-start | bytes 6291464 | tf_op jit(solution)/shard_map/ppermute | solution.py:33
  55.1 57.5 %collective-permute-done.7 = bf16[512,512]{1,0:T(8,128)(2,1)S(1)} collective-permute-done((bf16[512,512]{1,0:T(8,128)(2,1)S(1)}, bf16[512,512]{1,0:T(8,128)(2,1)S(1)}, u32[]{:S(2)}, u32[]{:S(2)}) %collective-permute-start.7) | collective-permute-done | bytes 524320 | tf_op jit(solution)/shard_map/ppermute | solution.py:41
  113.7 1.6 collective-permute-start.11
  115.4 2.9 %collective-permute-start.10 = (bf16[2,512,512]{2,1,0:T(8,128)(2,1)S(1)}, bf16[2,512,512]{2,1,0:T(8,128)(2,1)}, u32[]{:S(2)}, u32[]{:S(2)}) collective-permute-start(bf16[2,512,512]{2,1,0:T(8,128)(2,1)S(1)} %pad_maximum_fusion.2.rest_0_), channel_id=1, source_target_pairs={{0,2},{1,3},{2,0},{3,1},{4,6},{5,7},{6,4},{7,5},{8,10},{9,11},{10,... | collective-permute-start | bytes 3145736 | tf_op jit(solution)/shard_map/ppermute | solution.py:41
  119.7 7.3 %forward.1 = (bf16[2816,2048]{1,0:T(8,128)(2,1)}, f32[128,2048]{1,0:T(8,128)}) custom-call(s32[36]{0:T(128)S(1)} %concatenate.16.info, s32[1,256]{1,0:T(1,128)S(1)} %iota_add_fusion.pos_ref, s32[1,256]{1,0:T(1,128)S(1)} %bitcast.41, bf16[256,1024]{1,0:T(8,128)(2,1)} %rest_4_.1, bf16[4096,128]{1,0:T(8,128)(2,1)S(1)} %bitcast.39, ...), custom_call_target="tpu_custom_call" | custom-call | flops 100000000 | bytes 1048576 | tf_op jit(solution)/shard_map/forward/pallas_call | solution.py:140
  127.1 13.0 %collective-permute-done.11.rest_3_ = bf16[2,512,512]{2,1,0:T(8,128)(2,1)} collective-permute-done((bf16[2,512,512]{2,1,0:T(8,128)(2,1)S(1)}, bf16[2,512,512]{2,1,0:T(8,128)(2,1)}, u32[]{:S(2)}, u32[]{:S(2)}) %collective-permute-start.11) | collective-permute-done | bytes 1048608 | tf_op jit(solution)/shard_map/ppermute | solution.py:41
  140.1 23.6 %collective-permute-done.10.rest_2_ = bf16[2,512,512]{2,1,0:T(8,128)(2,1)} collective-permute-done((bf16[2,512,512]{2,1,0:T(8,128)(2,1)S(1)}, bf16[2,512,512]{2,1,0:T(8,128)(2,1)}, u32[]{:S(2)}, u32[]{:S(2)}) %collective-permute-start.10) | collective-permute-done | bytes 1048608 | tf_op jit(solution)/shard_map/ppermute | solution.py:41
  163.7 9.0 %project.1 = (f32[256,1024]{1,0:T(8,128)S(1)}, bf16[256,1024]{1,0:T(8,128)(2,1)S(1)}) custom-call(s32[16]{0:T(128)S(1)} %stack.124.slots, bf16[2,512,512]{2,1,0:T(8,128)(2,1)S(1)} %pad_maximum_fusion.2.rest_0_, bf16[2,512,512]{2,1,0:T(8,128)(2,1)} %collective-permute-done.9.rest_1_, bf16[2,512,512]{2,1,0:T(8,128)(2,1)} %collective-permute-done.10.rest_2_, ...), custom_call_target="tpu_custom_call" | custom-call | flops 4294967296 | bytes 12582912 | tf_op jit(solution)/shard_map/project/pallas_call | solution.py:314
  172.9 1.9 collective-permute-done.13.rest_1_
  174.8 5.4 %backward.1 = (bf16[256,1024]{1,0:T(8,128)(2,1)}, f32[8,256,256]{2,1,0:T(8,128)S(1)}, bf16[8,256,256]{2,1,0:T(8,128)(2,1)S(1)}) custom-call(s32[36]{0:T(128)S(1)} %concatenate.16.info, f32[256,1024]{1,0:T(8,128)S(1)} %get-tuple-element.41.rest_0_, bf16[256,1024]{1,0:T(8,128)(2,1)S(1)} %collective-permute-done.13.rest_1_, ...), custom_call_target="tpu_custom_call" | custom-call | flops 8000000000 | bytes 10485760 | tf_op jit(solution)/shard_map/backward/pallas_call | solution.py:234
  181.6 2.3 %collective-permute-done.14 = bf16[8,256,256]{2,1,0:T(8,128)(2,1)S(1)} collective-permute-done((bf16[8,256,256]{2,1,0:T(8,128)(2,1)S(1)}, bf16[8,256,256]{2,1,0:T(8,128)(2,1)S(1)}, u32[]{:S(2)}, u32[]{:S(2)}) %collective-permute-start.14) | collective-permute-done | bytes 1048608 | tf_op jit(solution)/shard_map/ppermute | solution.py:33
  184.2 31.0 %all_to_all.15 = bf16[8,256,256]{2,1,0:T(8,128)(2,1)S(1)} all-to-all(bf16[8,256,256]{2,1,0:T(8,128)(2,1)S(1)} %add_convert_fusion), channel_id=1, replica_groups={{0,16,32,48,64,80,96,112},{8,24,40,56,72,88,104,120},{1,17,33,49,65,81,..., dimensions={0} | all-to-all | bytes 2097152 | tf_op jit(solution)/shard_map/all_to_all | solution.py:418
  (50 shorter events, 11.6 us)
Async XLA Ops:
  0.6 7.4 %copy-start.4 = (bf16[256,128]{1,0:T(8,128)(2,1)S(1)}, bf16[256,128]{1,0:T(8,128)(2,1)}, u32[]{:S(2)}) copy-start(bf16[256,128]{1,0:T(8,128)(2,1)} %param.8) | copy-start | bytes 196612
  0.6 7.4 %copy-start.3 = (bf16[256,128]{1,0:T(8,128)(2,1)S(1)}, bf16[256,128]{1,0:T(8,128)(2,1)}, u32[]{:S(2)}) copy-start(bf16[256,128]{1,0:T(8,128)(2,1)} %param.7) | copy-start | bytes 196612
  0.7 7.5 %copy-start.2 = (bf16[256,1024]{1,0:T(8,128)(2,1)S(1)}, bf16[256,1024]{1,0:T(8,128)(2,1)}, u32[]{:S(2)}) copy-start(bf16[256,1024]{1,0:T(8,128)(2,1)} %param.9) | copy-start | bytes 1572868
  2.9 29.8 %collective-permute-start.5 = (bf16[512,512]{1,0:T(8,128)(2,1)}, bf16[512,512]{1,0:T(8,128)(2,1)}, u32[]{:S(2)}, u32[]{:S(2)}) collective-permute-start(bf16[512,512]{1,0:T(8,128)(2,1)} %get-tuple-element.48), channel_id=1, source_target_pairs={{0,96},{8,104},{16,112},{24,120},{32,0},{40,8},{48,16},{56,24},{64... | collective-permute-start | bytes 1572872 | tf_op jit(solution)/shard_map/ppermute | solution.py:33
  5.7 27.0 %collective-permute-start.4 = (bf16[512,512]{1,0:T(8,128)(2,1)}, bf16[512,512]{1,0:T(8,128)(2,1)}, u32[]{:S(2)}, u32[]{:S(2)}) collective-permute-start(bf16[512,512]{1,0:T(8,128)(2,1)} %get-tuple-element.48), channel_id=1, source_target_pairs={{0,32},{8,40},{16,48},{24,56},{32,64},{40,72},{48,80},{56,88},{64,... | collective-permute-start | bytes 1572872 | tf_op jit(solution)/shard_map/ppermute | solution.py:33
  5.7 27.0 %collective-permute-start.6 = (bf16[512,512]{1,0:T(8,128)(2,1)}, bf16[512,512]{1,0:T(8,128)(2,1)}, u32[]{:S(2)}, u32[]{:S(2)}) collective-permute-start(bf16[512,512]{1,0:T(8,128)(2,1)} %get-tuple-element.48), channel_id=1, source_target_pairs={{0,64},{8,72},{16,80},{24,88},{32,96},{40,104},{48,112},{56,120},{... | collective-permute-start | bytes 1572872 | tf_op jit(solution)/shard_map/ppermute | solution.py:33
  8.0 1.3 collective-permute-start
  8.2 9.0 %collective-permute-start.2 = (bf16[256,512]{1,0:T(8,128)(2,1)S(1)}, bf16[256,512]{1,0:T(8,128)(2,1)S(1)}, u32[]{:S(2)}, u32[]{:S(2)}) collective-permute-start(bf16[256,512]{1,0:T(8,128)(2,1)S(1)} %get-tuple-element.51), channel_id=1, source_target_pairs={{0,8},{8,0},{16,24},{24,16},{32,40},{40,32},{48,56},{56,48},{64,72... | collective-permute-start | bytes 786440 | tf_op jit(solution)/shard_map/ppermute | solution.py:33
  9.4 7.8 %collective-permute-start.1 = (bf16[512,128]{1,0:T(8,128)(2,1)S(1)}, bf16[512,128]{1,0:T(8,128)(2,1)S(1)}, u32[]{:S(2)}, u32[]{:S(2)}) collective-permute-start(bf16[512,128]{1,0:T(8,128)(2,1)S(1)} %pad_maximum_fusion.5), channel_id=1, source_target_pairs={{0,16},{8,24},{16,0},{24,8},{32,48},{40,56},{48,32},{56,40},{64,80... | collective-permute-start | bytes 393224 | tf_op jit(solution)/shard_map/ppermute | solution.py:33
  17.2 11.3 %copy-start.5 = (s32[8]{0:T(128)S(1)}, s32[8]{0:T(128)}, u32[]{:S(2)}) copy-start(s32[8]{0:T(128)} %param.11) | copy-start | bytes 100
  17.2 36.9 %copy-start.1 = (bf16[512,512]{1,0:T(8,128)(2,1)}, bf16[512,512]{1,0:T(8,128)(2,1)S(1)}, u32[]{:S(2)}) copy-start(bf16[512,512]{1,0:T(8,128)(2,1)S(1)} %pad_maximum_fusion.3) | copy-start | bytes 1572868
  18.4 24.6 %all-to-all-start = ((bf16[4,1024,128]{2,1,0:T(8,128)(2,1)}), bf16[4,1024,128]{2,1,0:T(8,128)(2,1)S(1)}, u32[]{:S(2)}, u32[]{:S(2)}) async-start(bf16[4,1024,128]{2,1,0:T(8,128)(2,1)} %broadcast_in_dim.31), calls=%async_computation | async-start | bytes 2097152 | tf_op jit(solution)/shard_map/all_to_all | solution.py:347
  25.1 15.2 %collective-permute-start.3 = (bf16[512,512]{1,0:T(8,128)(2,1)S(1)}, bf16[512,512]{1,0:T(8,128)(2,1)}, u32[]{:S(2)}, u32[]{:S(2)}) collective-permute-start(bf16[512,512]{1,0:T(8,128)(2,1)S(1)} %get-tuple-element.26), channel_id=1, source_target_pairs={{0,16},{8,24},{16,0},{24,8},{32,48},{40,56},{48,32},{56,40},{64,80... | collective-permute-start | bytes 1572872 | tf_op jit(solution)/shard_map/ppermute | solution.py:33
  45.3 4.9 %collective-permute-start.8 = (bf16[4096,128]{1,0:T(8,128)(2,1)S(1)}, bf16[4096,128]{1,0:T(8,128)(2,1)S(1)}, u32[]{:S(2)}, u32[]{:S(2)}) collective-permute-start(bf16[4096,128]{1,0:T(8,128)(2,1)S(1)} %bitcast.38), channel_id=1, source_target_pairs={{0,8},{8,0},{16,24},{24,16},{32,40},{40,32},{48,56},{56,48},{64,72... | collective-permute-start | bytes 3145736 | tf_op jit(solution)/shard_map/ppermute | solution.py:33
  45.3 118.4 %all-to-all-start.1 = ((bf16[4,2,512,512]{3,2,1,0:T(8,128)(2,1)}), bf16[4,2,512,512]{3,2,1,0:T(8,128)(2,1)}, u32[]{:S(2)}, u32[]{:S(2)}) async-start(bf16[4,2,512,512]{3,2,1,0:T(8,128)(2,1)} %broadcast_in_dim.32), calls=%async_computation.1 | async-start | bytes 8388608 | tf_op jit(solution)/shard_map/all_to_all | solution.py:347
  50.2 113.5 %collective-permute-start.12 = (bf16[4,512,512]{2,1,0:T(8,128)(2,1)}, bf16[4,512,512]{2,1,0:T(8,128)(2,1)}, u32[]{:S(2)}, u32[]{:S(2)}) collective-permute-start(bf16[4,512,512]{2,1,0:T(8,128)(2,1)} %pad_maximum_fusion.rest_5_), channel_id=1, source_target_pairs={{0,16},{8,24},{16,0},{24,8},{32,48},{40,56},{48,32},{56,40},{64,80... | collective-permute-start | bytes 6291464 | tf_op jit(solution)/shard_map/ppermute | solution.py:33
  54.1 58.5 %collective-permute-start.7 = (bf16[512,512]{1,0:T(8,128)(2,1)S(1)}, bf16[512,512]{1,0:T(8,128)(2,1)S(1)}, u32[]{:S(2)}, u32[]{:S(2)}) collective-permute-start(bf16[512,512]{1,0:T(8,128)(2,1)S(1)} %pad_maximum_fusion.3), channel_id=1, source_target_pairs={{0,4},{1,5},{2,6},{3,7},{4,0},{5,1},{6,2},{7,3},{8,12},{9,13},{10,... | collective-permute-start | bytes 1572872 | tf_op jit(solution)/shard_map/ppermute | solution.py:41
  113.7 26.3 %collective-permute-start.11 = (bf16[2,512,512]{2,1,0:T(8,128)(2,1)S(1)}, bf16[2,512,512]{2,1,0:T(8,128)(2,1)}, u32[]{:S(2)}, u32[]{:S(2)}) collective-permute-start(bf16[2,512,512]{2,1,0:T(8,128)(2,1)S(1)} %pad_maximum_fusion.2.rest_0_), channel_id=1, source_target_pairs={{0,1},{1,2},{2,3},{3,0},{4,5},{5,6},{6,7},{7,4},{8,9},{9,10},{10,1... | collective-permute-start | bytes 3145736 | tf_op jit(solution)/shard_map/ppermute | solution.py:41
  115.4 48.2 %collective-permute-start.10 = (bf16[2,512,512]{2,1,0:T(8,128)(2,1)S(1)}, bf16[2,512,512]{2,1,0:T(8,128)(2,1)}, u32[]{:S(2)}, u32[]{:S(2)}) collective-permute-start(bf16[2,512,512]{2,1,0:T(8,128)(2,1)S(1)} %pad_maximum_fusion.2.rest_0_), channel_id=1, source_target_pairs={{0,2},{1,3},{2,0},{3,1},{4,6},{5,7},{6,4},{7,5},{8,10},{9,11},{10,... | collective-permute-start | bytes 3145736 | tf_op jit(solution)/shard_map/ppermute | solution.py:41
  118.3 45.3 %collective-permute-start.9 = (bf16[2,512,512]{2,1,0:T(8,128)(2,1)S(1)}, bf16[2,512,512]{2,1,0:T(8,128)(2,1)}, u32[]{:S(2)}, u32[]{:S(2)}) collective-permute-start(bf16[2,512,512]{2,1,0:T(8,128)(2,1)S(1)} %pad_maximum_fusion.2.rest_0_), channel_id=1, source_target_pairs={{0,3},{1,0},{2,1},{3,2},{4,7},{5,4},{6,5},{7,6},{8,11},{9,8},{10,9... | collective-permute-start | bytes 3145736 | tf_op jit(solution)/shard_map/ppermute | solution.py:41
  163.6 11.2 %copy-start = (f32[128,2048]{1,0:T(8,128)S(1)}, f32[128,2048]{1,0:T(8,128)}, u32[]{:S(2)}) copy-start(f32[128,2048]{1,0:T(8,128)} %get-tuple-element.36.rest_3_) | copy-start | bytes 3145732
  172.6 2.2 %collective-permute-start.13 = (bf16[256,1024]{1,0:T(8,128)(2,1)S(1)}, bf16[256,1024]{1,0:T(8,128)(2,1)S(1)}, u32[]{:S(2)}, u32[]{:S(2)}) collective-permute-start(bf16[256,1024]{1,0:T(8,128)(2,1)S(1)} %get-tuple-element.42), channel_id=1, source_target_pairs={{0,8},{8,0},{16,24},{24,16},{32,40},{40,32},{48,56},{56,48},{64,72... | collective-permute-start | bytes 1572872 | tf_op jit(solution)/shard_map/ppermute | solution.py:33
  180.3 3.6 %collective-permute-start.14 = (bf16[8,256,256]{2,1,0:T(8,128)(2,1)S(1)}, bf16[8,256,256]{2,1,0:T(8,128)(2,1)S(1)}, u32[]{:S(2)}, u32[]{:S(2)}) collective-permute-start(bf16[8,256,256]{2,1,0:T(8,128)(2,1)S(1)} %get-tuple-element.46), channel_id=1, source_target_pairs={{0,8},{8,0},{16,24},{24,16},{32,40},{40,32},{48,56},{56,48},{64,72... | collective-permute-start | bytes 3145736 | tf_op jit(solution)/shard_map/ppermute | solution.py:33

commit v24 on v21

--- a/solution.py
+++ b/solution.py
@@ -382,7 +382,7 @@
 
     own = [out_weight[:SPLIT], out_weight[SPLIT:]]
     plane1 = around_x(own[1])
-    own0 = after(own[0], chip_pair)
+    own0 = own[0]
     pair0 = dp_move(own0, 0, 1, 0)
     grad_pair = tensor_move(chip_grad, 1, 0)
     copies = copy(jnp.stack([own0, pair0]), groups_x)

time: 159 us -> 158 us (level)
  no operation moved by 1% of the time
where the time goes in v24:
time: 158 us; the launch traced here: 157 us
  waiting for transfers between devices  51.6 us (33%)
  starting transfers between devices  31.7 us (20%)
  blocking collectives  31 us (20%)
  Pallas kernels  21.7 us (14%)
  local copies, waits for them, and re-layouts  8.02 us (5%)
  between operations  6.78 us (4%)
  other arithmetic  6.33 us (4%)
    ppermute x4, waiting for transfers between devices, tensor_move(): return lax.ppermute(value, 'tensor', pairs)  43 us
    all_to_all x1, blocking collectives, local(): lax.all_to_all(chip_sums, 'dp', 0, 0, axis_index_groups=groups, tiled=True)  31 us
    ppermute x11, starting transfers between devices, dp_move(): return lax.ppermute(value, 'dp', pairs)  16.5 us
    pallas_call x1, Pallas kernels, project(): pl.pallas_call(project_kernel, grid=(1,), in_specs=[pl.BlockSpec(memory_s...  8.98 us
    ppermute x11, waiting for transfers between devices, dp_move(): return lax.ppermute(value, 'dp', pairs)  8.57 us
    all_to_all x2, starting transfers between devices, exchange(): lax.all_to_all(copies, axis, 0, 0, axis_index_groups=groups, tiled=True)  8.38 us
    pallas_call x1, Pallas kernels, forward(): pl.pallas_call(forward_kernel, grid_spec=pltpu.PrefetchScalarGridSpec(num...  7.28 us
    ppermute x4, starting transfers between devices, tensor_move(): return lax.ppermute(value, 'tensor', pairs)  6.85 us
  transfers between devices with their start and end apart: 17, of which 8 were waited for; matrix products, arithmetic and copies ran while one was open for 5% of the time, Pallas kernels for 5%

profile of v24, /device:TPU:0, one launch (start us, length us, event | category | flops | bytes accessed | tf_op | source)
XLA Modules:
  0.0 157.1 jit_solution(11854704132987769404)
XLA Ops:
  0.7 2.5 %slice_bitcast_fusion.1 = (bf16[1,512,512]{2,1,0:T(8,128)(2,1)}, bf16[1,512,512]{2,1,0:T(8,128)(2,1)S(1)}, bf16[512,512]{1,0:T(8,128)(2,1)}, bf16[512,512]{1,0:T(8,128)(2,1)S(1)}) fusion(bf16[1024,512]{1,0:T(8,128)(2,1)} %param.10), kind=kLoop, calls=%fused_computation.34 | loop fusion | bytes 3145728 | tf_op jit(solution)/shard_map/stack | solution.py:390
  3.1 2.8 %collective-permute-start.6 = (bf16[512,512]{1,0:T(8,128)(2,1)}, bf16[512,512]{1,0:T(8,128)(2,1)}, u32[]{:S(2)}, u32[]{:S(2)}) collective-permute-start(bf16[512,512]{1,0:T(8,128)(2,1)} %get-tuple-element.45), channel_id=1, source_target_pairs={{0,96},{8,104},{16,112},{24,120},{32,0},{40,8},{48,16},{56,24},{64... | collective-permute-start | bytes 1572872 | tf_op jit(solution)/shard_map/ppermute | solution.py:33
  6.0 2.3 %collective-permute-start.7 = (bf16[512,512]{1,0:T(8,128)(2,1)}, bf16[512,512]{1,0:T(8,128)(2,1)}, u32[]{:S(2)}, u32[]{:S(2)}) collective-permute-start(bf16[512,512]{1,0:T(8,128)(2,1)} %get-tuple-element.45), channel_id=1, source_target_pairs={{0,64},{8,72},{16,80},{24,88},{32,96},{40,104},{48,112},{56,120},{... | collective-permute-start | bytes 1572872 | tf_op jit(solution)/shard_map/ppermute | solution.py:33
  9.6 4.0 %collective-permute-start.1 = (bf16[512,128]{1,0:T(8,128)(2,1)S(1)}, bf16[512,128]{1,0:T(8,128)(2,1)S(1)}, u32[]{:S(2)}, u32[]{:S(2)}) collective-permute-start(bf16[512,128]{1,0:T(8,128)(2,1)S(1)} %pad_maximum_fusion.5), channel_id=1, source_target_pairs={{0,16},{8,24},{16,0},{24,8},{32,48},{40,56},{48,32},{56,40},{64,80... | collective-permute-start | bytes 393224 | tf_op jit(solution)/shard_map/ppermute | solution.py:33
  17.4 3.2 %collective-permute-start.3 = (bf16[512,512]{1,0:T(8,128)(2,1)S(1)}, bf16[512,512]{1,0:T(8,128)(2,1)}, u32[]{:S(2)}, u32[]{:S(2)}) collective-permute-start(bf16[512,512]{1,0:T(8,128)(2,1)S(1)} %get-tuple-element.46), channel_id=1, source_target_pairs={{0,16},{8,24},{16,0},{24,8},{32,48},{40,56},{48,32},{56,40},{64,80... | collective-permute-start | bytes 1572872 | tf_op jit(solution)/shard_map/ppermute | solution.py:33
  21.9 3.5 %all-to-all-start = ((bf16[4,1024,128]{2,1,0:T(8,128)(2,1)}), bf16[4,1024,128]{2,1,0:T(8,128)(2,1)S(1)}, u32[]{:S(2)}, u32[]{:S(2)}) async-start(bf16[4,1024,128]{2,1,0:T(8,128)(2,1)} %broadcast_in_dim.31), calls=%async_computation | async-start | bytes 2097152 | tf_op jit(solution)/shard_map/all_to_all | solution.py:347
  30.7 3.1 %collective-permute-done.3 = bf16[512,512]{1,0:T(8,128)(2,1)} collective-permute-done((bf16[512,512]{1,0:T(8,128)(2,1)S(1)}, bf16[512,512]{1,0:T(8,128)(2,1)}, u32[]{:S(2)}, u32[]{:S(2)}) %collective-permute-start.3) | collective-permute-done | bytes 524320 | tf_op jit(solution)/shard_map/ppermute | solution.py:33
  35.0 3.2 %pad_maximum_fusion.rest_5_ = bf16[4,512,512]{2,1,0:T(8,128)(2,1)} fusion(bf16[1,512,512]{2,1,0:T(8,128)(2,1)} %bitcast.8, bf16[1,512,512]{2,1,0:T(8,128)(2,1)} %bitcast.7, bf16[1,512,512]{2,1,0:T(8,128)(2,1)} %bitcast.6, bf16[1,512,512]{2,1,0:T(8,128)(2,1)} %get-tuple-element.43), kind=kLoop, calls=%fused_computation | loop fusion | flops 3145728 | bytes 4194304 | tf_op jit(solution)/shard_map/stack | solution.py:390
  38.3 5.9 %collective-permute-done.4 = bf16[512,512]{1,0:T(8,128)(2,1)} collective-permute-done((bf16[512,512]{1,0:T(8,128)(2,1)S(1)}, bf16[512,512]{1,0:T(8,128)(2,1)}, u32[]{:S(2)}, u32[]{:S(2)}) %collective-permute-start.4) | collective-permute-done | bytes 524320 | tf_op jit(solution)/shard_map/ppermute | solution.py:41
  45.3 2.3 %broadcast_in_dim.32 = bf16[4,2,512,512]{3,2,1,0:T(8,128)(2,1)} broadcast(bf16[2,512,512]{2,1,0:T(8,128)(2,1)S(1)} %pad_maximum_fusion.1), dimensions={1,2,3} | broadcast | bytes 5242880 | tf_op jit(solution)/shard_map/broadcast_in_dim | solution.py:344
  47.6 4.9 %all-to-all-start.1 = ((bf16[4,2,512,512]{3,2,1,0:T(8,128)(2,1)}), bf16[4,2,512,512]{3,2,1,0:T(8,128)(2,1)}, u32[]{:S(2)}, u32[]{:S(2)}) async-start(bf16[4,2,512,512]{3,2,1,0:T(8,128)(2,1)} %broadcast_in_dim.32), calls=%async_computation.1 | async-start | bytes 8388608 | tf_op jit(solution)/shard_map/all_to_all | solution.py:347
  52.5 1.9 %collective-permute-start.12 = (bf16[4,512,512]{2,1,0:T(8,128)(2,1)}, bf16[4,512,512]{2,1,0:T(8,128)(2,1)}, u32[]{:S(2)}, u32[]{:S(2)}) collective-permute-start(bf16[4,512,512]{2,1,0:T(8,128)(2,1)} %pad_maximum_fusion.rest_5_), channel_id=1, source_target_pairs={{0,16},{8,24},{16,0},{24,8},{32,48},{40,56},{48,32},{56,40},{64,80... | collective-permute-start | bytes 6291464 | tf_op jit(solution)/shard_map/ppermute | solution.py:33
  54.4 1.6 %collective-permute-start.11 = (bf16[2,512,512]{2,1,0:T(8,128)(2,1)S(1)}, bf16[2,512,512]{2,1,0:T(8,128)(2,1)}, u32[]{:S(2)}, u32[]{:S(2)}) collective-permute-start(bf16[2,512,512]{2,1,0:T(8,128)(2,1)S(1)} %pad_maximum_fusion.2.rest_0_), channel_id=1, source_target_pairs={{0,1},{1,2},{2,3},{3,0},{4,5},{5,6},{6,7},{7,4},{8,9},{9,10},{10,1... | collective-permute-start | bytes 3145736 | tf_op jit(solution)/shard_map/ppermute | solution.py:41
  56.0 2.9 %collective-permute-start.10 = (bf16[2,512,512]{2,1,0:T(8,128)(2,1)S(1)}, bf16[2,512,512]{2,1,0:T(8,128)(2,1)}, u32[]{:S(2)}, u32[]{:S(2)}) collective-permute-start(bf16[2,512,512]{2,1,0:T(8,128)(2,1)S(1)} %pad_maximum_fusion.2.rest_0_), channel_id=1, source_target_pairs={{0,2},{1,3},{2,0},{3,1},{4,6},{5,7},{6,4},{7,5},{8,10},{9,11},{10,... | collective-permute-start | bytes 3145736 | tf_op jit(solution)/shard_map/ppermute | solution.py:41
  58.9 1.3 collective-permute-start.9
  60.3 7.3 %forward.1 = (bf16[2816,2048]{1,0:T(8,128)(2,1)}, f32[128,2048]{1,0:T(8,128)}) custom-call(s32[36]{0:T(128)S(1)} %concatenate.16.info, s32[1,256]{1,0:T(1,128)S(1)} %iota_add_fusion.pos_ref, s32[1,256]{1,0:T(1,128)S(1)} %bitcast.42, bf16[256,1024]{1,0:T(8,128)(2,1)} %rest_4_.1, bf16[4096,128]{1,0:T(8,128)(2,1)S(1)} %bitcast.40, ...), custom_call_target="tpu_custom_call" | custom-call | flops 100000000 | bytes 1048576 | tf_op jit(solution)/shard_map/forward/pallas_call | solution.py:140
  67.6 13.5 %collective-permute-done.11.rest_3_ = bf16[2,512,512]{2,1,0:T(8,128)(2,1)} collective-permute-done((bf16[2,512,512]{2,1,0:T(8,128)(2,1)S(1)}, bf16[2,512,512]{2,1,0:T(8,128)(2,1)}, u32[]{:S(2)}, u32[]{:S(2)}) %collective-permute-start.11) | collective-permute-done | bytes 1048608 | tf_op jit(solution)/shard_map/ppermute | solution.py:41
  81.0 23.6 %collective-permute-done.10.rest_2_ = bf16[2,512,512]{2,1,0:T(8,128)(2,1)} collective-permute-done((bf16[2,512,512]{2,1,0:T(8,128)(2,1)S(1)}, bf16[2,512,512]{2,1,0:T(8,128)(2,1)}, u32[]{:S(2)}, u32[]{:S(2)}) %collective-permute-start.10) | collective-permute-done | bytes 1048608 | tf_op jit(solution)/shard_map/ppermute | solution.py:41
  104.7 9.0 %project.1 = (f32[256,1024]{1,0:T(8,128)S(1)}, bf16[256,1024]{1,0:T(8,128)(2,1)S(1)}) custom-call(s32[16]{0:T(128)S(1)} %stack.127.slots, bf16[2,512,512]{2,1,0:T(8,128)(2,1)S(1)} %pad_maximum_fusion.2.rest_0_, bf16[2,512,512]{2,1,0:T(8,128)(2,1)} %collective-permute-done.9.rest_1_, bf16[2,512,512]{2,1,0:T(8,128)(2,1)} %collective-permute-done.10.rest_2_, ...), custom_call_target="tpu_custom_call" | custom-call | flops 4294967296 | bytes 12582912 | tf_op jit(solution)/shard_map/project/pallas_call | solution.py:314
  114.0 1.9 %collective-permute-done.13.rest_1_ = bf16[256,1024]{1,0:T(8,128)(2,1)S(1)} collective-permute-done((bf16[256,1024]{1,0:T(8,128)(2,1)S(1)}, bf16[256,1024]{1,0:T(8,128)(2,1)S(1)}, u32[]{:S(2)}, u32[]{:S(2)}) %collective-permute-start.13) | collective-permute-done | bytes 524320 | tf_op jit(solution)/shard_map/ppermute | solution.py:33
  115.9 5.4 %backward.1 = (bf16[256,1024]{1,0:T(8,128)(2,1)}, f32[8,256,256]{2,1,0:T(8,128)S(1)}, bf16[8,256,256]{2,1,0:T(8,128)(2,1)S(1)}) custom-call(s32[36]{0:T(128)S(1)} %concatenate.16.info, f32[256,1024]{1,0:T(8,128)S(1)} %get-tuple-element.37.rest_0_, bf16[256,1024]{1,0:T(8,128)(2,1)S(1)} %collective-permute-done.13.rest_1_, ...), custom_call_target="tpu_custom_call" | custom-call | flops 8000000000 | bytes 10485760 | tf_op jit(solution)/shard_map/backward/pallas_call | solution.py:234
  121.3 1.3 collective-permute-start.14
  122.6 2.3 %collective-permute-done.14 = bf16[8,256,256]{2,1,0:T(8,128)(2,1)S(1)} collective-permute-done((bf16[8,256,256]{2,1,0:T(8,128)(2,1)S(1)}, bf16[8,256,256]{2,1,0:T(8,128)(2,1)S(1)}, u32[]{:S(2)}, u32[]{:S(2)}) %collective-permute-start.14) | collective-permute-done | bytes 1048608 | tf_op jit(solution)/shard_map/ppermute | solution.py:33
  125.3 31.0 %all_to_all.15 = bf16[8,256,256]{2,1,0:T(8,128)(2,1)S(1)} all-to-all(bf16[8,256,256]{2,1,0:T(8,128)(2,1)S(1)} %add_convert_fusion), channel_id=1, replica_groups={{0,16,32,48,64,80,96,112},{8,24,40,56,72,88,104,120},{1,17,33,49,65,81,..., dimensions={0} | all-to-all | bytes 2097152 | tf_op jit(solution)/shard_map/all_to_all | solution.py:417
  (52 shorter events, 9.5 us)
Async XLA Ops:
  0.6 7.6 %copy-start.5 = (bf16[256,128]{1,0:T(8,128)(2,1)S(1)}, bf16[256,128]{1,0:T(8,128)(2,1)}, u32[]{:S(2)}) copy-start(bf16[256,128]{1,0:T(8,128)(2,1)} %param.8) | copy-start | bytes 196612
  0.6 7.6 %copy-start.4 = (bf16[256,128]{1,0:T(8,128)(2,1)S(1)}, bf16[256,128]{1,0:T(8,128)(2,1)}, u32[]{:S(2)}) copy-start(bf16[256,128]{1,0:T(8,128)(2,1)} %param.7) | copy-start | bytes 196612
  0.7 7.7 %copy-start.3 = (bf16[256,1024]{1,0:T(8,128)(2,1)S(1)}, bf16[256,1024]{1,0:T(8,128)(2,1)}, u32[]{:S(2)}) copy-start(bf16[256,1024]{1,0:T(8,128)(2,1)} %param.9) | copy-start | bytes 1572868
  3.1 31.9 %collective-permute-start.6 = (bf16[512,512]{1,0:T(8,128)(2,1)}, bf16[512,512]{1,0:T(8,128)(2,1)}, u32[]{:S(2)}, u32[]{:S(2)}) collective-permute-start(bf16[512,512]{1,0:T(8,128)(2,1)} %get-tuple-element.45), channel_id=1, source_target_pairs={{0,96},{8,104},{16,112},{24,120},{32,0},{40,8},{48,16},{56,24},{64... | collective-permute-start | bytes 1572872 | tf_op jit(solution)/shard_map/ppermute | solution.py:33
  6.0 29.1 %collective-permute-start.5 = (bf16[512,512]{1,0:T(8,128)(2,1)}, bf16[512,512]{1,0:T(8,128)(2,1)}, u32[]{:S(2)}, u32[]{:S(2)}) collective-permute-start(bf16[512,512]{1,0:T(8,128)(2,1)} %get-tuple-element.45), channel_id=1, source_target_pairs={{0,32},{8,40},{16,48},{24,56},{32,64},{40,72},{48,80},{56,88},{64,... | collective-permute-start | bytes 1572872 | tf_op jit(solution)/shard_map/ppermute | solution.py:33
  6.0 29.1 %collective-permute-start.7 = (bf16[512,512]{1,0:T(8,128)(2,1)}, bf16[512,512]{1,0:T(8,128)(2,1)}, u32[]{:S(2)}, u32[]{:S(2)}) collective-permute-start(bf16[512,512]{1,0:T(8,128)(2,1)} %get-tuple-element.45), channel_id=1, source_target_pairs={{0,64},{8,72},{16,80},{24,88},{32,96},{40,104},{48,112},{56,120},{... | collective-permute-start | bytes 1572872 | tf_op jit(solution)/shard_map/ppermute | solution.py:33
  8.3 1.3 collective-permute-start
  8.4 12.2 %collective-permute-start.2 = (bf16[256,512]{1,0:T(8,128)(2,1)S(1)}, bf16[256,512]{1,0:T(8,128)(2,1)S(1)}, u32[]{:S(2)}, u32[]{:S(2)}) collective-permute-start(bf16[256,512]{1,0:T(8,128)(2,1)S(1)} %get-tuple-element.48), channel_id=1, source_target_pairs={{0,8},{8,0},{16,24},{24,16},{32,40},{40,32},{48,56},{56,48},{64,72... | collective-permute-start | bytes 786440 | tf_op jit(solution)/shard_map/ppermute | solution.py:33
  9.6 7.8 %collective-permute-start.1 = (bf16[512,128]{1,0:T(8,128)(2,1)S(1)}, bf16[512,128]{1,0:T(8,128)(2,1)S(1)}, u32[]{:S(2)}, u32[]{:S(2)}) collective-permute-start(bf16[512,128]{1,0:T(8,128)(2,1)S(1)} %pad_maximum_fusion.5), channel_id=1, source_target_pairs={{0,16},{8,24},{16,0},{24,8},{32,48},{40,56},{48,32},{56,40},{64,80... | collective-permute-start | bytes 393224 | tf_op jit(solution)/shard_map/ppermute | solution.py:33
  17.4 16.4 %collective-permute-start.3 = (bf16[512,512]{1,0:T(8,128)(2,1)S(1)}, bf16[512,512]{1,0:T(8,128)(2,1)}, u32[]{:S(2)}, u32[]{:S(2)}) collective-permute-start(bf16[512,512]{1,0:T(8,128)(2,1)S(1)} %get-tuple-element.46), channel_id=1, source_target_pairs={{0,16},{8,24},{16,0},{24,8},{32,48},{40,56},{48,32},{56,40},{64,80... | collective-permute-start | bytes 1572872 | tf_op jit(solution)/shard_map/ppermute | solution.py:33
  20.7 4.8 %copy-start.6 = (s32[8]{0:T(128)S(1)}, s32[8]{0:T(128)}, u32[]{:S(2)}) copy-start(s32[8]{0:T(128)} %param.11) | copy-start | bytes 100
  20.7 14.3 %copy-start.1 = (bf16[512,512]{1,0:T(8,128)(2,1)}, bf16[512,512]{1,0:T(8,128)(2,1)S(1)}, u32[]{:S(2)}) copy-start(bf16[512,512]{1,0:T(8,128)(2,1)S(1)} %pad_maximum_fusion.3) | copy-start | bytes 1572868
  21.9 23.4 %all-to-all-start = ((bf16[4,1024,128]{2,1,0:T(8,128)(2,1)}), bf16[4,1024,128]{2,1,0:T(8,128)(2,1)S(1)}, u32[]{:S(2)}, u32[]{:S(2)}) async-start(bf16[4,1024,128]{2,1,0:T(8,128)(2,1)} %broadcast_in_dim.31), calls=%async_computation | async-start | bytes 2097152 | tf_op jit(solution)/shard_map/all_to_all | solution.py:347
  25.6 18.5 %collective-permute-start.4 = (bf16[512,512]{1,0:T(8,128)(2,1)S(1)}, bf16[512,512]{1,0:T(8,128)(2,1)}, u32[]{:S(2)}, u32[]{:S(2)}) collective-permute-start(bf16[512,512]{1,0:T(8,128)(2,1)S(1)} %pad_maximum_fusion.3), channel_id=1, source_target_pairs={{0,4},{1,5},{2,6},{3,7},{4,0},{5,1},{6,2},{7,3},{8,12},{9,13},{10,... | collective-permute-start | bytes 1572872 | tf_op jit(solution)/shard_map/ppermute | solution.py:41
  35.0 9.1 %copy-start.2 = (bf16[512,512]{1,0:T(8,128)(2,1)S(1)}, bf16[512,512]{1,0:T(8,128)(2,1)}, u32[]{:S(2)}) copy-start(bf16[512,512]{1,0:T(8,128)(2,1)} %copy-done.1) | copy-start | bytes 1572868
  47.6 4.9 %collective-permute-start.8 = (bf16[4096,128]{1,0:T(8,128)(2,1)S(1)}, bf16[4096,128]{1,0:T(8,128)(2,1)S(1)}, u32[]{:S(2)}, u32[]{:S(2)}) collective-permute-start(bf16[4096,128]{1,0:T(8,128)(2,1)S(1)} %bitcast.39), channel_id=1, source_target_pairs={{0,8},{8,0},{16,24},{24,16},{32,40},{40,32},{48,56},{56,48},{64,72... | collective-permute-start | bytes 3145736 | tf_op jit(solution)/shard_map/ppermute | solution.py:33
  47.6 57.1 %all-to-all-start.1 = ((bf16[4,2,512,512]{3,2,1,0:T(8,128)(2,1)}), bf16[4,2,512,512]{3,2,1,0:T(8,128)(2,1)}, u32[]{:S(2)}, u32[]{:S(2)}) async-start(bf16[4,2,512,512]{3,2,1,0:T(8,128)(2,1)} %broadcast_in_dim.32), calls=%async_computation.1 | async-start | bytes 8388608 | tf_op jit(solution)/shard_map/all_to_all | solution.py:347
  52.5 52.2 %collective-permute-start.12 = (bf16[4,512,512]{2,1,0:T(8,128)(2,1)}, bf16[4,512,512]{2,1,0:T(8,128)(2,1)}, u32[]{:S(2)}, u32[]{:S(2)}) collective-permute-start(bf16[4,512,512]{2,1,0:T(8,128)(2,1)} %pad_maximum_fusion.rest_5_), channel_id=1, source_target_pairs={{0,16},{8,24},{16,0},{24,8},{32,48},{40,56},{48,32},{56,40},{64,80... | collective-permute-start | bytes 6291464 | tf_op jit(solution)/shard_map/ppermute | solution.py:33
  54.4 26.7 %collective-permute-start.11 = (bf16[2,512,512]{2,1,0:T(8,128)(2,1)S(1)}, bf16[2,512,512]{2,1,0:T(8,128)(2,1)}, u32[]{:S(2)}, u32[]{:S(2)}) collective-permute-start(bf16[2,512,512]{2,1,0:T(8,128)(2,1)S(1)} %pad_maximum_fusion.2.rest_0_), channel_id=1, source_target_pairs={{0,1},{1,2},{2,3},{3,0},{4,5},{5,6},{6,7},{7,4},{8,9},{9,10},{10,1... | collective-permute-start | bytes 3145736 | tf_op jit(solution)/shard_map/ppermute | solution.py:41
  56.0 48.7 %collective-permute-start.10 = (bf16[2,512,512]{2,1,0:T(8,128)(2,1)S(1)}, bf16[2,512,512]{2,1,0:T(8,128)(2,1)}, u32[]{:S(2)}, u32[]{:S(2)}) collective-permute-start(bf16[2,512,512]{2,1,0:T(8,128)(2,1)S(1)} %pad_maximum_fusion.2.rest_0_), channel_id=1, source_target_pairs={{0,2},{1,3},{2,0},{3,1},{4,6},{5,7},{6,4},{7,5},{8,10},{9,11},{10,... | collective-permute-start | bytes 3145736 | tf_op jit(solution)/shard_map/ppermute | solution.py:41
  58.9 45.8 %collective-permute-start.9 = (bf16[2,512,512]{2,1,0:T(8,128)(2,1)S(1)}, bf16[2,512,512]{2,1,0:T(8,128)(2,1)}, u32[]{:S(2)}, u32[]{:S(2)}) collective-permute-start(bf16[2,512,512]{2,1,0:T(8,128)(2,1)S(1)} %pad_maximum_fusion.2.rest_0_), channel_id=1, source_target_pairs={{0,3},{1,0},{2,1},{3,2},{4,7},{5,4},{6,5},{7,6},{8,11},{9,8},{10,9... | collective-permute-start | bytes 3145736 | tf_op jit(solution)/shard_map/ppermute | solution.py:41
  104.7 11.2 %copy-start = (f32[128,2048]{1,0:T(8,128)S(1)}, f32[128,2048]{1,0:T(8,128)}, u32[]{:S(2)}) copy-start(f32[128,2048]{1,0:T(8,128)} %get-tuple-element.32.rest_3_) | copy-start | bytes 3145732
  113.7 2.2 %collective-permute-start.13 = (bf16[256,1024]{1,0:T(8,128)(2,1)S(1)}, bf16[256,1024]{1,0:T(8,128)(2,1)S(1)}, u32[]{:S(2)}, u32[]{:S(2)}) collective-permute-start(bf16[256,1024]{1,0:T(8,128)(2,1)S(1)} %get-tuple-element.38), channel_id=1, source_target_pairs={{0,8},{8,0},{16,24},{24,16},{32,40},{40,32},{48,56},{56,48},{64,72... | collective-permute-start | bytes 1572872 | tf_op jit(solution)/shard_map/ppermute | solution.py:33
  121.3 3.6 %collective-permute-start.14 = (bf16[8,256,256]{2,1,0:T(8,128)(2,1)S(1)}, bf16[8,256,256]{2,1,0:T(8,128)(2,1)S(1)}, u32[]{:S(2)}, u32[]{:S(2)}) collective-permute-start(bf16[8,256,256]{2,1,0:T(8,128)(2,1)S(1)} %get-tuple-element.42), channel_id=1, source_target_pairs={{0,8},{8,0},{16,24},{24,16},{32,40},{40,32},{48,56},{56,48},{64,72... | collective-permute-start | bytes 3145736 | tf_op jit(solution)/shard_map/ppermute | solution.py:33
